TPU v7x, 32 devices: a whole 2x2x4 slice. The times are simulated.
32 devices in a mesh: dp: 8 (over y, x, core), tensor: 4 (over z).
Axes of the slice: x: 2, y: 2, z: 4, core: 2. Of those that a mesh axis runs over, the one named last changes fastest.
Arguments:
- tokens: bfloat16 [4096, 8192], P('dp', 'tensor'), may hold values from -6 to 6
- ref_gain: float32 [8192], P('tensor'), may hold values from 0.1 to 1.9
- ref_weight: bfloat16 [8192, 512], P('tensor'), may hold values from -0.0625 to 0.0625
- pol_gain: float32 [8192], replicated, may hold values from 0.1 to 1.9
- pol_weight: bfloat16 [8192, 512], P('dp'), may hold values from -0.0625 to 0.0625
- lengths: int32 [8, 4, 8], P('dp', 'tensor'), may hold values from 1 to 32, 128 in all within a row
- bins: int32 [8, 4, 8], P('dp', 'tensor'), may hold values from 0 to 7, each once within a row
- advantage: float32 [8, 4, 8], P('dp', 'tensor'), may hold values from -4 to 4
- logprob_gap: float32 [4096], P(('dp', 'tensor')), may hold values from -1 to 1
- cotangent: bfloat16 [8, 4, 256, 512], P('dp', 'tensor'), may hold values from -6 to 6
Outputs:
- policy_values: bfloat16 [8, 4, 256, 512], P('dp', 'tensor')
- grad_weight: float32 [8192, 512], P(('dp', 'tensor'))
Inputs may be any that keep to these rules, and one draw needn't show every extreme that they name: `lengths`: lengths of the 8 sequences of one run, in the order in which they lie in it; they sum to 128, and the longest of every run is exactly 32. The sequences of one run go to distinct bins: each bin takes exactly one sequence of every run.
All inputs are finite; a program needn't handle non-finite values.
Results may differ from a plain program's by a relative error of at most 0.015.
Values may be sent and summed in bfloat16 or wider, within the bound.
No kernel may reach another device: no remote copies, remote signals or barrier semaphores. Data moves between devices by JAX's collectives and lax.ppermute only.
A program may use at most 64 MiB of HBM per device.

v0:
```python
import math

import jax
import jax.numpy as jnp
from jax import lax
from jax.sharding import PartitionSpec as P

EPS = 1e-06
BETA = 1.0


def rounded(values):
    return lax.optimization_barrier(values.astype(jnp.bfloat16)).astype(jnp.float32)


def on_device(
    tokens,
    ref_gain,
    ref_weight,
    pol_gain,
    pol_weight,
    lengths,
    bins,
    advantage,
    logprob_gap,
    cotangent,
):
    tensor_count = lax.axis_size("tensor")
    dp_count = lax.axis_size("dp")
    group_rows = tokens.shape[0]
    own_rows = group_rows // tensor_count
    slot_count = cotangent.shape[2]
    span_rows = slot_count // dp_count
    model_width = pol_gain.shape[0]
    value_width = ref_weight.shape[1]
    scaled = (tokens.astype(jnp.float32) * ref_gain[None, :]).astype(jnp.bfloat16)
    partial_value = rounded(jnp.dot(scaled, ref_weight, preferred_element_type=jnp.float32))
    summed = lax.psum(partial_value.astype(jnp.bfloat16), "tensor").astype(jnp.float32)
    owned_sum = lax.dynamic_slice_in_dim(summed, lax.axis_index("tensor") * own_rows, own_rows, 0)
    full_rows = lax.all_to_all(tokens, "tensor", split_axis=0, concat_axis=1, tiled=True)
    row_power = jnp.mean(jnp.square(full_rows.astype(jnp.float32)), axis=1)
    ref_values = (owned_sum * lax.rsqrt(row_power + EPS)[:, None]).astype(jnp.bfloat16)
    seq_lens = lengths.reshape(-1)
    seq_bins = bins.reshape(-1)
    seq_adv = advantage.reshape(-1)
    seq_starts = jnp.cumsum(seq_lens) - seq_lens
    chosen = seq_bins[None, :] == jnp.arange(dp_count, dtype=jnp.int32)[:, None]
    bin_len = jnp.sum(jnp.where(chosen, seq_lens[None, :], 0), axis=1)
    bin_start = jnp.sum(jnp.where(chosen, seq_starts[None, :], 0), axis=1)
    bin_adv = jnp.sum(jnp.where(chosen, seq_adv[None, :], jnp.float32(0.0)), axis=1)
    offsets = jnp.arange(span_rows, dtype=jnp.int32)
    usable = offsets[None, :] < bin_len[:, None]
    row_picks = jnp.clip(bin_start[:, None] + offsets[None, :], 0, own_rows - 1)
    send_rows = jnp.where(usable[:, :, None], full_rows[row_picks], jnp.zeros((), jnp.bfloat16))
    send_ref = jnp.where(usable[:, :, None], ref_values[row_picks], jnp.zeros((), jnp.bfloat16))
    len_float = bin_len.astype(jnp.float32)[:, None]
    importance = jnp.minimum(jnp.exp(logprob_gap[row_picks]), jnp.float32(2.0))
    coef_adv = jnp.where(
        usable, bin_adv[:, None] * importance / len_float, jnp.float32(0.0)
    ).astype(jnp.bfloat16)
    coef_pull = jnp.where(usable, BETA / len_float, jnp.float32(0.0)).astype(jnp.bfloat16)
    got_rows, got_ref, got_adv, got_pull = (
        lax.all_to_all(send_rows, "dp", split_axis=0, concat_axis=0, tiled=True),
        lax.all_to_all(send_ref, "dp", split_axis=0, concat_axis=0, tiled=True),
        lax.all_to_all(coef_adv, "dp", split_axis=0, concat_axis=0, tiled=True),
        lax.all_to_all(coef_pull, "dp", split_axis=0, concat_axis=0, tiled=True),
    )
    packed_rows = got_rows.reshape(slot_count, model_width)
    power = jnp.mean(jnp.square(packed_rows.astype(jnp.float32)), axis=1)
    normed = (
        packed_rows.astype(jnp.float32) * lax.rsqrt(power + EPS)[:, None] * pol_gain[None, :]
    ).astype(jnp.bfloat16)
    packed_ref = got_ref.reshape(slot_count, value_width).astype(jnp.float32)
    adv_column = got_adv.reshape(slot_count, 1).astype(jnp.float32)
    pull_column = got_pull.reshape(slot_count, 1).astype(jnp.float32)
    upstream = cotangent.reshape(slot_count, value_width).astype(jnp.float32)
    factor = 1.0 / math.sqrt(dp_count * tensor_count * seq_lens.shape[0])
    feature_block = normed
    values = jnp.dot(
        feature_block,
        lax.all_gather(pol_weight, "dp", axis=0, tiled=True),
        preferred_element_type=jnp.float32,
    )
    slope = (adv_column * upstream + pull_column * (values - packed_ref)).astype(jnp.bfloat16)
    feature_block = normed
    grad_weight = lax.psum_scatter(
        lax.dot_general(
            feature_block, slope, (((0,), (0,)), ((), ())), preferred_element_type=jnp.float32
        )
        * factor,
        ("dp", "tensor"),
        scatter_dimension=0,
        tiled=True,
    )
    policy_values = values.astype(jnp.bfloat16).reshape(1, 1, slot_count, value_width)
    return (policy_values, grad_weight)


def solution(mesh):
    in_specs = (
        P("dp", "tensor"),
        P("tensor"),
        P("tensor", None),
        P(),
        P("dp", None),
        P("dp", "tensor", None),
        P("dp", "tensor", None),
        P("dp", "tensor", None),
        P(("dp", "tensor")),
        P("dp", "tensor", None, None),
    )
    out_specs = (P("dp", "tensor", None, None), P(("dp", "tensor"), None))
    return jax.shard_map(
        on_device, mesh=mesh, in_specs=in_specs, out_specs=out_specs, check_vma=False
    )
```

profile of v0, /device:TPU:4, one launch (start us, length us, event | category | flops | bytes accessed | tf_op | source)
XLA Modules:
  0.0 563.9 jit_solution(6393061926077886438)
XLA Ops:
  8.1 1.5 copy-done
  9.6 3.6 fusion.4
  13.3 0.5 all-gather.2.cloned.1.call-update
  13.9 4.9 all-to-all-start
  18.7 0.2 reduce-window.8
  18.9 0.1 select_reduce_fusion.2
  19.2 0.1 reshape.312
  19.3 1.9 gather_fusion.1
  21.1 0.1 min.28
  21.2 0.1 select_reduce_fusion
  21.4 0.7 fusion.12
  22.0 0.7 fusion.13
  22.7 61.2 %all-to-all-done = bf16[4,128,2048]{2,1,0:T(8,128)(2,1)} async-done(((bf16[4,128,2048]{2,1,0:T(8,128)(2,1)}), bf16[4,128,2048]{2,1,0:T(8,128)(2,1)}, u32[]{:S(2)}, u32[]{:S(2)}) %all-to-all-start) | async-done | bytes 2097184 | tf_op jit(solution)/shard_map/all_to_all | solution.py:40
  84.0 4.2 all-to-all-start.2
  88.3 3.2 copy.16
  91.5 10.8 %gather_fusion = bf16[256,8192]{1,0:T(8,128)(2,1)} fusion(bf16[128,8192]{1,0:T(8,128)(2,1)} %bitcast.36, s32[1024]{0:T(1024)S(1)} %pad_clamp_fusion), kind=kCustom, calls=%fused_computation | custom fusion | bytes 8389632 | tf_op jit(solution)/shard_map/gather | solution.py:54
  102.3 4.2 all-to-all-start.3
  106.5 4.5 broadcast_select_fusion
  111.0 4.6 all-to-all-start.1
  115.8 2.1 multiply_reduce_fusion.1
  117.9 1.0 multiply_convert_fusion.4
  118.9 1.2 gather_fusion.2
  120.1 0.8 broadcast_select_fusion.1
  120.9 42.5 %all-to-all-done.1 = bf16[8,32,8192]{2,1,0:T(8,128)(2,1)} async-done(((bf16[8,32,8192]{2,1,0:T(8,128)(2,1)}), bf16[8,32,8192]{2,1,0:T(8,128)(2,1)}, u32[]{:S(2)}, u32[]{:S(2)}) %all-to-all-start.1) | async-done | bytes 4194336 | tf_op jit(solution)/shard_map/all_to_all | solution.py:63
  163.3 4.8 all-to-all-start.4
  168.1 3.1 multiply_reduce_fusion
  171.3 0.1 rsqrt.18
  171.3 5.3 fusion.1
  176.6 7.0 %fusion.14 = f32[256,512]{1,0:T(8,128)S(1)} fusion(bf16[256,8192]{1,0:T(8,128)(2,1)} %fusion.1, bf16[8192,512]{1,0:T(8,128)(2,1)} %all-gather.2.cloned.1.call-done), kind=kOutput, calls=%fused_computation.43 | convolution fusion | flops 2147483648 | bytes 13107200 | tf_op jit(solution)/shard_map/dot_general | solution.py:79
  183.7 10.4 %convolution_multiply_fusion = f32[8192,512]{1,0:T(8,128)} fusion(bf16[256,8192]{1,0:T(8,128)(2,1)} %fusion.1, f32[256,512]{1,0:T(8,128)S(1)} %fusion.14, bf16[256,512]{1,0:T(8,128)(2,1)S(1)} %bitcast.39, bf16[1,1,256,512]{3,2,1,0:T(8,128)(2,1)S(1)} %copy-done.2, f32[256]{0:T(256)S(1)} %reshape.308, f32[256]{0:T(256)S(1)} %reshape.306), kind=kOutput, calls=%fused_computation.3 | convolution fusion | flops 2152595456 | bytes 22022144 | tf_op jit(solution)/shard_map/dot_general | solution.py:87
  194.1 0.7 convert_bitcast_fusion
  194.8 361.7 %reduce-scatter.2.cloned.1.call-done = f32[256,512]{1,0:T(8,128)} async-done(((f32[8192,512]{1,0:T(8,128)}), f32[256,512]{1,0:T(8,128)}) %reduce-scatter.2.cloned.1.call-update) | async-done | bytes 524304 | tf_op jit(solution)/shard_map/reduce_scatter | solution.py:86
  (36 shorter events, 0.6 us)
Async XLA Ops:
  8.0 1.6 copy-start
  8.0 109.9 %all-reduce.2.cloned.1.call-start = ((), (), s32[]{:S(2)}) async-start(), calls=%async_computation.7 | async-start | bytes 1048576 | tf_op jit(solution)/shard_map/psum | solution.py:38
  13.2 5.5 copy-start.4
  13.2 5.7 %copy-start.5 = (s32[1,1,8]{2,1,0:T(1,128)S(1)}, s32[1,1,8]{2,1,0:T(1,128)}, u32[]{:S(2)}) copy-start(s32[1,1,8]{2,1,0:T(1,128)} %param.16) | copy-start | bytes 100
  13.2 6.0 %copy-start.1 = (f32[128]{0:T(128)S(1)}, f32[128]{0:T(128)}, u32[]{:S(2)}) copy-start(f32[128]{0:T(128)} %param.18) | copy-start | bytes 1540
  13.3 163.4 %all-gather.2.cloned.1.call-start = ((), (), s32[]{:S(2)}) async-start(), calls=%async_computation.6 | async-start | bytes 9437184 | tf_op jit(solution)/shard_map/all_gather | solution.py:81
  13.8 7.4 %copy-start.6 = (f32[1,1,8]{2,1,0:T(1,128)S(1)}, f32[1,1,8]{2,1,0:T(1,128)}, u32[]{:S(2)}) copy-start(f32[1,1,8]{2,1,0:T(1,128)} %param.17) | copy-start | bytes 100
  13.9 70.1 %all-to-all-start = ((bf16[4,128,2048]{2,1,0:T(8,128)(2,1)}), bf16[4,128,2048]{2,1,0:T(8,128)(2,1)}, u32[]{:S(2)}, u32[]{:S(2)}) async-start(bf16[4,128,2048]{2,1,0:T(8,128)(2,1)} %bitcast.38), calls=%async_computation | async-start | bytes 4194304 | tf_op jit(solution)/shard_map/all_to_all | solution.py:40
  84.0 18.3 %all-to-all-start.2 = ((bf16[8,1,32]{2,1,0:T(2,128)(2,1)}), bf16[8,1,32]{2,1,0:T(2,128)(2,1)S(1)}, u32[]{:S(2)}, u32[]{:S(2)}) async-start(bf16[8,1,32]{2,1,0:T(2,128)(2,1)} %fusion.13), calls=%async_computation.2 | async-start | bytes 8192 | tf_op jit(solution)/shard_map/all_to_all | solution.py:65
  102.3 8.7 %all-to-all-start.3 = ((bf16[8,1,32]{2,1,0:T(2,128)(2,1)}), bf16[8,1,32]{2,1,0:T(2,128)(2,1)S(1)}, u32[]{:S(2)}, u32[]{:S(2)}) async-start(bf16[8,1,32]{2,1,0:T(2,128)(2,1)} %fusion.12), calls=%async_computation.3 | async-start | bytes 8192 | tf_op jit(solution)/shard_map/all_to_all | solution.py:66
  111.0 52.3 %all-to-all-start.1 = ((bf16[8,32,8192]{2,1,0:T(8,128)(2,1)}), bf16[8,32,8192]{2,1,0:T(8,128)(2,1)}, u32[]{:S(2)}, u32[]{:S(2)}) async-start(bf16[8,32,8192]{2,1,0:T(8,128)(2,1)} %broadcast_select_fusion), calls=%async_computation.1 | async-start | bytes 8388608 | tf_op jit(solution)/shard_map/all_to_all | solution.py:63
  117.8 53.5 %copy-start.3 = (f32[8192]{0:T(1024)S(1)}, f32[8192]{0:T(1024)}, u32[]{:S(2)}) copy-start(f32[8192]{0:T(1024)} %param.13) | copy-start | bytes 98308
  163.3 20.3 %all-to-all-start.4 = ((bf16[8,32,512]{2,1,0:T(8,128)(2,1)}), bf16[8,32,512]{2,1,0:T(8,128)(2,1)S(1)}, u32[]{:S(2)}, u32[]{:S(2)}) async-start(bf16[8,32,512]{2,1,0:T(8,128)(2,1)} %broadcast_select_fusion.1), calls=%async_computation.4 | async-start | bytes 524288 | tf_op jit(solution)/shard_map/all_to_all | solution.py:64
  168.1 388.4 %reduce-scatter.2.cloned.1.call-start = ((), (), s32[]{:S(2)}) async-start(), calls=%async_computation.8 | async-start | bytes 17301504 | tf_op jit(solution)/shard_map/reduce_scatter | solution.py:86
  176.6 7.0 %copy-start.2 = (bf16[1,1,256,512]{3,2,1,0:T(8,128)(2,1)S(1)}, bf16[1,1,256,512]{3,2,1,0:T(8,128)(2,1)}, u32[]{:S(2)}) copy-start(bf16[1,1,256,512]{3,2,1,0:T(8,128)(2,1)} %param.19) | copy-start | bytes 786436
Sparse Core Ops, SparseCore 0:
  13.4 70.9 all-reduce.1
  194.2 362.2 reduce-scatter.1
Sparse Core Ops, SparseCore 1:
  15.6 55.0 all-gather.1
where the time goes:
time: 567 us; the launch traced here: 564 us
  waiting for transfers between devices  466 us (82%)
  starting transfers between devices  22.8 us (4%)
  matrix products  21 us (4%)
  other arithmetic  19.5 us (3%)
  local copies, waits for them, and re-layouts  19 us (3%)
  between operations  15.6 us (3%)
    reduce_scatter x1, waiting for transfers between devices, on_device(): lax.psum_scatter(lax.dot_general(feature_block, slope, (((0,), (0,)), (()...  362 us
    all_to_all x1, waiting for transfers between devices, on_device(): lax.all_to_all(tokens, 'tensor', split_axis=0, concat_axis=1, tiled=True)  61.2 us
    all_to_all x1, waiting for transfers between devices, on_device(): lax.all_to_all(send_rows, 'dp', split_axis=0, concat_axis=0, tiled=True)  42.5 us
  transfers between devices with their start and end apart: 8, of which 3 were waited for; matrix products, arithmetic and copies ran while one was open for 8% of the time, Pallas kernels for 0%

commit v1 on v0

v1 whole, which is shorter than its diff:
```python
import math

import jax
import jax.numpy as jnp
from jax import lax
from jax.sharding import PartitionSpec as P

EPS = 1e-06
BETA = 1.0
AXES = ("dp", "tensor")
BF16 = jnp.bfloat16
F32 = jnp.float32


def take_chunk(array, index, rows):
    return lax.dynamic_slice_in_dim(array, index * rows, rows, 0)


def sum_over_tensor(partial, rows, count):
    me = lax.axis_index("tensor")
    terms = [take_chunk(partial, me, rows)]
    for step in range(1, count):
        pairs = [(i, (i + step) % count) for i in range(count)]
        terms.append(
            lax.ppermute(take_chunk(partial, (me + step) % count, rows), "tensor", pairs)
        )
    return terms


def on_device(
    tokens,
    ref_gain,
    ref_weight,
    pol_gain,
    pol_weight,
    lengths,
    bins,
    advantage,
    logprob_gap,
    cotangent,
):
    tensor_count = lax.axis_size("tensor")
    dp_count = lax.axis_size("dp")
    t = lax.axis_index("tensor")
    d = lax.axis_index("dp")
    cores = dp_count // tensor_count
    assert cores == 2
    places = dp_count // cores
    levels = places.bit_length() - 1
    assert 1 << levels == places
    place = d // cores
    core = d % cores
    group_rows, block = tokens.shape
    own_rows = group_rows // tensor_count
    slot_count = cotangent.shape[2]
    span_rows = slot_count // dp_count
    value_width = ref_weight.shape[1]
    model_width = pol_gain.shape[0]
    shard = pol_weight.shape[0]
    factor = 1.0 / math.sqrt(dp_count * tensor_count * lengths.shape[2])

    def flat(p, c, z):
        return (p * cores + c) * tensor_count + z

    got_cot = lax.all_to_all(
        cotangent.reshape(slot_count, value_width), "dp", split_axis=0, concat_axis=0, tiled=True
    )

    relative = place ^ t
    piece_count = 2
    piece_rows = shard // piece_count
    pieces = []
    for piece in range(piece_count):
        held = pol_weight[piece * piece_rows : (piece + 1) * piece_rows]
        holders = [0]
        for stage in range(levels):
            bit = 1 << ((piece + stage) % levels)
            pairs = [
                (flat(q ^ z, c, z), flat(q ^ bit ^ z, c, z))
                for q in holders
                for c in range(cores)
                for z in range(tensor_count)
            ]
            got = lax.ppermute(held, AXES, pairs)
            getters = [q ^ bit for q in holders]
            is_getter = jnp.zeros((), jnp.bool_)
            for q in getters:
                is_getter = is_getter | (relative == q)
            held = jnp.where(is_getter, got, held)
            holders = holders + getters
        pieces.append(held)
    mine = jnp.concatenate(pieces, axis=0)
    swap = [(i, i ^ 1) for i in range(dp_count)]
    other = lax.ppermute(mine, "dp", swap)
    weight = jnp.where(
        core == 0,
        jnp.concatenate([mine, other], axis=0),
        jnp.concatenate([other, mine], axis=0),
    )

    tokens_f32 = tokens.astype(F32)
    scaled = (tokens_f32 * ref_gain[None, :]).astype(BF16)
    ref_part = jnp.dot(scaled, ref_weight, preferred_element_type=F32).astype(BF16)
    square = jnp.sum(jnp.square(tokens_f32), axis=1)
    square_sum = sum(sum_over_tensor(square, own_rows, tensor_count))
    row_scale = lax.rsqrt(square_sum / model_width + EPS)[:, None]
    ref_sum = sum(x.astype(F32) for x in sum_over_tensor(ref_part, own_rows, tensor_count))
    ref_values = (ref_sum * row_scale).astype(BF16).astype(F32)

    seq_lens = lengths.reshape(-1)
    seq_bins = bins.reshape(-1)
    seq_adv = advantage.reshape(-1)
    seq_starts = jnp.cumsum(seq_lens) - seq_lens
    row = jnp.arange(own_rows, dtype=jnp.int32)
    in_seq = (row[:, None] >= seq_starts[None, :]) & (
        row[:, None] < (seq_starts + seq_lens)[None, :]
    )
    row_slot = jnp.sum(
        jnp.where(in_seq, seq_bins * span_rows + row[:, None] - seq_starts[None, :], 0), axis=1
    )
    row_len = jnp.sum(jnp.where(in_seq, seq_lens[None, :], 0), axis=1).astype(F32)
    row_adv = jnp.sum(jnp.where(in_seq, seq_adv[None, :], 0.0), axis=1)
    importance = jnp.minimum(jnp.exp(logprob_gap), jnp.float32(2.0))
    coef_adv = (row_adv * importance / row_len).astype(BF16).astype(F32)[:, None]
    coef_pull = (BETA / row_len).astype(BF16).astype(F32)[:, None]
    slot = jnp.arange(slot_count, dtype=jnp.int32)
    row_at = (row_slot[:, None] == slot[None, :]).astype(BF16)
    slot_at = (slot[:, None] == row_slot[None, :]).astype(BF16)
    upstream = jnp.dot(row_at, got_cot, preferred_element_type=F32)

    pol_gain_block = lax.dynamic_slice_in_dim(pol_gain, t * block, block, 0)
    pol_scaled = (tokens_f32 * pol_gain_block[None, :]).astype(BF16)
    value_part = jnp.dot(pol_scaled, weight, preferred_element_type=F32).astype(BF16)
    value_sum = sum(x.astype(F32) for x in sum_over_tensor(value_part, own_rows, tensor_count))
    values = value_sum * row_scale
    sent = jnp.dot(slot_at, values.astype(BF16), preferred_element_type=F32).astype(BF16)
    policy_values = lax.all_to_all(sent, "dp", split_axis=0, concat_axis=0, tiled=True)

    slope = coef_adv * upstream + coef_pull * (values - ref_values)
    slope = (slope * row_scale).astype(BF16)
    slopes = jnp.zeros((group_rows, value_width), BF16)
    slopes = lax.dynamic_update_slice_in_dim(slopes, slope, t * own_rows, 0)
    for step in range(1, tensor_count):
        pairs = [(i, (i + step) % tensor_count) for i in range(tensor_count)]
        got = lax.ppermute(slope, "tensor", pairs)
        source = (t - step) % tensor_count
        slopes = lax.dynamic_update_slice_in_dim(slopes, got, source * own_rows, 0)

    grad = lax.dot_general(tokens, slopes, (((0,), (0,)), ((), ())), preferred_element_type=F32)
    grad = (grad * (pol_gain_block * factor)[:, None]).astype(BF16)
    kept = take_chunk(grad, core, shard)
    given = take_chunk(grad, 1 - core, shard)
    half = (kept.astype(F32) + lax.ppermute(given, "dp", swap).astype(F32)).astype(BF16)
    out_rows = shard // tensor_count
    total = take_chunk(half, place, out_rows).astype(F32)
    for step in range(1, places):
        pairs = [
            (p * cores + c, (p ^ step) * cores + c) for p in range(places) for c in range(cores)
        ]
        total = total + lax.ppermute(
            take_chunk(half, place ^ step, out_rows), "dp", pairs
        ).astype(F32)
    pairs = [
        (flat(p, c, z), flat(z, c, p))
        for p in range(places)
        for c in range(cores)
        for z in range(tensor_count)
    ]
    grad_weight = lax.ppermute(total.astype(BF16), AXES, pairs).astype(F32)
    return (policy_values.reshape(1, 1, slot_count, value_width), grad_weight)


def solution(mesh):
    in_specs = (
        P("dp", "tensor"),
        P("tensor"),
        P("tensor", None),
        P(),
        P("dp", None),
        P("dp", "tensor", None),
        P("dp", "tensor", None),
        P("dp", "tensor", None),
        P(("dp", "tensor")),
        P("dp", "tensor", None, None),
    )
    out_specs = (P("dp", "tensor", None, None), P(("dp", "tensor"), None))
    return jax.shard_map(
        on_device, mesh=mesh, in_specs=in_specs, out_specs=out_specs, check_vma=False
    )
```

time: 567 us -> 144 us (0.25)
  the two profiles are of different devices: /device:TPU:4 before, /device:TPU:2 now
where the time goes in v1:
time: 144 us
  waiting for transfers between devices  58.8 us (41%)
  starting transfers between devices  40.2 us (28%)
  matrix products  12.3 us (9%)
  other arithmetic  10.9 us (8%)
  blocking collectives  10.6 us (7%)
  local copies, waits for them, and re-layouts  9.9 us (7%)
    ppermute x4, waiting for transfers between devices, on_device(): got = lax.ppermute(held, AXES, pairs)  18.5 us
    ppermute x9, starting transfers between devices, sum_over_tensor(): lax.ppermute(take_chunk(partial, (me + step) % count, rows), 'tensor', pa...  18 us
    ppermute x3, waiting for transfers between devices, on_device(): lax.ppermute(take_chunk(half, place ^ step, out_rows), 'dp', pairs)  11.8 us
    ppermute x9, waiting for transfers between devices, sum_over_tensor(): lax.ppermute(take_chunk(partial, (me + step) % count, rows), 'tensor', pa...  10.8 us
    all_to_all x1, blocking collectives, on_device(): lax.all_to_all(sent, 'dp', split_axis=0, concat_axis=0, tiled=True)  10.6 us
    ppermute x3, waiting for transfers between devices, on_device(): got = lax.ppermute(slope, 'tensor', pairs)  8.99 us
    ppermute x4, starting transfers between devices, on_device(): got = lax.ppermute(held, AXES, pairs)  6.64 us
    ppermute x1, waiting for transfers between devices, on_device(): grad_weight = lax.ppermute(total.astype(BF16), AXES, pairs).astype(F32)  5.97 us
  transfers between devices with their start and end apart: 23, of which 13 were waited for; matrix products, arithmetic and copies ran while one was open for 10% of the time, Pallas kernels for 0%

profile of v1, /device:TPU:2, one launch (start us, length us, event | category | flops | bytes accessed | tf_op | source)
XLA Modules:
  0.0 143.7 jit_solution(14504104279378399151)
XLA Ops:
  0.7 2.4 %fusion.31 = (bf16[512,512]{1,0:T(8,128)(2,1)}, bf16[512,512]{1,0:T(8,128)(2,1)}) fusion(bf16[1024,512]{1,0:T(8,128)(2,1)} %param.14), kind=kLoop, calls=%fused_computation.70 | loop fusion | bytes 2097152 | tf_op jit(solution)/shard_map/slice | solution.py:74
  3.0 1.3 collective-permute-start
  4.3 1.5 %collective-permute-start.2 = (bf16[512,512]{1,0:T(8,128)(2,1)}, bf16[512,512]{1,0:T(8,128)(2,1)}, u32[]{:S(2)}, u32[]{:S(2)}) collective-permute-start(bf16[512,512]{1,0:T(8,128)(2,1)} %get-tuple-element.16), channel_id=1, source_target_pairs={{0,16},{9,25},{18,2},{27,11},{4,20},{13,29},{22,6},{31,15}} | collective-permute-start | bytes 1572872 | tf_op jit(solution)/shard_map/ppermute | solution.py:84
  5.8 13.1 %collective-permute-done = bf16[512,512]{1,0:T(8,128)(2,1)} collective-permute-done((bf16[512,512]{1,0:T(8,128)(2,1)}, bf16[512,512]{1,0:T(8,128)(2,1)}, u32[]{:S(2)}, u32[]{:S(2)}) %collective-permute-start) | collective-permute-done | bytes 524320 | tf_op jit(solution)/shard_map/ppermute | solution.py:84
  18.9 2.1 %broadcast_select_fusion.2 = (bf16[512,512]{1,0:T(8,128)(2,1)}, bf16[512,512]{1,0:T(8,128)(2,1)}) fusion(bf16[512,512]{1,0:T(8,128)(2,1)} %collective-permute-done, pred[]{:T(512)S(6)} %eq.61, bf16[1024,512]{1,0:T(8,128)(2,1)S(1)} %copy-done.1, bf16[512,512]{1,0:T(8,128)(2,1)} %collective-permute-done.2, pred[]{:T(512)S(6)} %eq.59), kind=kLoop, calls=%fused_computation.33 | loop fusion | flops 524288 | bytes 3145730 | tf_op jit(solution)/shard_map/jit(_where)/select_n | solution.py:89
  21.0 1.4 collective-permute-start.3
  23.6 6.5 %collective-permute-start.10 = (f32[128]{0:T(128)S(1)}, f32[128]{0:T(128)S(1)}, u32[]{:S(2)}, u32[]{:S(2)}) collective-permute-start(f32[128]{0:T(128)S(1)} %get-tuple-element.24), channel_id=1, source_target_pairs={{0,3},{1,0},{2,1},{3,2},{4,7},{5,4},{6,5},{7,6},{8,11},{9,8},{10,9... | collective-permute-start | bytes 1544 | tf_op jit(solution)/shard_map/ppermute | solution.py:25
  30.7 2.5 %collective-permute-start.1 = (bf16[512,512]{1,0:T(8,128)(2,1)S(1)}, bf16[512,512]{1,0:T(8,128)(2,1)S(1)}, u32[]{:S(2)}, u32[]{:S(2)}) collective-permute-start(bf16[512,512]{1,0:T(8,128)(2,1)S(1)} %copy-done.4), channel_id=1, source_target_pairs={{0,16},{9,25},{18,2},{27,11},{4,20},{13,29},{22,6},{31,15},{8,24},... | collective-permute-start | bytes 1572872 | tf_op jit(solution)/shard_map/ppermute | solution.py:84
  33.2 2.8 %fusion.23 = bf16[512,512]{1,0:T(8,128)(2,1)S(1)} fusion(bf16[2048,512]{1,0:T(8,128)(2,1)S(1)} %copy-done, bf16[512,2048]{1,0:T(8,128)(2,1)} %param.10, f32[2048]{0:T(1024)S(1)} %copy-done.17), kind=kOutput, calls=%fused_computation.25 | convolution fusion | flops 1077149696 | bytes 4726784 | tf_op jit(solution)/shard_map/dot_general | solution.py:103
  37.3 5.2 %collective-permute-done.1 = bf16[512,512]{1,0:T(8,128)(2,1)S(1)} collective-permute-done((bf16[512,512]{1,0:T(8,128)(2,1)S(1)}, bf16[512,512]{1,0:T(8,128)(2,1)S(1)}, u32[]{:S(2)}, u32[]{:S(2)}) %collective-permute-start.1) | collective-permute-done | bytes 524320 | tf_op jit(solution)/shard_map/ppermute | solution.py:84
  44.5 5.5 %collective-permute-start.13 = (bf16[128,512]{1,0:T(8,128)(2,1)S(1)}, bf16[128,512]{1,0:T(8,128)(2,1)}, u32[]{:S(2)}, u32[]{:S(2)}) collective-permute-start(bf16[128,512]{1,0:T(8,128)(2,1)S(1)} %get-tuple-element.18), channel_id=1, source_target_pairs={{0,3},{1,0},{2,1},{3,2},{4,7},{5,4},{6,5},{7,6},{8,11},{9,8},{10,9... | collective-permute-start | bytes 393224 | tf_op jit(solution)/shard_map/ppermute | solution.py:25
  50.0 3.8 %all-to-all-start.1 = ((bf16[8,32,512]{2,1,0:T(8,128)(2,1)}), bf16[8,32,512]{2,1,0:T(8,128)(2,1)S(1)}, u32[]{:S(2)}, u32[]{:S(2)}) async-start(bf16[8,32,512]{2,1,0:T(8,128)(2,1)} %bitcast.7), calls=%async_computation.1 | async-start | bytes 524288 | tf_op jit(solution)/shard_map/all_to_all | solution.py:65
  55.5 3.8 %fusion.20 = bf16[512,512]{1,0:T(8,128)(2,1)S(1)} fusion(bf16[1024,512]{1,0:T(8,128)(2,1)} %collective-permute-done.4, bf16[512,512]{1,0:T(8,128)(2,1)S(1)} %broadcast_select_fusion.1, bf16[512,512]{1,0:T(8,128)(2,1)} %copy-done.5, pred[]{:T(512)S(6)} %eq.58, bf16[512,2048]{1,0:T(8,128)(2,1)} %param.10, f32[2048]{0:T(1024)S(1)} %get-tuple-element.9), kind=kOutput, calls=%fused_computation.24 | convolution fusion | flops 1090781184 | bytes 4726785 | tf_op jit(solution)/shard_map/dot_general | solution.py:133
  61.4 3.2 %collective-permute-start.7 = (bf16[128,512]{1,0:T(8,128)(2,1)S(1)}, bf16[128,512]{1,0:T(8,128)(2,1)S(1)}, u32[]{:S(2)}, u32[]{:S(2)}) collective-permute-start(bf16[128,512]{1,0:T(8,128)(2,1)S(1)} %get-tuple-element.21), channel_id=1, source_target_pairs={{0,3},{1,0},{2,1},{3,2},{4,7},{5,4},{6,5},{7,6},{8,11},{9,8},{10,9... | collective-permute-start | bytes 393224 | tf_op jit(solution)/shard_map/ppermute | solution.py:25
  68.5 1.8 %collective-permute-done.7 = bf16[128,512]{1,0:T(8,128)(2,1)S(1)} collective-permute-done((bf16[128,512]{1,0:T(8,128)(2,1)S(1)}, bf16[128,512]{1,0:T(8,128)(2,1)S(1)}, u32[]{:S(2)}, u32[]{:S(2)}) %collective-permute-start.7) | collective-permute-done | bytes 131104 | tf_op jit(solution)/shard_map/ppermute | solution.py:25
  70.2 8.6 %collective-permute-done.6 = bf16[128,512]{1,0:T(8,128)(2,1)S(1)} collective-permute-done((bf16[128,512]{1,0:T(8,128)(2,1)S(1)}, bf16[128,512]{1,0:T(8,128)(2,1)S(1)}, u32[]{:S(2)}, u32[]{:S(2)}) %collective-permute-start.6) | collective-permute-done | bytes 131104 | tf_op jit(solution)/shard_map/ppermute | solution.py:25
  78.8 1.5 %constant_dynamic-update-slice_fusion.3 = (bf16[512,512]{1,0:T(8,128)(2,1)S(1)}, bf16[128,512]{1,0:T(8,128)(2,1)S(1)}) fusion(bf16[512,512]{1,0:T(8,128)(2,1)S(1)} %broadcast_in_dim.31, s32[]{:T(128)S(6)} %select_n.158, bf16[128,512]{1,0:T(8,128)(2,1)} %collective-permute-done.13, bf16[128,512]{1,0:T(8,128)(2,1)} %copy-done.16, ...), kind=kOutput, calls=%fused_computation.49 | convolution fusion | flops 35160064 | bytes 1574916 | tf_op jit(solution)/shard_map/dot_general | solution.py:129
  81.3 3.0 %collective-permute-start.16 = (bf16[128,512]{1,0:T(8,128)(2,1)S(1)}, bf16[128,512]{1,0:T(8,128)(2,1)S(1)}, u32[]{:S(2)}, u32[]{:S(2)}) collective-permute-start(bf16[128,512]{1,0:T(8,128)(2,1)S(1)} %get-tuple-element.29), channel_id=1, source_target_pairs={{0,3},{1,0},{2,1},{3,2},{4,7},{5,4},{6,5},{7,6},{8,11},{9,8},{10,9... | collective-permute-start | bytes 393224 | tf_op jit(solution)/shard_map/ppermute | solution.py:145
  84.2 4.4 %collective-permute-done.14 = bf16[128,512]{1,0:T(8,128)(2,1)S(1)} collective-permute-done((bf16[128,512]{1,0:T(8,128)(2,1)S(1)}, bf16[128,512]{1,0:T(8,128)(2,1)S(1)}, u32[]{:S(2)}, u32[]{:S(2)}) %collective-permute-start.14) | collective-permute-done | bytes 131104 | tf_op jit(solution)/shard_map/ppermute | solution.py:145
  88.7 4.6 %collective-permute-done.15 = bf16[128,512]{1,0:T(8,128)(2,1)S(1)} collective-permute-done((bf16[128,512]{1,0:T(8,128)(2,1)S(1)}, bf16[128,512]{1,0:T(8,128)(2,1)S(1)}, u32[]{:S(2)}, u32[]{:S(2)}) %collective-permute-start.15) | collective-permute-done | bytes 131104 | tf_op jit(solution)/shard_map/ppermute | solution.py:145
  93.3 2.9 %multiply_convert_fusion = bf16[512,2048]{1,0:T(8,128)(2,1)S(1)} fusion(bf16[512,512]{1,0:T(8,128)(2,1)S(1)} %constant_dynamic-update-slice_fusion, bf16[512,2048]{1,0:T(8,128)(2,1)} %param.10, f32[2048]{0:T(1024)S(1)} %get-tuple-element.8), kind=kOutput, calls=%fused_computation.6 | convolution fusion | flops 1075838976 | bytes 4726784 | tf_op jit(solution)/shard_map/dot_general | solution.py:149
  96.2 1.4 copy-done.3
  97.7 2.7 %collective-permute-done.17 = bf16[1024,512]{0,1:T(8,128)(2,1)} collective-permute-done((bf16[1024,512]{0,1:T(8,128)(2,1)S(1)}, bf16[1024,512]{0,1:T(8,128)(2,1)}, u32[]{:S(2)}, u32[]{:S(2)}) %collective-permute-start.17) | collective-permute-done | bytes 1048608 | tf_op jit(solution)/shard_map/ppermute | solution.py:153
  100.5 1.9 %fusion.16 = bf16[1024,512]{0,1:T(8,128)(2,1)S(1)} fusion(bf16[1024,512]{0,1:T(8,128)(2,1)} %collective-permute-done.17, bf16[512,2048]{1,0:T(8,128)(2,1)} %copy-done.3, s32[]{:T(128)S(6)} %select_n.173), kind=kLoop, calls=%fused_computation.20 | loop fusion | flops 2097152 | bytes 3145732 | tf_op jit(solution)/shard_map/convert_element_type | solution.py:153
  103.3 1.5 %collective-permute-start.20 = (bf16[256,512]{0,1:T(8,128)(2,1)}, bf16[256,512]{0,1:T(8,128)(2,1)}, u32[]{:S(2)}, u32[]{:S(2)}) collective-permute-start(bf16[256,512]{0,1:T(8,128)(2,1)} %get-tuple-element.11), channel_id=1, source_target_pairs={{0,24},{4,28},{8,16},{12,20},{16,8},{20,12},{24,0},{28,4},{1,25},{... | collective-permute-start | bytes 786440 | tf_op jit(solution)/shard_map/ppermute | solution.py:160
  105.3 1.6 %collective-permute-start.18 = (bf16[256,512]{0,1:T(8,128)(2,1)S(1)}, bf16[256,512]{0,1:T(8,128)(2,1)}, u32[]{:S(2)}, u32[]{:S(2)}) collective-permute-start(bf16[256,512]{0,1:T(8,128)(2,1)S(1)} %get-tuple-element.10), channel_id=1, source_target_pairs={{0,8},{4,12},{8,0},{12,4},{16,24},{20,28},{24,16},{28,20},{1,9},{5... | collective-permute-start | bytes 786440 | tf_op jit(solution)/shard_map/ppermute | solution.py:160
  106.8 6.9 %collective-permute-done.20 = bf16[256,512]{0,1:T(8,128)(2,1)} collective-permute-done((bf16[256,512]{0,1:T(8,128)(2,1)}, bf16[256,512]{0,1:T(8,128)(2,1)}, u32[]{:S(2)}, u32[]{:S(2)}) %collective-permute-start.20) | collective-permute-done | bytes 262176 | tf_op jit(solution)/shard_map/ppermute | solution.py:160
  113.7 4.8 %collective-permute-done.19 = bf16[256,512]{0,1:T(8,128)(2,1)} collective-permute-done((bf16[256,512]{0,1:T(8,128)(2,1)}, bf16[256,512]{0,1:T(8,128)(2,1)}, u32[]{:S(2)}, u32[]{:S(2)}) %collective-permute-start.19) | collective-permute-done | bytes 262176 | tf_op jit(solution)/shard_map/ppermute | solution.py:160
  119.8 4.3 %collective-permute-start.21 = (bf16[256,512]{0,1:T(8,128)(2,1)S(1)}, bf16[256,512]{0,1:T(8,128)(2,1)S(1)}, u32[]{:S(2)}, u32[]{:S(2)}) collective-permute-start(bf16[256,512]{0,1:T(8,128)(2,1)S(1)} %add_convert_fusion), channel_id=1, source_target_pairs={{0,0},{1,8},{2,16},{3,24},{4,4},{5,12},{6,20},{7,28},{8,1},{9,9},{... | collective-permute-start | bytes 786440 | tf_op jit(solution)/shard_map/ppermute | solution.py:169
  124.2 1.3 convolution_convert_fusion
  125.5 10.6 %all_to_all.21 = bf16[8,32,512]{2,1,0:T(8,128)(2,1)S(1)} all-to-all(bf16[8,32,512]{2,1,0:T(8,128)(2,1)S(1)} %bitcast.22), channel_id=1, replica_groups=mesh['dp'=8,'tensor'=4] {'dp'}, dimensions={0} | all-to-all | bytes 524288 | tf_op jit(solution)/shard_map/all_to_all | solution.py:137
  136.0 6.0 %collective-permute-done.21 = bf16[256,512]{0,1:T(8,128)(2,1)S(1)} collective-permute-done((bf16[256,512]{0,1:T(8,128)(2,1)S(1)}, bf16[256,512]{0,1:T(8,128)(2,1)S(1)}, u32[]{:S(2)}, u32[]{:S(2)}) %collective-permute-start.21) | collective-permute-done | bytes 262176 | tf_op jit(solution)/shard_map/ppermute | solution.py:169
  (85 shorter events, 17.9 us)
Async XLA Ops:
  0.6 32.5 %copy-start = (bf16[2048,512]{1,0:T(8,128)(2,1)S(1)}, bf16[2048,512]{1,0:T(8,128)(2,1)}, u32[]{:S(2)}) copy-start(bf16[2048,512]{1,0:T(8,128)(2,1)} %param.12) | copy-start | bytes 6291460
  0.6 18.3 %copy-start.1 = (bf16[1024,512]{1,0:T(8,128)(2,1)S(1)}, bf16[1024,512]{1,0:T(8,128)(2,1)}, u32[]{:S(2)}) copy-start(bf16[1024,512]{1,0:T(8,128)(2,1)} %param.14) | copy-start | bytes 3145732
  3.0 15.9 %collective-permute-start = (bf16[512,512]{1,0:T(8,128)(2,1)}, bf16[512,512]{1,0:T(8,128)(2,1)}, u32[]{:S(2)}, u32[]{:S(2)}) collective-permute-start(bf16[512,512]{1,0:T(8,128)(2,1)} %get-tuple-element.15), channel_id=1, source_target_pairs={{0,8},{9,1},{18,26},{27,19},{4,12},{13,5},{22,30},{31,23}} | collective-permute-start | bytes 1572872 | tf_op jit(solution)/shard_map/ppermute | solution.py:84
  4.3 14.6 %collective-permute-start.2 = (bf16[512,512]{1,0:T(8,128)(2,1)}, bf16[512,512]{1,0:T(8,128)(2,1)}, u32[]{:S(2)}, u32[]{:S(2)}) collective-permute-start(bf16[512,512]{1,0:T(8,128)(2,1)} %get-tuple-element.16), channel_id=1, source_target_pairs={{0,16},{9,25},{18,2},{27,11},{4,20},{13,29},{22,6},{31,15}} | collective-permute-start | bytes 1572872 | tf_op jit(solution)/shard_map/ppermute | solution.py:84
  5.8 16.7 %copy-start.2 = (bf16[512,2048]{1,0:T(8,128)(2,1)S(1)}, bf16[512,2048]{1,0:T(8,128)(2,1)}, u32[]{:S(2)}) copy-start(bf16[512,2048]{1,0:T(8,128)(2,1)} %param.10) | copy-start | bytes 6291460
  5.8 27.4 %copy-start.17 = (f32[2048]{0:T(1024)S(1)}, f32[2048]{0:T(1024)}, u32[]{:S(2)}) copy-start(f32[2048]{0:T(1024)} %param.11) | copy-start | bytes 24580
  21.0 15.1 %collective-permute-start.3 = (bf16[512,512]{1,0:T(8,128)(2,1)}, bf16[512,512]{1,0:T(8,128)(2,1)}, u32[]{:S(2)}, u32[]{:S(2)}) collective-permute-start(bf16[512,512]{1,0:T(8,128)(2,1)} %get-tuple-element.14), channel_id=1, source_target_pairs={{0,8},{9,1},{18,26},{27,19},{4,12},{13,5},{22,30},{31,23},{16,24},... | collective-permute-start | bytes 1572872 | tf_op jit(solution)/shard_map/ppermute | solution.py:84
  23.6 36.5 %collective-permute-start.10 = (f32[128]{0:T(128)S(1)}, f32[128]{0:T(128)S(1)}, u32[]{:S(2)}, u32[]{:S(2)}) collective-permute-start(f32[128]{0:T(128)S(1)} %get-tuple-element.24), channel_id=1, source_target_pairs={{0,3},{1,0},{2,1},{3,2},{4,7},{5,4},{6,5},{7,6},{8,11},{9,8},{10,9... | collective-permute-start | bytes 1544 | tf_op jit(solution)/shard_map/ppermute | solution.py:25
  30.1 30.8 %collective-permute-start.9 = (f32[128]{0:T(128)S(1)}, f32[128]{0:T(128)S(1)}, u32[]{:S(2)}, u32[]{:S(2)}) collective-permute-start(f32[128]{0:T(128)S(1)} %get-tuple-element.25), channel_id=1, source_target_pairs={{0,2},{1,3},{2,0},{3,1},{4,6},{5,7},{6,4},{7,5},{8,10},{9,11},{10,... | collective-permute-start | bytes 1544 | tf_op jit(solution)/shard_map/ppermute | solution.py:25
  30.1 34.5 %collective-permute-start.8 = (f32[128]{0:T(128)}, f32[128]{0:T(128)}, u32[]{:S(2)}, u32[]{:S(2)}) collective-permute-start(f32[128]{0:T(128)} %get-tuple-element.23), channel_id=1, source_target_pairs={{0,1},{1,2},{2,3},{3,0},{4,5},{5,6},{6,7},{7,4},{8,9},{9,10},{10,1... | collective-permute-start | bytes 1544 | tf_op jit(solution)/shard_map/ppermute | solution.py:25
  30.7 11.9 %collective-permute-start.1 = (bf16[512,512]{1,0:T(8,128)(2,1)S(1)}, bf16[512,512]{1,0:T(8,128)(2,1)S(1)}, u32[]{:S(2)}, u32[]{:S(2)}) collective-permute-start(bf16[512,512]{1,0:T(8,128)(2,1)S(1)} %copy-done.4), channel_id=1, source_target_pairs={{0,16},{9,25},{18,2},{27,11},{4,20},{13,29},{22,6},{31,15},{8,24},... | collective-permute-start | bytes 1572872 | tf_op jit(solution)/shard_map/ppermute | solution.py:84
  43.4 10.4 %copy-start.13 = (s32[1,1,8]{2,1,0:T(1,128)S(1)}, s32[1,1,8]{2,1,0:T(1,128)}, u32[]{:S(2)}) copy-start(s32[1,1,8]{2,1,0:T(1,128)} %param.15) | copy-start | bytes 100
  43.4 11.3 %copy-start.12 = (f32[1,1,8]{2,1,0:T(1,128)S(1)}, f32[1,1,8]{2,1,0:T(1,128)}, u32[]{:S(2)}) copy-start(f32[1,1,8]{2,1,0:T(1,128)} %param.17) | copy-start | bytes 100
  43.4 11.4 %copy-start.18 = (s32[1,1,8]{2,1,0:T(1,128)S(1)}, s32[1,1,8]{2,1,0:T(1,128)}, u32[]{:S(2)}) copy-start(s32[1,1,8]{2,1,0:T(1,128)} %param.16) | copy-start | bytes 100
  43.4 11.5 %copy-start.11 = (f32[128]{0:T(128)S(1)}, f32[128]{0:T(128)}, u32[]{:S(2)}) copy-start(f32[128]{0:T(128)} %param.18) | copy-start | bytes 1540
  44.5 10.9 %collective-permute-start.4 = (bf16[1024,512]{1,0:T(8,128)(2,1)}, bf16[1024,512]{1,0:T(8,128)(2,1)}, u32[]{:S(2)}, u32[]{:S(2)}) collective-permute-start(bf16[1024,512]{1,0:T(8,128)(2,1)} %pad_maximum_fusion), channel_id=1, source_target_pairs={{0,4},{4,0},{8,12},{12,8},{16,20},{20,16},{24,28},{28,24},{1,5},{5... | collective-permute-start | bytes 3145736 | tf_op jit(solution)/shard_map/ppermute | solution.py:94
  44.5 21.1 %collective-permute-start.13 = (bf16[128,512]{1,0:T(8,128)(2,1)S(1)}, bf16[128,512]{1,0:T(8,128)(2,1)}, u32[]{:S(2)}, u32[]{:S(2)}) collective-permute-start(bf16[128,512]{1,0:T(8,128)(2,1)S(1)} %get-tuple-element.18), channel_id=1, source_target_pairs={{0,3},{1,0},{2,1},{3,2},{4,7},{5,4},{6,5},{7,6},{8,11},{9,8},{10,9... | collective-permute-start | bytes 393224 | tf_op jit(solution)/shard_map/ppermute | solution.py:25
  50.0 18.4 %all-to-all-start.1 = ((bf16[8,32,512]{2,1,0:T(8,128)(2,1)}), bf16[8,32,512]{2,1,0:T(8,128)(2,1)S(1)}, u32[]{:S(2)}, u32[]{:S(2)}) async-start(bf16[8,32,512]{2,1,0:T(8,128)(2,1)} %bitcast.7), calls=%async_computation.1 | async-start | bytes 524288 | tf_op jit(solution)/shard_map/all_to_all | solution.py:65
  55.4 11.9 %collective-permute-start.12 = (bf16[128,512]{1,0:T(8,128)(2,1)S(1)}, bf16[128,512]{1,0:T(8,128)(2,1)S(1)}, u32[]{:S(2)}, u32[]{:S(2)}) collective-permute-start(bf16[128,512]{1,0:T(8,128)(2,1)S(1)} %get-tuple-element.19), channel_id=1, source_target_pairs={{0,2},{1,3},{2,0},{3,1},{4,6},{5,7},{6,4},{7,5},{8,10},{9,11},{10,... | collective-permute-start | bytes 393224 | tf_op jit(solution)/shard_map/ppermute | solution.py:25
  60.2 8.3 %collective-permute-start.11 = (bf16[128,512]{1,0:T(8,128)(2,1)S(1)}, bf16[128,512]{1,0:T(8,128)(2,1)}, u32[]{:S(2)}, u32[]{:S(2)}) collective-permute-start(bf16[128,512]{1,0:T(8,128)(2,1)S(1)} %get-tuple-element.17), channel_id=1, source_target_pairs={{0,1},{1,2},{2,3},{3,0},{4,5},{5,6},{6,7},{7,4},{8,9},{9,10},{10,1... | collective-permute-start | bytes 393224 | tf_op jit(solution)/shard_map/ppermute | solution.py:25
  61.4 8.8 %collective-permute-start.7 = (bf16[128,512]{1,0:T(8,128)(2,1)S(1)}, bf16[128,512]{1,0:T(8,128)(2,1)S(1)}, u32[]{:S(2)}, u32[]{:S(2)}) collective-permute-start(bf16[128,512]{1,0:T(8,128)(2,1)S(1)} %get-tuple-element.21), channel_id=1, source_target_pairs={{0,3},{1,0},{2,1},{3,2},{4,7},{5,4},{6,5},{7,6},{8,11},{9,8},{10,9... | collective-permute-start | bytes 393224 | tf_op jit(solution)/shard_map/ppermute | solution.py:25
  64.6 14.2 %collective-permute-start.6 = (bf16[128,512]{1,0:T(8,128)(2,1)S(1)}, bf16[128,512]{1,0:T(8,128)(2,1)S(1)}, u32[]{:S(2)}, u32[]{:S(2)}) collective-permute-start(bf16[128,512]{1,0:T(8,128)(2,1)S(1)} %get-tuple-element.22), channel_id=1, source_target_pairs={{0,2},{1,3},{2,0},{3,1},{4,6},{5,7},{6,4},{7,5},{8,10},{9,11},{10,... | collective-permute-start | bytes 393224 | tf_op jit(solution)/shard_map/ppermute | solution.py:25
  65.6 13.2 %collective-permute-start.5 = (bf16[128,512]{1,0:T(8,128)(2,1)S(1)}, bf16[128,512]{1,0:T(8,128)(2,1)S(1)}, u32[]{:S(2)}, u32[]{:S(2)}) collective-permute-start(bf16[128,512]{1,0:T(8,128)(2,1)S(1)} %get-tuple-element.20), channel_id=1, source_target_pairs={{0,1},{1,2},{2,3},{3,0},{4,5},{5,6},{6,7},{7,4},{8,9},{9,10},{10,1... | collective-permute-start | bytes 393224 | tf_op jit(solution)/shard_map/ppermute | solution.py:25
  80.4 8.3 %collective-permute-start.14 = (bf16[128,512]{1,0:T(8,128)(2,1)S(1)}, bf16[128,512]{1,0:T(8,128)(2,1)S(1)}, u32[]{:S(2)}, u32[]{:S(2)}) collective-permute-start(bf16[128,512]{1,0:T(8,128)(2,1)S(1)} %get-tuple-element.29), channel_id=1, source_target_pairs={{0,1},{1,2},{2,3},{3,0},{4,5},{5,6},{6,7},{7,4},{8,9},{9,10},{10,1... | collective-permute-start | bytes 393224 | tf_op jit(solution)/shard_map/ppermute | solution.py:145
  80.4 12.8 %collective-permute-start.15 = (bf16[128,512]{1,0:T(8,128)(2,1)S(1)}, bf16[128,512]{1,0:T(8,128)(2,1)S(1)}, u32[]{:S(2)}, u32[]{:S(2)}) collective-permute-start(bf16[128,512]{1,0:T(8,128)(2,1)S(1)} %get-tuple-element.29), channel_id=1, source_target_pairs={{0,2},{1,3},{2,0},{3,1},{4,6},{5,7},{6,4},{7,5},{8,10},{9,11},{10,... | collective-permute-start | bytes 393224 | tf_op jit(solution)/shard_map/ppermute | solution.py:145
  81.3 12.0 %collective-permute-start.16 = (bf16[128,512]{1,0:T(8,128)(2,1)S(1)}, bf16[128,512]{1,0:T(8,128)(2,1)S(1)}, u32[]{:S(2)}, u32[]{:S(2)}) collective-permute-start(bf16[128,512]{1,0:T(8,128)(2,1)S(1)} %get-tuple-element.29), channel_id=1, source_target_pairs={{0,3},{1,0},{2,1},{3,2},{4,7},{5,4},{6,5},{7,6},{8,11},{9,8},{10,9... | collective-permute-start | bytes 393224 | tf_op jit(solution)/shard_map/ppermute | solution.py:145
  97.6 2.9 %collective-permute-start.17 = (bf16[1024,512]{0,1:T(8,128)(2,1)S(1)}, bf16[1024,512]{0,1:T(8,128)(2,1)}, u32[]{:S(2)}, u32[]{:S(2)}) collective-permute-start(bf16[1024,512]{0,1:T(8,128)(2,1)S(1)} %dynamic-slice_bitcast_fusion), channel_id=1, source_target_pairs={{0,4},{4,0},{8,12},{12,8},{16,20},{20,16},{24,28},{28,24},{1,5},{5... | collective-permute-start | bytes 3145736 | tf_op jit(solution)/shard_map/ppermute | solution.py:153
  102.4 21.7 %copy-start.10 = (f32[128]{0:T(128)S(1)}, f32[128]{0:T(128)}, u32[]{:S(2)}) copy-start(f32[128]{0:T(128)} %add_rsqrt_fusion) | copy-start | bytes 1540
  103.3 10.4 %collective-permute-start.20 = (bf16[256,512]{0,1:T(8,128)(2,1)}, bf16[256,512]{0,1:T(8,128)(2,1)}, u32[]{:S(2)}, u32[]{:S(2)}) collective-permute-start(bf16[256,512]{0,1:T(8,128)(2,1)} %get-tuple-element.11), channel_id=1, source_target_pairs={{0,24},{4,28},{8,16},{12,20},{16,8},{20,12},{24,0},{28,4},{1,25},{... | collective-permute-start | bytes 786440 | tf_op jit(solution)/shard_map/ppermute | solution.py:160
  104.8 13.7 %collective-permute-start.19 = (bf16[256,512]{0,1:T(8,128)(2,1)}, bf16[256,512]{0,1:T(8,128)(2,1)}, u32[]{:S(2)}, u32[]{:S(2)}) collective-permute-start(bf16[256,512]{0,1:T(8,128)(2,1)} %get-tuple-element.12), channel_id=1, source_target_pairs={{0,16},{4,20},{8,24},{12,28},{16,0},{20,4},{24,8},{28,12},{1,17},{... | collective-permute-start | bytes 786440 | tf_op jit(solution)/shard_map/ppermute | solution.py:160
  105.3 13.3 %collective-permute-start.18 = (bf16[256,512]{0,1:T(8,128)(2,1)S(1)}, bf16[256,512]{0,1:T(8,128)(2,1)}, u32[]{:S(2)}, u32[]{:S(2)}) collective-permute-start(bf16[256,512]{0,1:T(8,128)(2,1)S(1)} %get-tuple-element.10), channel_id=1, source_target_pairs={{0,8},{4,12},{8,0},{12,4},{16,24},{20,28},{24,16},{28,20},{1,9},{5... | collective-permute-start | bytes 786440 | tf_op jit(solution)/shard_map/ppermute | solution.py:160
  119.8 22.2 %collective-permute-start.21 = (bf16[256,512]{0,1:T(8,128)(2,1)S(1)}, bf16[256,512]{0,1:T(8,128)(2,1)S(1)}, u32[]{:S(2)}, u32[]{:S(2)}) collective-permute-start(bf16[256,512]{0,1:T(8,128)(2,1)S(1)} %add_convert_fusion), channel_id=1, source_target_pairs={{0,0},{1,8},{2,16},{3,24},{4,4},{5,12},{6,20},{7,28},{8,1},{9,9},{... | collective-permute-start | bytes 786440 | tf_op jit(solution)/shard_map/ppermute | solution.py:169
  (10 other events, 26.1 us)

commit v2 on v1

v2 whole, which is shorter than its diff:
```python
import math

import jax
import jax.numpy as jnp
from jax import lax
from jax.sharding import PartitionSpec as P

EPS = 1e-06
BETA = 1.0
AXES = ("dp", "tensor")
BF16 = jnp.bfloat16
F32 = jnp.float32


def take_chunk(array, index, rows):
    return lax.dynamic_slice_in_dim(array, index * rows, rows, 0)


def dot(a, b):
    return jnp.dot(a, b, preferred_element_type=F32)


def dot_rows(a, b):
    return lax.dot_general(a, b, (((0,), (0,)), ((), ())), preferred_element_type=F32)


def swapped(array, dp_count):
    return lax.ppermute(array, "dp", [(i, i ^ 1) for i in range(dp_count)])


def scatter_over_tensor(partial, rows, count):
    me = lax.axis_index("tensor")
    got = []
    for step in range(1, count):
        pairs = [(i, (i + step) % count) for i in range(count)]
        part = take_chunk(partial, (me + step) % count, rows).astype(BF16)
        got.append(lax.ppermute(part, "tensor", pairs))
    return got


def on_device(
    tokens,
    ref_gain,
    ref_weight,
    pol_gain,
    pol_weight,
    lengths,
    bins,
    advantage,
    logprob_gap,
    cotangent,
):
    tensor_count = lax.axis_size("tensor")
    dp_count = lax.axis_size("dp")
    t = lax.axis_index("tensor")
    d = lax.axis_index("dp")
    cores = dp_count // tensor_count
    assert cores == 2
    places = dp_count // cores
    levels = places.bit_length() - 1
    assert 1 << levels == places
    place = d // cores
    core = d % cores
    group_rows, block = tokens.shape
    own_rows = group_rows // tensor_count
    slot_count = cotangent.shape[2]
    span_rows = slot_count // dp_count
    value_width = ref_weight.shape[1]
    model_width = pol_gain.shape[0]
    shard = pol_weight.shape[0]
    factor = 1.0 / math.sqrt(dp_count * tensor_count * lengths.shape[2])

    def flat(p, c, z):
        return (p * cores + c) * tensor_count + z

    relative = place ^ t
    gain_shard = take_chunk(pol_gain, d, shard)
    sent_weight = (pol_weight.astype(F32) * gain_shard[:, None]).astype(BF16)
    halves = 2
    half_rows = shard // halves
    held = [sent_weight[i * half_rows : (i + 1) * half_rows] for i in range(halves)]
    holders = [[0] for _ in range(halves)]

    def stage(number):
        for i in range(halves):
            bit = 1 << ((i + number) % levels)
            pairs = [
                (flat(q ^ z, c, z), flat(q ^ bit ^ z, c, z))
                for q in holders[i]
                for c in range(cores)
                for z in range(tensor_count)
            ]
            got = lax.ppermute(held[i], AXES, pairs)
            getters = [q ^ bit for q in holders[i]]
            is_getter = jnp.zeros((), jnp.bool_)
            for q in getters:
                is_getter = is_getter | (relative == q)
            held[i] = jnp.where(is_getter, got, held[i])
            holders[i] = holders[i] + getters

    stage(0)

    kept_rows = lax.dynamic_slice_in_dim(tokens, core * shard, shard, 1)
    given_rows = lax.dynamic_slice_in_dim(tokens, (1 - core) * shard, shard, 1)
    tokens_f32 = tokens.astype(F32)
    scaled = (tokens_f32 * ref_gain[None, :]).astype(BF16)
    ref_part = dot(scaled, ref_weight).astype(BF16)
    square = jnp.sum(jnp.square(tokens_f32), axis=1)

    tied = lax.optimization_barrier((*held, kept_rows, given_rows, ref_part, square))
    held = list(tied[:halves])
    kept_rows, given_rows, ref_part, square = tied[halves:]

    got_rows = swapped(given_rows, dp_count)
    ref_got = scatter_over_tensor(ref_part, own_rows, tensor_count)
    square_sum = take_chunk(lax.psum(square, "tensor"), t, own_rows)
    got_cot = lax.all_to_all(
        cotangent.reshape(slot_count, value_width), "dp", split_axis=0, concat_axis=0, tiled=True
    )
    for number in range(1, levels):
        stage(number)

    row_scale = lax.rsqrt(square_sum / model_width + EPS)[:, None]
    ref_sum = sum(x.astype(F32) for x in ref_got) + take_chunk(ref_part, t, own_rows).astype(F32)
    ref_values = (ref_sum * row_scale).astype(BF16).astype(F32)

    seq_lens = lengths.reshape(-1)
    seq_bins = bins.reshape(-1)
    seq_adv = advantage.reshape(-1)
    seq_starts = jnp.cumsum(seq_lens) - seq_lens
    row = jnp.arange(own_rows, dtype=jnp.int32)
    in_seq = (row[:, None] >= seq_starts[None, :]) & (
        row[:, None] < (seq_starts + seq_lens)[None, :]
    )
    row_slot = jnp.sum(
        jnp.where(in_seq, seq_bins * span_rows + row[:, None] - seq_starts[None, :], 0), axis=1
    )
    row_len = jnp.sum(jnp.where(in_seq, seq_lens[None, :], 0), axis=1).astype(F32)
    row_adv = jnp.sum(jnp.where(in_seq, seq_adv[None, :], 0.0), axis=1)
    importance = jnp.minimum(jnp.exp(logprob_gap), jnp.float32(2.0))
    coef_adv = (row_adv * importance / row_len).astype(BF16).astype(F32)[:, None]
    coef_pull = (BETA / row_len).astype(BF16).astype(F32)[:, None]
    slot = jnp.arange(slot_count, dtype=jnp.int32)
    row_at = (row_slot[:, None] == slot[None, :]).astype(BF16)
    slot_at = (slot[:, None] == row_slot[None, :]).astype(BF16)
    upstream = dot(row_at, got_cot)
    fixed = coef_adv * upstream - coef_pull * ref_values

    tied = lax.optimization_barrier((*held, fixed, coef_pull, row_scale, slot_at, got_rows))
    weight = jnp.concatenate(tied[:halves], axis=0)
    fixed, coef_pull, row_scale, slot_at, got_rows = tied[halves:]

    value_given = dot(got_rows, weight).astype(BF16)
    value_got = swapped(value_given, dp_count)
    value_part = dot(kept_rows, weight) + value_got.astype(F32)
    value_sum = take_chunk(value_part, t, own_rows)
    for got in scatter_over_tensor(value_part, own_rows, tensor_count):
        value_sum = value_sum + got.astype(F32)
    values = value_sum * row_scale

    slope = ((fixed + coef_pull * values) * row_scale).astype(BF16)
    slopes = jnp.zeros((group_rows, value_width), BF16)
    slopes = lax.dynamic_update_slice_in_dim(slopes, slope, t * own_rows, 0)
    for step in range(1, tensor_count):
        pairs = [(i, (i + step) % tensor_count) for i in range(tensor_count)]
        got = lax.ppermute(slope, "tensor", pairs)
        source = (t - step) % tensor_count
        slopes = lax.dynamic_update_slice_in_dim(slopes, got, source * own_rows, 0)
    slopes_got = swapped(slopes, dp_count)

    sent = dot(slot_at, values.astype(BF16)).astype(BF16)
    policy_values = lax.all_to_all(sent, "dp", split_axis=0, concat_axis=0, tiled=True)

    grad = dot_rows(kept_rows, slopes) + dot_rows(got_rows, slopes_got)
    gain_block = lax.dynamic_slice_in_dim(pol_gain, t * block + core * shard, shard, 0)
    grad = (grad * (gain_block * factor)[:, None]).astype(BF16)
    grad, policy_values = lax.optimization_barrier((grad, policy_values))
    out_rows = shard // tensor_count
    total = take_chunk(grad, place, out_rows).astype(F32)
    for step in range(1, places):
        pairs = [
            (p * cores + c, (p ^ step) * cores + c) for p in range(places) for c in range(cores)
        ]
        total = total + lax.ppermute(
            take_chunk(grad, place ^ step, out_rows), "dp", pairs
        ).astype(F32)
    pairs = [
        (flat(p, c, z), flat(z, c, p))
        for p in range(places)
        for c in range(cores)
        for z in range(tensor_count)
    ]
    grad_weight = lax.ppermute(total.astype(BF16), AXES, pairs).astype(F32)
    return (policy_values.reshape(1, 1, slot_count, value_width), grad_weight)


def solution(mesh):
    in_specs = (
        P("dp", "tensor"),
        P("tensor"),
        P("tensor", None),
        P(),
        P("dp", None),
        P("dp", "tensor", None),
        P("dp", "tensor", None),
        P("dp", "tensor", None),
        P(("dp", "tensor")),
        P("dp", "tensor", None, None),
    )
    out_specs = (P("dp", "tensor", None, None), P(("dp", "tensor"), None))
    return jax.shard_map(
        on_device, mesh=mesh, in_specs=in_specs, out_specs=out_specs, check_vma=False
    )
```

time: 144 us -> 153 us (1.062)
  the two profiles are of different devices: /device:TPU:2 before, /device:TPU:3 now
where the time goes in v2:
time: 153 us; the launch traced here: 152 us
  waiting for transfers between devices  54.2 us (35%)
  starting transfers between devices  48.6 us (32%)
  other arithmetic  13.9 us (9%)
  matrix products  13.8 us (9%)
  local copies, waits for them, and re-layouts  12.2 us (8%)
  blocking collectives  8.45 us (6%)
    ppermute x1, waiting for transfers between devices, on_device(): grad_weight = lax.ppermute(total.astype(BF16), AXES, pairs).astype(F32)  19.8 us
    ppermute x6, starting transfers between devices, scatter_over_tensor(): got.append(lax.ppermute(part, 'tensor', pairs))  14.5 us
    ppermute x3, waiting for transfers between devices, on_device(): lax.ppermute(take_chunk(grad, place ^ step, out_rows), 'dp', pairs)  11.4 us
    ppermute x6, waiting for transfers between devices, scatter_over_tensor(): got.append(lax.ppermute(part, 'tensor', pairs))  8.99 us
    dot_general x5, matrix products, dot(): return jnp.dot(a, b, preferred_element_type=F32)  8.87 us
    psum x1, blocking collectives, on_device(): square_sum = take_chunk(lax.psum(square, 'tensor'), t, own_rows)  8.45 us
    all_to_all x1, starting transfers between devices, on_device(): lax.all_to_all(cotangent.reshape(slot_count, value_width), 'dp', split_ax...  7.7 us
    ppermute x4, waiting for transfers between devices, stage(): got = lax.ppermute(held[i], AXES, pairs)  6.99 us
  transfers between devices with their start and end apart: 22, of which 9 were waited for; matrix products, arithmetic and copies ran while one was open for 18% of the time, Pallas kernels for 0%

profile of v2, /device:TPU:3, one launch (start us, length us, event | category | flops | bytes accessed | tf_op | source)
XLA Modules:
  0.0 151.9 jit_solution(4979206188724927316)
XLA Ops:
  6.9 7.7 %all-to-all-start = ((bf16[8,32,512]{2,1,0:T(8,128)(2,1)}), bf16[8,32,512]{2,1,0:T(8,128)(2,1)S(1)}, u32[]{:S(2)}, u32[]{:S(2)}) async-start(bf16[8,32,512]{2,1,0:T(8,128)(2,1)} %bitcast.31), calls=%async_computation | async-start | bytes 524288 | tf_op jit(solution)/shard_map/all_to_all | solution.py:117
  14.6 2.1 %fusion.1 = f32[512]{0:T(512)S(1)} fusion(bf16[512,2048]{1,0:T(8,128)(2,1)} %param.10), kind=kLoop, calls=%fused_computation.3 | loop fusion | flops 3145216 | bytes 2099200 | tf_op jit(solution)/shard_map/reduce_sum | solution.py:108
  18.2 3.0 %constant_dynamic-slice_fusion.6 = (bf16[512,1024]{1,0:T(8,128)(2,1)}, bf16[512,1024]{1,0:T(8,128)(2,1)}) fusion(bf16[512,2048]{1,0:T(8,128)(2,1)} %param.10, s32[]{:T(128)S(6)} %select_n.138, s32[]{:T(128)S(6)} %select_n.137), kind=kLoop, calls=%fused_computation.42 | loop fusion | bytes 4194312 | tf_op jit(solution)/shard_map/dynamic_slice | solution.py:104
  21.3 2.8 %fusion.5 = bf16[512,512]{1,0:T(8,128)(2,1)S(1)} fusion(bf16[2048,512]{1,0:T(8,128)(2,1)S(1)} %copy-done, bf16[512,2048]{1,0:T(8,128)(2,1)} %param.10, f32[2048]{0:T(1024)S(1)} %copy-done.9), kind=kOutput, calls=%fused_computation.9 | convolution fusion | flops 1077149696 | bytes 4726784 | tf_op jit(solution)/shard_map/dot_general | solution.py:20
  24.2 2.3 %broadcast_select_fusion.2 = (bf16[512,512]{1,0:T(8,128)(2,1)}, bf16[512,512]{1,0:T(8,128)(2,1)}) fusion(bf16[512,512]{1,0:T(8,128)(2,1)} %collective-permute-done.1, pred[]{:T(512)S(6)} %eq.50, bf16[1024,512]{1,0:T(8,128)(2,1)S(1)} %multiply_convert_fusion.1, bf16[512,512]{1,0:T(8,128)(2,1)} %collective-permute-done, pred[]{:T(512)S(6)} %eq.49), kind=kLoop, calls=%fused_computation.17 | loop fusion | flops 524288 | bytes 3145730 | tf_op jit(solution)/shard_map/jit(_where)/select_n | solution.py:98
  29.4 4.0 %collective-permute-start.5 = (bf16[128,512]{1,0:T(8,128)(2,1)}, bf16[128,512]{1,0:T(8,128)(2,1)}, u32[]{:S(2)}, u32[]{:S(2)}) collective-permute-start(bf16[128,512]{1,0:T(8,128)(2,1)} %get-tuple-element.50), channel_id=1, source_target_pairs={{0,2},{1,3},{2,0},{3,1},{4,6},{5,7},{6,4},{7,5},{8,10},{9,11},{10,... | collective-permute-start | bytes 393224 | tf_op jit(solution)/shard_map/ppermute | solution.py:37
  33.5 3.2 %collective-permute-start.6 = (bf16[128,512]{1,0:T(8,128)(2,1)S(1)}, bf16[128,512]{1,0:T(8,128)(2,1)}, u32[]{:S(2)}, u32[]{:S(2)}) collective-permute-start(bf16[128,512]{1,0:T(8,128)(2,1)S(1)} %get-tuple-element.49), channel_id=1, source_target_pairs={{0,3},{1,0},{2,1},{3,2},{4,7},{5,4},{6,5},{7,6},{8,11},{9,8},{10,9... | collective-permute-start | bytes 393224 | tf_op jit(solution)/shard_map/ppermute | solution.py:37
  36.7 8.5 %psum.7 = f32[512]{0:T(512)} all-reduce(f32[512]{0:T(512)S(1)} %fusion.1), channel_id=1, replica_groups=mesh['dp'=8,'tensor'=4] {'tensor'}, use_global_device_ids=true, to_apply=%region_5.6 | all-reduce | flops 512 | bytes 4096 | tf_op jit(solution)/shard_map/psum | solution.py:116
  46.4 2.4 %collective-permute-start.2 = (bf16[512,512]{1,0:T(8,128)(2,1)}, bf16[512,512]{1,0:T(8,128)(2,1)}, u32[]{:S(2)}, u32[]{:S(2)}) collective-permute-start(bf16[512,512]{1,0:T(8,128)(2,1)} %get-tuple-element.18), channel_id=1, source_target_pairs={{0,16},{9,25},{18,2},{27,11},{4,20},{13,29},{22,6},{31,15},{8,24},... | collective-permute-start | bytes 1572872 | tf_op jit(solution)/shard_map/ppermute | solution.py:93
  51.0 7.0 %collective-permute-done.2 = bf16[512,512]{1,0:T(8,128)(2,1)} collective-permute-done((bf16[512,512]{1,0:T(8,128)(2,1)}, bf16[512,512]{1,0:T(8,128)(2,1)}, u32[]{:S(2)}, u32[]{:S(2)}) %collective-permute-start.2) | collective-permute-done | bytes 524320 | tf_op jit(solution)/shard_map/ppermute | solution.py:93
  58.2 2.0 %convolution_convert_fusion = bf16[512,512]{1,0:T(8,128)(2,1)S(1)} fusion(bf16[512,1024]{1,0:T(8,128)(2,1)} %collective-permute-done.7, bf16[1024,512]{1,0:T(8,128)(2,1)S(1)} %constant_dynamic-update-slice_fusion), kind=kOutput, calls=%fused_computation.10 | convolution fusion | flops 537133056 | bytes 2621440 | tf_op jit(solution)/shard_map/dot_general | solution.py:20
  60.2 2.5 %collective-permute-start.8 = (bf16[512,512]{1,0:T(8,128)(2,1)S(1)}, bf16[512,512]{1,0:T(8,128)(2,1)S(1)}, u32[]{:S(2)}, u32[]{:S(2)}) collective-permute-start(bf16[512,512]{1,0:T(8,128)(2,1)S(1)} %convolution_convert_fusion), channel_id=1, source_target_pairs={{0,4},{4,0},{8,12},{12,8},{16,20},{20,16},{24,28},{28,24},{1,5},{5... | collective-permute-start | bytes 1572872 | tf_op jit(solution)/shard_map/ppermute | solution.py:28
  62.7 1.5 %collective-permute-done.8 = bf16[512,512]{1,0:T(8,128)(2,1)S(1)} collective-permute-done((bf16[512,512]{1,0:T(8,128)(2,1)S(1)}, bf16[512,512]{1,0:T(8,128)(2,1)S(1)}, u32[]{:S(2)}, u32[]{:S(2)}) %collective-permute-start.8) | collective-permute-done | bytes 524320 | tf_op jit(solution)/shard_map/ppermute | solution.py:28
  65.0 5.5 %collective-permute-start.10 = (bf16[128,512]{1,0:T(8,128)(2,1)S(1)}, bf16[128,512]{1,0:T(8,128)(2,1)S(1)}, u32[]{:S(2)}, u32[]{:S(2)}) collective-permute-start(bf16[128,512]{1,0:T(8,128)(2,1)S(1)} %get-tuple-element.43), channel_id=1, source_target_pairs={{0,2},{1,3},{2,0},{3,1},{4,6},{5,7},{6,4},{7,5},{8,10},{9,11},{10,... | collective-permute-start | bytes 393224 | tf_op jit(solution)/shard_map/ppermute | solution.py:37
  72.3 4.7 %collective-permute-done.10 = bf16[128,512]{1,0:T(8,128)(2,1)S(1)} collective-permute-done((bf16[128,512]{1,0:T(8,128)(2,1)S(1)}, bf16[128,512]{1,0:T(8,128)(2,1)S(1)}, u32[]{:S(2)}, u32[]{:S(2)}) %collective-permute-start.10) | collective-permute-done | bytes 131104 | tf_op jit(solution)/shard_map/ppermute | solution.py:37
  77.0 4.3 %collective-permute-done.9 = bf16[128,512]{1,0:T(8,128)(2,1)S(1)} collective-permute-done((bf16[128,512]{1,0:T(8,128)(2,1)S(1)}, bf16[128,512]{1,0:T(8,128)(2,1)S(1)}, u32[]{:S(2)}, u32[]{:S(2)}) %collective-permute-start.9) | collective-permute-done | bytes 131104 | tf_op jit(solution)/shard_map/ppermute | solution.py:37
  82.9 2.2 %collective-permute-start.12 = (bf16[128,512]{1,0:T(8,128)(2,1)}, bf16[128,512]{1,0:T(8,128)(2,1)}, u32[]{:S(2)}, u32[]{:S(2)}) collective-permute-start(bf16[128,512]{1,0:T(8,128)(2,1)} %get-tuple-element.35), channel_id=1, source_target_pairs={{0,1},{1,2},{2,3},{3,0},{4,5},{5,6},{6,7},{7,4},{8,9},{9,10},{10,1... | collective-permute-start | bytes 393224 | tf_op jit(solution)/shard_map/ppermute | solution.py:166
  85.1 1.9 %collective-permute-start.13 = (bf16[128,512]{1,0:T(8,128)(2,1)}, bf16[128,512]{1,0:T(8,128)(2,1)}, u32[]{:S(2)}, u32[]{:S(2)}) collective-permute-start(bf16[128,512]{1,0:T(8,128)(2,1)} %get-tuple-element.35), channel_id=1, source_target_pairs={{0,2},{1,3},{2,0},{3,1},{4,6},{5,7},{6,4},{7,5},{8,10},{9,11},{10,... | collective-permute-start | bytes 393224 | tf_op jit(solution)/shard_map/ppermute | solution.py:166
  87.1 2.4 %collective-permute-start.14 = (bf16[128,512]{1,0:T(8,128)(2,1)}, bf16[128,512]{1,0:T(8,128)(2,1)S(1)}, u32[]{:S(2)}, u32[]{:S(2)}) collective-permute-start(bf16[128,512]{1,0:T(8,128)(2,1)} %get-tuple-element.35), channel_id=1, source_target_pairs={{0,3},{1,0},{2,1},{3,2},{4,7},{5,4},{6,5},{7,6},{8,11},{9,8},{10,9... | collective-permute-start | bytes 393224 | tf_op jit(solution)/shard_map/ppermute | solution.py:166
  89.4 1.6 %constant_dynamic-update-slice_fusion.4 = bf16[512,512]{1,0:T(8,128)(2,1)} fusion(bf16[512,512]{1,0:T(8,128)(2,1)} %get-tuple-element.34, bf16[128,512]{1,0:T(8,128)(2,1)} %collective-permute-done.12, s32[]{:T(128)S(6)} %select_n.154), kind=kLoop, calls=%fused_computation.37 | loop fusion | bytes 262148 | tf_op jit(solution)/shard_map/dynamic_update_slice | solution.py:168
  91.0 5.1 %collective-permute-done.13 = bf16[128,512]{1,0:T(8,128)(2,1)} collective-permute-done((bf16[128,512]{1,0:T(8,128)(2,1)}, bf16[128,512]{1,0:T(8,128)(2,1)}, u32[]{:S(2)}, u32[]{:S(2)}) %collective-permute-start.13) | collective-permute-done | bytes 131104 | tf_op jit(solution)/shard_map/ppermute | solution.py:166
  96.1 1.6 %constant_dynamic-update-slice_fusion.3 = bf16[512,512]{1,0:T(8,128)(2,1)} fusion(bf16[512,512]{1,0:T(8,128)(2,1)} %constant_dynamic-update-slice_fusion.4, bf16[128,512]{1,0:T(8,128)(2,1)} %collective-permute-done.13, s32[]{:T(128)S(6)} %select_n.156), kind=kLoop, calls=%fused_computation.36 | loop fusion | bytes 262148 | tf_op jit(solution)/shard_map/dynamic_update_slice | solution.py:168
  98.9 2.0 %convolution_convert_fusion.1 = bf16[256,512]{1,0:T(8,128)(2,1)} fusion(bf16[256,128]{1,0:T(8,128)(2,1)} %fusion.10, bf16[128,512]{1,0:T(8,128)(2,1)S(1)} %collective-permute-done.11, bf16[128,512]{1,0:T(8,128)(2,1)S(1)} %collective-permute-done.10, bf16[128,512]{1,0:T(8,128)(2,1)S(1)} %collective-permute-done.9, f32[512,512]{1,0:T(8,128)} %copy-done.3, ...), kind=kOutput, calls=%fused_computation.11 | convolution fusion | flops 34209792 | bytes 983556 | tf_op jit(solution)/shard_map/dot_general | solution.py:20
  100.9 5.4 %all-to-all-start.1 = ((bf16[8,32,512]{2,1,0:T(8,128)(2,1)}), bf16[8,32,512]{2,1,0:T(8,128)(2,1)S(1)}, u32[]{:S(2)}, u32[]{:S(2)}) async-start(bf16[8,32,512]{2,1,0:T(8,128)(2,1)} %bitcast.11), calls=%async_computation.1 | async-start | bytes 524288 | tf_op jit(solution)/shard_map/all_to_all | solution.py:172
  106.3 2.1 %fusion.14 = f32[1024,512]{1,0:T(8,128)S(1)} fusion(bf16[512,1024]{1,0:T(8,128)(2,1)} %collective-permute-done.7, bf16[512,512]{1,0:T(8,128)(2,1)} %collective-permute-done.15), kind=kOutput, calls=%fused_computation.58 | convolution fusion | flops 536870912 | bytes 3670016 | tf_op jit(solution)/shard_map/dot_general | solution.py:24
  108.4 2.8 %multiply_convert_fusion = bf16[1024,512]{1,0:T(8,128)(2,1)} fusion(f32[1024,512]{1,0:T(8,128)S(1)} %fusion.14, bf16[512,1024]{1,0:T(8,128)(2,1)S(1)} %copy-done.1, bf16[512,512]{1,0:T(8,128)(2,1)} %constant_dynamic-update-slice_fusion.2, f32[1024]{0:T(1024)S(1)} %get-tuple-element.51), kind=kOutput, calls=%fused_computation.5 | convolution fusion | flops 538443776 | bytes 4722688 | tf_op jit(solution)/shard_map/dot_general | solution.py:24
  111.5 1.9 %constant_dynamic-slice_fusion.2 = (bf16[256,512]{1,0:T(8,128)(2,1)}, bf16[256,512]{1,0:T(8,128)(2,1)S(1)}, bf16[256,512]{1,0:T(8,128)(2,1)S(1)}) fusion(bf16[1024,512]{1,0:T(8,128)(2,1)} %multiply_convert_fusion, s32[]{:T(128)S(6)} %select_n.161, s32[]{:T(128)S(6)} %select_n.163, s32[]{:T(128)S(6)} %select_n.162), kind=kLoop, calls=%fused_computation.34 | loop fusion | bytes 1572876 | tf_op jit(solution)/shard_map/dynamic_slice | solution.py:16
  114.5 1.5 %collective-permute-start.18 = (bf16[256,512]{1,0:T(8,128)(2,1)S(1)}, bf16[256,512]{1,0:T(8,128)(2,1)}, u32[]{:S(2)}, u32[]{:S(2)}) collective-permute-start(bf16[256,512]{1,0:T(8,128)(2,1)S(1)} %get-tuple-element.39), channel_id=1, source_target_pairs={{0,24},{4,28},{8,16},{12,20},{16,8},{20,12},{24,0},{28,4},{1,25},{... | collective-permute-start | bytes 786440 | tf_op jit(solution)/shard_map/ppermute | solution.py:184
  116.1 4.8 %collective-permute-done.16 = bf16[256,512]{1,0:T(8,128)(2,1)S(1)} collective-permute-done((bf16[256,512]{1,0:T(8,128)(2,1)}, bf16[256,512]{1,0:T(8,128)(2,1)S(1)}, u32[]{:S(2)}, u32[]{:S(2)}) %collective-permute-start.16) | collective-permute-done | bytes 262176 | tf_op jit(solution)/shard_map/ppermute | solution.py:184
  120.9 6.6 %collective-permute-done.18 = bf16[256,512]{1,0:T(8,128)(2,1)} collective-permute-done((bf16[256,512]{1,0:T(8,128)(2,1)S(1)}, bf16[256,512]{1,0:T(8,128)(2,1)}, u32[]{:S(2)}, u32[]{:S(2)}) %collective-permute-start.18) | collective-permute-done | bytes 262176 | tf_op jit(solution)/shard_map/ppermute | solution.py:184
  128.6 1.9 %collective-permute-start.19 = (bf16[256,512]{1,0:T(8,128)(2,1)S(1)}, bf16[256,512]{1,0:T(8,128)(2,1)S(1)}, u32[]{:S(2)}, u32[]{:S(2)}) collective-permute-start(bf16[256,512]{1,0:T(8,128)(2,1)S(1)} %add_convert_fusion), channel_id=1, source_target_pairs={{0,0},{1,8},{2,16},{3,24},{4,4},{5,12},{6,20},{7,28},{8,1},{9,9},{... | collective-permute-start | bytes 786440 | tf_op jit(solution)/shard_map/ppermute | solution.py:193
  130.5 19.8 %collective-permute-done.19 = bf16[256,512]{1,0:T(8,128)(2,1)S(1)} collective-permute-done((bf16[256,512]{1,0:T(8,128)(2,1)S(1)}, bf16[256,512]{1,0:T(8,128)(2,1)S(1)}, u32[]{:S(2)}, u32[]{:S(2)}) %collective-permute-start.19) | collective-permute-done | bytes 262176 | tf_op jit(solution)/shard_map/ppermute | solution.py:193
  (72 shorter events, 24.0 us)
Async XLA Ops:
  0.6 20.7 %copy-start = (bf16[2048,512]{1,0:T(8,128)(2,1)S(1)}, bf16[2048,512]{1,0:T(8,128)(2,1)}, u32[]{:S(2)}) copy-start(bf16[2048,512]{1,0:T(8,128)(2,1)} %param.12) | copy-start | bytes 6291460
  3.0 13.6 %copy-start.7 = (s32[1,1,8]{2,1,0:T(1,128)S(1)}, s32[1,1,8]{2,1,0:T(1,128)}, u32[]{:S(2)}) copy-start(s32[1,1,8]{2,1,0:T(1,128)} %param.15) | copy-start | bytes 100
  3.0 13.8 %copy-start.10 = (s32[1,1,8]{2,1,0:T(1,128)S(1)}, s32[1,1,8]{2,1,0:T(1,128)}, u32[]{:S(2)}) copy-start(s32[1,1,8]{2,1,0:T(1,128)} %param.16) | copy-start | bytes 100
  4.1 20.1 %collective-permute-start = (bf16[512,512]{1,0:T(8,128)(2,1)}, bf16[512,512]{1,0:T(8,128)(2,1)}, u32[]{:S(2)}, u32[]{:S(2)}) collective-permute-start(bf16[512,512]{1,0:T(8,128)(2,1)} %get-tuple-element.47), channel_id=1, source_target_pairs={{0,8},{9,1},{18,26},{27,19},{4,12},{13,5},{22,30},{31,23}} | collective-permute-start | bytes 1572872 | tf_op jit(solution)/shard_map/ppermute | solution.py:93
  5.4 18.8 %collective-permute-start.1 = (bf16[512,512]{1,0:T(8,128)(2,1)}, bf16[512,512]{1,0:T(8,128)(2,1)}, u32[]{:S(2)}, u32[]{:S(2)}) collective-permute-start(bf16[512,512]{1,0:T(8,128)(2,1)} %get-tuple-element.46), channel_id=1, source_target_pairs={{0,16},{9,25},{18,2},{27,11},{4,20},{13,29},{22,6},{31,15}} | collective-permute-start | bytes 1572872 | tf_op jit(solution)/shard_map/ppermute | solution.py:93
  6.9 42.7 %all-to-all-start = ((bf16[8,32,512]{2,1,0:T(8,128)(2,1)}), bf16[8,32,512]{2,1,0:T(8,128)(2,1)S(1)}, u32[]{:S(2)}, u32[]{:S(2)}) async-start(bf16[8,32,512]{2,1,0:T(8,128)(2,1)} %bitcast.31), calls=%async_computation | async-start | bytes 524288 | tf_op jit(solution)/shard_map/all_to_all | solution.py:117
  18.2 3.1 %copy-start.9 = (f32[2048]{0:T(1024)S(1)}, f32[2048]{0:T(1024)}, u32[]{:S(2)}) copy-start(f32[2048]{0:T(1024)} %param.11) | copy-start | bytes 24580
  24.1 3.0 %copy-start.4 = (bf16[512,512]{1,0:T(8,128)(2,1)}, bf16[512,512]{1,0:T(8,128)(2,1)S(1)}, u32[]{:S(2)}) copy-start(bf16[512,512]{1,0:T(8,128)(2,1)S(1)} %fusion.5) | copy-start | bytes 1572868
  24.2 4.8 %copy-start.5 = (s32[128]{0:T(128)S(1)}, s32[128]{0:T(128)}, u32[]{:S(2)}) copy-start(s32[128]{0:T(128)} %get-tuple-element.33) | copy-start | bytes 1540
  24.2 4.7 %copy-start.6 = (f32[128]{0:T(128)S(1)}, f32[128]{0:T(128)}, u32[]{:S(2)}) copy-start(f32[128]{0:T(128)} %param.18) | copy-start | bytes 1540
  26.5 31.5 %copy-start.2 = (bf16[512,512]{1,0:T(8,128)(2,1)S(1)}, bf16[512,512]{1,0:T(8,128)(2,1)}, u32[]{:S(2)}) copy-start(bf16[512,512]{1,0:T(8,128)(2,1)} %get-tuple-element.18) | copy-start | bytes 1572868
  27.2 19.3 %collective-permute-start.4 = (bf16[128,512]{1,0:T(8,128)(2,1)}, bf16[128,512]{1,0:T(8,128)(2,1)}, u32[]{:S(2)}, u32[]{:S(2)}) collective-permute-start(bf16[128,512]{1,0:T(8,128)(2,1)} %get-tuple-element.48), channel_id=1, source_target_pairs={{0,1},{1,2},{2,3},{3,0},{4,5},{5,6},{6,7},{7,4},{8,9},{9,10},{10,1... | collective-permute-start | bytes 393224 | tf_op jit(solution)/shard_map/ppermute | solution.py:37
  27.2 23.7 %collective-permute-start.3 = (bf16[512,512]{1,0:T(8,128)(2,1)}, bf16[512,512]{1,0:T(8,128)(2,1)S(1)}, u32[]{:S(2)}, u32[]{:S(2)}) collective-permute-start(bf16[512,512]{1,0:T(8,128)(2,1)} %get-tuple-element.19), channel_id=1, source_target_pairs={{0,8},{9,1},{18,26},{27,19},{4,12},{13,5},{22,30},{31,23},{16,24},... | collective-permute-start | bytes 1572872 | tf_op jit(solution)/shard_map/ppermute | solution.py:93
  28.5 29.6 %collective-permute-start.7 = (bf16[512,1024]{1,0:T(8,128)(2,1)}, bf16[512,1024]{1,0:T(8,128)(2,1)}, u32[]{:S(2)}, u32[]{:S(2)}) collective-permute-start(bf16[512,1024]{1,0:T(8,128)(2,1)} %get-tuple-element.22), channel_id=1, source_target_pairs={{0,4},{4,0},{8,12},{12,8},{16,20},{20,16},{24,28},{28,24},{1,5},{5... | collective-permute-start | bytes 3145736 | tf_op jit(solution)/shard_map/ppermute | solution.py:28
  29.4 20.1 %collective-permute-start.5 = (bf16[128,512]{1,0:T(8,128)(2,1)}, bf16[128,512]{1,0:T(8,128)(2,1)}, u32[]{:S(2)}, u32[]{:S(2)}) collective-permute-start(bf16[128,512]{1,0:T(8,128)(2,1)} %get-tuple-element.50), channel_id=1, source_target_pairs={{0,2},{1,3},{2,0},{3,1},{4,6},{5,7},{6,4},{7,5},{8,10},{9,11},{10,... | collective-permute-start | bytes 393224 | tf_op jit(solution)/shard_map/ppermute | solution.py:37
  33.5 16.1 %collective-permute-start.6 = (bf16[128,512]{1,0:T(8,128)(2,1)S(1)}, bf16[128,512]{1,0:T(8,128)(2,1)}, u32[]{:S(2)}, u32[]{:S(2)}) collective-permute-start(bf16[128,512]{1,0:T(8,128)(2,1)S(1)} %get-tuple-element.49), channel_id=1, source_target_pairs={{0,3},{1,0},{2,1},{3,2},{4,7},{5,4},{6,5},{7,6},{8,11},{9,8},{10,9... | collective-permute-start | bytes 393224 | tf_op jit(solution)/shard_map/ppermute | solution.py:37
  46.4 11.6 %collective-permute-start.2 = (bf16[512,512]{1,0:T(8,128)(2,1)}, bf16[512,512]{1,0:T(8,128)(2,1)}, u32[]{:S(2)}, u32[]{:S(2)}) collective-permute-start(bf16[512,512]{1,0:T(8,128)(2,1)} %get-tuple-element.18), channel_id=1, source_target_pairs={{0,16},{9,25},{18,2},{27,11},{4,20},{13,29},{22,6},{31,15},{8,24},... | collective-permute-start | bytes 1572872 | tf_op jit(solution)/shard_map/ppermute | solution.py:93
  58.1 6.1 %copy-start.1 = (bf16[512,1024]{1,0:T(8,128)(2,1)S(1)}, bf16[512,1024]{1,0:T(8,128)(2,1)}, u32[]{:S(2)}) copy-start(bf16[512,1024]{1,0:T(8,128)(2,1)} %get-tuple-element.17) | copy-start | bytes 3145732
  60.2 4.1 %collective-permute-start.8 = (bf16[512,512]{1,0:T(8,128)(2,1)S(1)}, bf16[512,512]{1,0:T(8,128)(2,1)S(1)}, u32[]{:S(2)}, u32[]{:S(2)}) collective-permute-start(bf16[512,512]{1,0:T(8,128)(2,1)S(1)} %convolution_convert_fusion), channel_id=1, source_target_pairs={{0,4},{4,0},{8,12},{12,8},{16,20},{20,16},{24,28},{28,24},{1,5},{5... | collective-permute-start | bytes 1572872 | tf_op jit(solution)/shard_map/ppermute | solution.py:28
  65.0 18.0 %copy-start.3 = (f32[512,512]{1,0:T(8,128)}, f32[512,512]{1,0:T(8,128)S(1)}, u32[]{:S(2)}) copy-start(f32[512,512]{1,0:T(8,128)S(1)} %convolution_add_fusion) | copy-start | bytes 3145732
  65.0 11.9 %collective-permute-start.10 = (bf16[128,512]{1,0:T(8,128)(2,1)S(1)}, bf16[128,512]{1,0:T(8,128)(2,1)S(1)}, u32[]{:S(2)}, u32[]{:S(2)}) collective-permute-start(bf16[128,512]{1,0:T(8,128)(2,1)S(1)} %get-tuple-element.43), channel_id=1, source_target_pairs={{0,2},{1,3},{2,0},{3,1},{4,6},{5,7},{6,4},{7,5},{8,10},{9,11},{10,... | collective-permute-start | bytes 393224 | tf_op jit(solution)/shard_map/ppermute | solution.py:37
  70.6 6.4 %collective-permute-start.11 = (bf16[128,512]{1,0:T(8,128)(2,1)S(1)}, bf16[128,512]{1,0:T(8,128)(2,1)S(1)}, u32[]{:S(2)}, u32[]{:S(2)}) collective-permute-start(bf16[128,512]{1,0:T(8,128)(2,1)S(1)} %get-tuple-element.42), channel_id=1, source_target_pairs={{0,3},{1,0},{2,1},{3,2},{4,7},{5,4},{6,5},{7,6},{8,11},{9,8},{10,9... | collective-permute-start | bytes 393224 | tf_op jit(solution)/shard_map/ppermute | solution.py:37
  72.1 9.2 %collective-permute-start.9 = (bf16[128,512]{1,0:T(8,128)(2,1)S(1)}, bf16[128,512]{1,0:T(8,128)(2,1)S(1)}, u32[]{:S(2)}, u32[]{:S(2)}) collective-permute-start(bf16[128,512]{1,0:T(8,128)(2,1)S(1)} %get-tuple-element.41), channel_id=1, source_target_pairs={{0,1},{1,2},{2,3},{3,0},{4,5},{5,6},{6,7},{7,4},{8,9},{9,10},{10,1... | collective-permute-start | bytes 393224 | tf_op jit(solution)/shard_map/ppermute | solution.py:37
  82.9 6.5 %collective-permute-start.12 = (bf16[128,512]{1,0:T(8,128)(2,1)}, bf16[128,512]{1,0:T(8,128)(2,1)}, u32[]{:S(2)}, u32[]{:S(2)}) collective-permute-start(bf16[128,512]{1,0:T(8,128)(2,1)} %get-tuple-element.35), channel_id=1, source_target_pairs={{0,1},{1,2},{2,3},{3,0},{4,5},{5,6},{6,7},{7,4},{8,9},{9,10},{10,1... | collective-permute-start | bytes 393224 | tf_op jit(solution)/shard_map/ppermute | solution.py:166
  85.1 11.0 %collective-permute-start.13 = (bf16[128,512]{1,0:T(8,128)(2,1)}, bf16[128,512]{1,0:T(8,128)(2,1)}, u32[]{:S(2)}, u32[]{:S(2)}) collective-permute-start(bf16[128,512]{1,0:T(8,128)(2,1)} %get-tuple-element.35), channel_id=1, source_target_pairs={{0,2},{1,3},{2,0},{3,1},{4,6},{5,7},{6,4},{7,5},{8,10},{9,11},{10,... | collective-permute-start | bytes 393224 | tf_op jit(solution)/shard_map/ppermute | solution.py:166
  87.1 10.6 %collective-permute-start.14 = (bf16[128,512]{1,0:T(8,128)(2,1)}, bf16[128,512]{1,0:T(8,128)(2,1)S(1)}, u32[]{:S(2)}, u32[]{:S(2)}) collective-permute-start(bf16[128,512]{1,0:T(8,128)(2,1)} %get-tuple-element.35), channel_id=1, source_target_pairs={{0,3},{1,0},{2,1},{3,2},{4,7},{5,4},{6,5},{7,6},{8,11},{9,8},{10,9... | collective-permute-start | bytes 393224 | tf_op jit(solution)/shard_map/ppermute | solution.py:166
  98.3 8.0 %collective-permute-start.15 = (bf16[512,512]{1,0:T(8,128)(2,1)}, bf16[512,512]{1,0:T(8,128)(2,1)}, u32[]{:S(2)}, u32[]{:S(2)}) collective-permute-start(bf16[512,512]{1,0:T(8,128)(2,1)} %constant_dynamic-update-slice_fusion.2), channel_id=1, source_target_pairs={{0,4},{4,0},{8,12},{12,8},{16,20},{20,16},{24,28},{28,24},{1,5},{5... | collective-permute-start | bytes 1572872 | tf_op jit(solution)/shard_map/ppermute | solution.py:28
  100.9 10.7 %all-to-all-start.1 = ((bf16[8,32,512]{2,1,0:T(8,128)(2,1)}), bf16[8,32,512]{2,1,0:T(8,128)(2,1)S(1)}, u32[]{:S(2)}, u32[]{:S(2)}) async-start(bf16[8,32,512]{2,1,0:T(8,128)(2,1)} %bitcast.11), calls=%async_computation.1 | async-start | bytes 524288 | tf_op jit(solution)/shard_map/all_to_all | solution.py:172
  113.4 7.5 %collective-permute-start.16 = (bf16[256,512]{1,0:T(8,128)(2,1)}, bf16[256,512]{1,0:T(8,128)(2,1)S(1)}, u32[]{:S(2)}, u32[]{:S(2)}) collective-permute-start(bf16[256,512]{1,0:T(8,128)(2,1)} %get-tuple-element.38), channel_id=1, source_target_pairs={{0,8},{4,12},{8,0},{12,4},{16,24},{20,28},{24,16},{28,20},{1,9},{5... | collective-permute-start | bytes 786440 | tf_op jit(solution)/shard_map/ppermute | solution.py:184
  113.9 7.0 %collective-permute-start.17 = (bf16[256,512]{1,0:T(8,128)(2,1)S(1)}, bf16[256,512]{1,0:T(8,128)(2,1)S(1)}, u32[]{:S(2)}, u32[]{:S(2)}) collective-permute-start(bf16[256,512]{1,0:T(8,128)(2,1)S(1)} %get-tuple-element.40), channel_id=1, source_target_pairs={{0,16},{4,20},{8,24},{12,28},{16,0},{20,4},{24,8},{28,12},{1,17},{... | collective-permute-start | bytes 786440 | tf_op jit(solution)/shard_map/ppermute | solution.py:184
  114.5 12.9 %collective-permute-start.18 = (bf16[256,512]{1,0:T(8,128)(2,1)S(1)}, bf16[256,512]{1,0:T(8,128)(2,1)}, u32[]{:S(2)}, u32[]{:S(2)}) collective-permute-start(bf16[256,512]{1,0:T(8,128)(2,1)S(1)} %get-tuple-element.39), channel_id=1, source_target_pairs={{0,24},{4,28},{8,16},{12,20},{16,8},{20,12},{24,0},{28,4},{1,25},{... | collective-permute-start | bytes 786440 | tf_op jit(solution)/shard_map/ppermute | solution.py:184
  128.6 21.7 %collective-permute-start.19 = (bf16[256,512]{1,0:T(8,128)(2,1)S(1)}, bf16[256,512]{1,0:T(8,128)(2,1)S(1)}, u32[]{:S(2)}, u32[]{:S(2)}) collective-permute-start(bf16[256,512]{1,0:T(8,128)(2,1)S(1)} %add_convert_fusion), channel_id=1, source_target_pairs={{0,0},{1,8},{2,16},{3,24},{4,4},{5,12},{6,20},{7,28},{8,1},{9,9},{... | collective-permute-start | bytes 786440 | tf_op jit(solution)/shard_map/ppermute | solution.py:193
  (1 other events, 3.0 us)

commit v3 on v2

v3 whole, which is shorter than its diff:
```python
import functools
import math

import jax
import jax.numpy as jnp
from jax import lax
from jax.experimental import pallas as pl
from jax.experimental.pallas import tpu as pltpu
from jax.sharding import PartitionSpec as P

EPS = 1e-06
BETA = 1.0
AXES = ("dp", "tensor")
BF16 = jnp.bfloat16
F32 = jnp.float32
POWER_ROWS = 16
PARTS = 2


def dot(a, b):
    return jnp.dot(a, b, preferred_element_type=F32)


def dot_rows(a, b):
    return lax.dot_general(a, b, (((0,), (0,)), ((), ())), preferred_element_type=F32)


def swapped(array, dp_count):
    return lax.ppermute(array, "dp", [(i, i ^ 1) for i in range(dp_count)])


def shifted(array, count, step):
    return lax.ppermute(array, "tensor", [(i, (i + step) % count) for i in range(count)])


def prepare_kernel(count, steps, at, x_ref, gain_ref, weight_ref, given_ref, kept_ref, *refs):
    sent_refs, (rows_ref, total, square) = refs[:count], refs[count:]
    f = pl.program_id(0)
    own = x_ref.shape[0] // count
    for k in range(count):
        source = lax.rem(at[0] - k + count, count)
        rows_ref[k * own : (k + 1) * own, :] = x_ref[pl.ds(pl.multiple_of(source * own, own), own), :]
    rows = rows_ref[...]

    @pl.when(f < steps // 2)
    def _():
        given_ref[...] = rows

    @pl.when(f >= steps // 2)
    def _():
        kept_ref[...] = rows

    wide = rows.astype(F32)
    part = dot((wide * gain_ref[...]).astype(BF16), weight_ref[...])
    squares = jnp.sum(wide * wide, axis=1, keepdims=True)

    @pl.when(f == 0)
    def _():
        total[...] = part
        square[...] = squares

    @pl.when(f > 0)
    def _():
        total[...] += part
        square[...] += squares

    @pl.when(f == steps - 1)
    def _():
        for k in range(count):
            sent = sent_refs[k]
            sent[:own, :] = total[k * own : (k + 1) * own, :].astype(BF16)
            power = jnp.broadcast_to(square[k * own : (k + 1) * own, :], (own, 128)).T
            high = power[: POWER_ROWS // 2].astype(BF16).astype(F32)
            low = power[: POWER_ROWS // 2] - high
            sent[own:, :] = jnp.zeros((POWER_ROWS, sent.shape[1]), BF16)
            sent[own:, :own] = jnp.concatenate([high, low], axis=0).astype(BF16)


def grad_kernel(places, at, kept_ref, got_ref, slope_ref, slope_got_ref, gain_ref, *refs):
    out_refs, grad = refs[:places], refs[places]
    total = dot_rows(kept_ref[...], slope_ref[...]) + dot_rows(got_ref[...], slope_got_ref[...])
    grad[...] = total * gain_ref[...]
    rows = out_refs[0].shape[0]
    for s in range(places):
        chunk = grad[pl.ds(pl.multiple_of(at[s] * rows, rows), rows), :]
        out_refs[s][...] = chunk.astype(out_refs[s].dtype)


def on_device(
    tokens,
    ref_gain,
    ref_weight,
    pol_gain,
    pol_weight,
    lengths,
    bins,
    advantage,
    logprob_gap,
    cotangent,
):
    tensor_count = lax.axis_size("tensor")
    dp_count = lax.axis_size("dp")
    t = lax.axis_index("tensor")
    d = lax.axis_index("dp")
    cores = dp_count // tensor_count
    assert cores == 2
    places = dp_count // cores
    levels = places.bit_length() - 1
    assert 1 << levels == places
    place = d // cores
    core = d % cores
    group_rows, block = tokens.shape
    own_rows = group_rows // tensor_count
    slot_count = cotangent.shape[2]
    span_rows = slot_count // dp_count
    value_width = ref_weight.shape[1]
    model_width = pol_gain.shape[0]
    shard = pol_weight.shape[0]
    width = value_width // PARTS
    out_rows = shard // tensor_count
    factor = 1.0 / math.sqrt(dp_count * tensor_count * lengths.shape[2])
    relative = place ^ t

    def flat(p, c, z):
        return (p * cores + c) * tensor_count + z

    halves = 2
    half_rows = shard // halves
    gain_shard = lax.dynamic_slice_in_dim(pol_gain, d * shard, shard, 0)

    def first(j, i):
        rows = slice(i * half_rows, (i + 1) * half_rows)
        piece = pol_weight[rows, j * width : (j + 1) * width].astype(F32)
        return (piece * gain_shard[rows, None]).astype(BF16)

    def stage(number, held):
        result = []
        for i in range(halves):
            holders = [0]
            for before in range(number):
                bit = 1 << ((i + before) % levels)
                holders = holders + [q ^ bit for q in holders]
            bit = 1 << ((i + number) % levels)
            pairs = [
                (flat(q ^ z, c, z), flat(q ^ bit ^ z, c, z))
                for q in holders
                for c in range(cores)
                for z in range(tensor_count)
            ]
            got = lax.ppermute(held[i], AXES, pairs)
            is_getter = jnp.zeros((), jnp.bool_)
            for q in holders:
                is_getter = is_getter | (relative == (q ^ bit))
            result.append(jnp.where(is_getter, got, held[i]))
        return result

    held = [[first(j, i) for i in range(halves)] for j in range(PARTS)]
    held[0] = stage(0, held[0])

    steps = 4
    feature_step = block // steps
    at = jnp.stack([t, (1 - core) * (steps // 2)]).astype(jnp.int32)
    sent_shape = (own_rows + POWER_ROWS, value_width)

    def at_step(f, at):
        return lax.rem(f + at[1], steps)

    prepared = pl.pallas_call(
        functools.partial(prepare_kernel, tensor_count, steps),
        grid_spec=pltpu.PrefetchScalarGridSpec(
            num_scalar_prefetch=1,
            grid=(steps,),
            in_specs=[
                pl.BlockSpec((group_rows, feature_step), lambda f, at: (0, at_step(f, at))),
                pl.BlockSpec((1, feature_step), lambda f, at: (0, at_step(f, at))),
                pl.BlockSpec((feature_step, value_width), lambda f, at: (at_step(f, at), 0)),
            ],
            out_specs=[
                pl.BlockSpec(
                    (group_rows, feature_step), lambda f, at: (0, jnp.minimum(f, steps // 2 - 1))
                ),
                pl.BlockSpec(
                    (group_rows, feature_step), lambda f, at: (0, jnp.maximum(f - steps // 2, 0))
                ),
            ]
            + [pl.BlockSpec(sent_shape, lambda f, at: (0, 0))] * tensor_count,
            scratch_shapes=[
                pltpu.VMEM((group_rows, feature_step), BF16),
                pltpu.VMEM((group_rows, value_width), F32),
                pltpu.VMEM((group_rows, 1), F32),
            ],
        ),
        out_shape=[jax.ShapeDtypeStruct((group_rows, shard), BF16)] * 2
        + [jax.ShapeDtypeStruct(sent_shape, BF16)] * tensor_count,
        compiler_params=pltpu.CompilerParams(vmem_limit_bytes=32 * 2**20),
        cost_estimate=pl.CostEstimate(
            flops=2 * group_rows * block * value_width,
            bytes_accessed=8 * 2**20,
            transcendentals=0,
        ),
        name="prepare",
    )(at, tokens, ref_gain.reshape(1, block), ref_weight)
    given_rows, kept_rows, *ref_sent = prepared

    tied = lax.optimization_barrier((*held[0], *held[1], given_rows, kept_rows, *ref_sent))
    held[0], held[1] = list(tied[:halves]), list(tied[halves : 2 * halves])
    given_rows, kept_rows, *ref_sent = tied[2 * halves :]
    ref_got = [ref_sent[0]] + [
        shifted(ref_sent[k], tensor_count, -k) for k in range(1, tensor_count)
    ]
    for number in range(1, levels):
        held[0] = stage(number, held[0])
    for number in range(levels):
        held[1] = stage(number, held[1])
    got_rows = swapped(given_rows, dp_count)
    got_cot = lax.all_to_all(
        cotangent.reshape(slot_count, value_width), "dp", split_axis=0, concat_axis=0, tiled=True
    )

    seq_lens = lengths.reshape(-1)
    seq_bins = bins.reshape(-1)
    seq_adv = advantage.reshape(-1)
    seq_starts = jnp.cumsum(seq_lens) - seq_lens
    row = jnp.arange(own_rows, dtype=jnp.int32)
    in_seq = (row[:, None] >= seq_starts[None, :]) & (
        row[:, None] < (seq_starts + seq_lens)[None, :]
    )
    row_slot = jnp.sum(
        jnp.where(in_seq, seq_bins * span_rows + row[:, None] - seq_starts[None, :], 0), axis=1
    )
    row_len = jnp.sum(jnp.where(in_seq, seq_lens[None, :], 0), axis=1).astype(F32)
    row_adv = jnp.sum(jnp.where(in_seq, seq_adv[None, :], 0.0), axis=1)
    importance = jnp.minimum(jnp.exp(logprob_gap), jnp.float32(2.0))
    coef_adv = (row_adv * importance / row_len).astype(BF16).astype(F32)[:, None]
    coef_pull = (BETA / row_len).astype(BF16).astype(F32)[:, None]
    slot = jnp.arange(slot_count, dtype=jnp.int32)
    row_at = (row_slot[:, None] == slot[None, :]).astype(BF16)
    slot_at = (slot[:, None] == row_slot[None, :]).astype(BF16)
    upstream = dot(row_at, got_cot)

    ref_total = sum(x.astype(F32) for x in ref_got)
    half_power = POWER_ROWS // 2
    square_sum = ref_total[own_rows, :own_rows] + ref_total[own_rows + half_power, :own_rows]
    row_scale = lax.rsqrt(square_sum / model_width + EPS)[:, None]
    ref_values = (ref_total[:own_rows] * row_scale).astype(BF16).astype(F32)
    fixed = coef_adv * upstream - coef_pull * ref_values
    gain_block = lax.dynamic_slice_in_dim(pol_gain, t * block + core * shard, shard, 0)
    grad_gain = (gain_block * factor)[:, None]

    def turned(z):
        return sum(((z >> i) & 1) << (levels - 1 - i) for i in range(levels))

    chunk_at = jnp.stack([place ^ s ^ turned(t) for s in range(places)]).astype(jnp.int32)

    tied = lax.optimization_barrier(
        (*held[0], got_rows, kept_rows, row_scale, fixed, coef_pull, slot_at, grad_gain, chunk_at)
    )
    held[0] = list(tied[:halves])
    got_rows, kept_rows, row_scale, fixed, coef_pull, slot_at, grad_gain, chunk_at = tied[halves:]

    values, slopes = [], []
    for j in range(PARTS):
        weight = jnp.concatenate(held[j], axis=0)
        value_got = swapped(dot(got_rows, weight).astype(BF16), dp_count).astype(F32)
        value_part = dot(kept_rows, weight) + value_got
        total = value_part[:own_rows]
        for k in range(1, tensor_count):
            part = value_part[k * own_rows : (k + 1) * own_rows].astype(BF16)
            total = total + shifted(part, tensor_count, -k).astype(F32)
        values.append(total * row_scale)

        cols = slice(j * width, (j + 1) * width)
        slope = ((fixed[:, cols] + coef_pull * values[j]) * row_scale).astype(BF16)
        slopes.append(
            jnp.concatenate(
                [slope] + [shifted(slope, tensor_count, k) for k in range(1, tensor_count)], axis=0
            )
        )

    sent = dot(slot_at, jnp.concatenate(values, axis=1).astype(BF16)).astype(BF16)
    policy_values = lax.all_to_all(sent, "dp", split_axis=0, concat_axis=0, tiled=True)

    grads = []
    for j in range(PARTS):
        if j == PARTS - 1:
            slopes[j], policy_values = lax.optimization_barrier((slopes[j], policy_values))
        slopes_got = swapped(slopes[j], dp_count)
        chunks = pl.pallas_call(
            functools.partial(grad_kernel, places),
            grid_spec=pltpu.PrefetchScalarGridSpec(
                num_scalar_prefetch=1,
                grid=(1,),
                in_specs=[
                    pl.BlockSpec((group_rows, shard), lambda i, at: (0, 0)),
                    pl.BlockSpec((group_rows, shard), lambda i, at: (0, 0)),
                    pl.BlockSpec((group_rows, width), lambda i, at: (0, 0)),
                    pl.BlockSpec((group_rows, width), lambda i, at: (0, 0)),
                    pl.BlockSpec((shard, 1), lambda i, at: (0, 0)),
                ],
                out_specs=[pl.BlockSpec((out_rows, width), lambda i, at: (0, 0))] * places,
                scratch_shapes=[pltpu.VMEM((shard, width), F32)],
            ),
            out_shape=[
                jax.ShapeDtypeStruct((out_rows, width), F32 if s == 0 else BF16)
                for s in range(places)
            ],
            compiler_params=pltpu.CompilerParams(vmem_limit_bytes=32 * 2**20),
            cost_estimate=pl.CostEstimate(
                flops=4 * group_rows * shard * width,
                bytes_accessed=4 * 2**20,
                transcendentals=0,
            ),
            name="gradient",
        )(chunk_at, kept_rows, got_rows, slopes[j], slopes_got, grad_gain)
        total = chunks[0]
        for s in range(1, places):
            pairs = [
                (p * cores + c, (p ^ s) * cores + c) for p in range(places) for c in range(cores)
            ]
            total = total + lax.ppermute(chunks[s], "dp", pairs).astype(F32)
        pairs = [
            (flat(p, c, z), flat(z, c, p ^ turned(z)))
            for p in range(places)
            for c in range(cores)
            for z in range(tensor_count)
        ]
        grads.append(lax.ppermute(total.astype(BF16), AXES, pairs))
    grad_weight = jnp.concatenate(grads, axis=1).astype(F32)
    return (policy_values.reshape(1, 1, slot_count, value_width), grad_weight)


def solution(mesh):
    in_specs = (
        P("dp", "tensor"),
        P("tensor"),
        P("tensor", None),
        P(),
        P("dp", None),
        P("dp", "tensor", None),
        P("dp", "tensor", None),
        P("dp", "tensor", None),
        P(("dp", "tensor")),
        P("dp", "tensor", None, None),
    )
    out_specs = (P("dp", "tensor", None, None), P(("dp", "tensor"), None))
    return jax.shard_map(
        on_device, mesh=mesh, in_specs=in_specs, out_specs=out_specs, check_vma=False
    )
```

time: 153 us -> 126 us (0.82)
  the two profiles are of different devices: /device:TPU:3 before, /device:TPU:12 now
where the time goes in v3:
time: 126 us; the launch traced here: 125 us
  starting transfers between devices  57.7 us (46%)
  waiting for transfers between devices  36.8 us (29%)
  other arithmetic  12.1 us (10%)
  Pallas kernels  7.65 us (6%)
  local copies, waits for them, and re-layouts  6.29 us (5%)
  matrix products  3.85 us (3%)
    ppermute x15, starting transfers between devices, shifted(): lax.ppermute(array, 'tensor', [(i, (i + step) % count) for i in range(cou...  24 us
    ppermute x15, waiting for transfers between devices, shifted(): lax.ppermute(array, 'tensor', [(i, (i + step) % count) for i in range(cou...  14.8 us
    ppermute x8, starting transfers between devices, stage(): got = lax.ppermute(held[i], AXES, pairs)  10.6 us
    ppermute x6, waiting for transfers between devices, on_device(): total = total + lax.ppermute(chunks[s], 'dp', pairs).astype(F32)  7.53 us
    ppermute x8, waiting for transfers between devices, stage(): got = lax.ppermute(held[i], AXES, pairs)  7.42 us
    ppermute x6, starting transfers between devices, on_device(): total = total + lax.ppermute(chunks[s], 'dp', pairs).astype(F32)  7.11 us
    all_to_all x1, starting transfers between devices, on_device(): lax.all_to_all(cotangent.reshape(slot_count, value_width), 'dp', split_ax...  6.66 us
    select_n x8, other arithmetic, stage(): result.append(jnp.where(is_getter, got, held[i]))  6.03 us
  transfers between devices with their start and end apart: 38, of which 12 were waited for; matrix products, arithmetic and copies ran while one was open for 10% of the time, Pallas kernels for 6%

profile of v3, /device:TPU:12, one launch (start us, length us, event | category | flops | bytes accessed | tf_op | source)
XLA Modules:
  0.0 125.5 jit_solution(6503303090502899207)
XLA Ops:
  1.6 2.4 %multiply_convert_fusion = (bf16[512,256]{1,0:T(8,128)(2,1)}, bf16[512,256]{1,0:T(8,128)(2,1)}, bf16[512,256]{1,0:T(8,128)(2,1)}, bf16[512,256]{1,0:T(8,128)(2,1)}) fusion(bf16[1024,512]{1,0:T(8,128)(2,1)} %param.14, f32[512]{0:T(512)S(1)} %get-tuple-element.96, f32[512]{0:T(512)S(1)} %get-tuple-element.97), kind=kLoop, calls=%fused_computation.8 | loop fusion | flops 1572864 | bytes 2101248 | tf_op jit(solution)/shard_map/convert_element_type | solution.py:134
  6.7 6.7 %all-to-all-start = ((bf16[8,32,512]{2,1,0:T(8,128)(2,1)}), bf16[8,32,512]{2,1,0:T(8,128)(2,1)}, u32[]{:S(2)}, u32[]{:S(2)}) async-start(bf16[8,32,512]{2,1,0:T(8,128)(2,1)} %bitcast.9), calls=%async_computation | async-start | bytes 524288 | tf_op jit(solution)/shard_map/all_to_all | solution.py:216
  13.9 1.6 %copy-done.1 = bf16[2048,512]{1,0:T(8,128)(2,1)S(1)} copy-done((bf16[2048,512]{1,0:T(8,128)(2,1)S(1)}, bf16[2048,512]{1,0:T(8,128)(2,1)}, u32[]{:S(2)}) %copy-start.1) | copy-done | bytes 2097176
  15.5 3.8 %prepare.1 = (bf16[512,1024]{1,0:T(8,128)(2,1)S(1)}, bf16[512,1024]{1,0:T(8,128)(2,1)S(1)}, bf16[144,512]{1,0:T(8,128)(2,1)S(1)}, bf16[144,512]{1,0:T(8,128)(2,1...) custom-call(s32[2]{0:T(128)S(1)} %pad_add_fusion.at, bf16[512,2048]{1,0:T(8,128)(2,1)S(1)} %copy-done, ...), custom_call_target="tpu_custom_call" | custom-call | flops 1073741824 | bytes 8388608 | tf_op jit(solution)/shard_map/prepare/pallas_call | solution.py:168
  23.6 1.7 %collective-permute-start.5 = (bf16[144,512]{1,0:T(8,128)(2,1)}, bf16[144,512]{1,0:T(8,128)(2,1)S(1)}, u32[]{:S(2)}, u32[]{:S(2)}) collective-permute-start(bf16[144,512]{1,0:T(8,128)(2,1)} %copy-done.5), channel_id=1, source_target_pairs={{0,3},{1,0},{2,1},{3,2},{4,7},{5,4},{6,5},{7,6},{8,11},{9,8},{10,9... | collective-permute-start | bytes 442376 | tf_op jit(solution)/shard_map/ppermute | solution.py:33
  25.3 1.5 %collective-permute-start.6 = (bf16[144,512]{1,0:T(8,128)(2,1)}, bf16[144,512]{1,0:T(8,128)(2,1)S(1)}, u32[]{:S(2)}, u32[]{:S(2)}) collective-permute-start(bf16[144,512]{1,0:T(8,128)(2,1)} %copy-done.4), channel_id=1, source_target_pairs={{0,2},{1,3},{2,0},{3,1},{4,6},{5,7},{6,4},{7,5},{8,10},{9,11},{10,... | collective-permute-start | bytes 442376 | tf_op jit(solution)/shard_map/ppermute | solution.py:33
  26.8 2.3 %collective-permute-start.7 = (bf16[144,512]{1,0:T(8,128)(2,1)S(1)}, bf16[144,512]{1,0:T(8,128)(2,1)S(1)}, u32[]{:S(2)}, u32[]{:S(2)}) collective-permute-start(bf16[144,512]{1,0:T(8,128)(2,1)S(1)} %get-tuple-element.51), channel_id=1, source_target_pairs={{0,1},{1,2},{2,3},{3,0},{4,5},{5,6},{6,7},{7,4},{8,9},{9,10},{10,1... | collective-permute-start | bytes 442376 | tf_op jit(solution)/shard_map/ppermute | solution.py:33
  31.9 5.4 %collective-permute-done.6 = bf16[144,512]{1,0:T(8,128)(2,1)S(1)} collective-permute-done((bf16[144,512]{1,0:T(8,128)(2,1)}, bf16[144,512]{1,0:T(8,128)(2,1)S(1)}, u32[]{:S(2)}, u32[]{:S(2)}) %collective-permute-start.6) | collective-permute-done | bytes 147488 | tf_op jit(solution)/shard_map/ppermute | solution.py:33
  50.4 3.6 %collective-permute-done.9 = bf16[512,256]{1,0:T(8,128)(2,1)S(1)} collective-permute-done((bf16[512,256]{1,0:T(8,128)(2,1)S(1)}, bf16[512,256]{1,0:T(8,128)(2,1)S(1)}, u32[]{:S(2)}, u32[]{:S(2)}) %collective-permute-start.9) | collective-permute-done | bytes 262176 | tf_op jit(solution)/shard_map/ppermute | solution.py:150
  54.6 3.8 %collective-permute-done.11 = bf16[512,256]{1,0:T(8,128)(2,1)S(1)} collective-permute-done((bf16[512,256]{1,0:T(8,128)(2,1)S(1)}, bf16[512,256]{1,0:T(8,128)(2,1)S(1)}, u32[]{:S(2)}, u32[]{:S(2)}) %collective-permute-start.11) | collective-permute-done | bytes 262176 | tf_op jit(solution)/shard_map/ppermute | solution.py:150
  59.4 2.2 %collective-permute-start.20 = (bf16[128,256]{1,0:T(8,128)(2,1)S(1)}, bf16[128,256]{1,0:T(8,128)(2,1)S(1)}, u32[]{:S(2)}, u32[]{:S(2)}) collective-permute-start(bf16[128,256]{1,0:T(8,128)(2,1)S(1)} %get-tuple-element.88), channel_id=1, source_target_pairs={{0,3},{1,0},{2,1},{3,2},{4,7},{5,4},{6,5},{7,6},{8,11},{9,8},{10,9... | collective-permute-start | bytes 196616 | tf_op jit(solution)/shard_map/ppermute | solution.py:33
  62.1 2.7 %collective-permute-start.22 = (bf16[128,256]{1,0:T(8,128)(2,1)S(1)}, bf16[128,256]{1,0:T(8,128)(2,1)S(1)}, u32[]{:S(2)}, u32[]{:S(2)}) collective-permute-start(bf16[128,256]{1,0:T(8,128)(2,1)S(1)} %get-tuple-element.89), channel_id=1, source_target_pairs={{0,1},{1,2},{2,3},{3,0},{4,5},{5,6},{6,7},{7,4},{8,9},{9,10},{10,1... | collective-permute-start | bytes 196616 | tf_op jit(solution)/shard_map/ppermute | solution.py:33
  65.3 1.8 %collective-permute-start.14 = (bf16[128,256]{1,0:T(8,128)(2,1)S(1)}, bf16[128,256]{1,0:T(8,128)(2,1)S(1)}, u32[]{:S(2)}, u32[]{:S(2)}) collective-permute-start(bf16[128,256]{1,0:T(8,128)(2,1)S(1)} %get-tuple-element.93), channel_id=1, source_target_pairs={{0,2},{1,3},{2,0},{3,1},{4,6},{5,7},{6,4},{7,5},{8,10},{9,11},{10,... | collective-permute-start | bytes 196616 | tf_op jit(solution)/shard_map/ppermute | solution.py:33
  67.1 2.1 %collective-permute-start.15 = (bf16[128,256]{1,0:T(8,128)(2,1)S(1)}, bf16[128,256]{1,0:T(8,128)(2,1)S(1)}, u32[]{:S(2)}, u32[]{:S(2)}) collective-permute-start(bf16[128,256]{1,0:T(8,128)(2,1)S(1)} %get-tuple-element.92), channel_id=1, source_target_pairs={{0,1},{1,2},{2,3},{3,0},{4,5},{5,6},{6,7},{7,4},{8,9},{9,10},{10,1... | collective-permute-start | bytes 196616 | tf_op jit(solution)/shard_map/ppermute | solution.py:33
  69.1 2.1 %collective-permute-done.22 = bf16[128,256]{1,0:T(8,128)(2,1)S(1)} collective-permute-done((bf16[128,256]{1,0:T(8,128)(2,1)S(1)}, bf16[128,256]{1,0:T(8,128)(2,1)S(1)}, u32[]{:S(2)}, u32[]{:S(2)}) %collective-permute-start.22) | collective-permute-done | bytes 65568 | tf_op jit(solution)/shard_map/ppermute | solution.py:33
  71.3 2.5 %collective-permute-done.13 = bf16[128,256]{1,0:T(8,128)(2,1)S(1)} collective-permute-done((bf16[128,256]{1,0:T(8,128)(2,1)S(1)}, bf16[128,256]{1,0:T(8,128)(2,1)S(1)}, u32[]{:S(2)}, u32[]{:S(2)}) %collective-permute-start.13) | collective-permute-done | bytes 65568 | tf_op jit(solution)/shard_map/ppermute | solution.py:33
  73.9 2.5 %collective-permute-start.23 = (bf16[128,256]{1,0:T(8,128)(2,1)S(1)}, bf16[128,256]{1,0:T(8,128)(2,1)S(1)}, u32[]{:S(2)}, u32[]{:S(2)}) collective-permute-start(bf16[128,256]{1,0:T(8,128)(2,1)S(1)} %get-tuple-element.87), channel_id=1, source_target_pairs={{0,1},{1,2},{2,3},{3,0},{4,5},{5,6},{6,7},{7,4},{8,9},{9,10},{10,1... | collective-permute-start | bytes 196616 | tf_op jit(solution)/shard_map/ppermute | solution.py:33
  76.4 2.5 %collective-permute-start.24 = (bf16[128,256]{1,0:T(8,128)(2,1)S(1)}, bf16[128,256]{1,0:T(8,128)(2,1)S(1)}, u32[]{:S(2)}, u32[]{:S(2)}) collective-permute-start(bf16[128,256]{1,0:T(8,128)(2,1)S(1)} %get-tuple-element.87), channel_id=1, source_target_pairs={{0,2},{1,3},{2,0},{3,1},{4,6},{5,7},{6,4},{7,5},{8,10},{9,11},{10,... | collective-permute-start | bytes 196616 | tf_op jit(solution)/shard_map/ppermute | solution.py:33
  78.9 2.0 %collective-permute-start.16 = (bf16[128,256]{1,0:T(8,128)(2,1)S(1)}, bf16[128,256]{1,0:T(8,128)(2,1)S(1)}, u32[]{:S(2)}, u32[]{:S(2)}) collective-permute-start(bf16[128,256]{1,0:T(8,128)(2,1)S(1)} %get-tuple-element.85), channel_id=1, source_target_pairs={{0,1},{1,2},{2,3},{3,0},{4,5},{5,6},{6,7},{7,4},{8,9},{9,10},{10,1... | collective-permute-start | bytes 196616 | tf_op jit(solution)/shard_map/ppermute | solution.py:33
  81.0 2.2 %collective-permute-start.17 = (bf16[128,256]{1,0:T(8,128)(2,1)S(1)}, bf16[128,256]{1,0:T(8,128)(2,1)S(1)}, u32[]{:S(2)}, u32[]{:S(2)}) collective-permute-start(bf16[128,256]{1,0:T(8,128)(2,1)S(1)} %get-tuple-element.85), channel_id=1, source_target_pairs={{0,2},{1,3},{2,0},{3,1},{4,6},{5,7},{6,4},{7,5},{8,10},{9,11},{10,... | collective-permute-start | bytes 196616 | tf_op jit(solution)/shard_map/ppermute | solution.py:33
  84.1 5.0 %all-to-all-start.1 = ((bf16[8,32,512]{2,1,0:T(8,128)(2,1)}), bf16[8,32,512]{2,1,0:T(8,128)(2,1)S(1)}, u32[]{:S(2)}, u32[]{:S(2)}) async-start(bf16[8,32,512]{2,1,0:T(8,128)(2,1)} %bitcast.20), calls=%async_computation.1 | async-start | bytes 524288 | tf_op jit(solution)/shard_map/all_to_all | solution.py:281
  89.4 4.0 %collective-permute-done.18 = bf16[128,256]{1,0:T(8,128)(2,1)S(1)} collective-permute-done((bf16[128,256]{1,0:T(8,128)(2,1)S(1)}, bf16[128,256]{1,0:T(8,128)(2,1)S(1)}, u32[]{:S(2)}, u32[]{:S(2)}) %collective-permute-start.18) | collective-permute-done | bytes 65568 | tf_op jit(solution)/shard_map/ppermute | solution.py:33
  95.5 2.4 %gradient.2 = (f32[256,256]{1,0:T(8,128)S(1)}, bf16[256,256]{1,0:T(8,128)(2,1)S(1)}, bf16[256,256]{1,0:T(8,128)(2,1)S(1)}, bf16[256,256]{1,0:T(8,128)(2,1)S(1)}) custom-call(s32[4]{0:T(128)S(1)} %pad_add_fusion.1.at, bf16[512,1024]{1,0:T(8,128)(2,1)S(1)} %get-tuple-element.54.kept_ref, bf16[512,1024]{1,0:T(8,128)(2,1)S(1)} %collective-permute-done.4.got_ref, ...), custom_call_target="tpu_custom_call" | custom-call | flops 536870912 | bytes 4194304 | tf_op jit(solution)/shard_map/gradient/pallas_call | solution.py:288
  98.6 1.5 %collective-permute-start.28 = (bf16[256,256]{1,0:T(8,128)(2,1)S(1)}, bf16[256,256]{1,0:T(8,128)(2,1)S(1)}, u32[]{:S(2)}, u32[]{:S(2)}) collective-permute-start(bf16[256,256]{1,0:T(8,128)(2,1)S(1)} %get-tuple-element.67), channel_id=1, source_target_pairs={{0,16},{4,20},{8,24},{12,28},{16,0},{20,4},{24,8},{28,12},{1,17},{... | collective-permute-start | bytes 393224 | tf_op jit(solution)/shard_map/ppermute | solution.py:320
  100.1 1.5 %collective-permute-start.29 = (bf16[256,256]{1,0:T(8,128)(2,1)S(1)}, bf16[256,256]{1,0:T(8,128)(2,1)S(1)}, u32[]{:S(2)}, u32[]{:S(2)}) collective-permute-start(bf16[256,256]{1,0:T(8,128)(2,1)S(1)} %get-tuple-element.68), channel_id=1, source_target_pairs={{0,24},{4,28},{8,16},{12,20},{16,8},{20,12},{24,0},{28,4},{1,25},{... | collective-permute-start | bytes 393224 | tf_op jit(solution)/shard_map/ppermute | solution.py:320
  101.5 1.5 %gradient.3 = (f32[256,256]{1,0:T(8,128)S(1)}, bf16[256,256]{1,0:T(8,128)(2,1)S(1)}, bf16[256,256]{1,0:T(8,128)(2,1)S(1)}, bf16[256,256]{1,0:T(8,128)(2,1)S(1)}) custom-call(s32[4]{0:T(128)S(1)} %pad_add_fusion.1.at, bf16[512,1024]{1,0:T(8,128)(2,1)S(1)} %get-tuple-element.54.kept_ref, bf16[512,1024]{1,0:T(8,128)(2,1)S(1)} %collective-permute-done.4.got_ref, ...), custom_call_target="tpu_custom_call" | custom-call | flops 536870912 | bytes 4194304 | tf_op jit(solution)/shard_map/gradient/pallas_call | solution.py:288
  103.6 1.5 %collective-permute-start.33 = (bf16[256,256]{1,0:T(8,128)(2,1)S(1)}, bf16[256,256]{1,0:T(8,128)(2,1)S(1)}, u32[]{:S(2)}, u32[]{:S(2)}) collective-permute-start(bf16[256,256]{1,0:T(8,128)(2,1)S(1)} %get-tuple-element.72), channel_id=1, source_target_pairs={{0,16},{4,20},{8,24},{12,28},{16,0},{20,4},{24,8},{28,12},{1,17},{... | collective-permute-start | bytes 393224 | tf_op jit(solution)/shard_map/ppermute | solution.py:320
  106.6 1.5 %collective-permute-done.29 = bf16[256,256]{1,0:T(8,128)(2,1)S(1)} collective-permute-done((bf16[256,256]{1,0:T(8,128)(2,1)S(1)}, bf16[256,256]{1,0:T(8,128)(2,1)S(1)}, u32[]{:S(2)}, u32[]{:S(2)}) %collective-permute-start.29) | collective-permute-done | bytes 131104 | tf_op jit(solution)/shard_map/ppermute | solution.py:320
  108.1 1.9 %collective-permute-start.30 = (bf16[256,256]{1,0:T(8,128)(2,1)S(1)}, bf16[256,256]{1,0:T(8,128)(2,1)S(1)}, u32[]{:S(2)}, u32[]{:S(2)}) collective-permute-start(bf16[256,256]{1,0:T(8,128)(2,1)S(1)} %add_convert_fusion.1), channel_id=1, source_target_pairs={{0,0},{1,10},{2,17},{3,27},{4,4},{5,14},{6,21},{7,31},{8,1},{9,11}... | collective-permute-start | bytes 393224 | tf_op jit(solution)/shard_map/ppermute | solution.py:327
  110.8 5.3 %collective-permute-done.34 = bf16[256,256]{1,0:T(8,128)(2,1)S(1)} collective-permute-done((bf16[256,256]{1,0:T(8,128)(2,1)S(1)}, bf16[256,256]{1,0:T(8,128)(2,1)S(1)}, u32[]{:S(2)}, u32[]{:S(2)}) %collective-permute-start.34) | collective-permute-done | bytes 131104 | tf_op jit(solution)/shard_map/ppermute | solution.py:320
  116.1 1.9 %collective-permute-start.35 = (bf16[256,256]{1,0:T(8,128)(2,1)S(1)}, bf16[256,256]{1,0:T(8,128)(2,1)S(1)}, u32[]{:S(2)}, u32[]{:S(2)}) collective-permute-start(bf16[256,256]{1,0:T(8,128)(2,1)S(1)} %add_convert_fusion), channel_id=1, source_target_pairs={{0,0},{1,10},{2,17},{3,27},{4,4},{5,14},{6,21},{7,31},{8,1},{9,11}... | collective-permute-start | bytes 393224 | tf_op jit(solution)/shard_map/ppermute | solution.py:327
  118.1 5.8 %collective-permute-done.35 = bf16[256,256]{1,0:T(8,128)(2,1)S(1)} collective-permute-done((bf16[256,256]{1,0:T(8,128)(2,1)S(1)}, bf16[256,256]{1,0:T(8,128)(2,1)S(1)}, u32[]{:S(2)}, u32[]{:S(2)}) %collective-permute-start.35) | collective-permute-done | bytes 131104 | tf_op jit(solution)/shard_map/ppermute | solution.py:327
  (116 shorter events, 35.3 us)
Async XLA Ops:
  4.0 17.6 %collective-permute-start.1 = (bf16[512,256]{1,0:T(8,128)(2,1)}, bf16[512,256]{1,0:T(8,128)(2,1)}, u32[]{:S(2)}, u32[]{:S(2)}) collective-permute-start(bf16[512,256]{1,0:T(8,128)(2,1)} %get-tuple-element.77), channel_id=1, source_target_pairs={{0,16},{9,25},{18,2},{27,11},{4,20},{13,29},{22,6},{31,15}} | collective-permute-start | bytes 786440 | tf_op jit(solution)/shard_map/ppermute | solution.py:150
  5.4 17.2 %collective-permute-start = (bf16[512,256]{1,0:T(8,128)(2,1)}, bf16[512,256]{1,0:T(8,128)(2,1)}, u32[]{:S(2)}, u32[]{:S(2)}) collective-permute-start(bf16[512,256]{1,0:T(8,128)(2,1)} %get-tuple-element.80), channel_id=1, source_target_pairs={{0,8},{9,1},{18,26},{27,19},{4,12},{13,5},{22,30},{31,23}} | collective-permute-start | bytes 786440 | tf_op jit(solution)/shard_map/ppermute | solution.py:150
  6.7 35.8 %all-to-all-start = ((bf16[8,32,512]{2,1,0:T(8,128)(2,1)}), bf16[8,32,512]{2,1,0:T(8,128)(2,1)}, u32[]{:S(2)}, u32[]{:S(2)}) async-start(bf16[8,32,512]{2,1,0:T(8,128)(2,1)} %bitcast.9), calls=%async_computation | async-start | bytes 524288 | tf_op jit(solution)/shard_map/all_to_all | solution.py:216
  23.6 7.0 %collective-permute-start.5 = (bf16[144,512]{1,0:T(8,128)(2,1)}, bf16[144,512]{1,0:T(8,128)(2,1)S(1)}, u32[]{:S(2)}, u32[]{:S(2)}) collective-permute-start(bf16[144,512]{1,0:T(8,128)(2,1)} %copy-done.5), channel_id=1, source_target_pairs={{0,3},{1,0},{2,1},{3,2},{4,7},{5,4},{6,5},{7,6},{8,11},{9,8},{10,9... | collective-permute-start | bytes 442376 | tf_op jit(solution)/shard_map/ppermute | solution.py:33
  25.3 12.0 %collective-permute-start.6 = (bf16[144,512]{1,0:T(8,128)(2,1)}, bf16[144,512]{1,0:T(8,128)(2,1)S(1)}, u32[]{:S(2)}, u32[]{:S(2)}) collective-permute-start(bf16[144,512]{1,0:T(8,128)(2,1)} %copy-done.4), channel_id=1, source_target_pairs={{0,2},{1,3},{2,0},{3,1},{4,6},{5,7},{6,4},{7,5},{8,10},{9,11},{10,... | collective-permute-start | bytes 442376 | tf_op jit(solution)/shard_map/ppermute | solution.py:33
  26.8 12.6 %collective-permute-start.7 = (bf16[144,512]{1,0:T(8,128)(2,1)S(1)}, bf16[144,512]{1,0:T(8,128)(2,1)S(1)}, u32[]{:S(2)}, u32[]{:S(2)}) collective-permute-start(bf16[144,512]{1,0:T(8,128)(2,1)S(1)} %get-tuple-element.51), channel_id=1, source_target_pairs={{0,1},{1,2},{2,3},{3,0},{4,5},{5,6},{6,7},{7,4},{8,9},{9,10},{10,1... | collective-permute-start | bytes 442376 | tf_op jit(solution)/shard_map/ppermute | solution.py:33
  29.2 19.1 %collective-permute-start.3 = (bf16[512,256]{1,0:T(8,128)(2,1)S(1)}, bf16[512,256]{1,0:T(8,128)(2,1)}, u32[]{:S(2)}, u32[]{:S(2)}) collective-permute-start(bf16[512,256]{1,0:T(8,128)(2,1)S(1)} %broadcast_select_fusion.3), channel_id=1, source_target_pairs={{0,8},{9,1},{18,26},{27,19},{4,12},{13,5},{22,30},{31,23},{16,24},... | collective-permute-start | bytes 786440 | tf_op jit(solution)/shard_map/ppermute | solution.py:150
  30.5 23.5 %collective-permute-start.4 = (bf16[512,1024]{1,0:T(8,128)(2,1)}, bf16[512,1024]{1,0:T(8,128)(2,1)S(1)}, u32[]{:S(2)}, u32[]{:S(2)}) collective-permute-start(bf16[512,1024]{1,0:T(8,128)(2,1)} %copy-done.3), channel_id=1, source_target_pairs={{0,4},{4,0},{8,12},{12,8},{16,20},{20,16},{24,28},{28,24},{1,5},{5... | collective-permute-start | bytes 3145736 | tf_op jit(solution)/shard_map/ppermute | solution.py:29
  30.6 18.8 %collective-permute-start.2 = (bf16[512,256]{1,0:T(8,128)(2,1)S(1)}, bf16[512,256]{1,0:T(8,128)(2,1)}, u32[]{:S(2)}, u32[]{:S(2)}) collective-permute-start(bf16[512,256]{1,0:T(8,128)(2,1)S(1)} %broadcast_select_fusion.5), channel_id=1, source_target_pairs={{0,16},{9,25},{18,2},{27,11},{4,20},{13,29},{22,6},{31,15},{8,24},... | collective-permute-start | bytes 786440 | tf_op jit(solution)/shard_map/ppermute | solution.py:150
  37.3 6.4 %collective-permute-start.8 = (bf16[512,256]{1,0:T(8,128)(2,1)}, bf16[512,256]{1,0:T(8,128)(2,1)}, u32[]{:S(2)}, u32[]{:S(2)}) collective-permute-start(bf16[512,256]{1,0:T(8,128)(2,1)} %get-tuple-element.55), channel_id=1, source_target_pairs={{0,8},{9,1},{18,26},{27,19},{4,12},{13,5},{22,30},{31,23}} | collective-permute-start | bytes 786440 | tf_op jit(solution)/shard_map/ppermute | solution.py:150
  44.7 9.3 %collective-permute-start.9 = (bf16[512,256]{1,0:T(8,128)(2,1)S(1)}, bf16[512,256]{1,0:T(8,128)(2,1)S(1)}, u32[]{:S(2)}, u32[]{:S(2)}) collective-permute-start(bf16[512,256]{1,0:T(8,128)(2,1)S(1)} %broadcast_select_fusion.4), channel_id=1, source_target_pairs={{0,16},{9,25},{18,2},{27,11},{4,20},{13,29},{22,6},{31,15},{8,24},... | collective-permute-start | bytes 786440 | tf_op jit(solution)/shard_map/ppermute | solution.py:150
  47.0 11.4 %collective-permute-start.11 = (bf16[512,256]{1,0:T(8,128)(2,1)S(1)}, bf16[512,256]{1,0:T(8,128)(2,1)S(1)}, u32[]{:S(2)}, u32[]{:S(2)}) collective-permute-start(bf16[512,256]{1,0:T(8,128)(2,1)S(1)} %broadcast_select_fusion.2), channel_id=1, source_target_pairs={{0,8},{9,1},{18,26},{27,19},{4,12},{13,5},{22,30},{31,23},{16,24},... | collective-permute-start | bytes 786440 | tf_op jit(solution)/shard_map/ppermute | solution.py:150
  59.4 7.7 %collective-permute-start.20 = (bf16[128,256]{1,0:T(8,128)(2,1)S(1)}, bf16[128,256]{1,0:T(8,128)(2,1)S(1)}, u32[]{:S(2)}, u32[]{:S(2)}) collective-permute-start(bf16[128,256]{1,0:T(8,128)(2,1)S(1)} %get-tuple-element.88), channel_id=1, source_target_pairs={{0,3},{1,0},{2,1},{3,2},{4,7},{5,4},{6,5},{7,6},{8,11},{9,8},{10,9... | collective-permute-start | bytes 196616 | tf_op jit(solution)/shard_map/ppermute | solution.py:33
  61.6 7.5 %collective-permute-start.21 = (bf16[128,256]{1,0:T(8,128)(2,1)S(1)}, bf16[128,256]{1,0:T(8,128)(2,1)S(1)}, u32[]{:S(2)}, u32[]{:S(2)}) collective-permute-start(bf16[128,256]{1,0:T(8,128)(2,1)S(1)} %get-tuple-element.90), channel_id=1, source_target_pairs={{0,2},{1,3},{2,0},{3,1},{4,6},{5,7},{6,4},{7,5},{8,10},{9,11},{10,... | collective-permute-start | bytes 196616 | tf_op jit(solution)/shard_map/ppermute | solution.py:33
  62.1 9.2 %collective-permute-start.22 = (bf16[128,256]{1,0:T(8,128)(2,1)S(1)}, bf16[128,256]{1,0:T(8,128)(2,1)S(1)}, u32[]{:S(2)}, u32[]{:S(2)}) collective-permute-start(bf16[128,256]{1,0:T(8,128)(2,1)S(1)} %get-tuple-element.89), channel_id=1, source_target_pairs={{0,1},{1,2},{2,3},{3,0},{4,5},{5,6},{6,7},{7,4},{8,9},{9,10},{10,1... | collective-permute-start | bytes 196616 | tf_op jit(solution)/shard_map/ppermute | solution.py:33
  65.2 8.5 %collective-permute-start.13 = (bf16[128,256]{1,0:T(8,128)(2,1)S(1)}, bf16[128,256]{1,0:T(8,128)(2,1)S(1)}, u32[]{:S(2)}, u32[]{:S(2)}) collective-permute-start(bf16[128,256]{1,0:T(8,128)(2,1)S(1)} %get-tuple-element.91), channel_id=1, source_target_pairs={{0,3},{1,0},{2,1},{3,2},{4,7},{5,4},{6,5},{7,6},{8,11},{9,8},{10,9... | collective-permute-start | bytes 196616 | tf_op jit(solution)/shard_map/ppermute | solution.py:33
  65.3 8.5 %collective-permute-start.14 = (bf16[128,256]{1,0:T(8,128)(2,1)S(1)}, bf16[128,256]{1,0:T(8,128)(2,1)S(1)}, u32[]{:S(2)}, u32[]{:S(2)}) collective-permute-start(bf16[128,256]{1,0:T(8,128)(2,1)S(1)} %get-tuple-element.93), channel_id=1, source_target_pairs={{0,2},{1,3},{2,0},{3,1},{4,6},{5,7},{6,4},{7,5},{8,10},{9,11},{10,... | collective-permute-start | bytes 196616 | tf_op jit(solution)/shard_map/ppermute | solution.py:33
  67.1 6.7 %collective-permute-start.15 = (bf16[128,256]{1,0:T(8,128)(2,1)S(1)}, bf16[128,256]{1,0:T(8,128)(2,1)S(1)}, u32[]{:S(2)}, u32[]{:S(2)}) collective-permute-start(bf16[128,256]{1,0:T(8,128)(2,1)S(1)} %get-tuple-element.92), channel_id=1, source_target_pairs={{0,1},{1,2},{2,3},{3,0},{4,5},{5,6},{6,7},{7,4},{8,9},{9,10},{10,1... | collective-permute-start | bytes 196616 | tf_op jit(solution)/shard_map/ppermute | solution.py:33
  73.9 15.2 %collective-permute-start.23 = (bf16[128,256]{1,0:T(8,128)(2,1)S(1)}, bf16[128,256]{1,0:T(8,128)(2,1)S(1)}, u32[]{:S(2)}, u32[]{:S(2)}) collective-permute-start(bf16[128,256]{1,0:T(8,128)(2,1)S(1)} %get-tuple-element.87), channel_id=1, source_target_pairs={{0,1},{1,2},{2,3},{3,0},{4,5},{5,6},{6,7},{7,4},{8,9},{9,10},{10,1... | collective-permute-start | bytes 196616 | tf_op jit(solution)/shard_map/ppermute | solution.py:33
  76.4 12.7 %collective-permute-start.24 = (bf16[128,256]{1,0:T(8,128)(2,1)S(1)}, bf16[128,256]{1,0:T(8,128)(2,1)S(1)}, u32[]{:S(2)}, u32[]{:S(2)}) collective-permute-start(bf16[128,256]{1,0:T(8,128)(2,1)S(1)} %get-tuple-element.87), channel_id=1, source_target_pairs={{0,2},{1,3},{2,0},{3,1},{4,6},{5,7},{6,4},{7,5},{8,10},{9,11},{10,... | collective-permute-start | bytes 196616 | tf_op jit(solution)/shard_map/ppermute | solution.py:33
  78.9 10.2 %collective-permute-start.25 = (bf16[128,256]{1,0:T(8,128)(2,1)S(1)}, bf16[128,256]{1,0:T(8,128)(2,1)S(1)}, u32[]{:S(2)}, u32[]{:S(2)}) collective-permute-start(bf16[128,256]{1,0:T(8,128)(2,1)S(1)} %get-tuple-element.87), channel_id=1, source_target_pairs={{0,3},{1,0},{2,1},{3,2},{4,7},{5,4},{6,5},{7,6},{8,11},{9,8},{10,9... | collective-permute-start | bytes 196616 | tf_op jit(solution)/shard_map/ppermute | solution.py:33
  78.9 10.4 %collective-permute-start.16 = (bf16[128,256]{1,0:T(8,128)(2,1)S(1)}, bf16[128,256]{1,0:T(8,128)(2,1)S(1)}, u32[]{:S(2)}, u32[]{:S(2)}) collective-permute-start(bf16[128,256]{1,0:T(8,128)(2,1)S(1)} %get-tuple-element.85), channel_id=1, source_target_pairs={{0,1},{1,2},{2,3},{3,0},{4,5},{5,6},{6,7},{7,4},{8,9},{9,10},{10,1... | collective-permute-start | bytes 196616 | tf_op jit(solution)/shard_map/ppermute | solution.py:33
  81.0 8.4 %collective-permute-start.17 = (bf16[128,256]{1,0:T(8,128)(2,1)S(1)}, bf16[128,256]{1,0:T(8,128)(2,1)S(1)}, u32[]{:S(2)}, u32[]{:S(2)}) collective-permute-start(bf16[128,256]{1,0:T(8,128)(2,1)S(1)} %get-tuple-element.85), channel_id=1, source_target_pairs={{0,2},{1,3},{2,0},{3,1},{4,6},{5,7},{6,4},{7,5},{8,10},{9,11},{10,... | collective-permute-start | bytes 196616 | tf_op jit(solution)/shard_map/ppermute | solution.py:33
  84.1 10.5 %all-to-all-start.1 = ((bf16[8,32,512]{2,1,0:T(8,128)(2,1)}), bf16[8,32,512]{2,1,0:T(8,128)(2,1)S(1)}, u32[]{:S(2)}, u32[]{:S(2)}) async-start(bf16[8,32,512]{2,1,0:T(8,128)(2,1)} %bitcast.20), calls=%async_computation.1 | async-start | bytes 524288 | tf_op jit(solution)/shard_map/all_to_all | solution.py:281
  98.0 7.1 %collective-permute-start.27 = (bf16[256,256]{1,0:T(8,128)(2,1)S(1)}, bf16[256,256]{1,0:T(8,128)(2,1)S(1)}, u32[]{:S(2)}, u32[]{:S(2)}) collective-permute-start(bf16[256,256]{1,0:T(8,128)(2,1)S(1)} %get-tuple-element.66), channel_id=1, source_target_pairs={{0,8},{4,12},{8,0},{12,4},{16,24},{20,28},{24,16},{28,20},{1,9},{5... | collective-permute-start | bytes 393224 | tf_op jit(solution)/shard_map/ppermute | solution.py:320
  98.6 8.0 %collective-permute-start.28 = (bf16[256,256]{1,0:T(8,128)(2,1)S(1)}, bf16[256,256]{1,0:T(8,128)(2,1)S(1)}, u32[]{:S(2)}, u32[]{:S(2)}) collective-permute-start(bf16[256,256]{1,0:T(8,128)(2,1)S(1)} %get-tuple-element.67), channel_id=1, source_target_pairs={{0,16},{4,20},{8,24},{12,28},{16,0},{20,4},{24,8},{28,12},{1,17},{... | collective-permute-start | bytes 393224 | tf_op jit(solution)/shard_map/ppermute | solution.py:320
  100.1 8.0 %collective-permute-start.29 = (bf16[256,256]{1,0:T(8,128)(2,1)S(1)}, bf16[256,256]{1,0:T(8,128)(2,1)S(1)}, u32[]{:S(2)}, u32[]{:S(2)}) collective-permute-start(bf16[256,256]{1,0:T(8,128)(2,1)S(1)} %get-tuple-element.68), channel_id=1, source_target_pairs={{0,24},{4,28},{8,16},{12,20},{16,8},{20,12},{24,0},{28,4},{1,25},{... | collective-permute-start | bytes 393224 | tf_op jit(solution)/shard_map/ppermute | solution.py:320
  103.0 7.1 %collective-permute-start.32 = (bf16[256,256]{1,0:T(8,128)(2,1)S(1)}, bf16[256,256]{1,0:T(8,128)(2,1)S(1)}, u32[]{:S(2)}, u32[]{:S(2)}) collective-permute-start(bf16[256,256]{1,0:T(8,128)(2,1)S(1)} %get-tuple-element.71), channel_id=1, source_target_pairs={{0,8},{4,12},{8,0},{12,4},{16,24},{20,28},{24,16},{28,20},{1,9},{5... | collective-permute-start | bytes 393224 | tf_op jit(solution)/shard_map/ppermute | solution.py:320
  103.6 7.2 %collective-permute-start.33 = (bf16[256,256]{1,0:T(8,128)(2,1)S(1)}, bf16[256,256]{1,0:T(8,128)(2,1)S(1)}, u32[]{:S(2)}, u32[]{:S(2)}) collective-permute-start(bf16[256,256]{1,0:T(8,128)(2,1)S(1)} %get-tuple-element.72), channel_id=1, source_target_pairs={{0,16},{4,20},{8,24},{12,28},{16,0},{20,4},{24,8},{28,12},{1,17},{... | collective-permute-start | bytes 393224 | tf_op jit(solution)/shard_map/ppermute | solution.py:320
  105.1 11.0 %collective-permute-start.34 = (bf16[256,256]{1,0:T(8,128)(2,1)S(1)}, bf16[256,256]{1,0:T(8,128)(2,1)S(1)}, u32[]{:S(2)}, u32[]{:S(2)}) collective-permute-start(bf16[256,256]{1,0:T(8,128)(2,1)S(1)} %get-tuple-element.73), channel_id=1, source_target_pairs={{0,24},{4,28},{8,16},{12,20},{16,8},{20,12},{24,0},{28,4},{1,25},{... | collective-permute-start | bytes 393224 | tf_op jit(solution)/shard_map/ppermute | solution.py:320
  108.1 10.0 %collective-permute-start.30 = (bf16[256,256]{1,0:T(8,128)(2,1)S(1)}, bf16[256,256]{1,0:T(8,128)(2,1)S(1)}, u32[]{:S(2)}, u32[]{:S(2)}) collective-permute-start(bf16[256,256]{1,0:T(8,128)(2,1)S(1)} %add_convert_fusion.1), channel_id=1, source_target_pairs={{0,0},{1,10},{2,17},{3,27},{4,4},{5,14},{6,21},{7,31},{8,1},{9,11}... | collective-permute-start | bytes 393224 | tf_op jit(solution)/shard_map/ppermute | solution.py:327
  116.1 7.8 %collective-permute-start.35 = (bf16[256,256]{1,0:T(8,128)(2,1)S(1)}, bf16[256,256]{1,0:T(8,128)(2,1)S(1)}, u32[]{:S(2)}, u32[]{:S(2)}) collective-permute-start(bf16[256,256]{1,0:T(8,128)(2,1)S(1)} %add_convert_fusion), channel_id=1, source_target_pairs={{0,0},{1,10},{2,17},{3,27},{4,4},{5,14},{6,21},{7,31},{8,1},{9,11}... | collective-permute-start | bytes 393224 | tf_op jit(solution)/shard_map/ppermute | solution.py:327
  (20 other events, 144.1 us)

commit v4 on v3

--- a/solution.py
+++ b/solution.py
@@ -33,24 +33,26 @@
     return lax.ppermute(array, "tensor", [(i, (i + step) % count) for i in range(count)])
 
 
-def prepare_kernel(count, steps, at, x_ref, gain_ref, weight_ref, given_ref, kept_ref, *refs):
+def prepare_kernel(
+    count, steps, at, x_ref, gain_ref, weight_ref, pol_ref, given_ref, kept_ref, *refs
+):
     sent_refs, (rows_ref, total, square) = refs[:count], refs[count:]
     f = pl.program_id(0)
     own = x_ref.shape[0] // count
     for k in range(count):
         source = lax.rem(at[0] - k + count, count)
         rows_ref[k * own : (k + 1) * own, :] = x_ref[pl.ds(pl.multiple_of(source * own, own), own), :]
-    rows = rows_ref[...]
+    wide = rows_ref[...].astype(F32)
+    gained = (wide * pol_ref[...]).astype(BF16)
 
     @pl.when(f < steps // 2)
     def _():
-        given_ref[...] = rows
+        given_ref[...] = gained
 
     @pl.when(f >= steps // 2)
     def _():
-        kept_ref[...] = rows
-
-    wide = rows.astype(F32)
+        kept_ref[...] = gained
+
     part = dot((wide * gain_ref[...]).astype(BF16), weight_ref[...])
     squares = jnp.sum(wide * wide, axis=1, keepdims=True)
 
@@ -76,10 +78,43 @@
             sent[own:, :own] = jnp.concatenate([high, low], axis=0).astype(BF16)
 
 
-def grad_kernel(places, at, kept_ref, got_ref, slope_ref, slope_got_ref, gain_ref, *refs):
+def select_kernel(at, *refs):
+    count = len(refs) // 3
+    for i in range(count):
+        held_ref, got_ref, out_ref = refs[i], refs[count + i], refs[2 * count + i]
+
+        @pl.when(at[i] > 0)
+        def _():
+            out_ref[...] = got_ref[...]
+
+        @pl.when(at[i] <= 0)
+        def _():
+            out_ref[...] = held_ref[...]
+
+
+def value_kernel(at, got_rows_ref, kept_rows_ref, *refs):
+    given_ref, kept_ref, weight = refs[-3:]
+    count = (len(refs) - 3) // 2
+    rows = weight.shape[0] // count
+    for i in range(count):
+        held_ref, got_ref = refs[i], refs[count + i]
+
+        @pl.when(at[i] > 0)
+        def _():
+            weight[i * rows : (i + 1) * rows, :] = got_ref[...]
+
+        @pl.when(at[i] <= 0)
+        def _():
+            weight[i * rows : (i + 1) * rows, :] = held_ref[...]
+
+    given_ref[...] = dot(got_rows_ref[...], weight[...]).astype(BF16)
+    kept_ref[...] = dot(kept_rows_ref[...], weight[...])
+
+
+def grad_kernel(places, factor, at, kept_ref, got_ref, slope_ref, slope_got_ref, *refs):
     out_refs, grad = refs[:places], refs[places]
     total = dot_rows(kept_ref[...], slope_ref[...]) + dot_rows(got_ref[...], slope_got_ref[...])
-    grad[...] = total * gain_ref[...]
+    grad[...] = total * factor
     rows = out_refs[0].shape[0]
     for s in range(places):
         chunk = grad[pl.ds(pl.multiple_of(at[s] * rows, rows), rows), :]
@@ -126,15 +161,9 @@
 
     halves = 2
     half_rows = shard // halves
-    gain_shard = lax.dynamic_slice_in_dim(pol_gain, d * shard, shard, 0)
-
-    def first(j, i):
-        rows = slice(i * half_rows, (i + 1) * half_rows)
-        piece = pol_weight[rows, j * width : (j + 1) * width].astype(F32)
-        return (piece * gain_shard[rows, None]).astype(BF16)
 
     def stage(number, held):
-        result = []
+        got, is_getter = [], []
         for i in range(halves):
             holders = [0]
             for before in range(number):
@@ -147,15 +176,40 @@
                 for c in range(cores)
                 for z in range(tensor_count)
             ]
-            got = lax.ppermute(held[i], AXES, pairs)
-            is_getter = jnp.zeros((), jnp.bool_)
-            for q in holders:
-                is_getter = is_getter | (relative == (q ^ bit))
-            result.append(jnp.where(is_getter, got, held[i]))
-        return result
-
-    held = [[first(j, i) for i in range(halves)] for j in range(PARTS)]
-    held[0] = stage(0, held[0])
+            got.append(lax.ppermute(held[i], AXES, pairs))
+            is_getter.append(functools.reduce(jnp.logical_or, [relative == (q ^ bit) for q in holders]))
+        return got, jnp.stack(is_getter).astype(jnp.int32)
+
+    def whole(shape):
+        return pl.BlockSpec(shape, lambda i, at: (0,) * len(shape))
+
+    def select(held, got, is_getter):
+        shape = (half_rows, width)
+        return list(
+            pl.pallas_call(
+                select_kernel,
+                grid_spec=pltpu.PrefetchScalarGridSpec(
+                    num_scalar_prefetch=1,
+                    grid=(1,),
+                    in_specs=[whole(shape)] * (2 * halves),
+                    out_specs=[whole(shape)] * halves,
+                ),
+                out_shape=[jax.ShapeDtypeStruct(shape, BF16)] * halves,
+                cost_estimate=pl.CostEstimate(flops=0, bytes_accessed=2**20, transcendentals=0),
+                name="select",
+            )(is_getter, *held, *got)
+        )
+
+    held = [
+        [
+            pol_weight[i * half_rows : (i + 1) * half_rows, j * width : (j + 1) * width]
+            for i in range(halves)
+        ]
+        for j in range(PARTS)
+    ]
+    got = [None] * PARTS
+    flags = [None] * PARTS
+    got[0], flags[0] = stage(0, held[0])
 
     steps = 4
     feature_step = block // steps
@@ -174,6 +228,9 @@
                 pl.BlockSpec((group_rows, feature_step), lambda f, at: (0, at_step(f, at))),
                 pl.BlockSpec((1, feature_step), lambda f, at: (0, at_step(f, at))),
                 pl.BlockSpec((feature_step, value_width), lambda f, at: (at_step(f, at), 0)),
+                pl.BlockSpec(
+                    (1, feature_step), lambda f, at: (0, at[0] * steps + at_step(f, at))
+                ),
             ],
             out_specs=[
                 pl.BlockSpec(
@@ -192,30 +249,33 @@
         ),
         out_shape=[jax.ShapeDtypeStruct((group_rows, shard), BF16)] * 2
         + [jax.ShapeDtypeStruct(sent_shape, BF16)] * tensor_count,
-        compiler_params=pltpu.CompilerParams(vmem_limit_bytes=32 * 2**20),
+        compiler_params=pltpu.CompilerParams(vmem_limit_bytes=56 * 2**20),
         cost_estimate=pl.CostEstimate(
             flops=2 * group_rows * block * value_width,
             bytes_accessed=8 * 2**20,
             transcendentals=0,
         ),
         name="prepare",
-    )(at, tokens, ref_gain.reshape(1, block), ref_weight)
+    )(at, tokens, ref_gain.reshape(1, block), ref_weight, pol_gain.reshape(1, model_width))
     given_rows, kept_rows, *ref_sent = prepared
 
-    tied = lax.optimization_barrier((*held[0], *held[1], given_rows, kept_rows, *ref_sent))
-    held[0], held[1] = list(tied[:halves]), list(tied[halves : 2 * halves])
-    given_rows, kept_rows, *ref_sent = tied[2 * halves :]
     ref_got = [ref_sent[0]] + [
         shifted(ref_sent[k], tensor_count, -k) for k in range(1, tensor_count)
     ]
+    got_rows = swapped(given_rows, dp_count)
+
+    cot = cotangent.reshape(slot_count, value_width)
+    tied = lax.optimization_barrier((*got[0], *held[1], kept_rows, cot))
+    got[0], held[1] = list(tied[:halves]), list(tied[halves : 2 * halves])
+    kept_rows, cot = tied[2 * halves :]
     for number in range(1, levels):
-        held[0] = stage(number, held[0])
-    for number in range(levels):
-        held[1] = stage(number, held[1])
-    got_rows = swapped(given_rows, dp_count)
-    got_cot = lax.all_to_all(
-        cotangent.reshape(slot_count, value_width), "dp", split_axis=0, concat_axis=0, tiled=True
-    )
+        held[0] = select(held[0], got[0], flags[0])
+        got[0], flags[0] = stage(number, held[0])
+    got[1], flags[1] = stage(0, held[1])
+    for number in range(1, levels):
+        held[1] = select(held[1], got[1], flags[1])
+        got[1], flags[1] = stage(number, held[1])
+    got_cot = lax.all_to_all(cot, "dp", split_axis=0, concat_axis=0, tiled=True)
 
     seq_lens = lengths.reshape(-1)
     seq_bins = bins.reshape(-1)
@@ -244,25 +304,36 @@
     row_scale = lax.rsqrt(square_sum / model_width + EPS)[:, None]
     ref_values = (ref_total[:own_rows] * row_scale).astype(BF16).astype(F32)
     fixed = coef_adv * upstream - coef_pull * ref_values
-    gain_block = lax.dynamic_slice_in_dim(pol_gain, t * block + core * shard, shard, 0)
-    grad_gain = (gain_block * factor)[:, None]
 
     def turned(z):
         return sum(((z >> i) & 1) << (levels - 1 - i) for i in range(levels))
 
     chunk_at = jnp.stack([place ^ s ^ turned(t) for s in range(places)]).astype(jnp.int32)
 
-    tied = lax.optimization_barrier(
-        (*held[0], got_rows, kept_rows, row_scale, fixed, coef_pull, slot_at, grad_gain, chunk_at)
-    )
-    held[0] = list(tied[:halves])
-    got_rows, kept_rows, row_scale, fixed, coef_pull, slot_at, grad_gain, chunk_at = tied[halves:]
-
     values, slopes = [], []
     for j in range(PARTS):
-        weight = jnp.concatenate(held[j], axis=0)
-        value_got = swapped(dot(got_rows, weight).astype(BF16), dp_count).astype(F32)
-        value_part = dot(kept_rows, weight) + value_got
+        value_given, value_kept = pl.pallas_call(
+            value_kernel,
+            grid_spec=pltpu.PrefetchScalarGridSpec(
+                num_scalar_prefetch=1,
+                grid=(1,),
+                in_specs=[whole((group_rows, shard))] * 2 + [whole((half_rows, width))] * 2 * halves,
+                out_specs=[whole((group_rows, width))] * 2,
+                scratch_shapes=[pltpu.VMEM((shard, width), BF16)],
+            ),
+            out_shape=[
+                jax.ShapeDtypeStruct((group_rows, width), BF16),
+                jax.ShapeDtypeStruct((group_rows, width), F32),
+            ],
+            compiler_params=pltpu.CompilerParams(vmem_limit_bytes=32 * 2**20),
+            cost_estimate=pl.CostEstimate(
+                flops=4 * group_rows * shard * width,
+                bytes_accessed=4 * 2**20,
+                transcendentals=0,
+            ),
+            name="values",
+        )(flags[j], got_rows, kept_rows, *held[j], *got[j])
+        value_part = value_kept + swapped(value_given, dp_count).astype(F32)
         total = value_part[:own_rows]
         for k in range(1, tensor_count):
             part = value_part[k * own_rows : (k + 1) * own_rows].astype(BF16)
@@ -278,15 +349,12 @@
         )
 
     sent = dot(slot_at, jnp.concatenate(values, axis=1).astype(BF16)).astype(BF16)
-    policy_values = lax.all_to_all(sent, "dp", split_axis=0, concat_axis=0, tiled=True)
 
     grads = []
     for j in range(PARTS):
-        if j == PARTS - 1:
-            slopes[j], policy_values = lax.optimization_barrier((slopes[j], policy_values))
         slopes_got = swapped(slopes[j], dp_count)
         chunks = pl.pallas_call(
-            functools.partial(grad_kernel, places),
+            functools.partial(grad_kernel, places, factor),
             grid_spec=pltpu.PrefetchScalarGridSpec(
                 num_scalar_prefetch=1,
                 grid=(1,),
@@ -295,7 +363,6 @@
                     pl.BlockSpec((group_rows, shard), lambda i, at: (0, 0)),
                     pl.BlockSpec((group_rows, width), lambda i, at: (0, 0)),
                     pl.BlockSpec((group_rows, width), lambda i, at: (0, 0)),
-                    pl.BlockSpec((shard, 1), lambda i, at: (0, 0)),
                 ],
                 out_specs=[pl.BlockSpec((out_rows, width), lambda i, at: (0, 0))] * places,
                 scratch_shapes=[pltpu.VMEM((shard, width), F32)],
@@ -311,20 +378,24 @@
                 transcendentals=0,
             ),
             name="gradient",
-        )(chunk_at, kept_rows, got_rows, slopes[j], slopes_got, grad_gain)
+        )(chunk_at, kept_rows, got_rows, slopes[j], slopes_got)
         total = chunks[0]
         for s in range(1, places):
             pairs = [
                 (p * cores + c, (p ^ s) * cores + c) for p in range(places) for c in range(cores)
             ]
             total = total + lax.ppermute(chunks[s], "dp", pairs).astype(F32)
+        total = total.astype(BF16)
+        if j == 0:
+            total, sent = lax.optimization_barrier((total, sent))
+            policy_values = lax.all_to_all(sent, "dp", split_axis=0, concat_axis=0, tiled=True)
         pairs = [
             (flat(p, c, z), flat(z, c, p ^ turned(z)))
             for p in range(places)
             for c in range(cores)
             for z in range(tensor_count)
         ]
-        grads.append(lax.ppermute(total.astype(BF16), AXES, pairs))
+        grads.append(lax.ppermute(total, AXES, pairs))
     grad_weight = jnp.concatenate(grads, axis=1).astype(F32)
     return (policy_values.reshape(1, 1, slot_count, value_width), grad_weight)
 

time: 126 us -> 143 us (1.13)
  the two profiles are of different devices: /device:TPU:12 before, /device:TPU:0 now
where the time goes in v4:
time: 143 us; the launch traced here: 142 us
  starting transfers between devices  63.9 us (45%)
  waiting for transfers between devices  33.7 us (24%)
  Pallas kernels  19.5 us (14%)
  other arithmetic  14.2 us (10%)
  local copies, waits for them, and re-layouts  7.63 us (5%)
  matrix products  2.1 us (1%)
    ppermute x8, starting transfers between devices, stage(): got.append(lax.ppermute(held[i], AXES, pairs))  23.7 us
    ppermute x15, starting transfers between devices, shifted(): lax.ppermute(array, 'tensor', [(i, (i + step) % count) for i in range(cou...  17.8 us
    ppermute x15, waiting for transfers between devices, shifted(): lax.ppermute(array, 'tensor', [(i, (i + step) % count) for i in range(cou...  16 us
    all_to_all x1, starting transfers between devices, on_device(): lax.all_to_all(sent, 'dp', split_axis=0, concat_axis=0, tiled=True)  8.85 us
    ppermute x6, starting transfers between devices, on_device(): total = total + lax.ppermute(chunks[s], 'dp', pairs).astype(F32)  7.38 us
    pallas_call x1, Pallas kernels, on_device(): pl.pallas_call(functools.partial(prepare_kernel, tensor_count, steps), gr...  7.06 us
    ppermute x6, waiting for transfers between devices, on_device(): total = total + lax.ppermute(chunks[s], 'dp', pairs).astype(F32)  6.33 us
    all_to_all x1, waiting for transfers between devices, on_device(): lax.all_to_all(sent, 'dp', split_axis=0, concat_axis=0, tiled=True)  6.06 us
  transfers between devices with their start and end apart: 38, of which 15 were waited for; matrix products, arithmetic and copies ran while one was open for 11% of the time, Pallas kernels for 14%

profile of v4, /device:TPU:0, one launch (start us, length us, event | category | flops | bytes accessed | tf_op | source)
XLA Modules:
  0.0 142.2 jit_solution(4630396704898507823)
XLA Ops:
  0.6 2.0 %fusion.24 = (bf16[512,256]{1,0:T(8,128)(2,1)S(1)}, bf16[512,256]{1,0:T(8,128)(2,1)S(1)}, bf16[512,256]{1,0:T(8,128)(2,1)S(1)}, bf16[512,256]{1,0:T(8,128)(2,1)}) fusion(bf16[1024,512]{1,0:T(8,128)(2,1)} %param.14), kind=kLoop, calls=%fused_computation.57 | loop fusion | bytes 2097152 | tf_op jit(solution)/shard_map/slice | solution.py:205
  2.6 4.9 %collective-permute-start = (bf16[512,256]{1,0:T(8,128)(2,1)S(1)}, bf16[512,256]{1,0:T(8,128)(2,1)S(1)}, u32[]{:S(2)}, u32[]{:S(2)}) collective-permute-start(bf16[512,256]{1,0:T(8,128)(2,1)S(1)} %get-tuple-element.70.refs_0_), channel_id=1, source_target_pairs={{0,8},{9,1},{18,26},{27,19},{4,12},{13,5},{22,30},{31,23}} | collective-permute-start | bytes 786440 | tf_op jit(solution)/shard_map/ppermute | solution.py:179
  9.4 7.1 %prepare.1 = (bf16[512,1024]{1,0:T(8,128)(2,1)}, bf16[512,1024]{1,0:T(8,128)(2,1)}, bf16[144,512]{1,0:T(8,128)(2,1)}, bf16[144,512]{1,0:T(8,128)(2,1)}, bf16[144...) custom-call(s32[2]{0:T(128)} %pad_add_fusion.1.at, bf16[512,2048]{1,0:T(8,128)(2,1)} %x_ref.1, f32[1,2048]{1,0:T(1,128)} %bitcast.31, ...), custom_call_target="tpu_custom_call" | custom-call | flops 1073741824 | bytes 8388608 | tf_op jit(solution)/shard_map/prepare/pallas_call | solution.py:222
  22.3 3.1 %collective-permute-start.3 = (bf16[144,512]{1,0:T(8,128)(2,1)}, bf16[144,512]{1,0:T(8,128)(2,1)}, u32[]{:S(2)}, u32[]{:S(2)}) collective-permute-start(bf16[144,512]{1,0:T(8,128)(2,1)} %get-tuple-element.37), channel_id=1, source_target_pairs={{0,3},{1,0},{2,1},{3,2},{4,7},{5,4},{6,5},{7,6},{8,11},{9,8},{10,9... | collective-permute-start | bytes 442376 | tf_op jit(solution)/shard_map/ppermute | solution.py:33
  28.0 2.7 %select.8 = (bf16[512,256]{1,0:T(8,128)(2,1)}, bf16[512,256]{1,0:T(8,128)(2,1)}) custom-call(s32[2]{0:T(128)} %add_convert_fusion.3.at, bf16[512,256]{1,0:T(8,128)(2,1)} %copy-done.10, bf16[512,256]{1,0:T(8,128)(2,1)} %copy-done.9, bf16[512,256]{1,0:T(8,128)(2,1)} %copy-done.11, bf16[512,256]{1,0:T(8,128)(2,1)} %copy-done.12), custom_call_target="tpu_custom_call" | custom-call | bytes 1048576 | tf_op jit(solution)/shard_map/select/pallas_call | solution.py:189
  30.7 5.2 %collective-permute-start.6 = (bf16[512,256]{1,0:T(8,128)(2,1)}, bf16[512,256]{1,0:T(8,128)(2,1)S(1)}, u32[]{:S(2)}, u32[]{:S(2)}) collective-permute-start(bf16[512,256]{1,0:T(8,128)(2,1)} %get-tuple-element.42.refs_0_), channel_id=1, source_target_pairs={{0,16},{9,25},{18,2},{27,11},{4,20},{13,29},{22,6},{31,15},{8,24},... | collective-permute-start | bytes 786440 | tf_op jit(solution)/shard_map/ppermute | solution.py:179
  37.2 2.0 %collective-permute-start.19 = (bf16[512,256]{1,0:T(8,128)(2,1)}, bf16[512,256]{1,0:T(8,128)(2,1)}, u32[]{:S(2)}, u32[]{:S(2)}) collective-permute-start(bf16[512,256]{1,0:T(8,128)(2,1)} %get-tuple-element.50.refs_0_), channel_id=1, source_target_pairs={{0,8},{9,1},{18,26},{27,19},{4,12},{13,5},{22,30},{31,23}} | collective-permute-start | bytes 786440 | tf_op jit(solution)/shard_map/ppermute | solution.py:179
  39.3 2.0 %collective-permute-start.20 = (bf16[512,256]{1,0:T(8,128)(2,1)S(1)}, bf16[512,256]{1,0:T(8,128)(2,1)}, u32[]{:S(2)}, u32[]{:S(2)}) collective-permute-start(bf16[512,256]{1,0:T(8,128)(2,1)S(1)} %get-tuple-element.51.refs_1_), channel_id=1, source_target_pairs={{0,16},{9,25},{18,2},{27,11},{4,20},{13,29},{22,6},{31,15}} | collective-permute-start | bytes 786440 | tf_op jit(solution)/shard_map/ppermute | solution.py:179
  41.3 1.9 %convert_add_fusion.2 = f32[144,512]{1,0:T(8,128)} fusion(bf16[144,512]{1,0:T(8,128)(2,1)} %collective-permute-done.5, bf16[144,512]{1,0:T(8,128)(2,1)} %copy-done.13, bf16[144,512]{1,0:T(8,128)(2,1)} %collective-permute-done.3, bf16[144,512]{1,0:T(8,128)(2,1)} %get-tuple-element.36), kind=kLoop, calls=%fused_computation.5 | loop fusion | flops 516096 | bytes 884736 | tf_op jit(solution)/shard_map/add | solution.py:301
  43.2 5.2 %collective-permute-done.19.refs_2_ = bf16[512,256]{1,0:T(8,128)(2,1)} collective-permute-done((bf16[512,256]{1,0:T(8,128)(2,1)}, bf16[512,256]{1,0:T(8,128)(2,1)}, u32[]{:S(2)}, u32[]{:S(2)}) %collective-permute-start.19) | collective-permute-done | bytes 262176 | tf_op jit(solution)/shard_map/ppermute | solution.py:179
  48.5 2.7 %select.9 = (bf16[512,256]{1,0:T(8,128)(2,1)}, bf16[512,256]{1,0:T(8,128)(2,1)}) custom-call(s32[2]{0:T(128)} %add_convert_fusion.3.at, bf16[512,256]{1,0:T(8,128)(2,1)} %get-tuple-element.50.refs_0_, bf16[512,256]{1,0:T(8,128)(2,1)} %copy-done.8, bf16[512,256]{1,0:T(8,128)(2,1)} %collective-permute-done.19.refs_2_, ...), custom_call_target="tpu_custom_call" | custom-call | bytes 1048576 | tf_op jit(solution)/shard_map/select/pallas_call | solution.py:189
  51.1 3.8 %collective-permute-start.21 = (bf16[512,256]{1,0:T(8,128)(2,1)}, bf16[512,256]{1,0:T(8,128)(2,1)}, u32[]{:S(2)}, u32[]{:S(2)}) collective-permute-start(bf16[512,256]{1,0:T(8,128)(2,1)} %get-tuple-element.52.refs_0_), channel_id=1, source_target_pairs={{0,16},{9,25},{18,2},{27,11},{4,20},{13,29},{22,6},{31,15},{8,24},... | collective-permute-start | bytes 786440 | tf_op jit(solution)/shard_map/ppermute | solution.py:179
  54.9 3.3 %collective-permute-start.22 = (bf16[512,256]{1,0:T(8,128)(2,1)}, bf16[512,256]{1,0:T(8,128)(2,1)}, u32[]{:S(2)}, u32[]{:S(2)}) collective-permute-start(bf16[512,256]{1,0:T(8,128)(2,1)} %get-tuple-element.53.refs_1_), channel_id=1, source_target_pairs={{0,8},{9,1},{18,26},{27,19},{4,12},{13,5},{22,30},{31,23},{16,24},... | collective-permute-start | bytes 786440 | tf_op jit(solution)/shard_map/ppermute | solution.py:179
  59.9 2.0 %values.2 = (bf16[512,256]{1,0:T(8,128)(2,1)}, f32[512,256]{1,0:T(8,128)S(1)}) custom-call(s32[2]{0:T(128)S(1)} %add_convert_fusion.2.at, bf16[512,1024]{1,0:T(8,128)(2,1)S(1)} %collective-permute-done.2.got_rows_ref.got_ref, bf16[512,1024]{1,0:T(8,128)(2,1)S(1)} %copy-done, bf16[512,256]{1,0:T(8,128)(2,1)S(1)} %copy-done.1, bf16[512,256]{1,0:T(8,128)(2,1)S(1)} %copy-done.2, ...), custom_call_target="tpu_custom_call" | custom-call | flops 536870912 | bytes 4194304 | tf_op jit(solution)/shard_map/values/pallas_call | solution.py:315
  62.6 4.1 %all-to-all-start = ((bf16[8,32,512]{2,1,0:T(8,128)(2,1)}), bf16[8,32,512]{2,1,0:T(8,128)(2,1)}, u32[]{:S(2)}, u32[]{:S(2)}) async-start(bf16[8,32,512]{2,1,0:T(8,128)(2,1)} %bitcast.29), calls=%async_computation | async-start | bytes 524288 | tf_op jit(solution)/shard_map/all_to_all | solution.py:278
  68.6 2.3 %values.3 = (bf16[512,256]{1,0:T(8,128)(2,1)S(1)}, f32[512,256]{1,0:T(8,128)S(1)}) custom-call(s32[2]{0:T(128)S(1)} %add_convert_fusion.2.at, bf16[512,1024]{1,0:T(8,128)(2,1)S(1)} %collective-permute-done.2.got_rows_ref.got_ref, bf16[512,1024]{1,0:T(8,128)(2,1)S(1)} %copy-done, bf16[512,256]{1,0:T(8,128)(2,1)S(1)} %copy-done.5, ...), custom_call_target="tpu_custom_call" | custom-call | flops 536870912 | bytes 4194304 | tf_op jit(solution)/shard_map/values/pallas_call | solution.py:315
  71.5 1.8 %fusion.23 = (bf16[512,256]{1,0:T(8,128)(2,1)S(1)}, f32[512,256]{1,0:T(8,128)}) fusion(f32[512,256]{1,0:T(8,128)S(1)} %get-tuple-element.44, bf16[512,256]{1,0:T(8,128)(2,1)} %collective-permute-done.8), kind=kLoop, calls=%fused_computation.56 | loop fusion | flops 393216 | bytes 1572864 | tf_op jit(solution)/shard_map/convert.7
  73.4 3.7 %collective-permute-start.9 = (bf16[128,256]{1,0:T(8,128)(2,1)S(1)}, bf16[128,256]{1,0:T(8,128)(2,1)}, u32[]{:S(2)}, u32[]{:S(2)}) collective-permute-start(bf16[128,256]{1,0:T(8,128)(2,1)S(1)} %get-tuple-element.81), channel_id=1, source_target_pairs={{0,3},{1,0},{2,1},{3,2},{4,7},{5,4},{6,5},{7,6},{8,11},{9,8},{10,9... | collective-permute-start | bytes 196616 | tf_op jit(solution)/shard_map/ppermute | solution.py:33
  80.8 2.2 %collective-permute-start.24 = (bf16[128,256]{1,0:T(8,128)(2,1)S(1)}, bf16[128,256]{1,0:T(8,128)(2,1)}, u32[]{:S(2)}, u32[]{:S(2)}) collective-permute-start(bf16[128,256]{1,0:T(8,128)(2,1)S(1)} %get-tuple-element.78), channel_id=1, source_target_pairs={{0,3},{1,0},{2,1},{3,2},{4,7},{5,4},{6,5},{7,6},{8,11},{9,8},{10,9... | collective-permute-start | bytes 196616 | tf_op jit(solution)/shard_map/ppermute | solution.py:33
  84.3 3.3 %collective-permute-done.25 = bf16[128,256]{1,0:T(8,128)(2,1)} collective-permute-done((bf16[128,256]{1,0:T(8,128)(2,1)S(1)}, bf16[128,256]{1,0:T(8,128)(2,1)}, u32[]{:S(2)}, u32[]{:S(2)}) %collective-permute-start.25) | collective-permute-done | bytes 65568 | tf_op jit(solution)/shard_map/ppermute | solution.py:33
  88.8 1.9 %collective-permute-start.14 = (bf16[128,256]{1,0:T(8,128)(2,1)S(1)}, bf16[128,256]{1,0:T(8,128)(2,1)S(1)}, u32[]{:S(2)}, u32[]{:S(2)}) collective-permute-start(bf16[128,256]{1,0:T(8,128)(2,1)S(1)} %get-tuple-element.75), channel_id=1, source_target_pairs={{0,3},{1,0},{2,1},{3,2},{4,7},{5,4},{6,5},{7,6},{8,11},{9,8},{10,9... | collective-permute-start | bytes 196616 | tf_op jit(solution)/shard_map/ppermute | solution.py:33
  91.7 1.7 %collective-permute-done.14 = bf16[128,256]{1,0:T(8,128)(2,1)S(1)} collective-permute-done((bf16[128,256]{1,0:T(8,128)(2,1)S(1)}, bf16[128,256]{1,0:T(8,128)(2,1)S(1)}, u32[]{:S(2)}, u32[]{:S(2)}) %collective-permute-start.14) | collective-permute-done | bytes 65568 | tf_op jit(solution)/shard_map/ppermute | solution.py:33
  93.4 3.6 %collective-permute-done.13 = bf16[128,256]{1,0:T(8,128)(2,1)S(1)} collective-permute-done((bf16[128,256]{1,0:T(8,128)(2,1)S(1)}, bf16[128,256]{1,0:T(8,128)(2,1)S(1)}, u32[]{:S(2)}, u32[]{:S(2)}) %collective-permute-start.13) | collective-permute-done | bytes 65568 | tf_op jit(solution)/shard_map/ppermute | solution.py:33
  98.8 1.9 %collective-permute-start.28 = (bf16[128,256]{1,0:T(8,128)(2,1)S(1)}, bf16[128,256]{1,0:T(8,128)(2,1)S(1)}, u32[]{:S(2)}, u32[]{:S(2)}) collective-permute-start(bf16[128,256]{1,0:T(8,128)(2,1)S(1)} %get-tuple-element.77), channel_id=1, source_target_pairs={{0,1},{1,2},{2,3},{3,0},{4,5},{5,6},{6,7},{7,4},{8,9},{9,10},{10,1... | collective-permute-start | bytes 196616 | tf_op jit(solution)/shard_map/ppermute | solution.py:33
  100.8 1.5 %collective-permute-done.30 = bf16[128,256]{1,0:T(8,128)(2,1)S(1)} collective-permute-done((bf16[128,256]{1,0:T(8,128)(2,1)S(1)}, bf16[128,256]{1,0:T(8,128)(2,1)S(1)}, u32[]{:S(2)}, u32[]{:S(2)}) %collective-permute-start.30) | collective-permute-done | bytes 65568 | tf_op jit(solution)/shard_map/ppermute | solution.py:33
  102.4 4.3 %collective-permute-done.29 = bf16[128,256]{1,0:T(8,128)(2,1)S(1)} collective-permute-done((bf16[128,256]{1,0:T(8,128)(2,1)S(1)}, bf16[128,256]{1,0:T(8,128)(2,1)S(1)}, u32[]{:S(2)}, u32[]{:S(2)}) %collective-permute-start.29) | collective-permute-done | bytes 65568 | tf_op jit(solution)/shard_map/ppermute | solution.py:33
  108.1 3.2 %collective-permute-start.18 = (bf16[256,256]{1,0:T(8,128)(2,1)S(1)}, bf16[256,256]{1,0:T(8,128)(2,1)S(1)}, u32[]{:S(2)}, u32[]{:S(2)}) collective-permute-start(bf16[256,256]{1,0:T(8,128)(2,1)S(1)} %get-tuple-element.49), channel_id=1, source_target_pairs={{0,24},{4,28},{8,16},{12,20},{16,8},{20,12},{24,0},{28,4},{1,25},{... | collective-permute-start | bytes 393224 | tf_op jit(solution)/shard_map/ppermute | solution.py:387
  114.3 2.9 %collective-permute-start.34 = (bf16[256,256]{1,0:T(8,128)(2,1)S(1)}, bf16[256,256]{1,0:T(8,128)(2,1)S(1)}, u32[]{:S(2)}, u32[]{:S(2)}) collective-permute-start(bf16[256,256]{1,0:T(8,128)(2,1)S(1)} %get-tuple-element.61), channel_id=1, source_target_pairs={{0,24},{4,28},{8,16},{12,20},{16,8},{20,12},{24,0},{28,4},{1,25},{... | collective-permute-start | bytes 393224 | tf_op jit(solution)/shard_map/ppermute | solution.py:387
  119.1 2.6 %collective-permute-done.34 = bf16[256,256]{1,0:T(8,128)(2,1)S(1)} collective-permute-done((bf16[256,256]{1,0:T(8,128)(2,1)S(1)}, bf16[256,256]{1,0:T(8,128)(2,1)S(1)}, u32[]{:S(2)}, u32[]{:S(2)}) %collective-permute-start.34) | collective-permute-done | bytes 131104 | tf_op jit(solution)/shard_map/ppermute | solution.py:387
  121.6 2.3 %collective-permute-done.33 = bf16[256,256]{1,0:T(8,128)(2,1)S(1)} collective-permute-done((bf16[256,256]{1,0:T(8,128)(2,1)S(1)}, bf16[256,256]{1,0:T(8,128)(2,1)S(1)}, u32[]{:S(2)}, u32[]{:S(2)}) %collective-permute-start.33) | collective-permute-done | bytes 131104 | tf_op jit(solution)/shard_map/ppermute | solution.py:387
  125.7 8.9 %all-to-all-start.1 = ((bf16[8,32,512]{2,1,0:T(8,128)(2,1)}), bf16[8,32,512]{2,1,0:T(8,128)(2,1)S(1)}, u32[]{:S(2)}, u32[]{:S(2)}) async-start(bf16[8,32,512]{2,1,0:T(8,128)(2,1)} %bitcast.21), calls=%async_computation.1 | async-start | bytes 524288 | tf_op jit(solution)/shard_map/all_to_all | solution.py:391
  135.4 6.1 %all-to-all-done.1 = bf16[8,32,512]{2,1,0:T(8,128)(2,1)S(1)} async-done(((bf16[8,32,512]{2,1,0:T(8,128)(2,1)}), bf16[8,32,512]{2,1,0:T(8,128)(2,1)S(1)}, u32[]{:S(2)}, u32[]{:S(2)}) %all-to-all-start.1) | async-done | bytes 262176 | tf_op jit(solution)/shard_map/all_to_all | solution.py:391
  (113 shorter events, 35.3 us)
Async XLA Ops:
  2.6 19.7 %collective-permute-start = (bf16[512,256]{1,0:T(8,128)(2,1)S(1)}, bf16[512,256]{1,0:T(8,128)(2,1)S(1)}, u32[]{:S(2)}, u32[]{:S(2)}) collective-permute-start(bf16[512,256]{1,0:T(8,128)(2,1)S(1)} %get-tuple-element.70.refs_0_), channel_id=1, source_target_pairs={{0,8},{9,1},{18,26},{27,19},{4,12},{13,5},{22,30},{31,23}} | collective-permute-start | bytes 786440 | tf_op jit(solution)/shard_map/ppermute | solution.py:179
  7.5 19.8 %collective-permute-start.1 = (bf16[512,256]{1,0:T(8,128)(2,1)S(1)}, bf16[512,256]{1,0:T(8,128)(2,1)S(1)}, u32[]{:S(2)}, u32[]{:S(2)}) collective-permute-start(bf16[512,256]{1,0:T(8,128)(2,1)S(1)} %get-tuple-element.69.refs_1_), channel_id=1, source_target_pairs={{0,16},{9,25},{18,2},{27,11},{4,20},{13,29},{22,6},{31,15}} | collective-permute-start | bytes 786440 | tf_op jit(solution)/shard_map/ppermute | solution.py:179
  16.5 42.4 %collective-permute-start.2 = (bf16[512,1024]{1,0:T(8,128)(2,1)}, bf16[512,1024]{1,0:T(8,128)(2,1)S(1)}, u32[]{:S(2)}, u32[]{:S(2)}) collective-permute-start(bf16[512,1024]{1,0:T(8,128)(2,1)} %get-tuple-element.34), channel_id=1, source_target_pairs={{0,4},{4,0},{8,12},{12,8},{16,20},{20,16},{24,28},{28,24},{1,5},{5... | collective-permute-start | bytes 3145736 | tf_op jit(solution)/shard_map/ppermute | solution.py:29
  16.6 19.3 %collective-permute-start.5 = (bf16[144,512]{1,0:T(8,128)(2,1)}, bf16[144,512]{1,0:T(8,128)(2,1)}, u32[]{:S(2)}, u32[]{:S(2)}) collective-permute-start(bf16[144,512]{1,0:T(8,128)(2,1)} %get-tuple-element.39), channel_id=1, source_target_pairs={{0,1},{1,2},{2,3},{3,0},{4,5},{5,6},{6,7},{7,4},{8,9},{9,10},{10,1... | collective-permute-start | bytes 442376 | tf_op jit(solution)/shard_map/ppermute | solution.py:33
  16.7 20.5 %collective-permute-start.4 = (bf16[144,512]{1,0:T(8,128)(2,1)}, bf16[144,512]{1,0:T(8,128)(2,1)S(1)}, u32[]{:S(2)}, u32[]{:S(2)}) collective-permute-start(bf16[144,512]{1,0:T(8,128)(2,1)} %get-tuple-element.38), channel_id=1, source_target_pairs={{0,2},{1,3},{2,0},{3,1},{4,6},{5,7},{6,4},{7,5},{8,10},{9,11},{10,... | collective-permute-start | bytes 442376 | tf_op jit(solution)/shard_map/ppermute | solution.py:33
  22.3 16.9 %collective-permute-start.3 = (bf16[144,512]{1,0:T(8,128)(2,1)}, bf16[144,512]{1,0:T(8,128)(2,1)}, u32[]{:S(2)}, u32[]{:S(2)}) collective-permute-start(bf16[144,512]{1,0:T(8,128)(2,1)} %get-tuple-element.37), channel_id=1, source_target_pairs={{0,3},{1,0},{2,1},{3,2},{4,7},{5,4},{6,5},{7,6},{8,11},{9,8},{10,9... | collective-permute-start | bytes 442376 | tf_op jit(solution)/shard_map/ppermute | solution.py:33
  30.7 27.5 %collective-permute-start.6 = (bf16[512,256]{1,0:T(8,128)(2,1)}, bf16[512,256]{1,0:T(8,128)(2,1)S(1)}, u32[]{:S(2)}, u32[]{:S(2)}) collective-permute-start(bf16[512,256]{1,0:T(8,128)(2,1)} %get-tuple-element.42.refs_0_), channel_id=1, source_target_pairs={{0,16},{9,25},{18,2},{27,11},{4,20},{13,29},{22,6},{31,15},{8,24},... | collective-permute-start | bytes 786440 | tf_op jit(solution)/shard_map/ppermute | solution.py:179
  35.9 22.3 %collective-permute-start.7 = (bf16[512,256]{1,0:T(8,128)(2,1)}, bf16[512,256]{1,0:T(8,128)(2,1)S(1)}, u32[]{:S(2)}, u32[]{:S(2)}) collective-permute-start(bf16[512,256]{1,0:T(8,128)(2,1)} %get-tuple-element.43.refs_1_), channel_id=1, source_target_pairs={{0,8},{9,1},{18,26},{27,19},{4,12},{13,5},{22,30},{31,23},{16,24},... | collective-permute-start | bytes 786440 | tf_op jit(solution)/shard_map/ppermute | solution.py:179
  37.2 11.2 %collective-permute-start.19 = (bf16[512,256]{1,0:T(8,128)(2,1)}, bf16[512,256]{1,0:T(8,128)(2,1)}, u32[]{:S(2)}, u32[]{:S(2)}) collective-permute-start(bf16[512,256]{1,0:T(8,128)(2,1)} %get-tuple-element.50.refs_0_), channel_id=1, source_target_pairs={{0,8},{9,1},{18,26},{27,19},{4,12},{13,5},{22,30},{31,23}} | collective-permute-start | bytes 786440 | tf_op jit(solution)/shard_map/ppermute | solution.py:179
  39.3 9.2 %collective-permute-start.20 = (bf16[512,256]{1,0:T(8,128)(2,1)S(1)}, bf16[512,256]{1,0:T(8,128)(2,1)}, u32[]{:S(2)}, u32[]{:S(2)}) collective-permute-start(bf16[512,256]{1,0:T(8,128)(2,1)S(1)} %get-tuple-element.51.refs_1_), channel_id=1, source_target_pairs={{0,16},{9,25},{18,2},{27,11},{4,20},{13,29},{22,6},{31,15}} | collective-permute-start | bytes 786440 | tf_op jit(solution)/shard_map/ppermute | solution.py:179
  51.1 15.5 %collective-permute-start.21 = (bf16[512,256]{1,0:T(8,128)(2,1)}, bf16[512,256]{1,0:T(8,128)(2,1)}, u32[]{:S(2)}, u32[]{:S(2)}) collective-permute-start(bf16[512,256]{1,0:T(8,128)(2,1)} %get-tuple-element.52.refs_0_), channel_id=1, source_target_pairs={{0,16},{9,25},{18,2},{27,11},{4,20},{13,29},{22,6},{31,15},{8,24},... | collective-permute-start | bytes 786440 | tf_op jit(solution)/shard_map/ppermute | solution.py:179
  54.9 11.8 %collective-permute-start.22 = (bf16[512,256]{1,0:T(8,128)(2,1)}, bf16[512,256]{1,0:T(8,128)(2,1)}, u32[]{:S(2)}, u32[]{:S(2)}) collective-permute-start(bf16[512,256]{1,0:T(8,128)(2,1)} %get-tuple-element.53.refs_1_), channel_id=1, source_target_pairs={{0,8},{9,1},{18,26},{27,19},{4,12},{13,5},{22,30},{31,23},{16,24},... | collective-permute-start | bytes 786440 | tf_op jit(solution)/shard_map/ppermute | solution.py:179
  61.9 9.6 %collective-permute-start.8 = (bf16[512,256]{1,0:T(8,128)(2,1)}, bf16[512,256]{1,0:T(8,128)(2,1)}, u32[]{:S(2)}, u32[]{:S(2)}) collective-permute-start(bf16[512,256]{1,0:T(8,128)(2,1)} %get-tuple-element.45), channel_id=1, source_target_pairs={{0,4},{4,0},{8,12},{12,8},{16,20},{20,16},{24,28},{28,24},{1,5},{5... | collective-permute-start | bytes 786440 | tf_op jit(solution)/shard_map/ppermute | solution.py:29
  62.6 20.3 %all-to-all-start = ((bf16[8,32,512]{2,1,0:T(8,128)(2,1)}), bf16[8,32,512]{2,1,0:T(8,128)(2,1)}, u32[]{:S(2)}, u32[]{:S(2)}) async-start(bf16[8,32,512]{2,1,0:T(8,128)(2,1)} %bitcast.29), calls=%async_computation | async-start | bytes 524288 | tf_op jit(solution)/shard_map/all_to_all | solution.py:278
  73.3 6.8 %collective-permute-start.11 = (bf16[128,256]{1,0:T(8,128)(2,1)S(1)}, bf16[128,256]{1,0:T(8,128)(2,1)S(1)}, u32[]{:S(2)}, u32[]{:S(2)}) collective-permute-start(bf16[128,256]{1,0:T(8,128)(2,1)S(1)} %get-tuple-element.82), channel_id=1, source_target_pairs={{0,1},{1,2},{2,3},{3,0},{4,5},{5,6},{6,7},{7,4},{8,9},{9,10},{10,1... | collective-permute-start | bytes 196616 | tf_op jit(solution)/shard_map/ppermute | solution.py:33
  73.4 10.8 %collective-permute-start.10 = (bf16[128,256]{1,0:T(8,128)(2,1)S(1)}, bf16[128,256]{1,0:T(8,128)(2,1)}, u32[]{:S(2)}, u32[]{:S(2)}) collective-permute-start(bf16[128,256]{1,0:T(8,128)(2,1)S(1)} %get-tuple-element.83), channel_id=1, source_target_pairs={{0,2},{1,3},{2,0},{3,1},{4,6},{5,7},{6,4},{7,5},{8,10},{9,11},{10,... | collective-permute-start | bytes 196616 | tf_op jit(solution)/shard_map/ppermute | solution.py:33
  73.4 10.7 %collective-permute-start.9 = (bf16[128,256]{1,0:T(8,128)(2,1)S(1)}, bf16[128,256]{1,0:T(8,128)(2,1)}, u32[]{:S(2)}, u32[]{:S(2)}) collective-permute-start(bf16[128,256]{1,0:T(8,128)(2,1)S(1)} %get-tuple-element.81), channel_id=1, source_target_pairs={{0,3},{1,0},{2,1},{3,2},{4,7},{5,4},{6,5},{7,6},{8,11},{9,8},{10,9... | collective-permute-start | bytes 196616 | tf_op jit(solution)/shard_map/ppermute | solution.py:33
  77.3 7.0 %collective-permute-start.26 = (bf16[128,256]{1,0:T(8,128)(2,1)S(1)}, bf16[128,256]{1,0:T(8,128)(2,1)}, u32[]{:S(2)}, u32[]{:S(2)}) collective-permute-start(bf16[128,256]{1,0:T(8,128)(2,1)S(1)} %get-tuple-element.79), channel_id=1, source_target_pairs={{0,1},{1,2},{2,3},{3,0},{4,5},{5,6},{6,7},{7,4},{8,9},{9,10},{10,1... | collective-permute-start | bytes 196616 | tf_op jit(solution)/shard_map/ppermute | solution.py:33
  77.9 9.7 %collective-permute-start.25 = (bf16[128,256]{1,0:T(8,128)(2,1)S(1)}, bf16[128,256]{1,0:T(8,128)(2,1)}, u32[]{:S(2)}, u32[]{:S(2)}) collective-permute-start(bf16[128,256]{1,0:T(8,128)(2,1)S(1)} %get-tuple-element.80), channel_id=1, source_target_pairs={{0,2},{1,3},{2,0},{3,1},{4,6},{5,7},{6,4},{7,5},{8,10},{9,11},{10,... | collective-permute-start | bytes 196616 | tf_op jit(solution)/shard_map/ppermute | solution.py:33
  80.8 6.9 %collective-permute-start.24 = (bf16[128,256]{1,0:T(8,128)(2,1)S(1)}, bf16[128,256]{1,0:T(8,128)(2,1)}, u32[]{:S(2)}, u32[]{:S(2)}) collective-permute-start(bf16[128,256]{1,0:T(8,128)(2,1)S(1)} %get-tuple-element.78), channel_id=1, source_target_pairs={{0,3},{1,0},{2,1},{3,2},{4,7},{5,4},{6,5},{7,6},{8,11},{9,8},{10,9... | collective-permute-start | bytes 196616 | tf_op jit(solution)/shard_map/ppermute | solution.py:33
  97.8 9.0 %collective-permute-start.15 = (bf16[512,256]{1,0:T(8,128)(2,1)S(1)}, bf16[512,256]{1,0:T(8,128)(2,1)S(1)}, u32[]{:S(2)}, u32[]{:S(2)}) collective-permute-start(bf16[512,256]{1,0:T(8,128)(2,1)S(1)} %pad_maximum_fusion.slope_ref), channel_id=1, source_target_pairs={{0,4},{4,0},{8,12},{12,8},{16,20},{20,16},{24,28},{28,24},{1,5},{5... | collective-permute-start | bytes 786440 | tf_op jit(solution)/shard_map/ppermute | solution.py:29
  98.8 7.9 %collective-permute-start.29 = (bf16[128,256]{1,0:T(8,128)(2,1)S(1)}, bf16[128,256]{1,0:T(8,128)(2,1)S(1)}, u32[]{:S(2)}, u32[]{:S(2)}) collective-permute-start(bf16[128,256]{1,0:T(8,128)(2,1)S(1)} %get-tuple-element.77), channel_id=1, source_target_pairs={{0,2},{1,3},{2,0},{3,1},{4,6},{5,7},{6,4},{7,5},{8,10},{9,11},{10,... | collective-permute-start | bytes 196616 | tf_op jit(solution)/shard_map/ppermute | solution.py:33
  98.8 7.8 %collective-permute-start.28 = (bf16[128,256]{1,0:T(8,128)(2,1)S(1)}, bf16[128,256]{1,0:T(8,128)(2,1)S(1)}, u32[]{:S(2)}, u32[]{:S(2)}) collective-permute-start(bf16[128,256]{1,0:T(8,128)(2,1)S(1)} %get-tuple-element.77), channel_id=1, source_target_pairs={{0,1},{1,2},{2,3},{3,0},{4,5},{5,6},{6,7},{7,4},{8,9},{9,10},{10,1... | collective-permute-start | bytes 196616 | tf_op jit(solution)/shard_map/ppermute | solution.py:33
  108.1 9.6 %collective-permute-start.18 = (bf16[256,256]{1,0:T(8,128)(2,1)S(1)}, bf16[256,256]{1,0:T(8,128)(2,1)S(1)}, u32[]{:S(2)}, u32[]{:S(2)}) collective-permute-start(bf16[256,256]{1,0:T(8,128)(2,1)S(1)} %get-tuple-element.49), channel_id=1, source_target_pairs={{0,24},{4,28},{8,16},{12,20},{16,8},{20,12},{24,0},{28,4},{1,25},{... | collective-permute-start | bytes 393224 | tf_op jit(solution)/shard_map/ppermute | solution.py:387
  111.3 7.4 %collective-permute-start.17 = (bf16[256,256]{1,0:T(8,128)(2,1)S(1)}, bf16[256,256]{1,0:T(8,128)(2,1)S(1)}, u32[]{:S(2)}, u32[]{:S(2)}) collective-permute-start(bf16[256,256]{1,0:T(8,128)(2,1)S(1)} %get-tuple-element.48), channel_id=1, source_target_pairs={{0,16},{4,20},{8,24},{12,28},{16,0},{20,4},{24,8},{28,12},{1,17},{... | collective-permute-start | bytes 393224 | tf_op jit(solution)/shard_map/ppermute | solution.py:387
  111.9 7.1 %collective-permute-start.16 = (bf16[256,256]{1,0:T(8,128)(2,1)S(1)}, bf16[256,256]{1,0:T(8,128)(2,1)S(1)}, u32[]{:S(2)}, u32[]{:S(2)}) collective-permute-start(bf16[256,256]{1,0:T(8,128)(2,1)S(1)} %get-tuple-element.47), channel_id=1, source_target_pairs={{0,8},{4,12},{8,0},{12,4},{16,24},{20,28},{24,16},{28,20},{1,9},{5... | collective-permute-start | bytes 393224 | tf_op jit(solution)/shard_map/ppermute | solution.py:387
  114.3 7.3 %collective-permute-start.34 = (bf16[256,256]{1,0:T(8,128)(2,1)S(1)}, bf16[256,256]{1,0:T(8,128)(2,1)S(1)}, u32[]{:S(2)}, u32[]{:S(2)}) collective-permute-start(bf16[256,256]{1,0:T(8,128)(2,1)S(1)} %get-tuple-element.61), channel_id=1, source_target_pairs={{0,24},{4,28},{8,16},{12,20},{16,8},{20,12},{24,0},{28,4},{1,25},{... | collective-permute-start | bytes 393224 | tf_op jit(solution)/shard_map/ppermute | solution.py:387
  117.2 6.7 %collective-permute-start.33 = (bf16[256,256]{1,0:T(8,128)(2,1)S(1)}, bf16[256,256]{1,0:T(8,128)(2,1)S(1)}, u32[]{:S(2)}, u32[]{:S(2)}) collective-permute-start(bf16[256,256]{1,0:T(8,128)(2,1)S(1)} %get-tuple-element.60), channel_id=1, source_target_pairs={{0,16},{4,20},{8,24},{12,28},{16,0},{20,4},{24,8},{28,12},{1,17},{... | collective-permute-start | bytes 393224 | tf_op jit(solution)/shard_map/ppermute | solution.py:387
  117.7 6.5 %collective-permute-start.32 = (bf16[256,256]{1,0:T(8,128)(2,1)S(1)}, bf16[256,256]{1,0:T(8,128)(2,1)S(1)}, u32[]{:S(2)}, u32[]{:S(2)}) collective-permute-start(bf16[256,256]{1,0:T(8,128)(2,1)S(1)} %get-tuple-element.59), channel_id=1, source_target_pairs={{0,8},{4,12},{8,0},{12,4},{16,24},{20,28},{24,16},{28,20},{1,9},{5... | collective-permute-start | bytes 393224 | tf_op jit(solution)/shard_map/ppermute | solution.py:387
  124.3 10.2 %collective-permute-start.35 = (bf16[256,256]{1,0:T(8,128)(2,1)S(1)}, bf16[256,256]{1,0:T(8,128)(2,1)S(1)}, u32[]{:S(2)}, u32[]{:S(2)}) collective-permute-start(bf16[256,256]{1,0:T(8,128)(2,1)S(1)} %add_convert_fusion), channel_id=1, source_target_pairs={{0,0},{1,10},{2,17},{3,27},{4,4},{5,14},{6,21},{7,31},{8,1},{9,11}... | collective-permute-start | bytes 393224 | tf_op jit(solution)/shard_map/ppermute | solution.py:398
  125.0 9.5 %collective-permute-start.27 = (bf16[256,256]{1,0:T(8,128)(2,1)S(1)}, bf16[256,256]{1,0:T(8,128)(2,1)S(1)}, u32[]{:S(2)}, u32[]{:S(2)}) collective-permute-start(bf16[256,256]{1,0:T(8,128)(2,1)S(1)} %add_convert_fusion.1), channel_id=1, source_target_pairs={{0,0},{1,10},{2,17},{3,27},{4,4},{5,14},{6,21},{7,31},{8,1},{9,11}... | collective-permute-start | bytes 393224 | tf_op jit(solution)/shard_map/ppermute | solution.py:398
  125.7 15.8 %all-to-all-start.1 = ((bf16[8,32,512]{2,1,0:T(8,128)(2,1)}), bf16[8,32,512]{2,1,0:T(8,128)(2,1)S(1)}, u32[]{:S(2)}, u32[]{:S(2)}) async-start(bf16[8,32,512]{2,1,0:T(8,128)(2,1)} %bitcast.21), calls=%async_computation.1 | async-start | bytes 524288 | tf_op jit(solution)/shard_map/all_to_all | solution.py:391
  (24 other events, 259.2 us)

commit v5 on v3

v5 whole, which is shorter than its diff:
```python
import functools
import math

import jax
import jax.numpy as jnp
from jax import lax
from jax.experimental import pallas as pl
from jax.experimental.pallas import tpu as pltpu
from jax.sharding import PartitionSpec as P

EPS = 1e-06
BETA = 1.0
AXES = ("dp", "tensor")
BF16 = jnp.bfloat16
F32 = jnp.float32
POWER_ROWS = 16
PARTS = 2


def dot(a, b):
    return jnp.dot(a, b, preferred_element_type=F32)


def dot_rows(a, b):
    return lax.dot_general(a, b, (((0,), (0,)), ((), ())), preferred_element_type=F32)


def swapped(array, dp_count):
    return lax.ppermute(array, "dp", [(i, i ^ 1) for i in range(dp_count)])


def shifted(array, count, step):
    return lax.ppermute(array, "tensor", [(i, (i + step) % count) for i in range(count)])


def prepare_kernel(
    count, steps, at, x_ref, gain_ref, weight_ref, pol_ref, given_ref, kept_ref, *refs
):
    sent_refs, (rows_ref, total, square) = refs[:count], refs[count:]
    f = pl.program_id(0)
    own = x_ref.shape[0] // count
    for k in range(count):
        source = lax.rem(at[0] - k + count, count)
        rows_ref[k * own : (k + 1) * own, :] = x_ref[pl.ds(pl.multiple_of(source * own, own), own), :]
    wide = rows_ref[...].astype(F32)
    gained = (wide * pol_ref[...]).astype(BF16)

    @pl.when(f < steps // 2)
    def _():
        given_ref[...] = gained

    @pl.when(f >= steps // 2)
    def _():
        kept_ref[...] = gained

    part = dot((wide * gain_ref[...]).astype(BF16), weight_ref[...])
    squares = jnp.sum(wide * wide, axis=1, keepdims=True)

    @pl.when(f == 0)
    def _():
        total[...] = part
        square[...] = squares

    @pl.when(f > 0)
    def _():
        total[...] += part
        square[...] += squares

    @pl.when(f == steps - 1)
    def _():
        for k in range(count):
            sent = sent_refs[k]
            sent[:own, :] = total[k * own : (k + 1) * own, :].astype(BF16)
            power = jnp.broadcast_to(square[k * own : (k + 1) * own, :], (own, 128)).T
            high = power[: POWER_ROWS // 2].astype(BF16).astype(F32)
            low = power[: POWER_ROWS // 2] - high
            sent[own:, :] = jnp.zeros((POWER_ROWS, sent.shape[1]), BF16)
            sent[own:, :own] = jnp.concatenate([high, low], axis=0).astype(BF16)


def row_kernel(
    count, span, model_width, lengths, bins, advantage, gap_ref, cot_ref, *refs
):
    ref_refs, (fixed_ref, pull_ref, scale_ref, row_at_ref) = refs[:count], refs[count:]
    own = pull_ref.shape[0]
    slots = row_at_ref.shape[1]
    row = lax.broadcasted_iota(jnp.int32, (own, slots), 0)
    slot = lax.broadcasted_iota(jnp.int32, (own, slots), 1)
    chosen = jnp.zeros((own, slots), jnp.bool_)
    size = jnp.ones((own, 128), F32)
    weight = jnp.zeros((own, 128), F32)
    start = jnp.int32(0)
    for s in range(lengths.shape[0]):
        end = start + lengths[s]
        inside = (row >= start) & (row < end)
        chosen = chosen | (inside & (slot - bins[s] * span == row - start))
        size = jnp.where(inside[:, :128], lengths[s].astype(F32), size)
        weight = jnp.where(inside[:, :128], advantage[s], weight)
        start = end
    row_at = jnp.where(chosen, 1.0, 0.0).astype(BF16)
    row_at_ref[...] = row_at
    importance = jnp.minimum(jnp.exp(jnp.broadcast_to(gap_ref[...], (128, own)).T), 2.0)
    coef_adv = (weight * importance / size).astype(BF16).astype(F32)
    coef_pull = (BETA / size).astype(BF16).astype(F32)
    total = ref_refs[0][...].astype(F32)
    for ref in ref_refs[1:]:
        total = total + ref[...].astype(F32)
    half = POWER_ROWS // 2
    square = total[own : own + 1, :own] + total[own + half : own + half + 1, :own]
    scale = lax.rsqrt(jnp.broadcast_to(square, (128, own)).T / model_width + EPS)
    reference = (total[:own] * scale[:, :1]).astype(BF16).astype(F32)
    upstream = dot(row_at, cot_ref[...])
    fixed_ref[...] = (coef_adv[:, :1] * upstream - coef_pull[:, :1] * reference) * scale[:, :1]
    pull_ref[...] = coef_pull * scale * scale
    scale_ref[...] = scale


def grad_kernel(places, factor, at, kept_ref, got_ref, slope_ref, slope_got_ref, *refs):
    out_refs, grad = refs[:places], refs[places]
    total = dot_rows(kept_ref[...], slope_ref[...]) + dot_rows(got_ref[...], slope_got_ref[...])
    grad[...] = total * factor
    rows = out_refs[0].shape[0]
    for s in range(places):
        chunk = grad[pl.ds(pl.multiple_of(at[s] * rows, rows), rows), :]
        out_refs[s][...] = chunk.astype(out_refs[s].dtype)


def on_device(
    tokens,
    ref_gain,
    ref_weight,
    pol_gain,
    pol_weight,
    lengths,
    bins,
    advantage,
    logprob_gap,
    cotangent,
):
    tensor_count = lax.axis_size("tensor")
    dp_count = lax.axis_size("dp")
    t = lax.axis_index("tensor")
    d = lax.axis_index("dp")
    cores = dp_count // tensor_count
    assert cores == 2
    places = dp_count // cores
    levels = places.bit_length() - 1
    assert 1 << levels == places
    place = d // cores
    core = d % cores
    group_rows, block = tokens.shape
    own_rows = group_rows // tensor_count
    slot_count = cotangent.shape[2]
    span_rows = slot_count // dp_count
    value_width = ref_weight.shape[1]
    model_width = pol_gain.shape[0]
    shard = pol_weight.shape[0]
    width = value_width // PARTS
    out_rows = shard // tensor_count
    factor = 1.0 / math.sqrt(dp_count * tensor_count * lengths.shape[2])
    relative = place ^ t

    def flat(p, c, z):
        return (p * cores + c) * tensor_count + z

    halves = 2
    half_rows = shard // halves

    def stage(number, held):
        got, is_getter = [], []
        for i in range(halves):
            holders = [0]
            for before in range(number):
                bit = 1 << ((i + before) % levels)
                holders = holders + [q ^ bit for q in holders]
            bit = 1 << ((i + number) % levels)
            pairs = [
                (flat(q ^ z, c, z), flat(q ^ bit ^ z, c, z))
                for q in holders
                for c in range(cores)
                for z in range(tensor_count)
            ]
            got.append(lax.ppermute(held[i], AXES, pairs))
            is_getter.append(
                functools.reduce(jnp.logical_or, [relative == (q ^ bit) for q in holders])
            )
        return got, is_getter

    def select(held, got, is_getter):
        return [jnp.where(is_getter[i], got[i], held[i]) for i in range(halves)]

    held = [pol_weight[i * half_rows : (i + 1) * half_rows] for i in range(halves)]
    got, flags = stage(0, held)

    steps = 4
    feature_step = block // steps
    at = jnp.stack([t, (1 - core) * (steps // 2)]).astype(jnp.int32)
    sent_shape = (own_rows + POWER_ROWS, value_width)

    def at_step(f, at):
        return lax.rem(f + at[1], steps)

    prepared = pl.pallas_call(
        functools.partial(prepare_kernel, tensor_count, steps),
        grid_spec=pltpu.PrefetchScalarGridSpec(
            num_scalar_prefetch=1,
            grid=(steps,),
            in_specs=[
                pl.BlockSpec((group_rows, feature_step), lambda f, at: (0, at_step(f, at))),
                pl.BlockSpec((1, feature_step), lambda f, at: (0, at_step(f, at))),
                pl.BlockSpec((feature_step, value_width), lambda f, at: (at_step(f, at), 0)),
                pl.BlockSpec(
                    (1, feature_step), lambda f, at: (0, at[0] * steps + at_step(f, at))
                ),
            ],
            out_specs=[
                pl.BlockSpec(
                    (group_rows, feature_step), lambda f, at: (0, jnp.minimum(f, steps // 2 - 1))
                ),
                pl.BlockSpec(
                    (group_rows, feature_step), lambda f, at: (0, jnp.maximum(f - steps // 2, 0))
                ),
            ]
            + [pl.BlockSpec(sent_shape, lambda f, at: (0, 0))] * tensor_count,
            scratch_shapes=[
                pltpu.VMEM((group_rows, feature_step), BF16),
                pltpu.VMEM((group_rows, value_width), F32),
                pltpu.VMEM((group_rows, 1), F32),
            ],
        ),
        out_shape=[jax.ShapeDtypeStruct((group_rows, shard), BF16)] * 2
        + [jax.ShapeDtypeStruct(sent_shape, BF16)] * tensor_count,
        compiler_params=pltpu.CompilerParams(vmem_limit_bytes=56 * 2**20),
        cost_estimate=pl.CostEstimate(
            flops=2 * group_rows * block * value_width,
            bytes_accessed=8 * 2**20,
            transcendentals=0,
        ),
        name="prepare",
    )(at, tokens, ref_gain.reshape(1, block), ref_weight, pol_gain.reshape(1, model_width))
    given_rows, kept_rows, *ref_sent = prepared

    ref_got = [ref_sent[0]] + [
        shifted(ref_sent[k], tensor_count, -k) for k in range(1, tensor_count)
    ]
    got_rows = swapped(given_rows, dp_count)

    cot = cotangent.reshape(slot_count, value_width)
    *got, cot, kept_rows = lax.optimization_barrier((*got, cot, kept_rows))
    parts = []
    for j in range(PARTS):
        cols = slice(j * width, (j + 1) * width)
        held_part = select([x[:, cols] for x in held], [x[:, cols] for x in got], flags)
        for number in range(1, levels):
            got_part, flags_part = stage(number, held_part)
            if number < levels - 1:
                held_part = select(held_part, got_part, flags_part)
        parts.append((held_part, got_part, flags_part))
    got_cot = lax.all_to_all(cot, "dp", split_axis=0, concat_axis=0, tiled=True)

    def turned(z):
        return sum(((z >> i) & 1) << (levels - 1 - i) for i in range(levels))

    chunk_at = jnp.stack([place ^ s ^ turned(t) for s in range(places)]).astype(jnp.int32)

    values, slopes = [], []
    for j in range(PARTS):
        held_part, got_part, flags_part = parts[j]
        if j == 0:
            *got_part, got_cot = lax.optimization_barrier((*got_part, got_cot))
        weight = jnp.concatenate(select(held_part, got_part, flags_part), axis=0)
        value_given = dot(got_rows, weight).astype(BF16)
        if j == 0:
            tied = lax.optimization_barrier((value_given, lengths, bins, advantage, logprob_gap))
            value_given, lengths, bins, advantage, logprob_gap = tied
            smem = pl.BlockSpec(memory_space=pltpu.SMEM)
            vmem = pl.BlockSpec(memory_space=pltpu.VMEM)
            fixed, pull, row_scale, row_at = pl.pallas_call(
                functools.partial(row_kernel, tensor_count, span_rows, model_width),
                in_specs=[smem] * 3 + [vmem] * (2 + tensor_count),
                out_specs=[vmem] * 4,
                out_shape=[
                    jax.ShapeDtypeStruct((own_rows, value_width), F32),
                    jax.ShapeDtypeStruct((own_rows, 128), F32),
                    jax.ShapeDtypeStruct((own_rows, 128), F32),
                    jax.ShapeDtypeStruct((own_rows, slot_count), BF16),
                ],
                compiler_params=pltpu.CompilerParams(vmem_limit_bytes=16 * 2**20),
                cost_estimate=pl.CostEstimate(
                    flops=2 * own_rows * slot_count * value_width,
                    bytes_accessed=2**21,
                    transcendentals=0,
                ),
                name="rows",
            )(
                lengths.reshape(-1),
                bins.reshape(-1),
                advantage.reshape(-1),
                logprob_gap.reshape(1, own_rows),
                got_cot,
                *ref_got,
            )
        value_part = dot(kept_rows, weight) + swapped(value_given, dp_count).astype(F32)
        total = value_part[:own_rows]
        for k in range(1, tensor_count):
            part = value_part[k * own_rows : (k + 1) * own_rows].astype(BF16)
            total = total + shifted(part, tensor_count, -k).astype(F32)
        values.append(total * row_scale[:, :1])

        cols = slice(j * width, (j + 1) * width)
        slope = (fixed[:, cols] + pull[:, :1] * total).astype(BF16)
        slopes.append(
            jnp.concatenate(
                [slope] + [shifted(slope, tensor_count, k) for k in range(1, tensor_count)], axis=0
            )
        )

    sent = dot_rows(row_at, jnp.concatenate(values, axis=1).astype(BF16)).astype(BF16)

    grads = []
    for j in range(PARTS):
        slopes_got = swapped(slopes[j], dp_count)
        chunks = pl.pallas_call(
            functools.partial(grad_kernel, places, factor),
            grid_spec=pltpu.PrefetchScalarGridSpec(
                num_scalar_prefetch=1,
                grid=(1,),
                in_specs=[
                    pl.BlockSpec((group_rows, shard), lambda i, at: (0, 0)),
                    pl.BlockSpec((group_rows, shard), lambda i, at: (0, 0)),
                    pl.BlockSpec((group_rows, width), lambda i, at: (0, 0)),
                    pl.BlockSpec((group_rows, width), lambda i, at: (0, 0)),
                ],
                out_specs=[pl.BlockSpec((out_rows, width), lambda i, at: (0, 0))] * places,
                scratch_shapes=[pltpu.VMEM((shard, width), F32)],
            ),
            out_shape=[
                jax.ShapeDtypeStruct((out_rows, width), F32 if s == 0 else BF16)
                for s in range(places)
            ],
            compiler_params=pltpu.CompilerParams(vmem_limit_bytes=32 * 2**20),
            cost_estimate=pl.CostEstimate(
                flops=4 * group_rows * shard * width,
                bytes_accessed=4 * 2**20,
                transcendentals=0,
            ),
            name="gradient",
        )(chunk_at, kept_rows, got_rows, slopes[j], slopes_got)
        if j == PARTS - 1:
            *chunks, sent = lax.optimization_barrier((*chunks, sent))
            policy_values = lax.all_to_all(sent, "dp", split_axis=0, concat_axis=0, tiled=True)
        total = chunks[0]
        for s in range(1, places):
            pairs = [
                (p * cores + c, (p ^ s) * cores + c) for p in range(places) for c in range(cores)
            ]
            total = total + lax.ppermute(chunks[s], "dp", pairs).astype(F32)
        total = total.astype(BF16)
        pairs = [
            (flat(p, c, z), flat(z, c, p ^ turned(z)))
            for p in range(places)
            for c in range(cores)
            for z in range(tensor_count)
        ]
        grads.append(lax.ppermute(total, AXES, pairs))
    grad_weight = jnp.concatenate(grads, axis=1).astype(F32)
    return (policy_values.reshape(1, 1, slot_count, value_width), grad_weight)


def solution(mesh):
    in_specs = (
        P("dp", "tensor"),
        P("tensor"),
        P("tensor", None),
        P(),
        P("dp", None),
        P("dp", "tensor", None),
        P("dp", "tensor", None),
        P("dp", "tensor", None),
        P(("dp", "tensor")),
        P("dp", "tensor", None, None),
    )
    out_specs = (P("dp", "tensor", None, None), P(("dp", "tensor"), None))
    return jax.shard_map(
        on_device, mesh=mesh, in_specs=in_specs, out_specs=out_specs, check_vma=False
    )
```

time: 126 us -> 115 us (0.913)
  the two profiles are of different devices: /device:TPU:12 before, /device:TPU:4 now
where the time goes in v5:
time: 115 us; the launch traced here: 113 us
  starting transfers between devices  60.5 us (53%)
  waiting for transfers between devices  29.1 us (25%)
  Pallas kernels  11.1 us (10%)
  other arithmetic  5.76 us (5%)
  local copies, waits for them, and re-layouts  3.04 us (3%)
  matrix products  2.71 us (2%)
    ppermute x15, starting transfers between devices, shifted(): lax.ppermute(array, 'tensor', [(i, (i + step) % count) for i in range(cou...  25.6 us
    ppermute x15, waiting for transfers between devices, shifted(): lax.ppermute(array, 'tensor', [(i, (i + step) % count) for i in range(cou...  15 us
    ppermute x2, starting transfers between devices, on_device(): grads.append(lax.ppermute(total, AXES, pairs))  9.09 us
    pallas_call x1, Pallas kernels, on_device(): pl.pallas_call(functools.partial(prepare_kernel, tensor_count, steps), gr...  7.2 us
    ppermute x6, starting transfers between devices, stage(): got.append(lax.ppermute(held[i], AXES, pairs))  7.15 us
    ppermute x6, starting transfers between devices, on_device(): total = total + lax.ppermute(chunks[s], 'dp', pairs).astype(F32)  7.11 us
    ppermute x6, waiting for transfers between devices, stage(): got.append(lax.ppermute(held[i], AXES, pairs))  7.03 us
    all_to_all x1, starting transfers between devices, on_device(): got_cot = lax.all_to_all(cot, 'dp', split_axis=0, concat_axis=0, tiled=True)  6 us
  transfers between devices with their start and end apart: 36, of which 10 were waited for; matrix products, arithmetic and copies ran while one was open for 7% of the time, Pallas kernels for 10%

profile of v5, /device:TPU:4, one launch (start us, length us, event | category | flops | bytes accessed | tf_op | source)
XLA Modules:
  0.0 113.2 jit_solution(17599667782250485330)
XLA Ops:
  0.6 2.1 %fusion.12 = (bf16[512,512]{1,0:T(8,128)(2,1)S(1)}, bf16[512,512]{1,0:T(8,128)(2,1)}) fusion(bf16[1024,512]{1,0:T(8,128)(2,1)} %param.14), kind=kLoop, calls=%fused_computation.42 | loop fusion | bytes 2097152 | tf_op jit(solution)/shard_map/slice | solution.py:192
  3.4 1.3 %collective-permute-start.1 = (bf16[512,512]{1,0:T(8,128)(2,1)S(1)}, bf16[512,512]{1,0:T(8,128)(2,1)}, u32[]{:S(2)}, u32[]{:S(2)}) collective-permute-start(bf16[512,512]{1,0:T(8,128)(2,1)S(1)} %get-tuple-element.78), channel_id=1, source_target_pairs={{0,16},{9,25},{18,2},{27,11},{4,20},{13,29},{22,6},{31,15}} | collective-permute-start | bytes 1572872 | tf_op jit(solution)/shard_map/ppermute | solution.py:183
  5.3 7.2 %prepare.1 = (bf16[512,1024]{1,0:T(8,128)(2,1)}, bf16[512,1024]{1,0:T(8,128)(2,1)}, bf16[144,512]{1,0:T(8,128)(2,1)}, bf16[144,512]{1,0:T(8,128)(2,1)}, bf16[144...) custom-call(s32[2]{0:T(128)} %pad_add_fusion.1.at, bf16[512,2048]{1,0:T(8,128)(2,1)} %x_ref.1, f32[1,2048]{1,0:T(1,128)} %bitcast.30, ...), custom_call_target="tpu_custom_call" | custom-call | flops 1073741824 | bytes 8388608 | tf_op jit(solution)/shard_map/prepare/pallas_call | solution.py:203
  12.6 7.0 %collective-permute-done.1 = bf16[512,512]{1,0:T(8,128)(2,1)} collective-permute-done((bf16[512,512]{1,0:T(8,128)(2,1)S(1)}, bf16[512,512]{1,0:T(8,128)(2,1)}, u32[]{:S(2)}, u32[]{:S(2)}) %collective-permute-start.1) | collective-permute-done | bytes 524320 | tf_op jit(solution)/shard_map/ppermute | solution.py:183
  19.6 1.8 %slice_select_fusion.1 = (bf16[512,256]{1,0:T(8,128)(2,1)S(1)}, bf16[512,256]{1,0:T(8,128)(2,1)S(1)}, bf16[512,256]{1,0:T(8,128)(2,1)S(1)}, bf16[512,256]{1,0:T(8,128)(2,1)}) fusion(bf16[1024,512]{1,0:T(8,128)(2,1)S(1)} %copy-done.6, bf16[512,512]{1,0:T(8,128)(2,1)S(1)} %collective-permute-done, pred[]{:T(512)S(6)} %eq.10, ...), kind=kLoop, calls=%fused_computation.13 | loop fusion | flops 524288 | bytes 3145730 | tf_op jit(solution)/shard_map/jit(_where)/select_n | solution.py:190
  21.5 1.3 %collective-permute-start.3 = (bf16[512,256]{1,0:T(8,128)(2,1)S(1)}, bf16[512,256]{1,0:T(8,128)(2,1)S(1)}, u32[]{:S(2)}, u32[]{:S(2)}) collective-permute-start(bf16[512,256]{1,0:T(8,128)(2,1)S(1)} %get-tuple-element.73), channel_id=1, source_target_pairs={{0,16},{9,25},{18,2},{27,11},{4,20},{13,29},{22,6},{31,15},{8,24},... | collective-permute-start | bytes 786440 | tf_op jit(solution)/shard_map/ppermute | solution.py:183
  22.8 1.3 %collective-permute-start.4 = (bf16[512,256]{1,0:T(8,128)(2,1)S(1)}, bf16[512,256]{1,0:T(8,128)(2,1)S(1)}, u32[]{:S(2)}, u32[]{:S(2)}) collective-permute-start(bf16[512,256]{1,0:T(8,128)(2,1)S(1)} %get-tuple-element.76), channel_id=1, source_target_pairs={{0,8},{9,1},{18,26},{27,19},{4,12},{13,5},{22,30},{31,23},{16,24},... | collective-permute-start | bytes 786440 | tf_op jit(solution)/shard_map/ppermute | solution.py:183
  24.1 1.3 %collective-permute-start.9 = (bf16[512,256]{1,0:T(8,128)(2,1)}, bf16[512,256]{1,0:T(8,128)(2,1)S(1)}, u32[]{:S(2)}, u32[]{:S(2)}) collective-permute-start(bf16[512,256]{1,0:T(8,128)(2,1)} %get-tuple-element.77), channel_id=1, source_target_pairs={{0,8},{9,1},{18,26},{27,19},{4,12},{13,5},{22,30},{31,23},{16,24},... | collective-permute-start | bytes 786440 | tf_op jit(solution)/shard_map/ppermute | solution.py:183
  25.4 6.0 %all-to-all-start = ((bf16[8,32,512]{2,1,0:T(8,128)(2,1)}), bf16[8,32,512]{2,1,0:T(8,128)(2,1)S(1)}, u32[]{:S(2)}, u32[]{:S(2)}) async-start(bf16[8,32,512]{2,1,0:T(8,128)(2,1)} %bitcast.28), calls=%async_computation | async-start | bytes 524288 | tf_op jit(solution)/shard_map/all_to_all | solution.py:259
  32.7 3.7 %collective-permute-start.5 = (bf16[144,512]{1,0:T(8,128)(2,1)}, bf16[144,512]{1,0:T(8,128)(2,1)S(1)}, u32[]{:S(2)}, u32[]{:S(2)}) collective-permute-start(bf16[144,512]{1,0:T(8,128)(2,1)} %get-tuple-element.51), channel_id=1, source_target_pairs={{0,3},{1,0},{2,1},{3,2},{4,7},{5,4},{6,5},{7,6},{8,11},{9,8},{10,9... | collective-permute-start | bytes 442376 | tf_op jit(solution)/shard_map/ppermute | solution.py:33
  37.6 4.7 %collective-permute-start.7 = (bf16[144,512]{1,0:T(8,128)(2,1)}, bf16[144,512]{1,0:T(8,128)(2,1)S(1)}, u32[]{:S(2)}, u32[]{:S(2)}) collective-permute-start(bf16[144,512]{1,0:T(8,128)(2,1)} %get-tuple-element.53), channel_id=1, source_target_pairs={{0,1},{1,2},{2,3},{3,0},{4,5},{5,6},{6,7},{7,4},{8,9},{9,10},{10,1... | collective-permute-start | bytes 442376 | tf_op jit(solution)/shard_map/ppermute | solution.py:33
  44.9 4.6 %collective-permute-done.6.refs_2_ = bf16[144,512]{1,0:T(8,128)(2,1)S(1)} collective-permute-done((bf16[144,512]{1,0:T(8,128)(2,1)}, bf16[144,512]{1,0:T(8,128)(2,1)S(1)}, u32[]{:S(2)}, u32[]{:S(2)}) %collective-permute-start.6) | collective-permute-done | bytes 147488 | tf_op jit(solution)/shard_map/ppermute | solution.py:33
  52.3 1.9 %collective-permute-start.12 = (bf16[128,256]{1,0:T(8,128)(2,1)S(1)}, bf16[128,256]{1,0:T(8,128)(2,1)S(1)}, u32[]{:S(2)}, u32[]{:S(2)}) collective-permute-start(bf16[128,256]{1,0:T(8,128)(2,1)S(1)} %get-tuple-element.91), channel_id=1, source_target_pairs={{0,2},{1,3},{2,0},{3,1},{4,6},{5,7},{6,4},{7,5},{8,10},{9,11},{10,... | collective-permute-start | bytes 196616 | tf_op jit(solution)/shard_map/ppermute | solution.py:33
  54.1 2.8 %collective-permute-start.11 = (bf16[128,256]{1,0:T(8,128)(2,1)S(1)}, bf16[128,256]{1,0:T(8,128)(2,1)S(1)}, u32[]{:S(2)}, u32[]{:S(2)}) collective-permute-start(bf16[128,256]{1,0:T(8,128)(2,1)S(1)} %get-tuple-element.89), channel_id=1, source_target_pairs={{0,3},{1,0},{2,1},{3,2},{4,7},{5,4},{6,5},{7,6},{8,11},{9,8},{10,9... | collective-permute-start | bytes 196616 | tf_op jit(solution)/shard_map/ppermute | solution.py:33
  58.1 3.2 %collective-permute-start.19 = (bf16[128,256]{1,0:T(8,128)(2,1)S(1)}, bf16[128,256]{1,0:T(8,128)(2,1)S(1)}, u32[]{:S(2)}, u32[]{:S(2)}) collective-permute-start(bf16[128,256]{1,0:T(8,128)(2,1)S(1)} %get-tuple-element.86), channel_id=1, source_target_pairs={{0,3},{1,0},{2,1},{3,2},{4,7},{5,4},{6,5},{7,6},{8,11},{9,8},{10,9... | collective-permute-start | bytes 196616 | tf_op jit(solution)/shard_map/ppermute | solution.py:33
  61.5 2.2 %collective-permute-done.21 = bf16[128,256]{1,0:T(8,128)(2,1)S(1)} collective-permute-done((bf16[128,256]{1,0:T(8,128)(2,1)S(1)}, bf16[128,256]{1,0:T(8,128)(2,1)S(1)}, u32[]{:S(2)}, u32[]{:S(2)}) %collective-permute-start.21) | collective-permute-done | bytes 65568 | tf_op jit(solution)/shard_map/ppermute | solution.py:33
  63.7 2.0 %collective-permute-done.20 = bf16[128,256]{1,0:T(8,128)(2,1)S(1)} collective-permute-done((bf16[128,256]{1,0:T(8,128)(2,1)S(1)}, bf16[128,256]{1,0:T(8,128)(2,1)S(1)}, u32[]{:S(2)}, u32[]{:S(2)}) %collective-permute-start.20) | collective-permute-done | bytes 65568 | tf_op jit(solution)/shard_map/ppermute | solution.py:33
  65.8 2.7 %collective-permute-start.16 = (bf16[128,256]{1,0:T(8,128)(2,1)S(1)}, bf16[128,256]{1,0:T(8,128)(2,1)S(1)}, u32[]{:S(2)}, u32[]{:S(2)}) collective-permute-start(bf16[128,256]{1,0:T(8,128)(2,1)S(1)} %get-tuple-element.83), channel_id=1, source_target_pairs={{0,3},{1,0},{2,1},{3,2},{4,7},{5,4},{6,5},{7,6},{8,11},{9,8},{10,9... | collective-permute-start | bytes 196616 | tf_op jit(solution)/shard_map/ppermute | solution.py:33
  69.2 3.2 %collective-permute-start.24 = (bf16[128,256]{1,0:T(8,128)(2,1)S(1)}, bf16[128,256]{1,0:T(8,128)(2,1)S(1)}, u32[]{:S(2)}, u32[]{:S(2)}) collective-permute-start(bf16[128,256]{1,0:T(8,128)(2,1)S(1)} %get-tuple-element.85), channel_id=1, source_target_pairs={{0,3},{1,0},{2,1},{3,2},{4,7},{5,4},{6,5},{7,6},{8,11},{9,8},{10,9... | collective-permute-start | bytes 196616 | tf_op jit(solution)/shard_map/ppermute | solution.py:33
  73.6 3.7 %collective-permute-done.15 = bf16[128,256]{1,0:T(8,128)(2,1)S(1)} collective-permute-done((bf16[128,256]{1,0:T(8,128)(2,1)S(1)}, bf16[128,256]{1,0:T(8,128)(2,1)S(1)}, u32[]{:S(2)}, u32[]{:S(2)}) %collective-permute-start.15) | collective-permute-done | bytes 65568 | tf_op jit(solution)/shard_map/ppermute | solution.py:33
  77.4 2.4 %collective-permute-done.23 = bf16[128,256]{1,0:T(8,128)(2,1)S(1)} collective-permute-done((bf16[128,256]{1,0:T(8,128)(2,1)S(1)}, bf16[128,256]{1,0:T(8,128)(2,1)S(1)}, u32[]{:S(2)}, u32[]{:S(2)}) %collective-permute-start.23) | collective-permute-done | bytes 65568 | tf_op jit(solution)/shard_map/ppermute | solution.py:33
  80.9 1.4 %gradient.2 = (f32[256,256]{1,0:T(8,128)S(1)}, bf16[256,256]{1,0:T(8,128)(2,1)S(1)}, bf16[256,256]{1,0:T(8,128)(2,1)S(1)}, bf16[256,256]{1,0:T(8,128)(2,1)S(1)}) custom-call(s32[4]{0:T(128)S(1)} %pad_add_fusion.at, bf16[512,1024]{1,0:T(8,128)(2,1)S(1)} %copy-done, bf16[512,1024]{1,0:T(8,128)(2,1)S(1)} %collective-permute-done.2.got_ref, ...), custom_call_target="tpu_custom_call" | custom-call | flops 536870912 | bytes 4194304 | tf_op jit(solution)/shard_map/gradient/pallas_call | solution.py:323
  82.3 1.5 %collective-permute-start.32 = (bf16[256,256]{1,0:T(8,128)(2,1)S(1)}, bf16[256,256]{1,0:T(8,128)(2,1)}, u32[]{:S(2)}, u32[]{:S(2)}) collective-permute-start(bf16[256,256]{1,0:T(8,128)(2,1)S(1)} %get-tuple-element.71), channel_id=1, source_target_pairs={{0,24},{4,28},{8,16},{12,20},{16,8},{20,12},{24,0},{28,4},{1,25},{... | collective-permute-start | bytes 393224 | tf_op jit(solution)/shard_map/ppermute | solution.py:357
  83.8 1.6 %collective-permute-start.31 = (bf16[256,256]{1,0:T(8,128)(2,1)S(1)}, bf16[256,256]{1,0:T(8,128)(2,1)}, u32[]{:S(2)}, u32[]{:S(2)}) collective-permute-start(bf16[256,256]{1,0:T(8,128)(2,1)S(1)} %get-tuple-element.70), channel_id=1, source_target_pairs={{0,16},{4,20},{8,24},{12,28},{16,0},{20,4},{24,8},{28,12},{1,17},{... | collective-permute-start | bytes 393224 | tf_op jit(solution)/shard_map/ppermute | solution.py:357
  85.8 4.7 %all-to-all-start.1 = ((bf16[8,32,512]{2,1,0:T(8,128)(2,1)}), bf16[8,32,512]{2,1,0:T(8,128)(2,1)S(1)}, u32[]{:S(2)}, u32[]{:S(2)}) async-start(bf16[8,32,512]{2,1,0:T(8,128)(2,1)} %bitcast.15), calls=%async_computation.1 | async-start | bytes 524288 | tf_op jit(solution)/shard_map/all_to_all | solution.py:351
  90.5 1.4 %gradient.3 = (f32[256,256]{1,0:T(8,128)S(1)}, bf16[256,256]{1,0:T(8,128)(2,1)S(1)}, bf16[256,256]{1,0:T(8,128)(2,1)S(1)}, bf16[256,256]{1,0:T(8,128)(2,1)S(1)}) custom-call(s32[4]{0:T(128)S(1)} %pad_add_fusion.at, bf16[512,1024]{1,0:T(8,128)(2,1)S(1)} %copy-done, bf16[512,1024]{1,0:T(8,128)(2,1)S(1)} %collective-permute-done.2.got_ref, ...), custom_call_target="tpu_custom_call" | custom-call | flops 536870912 | bytes 4194304 | tf_op jit(solution)/shard_map/gradient/pallas_call | solution.py:323
  91.9 1.5 %collective-permute-start.28 = (bf16[256,256]{1,0:T(8,128)(2,1)S(1)}, bf16[256,256]{1,0:T(8,128)(2,1)S(1)}, u32[]{:S(2)}, u32[]{:S(2)}) collective-permute-start(bf16[256,256]{1,0:T(8,128)(2,1)S(1)} %get-tuple-element.67), channel_id=1, source_target_pairs={{0,24},{4,28},{8,16},{12,20},{16,8},{20,12},{24,0},{28,4},{1,25},{... | collective-permute-start | bytes 393224 | tf_op jit(solution)/shard_map/ppermute | solution.py:357
  93.4 1.5 %collective-permute-start.27 = (bf16[256,256]{1,0:T(8,128)(2,1)S(1)}, bf16[256,256]{1,0:T(8,128)(2,1)S(1)}, u32[]{:S(2)}, u32[]{:S(2)}) collective-permute-start(bf16[256,256]{1,0:T(8,128)(2,1)S(1)} %get-tuple-element.66), channel_id=1, source_target_pairs={{0,16},{4,20},{8,24},{12,28},{16,0},{20,4},{24,8},{28,12},{1,17},{... | collective-permute-start | bytes 393224 | tf_op jit(solution)/shard_map/ppermute | solution.py:357
  96.5 2.5 %collective-permute-start.33 = (bf16[256,256]{1,0:T(8,128)(2,1)S(1)}, bf16[256,256]{1,0:T(8,128)(2,1)S(1)}, u32[]{:S(2)}, u32[]{:S(2)}) collective-permute-start(bf16[256,256]{1,0:T(8,128)(2,1)S(1)} %add_convert_fusion), channel_id=1, source_target_pairs={{0,0},{1,10},{2,17},{3,27},{4,4},{5,14},{6,21},{7,31},{8,1},{9,11}... | collective-permute-start | bytes 393224 | tf_op jit(solution)/shard_map/ppermute | solution.py:365
  99.2 2.3 %collective-permute-done.27 = bf16[256,256]{1,0:T(8,128)(2,1)S(1)} collective-permute-done((bf16[256,256]{1,0:T(8,128)(2,1)S(1)}, bf16[256,256]{1,0:T(8,128)(2,1)S(1)}, u32[]{:S(2)}, u32[]{:S(2)}) %collective-permute-start.27) | collective-permute-done | bytes 131104 | tf_op jit(solution)/shard_map/ppermute | solution.py:357
  101.7 6.6 %collective-permute-start.29 = (bf16[256,256]{1,0:T(8,128)(2,1)S(1)}, bf16[256,256]{1,0:T(8,128)(2,1)S(1)}, u32[]{:S(2)}, u32[]{:S(2)}) collective-permute-start(bf16[256,256]{1,0:T(8,128)(2,1)S(1)} %add_convert_fusion.1), channel_id=1, source_target_pairs={{0,0},{1,10},{2,17},{3,27},{4,4},{5,14},{6,21},{7,31},{8,1},{9,11}... | collective-permute-start | bytes 393224 | tf_op jit(solution)/shard_map/ppermute | solution.py:365
  108.3 3.3 %collective-permute-done.29 = bf16[256,256]{1,0:T(8,128)(2,1)S(1)} collective-permute-done((bf16[256,256]{1,0:T(8,128)(2,1)S(1)}, bf16[256,256]{1,0:T(8,128)(2,1)S(1)}, u32[]{:S(2)}, u32[]{:S(2)}) %collective-permute-start.29) | collective-permute-done | bytes 131104 | tf_op jit(solution)/shard_map/ppermute | solution.py:365
  (81 shorter events, 17.2 us)
Async XLA Ops:
  2.7 9.9 %collective-permute-start = (bf16[512,512]{1,0:T(8,128)(2,1)}, bf16[512,512]{1,0:T(8,128)(2,1)S(1)}, u32[]{:S(2)}, u32[]{:S(2)}) collective-permute-start(bf16[512,512]{1,0:T(8,128)(2,1)} %get-tuple-element.79), channel_id=1, source_target_pairs={{0,8},{9,1},{18,26},{27,19},{4,12},{13,5},{22,30},{31,23}} | collective-permute-start | bytes 1572872 | tf_op jit(solution)/shard_map/ppermute | solution.py:183
  3.4 16.3 %collective-permute-start.1 = (bf16[512,512]{1,0:T(8,128)(2,1)S(1)}, bf16[512,512]{1,0:T(8,128)(2,1)}, u32[]{:S(2)}, u32[]{:S(2)}) collective-permute-start(bf16[512,512]{1,0:T(8,128)(2,1)S(1)} %get-tuple-element.78), channel_id=1, source_target_pairs={{0,16},{9,25},{18,2},{27,11},{4,20},{13,29},{22,6},{31,15}} | collective-permute-start | bytes 1572872 | tf_op jit(solution)/shard_map/ppermute | solution.py:183
  12.5 30.9 %collective-permute-start.2 = (bf16[512,1024]{1,0:T(8,128)(2,1)}, bf16[512,1024]{1,0:T(8,128)(2,1)S(1)}, u32[]{:S(2)}, u32[]{:S(2)}) collective-permute-start(bf16[512,1024]{1,0:T(8,128)(2,1)} %get-tuple-element.39), channel_id=1, source_target_pairs={{0,4},{4,0},{8,12},{12,8},{16,20},{20,16},{24,28},{28,24},{1,5},{5... | collective-permute-start | bytes 3145736 | tf_op jit(solution)/shard_map/ppermute | solution.py:29
  21.5 11.2 %collective-permute-start.3 = (bf16[512,256]{1,0:T(8,128)(2,1)S(1)}, bf16[512,256]{1,0:T(8,128)(2,1)S(1)}, u32[]{:S(2)}, u32[]{:S(2)}) collective-permute-start(bf16[512,256]{1,0:T(8,128)(2,1)S(1)} %get-tuple-element.73), channel_id=1, source_target_pairs={{0,16},{9,25},{18,2},{27,11},{4,20},{13,29},{22,6},{31,15},{8,24},... | collective-permute-start | bytes 786440 | tf_op jit(solution)/shard_map/ppermute | solution.py:183
  22.8 13.7 %collective-permute-start.4 = (bf16[512,256]{1,0:T(8,128)(2,1)S(1)}, bf16[512,256]{1,0:T(8,128)(2,1)S(1)}, u32[]{:S(2)}, u32[]{:S(2)}) collective-permute-start(bf16[512,256]{1,0:T(8,128)(2,1)S(1)} %get-tuple-element.76), channel_id=1, source_target_pairs={{0,8},{9,1},{18,26},{27,19},{4,12},{13,5},{22,30},{31,23},{16,24},... | collective-permute-start | bytes 786440 | tf_op jit(solution)/shard_map/ppermute | solution.py:183
  24.1 13.5 %collective-permute-start.9 = (bf16[512,256]{1,0:T(8,128)(2,1)}, bf16[512,256]{1,0:T(8,128)(2,1)S(1)}, u32[]{:S(2)}, u32[]{:S(2)}) collective-permute-start(bf16[512,256]{1,0:T(8,128)(2,1)} %get-tuple-element.77), channel_id=1, source_target_pairs={{0,8},{9,1},{18,26},{27,19},{4,12},{13,5},{22,30},{31,23},{16,24},... | collective-permute-start | bytes 786440 | tf_op jit(solution)/shard_map/ppermute | solution.py:183
  25.4 12.2 %all-to-all-start = ((bf16[8,32,512]{2,1,0:T(8,128)(2,1)}), bf16[8,32,512]{2,1,0:T(8,128)(2,1)S(1)}, u32[]{:S(2)}, u32[]{:S(2)}) async-start(bf16[8,32,512]{2,1,0:T(8,128)(2,1)} %bitcast.28), calls=%async_computation | async-start | bytes 524288 | tf_op jit(solution)/shard_map/all_to_all | solution.py:259
  31.4 11.8 %collective-permute-start.8 = (bf16[512,256]{1,0:T(8,128)(2,1)S(1)}, bf16[512,256]{1,0:T(8,128)(2,1)S(1)}, u32[]{:S(2)}, u32[]{:S(2)}) collective-permute-start(bf16[512,256]{1,0:T(8,128)(2,1)S(1)} %get-tuple-element.72), channel_id=1, source_target_pairs={{0,16},{9,25},{18,2},{27,11},{4,20},{13,29},{22,6},{31,15},{8,24},... | collective-permute-start | bytes 786440 | tf_op jit(solution)/shard_map/ppermute | solution.py:183
  32.7 12.2 %collective-permute-start.5 = (bf16[144,512]{1,0:T(8,128)(2,1)}, bf16[144,512]{1,0:T(8,128)(2,1)S(1)}, u32[]{:S(2)}, u32[]{:S(2)}) collective-permute-start(bf16[144,512]{1,0:T(8,128)(2,1)} %get-tuple-element.51), channel_id=1, source_target_pairs={{0,3},{1,0},{2,1},{3,2},{4,7},{5,4},{6,5},{7,6},{8,11},{9,8},{10,9... | collective-permute-start | bytes 442376 | tf_op jit(solution)/shard_map/ppermute | solution.py:33
  36.4 13.1 %collective-permute-start.6 = (bf16[144,512]{1,0:T(8,128)(2,1)}, bf16[144,512]{1,0:T(8,128)(2,1)S(1)}, u32[]{:S(2)}, u32[]{:S(2)}) collective-permute-start(bf16[144,512]{1,0:T(8,128)(2,1)} %get-tuple-element.52), channel_id=1, source_target_pairs={{0,2},{1,3},{2,0},{3,1},{4,6},{5,7},{6,4},{7,5},{8,10},{9,11},{10,... | collective-permute-start | bytes 442376 | tf_op jit(solution)/shard_map/ppermute | solution.py:33
  37.6 12.0 %collective-permute-start.7 = (bf16[144,512]{1,0:T(8,128)(2,1)}, bf16[144,512]{1,0:T(8,128)(2,1)S(1)}, u32[]{:S(2)}, u32[]{:S(2)}) collective-permute-start(bf16[144,512]{1,0:T(8,128)(2,1)} %get-tuple-element.53), channel_id=1, source_target_pairs={{0,1},{1,2},{2,3},{3,0},{4,5},{5,6},{6,7},{7,4},{8,9},{9,10},{10,1... | collective-permute-start | bytes 442376 | tf_op jit(solution)/shard_map/ppermute | solution.py:33
  43.9 6.9 %collective-permute-start.10 = (bf16[512,256]{1,0:T(8,128)(2,1)S(1)}, bf16[512,256]{1,0:T(8,128)(2,1)S(1)}, u32[]{:S(2)}, u32[]{:S(2)}) collective-permute-start(bf16[512,256]{1,0:T(8,128)(2,1)S(1)} %convolution_convert_fusion.1), channel_id=1, source_target_pairs={{0,4},{4,0},{8,12},{12,8},{16,20},{20,16},{24,28},{28,24},{1,5},{5... | collective-permute-start | bytes 786440 | tf_op jit(solution)/shard_map/ppermute | solution.py:29
  44.4 12.6 %collective-permute-start.18 = (bf16[512,256]{1,0:T(8,128)(2,1)S(1)}, bf16[512,256]{1,0:T(8,128)(2,1)S(1)}, u32[]{:S(2)}, u32[]{:S(2)}) collective-permute-start(bf16[512,256]{1,0:T(8,128)(2,1)S(1)} %convolution_convert_fusion.2), channel_id=1, source_target_pairs={{0,4},{4,0},{8,12},{12,8},{16,20},{20,16},{24,28},{28,24},{1,5},{5... | collective-permute-start | bytes 786440 | tf_op jit(solution)/shard_map/ppermute | solution.py:29
  51.3 6.8 %collective-permute-start.13 = (bf16[128,256]{1,0:T(8,128)(2,1)S(1)}, bf16[128,256]{1,0:T(8,128)(2,1)S(1)}, u32[]{:S(2)}, u32[]{:S(2)}) collective-permute-start(bf16[128,256]{1,0:T(8,128)(2,1)S(1)} %get-tuple-element.90), channel_id=1, source_target_pairs={{0,1},{1,2},{2,3},{3,0},{4,5},{5,6},{6,7},{7,4},{8,9},{9,10},{10,1... | collective-permute-start | bytes 196616 | tf_op jit(solution)/shard_map/ppermute | solution.py:33
  52.3 9.2 %collective-permute-start.12 = (bf16[128,256]{1,0:T(8,128)(2,1)S(1)}, bf16[128,256]{1,0:T(8,128)(2,1)S(1)}, u32[]{:S(2)}, u32[]{:S(2)}) collective-permute-start(bf16[128,256]{1,0:T(8,128)(2,1)S(1)} %get-tuple-element.91), channel_id=1, source_target_pairs={{0,2},{1,3},{2,0},{3,1},{4,6},{5,7},{6,4},{7,5},{8,10},{9,11},{10,... | collective-permute-start | bytes 196616 | tf_op jit(solution)/shard_map/ppermute | solution.py:33
  54.1 7.3 %collective-permute-start.11 = (bf16[128,256]{1,0:T(8,128)(2,1)S(1)}, bf16[128,256]{1,0:T(8,128)(2,1)S(1)}, u32[]{:S(2)}, u32[]{:S(2)}) collective-permute-start(bf16[128,256]{1,0:T(8,128)(2,1)S(1)} %get-tuple-element.89), channel_id=1, source_target_pairs={{0,3},{1,0},{2,1},{3,2},{4,7},{5,4},{6,5},{7,6},{8,11},{9,8},{10,9... | collective-permute-start | bytes 196616 | tf_op jit(solution)/shard_map/ppermute | solution.py:33
  57.5 8.1 %collective-permute-start.20 = (bf16[128,256]{1,0:T(8,128)(2,1)S(1)}, bf16[128,256]{1,0:T(8,128)(2,1)S(1)}, u32[]{:S(2)}, u32[]{:S(2)}) collective-permute-start(bf16[128,256]{1,0:T(8,128)(2,1)S(1)} %get-tuple-element.88), channel_id=1, source_target_pairs={{0,2},{1,3},{2,0},{3,1},{4,6},{5,7},{6,4},{7,5},{8,10},{9,11},{10,... | collective-permute-start | bytes 196616 | tf_op jit(solution)/shard_map/ppermute | solution.py:33
  58.1 7.6 %collective-permute-start.19 = (bf16[128,256]{1,0:T(8,128)(2,1)S(1)}, bf16[128,256]{1,0:T(8,128)(2,1)S(1)}, u32[]{:S(2)}, u32[]{:S(2)}) collective-permute-start(bf16[128,256]{1,0:T(8,128)(2,1)S(1)} %get-tuple-element.86), channel_id=1, source_target_pairs={{0,3},{1,0},{2,1},{3,2},{4,7},{5,4},{6,5},{7,6},{8,11},{9,8},{10,9... | collective-permute-start | bytes 196616 | tf_op jit(solution)/shard_map/ppermute | solution.py:33
  65.8 7.8 %collective-permute-start.16 = (bf16[128,256]{1,0:T(8,128)(2,1)S(1)}, bf16[128,256]{1,0:T(8,128)(2,1)S(1)}, u32[]{:S(2)}, u32[]{:S(2)}) collective-permute-start(bf16[128,256]{1,0:T(8,128)(2,1)S(1)} %get-tuple-element.83), channel_id=1, source_target_pairs={{0,3},{1,0},{2,1},{3,2},{4,7},{5,4},{6,5},{7,6},{8,11},{9,8},{10,9... | collective-permute-start | bytes 196616 | tf_op jit(solution)/shard_map/ppermute | solution.py:33
  68.5 8.8 %collective-permute-start.15 = (bf16[128,256]{1,0:T(8,128)(2,1)S(1)}, bf16[128,256]{1,0:T(8,128)(2,1)S(1)}, u32[]{:S(2)}, u32[]{:S(2)}) collective-permute-start(bf16[128,256]{1,0:T(8,128)(2,1)S(1)} %get-tuple-element.83), channel_id=1, source_target_pairs={{0,2},{1,3},{2,0},{3,1},{4,6},{5,7},{6,4},{7,5},{8,10},{9,11},{10,... | collective-permute-start | bytes 196616 | tf_op jit(solution)/shard_map/ppermute | solution.py:33
  68.6 8.7 %collective-permute-start.14 = (bf16[128,256]{1,0:T(8,128)(2,1)S(1)}, bf16[128,256]{1,0:T(8,128)(2,1)S(1)}, u32[]{:S(2)}, u32[]{:S(2)}) collective-permute-start(bf16[128,256]{1,0:T(8,128)(2,1)S(1)} %get-tuple-element.83), channel_id=1, source_target_pairs={{0,1},{1,2},{2,3},{3,0},{4,5},{5,6},{6,7},{7,4},{8,9},{9,10},{10,1... | collective-permute-start | bytes 196616 | tf_op jit(solution)/shard_map/ppermute | solution.py:33
  69.2 8.2 %collective-permute-start.24 = (bf16[128,256]{1,0:T(8,128)(2,1)S(1)}, bf16[128,256]{1,0:T(8,128)(2,1)S(1)}, u32[]{:S(2)}, u32[]{:S(2)}) collective-permute-start(bf16[128,256]{1,0:T(8,128)(2,1)S(1)} %get-tuple-element.85), channel_id=1, source_target_pairs={{0,3},{1,0},{2,1},{3,2},{4,7},{5,4},{6,5},{7,6},{8,11},{9,8},{10,9... | collective-permute-start | bytes 196616 | tf_op jit(solution)/shard_map/ppermute | solution.py:33
  72.5 7.3 %collective-permute-start.23 = (bf16[128,256]{1,0:T(8,128)(2,1)S(1)}, bf16[128,256]{1,0:T(8,128)(2,1)S(1)}, u32[]{:S(2)}, u32[]{:S(2)}) collective-permute-start(bf16[128,256]{1,0:T(8,128)(2,1)S(1)} %get-tuple-element.85), channel_id=1, source_target_pairs={{0,2},{1,3},{2,0},{3,1},{4,6},{5,7},{6,4},{7,5},{8,10},{9,11},{10,... | collective-permute-start | bytes 196616 | tf_op jit(solution)/shard_map/ppermute | solution.py:33
  79.8 10.7 %collective-permute-start.25 = (bf16[512,256]{1,0:T(8,128)(2,1)S(1)}, bf16[512,256]{1,0:T(8,128)(2,1)S(1)}, u32[]{:S(2)}, u32[]{:S(2)}) collective-permute-start(bf16[512,256]{1,0:T(8,128)(2,1)S(1)} %pad_maximum_fusion.7.slope_ref), channel_id=1, source_target_pairs={{0,4},{4,0},{8,12},{12,8},{16,20},{20,16},{24,28},{28,24},{1,5},{5... | collective-permute-start | bytes 786440 | tf_op jit(solution)/shard_map/ppermute | solution.py:29
  82.3 12.6 %collective-permute-start.32 = (bf16[256,256]{1,0:T(8,128)(2,1)S(1)}, bf16[256,256]{1,0:T(8,128)(2,1)}, u32[]{:S(2)}, u32[]{:S(2)}) collective-permute-start(bf16[256,256]{1,0:T(8,128)(2,1)S(1)} %get-tuple-element.71), channel_id=1, source_target_pairs={{0,24},{4,28},{8,16},{12,20},{16,8},{20,12},{24,0},{28,4},{1,25},{... | collective-permute-start | bytes 393224 | tf_op jit(solution)/shard_map/ppermute | solution.py:357
  83.8 11.7 %collective-permute-start.31 = (bf16[256,256]{1,0:T(8,128)(2,1)S(1)}, bf16[256,256]{1,0:T(8,128)(2,1)}, u32[]{:S(2)}, u32[]{:S(2)}) collective-permute-start(bf16[256,256]{1,0:T(8,128)(2,1)S(1)} %get-tuple-element.70), channel_id=1, source_target_pairs={{0,16},{4,20},{8,24},{12,28},{16,0},{20,4},{24,8},{28,12},{1,17},{... | collective-permute-start | bytes 393224 | tf_op jit(solution)/shard_map/ppermute | solution.py:357
  85.4 10.1 %collective-permute-start.30 = (bf16[256,256]{1,0:T(8,128)(2,1)S(1)}, bf16[256,256]{1,0:T(8,128)(2,1)}, u32[]{:S(2)}, u32[]{:S(2)}) collective-permute-start(bf16[256,256]{1,0:T(8,128)(2,1)S(1)} %get-tuple-element.69), channel_id=1, source_target_pairs={{0,8},{4,12},{8,0},{12,4},{16,24},{20,28},{24,16},{28,20},{1,9},{5... | collective-permute-start | bytes 393224 | tf_op jit(solution)/shard_map/ppermute | solution.py:357
  85.8 22.5 %all-to-all-start.1 = ((bf16[8,32,512]{2,1,0:T(8,128)(2,1)}), bf16[8,32,512]{2,1,0:T(8,128)(2,1)S(1)}, u32[]{:S(2)}, u32[]{:S(2)}) async-start(bf16[8,32,512]{2,1,0:T(8,128)(2,1)} %bitcast.15), calls=%async_computation.1 | async-start | bytes 524288 | tf_op jit(solution)/shard_map/all_to_all | solution.py:351
  91.9 7.4 %collective-permute-start.28 = (bf16[256,256]{1,0:T(8,128)(2,1)S(1)}, bf16[256,256]{1,0:T(8,128)(2,1)S(1)}, u32[]{:S(2)}, u32[]{:S(2)}) collective-permute-start(bf16[256,256]{1,0:T(8,128)(2,1)S(1)} %get-tuple-element.67), channel_id=1, source_target_pairs={{0,24},{4,28},{8,16},{12,20},{16,8},{20,12},{24,0},{28,4},{1,25},{... | collective-permute-start | bytes 393224 | tf_op jit(solution)/shard_map/ppermute | solution.py:357
  93.4 8.2 %collective-permute-start.27 = (bf16[256,256]{1,0:T(8,128)(2,1)S(1)}, bf16[256,256]{1,0:T(8,128)(2,1)S(1)}, u32[]{:S(2)}, u32[]{:S(2)}) collective-permute-start(bf16[256,256]{1,0:T(8,128)(2,1)S(1)} %get-tuple-element.66), channel_id=1, source_target_pairs={{0,16},{4,20},{8,24},{12,28},{16,0},{20,4},{24,8},{28,12},{1,17},{... | collective-permute-start | bytes 393224 | tf_op jit(solution)/shard_map/ppermute | solution.py:357
  96.5 11.8 %collective-permute-start.33 = (bf16[256,256]{1,0:T(8,128)(2,1)S(1)}, bf16[256,256]{1,0:T(8,128)(2,1)S(1)}, u32[]{:S(2)}, u32[]{:S(2)}) collective-permute-start(bf16[256,256]{1,0:T(8,128)(2,1)S(1)} %add_convert_fusion), channel_id=1, source_target_pairs={{0,0},{1,10},{2,17},{3,27},{4,4},{5,14},{6,21},{7,31},{8,1},{9,11}... | collective-permute-start | bytes 393224 | tf_op jit(solution)/shard_map/ppermute | solution.py:365
  101.7 10.0 %collective-permute-start.29 = (bf16[256,256]{1,0:T(8,128)(2,1)S(1)}, bf16[256,256]{1,0:T(8,128)(2,1)S(1)}, u32[]{:S(2)}, u32[]{:S(2)}) collective-permute-start(bf16[256,256]{1,0:T(8,128)(2,1)S(1)} %add_convert_fusion.1), channel_id=1, source_target_pairs={{0,0},{1,10},{2,17},{3,27},{4,4},{5,14},{6,21},{7,31},{8,1},{9,11}... | collective-permute-start | bytes 393224 | tf_op jit(solution)/shard_map/ppermute | solution.py:365
  (11 other events, 75.2 us)

commit v6 on v5

--- a/solution.py
+++ b/solution.py
@@ -29,8 +29,12 @@
     return lax.ppermute(array, "dp", [(i, i ^ 1) for i in range(dp_count)])
 
 
-def shifted(array, count, step):
-    return lax.ppermute(array, "tensor", [(i, (i + step) % count) for i in range(count)])
+def turned(index, levels):
+    return sum(((index >> i) & 1) << (levels - 1 - i) for i in range(levels))
+
+
+def crossed(array, count, step):
+    return lax.ppermute(array, "tensor", [(i, i ^ step) for i in range(count)])
 
 
 def prepare_kernel(
@@ -39,9 +43,10 @@
     sent_refs, (rows_ref, total, square) = refs[:count], refs[count:]
     f = pl.program_id(0)
     own = x_ref.shape[0] // count
-    for k in range(count):
-        source = lax.rem(at[0] - k + count, count)
-        rows_ref[k * own : (k + 1) * own, :] = x_ref[pl.ds(pl.multiple_of(source * own, own), own), :]
+    levels = count.bit_length() - 1
+    for i in range(count):
+        source = jnp.bitwise_xor(at[0], turned(i, levels))
+        rows_ref[i * own : (i + 1) * own, :] = x_ref[pl.ds(pl.multiple_of(source * own, own), own), :]
     wide = rows_ref[...].astype(F32)
     gained = (wide * pol_ref[...]).astype(BF16)
 
@@ -68,10 +73,10 @@
 
     @pl.when(f == steps - 1)
     def _():
-        for k in range(count):
-            sent = sent_refs[k]
-            sent[:own, :] = total[k * own : (k + 1) * own, :].astype(BF16)
-            power = jnp.broadcast_to(square[k * own : (k + 1) * own, :], (own, 128)).T
+        for i in range(count):
+            sent = sent_refs[turned(i, levels)]
+            sent[:own, :] = total[i * own : (i + 1) * own, :].astype(BF16)
+            power = jnp.broadcast_to(square[i * own : (i + 1) * own, :], (own, 128)).T
             high = power[: POWER_ROWS // 2].astype(BF16).astype(F32)
             low = power[: POWER_ROWS // 2] - high
             sent[own:, :] = jnp.zeros((POWER_ROWS, sent.shape[1]), BF16)
@@ -145,7 +150,7 @@
     assert cores == 2
     places = dp_count // cores
     levels = places.bit_length() - 1
-    assert 1 << levels == places
+    assert 1 << levels == places == tensor_count
     place = d // cores
     core = d % cores
     group_rows, block = tokens.shape
@@ -163,34 +168,22 @@
     def flat(p, c, z):
         return (p * cores + c) * tensor_count + z
 
-    halves = 2
-    half_rows = shard // halves
-
     def stage(number, held):
-        got, is_getter = [], []
-        for i in range(halves):
+        pairs, is_getter = [], jnp.zeros((), jnp.bool_)
+        for c in range(cores):
             holders = [0]
             for before in range(number):
-                bit = 1 << ((i + before) % levels)
+                bit = 1 << ((c + before) % levels)
                 holders = holders + [q ^ bit for q in holders]
-            bit = 1 << ((i + number) % levels)
-            pairs = [
-                (flat(q ^ z, c, z), flat(q ^ bit ^ z, c, z))
-                for q in holders
-                for c in range(cores)
-                for z in range(tensor_count)
-            ]
-            got.append(lax.ppermute(held[i], AXES, pairs))
-            is_getter.append(
-                functools.reduce(jnp.logical_or, [relative == (q ^ bit) for q in holders])
-            )
-        return got, is_getter
-
-    def select(held, got, is_getter):
-        return [jnp.where(is_getter[i], got[i], held[i]) for i in range(halves)]
-
-    held = [pol_weight[i * half_rows : (i + 1) * half_rows] for i in range(halves)]
-    got, flags = stage(0, held)
+            bit = 1 << ((c + number) % levels)
+            for q in holders:
+                pairs += [
+                    (flat(q ^ z, c, z), flat(q ^ bit ^ z, c, z)) for z in range(tensor_count)
+                ]
+                is_getter = is_getter | ((core == c) & (relative == (q ^ bit)))
+        return lax.ppermute(held, AXES, pairs), is_getter
+
+    got, is_getter = stage(0, pol_weight)
 
     steps = 4
     feature_step = block // steps
@@ -241,38 +234,33 @@
     given_rows, kept_rows, *ref_sent = prepared
 
     ref_got = [ref_sent[0]] + [
-        shifted(ref_sent[k], tensor_count, -k) for k in range(1, tensor_count)
+        crossed(ref_sent[k], tensor_count, k) for k in range(1, tensor_count)
     ]
     got_rows = swapped(given_rows, dp_count)
 
     cot = cotangent.reshape(slot_count, value_width)
-    *got, cot, kept_rows = lax.optimization_barrier((*got, cot, kept_rows))
+    got, cot, kept_rows = lax.optimization_barrier((got, cot, kept_rows))
     parts = []
     for j in range(PARTS):
         cols = slice(j * width, (j + 1) * width)
-        held_part = select([x[:, cols] for x in held], [x[:, cols] for x in got], flags)
+        held_part = jnp.where(is_getter, got[:, cols], pol_weight[:, cols])
         for number in range(1, levels):
-            got_part, flags_part = stage(number, held_part)
+            got_part, is_getter_part = stage(number, held_part)
             if number < levels - 1:
-                held_part = select(held_part, got_part, flags_part)
-        parts.append((held_part, got_part, flags_part))
+                held_part = jnp.where(is_getter_part, got_part, held_part)
+        parts.append((held_part, got_part, is_getter_part))
     got_cot = lax.all_to_all(cot, "dp", split_axis=0, concat_axis=0, tiled=True)
 
-    def turned(z):
-        return sum(((z >> i) & 1) << (levels - 1 - i) for i in range(levels))
-
-    chunk_at = jnp.stack([place ^ s ^ turned(t) for s in range(places)]).astype(jnp.int32)
+    chunk_at = jnp.stack([place ^ s ^ turned(t, levels) for s in range(places)]).astype(jnp.int32)
 
     values, slopes = [], []
     for j in range(PARTS):
-        held_part, got_part, flags_part = parts[j]
+        held_part, got_part, is_getter_part = parts[j]
         if j == 0:
-            *got_part, got_cot = lax.optimization_barrier((*got_part, got_cot))
-        weight = jnp.concatenate(select(held_part, got_part, flags_part), axis=0)
+            got_part, got_cot, *ref_got = lax.optimization_barrier((got_part, got_cot, *ref_got))
+        weight = jnp.where(is_getter_part, got_part, held_part)
         value_given = dot(got_rows, weight).astype(BF16)
         if j == 0:
-            tied = lax.optimization_barrier((value_given, lengths, bins, advantage, logprob_gap))
-            value_given, lengths, bins, advantage, logprob_gap = tied
             smem = pl.BlockSpec(memory_space=pltpu.SMEM)
             vmem = pl.BlockSpec(memory_space=pltpu.VMEM)
             fixed, pull, row_scale, row_at = pl.pallas_call(
@@ -301,25 +289,27 @@
                 *ref_got,
             )
         value_part = dot(kept_rows, weight) + swapped(value_given, dp_count).astype(F32)
-        total = value_part[:own_rows]
-        for k in range(1, tensor_count):
-            part = value_part[k * own_rows : (k + 1) * own_rows].astype(BF16)
-            total = total + shifted(part, tensor_count, -k).astype(F32)
+        total = value_part
+        for level in range(levels):
+            rows = total.shape[0] // 2
+            sent = total[rows:].astype(BF16)
+            total = total[:rows] + crossed(sent, tensor_count, 1 << level).astype(F32)
         values.append(total * row_scale[:, :1])
 
         cols = slice(j * width, (j + 1) * width)
         slope = (fixed[:, cols] + pull[:, :1] * total).astype(BF16)
-        slopes.append(
-            jnp.concatenate(
-                [slope] + [shifted(slope, tensor_count, k) for k in range(1, tensor_count)], axis=0
-            )
-        )
+        for level in reversed(range(levels)):
+            got = crossed(slope, tensor_count, 1 << level)
+            slope = jnp.concatenate([slope, got], axis=0)
+        slopes.append(slope)
 
     sent = dot_rows(row_at, jnp.concatenate(values, axis=1).astype(BF16)).astype(BF16)
 
-    grads = []
+    grad_own, grad_got = [], []
     for j in range(PARTS):
         slopes_got = swapped(slopes[j], dp_count)
+        if j > 0:
+            slopes_got, grad_own[j - 1] = lax.optimization_barrier((slopes_got, grad_own[j - 1]))
         chunks = pl.pallas_call(
             functools.partial(grad_kernel, places, factor),
             grid_spec=pltpu.PrefetchScalarGridSpec(
@@ -346,18 +336,21 @@
             ),
             name="gradient",
         )(chunk_at, kept_rows, got_rows, slopes[j], slopes_got)
+        grad_own.append(chunks[0])
+        grad_got.append([])
         if j == PARTS - 1:
-            *chunks, sent = lax.optimization_barrier((*chunks, sent))
+            grad_own[j], sent = lax.optimization_barrier((grad_own[j], sent))
             policy_values = lax.all_to_all(sent, "dp", split_axis=0, concat_axis=0, tiled=True)
-        total = chunks[0]
         for s in range(1, places):
             pairs = [
                 (p * cores + c, (p ^ s) * cores + c) for p in range(places) for c in range(cores)
             ]
-            total = total + lax.ppermute(chunks[s], "dp", pairs).astype(F32)
-        total = total.astype(BF16)
+            grad_got[j].append(lax.ppermute(chunks[s], "dp", pairs))
+    grads = []
+    for j in range(PARTS):
+        total = (grad_own[j] + sum(x.astype(F32) for x in grad_got[j])).astype(BF16)
         pairs = [
-            (flat(p, c, z), flat(z, c, p ^ turned(z)))
+            (flat(p, c, z), flat(z, c, p ^ turned(z, levels)))
             for p in range(places)
             for c in range(cores)
             for z in range(tensor_count)

time: 115 us -> 113 us (0.983)
  starting transfers between devices: 60.5 us -> 49.6 us
  waiting for transfers between devices: 29.1 us -> 35.7 us
  matrix products: 2.71 us -> 6.57 us
  other arithmetic: 5.76 us -> 4.1 us
    ppermute x27 -> x20, starting transfers between devices: 39.9 us -> 34.3 us  [the longest x11 23 us: crossed(): return lax.ppermute(array, 'tensor', [(i, i ^ step) for i in range(count)])]
    ppermute x27 -> x20, waiting for transfers between devices: 24.6 us -> 30.1 us  [the longest x11 22.7 us: crossed(): return lax.ppermute(array, 'tensor', [(i, i ^ step) for i in range(count)])]
    dot_general x4, matrix products: 1.76 us -> 5.62 us  [dot(): return jnp.dot(a, b, preferred_element_type=F32)]
    all_to_all x1, starting transfers between devices: 6 us -> 3.36 us  [on_device(): got_cot = lax.all_to_all(cot, 'dp', split_axis=0, concat_axis=0, tiled=True)]
    ppermute x2, starting transfers between devices: 9.09 us -> 6.52 us  [on_device(): grads.append(lax.ppermute(total, AXES, pairs))]
    ppermute x2, waiting for transfers between devices: 3.32 us -> 5.56 us  [on_device(): grads.append(lax.ppermute(total, AXES, pairs))]
    slice x4, local copies, waits for them, and re-layouts: 2.2 us -> 0.05 us  [on_device(): sent = total[rows:].astype(BF16)]
    unnamed x15 -> x35, local copies, waits for them, and re-layouts: 0.74 us -> 2.53 us
  transfers between devices with their start and end apart: 36 -> 29, of which waited for: 10 -> 12; matrix products, arithmetic and copies ran while one was open for 7% -> 8% of each run, Pallas kernels for 10% -> 9%
where the time goes in v6:
time: 113 us; the launch traced here: 111 us
  starting transfers between devices  49.6 us (44%)
  waiting for transfers between devices  35.7 us (32%)
  Pallas kernels  11.6 us (10%)
  matrix products  6.57 us (6%)
  other arithmetic  4.1 us (4%)
  local copies, waits for them, and re-layouts  2.69 us (2%)
    ppermute x11, starting transfers between devices, crossed(): return lax.ppermute(array, 'tensor', [(i, i ^ step) for i in range(count)])  23 us
    ppermute x11, waiting for transfers between devices, crossed(): return lax.ppermute(array, 'tensor', [(i, i ^ step) for i in range(count)])  22.7 us
    ppermute x6, starting transfers between devices, on_device(): grad_got[j].append(lax.ppermute(chunks[s], 'dp', pairs))  7.93 us
    ppermute x6, waiting for transfers between devices, on_device(): grad_got[j].append(lax.ppermute(chunks[s], 'dp', pairs))  7.35 us
    pallas_call x1, Pallas kernels, on_device(): pl.pallas_call(functools.partial(prepare_kernel, tensor_count, steps), gr...  7.12 us
    ppermute x2, starting transfers between devices, on_device(): grads.append(lax.ppermute(total, AXES, pairs))  6.52 us
    dot_general x4, matrix products, dot(): return jnp.dot(a, b, preferred_element_type=F32)  5.62 us
    ppermute x2, waiting for transfers between devices, on_device(): grads.append(lax.ppermute(total, AXES, pairs))  5.56 us
  transfers between devices with their start and end apart: 29, of which 12 were waited for; matrix products, arithmetic and copies ran while one was open for 8% of the time, Pallas kernels for 9%

profile of v6, /device:TPU:4, one launch (start us, length us, event | category | flops | bytes accessed | tf_op | source)
XLA Modules:
  0.0 111.3 jit_solution(3170046293247020025)
XLA Ops:
  2.0 7.1 %prepare.1 = (bf16[512,1024]{1,0:T(8,128)(2,1)}, bf16[512,1024]{1,0:T(8,128)(2,1)}, bf16[144,512]{1,0:T(8,128)(2,1)}, bf16[144,512]{1,0:T(8,128)(2,1)}, bf16[144...) custom-call(s32[2]{0:T(128)} %pad_add_fusion.1.at, bf16[512,2048]{1,0:T(8,128)(2,1)} %x_ref.1, f32[1,2048]{1,0:T(1,128)} %bitcast.29, ...), custom_call_target="tpu_custom_call" | custom-call | flops 1073741824 | bytes 8388608 | tf_op jit(solution)/shard_map/prepare/pallas_call | solution.py:196
  10.5 1.6 %slice_select_fusion = (bf16[1024,256]{1,0:T(8,128)(2,1)S(1)}, bf16[1024,256]{1,0:T(8,128)(2,1)S(1)}) fusion(bf16[1024,512]{1,0:T(8,128)(2,1)} %param.14, bf16[1024,512]{1,0:T(8,128)(2,1)} %copy-done.13, pred[]{:T(512)S(6)} %or.15), kind=kLoop, calls=%fused_computation.5 | loop fusion | flops 524288 | bytes 3145729 | tf_op jit(solution)/shard_map/jit(_where)/select_n | solution.py:246
  12.2 1.3 %collective-permute-start.6 = (bf16[1024,256]{1,0:T(8,128)(2,1)S(1)}, bf16[1024,256]{1,0:T(8,128)(2,1)S(1)}, u32[]{:S(2)}, u32[]{:S(2)}) collective-permute-start(bf16[1024,256]{1,0:T(8,128)(2,1)S(1)} %get-tuple-element.64), channel_id=1, source_target_pairs={{0,16},{9,25},{18,2},{27,11},{8,24},{1,17},{26,10},{19,3},{4,12},{... | collective-permute-start | bytes 1572872 | tf_op jit(solution)/shard_map/ppermute | solution.py:184
  13.5 1.3 %collective-permute-start.2 = (bf16[1024,256]{1,0:T(8,128)(2,1)S(1)}, bf16[1024,256]{1,0:T(8,128)(2,1)}, u32[]{:S(2)}, u32[]{:S(2)}) collective-permute-start(bf16[1024,256]{1,0:T(8,128)(2,1)S(1)} %get-tuple-element.65), channel_id=1, source_target_pairs={{0,16},{9,25},{18,2},{27,11},{8,24},{1,17},{26,10},{19,3},{4,12},{... | collective-permute-start | bytes 1572872 | tf_op jit(solution)/shard_map/ppermute | solution.py:184
  14.8 1.3 %collective-permute-start.3 = (bf16[144,512]{1,0:T(8,128)(2,1)}, bf16[144,512]{1,0:T(8,128)(2,1)S(1)}, u32[]{:S(2)}, u32[]{:S(2)}) collective-permute-start(bf16[144,512]{1,0:T(8,128)(2,1)} %get-tuple-element.39), channel_id=1, source_target_pairs={{0,1},{1,0},{2,3},{3,2},{4,5},{5,4},{6,7},{7,6},{8,9},{9,8},{10,11... | collective-permute-start | bytes 442376 | tf_op jit(solution)/shard_map/ppermute | solution.py:37
  16.1 11.7 %collective-permute-start.4 = (bf16[144,512]{1,0:T(8,128)(2,1)}, bf16[144,512]{1,0:T(8,128)(2,1)S(1)}, u32[]{:S(2)}, u32[]{:S(2)}) collective-permute-start(bf16[144,512]{1,0:T(8,128)(2,1)} %get-tuple-element.40), channel_id=1, source_target_pairs={{0,2},{1,3},{2,0},{3,1},{4,6},{5,7},{6,4},{7,5},{8,10},{9,11},{10,... | collective-permute-start | bytes 442376 | tf_op jit(solution)/shard_map/ppermute | solution.py:37
  27.7 3.4 %all-to-all-start = ((bf16[8,32,512]{2,1,0:T(8,128)(2,1)}), bf16[8,32,512]{2,1,0:T(8,128)(2,1)S(1)}, u32[]{:S(2)}, u32[]{:S(2)}) async-start(bf16[8,32,512]{2,1,0:T(8,128)(2,1)} %bitcast.13), calls=%async_computation | async-start | bytes 524288 | tf_op jit(solution)/shard_map/all_to_all | solution.py:252
  34.0 5.2 %collective-permute-done.5.refs_3_ = bf16[144,512]{1,0:T(8,128)(2,1)S(1)} collective-permute-done((bf16[144,512]{1,0:T(8,128)(2,1)}, bf16[144,512]{1,0:T(8,128)(2,1)S(1)}, u32[]{:S(2)}, u32[]{:S(2)}) %collective-permute-start.5) | collective-permute-done | bytes 147488 | tf_op jit(solution)/shard_map/ppermute | solution.py:37
  39.2 1.6 %convolution_convert_fusion.1 = bf16[512,256]{1,0:T(8,128)(2,1)S(1)} fusion(bf16[512,1024]{1,0:T(8,128)(2,1)S(1)} %collective-permute-done.1.got_ref, bf16[1024,256]{1,0:T(8,128)(2,1)} %collective-permute-done.2, bf16[1024,256]{1,0:T(8,128)(2,1)S(1)} %get-tuple-element.65, pred[]{:T(512)S(6)} %or.18), kind=kOutput, calls=%fused_computation.3 | convolution fusion | flops 268828672 | bytes 2359297 | tf_op jit(solution)/shard_map/dot_general | solution.py:21
  42.0 1.4 %convolution_add_fusion.1 = f32[512,256]{1,0:T(8,128)S(1)} fusion(bf16[512,1024]{1,0:T(8,128)(2,1)S(1)} %copy-done, bf16[512,256]{1,0:T(8,128)(2,1)} %collective-permute-done.7, bf16[1024,256]{1,0:T(8,128)(2,1)S(1)} %copy-done.15, bf16[1024,256]{1,0:T(8,128)(2,1)S(1)} %copy-done.12, pred[]{:T(512)S(6)} %or.18), kind=kOutput, calls=%fused_computation.1 | convolution fusion | flops 268959744 | bytes 2883585 | tf_op jit(solution)/shard_map/dot_general | solution.py:21
  43.5 2.7 %collective-permute-start.8 = (bf16[256,256]{1,0:T(8,128)(2,1)S(1)}, bf16[256,256]{1,0:T(8,128)(2,1)S(1)}, u32[]{:S(2)}, u32[]{:S(2)}) collective-permute-start(bf16[256,256]{1,0:T(8,128)(2,1)S(1)} %slice.103), channel_id=1, source_target_pairs={{0,1},{1,0},{2,3},{3,2},{4,5},{5,4},{6,7},{7,6},{8,9},{9,8},{10,11... | collective-permute-start | bytes 393224 | tf_op jit(solution)/shard_map/ppermute | solution.py:37
  46.2 1.5 %convolution_add_fusion = f32[512,256]{1,0:T(8,128)S(1)} fusion(bf16[512,1024]{1,0:T(8,128)(2,1)S(1)} %copy-done, bf16[512,256]{1,0:T(8,128)(2,1)S(1)} %collective-permute-done.13, bf16[1024,256]{1,0:T(8,128)(2,1)} %collective-permute-done.2, bf16[1024,256]{1,0:T(8,128)(2,1)S(1)} %copy-done.10, pred[]{:T(512)S(6)} %or.18), kind=kOutput, calls=%fused_computation | convolution fusion | flops 268959744 | bytes 2883585 | tf_op jit(solution)/shard_map/dot_general | solution.py:21
  47.8 2.7 %collective-permute-done.8 = bf16[256,256]{1,0:T(8,128)(2,1)S(1)} collective-permute-done((bf16[256,256]{1,0:T(8,128)(2,1)S(1)}, bf16[256,256]{1,0:T(8,128)(2,1)S(1)}, u32[]{:S(2)}, u32[]{:S(2)}) %collective-permute-start.8) | collective-permute-done | bytes 131104 | tf_op jit(solution)/shard_map/ppermute | solution.py:37
  51.2 1.9 %collective-permute-done.14 = bf16[256,256]{1,0:T(8,128)(2,1)S(1)} collective-permute-done((bf16[256,256]{1,0:T(8,128)(2,1)S(1)}, bf16[256,256]{1,0:T(8,128)(2,1)S(1)}, u32[]{:S(2)}, u32[]{:S(2)}) %collective-permute-start.14) | collective-permute-done | bytes 131104 | tf_op jit(solution)/shard_map/ppermute | solution.py:37
  53.8 3.5 %collective-permute-done.9 = bf16[128,256]{1,0:T(8,128)(2,1)S(1)} collective-permute-done((bf16[128,256]{1,0:T(8,128)(2,1)S(1)}, bf16[128,256]{1,0:T(8,128)(2,1)S(1)}, u32[]{:S(2)}, u32[]{:S(2)}) %collective-permute-start.9) | collective-permute-done | bytes 65568 | tf_op jit(solution)/shard_map/ppermute | solution.py:37
  57.3 1.7 %collective-permute-done.15 = bf16[128,256]{1,0:T(8,128)(2,1)S(1)} collective-permute-done((bf16[128,256]{1,0:T(8,128)(2,1)S(1)}, bf16[128,256]{1,0:T(8,128)(2,1)S(1)}, u32[]{:S(2)}, u32[]{:S(2)}) %collective-permute-start.15) | collective-permute-done | bytes 65568 | tf_op jit(solution)/shard_map/ppermute | solution.py:37
  59.7 2.9 %collective-permute-start.10 = (bf16[128,256]{1,0:T(8,128)(2,1)S(1)}, bf16[128,256]{1,0:T(8,128)(2,1)S(1)}, u32[]{:S(2)}, u32[]{:S(2)}) collective-permute-start(bf16[128,256]{1,0:T(8,128)(2,1)S(1)} %get-tuple-element.69), channel_id=1, source_target_pairs={{0,2},{1,3},{2,0},{3,1},{4,6},{5,7},{6,4},{7,5},{8,10},{9,11},{10,... | collective-permute-start | bytes 196616 | tf_op jit(solution)/shard_map/ppermute | solution.py:37
  62.6 2.2 %collective-permute-done.16 = bf16[128,256]{1,0:T(8,128)(2,1)S(1)} collective-permute-done((bf16[128,256]{1,0:T(8,128)(2,1)S(1)}, bf16[128,256]{1,0:T(8,128)(2,1)S(1)}, u32[]{:S(2)}, u32[]{:S(2)}) %collective-permute-start.16) | collective-permute-done | bytes 65568 | tf_op jit(solution)/shard_map/ppermute | solution.py:37
  64.9 2.3 %collective-permute-start.17 = (bf16[256,256]{1,0:T(8,128)(2,1)S(1)}, bf16[256,256]{1,0:T(8,128)(2,1)S(1)}, u32[]{:S(2)}, u32[]{:S(2)}) collective-permute-start(bf16[256,256]{1,0:T(8,128)(2,1)S(1)} %pad_maximum_fusion.3), channel_id=1, source_target_pairs={{0,1},{1,0},{2,3},{3,2},{4,5},{5,4},{6,7},{7,6},{8,9},{9,8},{10,11... | collective-permute-start | bytes 393224 | tf_op jit(solution)/shard_map/ppermute | solution.py:37
  67.9 2.9 %collective-permute-done.17 = bf16[256,256]{1,0:T(8,128)(2,1)S(1)} collective-permute-done((bf16[256,256]{1,0:T(8,128)(2,1)S(1)}, bf16[256,256]{1,0:T(8,128)(2,1)S(1)}, u32[]{:S(2)}, u32[]{:S(2)}) %collective-permute-start.17) | collective-permute-done | bytes 131104 | tf_op jit(solution)/shard_map/ppermute | solution.py:37
  70.9 1.9 %collective-permute-done.11 = bf16[256,256]{1,0:T(8,128)(2,1)S(1)} collective-permute-done((bf16[256,256]{1,0:T(8,128)(2,1)S(1)}, bf16[256,256]{1,0:T(8,128)(2,1)S(1)}, u32[]{:S(2)}, u32[]{:S(2)}) %collective-permute-start.11) | collective-permute-done | bytes 131104 | tf_op jit(solution)/shard_map/ppermute | solution.py:37
  73.0 1.4 %gradient.2 = (f32[256,256]{1,0:T(8,128)S(1)}, bf16[256,256]{1,0:T(8,128)(2,1)S(1)}, bf16[256,256]{1,0:T(8,128)(2,1)S(1)}, bf16[256,256]{1,0:T(8,128)(2,1)S(1)}) custom-call(s32[4]{0:T(128)S(1)} %pad_add_fusion.at, bf16[512,1024]{1,0:T(8,128)(2,1)S(1)} %copy-done, bf16[512,1024]{1,0:T(8,128)(2,1)S(1)} %collective-permute-done.1.got_ref, ...), custom_call_target="tpu_custom_call" | custom-call | flops 536870912 | bytes 4194304 | tf_op jit(solution)/shard_map/gradient/pallas_call | solution.py:313
  74.5 2.1 %gradient.3 = (f32[256,256]{1,0:T(8,128)S(1)}, bf16[256,256]{1,0:T(8,128)(2,1)S(1)}, bf16[256,256]{1,0:T(8,128)(2,1)S(1)}, bf16[256,256]{1,0:T(8,128)(2,1)}) custom-call(s32[4]{0:T(128)S(1)} %pad_add_fusion.at, bf16[512,1024]{1,0:T(8,128)(2,1)S(1)} %copy-done, bf16[512,1024]{1,0:T(8,128)(2,1)S(1)} %collective-permute-done.1.got_ref, ...), custom_call_target="tpu_custom_call" | custom-call | flops 536870912 | bytes 4194304 | tf_op jit(solution)/shard_map/gradient/pallas_call | solution.py:313
  77.4 3.6 %collective-permute-start.24 = (bf16[256,256]{1,0:T(8,128)(2,1)S(1)}, bf16[256,256]{1,0:T(8,128)(2,1)S(1)}, u32[]{:S(2)}, u32[]{:S(2)}) collective-permute-start(bf16[256,256]{1,0:T(8,128)(2,1)S(1)} %get-tuple-element.62), channel_id=1, source_target_pairs={{0,16},{4,20},{8,24},{12,28},{16,0},{20,4},{24,8},{28,12},{1,17},{... | collective-permute-start | bytes 393224 | tf_op jit(solution)/shard_map/ppermute | solution.py:348
  81.9 4.8 %all-to-all-start.1 = ((bf16[8,32,512]{2,1,0:T(8,128)(2,1)}), bf16[8,32,512]{2,1,0:T(8,128)(2,1)S(1)}, u32[]{:S(2)}, u32[]{:S(2)}) async-start(bf16[8,32,512]{2,1,0:T(8,128)(2,1)} %bitcast.15), calls=%async_computation.1 | async-start | bytes 524288 | tf_op jit(solution)/shard_map/all_to_all | solution.py:343
  86.7 1.5 %collective-permute-start.21 = (bf16[256,256]{1,0:T(8,128)(2,1)}, bf16[256,256]{1,0:T(8,128)(2,1)S(1)}, u32[]{:S(2)}, u32[]{:S(2)}) collective-permute-start(bf16[256,256]{1,0:T(8,128)(2,1)} %copy-done.8), channel_id=1, source_target_pairs={{0,24},{4,28},{8,16},{12,20},{16,8},{20,12},{24,0},{28,4},{1,25},{... | collective-permute-start | bytes 393224 | tf_op jit(solution)/shard_map/ppermute | solution.py:348
  88.2 1.5 %collective-permute-start.20 = (bf16[256,256]{1,0:T(8,128)(2,1)}, bf16[256,256]{1,0:T(8,128)(2,1)S(1)}, u32[]{:S(2)}, u32[]{:S(2)}) collective-permute-start(bf16[256,256]{1,0:T(8,128)(2,1)} %copy-done.7), channel_id=1, source_target_pairs={{0,16},{4,20},{8,24},{12,28},{16,0},{20,4},{24,8},{28,12},{1,17},{... | collective-permute-start | bytes 393224 | tf_op jit(solution)/shard_map/ppermute | solution.py:348
  90.3 2.6 %collective-permute-start.26 = (bf16[256,256]{1,0:T(8,128)(2,1)S(1)}, bf16[256,256]{1,0:T(8,128)(2,1)S(1)}, u32[]{:S(2)}, u32[]{:S(2)}) collective-permute-start(bf16[256,256]{1,0:T(8,128)(2,1)S(1)} %add_convert_fusion), channel_id=1, source_target_pairs={{0,0},{1,10},{2,17},{3,27},{4,4},{5,14},{6,21},{7,31},{8,1},{9,11}... | collective-permute-start | bytes 393224 | tf_op jit(solution)/shard_map/ppermute | solution.py:358
  92.8 2.6 %collective-permute-done.21 = bf16[256,256]{1,0:T(8,128)(2,1)S(1)} collective-permute-done((bf16[256,256]{1,0:T(8,128)(2,1)}, bf16[256,256]{1,0:T(8,128)(2,1)S(1)}, u32[]{:S(2)}, u32[]{:S(2)}) %collective-permute-start.21) | collective-permute-done | bytes 131104 | tf_op jit(solution)/shard_map/ppermute | solution.py:348
  95.4 4.7 %collective-permute-done.20 = bf16[256,256]{1,0:T(8,128)(2,1)S(1)} collective-permute-done((bf16[256,256]{1,0:T(8,128)(2,1)}, bf16[256,256]{1,0:T(8,128)(2,1)S(1)}, u32[]{:S(2)}, u32[]{:S(2)}) %collective-permute-start.20) | collective-permute-done | bytes 131104 | tf_op jit(solution)/shard_map/ppermute | solution.py:348
  100.2 4.0 %collective-permute-start.22 = (bf16[256,256]{1,0:T(8,128)(2,1)S(1)}, bf16[256,256]{1,0:T(8,128)(2,1)S(1)}, u32[]{:S(2)}, u32[]{:S(2)}) collective-permute-start(bf16[256,256]{1,0:T(8,128)(2,1)S(1)} %add_convert_fusion.1), channel_id=1, source_target_pairs={{0,0},{1,10},{2,17},{3,27},{4,4},{5,14},{6,21},{7,31},{8,1},{9,11}... | collective-permute-start | bytes 393224 | tf_op jit(solution)/shard_map/ppermute | solution.py:358
  104.2 5.6 %collective-permute-done.22 = bf16[256,256]{1,0:T(8,128)(2,1)S(1)} collective-permute-done((bf16[256,256]{1,0:T(8,128)(2,1)S(1)}, bf16[256,256]{1,0:T(8,128)(2,1)S(1)}, u32[]{:S(2)}, u32[]{:S(2)}) %collective-permute-start.22) | collective-permute-done | bytes 131104 | tf_op jit(solution)/shard_map/ppermute | solution.py:358
  (88 shorter events, 13.9 us)
Async XLA Ops:
  0.6 8.9 %collective-permute-start = (bf16[1024,512]{1,0:T(8,128)(2,1)}, bf16[1024,512]{1,0:T(8,128)(2,1)S(1)}, u32[]{:S(2)}, u32[]{:S(2)}) collective-permute-start(bf16[1024,512]{1,0:T(8,128)(2,1)} %param.14), channel_id=1, source_target_pairs={{0,8},{9,1},{18,26},{27,19},{4,20},{13,29},{22,6},{31,15}} | collective-permute-start | bytes 3145736 | tf_op jit(solution)/shard_map/ppermute | solution.py:184
  9.1 22.0 %collective-permute-start.1 = (bf16[512,1024]{1,0:T(8,128)(2,1)}, bf16[512,1024]{1,0:T(8,128)(2,1)S(1)}, u32[]{:S(2)}, u32[]{:S(2)}) collective-permute-start(bf16[512,1024]{1,0:T(8,128)(2,1)} %get-tuple-element.35), channel_id=1, source_target_pairs={{0,4},{4,0},{8,12},{12,8},{16,20},{20,16},{24,28},{28,24},{1,5},{5... | collective-permute-start | bytes 3145736 | tf_op jit(solution)/shard_map/ppermute | solution.py:29
  12.2 19.8 %copy-start.11 = (bf16[1024,256]{1,0:T(8,128)(2,1)}, bf16[1024,256]{1,0:T(8,128)(2,1)S(1)}, u32[]{:S(2)}) copy-start(bf16[1024,256]{1,0:T(8,128)(2,1)S(1)} %get-tuple-element.64) | copy-start | bytes 1572868
  12.2 28.6 %copy-start.9 = (bf16[1024,256]{1,0:T(8,128)(2,1)}, bf16[1024,256]{1,0:T(8,128)(2,1)S(1)}, u32[]{:S(2)}) copy-start(bf16[1024,256]{1,0:T(8,128)(2,1)S(1)} %get-tuple-element.65) | copy-start | bytes 1572868
  12.2 19.8 %collective-permute-start.6 = (bf16[1024,256]{1,0:T(8,128)(2,1)S(1)}, bf16[1024,256]{1,0:T(8,128)(2,1)S(1)}, u32[]{:S(2)}, u32[]{:S(2)}) collective-permute-start(bf16[1024,256]{1,0:T(8,128)(2,1)S(1)} %get-tuple-element.64), channel_id=1, source_target_pairs={{0,16},{9,25},{18,2},{27,11},{8,24},{1,17},{26,10},{19,3},{4,12},{... | collective-permute-start | bytes 1572872 | tf_op jit(solution)/shard_map/ppermute | solution.py:184
  13.5 25.7 %collective-permute-start.2 = (bf16[1024,256]{1,0:T(8,128)(2,1)S(1)}, bf16[1024,256]{1,0:T(8,128)(2,1)}, u32[]{:S(2)}, u32[]{:S(2)}) collective-permute-start(bf16[1024,256]{1,0:T(8,128)(2,1)S(1)} %get-tuple-element.65), channel_id=1, source_target_pairs={{0,16},{9,25},{18,2},{27,11},{8,24},{1,17},{26,10},{19,3},{4,12},{... | collective-permute-start | bytes 1572872 | tf_op jit(solution)/shard_map/ppermute | solution.py:184
  14.8 19.2 %collective-permute-start.3 = (bf16[144,512]{1,0:T(8,128)(2,1)}, bf16[144,512]{1,0:T(8,128)(2,1)S(1)}, u32[]{:S(2)}, u32[]{:S(2)}) collective-permute-start(bf16[144,512]{1,0:T(8,128)(2,1)} %get-tuple-element.39), channel_id=1, source_target_pairs={{0,1},{1,0},{2,3},{3,2},{4,5},{5,4},{6,7},{7,6},{8,9},{9,8},{10,11... | collective-permute-start | bytes 442376 | tf_op jit(solution)/shard_map/ppermute | solution.py:37
  16.1 17.9 %collective-permute-start.4 = (bf16[144,512]{1,0:T(8,128)(2,1)}, bf16[144,512]{1,0:T(8,128)(2,1)S(1)}, u32[]{:S(2)}, u32[]{:S(2)}) collective-permute-start(bf16[144,512]{1,0:T(8,128)(2,1)} %get-tuple-element.40), channel_id=1, source_target_pairs={{0,2},{1,3},{2,0},{3,1},{4,6},{5,7},{6,4},{7,5},{8,10},{9,11},{10,... | collective-permute-start | bytes 442376 | tf_op jit(solution)/shard_map/ppermute | solution.py:37
  27.7 11.4 %all-to-all-start = ((bf16[8,32,512]{2,1,0:T(8,128)(2,1)}), bf16[8,32,512]{2,1,0:T(8,128)(2,1)S(1)}, u32[]{:S(2)}, u32[]{:S(2)}) async-start(bf16[8,32,512]{2,1,0:T(8,128)(2,1)} %bitcast.13), calls=%async_computation | async-start | bytes 524288 | tf_op jit(solution)/shard_map/all_to_all | solution.py:252
  31.1 9.8 %copy-start.1 = (bf16[144,512]{1,0:T(8,128)(2,1)S(1)}, bf16[144,512]{1,0:T(8,128)(2,1)}, u32[]{:S(2)}) copy-start(bf16[144,512]{1,0:T(8,128)(2,1)} %get-tuple-element.43.refs_0_) | copy-start | bytes 442372
  31.2 8.0 %collective-permute-start.5 = (bf16[144,512]{1,0:T(8,128)(2,1)}, bf16[144,512]{1,0:T(8,128)(2,1)S(1)}, u32[]{:S(2)}, u32[]{:S(2)}) collective-permute-start(bf16[144,512]{1,0:T(8,128)(2,1)} %get-tuple-element.41), channel_id=1, source_target_pairs={{0,3},{1,2},{2,1},{3,0},{4,7},{5,6},{6,5},{7,4},{8,11},{9,10},{10,... | collective-permute-start | bytes 442376 | tf_op jit(solution)/shard_map/ppermute | solution.py:37
  33.9 8.1 %collective-permute-start.7 = (bf16[512,256]{1,0:T(8,128)(2,1)}, bf16[512,256]{1,0:T(8,128)(2,1)}, u32[]{:S(2)}, u32[]{:S(2)}) collective-permute-start(bf16[512,256]{1,0:T(8,128)(2,1)} %convolution_convert_fusion.2), channel_id=1, source_target_pairs={{0,4},{4,0},{8,12},{12,8},{16,20},{20,16},{24,28},{28,24},{1,5},{5... | collective-permute-start | bytes 786440 | tf_op jit(solution)/shard_map/ppermute | solution.py:29
  40.8 5.4 %collective-permute-start.13 = (bf16[512,256]{1,0:T(8,128)(2,1)S(1)}, bf16[512,256]{1,0:T(8,128)(2,1)S(1)}, u32[]{:S(2)}, u32[]{:S(2)}) collective-permute-start(bf16[512,256]{1,0:T(8,128)(2,1)S(1)} %convolution_convert_fusion.1), channel_id=1, source_target_pairs={{0,4},{4,0},{8,12},{12,8},{16,20},{20,16},{24,28},{28,24},{1,5},{5... | collective-permute-start | bytes 786440 | tf_op jit(solution)/shard_map/ppermute | solution.py:29
  43.5 7.0 %collective-permute-start.8 = (bf16[256,256]{1,0:T(8,128)(2,1)S(1)}, bf16[256,256]{1,0:T(8,128)(2,1)S(1)}, u32[]{:S(2)}, u32[]{:S(2)}) collective-permute-start(bf16[256,256]{1,0:T(8,128)(2,1)S(1)} %slice.103), channel_id=1, source_target_pairs={{0,1},{1,0},{2,3},{3,2},{4,5},{5,4},{6,7},{7,6},{8,9},{9,8},{10,11... | collective-permute-start | bytes 393224 | tf_op jit(solution)/shard_map/ppermute | solution.py:37
  47.7 5.4 %collective-permute-start.14 = (bf16[256,256]{1,0:T(8,128)(2,1)S(1)}, bf16[256,256]{1,0:T(8,128)(2,1)S(1)}, u32[]{:S(2)}, u32[]{:S(2)}) collective-permute-start(bf16[256,256]{1,0:T(8,128)(2,1)S(1)} %slice.102), channel_id=1, source_target_pairs={{0,1},{1,0},{2,3},{3,2},{4,5},{5,4},{6,7},{7,6},{8,9},{9,8},{10,11... | collective-permute-start | bytes 393224 | tf_op jit(solution)/shard_map/ppermute | solution.py:37
  50.6 6.7 %collective-permute-start.9 = (bf16[128,256]{1,0:T(8,128)(2,1)S(1)}, bf16[128,256]{1,0:T(8,128)(2,1)S(1)}, u32[]{:S(2)}, u32[]{:S(2)}) collective-permute-start(bf16[128,256]{1,0:T(8,128)(2,1)S(1)} %slice.105), channel_id=1, source_target_pairs={{0,2},{1,3},{2,0},{3,1},{4,6},{5,7},{6,4},{7,5},{8,10},{9,11},{10,... | collective-permute-start | bytes 196616 | tf_op jit(solution)/shard_map/ppermute | solution.py:37
  53.2 5.8 %collective-permute-start.15 = (bf16[128,256]{1,0:T(8,128)(2,1)S(1)}, bf16[128,256]{1,0:T(8,128)(2,1)S(1)}, u32[]{:S(2)}, u32[]{:S(2)}) collective-permute-start(bf16[128,256]{1,0:T(8,128)(2,1)S(1)} %slice.104), channel_id=1, source_target_pairs={{0,2},{1,3},{2,0},{3,1},{4,6},{5,7},{6,4},{7,5},{8,10},{9,11},{10,... | collective-permute-start | bytes 196616 | tf_op jit(solution)/shard_map/ppermute | solution.py:37
  59.7 5.2 %collective-permute-start.16 = (bf16[128,256]{1,0:T(8,128)(2,1)S(1)}, bf16[128,256]{1,0:T(8,128)(2,1)S(1)}, u32[]{:S(2)}, u32[]{:S(2)}) collective-permute-start(bf16[128,256]{1,0:T(8,128)(2,1)S(1)} %get-tuple-element.70), channel_id=1, source_target_pairs={{0,2},{1,3},{2,0},{3,1},{4,6},{5,7},{6,4},{7,5},{8,10},{9,11},{10,... | collective-permute-start | bytes 196616 | tf_op jit(solution)/shard_map/ppermute | solution.py:37
  59.7 8.1 %collective-permute-start.10 = (bf16[128,256]{1,0:T(8,128)(2,1)S(1)}, bf16[128,256]{1,0:T(8,128)(2,1)S(1)}, u32[]{:S(2)}, u32[]{:S(2)}) collective-permute-start(bf16[128,256]{1,0:T(8,128)(2,1)S(1)} %get-tuple-element.69), channel_id=1, source_target_pairs={{0,2},{1,3},{2,0},{3,1},{4,6},{5,7},{6,4},{7,5},{8,10},{9,11},{10,... | collective-permute-start | bytes 196616 | tf_op jit(solution)/shard_map/ppermute | solution.py:37
  64.9 5.9 %collective-permute-start.17 = (bf16[256,256]{1,0:T(8,128)(2,1)S(1)}, bf16[256,256]{1,0:T(8,128)(2,1)S(1)}, u32[]{:S(2)}, u32[]{:S(2)}) collective-permute-start(bf16[256,256]{1,0:T(8,128)(2,1)S(1)} %pad_maximum_fusion.3), channel_id=1, source_target_pairs={{0,1},{1,0},{2,3},{3,2},{4,5},{5,4},{6,7},{7,6},{8,9},{9,8},{10,11... | collective-permute-start | bytes 393224 | tf_op jit(solution)/shard_map/ppermute | solution.py:37
  67.8 5.0 %collective-permute-start.11 = (bf16[256,256]{1,0:T(8,128)(2,1)S(1)}, bf16[256,256]{1,0:T(8,128)(2,1)S(1)}, u32[]{:S(2)}, u32[]{:S(2)}) collective-permute-start(bf16[256,256]{1,0:T(8,128)(2,1)S(1)} %pad_maximum_fusion.2), channel_id=1, source_target_pairs={{0,1},{1,0},{2,3},{3,2},{4,5},{5,4},{6,7},{7,6},{8,9},{9,8},{10,11... | collective-permute-start | bytes 393224 | tf_op jit(solution)/shard_map/ppermute | solution.py:37
  70.8 2.2 %collective-permute-start.18 = (bf16[512,256]{1,0:T(8,128)(2,1)S(1)}, bf16[512,256]{1,0:T(8,128)(2,1)S(1)}, u32[]{:S(2)}, u32[]{:S(2)}) collective-permute-start(bf16[512,256]{1,0:T(8,128)(2,1)S(1)} %pad_maximum_fusion.1.slope_ref), channel_id=1, source_target_pairs={{0,4},{4,0},{8,12},{12,8},{16,20},{20,16},{24,28},{28,24},{1,5},{5... | collective-permute-start | bytes 786440 | tf_op jit(solution)/shard_map/ppermute | solution.py:29
  72.9 1.6 %collective-permute-start.12 = (bf16[512,256]{1,0:T(8,128)(2,1)S(1)}, bf16[512,256]{1,0:T(8,128)(2,1)S(1)}, u32[]{:S(2)}, u32[]{:S(2)}) collective-permute-start(bf16[512,256]{1,0:T(8,128)(2,1)S(1)} %pad_maximum_fusion.slope_ref), channel_id=1, source_target_pairs={{0,4},{4,0},{8,12},{12,8},{16,20},{20,16},{24,28},{28,24},{1,5},{5... | collective-permute-start | bytes 786440 | tf_op jit(solution)/shard_map/ppermute | solution.py:29
  76.5 13.1 %collective-permute-start.25 = (bf16[256,256]{1,0:T(8,128)(2,1)}, bf16[256,256]{1,0:T(8,128)(2,1)S(1)}, u32[]{:S(2)}, u32[]{:S(2)}) collective-permute-start(bf16[256,256]{1,0:T(8,128)(2,1)} %get-tuple-element.63), channel_id=1, source_target_pairs={{0,24},{4,28},{8,16},{12,20},{16,8},{20,12},{24,0},{28,4},{1,25},{... | collective-permute-start | bytes 393224 | tf_op jit(solution)/shard_map/ppermute | solution.py:348
  77.4 12.8 %collective-permute-start.24 = (bf16[256,256]{1,0:T(8,128)(2,1)S(1)}, bf16[256,256]{1,0:T(8,128)(2,1)S(1)}, u32[]{:S(2)}, u32[]{:S(2)}) collective-permute-start(bf16[256,256]{1,0:T(8,128)(2,1)S(1)} %get-tuple-element.62), channel_id=1, source_target_pairs={{0,16},{4,20},{8,24},{12,28},{16,0},{20,4},{24,8},{28,12},{1,17},{... | collective-permute-start | bytes 393224 | tf_op jit(solution)/shard_map/ppermute | solution.py:348
  81.0 9.2 %collective-permute-start.23 = (bf16[256,256]{1,0:T(8,128)(2,1)S(1)}, bf16[256,256]{1,0:T(8,128)(2,1)S(1)}, u32[]{:S(2)}, u32[]{:S(2)}) collective-permute-start(bf16[256,256]{1,0:T(8,128)(2,1)S(1)} %get-tuple-element.61), channel_id=1, source_target_pairs={{0,8},{4,12},{8,0},{12,4},{16,24},{20,28},{24,16},{28,20},{1,9},{5... | collective-permute-start | bytes 393224 | tf_op jit(solution)/shard_map/ppermute | solution.py:348
  81.9 22.3 %all-to-all-start.1 = ((bf16[8,32,512]{2,1,0:T(8,128)(2,1)}), bf16[8,32,512]{2,1,0:T(8,128)(2,1)S(1)}, u32[]{:S(2)}, u32[]{:S(2)}) async-start(bf16[8,32,512]{2,1,0:T(8,128)(2,1)} %bitcast.15), calls=%async_computation.1 | async-start | bytes 524288 | tf_op jit(solution)/shard_map/all_to_all | solution.py:343
  86.7 8.8 %collective-permute-start.21 = (bf16[256,256]{1,0:T(8,128)(2,1)}, bf16[256,256]{1,0:T(8,128)(2,1)S(1)}, u32[]{:S(2)}, u32[]{:S(2)}) collective-permute-start(bf16[256,256]{1,0:T(8,128)(2,1)} %copy-done.8), channel_id=1, source_target_pairs={{0,24},{4,28},{8,16},{12,20},{16,8},{20,12},{24,0},{28,4},{1,25},{... | collective-permute-start | bytes 393224 | tf_op jit(solution)/shard_map/ppermute | solution.py:348
  88.2 12.0 %collective-permute-start.20 = (bf16[256,256]{1,0:T(8,128)(2,1)}, bf16[256,256]{1,0:T(8,128)(2,1)S(1)}, u32[]{:S(2)}, u32[]{:S(2)}) collective-permute-start(bf16[256,256]{1,0:T(8,128)(2,1)} %copy-done.7), channel_id=1, source_target_pairs={{0,16},{4,20},{8,24},{12,28},{16,0},{20,4},{24,8},{28,12},{1,17},{... | collective-permute-start | bytes 393224 | tf_op jit(solution)/shard_map/ppermute | solution.py:348
  89.6 10.5 %collective-permute-start.19 = (bf16[256,256]{1,0:T(8,128)(2,1)}, bf16[256,256]{1,0:T(8,128)(2,1)S(1)}, u32[]{:S(2)}, u32[]{:S(2)}) collective-permute-start(bf16[256,256]{1,0:T(8,128)(2,1)} %copy-done.6), channel_id=1, source_target_pairs={{0,8},{4,12},{8,0},{12,4},{16,24},{20,28},{24,16},{28,20},{1,9},{5... | collective-permute-start | bytes 393224 | tf_op jit(solution)/shard_map/ppermute | solution.py:348
  90.3 14.0 %collective-permute-start.26 = (bf16[256,256]{1,0:T(8,128)(2,1)S(1)}, bf16[256,256]{1,0:T(8,128)(2,1)S(1)}, u32[]{:S(2)}, u32[]{:S(2)}) collective-permute-start(bf16[256,256]{1,0:T(8,128)(2,1)S(1)} %add_convert_fusion), channel_id=1, source_target_pairs={{0,0},{1,10},{2,17},{3,27},{4,4},{5,14},{6,21},{7,31},{8,1},{9,11}... | collective-permute-start | bytes 393224 | tf_op jit(solution)/shard_map/ppermute | solution.py:358
  100.2 9.6 %collective-permute-start.22 = (bf16[256,256]{1,0:T(8,128)(2,1)S(1)}, bf16[256,256]{1,0:T(8,128)(2,1)S(1)}, u32[]{:S(2)}, u32[]{:S(2)}) collective-permute-start(bf16[256,256]{1,0:T(8,128)(2,1)S(1)} %add_convert_fusion.1), channel_id=1, source_target_pairs={{0,0},{1,10},{2,17},{3,27},{4,4},{5,14},{6,21},{7,31},{8,1},{9,11}... | collective-permute-start | bytes 393224 | tf_op jit(solution)/shard_map/ppermute | solution.py:358
  (14 other events, 90.2 us)

commit v7 on v6

--- a/solution.py
+++ b/solution.py
@@ -37,18 +37,18 @@
     return lax.ppermute(array, "tensor", [(i, i ^ step) for i in range(count)])
 
 
-def prepare_kernel(
-    count, steps, at, x_ref, gain_ref, weight_ref, pol_ref, given_ref, kept_ref, *refs
-):
-    sent_refs, (rows_ref, total, square) = refs[:count], refs[count:]
-    f = pl.program_id(0)
+def ordered(count, at, x_ref, rows_ref):
+    levels = count.bit_length() - 1
     own = x_ref.shape[0] // count
-    levels = count.bit_length() - 1
     for i in range(count):
         source = jnp.bitwise_xor(at[0], turned(i, levels))
         rows_ref[i * own : (i + 1) * own, :] = x_ref[pl.ds(pl.multiple_of(source * own, own), own), :]
-    wide = rows_ref[...].astype(F32)
-    gained = (wide * pol_ref[...]).astype(BF16)
+    return rows_ref[...].astype(F32)
+
+
+def split_kernel(count, steps, at, x_ref, gain_ref, given_ref, kept_ref, rows_ref):
+    f = pl.program_id(0)
+    gained = (ordered(count, at, x_ref, rows_ref) * gain_ref[...]).astype(BF16)
 
     @pl.when(f < steps // 2)
     def _():
@@ -58,6 +58,13 @@
     def _():
         kept_ref[...] = gained
 
+
+def reference_kernel(
+    count, steps, at, x_ref, gain_ref, weight_ref, kept_ref, sent_ref, rows_ref, total, square
+):
+    f = pl.program_id(0)
+    own = x_ref.shape[0] // count
+    wide = ordered(count, at, x_ref, rows_ref)
     part = dot((wide * gain_ref[...]).astype(BF16), weight_ref[...])
     squares = jnp.sum(wide * wide, axis=1, keepdims=True)
 
@@ -74,19 +81,19 @@
     @pl.when(f == steps - 1)
     def _():
         for i in range(count):
-            sent = sent_refs[turned(i, levels)]
-            sent[:own, :] = total[i * own : (i + 1) * own, :].astype(BF16)
+            out = (kept_ref, sent_ref)[i // (count // 2)].at[i % (count // 2)]
+            out[:own, :] = total[i * own : (i + 1) * own, :].astype(BF16)
             power = jnp.broadcast_to(square[i * own : (i + 1) * own, :], (own, 128)).T
             high = power[: POWER_ROWS // 2].astype(BF16).astype(F32)
             low = power[: POWER_ROWS // 2] - high
-            sent[own:, :] = jnp.zeros((POWER_ROWS, sent.shape[1]), BF16)
-            sent[own:, :own] = jnp.concatenate([high, low], axis=0).astype(BF16)
+            out[own:, :] = jnp.zeros((POWER_ROWS, out.shape[1]), BF16)
+            out[own:, :own] = jnp.concatenate([high, low], axis=0).astype(BF16)
 
 
 def row_kernel(
-    count, span, model_width, lengths, bins, advantage, gap_ref, cot_ref, *refs
+    span, model_width, lengths, bins, advantage, gap_ref, cot_ref, kept_ref, got_ref, *refs
 ):
-    ref_refs, (fixed_ref, pull_ref, scale_ref, row_at_ref) = refs[:count], refs[count:]
+    fixed_ref, pull_ref, scale_ref, row_at_ref = refs
     own = pull_ref.shape[0]
     slots = row_at_ref.shape[1]
     row = lax.broadcasted_iota(jnp.int32, (own, slots), 0)
@@ -107,11 +114,10 @@
     importance = jnp.minimum(jnp.exp(jnp.broadcast_to(gap_ref[...], (128, own)).T), 2.0)
     coef_adv = (weight * importance / size).astype(BF16).astype(F32)
     coef_pull = (BETA / size).astype(BF16).astype(F32)
-    total = ref_refs[0][...].astype(F32)
-    for ref in ref_refs[1:]:
-        total = total + ref[...].astype(F32)
-    half = POWER_ROWS // 2
-    square = total[own : own + 1, :own] + total[own + half : own + half + 1, :own]
+    total = kept_ref[...].astype(F32) + got_ref[...].astype(F32)
+    square = jnp.zeros((1, own), F32)
+    for power_row in range(own, total.shape[0], POWER_ROWS // 2):
+        square = square + total[power_row : power_row + 1, :own]
     scale = lax.rsqrt(jnp.broadcast_to(square, (128, own)).T / model_width + EPS)
     reference = (total[:own] * scale[:, :1]).astype(BF16).astype(F32)
     upstream = dot(row_at, cot_ref[...])
@@ -183,25 +189,40 @@
                 is_getter = is_getter | ((core == c) & (relative == (q ^ bit)))
         return lax.ppermute(held, AXES, pairs), is_getter
 
-    got, is_getter = stage(0, pol_weight)
+    cot = cotangent.reshape(slot_count, value_width)
+    got_cot = lax.all_to_all(cot, "dp", split_axis=0, concat_axis=0, tiled=True)
+    held, got, is_getter = [], [], [None] * PARTS
+    rest = pol_weight
+    for j in range(PARTS):
+        held.append(rest[:, j * width : (j + 1) * width])
+        if j < PARTS - 1:
+            held[j], rest = lax.optimization_barrier((held[j], rest))
+        part, is_getter[j] = stage(0, held[j])
+        got.append(part)
+
+    def later_stages(j):
+        for number in range(1, levels):
+            held[j] = jnp.where(is_getter[j], got[j], held[j])
+            got[j], is_getter[j] = stage(number, held[j])
 
     steps = 4
     feature_step = block // steps
     at = jnp.stack([t, (1 - core) * (steps // 2)]).astype(jnp.int32)
-    sent_shape = (own_rows + POWER_ROWS, value_width)
 
     def at_step(f, at):
         return lax.rem(f + at[1], steps)
 
-    prepared = pl.pallas_call(
-        functools.partial(prepare_kernel, tensor_count, steps),
+    rows_spec = pl.BlockSpec((group_rows, feature_step), lambda f, at: (0, at_step(f, at)))
+    rows_scratch = pltpu.VMEM((group_rows, feature_step), BF16)
+    got[0], tokens, pol_gain = lax.optimization_barrier((got[0], tokens, pol_gain))
+    later_stages(0)
+    given_rows, kept_rows = pl.pallas_call(
+        functools.partial(split_kernel, tensor_count, steps),
         grid_spec=pltpu.PrefetchScalarGridSpec(
             num_scalar_prefetch=1,
             grid=(steps,),
             in_specs=[
-                pl.BlockSpec((group_rows, feature_step), lambda f, at: (0, at_step(f, at))),
-                pl.BlockSpec((1, feature_step), lambda f, at: (0, at_step(f, at))),
-                pl.BlockSpec((feature_step, value_width), lambda f, at: (at_step(f, at), 0)),
+                rows_spec,
                 pl.BlockSpec(
                     (1, feature_step), lambda f, at: (0, at[0] * steps + at_step(f, at))
                 ),
@@ -213,59 +234,68 @@
                 pl.BlockSpec(
                     (group_rows, feature_step), lambda f, at: (0, jnp.maximum(f - steps // 2, 0))
                 ),
-            ]
-            + [pl.BlockSpec(sent_shape, lambda f, at: (0, 0))] * tensor_count,
+            ],
+            scratch_shapes=[rows_scratch],
+        ),
+        out_shape=[jax.ShapeDtypeStruct((group_rows, shard), BF16)] * 2,
+        compiler_params=pltpu.CompilerParams(vmem_limit_bytes=56 * 2**20),
+        cost_estimate=pl.CostEstimate(
+            flops=group_rows * block, bytes_accessed=4 * 2**20, transcendentals=0
+        ),
+        name="split",
+    )(at, tokens, pol_gain.reshape(1, model_width))
+    got_rows = swapped(given_rows, dp_count)
+
+    got[1:], tokens = lax.optimization_barrier((got[1:], tokens))
+    for j in range(1, PARTS):
+        later_stages(j)
+    ref_shape = (tensor_count // 2, own_rows + POWER_ROWS, value_width)
+    ref_kept, ref_sent = pl.pallas_call(
+        functools.partial(reference_kernel, tensor_count, steps),
+        grid_spec=pltpu.PrefetchScalarGridSpec(
+            num_scalar_prefetch=1,
+            grid=(steps,),
+            in_specs=[
+                rows_spec,
+                pl.BlockSpec((1, feature_step), lambda f, at: (0, at_step(f, at))),
+                pl.BlockSpec((feature_step, value_width), lambda f, at: (at_step(f, at), 0)),
+            ],
+            out_specs=[pl.BlockSpec(ref_shape, lambda f, at: (0, 0, 0))] * 2,
             scratch_shapes=[
-                pltpu.VMEM((group_rows, feature_step), BF16),
+                rows_scratch,
                 pltpu.VMEM((group_rows, value_width), F32),
                 pltpu.VMEM((group_rows, 1), F32),
             ],
         ),
-        out_shape=[jax.ShapeDtypeStruct((group_rows, shard), BF16)] * 2
-        + [jax.ShapeDtypeStruct(sent_shape, BF16)] * tensor_count,
+        out_shape=[jax.ShapeDtypeStruct(ref_shape, BF16)] * 2,
         compiler_params=pltpu.CompilerParams(vmem_limit_bytes=56 * 2**20),
         cost_estimate=pl.CostEstimate(
             flops=2 * group_rows * block * value_width,
-            bytes_accessed=8 * 2**20,
+            bytes_accessed=5 * 2**20,
             transcendentals=0,
         ),
-        name="prepare",
-    )(at, tokens, ref_gain.reshape(1, block), ref_weight, pol_gain.reshape(1, model_width))
-    given_rows, kept_rows, *ref_sent = prepared
-
-    ref_got = [ref_sent[0]] + [
-        crossed(ref_sent[k], tensor_count, k) for k in range(1, tensor_count)
-    ]
-    got_rows = swapped(given_rows, dp_count)
-
-    cot = cotangent.reshape(slot_count, value_width)
-    got, cot, kept_rows = lax.optimization_barrier((got, cot, kept_rows))
-    parts = []
-    for j in range(PARTS):
-        cols = slice(j * width, (j + 1) * width)
-        held_part = jnp.where(is_getter, got[:, cols], pol_weight[:, cols])
-        for number in range(1, levels):
-            got_part, is_getter_part = stage(number, held_part)
-            if number < levels - 1:
-                held_part = jnp.where(is_getter_part, got_part, held_part)
-        parts.append((held_part, got_part, is_getter_part))
-    got_cot = lax.all_to_all(cot, "dp", split_axis=0, concat_axis=0, tiled=True)
+        name="reference",
+    )(at, tokens, ref_gain.reshape(1, block), ref_weight)
+    ref_got = crossed(ref_sent, tensor_count, 1)
+    for level in range(1, levels):
+        ref_sum = (ref_kept[:, :own_rows].astype(F32) + ref_got[:, :own_rows].astype(F32)).astype(BF16)
+        ref_all = jnp.concatenate([ref_sum, ref_kept[:, own_rows:], ref_got[:, own_rows:]], axis=1)
+        half_count = ref_all.shape[0] // 2
+        ref_kept = ref_all[:half_count]
+        ref_got = crossed(ref_all[half_count:], tensor_count, 1 << level)
 
     chunk_at = jnp.stack([place ^ s ^ turned(t, levels) for s in range(places)]).astype(jnp.int32)
 
     values, slopes = [], []
     for j in range(PARTS):
-        held_part, got_part, is_getter_part = parts[j]
-        if j == 0:
-            got_part, got_cot, *ref_got = lax.optimization_barrier((got_part, got_cot, *ref_got))
-        weight = jnp.where(is_getter_part, got_part, held_part)
+        weight = jnp.where(is_getter[j], got[j], held[j])
         value_given = dot(got_rows, weight).astype(BF16)
         if j == 0:
             smem = pl.BlockSpec(memory_space=pltpu.SMEM)
             vmem = pl.BlockSpec(memory_space=pltpu.VMEM)
             fixed, pull, row_scale, row_at = pl.pallas_call(
-                functools.partial(row_kernel, tensor_count, span_rows, model_width),
-                in_specs=[smem] * 3 + [vmem] * (2 + tensor_count),
+                functools.partial(row_kernel, span_rows, model_width),
+                in_specs=[smem] * 3 + [vmem] * 4,
                 out_specs=[vmem] * 4,
                 out_shape=[
                     jax.ShapeDtypeStruct((own_rows, value_width), F32),
@@ -286,7 +316,8 @@
                 advantage.reshape(-1),
                 logprob_gap.reshape(1, own_rows),
                 got_cot,
-                *ref_got,
+                ref_kept[0],
+                ref_got[0],
             )
         value_part = dot(kept_rows, weight) + swapped(value_given, dp_count).astype(F32)
         total = value_part
@@ -299,8 +330,7 @@
         cols = slice(j * width, (j + 1) * width)
         slope = (fixed[:, cols] + pull[:, :1] * total).astype(BF16)
         for level in reversed(range(levels)):
-            got = crossed(slope, tensor_count, 1 << level)
-            slope = jnp.concatenate([slope, got], axis=0)
+            slope = jnp.concatenate([slope, crossed(slope, tensor_count, 1 << level)], axis=0)
         slopes.append(slope)
 
     sent = dot_rows(row_at, jnp.concatenate(values, axis=1).astype(BF16)).astype(BF16)
@@ -338,14 +368,13 @@
         )(chunk_at, kept_rows, got_rows, slopes[j], slopes_got)
         grad_own.append(chunks[0])
         grad_got.append([])
-        if j == PARTS - 1:
-            grad_own[j], sent = lax.optimization_barrier((grad_own[j], sent))
-            policy_values = lax.all_to_all(sent, "dp", split_axis=0, concat_axis=0, tiled=True)
         for s in range(1, places):
             pairs = [
                 (p * cores + c, (p ^ s) * cores + c) for p in range(places) for c in range(cores)
             ]
             grad_got[j].append(lax.ppermute(chunks[s], "dp", pairs))
+    grad_got[0][-1], sent = lax.optimization_barrier((grad_got[0][-1], sent))
+    policy_values = lax.all_to_all(sent, "dp", split_axis=0, concat_axis=0, tiled=True)
     grads = []
     for j in range(PARTS):
         total = (grad_own[j] + sum(x.astype(F32) for x in grad_got[j])).astype(BF16)

time: 113 us -> 114 us (level)
  the two profiles are of different devices: /device:TPU:4 before, /device:TPU:0 now
where the time goes in v7:
time: 114 us; the launch traced here: 113 us
  starting transfers between devices  51.7 us (45%)
  waiting for transfers between devices  36.5 us (32%)
  Pallas kernels  15 us (13%)
  local copies, waits for them, and re-layouts  3.85 us (3%)
  matrix products  2.75 us (2%)
  other arithmetic  2.08 us (2%)
    ppermute x10, waiting for transfers between devices, crossed(): return lax.ppermute(array, 'tensor', [(i, i ^ step) for i in range(count)])  22.6 us
    ppermute x10, starting transfers between devices, crossed(): return lax.ppermute(array, 'tensor', [(i, i ^ step) for i in range(count)])  19.7 us
    ppermute x4, starting transfers between devices, stage(): return (lax.ppermute(held, AXES, pairs), is_getter)  10.6 us
    all_to_all x1, starting transfers between devices, on_device(): lax.all_to_all(sent, 'dp', split_axis=0, concat_axis=0, tiled=True)  7.92 us
    ppermute x6, starting transfers between devices, on_device(): grad_got[j].append(lax.ppermute(chunks[s], 'dp', pairs))  7.75 us
    all_to_all x1, waiting for transfers between devices, on_device(): lax.all_to_all(sent, 'dp', split_axis=0, concat_axis=0, tiled=True)  6.06 us
    pallas_call x1, Pallas kernels, on_device(): pl.pallas_call(functools.partial(reference_kernel, tensor_count, steps),...  6.06 us
    ppermute x6, waiting for transfers between devices, on_device(): grad_got[j].append(lax.ppermute(chunks[s], 'dp', pairs))  5.46 us
  transfers between devices with their start and end apart: 29, of which 15 were waited for; matrix products, arithmetic and copies ran while one was open for 6% of the time, Pallas kernels for 13%

profile of v7, /device:TPU:0, one launch (start us, length us, event | category | flops | bytes accessed | tf_op | source)
XLA Modules:
  0.0 112.9 jit_solution(6268284934356324596)
XLA Ops:
  1.7 4.9 %collective-permute-start = (bf16[1024,256]{1,0:T(8,128)(2,1)S(1)}, bf16[1024,256]{1,0:T(8,128)(2,1)S(1)}, u32[]{:S(2)}, u32[]{:S(2)}) collective-permute-start(bf16[1024,256]{1,0:T(8,128)(2,1)S(1)} %slice.66), channel_id=1, source_target_pairs={{0,8},{9,1},{18,26},{27,19},{4,20},{13,29},{22,6},{31,15}} | collective-permute-start | bytes 1572872 | tf_op jit(solution)/shard_map/ppermute | solution.py:190
  6.6 1.1 slice.67
  7.7 1.3 %collective-permute-start.2 = (bf16[1024,256]{1,0:T(8,128)(2,1)S(1)}, bf16[1024,256]{1,0:T(8,128)(2,1)S(1)}, u32[]{:S(2)}, u32[]{:S(2)}) collective-permute-start(bf16[1024,256]{1,0:T(8,128)(2,1)S(1)} %slice.67), channel_id=1, source_target_pairs={{0,8},{9,1},{18,26},{27,19},{4,20},{13,29},{22,6},{31,15}} | collective-permute-start | bytes 1572872 | tf_op jit(solution)/shard_map/ppermute | solution.py:190
  9.0 3.4 %all-to-all-start = ((bf16[8,32,512]{2,1,0:T(8,128)(2,1)}), bf16[8,32,512]{2,1,0:T(8,128)(2,1)S(1)}, u32[]{:S(2)}, u32[]{:S(2)}) async-start(bf16[8,32,512]{2,1,0:T(8,128)(2,1)} %bitcast.11), calls=%async_computation | async-start | bytes 524288 | tf_op jit(solution)/shard_map/all_to_all | solution.py:193
  13.2 5.1 %split.1 = (bf16[512,1024]{1,0:T(8,128)(2,1)}, bf16[512,1024]{1,0:T(8,128)(2,1)}) custom-call(s32[2]{0:T(128)} %pad_add_fusion.1.at, bf16[512,2048]{1,0:T(8,128)(2,1)} %x_ref.1, f32[1,8192]{1,0:T(1,128)} %bitcast.31), custom_call_target="tpu_custom_call" | custom-call | flops 1048576 | bytes 4194304 | tf_op jit(solution)/shard_map/split/pallas_call | solution.py:219
  18.5 1.7 %collective-permute-done.2 = bf16[1024,256]{1,0:T(8,128)(2,1)S(1)} collective-permute-done((bf16[1024,256]{1,0:T(8,128)(2,1)S(1)}, bf16[1024,256]{1,0:T(8,128)(2,1)S(1)}, u32[]{:S(2)}, u32[]{:S(2)}) %collective-permute-start.2) | collective-permute-done | bytes 524320 | tf_op jit(solution)/shard_map/ppermute | solution.py:190
  20.3 6.1 %reference.1 = (bf16[2,144,512]{2,1,0:T(8,128)(2,1)}, bf16[2,144,512]{2,1,0:T(8,128)(2,1)}) custom-call(s32[2]{0:T(128)} %pad_add_fusion.1.at, bf16[512,2048]{1,0:T(8,128)(2,1)} %x_ref.1, f32[1,2048]{1,0:T(1,128)} %bitcast.32, bf16[2048,512]{1,0:T(8,128)(2,1)} %weight_ref.1), custom_call_target="tpu_custom_call" | custom-call | flops 1073741824 | bytes 5242880 | tf_op jit(solution)/shard_map/reference/pallas_call | solution.py:253
  26.3 2.6 %collective-permute-start.3 = (bf16[2,144,512]{2,1,0:T(8,128)(2,1)}, bf16[2,144,512]{2,1,0:T(8,128)(2,1)S(1)}, u32[]{:S(2)}, u32[]{:S(2)}) collective-permute-start(bf16[2,144,512]{2,1,0:T(8,128)(2,1)} %get-tuple-element.37), channel_id=1, source_target_pairs={{0,1},{1,0},{2,3},{3,2},{4,5},{5,4},{6,7},{7,6},{8,9},{9,8},{10,11... | collective-permute-start | bytes 884744 | tf_op jit(solution)/shard_map/ppermute | solution.py:37
  29.1 2.2 %collective-permute-start.5 = (bf16[1024,256]{1,0:T(8,128)(2,1)S(1)}, bf16[1024,256]{1,0:T(8,128)(2,1)}, u32[]{:S(2)}, u32[]{:S(2)}) collective-permute-start(bf16[1024,256]{1,0:T(8,128)(2,1)S(1)} %broadcast_select_fusion.1), channel_id=1, source_target_pairs={{0,16},{9,25},{18,2},{27,11},{8,24},{1,17},{26,10},{19,3},{4,12},{... | collective-permute-start | bytes 1572872 | tf_op jit(solution)/shard_map/ppermute | solution.py:190
  32.1 2.1 %collective-permute-start.13 = (bf16[1024,256]{1,0:T(8,128)(2,1)S(1)}, bf16[1024,256]{1,0:T(8,128)(2,1)}, u32[]{:S(2)}, u32[]{:S(2)}) collective-permute-start(bf16[1024,256]{1,0:T(8,128)(2,1)S(1)} %broadcast_select_fusion), channel_id=1, source_target_pairs={{0,16},{9,25},{18,2},{27,11},{8,24},{1,17},{26,10},{19,3},{4,12},{... | collective-permute-start | bytes 1572872 | tf_op jit(solution)/shard_map/ppermute | solution.py:190
  35.9 10.2 %collective-permute-done.4 = bf16[1,160,512]{2,1,0:T(8,128)(2,1)S(1)} collective-permute-done((bf16[1,160,512]{2,1,0:T(8,128)(2,1)S(1)}, bf16[1,160,512]{2,1,0:T(8,128)(2,1)S(1)}, u32[]{:S(2)}, u32[]{:S(2)}) %collective-permute-start.4) | collective-permute-done | bytes 163872 | tf_op jit(solution)/shard_map/ppermute | solution.py:37
  50.9 1.5 %collective-permute-start.15 = (bf16[256,256]{1,0:T(8,128)(2,1)S(1)}, bf16[256,256]{1,0:T(8,128)(2,1)S(1)}, u32[]{:S(2)}, u32[]{:S(2)}) collective-permute-start(bf16[256,256]{1,0:T(8,128)(2,1)S(1)} %slice.122), channel_id=1, source_target_pairs={{0,1},{1,0},{2,3},{3,2},{4,5},{5,4},{6,7},{7,6},{8,9},{9,8},{10,11... | collective-permute-start | bytes 393224 | tf_op jit(solution)/shard_map/ppermute | solution.py:37
  52.4 3.8 %collective-permute-done.7 = bf16[256,256]{1,0:T(8,128)(2,1)S(1)} collective-permute-done((bf16[256,256]{1,0:T(8,128)(2,1)S(1)}, bf16[256,256]{1,0:T(8,128)(2,1)S(1)}, u32[]{:S(2)}, u32[]{:S(2)}) %collective-permute-start.7) | collective-permute-done | bytes 131104 | tf_op jit(solution)/shard_map/ppermute | solution.py:37
  56.2 3.5 %collective-permute-start.8 = (bf16[128,256]{1,0:T(8,128)(2,1)S(1)}, bf16[128,256]{1,0:T(8,128)(2,1)S(1)}, u32[]{:S(2)}, u32[]{:S(2)}) collective-permute-start(bf16[128,256]{1,0:T(8,128)(2,1)S(1)} %slice.125), channel_id=1, source_target_pairs={{0,2},{1,3},{2,0},{3,1},{4,6},{5,7},{6,4},{7,5},{8,10},{9,11},{10,... | collective-permute-start | bytes 196616 | tf_op jit(solution)/shard_map/ppermute | solution.py:37
  59.8 2.9 %collective-permute-start.16 = (bf16[128,256]{1,0:T(8,128)(2,1)S(1)}, bf16[128,256]{1,0:T(8,128)(2,1)S(1)}, u32[]{:S(2)}, u32[]{:S(2)}) collective-permute-start(bf16[128,256]{1,0:T(8,128)(2,1)S(1)} %slice.124), channel_id=1, source_target_pairs={{0,2},{1,3},{2,0},{3,1},{4,6},{5,7},{6,4},{7,5},{8,10},{9,11},{10,... | collective-permute-start | bytes 196616 | tf_op jit(solution)/shard_map/ppermute | solution.py:37
  62.8 2.2 %collective-permute-done.16 = bf16[128,256]{1,0:T(8,128)(2,1)S(1)} collective-permute-done((bf16[128,256]{1,0:T(8,128)(2,1)S(1)}, bf16[128,256]{1,0:T(8,128)(2,1)S(1)}, u32[]{:S(2)}, u32[]{:S(2)}) %collective-permute-start.16) | collective-permute-done | bytes 65568 | tf_op jit(solution)/shard_map/ppermute | solution.py:37
  65.1 3.0 %collective-permute-start.9 = (bf16[128,256]{1,0:T(8,128)(2,1)S(1)}, bf16[128,256]{1,0:T(8,128)(2,1)S(1)}, u32[]{:S(2)}, u32[]{:S(2)}) collective-permute-start(bf16[128,256]{1,0:T(8,128)(2,1)S(1)} %get-tuple-element.59), channel_id=1, source_target_pairs={{0,2},{1,3},{2,0},{3,1},{4,6},{5,7},{6,4},{7,5},{8,10},{9,11},{10,... | collective-permute-start | bytes 196616 | tf_op jit(solution)/shard_map/ppermute | solution.py:37
  68.2 2.5 %collective-permute-done.9 = bf16[128,256]{1,0:T(8,128)(2,1)S(1)} collective-permute-done((bf16[128,256]{1,0:T(8,128)(2,1)S(1)}, bf16[128,256]{1,0:T(8,128)(2,1)S(1)}, u32[]{:S(2)}, u32[]{:S(2)}) %collective-permute-start.9) | collective-permute-done | bytes 65568 | tf_op jit(solution)/shard_map/ppermute | solution.py:37
  70.7 2.5 %collective-permute-start.10 = (bf16[256,256]{1,0:T(8,128)(2,1)S(1)}, bf16[256,256]{1,0:T(8,128)(2,1)S(1)}, u32[]{:S(2)}, u32[]{:S(2)}) collective-permute-start(bf16[256,256]{1,0:T(8,128)(2,1)S(1)} %pad_maximum_fusion.3), channel_id=1, source_target_pairs={{0,1},{1,0},{2,3},{3,2},{4,5},{5,4},{6,7},{7,6},{8,9},{9,8},{10,11... | collective-permute-start | bytes 393224 | tf_op jit(solution)/shard_map/ppermute | solution.py:37
  73.3 2.4 %collective-permute-start.18 = (bf16[256,256]{1,0:T(8,128)(2,1)S(1)}, bf16[256,256]{1,0:T(8,128)(2,1)S(1)}, u32[]{:S(2)}, u32[]{:S(2)}) collective-permute-start(bf16[256,256]{1,0:T(8,128)(2,1)S(1)} %pad_maximum_fusion.4), channel_id=1, source_target_pairs={{0,1},{1,0},{2,3},{3,2},{4,5},{5,4},{6,7},{7,6},{8,9},{9,8},{10,11... | collective-permute-start | bytes 393224 | tf_op jit(solution)/shard_map/ppermute | solution.py:37
  75.7 1.2 %collective-permute-done.10 = bf16[256,256]{1,0:T(8,128)(2,1)S(1)} collective-permute-done((bf16[256,256]{1,0:T(8,128)(2,1)S(1)}, bf16[256,256]{1,0:T(8,128)(2,1)S(1)}, u32[]{:S(2)}, u32[]{:S(2)}) %collective-permute-start.10) | collective-permute-done | bytes 131104 | tf_op jit(solution)/shard_map/ppermute | solution.py:37
  77.0 1.6 %collective-permute-done.18 = bf16[256,256]{1,0:T(8,128)(2,1)S(1)} collective-permute-done((bf16[256,256]{1,0:T(8,128)(2,1)S(1)}, bf16[256,256]{1,0:T(8,128)(2,1)S(1)}, u32[]{:S(2)}, u32[]{:S(2)}) %collective-permute-start.18) | collective-permute-done | bytes 131104 | tf_op jit(solution)/shard_map/ppermute | solution.py:37
  78.9 1.4 %gradient.2 = (f32[256,256]{1,0:T(8,128)S(1)}, bf16[256,256]{1,0:T(8,128)(2,1)S(1)}, bf16[256,256]{1,0:T(8,128)(2,1)S(1)}, bf16[256,256]{1,0:T(8,128)(2,1)S(1)}) custom-call(s32[4]{0:T(128)S(1)} %pad_add_fusion.at, bf16[512,1024]{1,0:T(8,128)(2,1)S(1)} %copy-done, bf16[512,1024]{1,0:T(8,128)(2,1)S(1)} %collective-permute-done.1.got_ref, ...), custom_call_target="tpu_custom_call" | custom-call | flops 536870912 | bytes 4194304 | tf_op jit(solution)/shard_map/gradient/pallas_call | solution.py:343
  80.3 3.6 %collective-permute-start.12 = (bf16[256,256]{1,0:T(8,128)(2,1)S(1)}, bf16[256,256]{1,0:T(8,128)(2,1)S(1)}, u32[]{:S(2)}, u32[]{:S(2)}) collective-permute-start(bf16[256,256]{1,0:T(8,128)(2,1)S(1)} %get-tuple-element.41), channel_id=1, source_target_pairs={{0,24},{4,28},{8,16},{12,20},{16,8},{20,12},{24,0},{28,4},{1,25},{... | collective-permute-start | bytes 393224 | tf_op jit(solution)/shard_map/ppermute | solution.py:375
  83.8 1.4 %gradient.3 = (f32[256,256]{1,0:T(8,128)S(1)}, bf16[256,256]{1,0:T(8,128)(2,1)S(1)}, bf16[256,256]{1,0:T(8,128)(2,1)S(1)}, bf16[256,256]{1,0:T(8,128)(2,1)S(1)}) custom-call(s32[4]{0:T(128)S(1)} %pad_add_fusion.at, bf16[512,1024]{1,0:T(8,128)(2,1)S(1)} %copy-done, bf16[512,1024]{1,0:T(8,128)(2,1)S(1)} %collective-permute-done.1.got_ref, ...), custom_call_target="tpu_custom_call" | custom-call | flops 536870912 | bytes 4194304 | tf_op jit(solution)/shard_map/gradient/pallas_call | solution.py:343
  85.3 1.1 collective-permute-start.24
  86.4 2.4 %collective-permute-start.23 = (bf16[256,256]{1,0:T(8,128)(2,1)S(1)}, bf16[256,256]{1,0:T(8,128)(2,1)S(1)}, u32[]{:S(2)}, u32[]{:S(2)}) collective-permute-start(bf16[256,256]{1,0:T(8,128)(2,1)S(1)} %get-tuple-element.53), channel_id=1, source_target_pairs={{0,8},{4,12},{8,0},{12,4},{16,24},{20,28},{24,16},{28,20},{1,9},{5... | collective-permute-start | bytes 393224 | tf_op jit(solution)/shard_map/ppermute | solution.py:375
  90.4 2.2 %collective-permute-done.25 = bf16[256,256]{1,0:T(8,128)(2,1)S(1)} collective-permute-done((bf16[256,256]{1,0:T(8,128)(2,1)S(1)}, bf16[256,256]{1,0:T(8,128)(2,1)S(1)}, u32[]{:S(2)}, u32[]{:S(2)}) %collective-permute-start.25) | collective-permute-done | bytes 131104 | tf_op jit(solution)/shard_map/ppermute | solution.py:375
  92.6 1.9 %collective-permute-done.24 = bf16[256,256]{1,0:T(8,128)(2,1)S(1)} collective-permute-done((bf16[256,256]{1,0:T(8,128)(2,1)S(1)}, bf16[256,256]{1,0:T(8,128)(2,1)S(1)}, u32[]{:S(2)}, u32[]{:S(2)}) %collective-permute-start.24) | collective-permute-done | bytes 131104 | tf_op jit(solution)/shard_map/ppermute | solution.py:375
  95.3 1.3 %collective-permute-done.21 = bf16[256,256]{1,0:T(8,128)(2,1)S(1)} collective-permute-done((bf16[256,256]{1,0:T(8,128)(2,1)S(1)}, bf16[256,256]{1,0:T(8,128)(2,1)S(1)}, u32[]{:S(2)}, u32[]{:S(2)}) %collective-permute-start.21) | collective-permute-done | bytes 131104 | tf_op jit(solution)/shard_map/ppermute | solution.py:375
  97.3 7.9 %all-to-all-start.1 = ((bf16[8,32,512]{2,1,0:T(8,128)(2,1)}), bf16[8,32,512]{2,1,0:T(8,128)(2,1)S(1)}, u32[]{:S(2)}, u32[]{:S(2)}) async-start(bf16[8,32,512]{2,1,0:T(8,128)(2,1)} %bitcast.16), calls=%async_computation.1 | async-start | bytes 524288 | tf_op jit(solution)/shard_map/all_to_all | solution.py:377
  106.1 6.1 %all-to-all-done.1 = bf16[8,32,512]{2,1,0:T(8,128)(2,1)S(1)} async-done(((bf16[8,32,512]{2,1,0:T(8,128)(2,1)}), bf16[8,32,512]{2,1,0:T(8,128)(2,1)S(1)}, u32[]{:S(2)}, u32[]{:S(2)}) %all-to-all-start.1) | async-done | bytes 262176 | tf_op jit(solution)/shard_map/all_to_all | solution.py:377
  (83 shorter events, 14.9 us)
Async XLA Ops:
  1.7 11.5 %collective-permute-start = (bf16[1024,256]{1,0:T(8,128)(2,1)S(1)}, bf16[1024,256]{1,0:T(8,128)(2,1)S(1)}, u32[]{:S(2)}, u32[]{:S(2)}) collective-permute-start(bf16[1024,256]{1,0:T(8,128)(2,1)S(1)} %slice.66), channel_id=1, source_target_pairs={{0,8},{9,1},{18,26},{27,19},{4,20},{13,29},{22,6},{31,15}} | collective-permute-start | bytes 1572872 | tf_op jit(solution)/shard_map/ppermute | solution.py:190
  7.7 12.6 %collective-permute-start.2 = (bf16[1024,256]{1,0:T(8,128)(2,1)S(1)}, bf16[1024,256]{1,0:T(8,128)(2,1)S(1)}, u32[]{:S(2)}, u32[]{:S(2)}) collective-permute-start(bf16[1024,256]{1,0:T(8,128)(2,1)S(1)} %slice.67), channel_id=1, source_target_pairs={{0,8},{9,1},{18,26},{27,19},{4,20},{13,29},{22,6},{31,15}} | collective-permute-start | bytes 1572872 | tf_op jit(solution)/shard_map/ppermute | solution.py:190
  9.0 26.9 %all-to-all-start = ((bf16[8,32,512]{2,1,0:T(8,128)(2,1)}), bf16[8,32,512]{2,1,0:T(8,128)(2,1)S(1)}, u32[]{:S(2)}, u32[]{:S(2)}) async-start(bf16[8,32,512]{2,1,0:T(8,128)(2,1)} %bitcast.11), calls=%async_computation | async-start | bytes 524288 | tf_op jit(solution)/shard_map/all_to_all | solution.py:193
  18.3 28.9 %collective-permute-start.1 = (bf16[512,1024]{1,0:T(8,128)(2,1)}, bf16[512,1024]{1,0:T(8,128)(2,1)S(1)}, u32[]{:S(2)}, u32[]{:S(2)}) collective-permute-start(bf16[512,1024]{1,0:T(8,128)(2,1)} %get-tuple-element.33), channel_id=1, source_target_pairs={{0,4},{4,0},{8,12},{12,8},{16,20},{20,16},{24,28},{28,24},{1,5},{5... | collective-permute-start | bytes 3145736 | tf_op jit(solution)/shard_map/ppermute | solution.py:29
  26.3 8.9 %collective-permute-start.3 = (bf16[2,144,512]{2,1,0:T(8,128)(2,1)}, bf16[2,144,512]{2,1,0:T(8,128)(2,1)S(1)}, u32[]{:S(2)}, u32[]{:S(2)}) collective-permute-start(bf16[2,144,512]{2,1,0:T(8,128)(2,1)} %get-tuple-element.37), channel_id=1, source_target_pairs={{0,1},{1,0},{2,3},{3,2},{4,5},{5,4},{6,7},{7,6},{8,9},{9,8},{10,11... | collective-permute-start | bytes 884744 | tf_op jit(solution)/shard_map/ppermute | solution.py:37
  29.0 17.1 %copy-start.1 = (s32[1,1,8]{2,1,0:T(1,128)S(1)}, s32[1,1,8]{2,1,0:T(1,128)}, u32[]{:S(2)}) copy-start(s32[1,1,8]{2,1,0:T(1,128)} %param.15) | copy-start | bytes 100
  29.0 17.1 %copy-start.2 = (s32[1,1,8]{2,1,0:T(1,128)S(1)}, s32[1,1,8]{2,1,0:T(1,128)}, u32[]{:S(2)}) copy-start(s32[1,1,8]{2,1,0:T(1,128)} %param.16) | copy-start | bytes 100
  29.0 17.1 %copy-start.3 = (f32[1,1,8]{2,1,0:T(1,128)S(1)}, f32[1,1,8]{2,1,0:T(1,128)}, u32[]{:S(2)}) copy-start(f32[1,1,8]{2,1,0:T(1,128)} %param.17) | copy-start | bytes 100
  29.1 18.2 %collective-permute-start.5 = (bf16[1024,256]{1,0:T(8,128)(2,1)S(1)}, bf16[1024,256]{1,0:T(8,128)(2,1)}, u32[]{:S(2)}, u32[]{:S(2)}) collective-permute-start(bf16[1024,256]{1,0:T(8,128)(2,1)S(1)} %broadcast_select_fusion.1), channel_id=1, source_target_pairs={{0,16},{9,25},{18,2},{27,11},{8,24},{1,17},{26,10},{19,3},{4,12},{... | collective-permute-start | bytes 1572872 | tf_op jit(solution)/shard_map/ppermute | solution.py:190
  32.1 15.8 %collective-permute-start.13 = (bf16[1024,256]{1,0:T(8,128)(2,1)S(1)}, bf16[1024,256]{1,0:T(8,128)(2,1)}, u32[]{:S(2)}, u32[]{:S(2)}) collective-permute-start(bf16[1024,256]{1,0:T(8,128)(2,1)S(1)} %broadcast_select_fusion), channel_id=1, source_target_pairs={{0,16},{9,25},{18,2},{27,11},{8,24},{1,17},{26,10},{19,3},{4,12},{... | collective-permute-start | bytes 1572872 | tf_op jit(solution)/shard_map/ppermute | solution.py:190
  35.4 10.8 %collective-permute-start.4 = (bf16[1,160,512]{2,1,0:T(8,128)(2,1)S(1)}, bf16[1,160,512]{2,1,0:T(8,128)(2,1)S(1)}, u32[]{:S(2)}, u32[]{:S(2)}) collective-permute-start(bf16[1,160,512]{2,1,0:T(8,128)(2,1)S(1)} %get-tuple-element.60), channel_id=1, source_target_pairs={{0,2},{1,3},{2,0},{3,1},{4,6},{5,7},{6,4},{7,5},{8,10},{9,11},{10,... | collective-permute-start | bytes 491528 | tf_op jit(solution)/shard_map/ppermute | solution.py:37
  47.7 1.6 %collective-permute-start.6 = (bf16[512,256]{1,0:T(8,128)(2,1)S(1)}, bf16[512,256]{1,0:T(8,128)(2,1)S(1)}, u32[]{:S(2)}, u32[]{:S(2)}) collective-permute-start(bf16[512,256]{1,0:T(8,128)(2,1)S(1)} %convolution_convert_fusion.2), channel_id=1, source_target_pairs={{0,4},{4,0},{8,12},{12,8},{16,20},{20,16},{24,28},{28,24},{1,5},{5... | collective-permute-start | bytes 786440 | tf_op jit(solution)/shard_map/ppermute | solution.py:29
  48.3 2.1 %collective-permute-start.14 = (bf16[512,256]{1,0:T(8,128)(2,1)S(1)}, bf16[512,256]{1,0:T(8,128)(2,1)S(1)}, u32[]{:S(2)}, u32[]{:S(2)}) collective-permute-start(bf16[512,256]{1,0:T(8,128)(2,1)S(1)} %convolution_convert_fusion.1), channel_id=1, source_target_pairs={{0,4},{4,0},{8,12},{12,8},{16,20},{20,16},{24,28},{28,24},{1,5},{5... | collective-permute-start | bytes 786440 | tf_op jit(solution)/shard_map/ppermute | solution.py:29
  49.8 6.4 %collective-permute-start.7 = (bf16[256,256]{1,0:T(8,128)(2,1)S(1)}, bf16[256,256]{1,0:T(8,128)(2,1)S(1)}, u32[]{:S(2)}, u32[]{:S(2)}) collective-permute-start(bf16[256,256]{1,0:T(8,128)(2,1)S(1)} %slice.123), channel_id=1, source_target_pairs={{0,1},{1,0},{2,3},{3,2},{4,5},{5,4},{6,7},{7,6},{8,9},{9,8},{10,11... | collective-permute-start | bytes 393224 | tf_op jit(solution)/shard_map/ppermute | solution.py:37
  50.9 8.8 %collective-permute-start.15 = (bf16[256,256]{1,0:T(8,128)(2,1)S(1)}, bf16[256,256]{1,0:T(8,128)(2,1)S(1)}, u32[]{:S(2)}, u32[]{:S(2)}) collective-permute-start(bf16[256,256]{1,0:T(8,128)(2,1)S(1)} %slice.122), channel_id=1, source_target_pairs={{0,1},{1,0},{2,3},{3,2},{4,5},{5,4},{6,7},{7,6},{8,9},{9,8},{10,11... | collective-permute-start | bytes 393224 | tf_op jit(solution)/shard_map/ppermute | solution.py:37
  56.2 6.6 %collective-permute-start.8 = (bf16[128,256]{1,0:T(8,128)(2,1)S(1)}, bf16[128,256]{1,0:T(8,128)(2,1)S(1)}, u32[]{:S(2)}, u32[]{:S(2)}) collective-permute-start(bf16[128,256]{1,0:T(8,128)(2,1)S(1)} %slice.125), channel_id=1, source_target_pairs={{0,2},{1,3},{2,0},{3,1},{4,6},{5,7},{6,4},{7,5},{8,10},{9,11},{10,... | collective-permute-start | bytes 196616 | tf_op jit(solution)/shard_map/ppermute | solution.py:37
  59.8 5.2 %collective-permute-start.16 = (bf16[128,256]{1,0:T(8,128)(2,1)S(1)}, bf16[128,256]{1,0:T(8,128)(2,1)S(1)}, u32[]{:S(2)}, u32[]{:S(2)}) collective-permute-start(bf16[128,256]{1,0:T(8,128)(2,1)S(1)} %slice.124), channel_id=1, source_target_pairs={{0,2},{1,3},{2,0},{3,1},{4,6},{5,7},{6,4},{7,5},{8,10},{9,11},{10,... | collective-permute-start | bytes 196616 | tf_op jit(solution)/shard_map/ppermute | solution.py:37
  65.1 5.6 %collective-permute-start.9 = (bf16[128,256]{1,0:T(8,128)(2,1)S(1)}, bf16[128,256]{1,0:T(8,128)(2,1)S(1)}, u32[]{:S(2)}, u32[]{:S(2)}) collective-permute-start(bf16[128,256]{1,0:T(8,128)(2,1)S(1)} %get-tuple-element.59), channel_id=1, source_target_pairs={{0,2},{1,3},{2,0},{3,1},{4,6},{5,7},{6,4},{7,5},{8,10},{9,11},{10,... | collective-permute-start | bytes 196616 | tf_op jit(solution)/shard_map/ppermute | solution.py:37
  68.1 5.2 %collective-permute-start.17 = (bf16[128,256]{1,0:T(8,128)(2,1)S(1)}, bf16[128,256]{1,0:T(8,128)(2,1)S(1)}, u32[]{:S(2)}, u32[]{:S(2)}) collective-permute-start(bf16[128,256]{1,0:T(8,128)(2,1)S(1)} %get-tuple-element.63), channel_id=1, source_target_pairs={{0,2},{1,3},{2,0},{3,1},{4,6},{5,7},{6,4},{7,5},{8,10},{9,11},{10,... | collective-permute-start | bytes 196616 | tf_op jit(solution)/shard_map/ppermute | solution.py:37
  70.7 6.2 %collective-permute-start.10 = (bf16[256,256]{1,0:T(8,128)(2,1)S(1)}, bf16[256,256]{1,0:T(8,128)(2,1)S(1)}, u32[]{:S(2)}, u32[]{:S(2)}) collective-permute-start(bf16[256,256]{1,0:T(8,128)(2,1)S(1)} %pad_maximum_fusion.3), channel_id=1, source_target_pairs={{0,1},{1,0},{2,3},{3,2},{4,5},{5,4},{6,7},{7,6},{8,9},{9,8},{10,11... | collective-permute-start | bytes 393224 | tf_op jit(solution)/shard_map/ppermute | solution.py:37
  73.3 5.4 %collective-permute-start.18 = (bf16[256,256]{1,0:T(8,128)(2,1)S(1)}, bf16[256,256]{1,0:T(8,128)(2,1)S(1)}, u32[]{:S(2)}, u32[]{:S(2)}) collective-permute-start(bf16[256,256]{1,0:T(8,128)(2,1)S(1)} %pad_maximum_fusion.4), channel_id=1, source_target_pairs={{0,1},{1,0},{2,3},{3,2},{4,5},{5,4},{6,7},{7,6},{8,9},{9,8},{10,11... | collective-permute-start | bytes 393224 | tf_op jit(solution)/shard_map/ppermute | solution.py:37
  77.0 1.9 %collective-permute-start.11 = (bf16[512,256]{1,0:T(8,128)(2,1)S(1)}, bf16[512,256]{1,0:T(8,128)(2,1)S(1)}, u32[]{:S(2)}, u32[]{:S(2)}) collective-permute-start(bf16[512,256]{1,0:T(8,128)(2,1)S(1)} %pad_maximum_fusion.1.slope_ref), channel_id=1, source_target_pairs={{0,4},{4,0},{8,12},{12,8},{16,20},{20,16},{24,28},{28,24},{1,5},{5... | collective-permute-start | bytes 786440 | tf_op jit(solution)/shard_map/ppermute | solution.py:29
  78.7 5.1 %collective-permute-start.19 = (bf16[512,256]{1,0:T(8,128)(2,1)S(1)}, bf16[512,256]{1,0:T(8,128)(2,1)S(1)}, u32[]{:S(2)}, u32[]{:S(2)}) collective-permute-start(bf16[512,256]{1,0:T(8,128)(2,1)S(1)} %pad_maximum_fusion.2.slope_ref), channel_id=1, source_target_pairs={{0,4},{4,0},{8,12},{12,8},{16,20},{20,16},{24,28},{28,24},{1,5},{5... | collective-permute-start | bytes 786440 | tf_op jit(solution)/shard_map/ppermute | solution.py:29
  80.3 9.5 %collective-permute-start.12 = (bf16[256,256]{1,0:T(8,128)(2,1)S(1)}, bf16[256,256]{1,0:T(8,128)(2,1)S(1)}, u32[]{:S(2)}, u32[]{:S(2)}) collective-permute-start(bf16[256,256]{1,0:T(8,128)(2,1)S(1)} %get-tuple-element.41), channel_id=1, source_target_pairs={{0,24},{4,28},{8,16},{12,20},{16,8},{20,12},{24,0},{28,4},{1,25},{... | collective-permute-start | bytes 393224 | tf_op jit(solution)/shard_map/ppermute | solution.py:375
  85.2 7.3 %collective-permute-start.25 = (bf16[256,256]{1,0:T(8,128)(2,1)S(1)}, bf16[256,256]{1,0:T(8,128)(2,1)S(1)}, u32[]{:S(2)}, u32[]{:S(2)}) collective-permute-start(bf16[256,256]{1,0:T(8,128)(2,1)S(1)} %get-tuple-element.55), channel_id=1, source_target_pairs={{0,24},{4,28},{8,16},{12,20},{16,8},{20,12},{24,0},{28,4},{1,25},{... | collective-permute-start | bytes 393224 | tf_op jit(solution)/shard_map/ppermute | solution.py:375
  85.3 9.2 %collective-permute-start.24 = (bf16[256,256]{1,0:T(8,128)(2,1)S(1)}, bf16[256,256]{1,0:T(8,128)(2,1)S(1)}, u32[]{:S(2)}, u32[]{:S(2)}) collective-permute-start(bf16[256,256]{1,0:T(8,128)(2,1)S(1)} %get-tuple-element.54), channel_id=1, source_target_pairs={{0,16},{4,20},{8,24},{12,28},{16,0},{20,4},{24,8},{28,12},{1,17},{... | collective-permute-start | bytes 393224 | tf_op jit(solution)/shard_map/ppermute | solution.py:375
  86.4 8.1 %collective-permute-start.23 = (bf16[256,256]{1,0:T(8,128)(2,1)S(1)}, bf16[256,256]{1,0:T(8,128)(2,1)S(1)}, u32[]{:S(2)}, u32[]{:S(2)}) collective-permute-start(bf16[256,256]{1,0:T(8,128)(2,1)S(1)} %get-tuple-element.53), channel_id=1, source_target_pairs={{0,8},{4,12},{8,0},{12,4},{16,24},{20,28},{24,16},{28,20},{1,9},{5... | collective-permute-start | bytes 393224 | tf_op jit(solution)/shard_map/ppermute | solution.py:375
  89.7 6.8 %collective-permute-start.21 = (bf16[256,256]{1,0:T(8,128)(2,1)S(1)}, bf16[256,256]{1,0:T(8,128)(2,1)S(1)}, u32[]{:S(2)}, u32[]{:S(2)}) collective-permute-start(bf16[256,256]{1,0:T(8,128)(2,1)S(1)} %get-tuple-element.49), channel_id=1, source_target_pairs={{0,16},{4,20},{8,24},{12,28},{16,0},{20,4},{24,8},{28,12},{1,17},{... | collective-permute-start | bytes 393224 | tf_op jit(solution)/shard_map/ppermute | solution.py:375
  89.7 6.8 %collective-permute-start.20 = (bf16[256,256]{1,0:T(8,128)(2,1)S(1)}, bf16[256,256]{1,0:T(8,128)(2,1)S(1)}, u32[]{:S(2)}, u32[]{:S(2)}) collective-permute-start(bf16[256,256]{1,0:T(8,128)(2,1)S(1)} %get-tuple-element.48), channel_id=1, source_target_pairs={{0,8},{4,12},{8,0},{12,4},{16,24},{20,28},{24,16},{28,20},{1,9},{5... | collective-permute-start | bytes 393224 | tf_op jit(solution)/shard_map/ppermute | solution.py:375
  94.6 10.7 %collective-permute-start.26 = (bf16[256,256]{1,0:T(8,128)(2,1)S(1)}, bf16[256,256]{1,0:T(8,128)(2,1)S(1)}, u32[]{:S(2)}, u32[]{:S(2)}) collective-permute-start(bf16[256,256]{1,0:T(8,128)(2,1)S(1)} %add_convert_fusion.1), channel_id=1, source_target_pairs={{0,0},{1,10},{2,17},{3,27},{4,4},{5,14},{6,21},{7,31},{8,1},{9,11}... | collective-permute-start | bytes 393224 | tf_op jit(solution)/shard_map/ppermute | solution.py:387
  96.6 8.6 %collective-permute-start.22 = (bf16[256,256]{1,0:T(8,128)(2,1)S(1)}, bf16[256,256]{1,0:T(8,128)(2,1)S(1)}, u32[]{:S(2)}, u32[]{:S(2)}) collective-permute-start(bf16[256,256]{1,0:T(8,128)(2,1)S(1)} %add_convert_fusion.2), channel_id=1, source_target_pairs={{0,0},{1,10},{2,17},{3,27},{4,4},{5,14},{6,21},{7,31},{8,1},{9,11}... | collective-permute-start | bytes 393224 | tf_op jit(solution)/shard_map/ppermute | solution.py:387
  97.3 14.9 %all-to-all-start.1 = ((bf16[8,32,512]{2,1,0:T(8,128)(2,1)}), bf16[8,32,512]{2,1,0:T(8,128)(2,1)S(1)}, u32[]{:S(2)}, u32[]{:S(2)}) async-start(bf16[8,32,512]{2,1,0:T(8,128)(2,1)} %bitcast.16), calls=%async_computation.1 | async-start | bytes 524288 | tf_op jit(solution)/shard_map/all_to_all | solution.py:377
  (7 other events, 59.7 us)

commit v8 on v6

--- a/solution.py
+++ b/solution.py
@@ -120,14 +120,17 @@
     scale_ref[...] = scale
 
 
-def grad_kernel(places, factor, at, kept_ref, got_ref, slope_ref, slope_got_ref, *refs):
-    out_refs, grad = refs[:places], refs[places]
+def grad_kernel(factor, at, kept_ref, got_ref, slope_ref, slope_got_ref, *refs):
+    *out_refs, grad = refs
     total = dot_rows(kept_ref[...], slope_ref[...]) + dot_rows(got_ref[...], slope_got_ref[...])
     grad[...] = total * factor
-    rows = out_refs[0].shape[0]
-    for s in range(places):
+    rows = grad.shape[0] // at.shape[0]
+    count = at.shape[0] // 2
+    for s in range(2 * count):
         chunk = grad[pl.ds(pl.multiple_of(at[s] * rows, rows), rows), :]
-        out_refs[s][...] = chunk.astype(out_refs[s].dtype)
+        out_ref = out_refs[s // count]
+        place = s % count
+        out_ref[place * rows : (place + 1) * rows, :] = chunk.astype(out_ref.dtype)
 
 
 def on_device(
@@ -161,7 +164,6 @@
     model_width = pol_gain.shape[0]
     shard = pol_weight.shape[0]
     width = value_width // PARTS
-    out_rows = shard // tensor_count
     factor = 1.0 / math.sqrt(dp_count * tensor_count * lengths.shape[2])
     relative = place ^ t
 
@@ -251,7 +253,14 @@
         parts.append((held_part, got_part, is_getter_part))
     got_cot = lax.all_to_all(cot, "dp", split_axis=0, concat_axis=0, tiled=True)
 
-    chunk_at = jnp.stack([place ^ s ^ turned(t, levels) for s in range(places)]).astype(jnp.int32)
+    def plane_bit(level):
+        return jnp.where(core == 0, 1 << (level % levels), 1 << ((1 + level) % levels))
+
+    chunk_at = []
+    for i in range(places):
+        away = sum(plane_bit(level) * ((i >> (levels - 1 - level)) & 1) for level in range(levels))
+        chunk_at.append(place ^ away ^ turned(t, levels))
+    chunk_at = jnp.stack(chunk_at).astype(jnp.int32)
 
     values, slopes = [], []
     for j in range(PARTS):
@@ -299,19 +308,19 @@
         cols = slice(j * width, (j + 1) * width)
         slope = (fixed[:, cols] + pull[:, :1] * total).astype(BF16)
         for level in reversed(range(levels)):
-            got = crossed(slope, tensor_count, 1 << level)
-            slope = jnp.concatenate([slope, got], axis=0)
+            slope = jnp.concatenate([slope, crossed(slope, tensor_count, 1 << level)], axis=0)
         slopes.append(slope)
 
     sent = dot_rows(row_at, jnp.concatenate(values, axis=1).astype(BF16)).astype(BF16)
 
-    grad_own, grad_got = [], []
+    slopes[0], sent = lax.optimization_barrier((slopes[0], sent))
+    policy_values = lax.all_to_all(sent, "dp", split_axis=0, concat_axis=0, tiled=True)
+
+    grad_kept, grad_sent = [], []
     for j in range(PARTS):
         slopes_got = swapped(slopes[j], dp_count)
-        if j > 0:
-            slopes_got, grad_own[j - 1] = lax.optimization_barrier((slopes_got, grad_own[j - 1]))
         chunks = pl.pallas_call(
-            functools.partial(grad_kernel, places, factor),
+            functools.partial(grad_kernel, factor),
             grid_spec=pltpu.PrefetchScalarGridSpec(
                 num_scalar_prefetch=1,
                 grid=(1,),
@@ -321,12 +330,12 @@
                     pl.BlockSpec((group_rows, width), lambda i, at: (0, 0)),
                     pl.BlockSpec((group_rows, width), lambda i, at: (0, 0)),
                 ],
-                out_specs=[pl.BlockSpec((out_rows, width), lambda i, at: (0, 0))] * places,
+                out_specs=[pl.BlockSpec((shard // 2, width), lambda i, at: (0, 0))] * 2,
                 scratch_shapes=[pltpu.VMEM((shard, width), F32)],
             ),
             out_shape=[
-                jax.ShapeDtypeStruct((out_rows, width), F32 if s == 0 else BF16)
-                for s in range(places)
+                jax.ShapeDtypeStruct((shard // 2, width), F32),
+                jax.ShapeDtypeStruct((shard // 2, width), BF16),
             ],
             compiler_params=pltpu.CompilerParams(vmem_limit_bytes=32 * 2**20),
             cost_estimate=pl.CostEstimate(
@@ -336,27 +345,29 @@
             ),
             name="gradient",
         )(chunk_at, kept_rows, got_rows, slopes[j], slopes_got)
-        grad_own.append(chunks[0])
-        grad_got.append([])
-        if j == PARTS - 1:
-            grad_own[j], sent = lax.optimization_barrier((grad_own[j], sent))
-            policy_values = lax.all_to_all(sent, "dp", split_axis=0, concat_axis=0, tiled=True)
-        for s in range(1, places):
-            pairs = [
-                (p * cores + c, (p ^ s) * cores + c) for p in range(places) for c in range(cores)
-            ]
-            grad_got[j].append(lax.ppermute(chunks[s], "dp", pairs))
+        grad_kept.append(chunks[0])
+        grad_sent.append(chunks[1])
     grads = []
     for j in range(PARTS):
-        total = (grad_own[j] + sum(x.astype(F32) for x in grad_got[j])).astype(BF16)
-        pairs = [
-            (flat(p, c, z), flat(z, c, p ^ turned(z, levels)))
-            for p in range(places)
-            for c in range(cores)
-            for z in range(tensor_count)
-        ]
-        grads.append(lax.ppermute(total, AXES, pairs))
-    grad_weight = jnp.concatenate(grads, axis=1).astype(F32)
+        total, given = grad_kept[j], grad_sent[j]
+        for level in range(levels):
+            pairs = [
+                (p * cores + c, (p ^ (1 << ((c + level) % levels))) * cores + c)
+                for p in range(places)
+                for c in range(cores)
+            ]
+            total = total + lax.ppermute(given, "dp", pairs).astype(F32)
+            half_rows = total.shape[0] // 2
+            if level < levels - 1:
+                total, given = total[:half_rows], total[half_rows:].astype(BF16)
+        grads.append(total.astype(BF16))
+    pairs = [
+        (flat(p, c, z), flat(z, c, p ^ turned(z, levels)))
+        for p in range(places)
+        for c in range(cores)
+        for z in range(tensor_count)
+    ]
+    grad_weight = lax.ppermute(jnp.concatenate(grads, axis=1), AXES, pairs).astype(F32)
     return (policy_values.reshape(1, 1, slot_count, value_width), grad_weight)
 
 

time: 113 us -> 113 us (level)
  the two profiles are of different devices: /device:TPU:4 before, /device:TPU:0 now
where the time goes in v8:
time: 113 us
  waiting for transfers between devices  44 us (39%)
  starting transfers between devices  35.7 us (32%)
  blocking collectives  13 us (12%)
  Pallas kernels  10.8 us (10%)
  other arithmetic  3.57 us (3%)
  local copies, waits for them, and re-layouts  2.63 us (2%)
  matrix products  2.04 us (2%)
  between operations  1.15 us (1%)
    ppermute x11, waiting for transfers between devices, crossed(): return lax.ppermute(array, 'tensor', [(i, i ^ step) for i in range(count)])  28.3 us
    ppermute x11, starting transfers between devices, crossed(): return lax.ppermute(array, 'tensor', [(i, i ^ step) for i in range(count)])  20.2 us
    all_to_all x1, blocking collectives, on_device(): lax.all_to_all(sent, 'dp', split_axis=0, concat_axis=0, tiled=True)  13 us
    ppermute x4, waiting for transfers between devices, on_device(): total = total + lax.ppermute(given, 'dp', pairs).astype(F32)  10.8 us
    ppermute x3, starting transfers between devices, stage(): return (lax.ppermute(held, AXES, pairs), is_getter)  8.32 us
    pallas_call x1, Pallas kernels, on_device(): pl.pallas_call(functools.partial(prepare_kernel, tensor_count, steps), gr...  6.95 us
    ppermute x3, waiting for transfers between devices, stage(): return (lax.ppermute(held, AXES, pairs), is_getter)  4.85 us
    all_to_all x1, starting transfers between devices, on_device(): got_cot = lax.all_to_all(cot, 'dp', split_axis=0, concat_axis=0, tiled=True)  3.41 us
  transfers between devices with their start and end apart: 25, of which 12 were waited for; matrix products, arithmetic and copies ran while one was open for 4% of the time, Pallas kernels for 10%

profile of v8, /device:TPU:0, one launch (start us, length us, event | category | flops | bytes accessed | tf_op | source)
XLA Modules:
  0.0 112.9 jit_solution(2152240796730082972)
XLA Ops:
  0.6 4.9 %collective-permute-start = (bf16[1024,512]{1,0:T(8,128)(2,1)}, bf16[1024,512]{1,0:T(8,128)(2,1)S(1)}, u32[]{:S(2)}, u32[]{:S(2)}) collective-permute-start(bf16[1024,512]{1,0:T(8,128)(2,1)} %param.14), channel_id=1, source_target_pairs={{0,8},{9,1},{18,26},{27,19},{4,20},{13,29},{22,6},{31,15}} | collective-permute-start | bytes 3145736 | tf_op jit(solution)/shard_map/ppermute | solution.py:186
  6.2 7.0 %prepare.1 = (bf16[512,1024]{1,0:T(8,128)(2,1)}, bf16[512,1024]{1,0:T(8,128)(2,1)}, bf16[144,512]{1,0:T(8,128)(2,1)}, bf16[144,512]{1,0:T(8,128)(2,1)}, bf16[144...) custom-call(s32[2]{0:T(128)} %pad_add_fusion.at, bf16[512,2048]{1,0:T(8,128)(2,1)} %x_ref.1, f32[1,2048]{1,0:T(1,128)} %bitcast.30, ...), custom_call_target="tpu_custom_call" | custom-call | flops 1073741824 | bytes 8388608 | tf_op jit(solution)/shard_map/prepare/pallas_call | solution.py:198
  13.2 4.8 %collective-permute-done = bf16[1024,512]{1,0:T(8,128)(2,1)S(1)} collective-permute-done((bf16[1024,512]{1,0:T(8,128)(2,1)}, bf16[1024,512]{1,0:T(8,128)(2,1)S(1)}, u32[]{:S(2)}, u32[]{:S(2)}) %collective-permute-start) | collective-permute-done | bytes 1048608 | tf_op jit(solution)/shard_map/ppermute | solution.py:186
  18.1 1.0 copy-done.8
  19.1 1.6 %slice_select_fusion = (bf16[1024,256]{1,0:T(8,128)(2,1)S(1)}, bf16[1024,256]{1,0:T(8,128)(2,1)S(1)}) fusion(bf16[1024,512]{1,0:T(8,128)(2,1)} %param.14, bf16[1024,512]{1,0:T(8,128)(2,1)} %copy-done.8, pred[]{:T(512)S(6)} %or.15), kind=kLoop, calls=%fused_computation.7 | loop fusion | flops 524288 | bytes 3145729 | tf_op jit(solution)/shard_map/jit(_where)/select_n | solution.py:248
  20.7 1.3 %collective-permute-start.1 = (bf16[1024,256]{1,0:T(8,128)(2,1)S(1)}, bf16[1024,256]{1,0:T(8,128)(2,1)S(1)}, u32[]{:S(2)}, u32[]{:S(2)}) collective-permute-start(bf16[1024,256]{1,0:T(8,128)(2,1)S(1)} %get-tuple-element.53), channel_id=1, source_target_pairs={{0,16},{9,25},{18,2},{27,11},{8,24},{1,17},{26,10},{19,3},{4,12},{... | collective-permute-start | bytes 1572872 | tf_op jit(solution)/shard_map/ppermute | solution.py:186
  22.0 2.5 %collective-permute-start.2 = (bf16[144,512]{1,0:T(8,128)(2,1)S(1)}, bf16[144,512]{1,0:T(8,128)(2,1)S(1)}, u32[]{:S(2)}, u32[]{:S(2)}) collective-permute-start(bf16[144,512]{1,0:T(8,128)(2,1)S(1)} %copy-done.12), channel_id=1, source_target_pairs={{0,1},{1,0},{2,3},{3,2},{4,5},{5,4},{6,7},{7,6},{8,9},{9,8},{10,11... | collective-permute-start | bytes 442376 | tf_op jit(solution)/shard_map/ppermute | solution.py:37
  24.6 2.1 %collective-permute-start.11 = (bf16[1024,256]{1,0:T(8,128)(2,1)S(1)}, bf16[1024,256]{1,0:T(8,128)(2,1)}, u32[]{:S(2)}, u32[]{:S(2)}) collective-permute-start(bf16[1024,256]{1,0:T(8,128)(2,1)S(1)} %get-tuple-element.52), channel_id=1, source_target_pairs={{0,16},{9,25},{18,2},{27,11},{8,24},{1,17},{26,10},{19,3},{4,12},{... | collective-permute-start | bytes 1572872 | tf_op jit(solution)/shard_map/ppermute | solution.py:186
  26.7 3.4 %all-to-all-start = ((bf16[8,32,512]{2,1,0:T(8,128)(2,1)}), bf16[8,32,512]{2,1,0:T(8,128)(2,1)S(1)}, u32[]{:S(2)}, u32[]{:S(2)}) async-start(bf16[8,32,512]{2,1,0:T(8,128)(2,1)} %bitcast.9), calls=%async_computation | async-start | bytes 524288 | tf_op jit(solution)/shard_map/all_to_all | solution.py:254
  30.1 2.0 %collective-permute-start.3 = (bf16[144,512]{1,0:T(8,128)(2,1)}, bf16[144,512]{1,0:T(8,128)(2,1)S(1)}, u32[]{:S(2)}, u32[]{:S(2)}) collective-permute-start(bf16[144,512]{1,0:T(8,128)(2,1)} %get-tuple-element.32), channel_id=1, source_target_pairs={{0,2},{1,3},{2,0},{3,1},{4,6},{5,7},{6,4},{7,5},{8,10},{9,11},{10,... | collective-permute-start | bytes 442376 | tf_op jit(solution)/shard_map/ppermute | solution.py:37
  32.1 0.9 collective-permute-start.4
  33.0 11.0 %collective-permute-done.3.refs_2_ = bf16[144,512]{1,0:T(8,128)(2,1)S(1)} collective-permute-done((bf16[144,512]{1,0:T(8,128)(2,1)}, bf16[144,512]{1,0:T(8,128)(2,1)S(1)}, u32[]{:S(2)}, u32[]{:S(2)}) %collective-permute-start.3) | collective-permute-done | bytes 147488 | tf_op jit(solution)/shard_map/ppermute | solution.py:37
  46.4 1.1 rows.1
  48.0 4.5 %collective-permute-start.7 = (bf16[256,256]{1,0:T(8,128)(2,1)S(1)}, bf16[256,256]{1,0:T(8,128)(2,1)S(1)}, u32[]{:S(2)}, u32[]{:S(2)}) collective-permute-start(bf16[256,256]{1,0:T(8,128)(2,1)S(1)} %slice.135), channel_id=1, source_target_pairs={{0,1},{1,0},{2,3},{3,2},{4,5},{5,4},{6,7},{7,6},{8,9},{9,8},{10,11... | collective-permute-start | bytes 393224 | tf_op jit(solution)/shard_map/ppermute | solution.py:37
  53.1 3.7 %collective-permute-done.7 = bf16[256,256]{1,0:T(8,128)(2,1)S(1)} collective-permute-done((bf16[256,256]{1,0:T(8,128)(2,1)S(1)}, bf16[256,256]{1,0:T(8,128)(2,1)S(1)}, u32[]{:S(2)}, u32[]{:S(2)}) %collective-permute-start.7) | collective-permute-done | bytes 131104 | tf_op jit(solution)/shard_map/ppermute | solution.py:37
  56.8 3.2 %collective-permute-start.8 = (bf16[128,256]{1,0:T(8,128)(2,1)S(1)}, bf16[128,256]{1,0:T(8,128)(2,1)S(1)}, u32[]{:S(2)}, u32[]{:S(2)}) collective-permute-start(bf16[128,256]{1,0:T(8,128)(2,1)S(1)} %slice.137), channel_id=1, source_target_pairs={{0,2},{1,3},{2,0},{3,1},{4,6},{5,7},{6,4},{7,5},{8,10},{9,11},{10,... | collective-permute-start | bytes 196616 | tf_op jit(solution)/shard_map/ppermute | solution.py:37
  60.0 2.8 %collective-permute-start.14 = (bf16[128,256]{1,0:T(8,128)(2,1)S(1)}, bf16[128,256]{1,0:T(8,128)(2,1)S(1)}, u32[]{:S(2)}, u32[]{:S(2)}) collective-permute-start(bf16[128,256]{1,0:T(8,128)(2,1)S(1)} %slice.136), channel_id=1, source_target_pairs={{0,2},{1,3},{2,0},{3,1},{4,6},{5,7},{6,4},{7,5},{8,10},{9,11},{10,... | collective-permute-start | bytes 196616 | tf_op jit(solution)/shard_map/ppermute | solution.py:37
  62.9 3.4 %collective-permute-done.14 = bf16[128,256]{1,0:T(8,128)(2,1)S(1)} collective-permute-done((bf16[128,256]{1,0:T(8,128)(2,1)S(1)}, bf16[128,256]{1,0:T(8,128)(2,1)S(1)}, u32[]{:S(2)}, u32[]{:S(2)}) %collective-permute-start.14) | collective-permute-done | bytes 65568 | tf_op jit(solution)/shard_map/ppermute | solution.py:37
  66.5 1.7 %collective-permute-start.18 = (bf16[128,256]{1,0:T(8,128)(2,1)S(1)}, bf16[128,256]{1,0:T(8,128)(2,1)S(1)}, u32[]{:S(2)}, u32[]{:S(2)}) collective-permute-start(bf16[128,256]{1,0:T(8,128)(2,1)S(1)} %get-tuple-element.59), channel_id=1, source_target_pairs={{0,2},{1,3},{2,0},{3,1},{4,6},{5,7},{6,4},{7,5},{8,10},{9,11},{10,... | collective-permute-start | bytes 196616 | tf_op jit(solution)/shard_map/ppermute | solution.py:37
  68.1 1.3 %collective-permute-start.9 = (bf16[128,256]{1,0:T(8,128)(2,1)S(1)}, bf16[128,256]{1,0:T(8,128)(2,1)S(1)}, u32[]{:S(2)}, u32[]{:S(2)}) collective-permute-start(bf16[128,256]{1,0:T(8,128)(2,1)S(1)} %get-tuple-element.57), channel_id=1, source_target_pairs={{0,2},{1,3},{2,0},{3,1},{4,6},{5,7},{6,4},{7,5},{8,10},{9,11},{10,... | collective-permute-start | bytes 196616 | tf_op jit(solution)/shard_map/ppermute | solution.py:37
  69.5 4.3 %collective-permute-done.18 = bf16[128,256]{1,0:T(8,128)(2,1)S(1)} collective-permute-done((bf16[128,256]{1,0:T(8,128)(2,1)S(1)}, bf16[128,256]{1,0:T(8,128)(2,1)S(1)}, u32[]{:S(2)}, u32[]{:S(2)}) %collective-permute-start.18) | collective-permute-done | bytes 65568 | tf_op jit(solution)/shard_map/ppermute | solution.py:37
  74.8 1.2 %collective-permute-start.10 = (bf16[256,256]{1,0:T(8,128)(2,1)S(1)}, bf16[256,256]{1,0:T(8,128)(2,1)S(1)}, u32[]{:S(2)}, u32[]{:S(2)}) collective-permute-start(bf16[256,256]{1,0:T(8,128)(2,1)S(1)} %pad_maximum_fusion.3), channel_id=1, source_target_pairs={{0,1},{1,0},{2,3},{3,2},{4,5},{5,4},{6,7},{7,6},{8,9},{9,8},{10,11... | collective-permute-start | bytes 393224 | tf_op jit(solution)/shard_map/ppermute | solution.py:37
  76.0 3.9 %collective-permute-done.19 = bf16[256,256]{1,0:T(8,128)(2,1)S(1)} collective-permute-done((bf16[256,256]{1,0:T(8,128)(2,1)S(1)}, bf16[256,256]{1,0:T(8,128)(2,1)S(1)}, u32[]{:S(2)}, u32[]{:S(2)}) %collective-permute-start.19) | collective-permute-done | bytes 131104 | tf_op jit(solution)/shard_map/ppermute | solution.py:37
  80.2 1.1 collective-permute-done.10
  81.5 1.4 %gradient.3 = (f32[512,256]{1,0:T(8,128)S(1)}, bf16[512,256]{1,0:T(8,128)(2,1)S(1)}) custom-call(s32[4]{0:T(128)S(1)} %pad_add_fusion.1.at, bf16[512,1024]{1,0:T(8,128)(2,1)S(1)} %copy-done, bf16[512,1024]{1,0:T(8,128)(2,1)S(1)} %collective-permute-done.5.got_ref, bf16[512,256]{1,0:T(8,128)(2,1)S(1)} %pad_maximum_fusion.1.slope_ref, ...), custom_call_target="tpu_custom_call" | custom-call | flops 536870912 | bytes 4194304 | tf_op jit(solution)/shard_map/gradient/pallas_call | solution.py:322
  83.0 1.4 %gradient.2 = (f32[512,256]{1,0:T(8,128)S(1)}, bf16[512,256]{1,0:T(8,128)(2,1)S(1)}) custom-call(s32[4]{0:T(128)S(1)} %pad_add_fusion.1.at, bf16[512,1024]{1,0:T(8,128)(2,1)S(1)} %copy-done, bf16[512,1024]{1,0:T(8,128)(2,1)S(1)} %collective-permute-done.5.got_ref, bf16[512,256]{1,0:T(8,128)(2,1)S(1)} %pad_maximum_fusion.slope_ref, ...), custom_call_target="tpu_custom_call" | custom-call | flops 536870912 | bytes 4194304 | tf_op jit(solution)/shard_map/gradient/pallas_call | solution.py:322
  84.4 2.0 %collective-permute-start.16 = (bf16[512,256]{1,0:T(8,128)(2,1)S(1)}, bf16[512,256]{1,0:T(8,128)(2,1)S(1)}, u32[]{:S(2)}, u32[]{:S(2)}) collective-permute-start(bf16[512,256]{1,0:T(8,128)(2,1)S(1)} %get-tuple-element.49), channel_id=1, source_target_pairs={{0,8},{4,20},{8,0},{12,28},{16,24},{20,4},{24,16},{28,12},{1,9},{5... | collective-permute-start | bytes 786440 | tf_op jit(solution)/shard_map/ppermute | solution.py:359
  86.5 2.9 %collective-permute-done.21 = bf16[512,256]{1,0:T(8,128)(2,1)S(1)} collective-permute-done((bf16[512,256]{1,0:T(8,128)(2,1)S(1)}, bf16[512,256]{1,0:T(8,128)(2,1)S(1)}, u32[]{:S(2)}, u32[]{:S(2)}) %collective-permute-start.21) | collective-permute-done | bytes 262176 | tf_op jit(solution)/shard_map/ppermute | solution.py:359
  89.5 3.0 %collective-permute-done.16 = bf16[512,256]{1,0:T(8,128)(2,1)S(1)} collective-permute-done((bf16[512,256]{1,0:T(8,128)(2,1)S(1)}, bf16[512,256]{1,0:T(8,128)(2,1)S(1)}, u32[]{:S(2)}, u32[]{:S(2)}) %collective-permute-start.16) | collective-permute-done | bytes 262176 | tf_op jit(solution)/shard_map/ppermute | solution.py:359
  92.7 1.8 %collective-permute-done.22 = bf16[256,256]{1,0:T(8,128)(2,1)S(1)} collective-permute-done((bf16[256,256]{1,0:T(8,128)(2,1)S(1)}, bf16[256,256]{1,0:T(8,128)(2,1)S(1)}, u32[]{:S(2)}, u32[]{:S(2)}) %collective-permute-start.22) | collective-permute-done | bytes 131104 | tf_op jit(solution)/shard_map/ppermute | solution.py:359
  94.5 3.2 %collective-permute-done.17 = bf16[256,256]{1,0:T(8,128)(2,1)S(1)} collective-permute-done((bf16[256,256]{1,0:T(8,128)(2,1)S(1)}, bf16[256,256]{1,0:T(8,128)(2,1)S(1)}, u32[]{:S(2)}, u32[]{:S(2)}) %collective-permute-start.17) | collective-permute-done | bytes 131104 | tf_op jit(solution)/shard_map/ppermute | solution.py:359
  98.4 13.0 %all_to_all.21 = bf16[8,32,512]{2,1,0:T(8,128)(2,1)S(1)} all-to-all(bf16[8,32,512]{2,1,0:T(8,128)(2,1)S(1)} %bitcast.27), channel_id=1, replica_groups=mesh['dp'=8,'tensor'=4] {'dp'}, dimensions={0} | all-to-all | bytes 524288 | tf_op jit(solution)/shard_map/all_to_all | solution.py:317
  (78 shorter events, 8.5 us)
Async XLA Ops:
  0.6 17.5 %collective-permute-start = (bf16[1024,512]{1,0:T(8,128)(2,1)}, bf16[1024,512]{1,0:T(8,128)(2,1)S(1)}, u32[]{:S(2)}, u32[]{:S(2)}) collective-permute-start(bf16[1024,512]{1,0:T(8,128)(2,1)} %param.14), channel_id=1, source_target_pairs={{0,8},{9,1},{18,26},{27,19},{4,20},{13,29},{22,6},{31,15}} | collective-permute-start | bytes 3145736 | tf_op jit(solution)/shard_map/ppermute | solution.py:186
  13.1 8.9 %copy-start.12 = (bf16[144,512]{1,0:T(8,128)(2,1)S(1)}, bf16[144,512]{1,0:T(8,128)(2,1)}, u32[]{:S(2)}) copy-start(bf16[144,512]{1,0:T(8,128)(2,1)} %get-tuple-element.31) | copy-start | bytes 442372
  13.1 18.9 %copy-start.11 = (bf16[144,512]{1,0:T(8,128)(2,1)S(1)}, bf16[144,512]{1,0:T(8,128)(2,1)}, u32[]{:S(2)}) copy-start(bf16[144,512]{1,0:T(8,128)(2,1)} %get-tuple-element.33) | copy-start | bytes 442372
  13.1 31.0 %collective-permute-start.5 = (bf16[512,1024]{1,0:T(8,128)(2,1)}, bf16[512,1024]{1,0:T(8,128)(2,1)S(1)}, u32[]{:S(2)}, u32[]{:S(2)}) collective-permute-start(bf16[512,1024]{1,0:T(8,128)(2,1)} %get-tuple-element.43), channel_id=1, source_target_pairs={{0,4},{4,0},{8,12},{12,8},{16,20},{20,16},{24,28},{28,24},{1,5},{5... | collective-permute-start | bytes 3145736 | tf_op jit(solution)/shard_map/ppermute | solution.py:29
  20.7 23.4 %copy-start.6 = (bf16[1024,256]{1,0:T(8,128)(2,1)}, bf16[1024,256]{1,0:T(8,128)(2,1)S(1)}, u32[]{:S(2)}) copy-start(bf16[1024,256]{1,0:T(8,128)(2,1)S(1)} %get-tuple-element.53) | copy-start | bytes 1572868
  20.7 23.3 %collective-permute-start.1 = (bf16[1024,256]{1,0:T(8,128)(2,1)S(1)}, bf16[1024,256]{1,0:T(8,128)(2,1)S(1)}, u32[]{:S(2)}, u32[]{:S(2)}) collective-permute-start(bf16[1024,256]{1,0:T(8,128)(2,1)S(1)} %get-tuple-element.53), channel_id=1, source_target_pairs={{0,16},{9,25},{18,2},{27,11},{8,24},{1,17},{26,10},{19,3},{4,12},{... | collective-permute-start | bytes 1572872 | tf_op jit(solution)/shard_map/ppermute | solution.py:186
  22.0 10.0 %collective-permute-start.2 = (bf16[144,512]{1,0:T(8,128)(2,1)S(1)}, bf16[144,512]{1,0:T(8,128)(2,1)S(1)}, u32[]{:S(2)}, u32[]{:S(2)}) collective-permute-start(bf16[144,512]{1,0:T(8,128)(2,1)S(1)} %copy-done.12), channel_id=1, source_target_pairs={{0,1},{1,0},{2,3},{3,2},{4,5},{5,4},{6,7},{7,6},{8,9},{9,8},{10,11... | collective-permute-start | bytes 442376 | tf_op jit(solution)/shard_map/ppermute | solution.py:37
  24.6 20.8 %collective-permute-start.11 = (bf16[1024,256]{1,0:T(8,128)(2,1)S(1)}, bf16[1024,256]{1,0:T(8,128)(2,1)}, u32[]{:S(2)}, u32[]{:S(2)}) collective-permute-start(bf16[1024,256]{1,0:T(8,128)(2,1)S(1)} %get-tuple-element.52), channel_id=1, source_target_pairs={{0,16},{9,25},{18,2},{27,11},{8,24},{1,17},{26,10},{19,3},{4,12},{... | collective-permute-start | bytes 1572872 | tf_op jit(solution)/shard_map/ppermute | solution.py:186
  26.7 17.3 %all-to-all-start = ((bf16[8,32,512]{2,1,0:T(8,128)(2,1)}), bf16[8,32,512]{2,1,0:T(8,128)(2,1)S(1)}, u32[]{:S(2)}, u32[]{:S(2)}) async-start(bf16[8,32,512]{2,1,0:T(8,128)(2,1)} %bitcast.9), calls=%async_computation | async-start | bytes 524288 | tf_op jit(solution)/shard_map/all_to_all | solution.py:254
  30.1 13.9 %collective-permute-start.3 = (bf16[144,512]{1,0:T(8,128)(2,1)}, bf16[144,512]{1,0:T(8,128)(2,1)S(1)}, u32[]{:S(2)}, u32[]{:S(2)}) collective-permute-start(bf16[144,512]{1,0:T(8,128)(2,1)} %get-tuple-element.32), channel_id=1, source_target_pairs={{0,2},{1,3},{2,0},{3,1},{4,6},{5,7},{6,4},{7,5},{8,10},{9,11},{10,... | collective-permute-start | bytes 442376 | tf_op jit(solution)/shard_map/ppermute | solution.py:37
  32.1 12.0 %collective-permute-start.4 = (bf16[144,512]{1,0:T(8,128)(2,1)S(1)}, bf16[144,512]{1,0:T(8,128)(2,1)S(1)}, u32[]{:S(2)}, u32[]{:S(2)}) collective-permute-start(bf16[144,512]{1,0:T(8,128)(2,1)S(1)} %copy-done.11), channel_id=1, source_target_pairs={{0,3},{1,2},{2,1},{3,0},{4,7},{5,6},{6,5},{7,4},{8,11},{9,10},{10,... | collective-permute-start | bytes 442376 | tf_op jit(solution)/shard_map/ppermute | solution.py:37
  44.0 2.4 %copy-start.1 = (bf16[144,512]{1,0:T(8,128)(2,1)S(1)}, bf16[144,512]{1,0:T(8,128)(2,1)}, u32[]{:S(2)}) copy-start(bf16[144,512]{1,0:T(8,128)(2,1)} %get-tuple-element.35.refs_0_) | copy-start | bytes 442372
  44.0 2.4 %copy-start.2 = (s32[1,1,8]{2,1,0:T(1,128)S(1)}, s32[1,1,8]{2,1,0:T(1,128)}, u32[]{:S(2)}) copy-start(s32[1,1,8]{2,1,0:T(1,128)} %param.15) | copy-start | bytes 100
  44.1 2.3 %copy-start.3 = (s32[1,1,8]{2,1,0:T(1,128)S(1)}, s32[1,1,8]{2,1,0:T(1,128)}, u32[]{:S(2)}) copy-start(s32[1,1,8]{2,1,0:T(1,128)} %param.16) | copy-start | bytes 100
  44.1 2.3 %copy-start.4 = (f32[1,1,8]{2,1,0:T(1,128)S(1)}, f32[1,1,8]{2,1,0:T(1,128)}, u32[]{:S(2)}) copy-start(f32[1,1,8]{2,1,0:T(1,128)} %param.17) | copy-start | bytes 100
  45.3 2.2 %collective-permute-start.6 = (bf16[512,256]{1,0:T(8,128)(2,1)S(1)}, bf16[512,256]{1,0:T(8,128)(2,1)S(1)}, u32[]{:S(2)}, u32[]{:S(2)}) collective-permute-start(bf16[512,256]{1,0:T(8,128)(2,1)S(1)} %convolution_convert_fusion.2), channel_id=1, source_target_pairs={{0,4},{4,0},{8,12},{12,8},{16,20},{20,16},{24,28},{28,24},{1,5},{5... | collective-permute-start | bytes 786440 | tf_op jit(solution)/shard_map/ppermute | solution.py:29
  45.8 6.6 %collective-permute-start.12 = (bf16[512,256]{1,0:T(8,128)(2,1)S(1)}, bf16[512,256]{1,0:T(8,128)(2,1)S(1)}, u32[]{:S(2)}, u32[]{:S(2)}) collective-permute-start(bf16[512,256]{1,0:T(8,128)(2,1)S(1)} %convolution_convert_fusion.1), channel_id=1, source_target_pairs={{0,4},{4,0},{8,12},{12,8},{16,20},{20,16},{24,28},{28,24},{1,5},{5... | collective-permute-start | bytes 786440 | tf_op jit(solution)/shard_map/ppermute | solution.py:29
  48.0 8.8 %collective-permute-start.7 = (bf16[256,256]{1,0:T(8,128)(2,1)S(1)}, bf16[256,256]{1,0:T(8,128)(2,1)S(1)}, u32[]{:S(2)}, u32[]{:S(2)}) collective-permute-start(bf16[256,256]{1,0:T(8,128)(2,1)S(1)} %slice.135), channel_id=1, source_target_pairs={{0,1},{1,0},{2,3},{3,2},{4,5},{5,4},{6,7},{7,6},{8,9},{9,8},{10,11... | collective-permute-start | bytes 393224 | tf_op jit(solution)/shard_map/ppermute | solution.py:37
  53.0 7.0 %collective-permute-start.13 = (bf16[256,256]{1,0:T(8,128)(2,1)S(1)}, bf16[256,256]{1,0:T(8,128)(2,1)S(1)}, u32[]{:S(2)}, u32[]{:S(2)}) collective-permute-start(bf16[256,256]{1,0:T(8,128)(2,1)S(1)} %slice.134), channel_id=1, source_target_pairs={{0,1},{1,0},{2,3},{3,2},{4,5},{5,4},{6,7},{7,6},{8,9},{9,8},{10,11... | collective-permute-start | bytes 393224 | tf_op jit(solution)/shard_map/ppermute | solution.py:37
  56.8 6.1 %collective-permute-start.8 = (bf16[128,256]{1,0:T(8,128)(2,1)S(1)}, bf16[128,256]{1,0:T(8,128)(2,1)S(1)}, u32[]{:S(2)}, u32[]{:S(2)}) collective-permute-start(bf16[128,256]{1,0:T(8,128)(2,1)S(1)} %slice.137), channel_id=1, source_target_pairs={{0,2},{1,3},{2,0},{3,1},{4,6},{5,7},{6,4},{7,5},{8,10},{9,11},{10,... | collective-permute-start | bytes 196616 | tf_op jit(solution)/shard_map/ppermute | solution.py:37
  60.0 6.3 %collective-permute-start.14 = (bf16[128,256]{1,0:T(8,128)(2,1)S(1)}, bf16[128,256]{1,0:T(8,128)(2,1)S(1)}, u32[]{:S(2)}, u32[]{:S(2)}) collective-permute-start(bf16[128,256]{1,0:T(8,128)(2,1)S(1)} %slice.136), channel_id=1, source_target_pairs={{0,2},{1,3},{2,0},{3,1},{4,6},{5,7},{6,4},{7,5},{8,10},{9,11},{10,... | collective-permute-start | bytes 196616 | tf_op jit(solution)/shard_map/ppermute | solution.py:37
  66.5 7.3 %collective-permute-start.18 = (bf16[128,256]{1,0:T(8,128)(2,1)S(1)}, bf16[128,256]{1,0:T(8,128)(2,1)S(1)}, u32[]{:S(2)}, u32[]{:S(2)}) collective-permute-start(bf16[128,256]{1,0:T(8,128)(2,1)S(1)} %get-tuple-element.59), channel_id=1, source_target_pairs={{0,2},{1,3},{2,0},{3,1},{4,6},{5,7},{6,4},{7,5},{8,10},{9,11},{10,... | collective-permute-start | bytes 196616 | tf_op jit(solution)/shard_map/ppermute | solution.py:37
  68.1 6.6 %collective-permute-start.9 = (bf16[128,256]{1,0:T(8,128)(2,1)S(1)}, bf16[128,256]{1,0:T(8,128)(2,1)S(1)}, u32[]{:S(2)}, u32[]{:S(2)}) collective-permute-start(bf16[128,256]{1,0:T(8,128)(2,1)S(1)} %get-tuple-element.57), channel_id=1, source_target_pairs={{0,2},{1,3},{2,0},{3,1},{4,6},{5,7},{6,4},{7,5},{8,10},{9,11},{10,... | collective-permute-start | bytes 196616 | tf_op jit(solution)/shard_map/ppermute | solution.py:37
  73.8 6.0 %collective-permute-start.19 = (bf16[256,256]{1,0:T(8,128)(2,1)S(1)}, bf16[256,256]{1,0:T(8,128)(2,1)S(1)}, u32[]{:S(2)}, u32[]{:S(2)}) collective-permute-start(bf16[256,256]{1,0:T(8,128)(2,1)S(1)} %pad_maximum_fusion.4), channel_id=1, source_target_pairs={{0,1},{1,0},{2,3},{3,2},{4,5},{5,4},{6,7},{7,6},{8,9},{9,8},{10,11... | collective-permute-start | bytes 393224 | tf_op jit(solution)/shard_map/ppermute | solution.py:37
  74.8 6.5 %collective-permute-start.10 = (bf16[256,256]{1,0:T(8,128)(2,1)S(1)}, bf16[256,256]{1,0:T(8,128)(2,1)S(1)}, u32[]{:S(2)}, u32[]{:S(2)}) collective-permute-start(bf16[256,256]{1,0:T(8,128)(2,1)S(1)} %pad_maximum_fusion.3), channel_id=1, source_target_pairs={{0,1},{1,0},{2,3},{3,2},{4,5},{5,4},{6,7},{7,6},{8,9},{9,8},{10,11... | collective-permute-start | bytes 393224 | tf_op jit(solution)/shard_map/ppermute | solution.py:37
  79.9 1.6 %collective-permute-start.20 = (bf16[512,256]{1,0:T(8,128)(2,1)S(1)}, bf16[512,256]{1,0:T(8,128)(2,1)S(1)}, u32[]{:S(2)}, u32[]{:S(2)}) collective-permute-start(bf16[512,256]{1,0:T(8,128)(2,1)S(1)} %pad_maximum_fusion.1.slope_ref), channel_id=1, source_target_pairs={{0,4},{4,0},{8,12},{12,8},{16,20},{20,16},{24,28},{28,24},{1,5},{5... | collective-permute-start | bytes 786440 | tf_op jit(solution)/shard_map/ppermute | solution.py:29
  81.3 1.8 %collective-permute-start.15 = (bf16[512,256]{1,0:T(8,128)(2,1)S(1)}, bf16[512,256]{1,0:T(8,128)(2,1)S(1)}, u32[]{:S(2)}, u32[]{:S(2)}) collective-permute-start(bf16[512,256]{1,0:T(8,128)(2,1)S(1)} %pad_maximum_fusion.slope_ref), channel_id=1, source_target_pairs={{0,4},{4,0},{8,12},{12,8},{16,20},{20,16},{24,28},{28,24},{1,5},{5... | collective-permute-start | bytes 786440 | tf_op jit(solution)/shard_map/ppermute | solution.py:29
  82.9 6.4 %collective-permute-start.21 = (bf16[512,256]{1,0:T(8,128)(2,1)S(1)}, bf16[512,256]{1,0:T(8,128)(2,1)S(1)}, u32[]{:S(2)}, u32[]{:S(2)}) collective-permute-start(bf16[512,256]{1,0:T(8,128)(2,1)S(1)} %get-tuple-element.51), channel_id=1, source_target_pairs={{0,8},{4,20},{8,0},{12,28},{16,24},{20,4},{24,16},{28,12},{1,9},{5... | collective-permute-start | bytes 786440 | tf_op jit(solution)/shard_map/ppermute | solution.py:359
  84.4 8.1 %collective-permute-start.16 = (bf16[512,256]{1,0:T(8,128)(2,1)S(1)}, bf16[512,256]{1,0:T(8,128)(2,1)S(1)}, u32[]{:S(2)}, u32[]{:S(2)}) collective-permute-start(bf16[512,256]{1,0:T(8,128)(2,1)S(1)} %get-tuple-element.49), channel_id=1, source_target_pairs={{0,8},{4,20},{8,0},{12,28},{16,24},{20,4},{24,16},{28,12},{1,9},{5... | collective-permute-start | bytes 786440 | tf_op jit(solution)/shard_map/ppermute | solution.py:359
  89.4 5.0 %collective-permute-start.22 = (bf16[256,256]{1,0:T(8,128)(2,1)S(1)}, bf16[256,256]{1,0:T(8,128)(2,1)S(1)}, u32[]{:S(2)}, u32[]{:S(2)}) collective-permute-start(bf16[256,256]{1,0:T(8,128)(2,1)S(1)} %slice.132), channel_id=1, source_target_pairs={{0,16},{4,12},{8,24},{12,4},{16,0},{20,28},{24,8},{28,20},{1,17},{... | collective-permute-start | bytes 393224 | tf_op jit(solution)/shard_map/ppermute | solution.py:359
  92.6 5.0 %collective-permute-start.17 = (bf16[256,256]{1,0:T(8,128)(2,1)S(1)}, bf16[256,256]{1,0:T(8,128)(2,1)S(1)}, u32[]{:S(2)}, u32[]{:S(2)}) collective-permute-start(bf16[256,256]{1,0:T(8,128)(2,1)S(1)} %slice.133), channel_id=1, source_target_pairs={{0,16},{4,12},{8,24},{12,4},{16,0},{20,28},{24,8},{28,20},{1,17},{... | collective-permute-start | bytes 393224 | tf_op jit(solution)/shard_map/ppermute | solution.py:359
  97.7 13.7 %collective-permute-start.23 = (bf16[256,512]{1,0:T(8,128)(2,1)S(1)}, bf16[256,512]{1,0:T(8,128)(2,1)S(1)}, u32[]{:S(2)}, u32[]{:S(2)}) collective-permute-start(bf16[256,512]{1,0:T(8,128)(2,1)S(1)} %pad_maximum_fusion.2), channel_id=1, source_target_pairs={{0,0},{1,10},{2,17},{3,27},{4,4},{5,14},{6,21},{7,31},{8,1},{9,11}... | collective-permute-start | bytes 786440 | tf_op jit(solution)/shard_map/ppermute | solution.py:370
  (6 other events, 10.8 us)

commit v9 on v8

--- a/solution.py
+++ b/solution.py
@@ -262,43 +262,47 @@
         chunk_at.append(place ^ away ^ turned(t, levels))
     chunk_at = jnp.stack(chunk_at).astype(jnp.int32)
 
-    values, slopes = [], []
+    value_parts = []
     for j in range(PARTS):
         held_part, got_part, is_getter_part = parts[j]
-        if j == 0:
-            got_part, got_cot, *ref_got = lax.optimization_barrier((got_part, got_cot, *ref_got))
+        if j == PARTS - 1:
+            got_part, got_cot = lax.optimization_barrier((got_part, got_cot))
         weight = jnp.where(is_getter_part, got_part, held_part)
         value_given = dot(got_rows, weight).astype(BF16)
-        if j == 0:
-            smem = pl.BlockSpec(memory_space=pltpu.SMEM)
-            vmem = pl.BlockSpec(memory_space=pltpu.VMEM)
-            fixed, pull, row_scale, row_at = pl.pallas_call(
-                functools.partial(row_kernel, tensor_count, span_rows, model_width),
-                in_specs=[smem] * 3 + [vmem] * (2 + tensor_count),
-                out_specs=[vmem] * 4,
-                out_shape=[
-                    jax.ShapeDtypeStruct((own_rows, value_width), F32),
-                    jax.ShapeDtypeStruct((own_rows, 128), F32),
-                    jax.ShapeDtypeStruct((own_rows, 128), F32),
-                    jax.ShapeDtypeStruct((own_rows, slot_count), BF16),
-                ],
-                compiler_params=pltpu.CompilerParams(vmem_limit_bytes=16 * 2**20),
-                cost_estimate=pl.CostEstimate(
-                    flops=2 * own_rows * slot_count * value_width,
-                    bytes_accessed=2**21,
-                    transcendentals=0,
-                ),
-                name="rows",
-            )(
-                lengths.reshape(-1),
-                bins.reshape(-1),
-                advantage.reshape(-1),
-                logprob_gap.reshape(1, own_rows),
-                got_cot,
-                *ref_got,
-            )
-        value_part = dot(kept_rows, weight) + swapped(value_given, dp_count).astype(F32)
-        total = value_part
+        value_got = swapped(value_given, dp_count).astype(F32)
+        value_parts.append(dot(kept_rows, weight) + value_got)
+
+    smem = pl.BlockSpec(memory_space=pltpu.SMEM)
+    vmem = pl.BlockSpec(memory_space=pltpu.VMEM)
+    fixed, pull, row_scale, row_at = pl.pallas_call(
+        functools.partial(row_kernel, tensor_count, span_rows, model_width),
+        in_specs=[smem] * 3 + [vmem] * (2 + tensor_count),
+        out_specs=[vmem] * 4,
+        out_shape=[
+            jax.ShapeDtypeStruct((own_rows, value_width), F32),
+            jax.ShapeDtypeStruct((own_rows, 128), F32),
+            jax.ShapeDtypeStruct((own_rows, 128), F32),
+            jax.ShapeDtypeStruct((own_rows, slot_count), BF16),
+        ],
+        compiler_params=pltpu.CompilerParams(vmem_limit_bytes=16 * 2**20),
+        cost_estimate=pl.CostEstimate(
+            flops=2 * own_rows * slot_count * value_width,
+            bytes_accessed=2**21,
+            transcendentals=0,
+        ),
+        name="rows",
+    )(
+        lengths.reshape(-1),
+        bins.reshape(-1),
+        advantage.reshape(-1),
+        logprob_gap.reshape(1, own_rows),
+        got_cot,
+        *ref_got,
+    )
+
+    values, slopes = [], []
+    for j in range(PARTS):
+        total = value_parts[j]
         for level in range(levels):
             rows = total.shape[0] // 2
             sent = total[rows:].astype(BF16)

time: 113 us -> 106 us (0.938)
  waiting for transfers between devices: 44 us -> 33.3 us
  starting transfers between devices: 35.7 us -> 38.1 us
  matrix products: 2.04 us -> 3.7 us
    ppermute x11, waiting for transfers between devices: 28.3 us -> 12.8 us  [crossed(): return lax.ppermute(array, 'tensor', [(i, i ^ step) for i in range(count)])]
    all_to_all x1, waiting for transfers between devices: 0.01 us -> 3.82 us  [on_device(): got_cot = lax.all_to_all(cot, 'dp', split_axis=0, concat_axis=0, tiled=True)]
    all_to_all x1, starting transfers between devices: 3.41 us -> 5.38 us  [on_device(): got_cot = lax.all_to_all(cot, 'dp', split_axis=0, concat_axis=0, tiled=True)]
    dot_general x4, matrix products: 1.79 us -> 3.46 us  [dot(): return jnp.dot(a, b, preferred_element_type=F32)]
    ppermute x4, starting transfers between devices: 2.3 us -> 3.66 us  [on_device(): total = total + lax.ppermute(given, 'dp', pairs).astype(F32)]
    unnamed x27 -> x23, local copies, waits for them, and re-layouts: 2.44 us -> 2.52 us
  transfers between devices with their start and end apart: 25 -> 25, of which waited for: 12 -> 13; matrix products, arithmetic and copies ran while one was open for 4% -> 6% of each run, Pallas kernels for 10% -> 10%
where the time goes in v9:
time: 106 us
  starting transfers between devices  38.1 us (36%)
  waiting for transfers between devices  33.3 us (31%)
  blocking collectives  12.3 us (12%)
  Pallas kernels  10.9 us (10%)
  matrix products  3.7 us (3%)
  other arithmetic  3.55 us (3%)
  local copies, waits for them, and re-layouts  2.71 us (3%)
    ppermute x11, starting transfers between devices, crossed(): return lax.ppermute(array, 'tensor', [(i, i ^ step) for i in range(count)])  19.5 us
    ppermute x11, waiting for transfers between devices, crossed(): return lax.ppermute(array, 'tensor', [(i, i ^ step) for i in range(count)])  12.8 us
    all_to_all x1, blocking collectives, on_device(): lax.all_to_all(sent, 'dp', split_axis=0, concat_axis=0, tiled=True)  12.3 us
    ppermute x4, waiting for transfers between devices, on_device(): total = total + lax.ppermute(given, 'dp', pairs).astype(F32)  11.9 us
    ppermute x3, starting transfers between devices, stage(): return (lax.ppermute(held, AXES, pairs), is_getter)  8.34 us
    pallas_call x1, Pallas kernels, on_device(): pl.pallas_call(functools.partial(prepare_kernel, tensor_count, steps), gr...  7.03 us
    all_to_all x1, starting transfers between devices, on_device(): got_cot = lax.all_to_all(cot, 'dp', split_axis=0, concat_axis=0, tiled=True)  5.38 us
    ppermute x3, waiting for transfers between devices, stage(): return (lax.ppermute(held, AXES, pairs), is_getter)  4.8 us
  transfers between devices with their start and end apart: 25, of which 13 were waited for; matrix products, arithmetic and copies ran while one was open for 6% of the time, Pallas kernels for 10%

profile of v9, /device:TPU:0, one launch (start us, length us, event | category | flops | bytes accessed | tf_op | source)
XLA Modules:
  0.0 105.6 jit_solution(315656602006005538)
XLA Ops:
  0.6 4.9 %collective-permute-start = (bf16[1024,512]{1,0:T(8,128)(2,1)}, bf16[1024,512]{1,0:T(8,128)(2,1)S(1)}, u32[]{:S(2)}, u32[]{:S(2)}) collective-permute-start(bf16[1024,512]{1,0:T(8,128)(2,1)} %param.14), channel_id=1, source_target_pairs={{0,8},{9,1},{18,26},{27,19},{4,20},{13,29},{22,6},{31,15}} | collective-permute-start | bytes 3145736 | tf_op jit(solution)/shard_map/ppermute | solution.py:186
  6.2 7.0 %prepare.1 = (bf16[512,1024]{1,0:T(8,128)(2,1)}, bf16[512,1024]{1,0:T(8,128)(2,1)}, bf16[144,512]{1,0:T(8,128)(2,1)}, bf16[144,512]{1,0:T(8,128)(2,1)}, bf16[144...) custom-call(s32[2]{0:T(128)} %pad_add_fusion.at, bf16[512,2048]{1,0:T(8,128)(2,1)} %x_ref.1, f32[1,2048]{1,0:T(1,128)} %bitcast.30, ...), custom_call_target="tpu_custom_call" | custom-call | flops 1073741824 | bytes 8388608 | tf_op jit(solution)/shard_map/prepare/pallas_call | solution.py:198
  13.3 4.8 %collective-permute-done = bf16[1024,512]{1,0:T(8,128)(2,1)S(1)} collective-permute-done((bf16[1024,512]{1,0:T(8,128)(2,1)}, bf16[1024,512]{1,0:T(8,128)(2,1)S(1)}, u32[]{:S(2)}, u32[]{:S(2)}) %collective-permute-start) | collective-permute-done | bytes 1048608 | tf_op jit(solution)/shard_map/ppermute | solution.py:186
  18.1 1.0 copy-done.8
  19.1 1.6 %slice_select_fusion = (bf16[1024,256]{1,0:T(8,128)(2,1)S(1)}, bf16[1024,256]{1,0:T(8,128)(2,1)S(1)}) fusion(bf16[1024,512]{1,0:T(8,128)(2,1)} %param.14, bf16[1024,512]{1,0:T(8,128)(2,1)} %copy-done.8, pred[]{:T(512)S(6)} %or.15), kind=kLoop, calls=%fused_computation.7 | loop fusion | flops 524288 | bytes 3145729 | tf_op jit(solution)/shard_map/jit(_where)/select_n | solution.py:248
  20.7 1.3 %collective-permute-start.5 = (bf16[1024,256]{1,0:T(8,128)(2,1)S(1)}, bf16[1024,256]{1,0:T(8,128)(2,1)S(1)}, u32[]{:S(2)}, u32[]{:S(2)}) collective-permute-start(bf16[1024,256]{1,0:T(8,128)(2,1)S(1)} %get-tuple-element.44), channel_id=1, source_target_pairs={{0,16},{9,25},{18,2},{27,11},{8,24},{1,17},{26,10},{19,3},{4,12},{... | collective-permute-start | bytes 1572872 | tf_op jit(solution)/shard_map/ppermute | solution.py:186
  22.0 2.1 %collective-permute-start.1 = (bf16[1024,256]{1,0:T(8,128)(2,1)S(1)}, bf16[1024,256]{1,0:T(8,128)(2,1)}, u32[]{:S(2)}, u32[]{:S(2)}) collective-permute-start(bf16[1024,256]{1,0:T(8,128)(2,1)S(1)} %get-tuple-element.45), channel_id=1, source_target_pairs={{0,16},{9,25},{18,2},{27,11},{8,24},{1,17},{26,10},{19,3},{4,12},{... | collective-permute-start | bytes 1572872 | tf_op jit(solution)/shard_map/ppermute | solution.py:186
  24.2 2.5 %collective-permute-start.2 = (bf16[144,512]{1,0:T(8,128)(2,1)}, bf16[144,512]{1,0:T(8,128)(2,1)S(1)}, u32[]{:S(2)}, u32[]{:S(2)}) collective-permute-start(bf16[144,512]{1,0:T(8,128)(2,1)} %get-tuple-element.28), channel_id=1, source_target_pairs={{0,1},{1,0},{2,3},{3,2},{4,5},{5,4},{6,7},{7,6},{8,9},{9,8},{10,11... | collective-permute-start | bytes 442376 | tf_op jit(solution)/shard_map/ppermute | solution.py:37
  26.6 5.4 %all-to-all-start = ((bf16[8,32,512]{2,1,0:T(8,128)(2,1)}), bf16[8,32,512]{2,1,0:T(8,128)(2,1)S(1)}, u32[]{:S(2)}, u32[]{:S(2)}) async-start(bf16[8,32,512]{2,1,0:T(8,128)(2,1)} %bitcast.9), calls=%async_computation | async-start | bytes 524288 | tf_op jit(solution)/shard_map/all_to_all | solution.py:254
  32.1 0.9 collective-permute-start.4
  33.7 1.2 %convolution_convert_fusion.2 = bf16[512,256]{1,0:T(8,128)(2,1)} fusion(bf16[512,1024]{1,0:T(8,128)(2,1)S(1)} %collective-permute-done.6.got_ref, bf16[1024,256]{1,0:T(8,128)(2,1)S(1)} %collective-permute-done.5, bf16[1024,256]{1,0:T(8,128)(2,1)S(1)} %get-tuple-element.44, pred[]{:T(512)S(6)} %or.18), kind=kOutput, calls=%fused_computation.4 | convolution fusion | flops 268828672 | bytes 2359297 | tf_op jit(solution)/shard_map/dot_general | solution.py:21
  35.1 3.8 %all-to-all-done = bf16[8,32,512]{2,1,0:T(8,128)(2,1)S(1)} async-done(((bf16[8,32,512]{2,1,0:T(8,128)(2,1)}), bf16[8,32,512]{2,1,0:T(8,128)(2,1)S(1)}, u32[]{:S(2)}, u32[]{:S(2)}) %all-to-all-start) | async-done | bytes 262176 | tf_op jit(solution)/shard_map/all_to_all | solution.py:254
  39.5 1.0 collective-permute-done.4.refs_3_
  40.5 1.1 %rows.1 = (f32[128,512]{1,0:T(8,128)S(1)}, f32[128,128]{1,0:T(8,128)S(1)}, f32[128,128]{1,0:T(8,128)S(1)}, bf16[128,256]{1,0:T(8,128)(2,1)S(1)}) custom-call(s32[8]{0:T(128)S(1)} %bitcast.23, s32[8]{0:T(128)S(1)} %bitcast.24, f32[8]{0:T(128)S(1)} %bitcast.25, f32[1,128]{1,0:T(1,128)S(1)} %bitcast.26, bf16[256,512]{1,0:T(8,128)(2,1)S(1)} %bitcast.22, ...), custom_call_target="tpu_custom_call" | custom-call | flops 33554432 | bytes 2097152 | tf_op jit(solution)/shard_map/rows/pallas_call | solution.py:277
  41.6 1.4 %convolution_add_fusion.1 = f32[512,256]{1,0:T(8,128)S(1)} fusion(bf16[512,1024]{1,0:T(8,128)(2,1)S(1)} %copy-done, bf16[512,256]{1,0:T(8,128)(2,1)} %collective-permute-done.7, bf16[1024,256]{1,0:T(8,128)(2,1)S(1)} %copy-done.10, bf16[1024,256]{1,0:T(8,128)(2,1)S(1)} %copy-done.7, pred[]{:T(512)S(6)} %or.18), kind=kOutput, calls=%fused_computation.1 | convolution fusion | flops 268959744 | bytes 2883585 | tf_op jit(solution)/shard_map/dot_general | solution.py:21
  43.1 2.7 %collective-permute-start.8 = (bf16[256,256]{1,0:T(8,128)(2,1)S(1)}, bf16[256,256]{1,0:T(8,128)(2,1)S(1)}, u32[]{:S(2)}, u32[]{:S(2)}) collective-permute-start(bf16[256,256]{1,0:T(8,128)(2,1)S(1)} %slice.135), channel_id=1, source_target_pairs={{0,1},{1,0},{2,3},{3,2},{4,5},{5,4},{6,7},{7,6},{8,9},{9,8},{10,11... | collective-permute-start | bytes 393224 | tf_op jit(solution)/shard_map/ppermute | solution.py:37
  46.3 3.6 %collective-permute-done.8 = bf16[256,256]{1,0:T(8,128)(2,1)S(1)} collective-permute-done((bf16[256,256]{1,0:T(8,128)(2,1)S(1)}, bf16[256,256]{1,0:T(8,128)(2,1)S(1)}, u32[]{:S(2)}, u32[]{:S(2)}) %collective-permute-start.8) | collective-permute-done | bytes 131104 | tf_op jit(solution)/shard_map/ppermute | solution.py:37
  50.0 3.0 %collective-permute-start.9 = (bf16[128,256]{1,0:T(8,128)(2,1)S(1)}, bf16[128,256]{1,0:T(8,128)(2,1)S(1)}, u32[]{:S(2)}, u32[]{:S(2)}) collective-permute-start(bf16[128,256]{1,0:T(8,128)(2,1)S(1)} %slice.137), channel_id=1, source_target_pairs={{0,2},{1,3},{2,0},{3,1},{4,6},{5,7},{6,4},{7,5},{8,10},{9,11},{10,... | collective-permute-start | bytes 196616 | tf_op jit(solution)/shard_map/ppermute | solution.py:37
  53.0 2.9 %collective-permute-start.14 = (bf16[128,256]{1,0:T(8,128)(2,1)S(1)}, bf16[128,256]{1,0:T(8,128)(2,1)S(1)}, u32[]{:S(2)}, u32[]{:S(2)}) collective-permute-start(bf16[128,256]{1,0:T(8,128)(2,1)S(1)} %slice.136), channel_id=1, source_target_pairs={{0,2},{1,3},{2,0},{3,1},{4,6},{5,7},{6,4},{7,5},{8,10},{9,11},{10,... | collective-permute-start | bytes 196616 | tf_op jit(solution)/shard_map/ppermute | solution.py:37
  56.0 2.8 %collective-permute-done.14 = bf16[128,256]{1,0:T(8,128)(2,1)S(1)} collective-permute-done((bf16[128,256]{1,0:T(8,128)(2,1)S(1)}, bf16[128,256]{1,0:T(8,128)(2,1)S(1)}, u32[]{:S(2)}, u32[]{:S(2)}) %collective-permute-start.14) | collective-permute-done | bytes 65568 | tf_op jit(solution)/shard_map/ppermute | solution.py:37
  58.9 2.5 %collective-permute-start.18 = (bf16[128,256]{1,0:T(8,128)(2,1)S(1)}, bf16[128,256]{1,0:T(8,128)(2,1)S(1)}, u32[]{:S(2)}, u32[]{:S(2)}) collective-permute-start(bf16[128,256]{1,0:T(8,128)(2,1)S(1)} %get-tuple-element.51), channel_id=1, source_target_pairs={{0,2},{1,3},{2,0},{3,1},{4,6},{5,7},{6,4},{7,5},{8,10},{9,11},{10,... | collective-permute-start | bytes 196616 | tf_op jit(solution)/shard_map/ppermute | solution.py:37
  61.9 2.4 %collective-permute-done.18 = bf16[128,256]{1,0:T(8,128)(2,1)S(1)} collective-permute-done((bf16[128,256]{1,0:T(8,128)(2,1)S(1)}, bf16[128,256]{1,0:T(8,128)(2,1)S(1)}, u32[]{:S(2)}, u32[]{:S(2)}) %collective-permute-start.18) | collective-permute-done | bytes 65568 | tf_op jit(solution)/shard_map/ppermute | solution.py:37
  64.3 1.9 %collective-permute-start.19 = (bf16[256,256]{1,0:T(8,128)(2,1)S(1)}, bf16[256,256]{1,0:T(8,128)(2,1)S(1)}, u32[]{:S(2)}, u32[]{:S(2)}) collective-permute-start(bf16[256,256]{1,0:T(8,128)(2,1)S(1)} %pad_maximum_fusion.4), channel_id=1, source_target_pairs={{0,1},{1,0},{2,3},{3,2},{4,5},{5,4},{6,7},{7,6},{8,9},{9,8},{10,11... | collective-permute-start | bytes 393224 | tf_op jit(solution)/shard_map/ppermute | solution.py:37
  66.6 2.7 %collective-permute-start.11 = (bf16[256,256]{1,0:T(8,128)(2,1)S(1)}, bf16[256,256]{1,0:T(8,128)(2,1)S(1)}, u32[]{:S(2)}, u32[]{:S(2)}) collective-permute-start(bf16[256,256]{1,0:T(8,128)(2,1)S(1)} %pad_maximum_fusion.3), channel_id=1, source_target_pairs={{0,1},{1,0},{2,3},{3,2},{4,5},{5,4},{6,7},{7,6},{8,9},{9,8},{10,11... | collective-permute-start | bytes 393224 | tf_op jit(solution)/shard_map/ppermute | solution.py:37
  70.3 2.0 %collective-permute-done.11 = bf16[256,256]{1,0:T(8,128)(2,1)S(1)} collective-permute-done((bf16[256,256]{1,0:T(8,128)(2,1)S(1)}, bf16[256,256]{1,0:T(8,128)(2,1)S(1)}, u32[]{:S(2)}, u32[]{:S(2)}) %collective-permute-start.11) | collective-permute-done | bytes 131104 | tf_op jit(solution)/shard_map/ppermute | solution.py:37
  72.4 1.4 %gradient.3 = (f32[512,256]{1,0:T(8,128)S(1)}, bf16[512,256]{1,0:T(8,128)(2,1)S(1)}) custom-call(s32[4]{0:T(128)S(1)} %pad_add_fusion.1.at, bf16[512,1024]{1,0:T(8,128)(2,1)S(1)} %copy-done, bf16[512,1024]{1,0:T(8,128)(2,1)S(1)} %collective-permute-done.6.got_ref, bf16[512,256]{1,0:T(8,128)(2,1)S(1)} %pad_maximum_fusion.1.slope_ref, ...), custom_call_target="tpu_custom_call" | custom-call | flops 536870912 | bytes 4194304 | tf_op jit(solution)/shard_map/gradient/pallas_call | solution.py:326
  73.8 3.4 %collective-permute-start.21 = (bf16[512,256]{1,0:T(8,128)(2,1)S(1)}, bf16[512,256]{1,0:T(8,128)(2,1)S(1)}, u32[]{:S(2)}, u32[]{:S(2)}) collective-permute-start(bf16[512,256]{1,0:T(8,128)(2,1)S(1)} %get-tuple-element.43), channel_id=1, source_target_pairs={{0,8},{4,20},{8,0},{12,28},{16,24},{20,4},{24,16},{28,12},{1,9},{5... | collective-permute-start | bytes 786440 | tf_op jit(solution)/shard_map/ppermute | solution.py:363
  77.3 1.4 %gradient.2 = (f32[512,256]{1,0:T(8,128)S(1)}, bf16[512,256]{1,0:T(8,128)(2,1)S(1)}) custom-call(s32[4]{0:T(128)S(1)} %pad_add_fusion.1.at, bf16[512,1024]{1,0:T(8,128)(2,1)S(1)} %copy-done, bf16[512,1024]{1,0:T(8,128)(2,1)S(1)} %collective-permute-done.6.got_ref, bf16[512,256]{1,0:T(8,128)(2,1)S(1)} %pad_maximum_fusion.slope_ref, ...), custom_call_target="tpu_custom_call" | custom-call | flops 536870912 | bytes 4194304 | tf_op jit(solution)/shard_map/gradient/pallas_call | solution.py:326
  78.8 2.9 %collective-permute-done.21 = bf16[512,256]{1,0:T(8,128)(2,1)S(1)} collective-permute-done((bf16[512,256]{1,0:T(8,128)(2,1)S(1)}, bf16[512,256]{1,0:T(8,128)(2,1)S(1)}, u32[]{:S(2)}, u32[]{:S(2)}) %collective-permute-start.21) | collective-permute-done | bytes 262176 | tf_op jit(solution)/shard_map/ppermute | solution.py:363
  81.8 4.1 %collective-permute-done.16 = bf16[512,256]{1,0:T(8,128)(2,1)S(1)} collective-permute-done((bf16[512,256]{1,0:T(8,128)(2,1)S(1)}, bf16[512,256]{1,0:T(8,128)(2,1)S(1)}, u32[]{:S(2)}, u32[]{:S(2)}) %collective-permute-start.16) | collective-permute-done | bytes 262176 | tf_op jit(solution)/shard_map/ppermute | solution.py:363
  86.8 4.2 %collective-permute-done.17 = bf16[256,256]{1,0:T(8,128)(2,1)S(1)} collective-permute-done((bf16[256,256]{1,0:T(8,128)(2,1)S(1)}, bf16[256,256]{1,0:T(8,128)(2,1)S(1)}, u32[]{:S(2)}, u32[]{:S(2)}) %collective-permute-start.17) | collective-permute-done | bytes 131104 | tf_op jit(solution)/shard_map/ppermute | solution.py:363
  91.8 12.3 %all_to_all.21 = bf16[8,32,512]{2,1,0:T(8,128)(2,1)S(1)} all-to-all(bf16[8,32,512]{2,1,0:T(8,128)(2,1)S(1)} %bitcast.27), channel_id=1, replica_groups=mesh['dp'=8,'tensor'=4] {'dp'}, dimensions={0} | all-to-all | bytes 524288 | tf_op jit(solution)/shard_map/all_to_all | solution.py:321
  (74 shorter events, 8.7 us)
Async XLA Ops:
  0.6 17.5 %collective-permute-start = (bf16[1024,512]{1,0:T(8,128)(2,1)}, bf16[1024,512]{1,0:T(8,128)(2,1)S(1)}, u32[]{:S(2)}, u32[]{:S(2)}) collective-permute-start(bf16[1024,512]{1,0:T(8,128)(2,1)} %param.14), channel_id=1, source_target_pairs={{0,8},{9,1},{18,26},{27,19},{4,20},{13,29},{22,6},{31,15}} | collective-permute-start | bytes 3145736 | tf_op jit(solution)/shard_map/ppermute | solution.py:186
  13.2 18.8 %collective-permute-start.6 = (bf16[512,1024]{1,0:T(8,128)(2,1)}, bf16[512,1024]{1,0:T(8,128)(2,1)S(1)}, u32[]{:S(2)}, u32[]{:S(2)}) collective-permute-start(bf16[512,1024]{1,0:T(8,128)(2,1)} %get-tuple-element.34), channel_id=1, source_target_pairs={{0,4},{4,0},{8,12},{12,8},{16,20},{20,16},{24,28},{28,24},{1,5},{5... | collective-permute-start | bytes 3145736 | tf_op jit(solution)/shard_map/ppermute | solution.py:29
  20.7 12.3 %copy-start.6 = (bf16[1024,256]{1,0:T(8,128)(2,1)}, bf16[1024,256]{1,0:T(8,128)(2,1)S(1)}, u32[]{:S(2)}) copy-start(bf16[1024,256]{1,0:T(8,128)(2,1)S(1)} %get-tuple-element.44) | copy-start | bytes 1572868
  20.7 12.2 %collective-permute-start.5 = (bf16[1024,256]{1,0:T(8,128)(2,1)S(1)}, bf16[1024,256]{1,0:T(8,128)(2,1)S(1)}, u32[]{:S(2)}, u32[]{:S(2)}) collective-permute-start(bf16[1024,256]{1,0:T(8,128)(2,1)S(1)} %get-tuple-element.44), channel_id=1, source_target_pairs={{0,16},{9,25},{18,2},{27,11},{8,24},{1,17},{26,10},{19,3},{4,12},{... | collective-permute-start | bytes 1572872 | tf_op jit(solution)/shard_map/ppermute | solution.py:186
  22.0 16.9 %collective-permute-start.1 = (bf16[1024,256]{1,0:T(8,128)(2,1)S(1)}, bf16[1024,256]{1,0:T(8,128)(2,1)}, u32[]{:S(2)}, u32[]{:S(2)}) collective-permute-start(bf16[1024,256]{1,0:T(8,128)(2,1)S(1)} %get-tuple-element.45), channel_id=1, source_target_pairs={{0,16},{9,25},{18,2},{27,11},{8,24},{1,17},{26,10},{19,3},{4,12},{... | collective-permute-start | bytes 1572872 | tf_op jit(solution)/shard_map/ppermute | solution.py:186
  24.2 15.3 %collective-permute-start.2 = (bf16[144,512]{1,0:T(8,128)(2,1)}, bf16[144,512]{1,0:T(8,128)(2,1)S(1)}, u32[]{:S(2)}, u32[]{:S(2)}) collective-permute-start(bf16[144,512]{1,0:T(8,128)(2,1)} %get-tuple-element.28), channel_id=1, source_target_pairs={{0,1},{1,0},{2,3},{3,2},{4,5},{5,4},{6,7},{7,6},{8,9},{9,8},{10,11... | collective-permute-start | bytes 442376 | tf_op jit(solution)/shard_map/ppermute | solution.py:37
  26.6 12.9 %collective-permute-start.3 = (bf16[144,512]{1,0:T(8,128)(2,1)}, bf16[144,512]{1,0:T(8,128)(2,1)S(1)}, u32[]{:S(2)}, u32[]{:S(2)}) collective-permute-start(bf16[144,512]{1,0:T(8,128)(2,1)} %get-tuple-element.29), channel_id=1, source_target_pairs={{0,2},{1,3},{2,0},{3,1},{4,6},{5,7},{6,4},{7,5},{8,10},{9,11},{10,... | collective-permute-start | bytes 442376 | tf_op jit(solution)/shard_map/ppermute | solution.py:37
  26.6 12.3 %all-to-all-start = ((bf16[8,32,512]{2,1,0:T(8,128)(2,1)}), bf16[8,32,512]{2,1,0:T(8,128)(2,1)S(1)}, u32[]{:S(2)}, u32[]{:S(2)}) async-start(bf16[8,32,512]{2,1,0:T(8,128)(2,1)} %bitcast.9), calls=%async_computation | async-start | bytes 524288 | tf_op jit(solution)/shard_map/all_to_all | solution.py:254
  32.0 8.5 %copy-start.1 = (bf16[144,512]{1,0:T(8,128)(2,1)S(1)}, bf16[144,512]{1,0:T(8,128)(2,1)}, u32[]{:S(2)}) copy-start(bf16[144,512]{1,0:T(8,128)(2,1)} %get-tuple-element.27.refs_0_) | copy-start | bytes 442372
  32.0 8.5 %copy-start.2 = (s32[1,1,8]{2,1,0:T(1,128)S(1)}, s32[1,1,8]{2,1,0:T(1,128)}, u32[]{:S(2)}) copy-start(s32[1,1,8]{2,1,0:T(1,128)} %param.15) | copy-start | bytes 100
  32.0 8.5 %copy-start.3 = (s32[1,1,8]{2,1,0:T(1,128)S(1)}, s32[1,1,8]{2,1,0:T(1,128)}, u32[]{:S(2)}) copy-start(s32[1,1,8]{2,1,0:T(1,128)} %param.16) | copy-start | bytes 100
  32.0 8.5 %copy-start.4 = (f32[1,1,8]{2,1,0:T(1,128)S(1)}, f32[1,1,8]{2,1,0:T(1,128)}, u32[]{:S(2)}) copy-start(f32[1,1,8]{2,1,0:T(1,128)} %param.17) | copy-start | bytes 100
  32.1 8.5 %copy-start.5 = (f32[128]{0:T(128)S(1)}, f32[128]{0:T(128)}, u32[]{:S(2)}) copy-start(f32[128]{0:T(128)} %param.18) | copy-start | bytes 1540
  32.1 8.4 %collective-permute-start.4 = (bf16[144,512]{1,0:T(8,128)(2,1)}, bf16[144,512]{1,0:T(8,128)(2,1)S(1)}, u32[]{:S(2)}, u32[]{:S(2)}) collective-permute-start(bf16[144,512]{1,0:T(8,128)(2,1)} %get-tuple-element.30), channel_id=1, source_target_pairs={{0,3},{1,2},{2,1},{3,0},{4,7},{5,6},{6,5},{7,4},{8,11},{9,10},{10,... | collective-permute-start | bytes 442376 | tf_op jit(solution)/shard_map/ppermute | solution.py:37
  34.9 6.7 %copy-start = (bf16[512,1024]{1,0:T(8,128)(2,1)S(1)}, bf16[512,1024]{1,0:T(8,128)(2,1)}, u32[]{:S(2)}) copy-start(bf16[512,1024]{1,0:T(8,128)(2,1)} %get-tuple-element.33.kept_ref) | copy-start | bytes 3145732
  34.9 6.7 %collective-permute-start.7 = (bf16[512,256]{1,0:T(8,128)(2,1)}, bf16[512,256]{1,0:T(8,128)(2,1)}, u32[]{:S(2)}, u32[]{:S(2)}) collective-permute-start(bf16[512,256]{1,0:T(8,128)(2,1)} %convolution_convert_fusion.2), channel_id=1, source_target_pairs={{0,4},{4,0},{8,12},{12,8},{16,20},{20,16},{24,28},{28,24},{1,5},{5... | collective-permute-start | bytes 786440 | tf_op jit(solution)/shard_map/ppermute | solution.py:29
  39.4 6.4 %collective-permute-start.12 = (bf16[512,256]{1,0:T(8,128)(2,1)S(1)}, bf16[512,256]{1,0:T(8,128)(2,1)S(1)}, u32[]{:S(2)}, u32[]{:S(2)}) collective-permute-start(bf16[512,256]{1,0:T(8,128)(2,1)S(1)} %convolution_convert_fusion.1), channel_id=1, source_target_pairs={{0,4},{4,0},{8,12},{12,8},{16,20},{20,16},{24,28},{28,24},{1,5},{5... | collective-permute-start | bytes 786440 | tf_op jit(solution)/shard_map/ppermute | solution.py:29
  43.1 6.9 %collective-permute-start.8 = (bf16[256,256]{1,0:T(8,128)(2,1)S(1)}, bf16[256,256]{1,0:T(8,128)(2,1)S(1)}, u32[]{:S(2)}, u32[]{:S(2)}) collective-permute-start(bf16[256,256]{1,0:T(8,128)(2,1)S(1)} %slice.135), channel_id=1, source_target_pairs={{0,1},{1,0},{2,3},{3,2},{4,5},{5,4},{6,7},{7,6},{8,9},{9,8},{10,11... | collective-permute-start | bytes 393224 | tf_op jit(solution)/shard_map/ppermute | solution.py:37
  46.2 6.7 %collective-permute-start.13 = (bf16[256,256]{1,0:T(8,128)(2,1)S(1)}, bf16[256,256]{1,0:T(8,128)(2,1)S(1)}, u32[]{:S(2)}, u32[]{:S(2)}) collective-permute-start(bf16[256,256]{1,0:T(8,128)(2,1)S(1)} %slice.134), channel_id=1, source_target_pairs={{0,1},{1,0},{2,3},{3,2},{4,5},{5,4},{6,7},{7,6},{8,9},{9,8},{10,11... | collective-permute-start | bytes 393224 | tf_op jit(solution)/shard_map/ppermute | solution.py:37
  50.0 6.0 %collective-permute-start.9 = (bf16[128,256]{1,0:T(8,128)(2,1)S(1)}, bf16[128,256]{1,0:T(8,128)(2,1)S(1)}, u32[]{:S(2)}, u32[]{:S(2)}) collective-permute-start(bf16[128,256]{1,0:T(8,128)(2,1)S(1)} %slice.137), channel_id=1, source_target_pairs={{0,2},{1,3},{2,0},{3,1},{4,6},{5,7},{6,4},{7,5},{8,10},{9,11},{10,... | collective-permute-start | bytes 196616 | tf_op jit(solution)/shard_map/ppermute | solution.py:37
  53.0 5.8 %collective-permute-start.14 = (bf16[128,256]{1,0:T(8,128)(2,1)S(1)}, bf16[128,256]{1,0:T(8,128)(2,1)S(1)}, u32[]{:S(2)}, u32[]{:S(2)}) collective-permute-start(bf16[128,256]{1,0:T(8,128)(2,1)S(1)} %slice.136), channel_id=1, source_target_pairs={{0,2},{1,3},{2,0},{3,1},{4,6},{5,7},{6,4},{7,5},{8,10},{9,11},{10,... | collective-permute-start | bytes 196616 | tf_op jit(solution)/shard_map/ppermute | solution.py:37
  58.9 5.3 %collective-permute-start.18 = (bf16[128,256]{1,0:T(8,128)(2,1)S(1)}, bf16[128,256]{1,0:T(8,128)(2,1)S(1)}, u32[]{:S(2)}, u32[]{:S(2)}) collective-permute-start(bf16[128,256]{1,0:T(8,128)(2,1)S(1)} %get-tuple-element.51), channel_id=1, source_target_pairs={{0,2},{1,3},{2,0},{3,1},{4,6},{5,7},{6,4},{7,5},{8,10},{9,11},{10,... | collective-permute-start | bytes 196616 | tf_op jit(solution)/shard_map/ppermute | solution.py:37
  61.4 5.3 %collective-permute-start.10 = (bf16[128,256]{1,0:T(8,128)(2,1)S(1)}, bf16[128,256]{1,0:T(8,128)(2,1)S(1)}, u32[]{:S(2)}, u32[]{:S(2)}) collective-permute-start(bf16[128,256]{1,0:T(8,128)(2,1)S(1)} %get-tuple-element.49), channel_id=1, source_target_pairs={{0,2},{1,3},{2,0},{3,1},{4,6},{5,7},{6,4},{7,5},{8,10},{9,11},{10,... | collective-permute-start | bytes 196616 | tf_op jit(solution)/shard_map/ppermute | solution.py:37
  64.3 5.7 %collective-permute-start.19 = (bf16[256,256]{1,0:T(8,128)(2,1)S(1)}, bf16[256,256]{1,0:T(8,128)(2,1)S(1)}, u32[]{:S(2)}, u32[]{:S(2)}) collective-permute-start(bf16[256,256]{1,0:T(8,128)(2,1)S(1)} %pad_maximum_fusion.4), channel_id=1, source_target_pairs={{0,1},{1,0},{2,3},{3,2},{4,5},{5,4},{6,7},{7,6},{8,9},{9,8},{10,11... | collective-permute-start | bytes 393224 | tf_op jit(solution)/shard_map/ppermute | solution.py:37
  66.6 5.6 %collective-permute-start.11 = (bf16[256,256]{1,0:T(8,128)(2,1)S(1)}, bf16[256,256]{1,0:T(8,128)(2,1)S(1)}, u32[]{:S(2)}, u32[]{:S(2)}) collective-permute-start(bf16[256,256]{1,0:T(8,128)(2,1)S(1)} %pad_maximum_fusion.3), channel_id=1, source_target_pairs={{0,1},{1,0},{2,3},{3,2},{4,5},{5,4},{6,7},{7,6},{8,9},{9,8},{10,11... | collective-permute-start | bytes 393224 | tf_op jit(solution)/shard_map/ppermute | solution.py:37
  69.9 2.5 %collective-permute-start.20 = (bf16[512,256]{1,0:T(8,128)(2,1)S(1)}, bf16[512,256]{1,0:T(8,128)(2,1)S(1)}, u32[]{:S(2)}, u32[]{:S(2)}) collective-permute-start(bf16[512,256]{1,0:T(8,128)(2,1)S(1)} %pad_maximum_fusion.1.slope_ref), channel_id=1, source_target_pairs={{0,4},{4,0},{8,12},{12,8},{16,20},{20,16},{24,28},{28,24},{1,5},{5... | collective-permute-start | bytes 786440 | tf_op jit(solution)/shard_map/ppermute | solution.py:29
  72.3 5.0 %collective-permute-start.15 = (bf16[512,256]{1,0:T(8,128)(2,1)S(1)}, bf16[512,256]{1,0:T(8,128)(2,1)S(1)}, u32[]{:S(2)}, u32[]{:S(2)}) collective-permute-start(bf16[512,256]{1,0:T(8,128)(2,1)S(1)} %pad_maximum_fusion.slope_ref), channel_id=1, source_target_pairs={{0,4},{4,0},{8,12},{12,8},{16,20},{20,16},{24,28},{28,24},{1,5},{5... | collective-permute-start | bytes 786440 | tf_op jit(solution)/shard_map/ppermute | solution.py:29
  73.8 7.8 %collective-permute-start.21 = (bf16[512,256]{1,0:T(8,128)(2,1)S(1)}, bf16[512,256]{1,0:T(8,128)(2,1)S(1)}, u32[]{:S(2)}, u32[]{:S(2)}) collective-permute-start(bf16[512,256]{1,0:T(8,128)(2,1)S(1)} %get-tuple-element.43), channel_id=1, source_target_pairs={{0,8},{4,20},{8,0},{12,28},{16,24},{20,4},{24,16},{28,12},{1,9},{5... | collective-permute-start | bytes 786440 | tf_op jit(solution)/shard_map/ppermute | solution.py:363
  78.7 7.2 %collective-permute-start.16 = (bf16[512,256]{1,0:T(8,128)(2,1)S(1)}, bf16[512,256]{1,0:T(8,128)(2,1)S(1)}, u32[]{:S(2)}, u32[]{:S(2)}) collective-permute-start(bf16[512,256]{1,0:T(8,128)(2,1)S(1)} %get-tuple-element.41), channel_id=1, source_target_pairs={{0,8},{4,20},{8,0},{12,28},{16,24},{20,4},{24,16},{28,12},{1,9},{5... | collective-permute-start | bytes 786440 | tf_op jit(solution)/shard_map/ppermute | solution.py:363
  81.7 5.0 %collective-permute-start.22 = (bf16[256,256]{1,0:T(8,128)(2,1)S(1)}, bf16[256,256]{1,0:T(8,128)(2,1)S(1)}, u32[]{:S(2)}, u32[]{:S(2)}) collective-permute-start(bf16[256,256]{1,0:T(8,128)(2,1)S(1)} %slice.132), channel_id=1, source_target_pairs={{0,16},{4,12},{8,24},{12,4},{16,0},{20,28},{24,8},{28,20},{1,17},{... | collective-permute-start | bytes 393224 | tf_op jit(solution)/shard_map/ppermute | solution.py:363
  86.0 5.0 %collective-permute-start.17 = (bf16[256,256]{1,0:T(8,128)(2,1)S(1)}, bf16[256,256]{1,0:T(8,128)(2,1)S(1)}, u32[]{:S(2)}, u32[]{:S(2)}) collective-permute-start(bf16[256,256]{1,0:T(8,128)(2,1)S(1)} %slice.133), channel_id=1, source_target_pairs={{0,16},{4,12},{8,24},{12,4},{16,0},{20,28},{24,8},{28,20},{1,17},{... | collective-permute-start | bytes 393224 | tf_op jit(solution)/shard_map/ppermute | solution.py:363
  91.1 13.0 %collective-permute-start.23 = (bf16[256,512]{1,0:T(8,128)(2,1)S(1)}, bf16[256,512]{1,0:T(8,128)(2,1)S(1)}, u32[]{:S(2)}, u32[]{:S(2)}) collective-permute-start(bf16[256,512]{1,0:T(8,128)(2,1)S(1)} %pad_maximum_fusion.2), channel_id=1, source_target_pairs={{0,0},{1,10},{2,17},{3,27},{4,4},{5,14},{6,21},{7,31},{8,1},{9,11}... | collective-permute-start | bytes 786440 | tf_op jit(solution)/shard_map/ppermute | solution.py:374
  (4 other events, 7.1 us)

commit v10 on v9

--- a/solution.py
+++ b/solution.py
@@ -317,9 +317,6 @@
 
     sent = dot_rows(row_at, jnp.concatenate(values, axis=1).astype(BF16)).astype(BF16)
 
-    slopes[0], sent = lax.optimization_barrier((slopes[0], sent))
-    policy_values = lax.all_to_all(sent, "dp", split_axis=0, concat_axis=0, tiled=True)
-
     grad_kept, grad_sent = [], []
     for j in range(PARTS):
         slopes_got = swapped(slopes[j], dp_count)
@@ -351,6 +348,8 @@
         )(chunk_at, kept_rows, got_rows, slopes[j], slopes_got)
         grad_kept.append(chunks[0])
         grad_sent.append(chunks[1])
+    *grad_kept, sent = lax.optimization_barrier((*grad_kept, sent))
+    policy_values = lax.all_to_all(sent, "dp", split_axis=0, concat_axis=0, tiled=True)
     grads = []
     for j in range(PARTS):
         total, given = grad_kept[j], grad_sent[j]

time: 106 us -> 108 us (1.019)
  waiting for transfers between devices: 33.3 us -> 36.6 us
  matrix products: 3.7 us -> 2.04 us
    ppermute x11, waiting for transfers between devices: 12.8 us -> 21.1 us  [crossed(): return lax.ppermute(array, 'tensor', [(i, i ^ step) for i in range(count)])]
    ppermute x4, waiting for transfers between devices: 11.9 us -> 9 us  [on_device(): total = total + lax.ppermute(given, 'dp', pairs).astype(F32)]
    all_to_all x1, waiting for transfers between devices: 3.82 us -> 1.63 us  [on_device(): got_cot = lax.all_to_all(cot, 'dp', split_axis=0, concat_axis=0, tiled=True)]
    all_to_all x1, starting transfers between devices: 5.38 us -> 3.65 us  [on_device(): got_cot = lax.all_to_all(cot, 'dp', split_axis=0, concat_axis=0, tiled=True)]
    dot_general x4, matrix products: 3.46 us -> 1.8 us  [dot(): return jnp.dot(a, b, preferred_element_type=F32)]
    unnamed x23 -> x29, local copies, waits for them, and re-layouts: 2.52 us -> 1.74 us
  transfers between devices with their start and end apart: 25 -> 25, of which waited for: 13 -> 14; matrix products, arithmetic and copies ran while one was open for 6% -> 4% of each run, Pallas kernels for 10% -> 10%
where the time goes in v10:
time: 108 us
  starting transfers between devices  38.5 us (36%)
  waiting for transfers between devices  36.6 us (34%)
  blocking collectives  13.2 us (12%)
  Pallas kernels  10.8 us (10%)
  other arithmetic  3.55 us (3%)
  matrix products  2.04 us (2%)
  local copies, waits for them, and re-layouts  1.93 us (2%)
  between operations  1.1 us (1%)
    ppermute x11, waiting for transfers between devices, crossed(): return lax.ppermute(array, 'tensor', [(i, i ^ step) for i in range(count)])  21.1 us
    ppermute x11, starting transfers between devices, crossed(): return lax.ppermute(array, 'tensor', [(i, i ^ step) for i in range(count)])  20.4 us
    all_to_all x1, blocking collectives, on_device(): lax.all_to_all(sent, 'dp', split_axis=0, concat_axis=0, tiled=True)  13.2 us
    ppermute x4, waiting for transfers between devices, on_device(): total = total + lax.ppermute(given, 'dp', pairs).astype(F32)  9 us
    ppermute x3, starting transfers between devices, stage(): return (lax.ppermute(held, AXES, pairs), is_getter)  8.33 us
    pallas_call x1, Pallas kernels, on_device(): pl.pallas_call(functools.partial(prepare_kernel, tensor_count, steps), gr...  6.96 us
    ppermute x3, waiting for transfers between devices, stage(): return (lax.ppermute(held, AXES, pairs), is_getter)  4.86 us
    ppermute x4, starting transfers between devices, on_device(): total = total + lax.ppermute(given, 'dp', pairs).astype(F32)  4.66 us
  transfers between devices with their start and end apart: 25, of which 14 were waited for; matrix products, arithmetic and copies ran while one was open for 4% of the time, Pallas kernels for 10%

profile of v10, /device:TPU:0, one launch (start us, length us, event | category | flops | bytes accessed | tf_op | source)
XLA Modules:
  0.0 107.7 jit_solution(9615442282984587628)
XLA Ops:
  0.6 4.9 %collective-permute-start = (bf16[1024,512]{1,0:T(8,128)(2,1)}, bf16[1024,512]{1,0:T(8,128)(2,1)S(1)}, u32[]{:S(2)}, u32[]{:S(2)}) collective-permute-start(bf16[1024,512]{1,0:T(8,128)(2,1)} %param.14), channel_id=1, source_target_pairs={{0,8},{9,1},{18,26},{27,19},{4,20},{13,29},{22,6},{31,15}} | collective-permute-start | bytes 3145736 | tf_op jit(solution)/shard_map/ppermute | solution.py:186
  6.2 7.0 %prepare.1 = (bf16[512,1024]{1,0:T(8,128)(2,1)}, bf16[512,1024]{1,0:T(8,128)(2,1)}, bf16[144,512]{1,0:T(8,128)(2,1)}, bf16[144,512]{1,0:T(8,128)(2,1)}, bf16[144...) custom-call(s32[2]{0:T(128)} %pad_add_fusion.1.at, bf16[512,2048]{1,0:T(8,128)(2,1)} %x_ref.1, f32[1,2048]{1,0:T(1,128)} %bitcast.30, ...), custom_call_target="tpu_custom_call" | custom-call | flops 1073741824 | bytes 8388608 | tf_op jit(solution)/shard_map/prepare/pallas_call | solution.py:198
  13.2 4.9 %collective-permute-done = bf16[1024,512]{1,0:T(8,128)(2,1)S(1)} collective-permute-done((bf16[1024,512]{1,0:T(8,128)(2,1)}, bf16[1024,512]{1,0:T(8,128)(2,1)S(1)}, u32[]{:S(2)}, u32[]{:S(2)}) %collective-permute-start) | collective-permute-done | bytes 1048608 | tf_op jit(solution)/shard_map/ppermute | solution.py:186
  19.1 1.6 %slice_select_fusion = (bf16[1024,256]{1,0:T(8,128)(2,1)S(1)}, bf16[1024,256]{1,0:T(8,128)(2,1)S(1)}) fusion(bf16[1024,512]{1,0:T(8,128)(2,1)} %param.14, bf16[1024,512]{1,0:T(8,128)(2,1)} %copy-done.10, pred[]{:T(512)S(6)} %or.15), kind=kLoop, calls=%fused_computation.7 | loop fusion | flops 524288 | bytes 3145729 | tf_op jit(solution)/shard_map/jit(_where)/select_n | solution.py:248
  20.7 1.3 %collective-permute-start.2 = (bf16[1024,256]{1,0:T(8,128)(2,1)S(1)}, bf16[1024,256]{1,0:T(8,128)(2,1)S(1)}, u32[]{:S(2)}, u32[]{:S(2)}) collective-permute-start(bf16[1024,256]{1,0:T(8,128)(2,1)S(1)} %get-tuple-element.47), channel_id=1, source_target_pairs={{0,16},{9,25},{18,2},{27,11},{8,24},{1,17},{26,10},{19,3},{4,12},{... | collective-permute-start | bytes 1572872 | tf_op jit(solution)/shard_map/ppermute | solution.py:186
  22.1 2.1 %collective-permute-start.6 = (bf16[1024,256]{1,0:T(8,128)(2,1)S(1)}, bf16[1024,256]{1,0:T(8,128)(2,1)}, u32[]{:S(2)}, u32[]{:S(2)}) collective-permute-start(bf16[1024,256]{1,0:T(8,128)(2,1)S(1)} %get-tuple-element.46), channel_id=1, source_target_pairs={{0,16},{9,25},{18,2},{27,11},{8,24},{1,17},{26,10},{19,3},{4,12},{... | collective-permute-start | bytes 1572872 | tf_op jit(solution)/shard_map/ppermute | solution.py:186
  24.2 3.7 %all-to-all-start = ((bf16[8,32,512]{2,1,0:T(8,128)(2,1)}), bf16[8,32,512]{2,1,0:T(8,128)(2,1)S(1)}, u32[]{:S(2)}, u32[]{:S(2)}) async-start(bf16[8,32,512]{2,1,0:T(8,128)(2,1)} %bitcast.13), calls=%async_computation | async-start | bytes 524288 | tf_op jit(solution)/shard_map/all_to_all | solution.py:254
  27.8 2.3 %collective-permute-start.3 = (bf16[144,512]{1,0:T(8,128)(2,1)}, bf16[144,512]{1,0:T(8,128)(2,1)S(1)}, u32[]{:S(2)}, u32[]{:S(2)}) collective-permute-start(bf16[144,512]{1,0:T(8,128)(2,1)} %get-tuple-element.31), channel_id=1, source_target_pairs={{0,1},{1,0},{2,3},{3,2},{4,5},{5,4},{6,7},{7,6},{8,9},{9,8},{10,11... | collective-permute-start | bytes 442376 | tf_op jit(solution)/shard_map/ppermute | solution.py:37
  30.1 1.9 %collective-permute-start.4 = (bf16[144,512]{1,0:T(8,128)(2,1)}, bf16[144,512]{1,0:T(8,128)(2,1)S(1)}, u32[]{:S(2)}, u32[]{:S(2)}) collective-permute-start(bf16[144,512]{1,0:T(8,128)(2,1)} %get-tuple-element.32), channel_id=1, source_target_pairs={{0,2},{1,3},{2,0},{3,1},{4,6},{5,7},{6,4},{7,5},{8,10},{9,11},{10,... | collective-permute-start | bytes 442376 | tf_op jit(solution)/shard_map/ppermute | solution.py:37
  32.0 3.6 %collective-permute-start.5 = (bf16[144,512]{1,0:T(8,128)(2,1)S(1)}, bf16[144,512]{1,0:T(8,128)(2,1)S(1)}, u32[]{:S(2)}, u32[]{:S(2)}) collective-permute-start(bf16[144,512]{1,0:T(8,128)(2,1)S(1)} %copy-done.13), channel_id=1, source_target_pairs={{0,3},{1,2},{2,1},{3,0},{4,7},{5,6},{6,5},{7,4},{8,11},{9,10},{10,... | collective-permute-start | bytes 442376 | tf_op jit(solution)/shard_map/ppermute | solution.py:37
  35.6 1.6 %all-to-all-done = bf16[8,32,512]{2,1,0:T(8,128)(2,1)S(1)} async-done(((bf16[8,32,512]{2,1,0:T(8,128)(2,1)}), bf16[8,32,512]{2,1,0:T(8,128)(2,1)S(1)}, u32[]{:S(2)}, u32[]{:S(2)}) %all-to-all-start) | async-done | bytes 262176 | tf_op jit(solution)/shard_map/all_to_all | solution.py:254
  38.9 5.4 %collective-permute-done.4.refs_2_ = bf16[144,512]{1,0:T(8,128)(2,1)S(1)} collective-permute-done((bf16[144,512]{1,0:T(8,128)(2,1)}, bf16[144,512]{1,0:T(8,128)(2,1)S(1)}, u32[]{:S(2)}, u32[]{:S(2)}) %collective-permute-start.4) | collective-permute-done | bytes 147488 | tf_op jit(solution)/shard_map/ppermute | solution.py:37
  45.9 2.9 %collective-permute-start.14 = (bf16[256,256]{1,0:T(8,128)(2,1)S(1)}, bf16[256,256]{1,0:T(8,128)(2,1)S(1)}, u32[]{:S(2)}, u32[]{:S(2)}) collective-permute-start(bf16[256,256]{1,0:T(8,128)(2,1)S(1)} %slice.134), channel_id=1, source_target_pairs={{0,1},{1,0},{2,3},{3,2},{4,5},{5,4},{6,7},{7,6},{8,9},{9,8},{10,11... | collective-permute-start | bytes 393224 | tf_op jit(solution)/shard_map/ppermute | solution.py:37
  49.4 3.3 %collective-permute-done.14 = bf16[256,256]{1,0:T(8,128)(2,1)S(1)} collective-permute-done((bf16[256,256]{1,0:T(8,128)(2,1)S(1)}, bf16[256,256]{1,0:T(8,128)(2,1)S(1)}, u32[]{:S(2)}, u32[]{:S(2)}) %collective-permute-start.14) | collective-permute-done | bytes 131104 | tf_op jit(solution)/shard_map/ppermute | solution.py:37
  52.7 3.9 %collective-permute-start.15 = (bf16[128,256]{1,0:T(8,128)(2,1)S(1)}, bf16[128,256]{1,0:T(8,128)(2,1)S(1)}, u32[]{:S(2)}, u32[]{:S(2)}) collective-permute-start(bf16[128,256]{1,0:T(8,128)(2,1)S(1)} %slice.136), channel_id=1, source_target_pairs={{0,2},{1,3},{2,0},{3,1},{4,6},{5,7},{6,4},{7,5},{8,10},{9,11},{10,... | collective-permute-start | bytes 196616 | tf_op jit(solution)/shard_map/ppermute | solution.py:37
  56.7 2.1 %collective-permute-start.9 = (bf16[128,256]{1,0:T(8,128)(2,1)S(1)}, bf16[128,256]{1,0:T(8,128)(2,1)S(1)}, u32[]{:S(2)}, u32[]{:S(2)}) collective-permute-start(bf16[128,256]{1,0:T(8,128)(2,1)S(1)} %slice.137), channel_id=1, source_target_pairs={{0,2},{1,3},{2,0},{3,1},{4,6},{5,7},{6,4},{7,5},{8,10},{9,11},{10,... | collective-permute-start | bytes 196616 | tf_op jit(solution)/shard_map/ppermute | solution.py:37
  58.9 1.6 %collective-permute-done.15 = bf16[128,256]{1,0:T(8,128)(2,1)S(1)} collective-permute-done((bf16[128,256]{1,0:T(8,128)(2,1)S(1)}, bf16[128,256]{1,0:T(8,128)(2,1)S(1)}, u32[]{:S(2)}, u32[]{:S(2)}) %collective-permute-start.15) | collective-permute-done | bytes 65568 | tf_op jit(solution)/shard_map/ppermute | solution.py:37
  60.5 1.7 %collective-permute-done.9 = bf16[128,256]{1,0:T(8,128)(2,1)S(1)} collective-permute-done((bf16[128,256]{1,0:T(8,128)(2,1)S(1)}, bf16[128,256]{1,0:T(8,128)(2,1)S(1)}, u32[]{:S(2)}, u32[]{:S(2)}) %collective-permute-start.9) | collective-permute-done | bytes 65568 | tf_op jit(solution)/shard_map/ppermute | solution.py:37
  62.3 1.9 %collective-permute-start.16 = (bf16[128,256]{1,0:T(8,128)(2,1)S(1)}, bf16[128,256]{1,0:T(8,128)(2,1)S(1)}, u32[]{:S(2)}, u32[]{:S(2)}) collective-permute-start(bf16[128,256]{1,0:T(8,128)(2,1)S(1)} %get-tuple-element.51), channel_id=1, source_target_pairs={{0,2},{1,3},{2,0},{3,1},{4,6},{5,7},{6,4},{7,5},{8,10},{9,11},{10,... | collective-permute-start | bytes 196616 | tf_op jit(solution)/shard_map/ppermute | solution.py:37
  64.2 1.1 collective-permute-start.10
  65.2 2.3 %collective-permute-done.16 = bf16[128,256]{1,0:T(8,128)(2,1)S(1)} collective-permute-done((bf16[128,256]{1,0:T(8,128)(2,1)S(1)}, bf16[128,256]{1,0:T(8,128)(2,1)S(1)}, u32[]{:S(2)}, u32[]{:S(2)}) %collective-permute-start.16) | collective-permute-done | bytes 65568 | tf_op jit(solution)/shard_map/ppermute | solution.py:37
  67.6 2.4 %collective-permute-done.10 = bf16[128,256]{1,0:T(8,128)(2,1)S(1)} collective-permute-done((bf16[128,256]{1,0:T(8,128)(2,1)S(1)}, bf16[128,256]{1,0:T(8,128)(2,1)S(1)}, u32[]{:S(2)}, u32[]{:S(2)}) %collective-permute-start.10) | collective-permute-done | bytes 65568 | tf_op jit(solution)/shard_map/ppermute | solution.py:37
  70.6 2.0 %collective-permute-done.17 = bf16[256,256]{1,0:T(8,128)(2,1)S(1)} collective-permute-done((bf16[256,256]{1,0:T(8,128)(2,1)S(1)}, bf16[256,256]{1,0:T(8,128)(2,1)S(1)}, u32[]{:S(2)}, u32[]{:S(2)}) %collective-permute-start.17) | collective-permute-done | bytes 131104 | tf_op jit(solution)/shard_map/ppermute | solution.py:37
  72.7 2.4 %collective-permute-done.11 = bf16[256,256]{1,0:T(8,128)(2,1)S(1)} collective-permute-done((bf16[256,256]{1,0:T(8,128)(2,1)S(1)}, bf16[256,256]{1,0:T(8,128)(2,1)S(1)}, u32[]{:S(2)}, u32[]{:S(2)}) %collective-permute-start.11) | collective-permute-done | bytes 131104 | tf_op jit(solution)/shard_map/ppermute | solution.py:37
  75.3 1.4 %gradient.3 = (f32[512,256]{1,0:T(8,128)S(1)}, bf16[512,256]{1,0:T(8,128)(2,1)S(1)}) custom-call(s32[4]{0:T(128)S(1)} %pad_add_fusion.at, bf16[512,1024]{1,0:T(8,128)(2,1)S(1)} %copy-done, bf16[512,1024]{1,0:T(8,128)(2,1)S(1)} %collective-permute-done.1.got_ref, bf16[512,256]{1,0:T(8,128)(2,1)S(1)} %pad_maximum_fusion.1.slope_ref, ...), custom_call_target="tpu_custom_call" | custom-call | flops 536870912 | bytes 4194304 | tf_op jit(solution)/shard_map/gradient/pallas_call | solution.py:323
  76.7 1.8 %collective-permute-start.21 = (bf16[512,256]{1,0:T(8,128)(2,1)S(1)}, bf16[512,256]{1,0:T(8,128)(2,1)S(1)}, u32[]{:S(2)}, u32[]{:S(2)}) collective-permute-start(bf16[512,256]{1,0:T(8,128)(2,1)S(1)} %get-tuple-element.45), channel_id=1, source_target_pairs={{0,8},{4,20},{8,0},{12,28},{16,24},{20,4},{24,16},{28,12},{1,9},{5... | collective-permute-start | bytes 786440 | tf_op jit(solution)/shard_map/ppermute | solution.py:362
  78.5 1.4 %gradient.2 = (f32[512,256]{1,0:T(8,128)S(1)}, bf16[512,256]{1,0:T(8,128)(2,1)S(1)}) custom-call(s32[4]{0:T(128)S(1)} %pad_add_fusion.at, bf16[512,1024]{1,0:T(8,128)(2,1)S(1)} %copy-done, bf16[512,1024]{1,0:T(8,128)(2,1)S(1)} %collective-permute-done.1.got_ref, bf16[512,256]{1,0:T(8,128)(2,1)S(1)} %pad_maximum_fusion.slope_ref, ...), custom_call_target="tpu_custom_call" | custom-call | flops 536870912 | bytes 4194304 | tf_op jit(solution)/shard_map/gradient/pallas_call | solution.py:323
  80.5 2.6 %collective-permute-done.21 = bf16[512,256]{1,0:T(8,128)(2,1)S(1)} collective-permute-done((bf16[512,256]{1,0:T(8,128)(2,1)S(1)}, bf16[512,256]{1,0:T(8,128)(2,1)S(1)}, u32[]{:S(2)}, u32[]{:S(2)}) %collective-permute-start.21) | collective-permute-done | bytes 262176 | tf_op jit(solution)/shard_map/ppermute | solution.py:362
  83.2 1.6 %collective-permute-start.22 = (bf16[256,256]{1,0:T(8,128)(2,1)S(1)}, bf16[256,256]{1,0:T(8,128)(2,1)S(1)}, u32[]{:S(2)}, u32[]{:S(2)}) collective-permute-start(bf16[256,256]{1,0:T(8,128)(2,1)S(1)} %slice.132), channel_id=1, source_target_pairs={{0,16},{4,12},{8,24},{12,4},{16,0},{20,28},{24,8},{28,20},{1,17},{... | collective-permute-start | bytes 393224 | tf_op jit(solution)/shard_map/ppermute | solution.py:362
  84.8 2.3 %collective-permute-done.19 = bf16[512,256]{1,0:T(8,128)(2,1)S(1)} collective-permute-done((bf16[512,256]{1,0:T(8,128)(2,1)S(1)}, bf16[512,256]{1,0:T(8,128)(2,1)S(1)}, u32[]{:S(2)}, u32[]{:S(2)}) %collective-permute-start.19) | collective-permute-done | bytes 262176 | tf_op jit(solution)/shard_map/ppermute | solution.py:362
  88.3 3.9 %collective-permute-done.20 = bf16[256,256]{1,0:T(8,128)(2,1)S(1)} collective-permute-done((bf16[256,256]{1,0:T(8,128)(2,1)S(1)}, bf16[256,256]{1,0:T(8,128)(2,1)S(1)}, u32[]{:S(2)}, u32[]{:S(2)}) %collective-permute-start.20) | collective-permute-done | bytes 131104 | tf_op jit(solution)/shard_map/ppermute | solution.py:362
  93.0 13.2 %all_to_all.21 = bf16[8,32,512]{2,1,0:T(8,128)(2,1)S(1)} all-to-all(bf16[8,32,512]{2,1,0:T(8,128)(2,1)S(1)} %bitcast.27), channel_id=1, replica_groups=mesh['dp'=8,'tensor'=4] {'dp'}, dimensions={0} | all-to-all | bytes 524288 | tf_op jit(solution)/shard_map/all_to_all | solution.py:352
  (80 shorter events, 10.7 us)
Async XLA Ops:
  0.6 17.5 %collective-permute-start = (bf16[1024,512]{1,0:T(8,128)(2,1)}, bf16[1024,512]{1,0:T(8,128)(2,1)S(1)}, u32[]{:S(2)}, u32[]{:S(2)}) collective-permute-start(bf16[1024,512]{1,0:T(8,128)(2,1)} %param.14), channel_id=1, source_target_pairs={{0,8},{9,1},{18,26},{27,19},{4,20},{13,29},{22,6},{31,15}} | collective-permute-start | bytes 3145736 | tf_op jit(solution)/shard_map/ppermute | solution.py:186
  13.1 18.9 %copy-start.13 = (bf16[144,512]{1,0:T(8,128)(2,1)S(1)}, bf16[144,512]{1,0:T(8,128)(2,1)}, u32[]{:S(2)}) copy-start(bf16[144,512]{1,0:T(8,128)(2,1)} %get-tuple-element.33) | copy-start | bytes 442372
  13.1 24.1 %collective-permute-start.1 = (bf16[512,1024]{1,0:T(8,128)(2,1)}, bf16[512,1024]{1,0:T(8,128)(2,1)S(1)}, u32[]{:S(2)}, u32[]{:S(2)}) collective-permute-start(bf16[512,1024]{1,0:T(8,128)(2,1)} %get-tuple-element.26), channel_id=1, source_target_pairs={{0,4},{4,0},{8,12},{12,8},{16,20},{20,16},{24,28},{28,24},{1,5},{5... | collective-permute-start | bytes 3145736 | tf_op jit(solution)/shard_map/ppermute | solution.py:29
  20.7 16.6 %copy-start.8 = (bf16[1024,256]{1,0:T(8,128)(2,1)}, bf16[1024,256]{1,0:T(8,128)(2,1)S(1)}, u32[]{:S(2)}) copy-start(bf16[1024,256]{1,0:T(8,128)(2,1)S(1)} %get-tuple-element.47) | copy-start | bytes 1572868
  20.7 17.6 %copy-start.6 = (bf16[1024,256]{1,0:T(8,128)(2,1)}, bf16[1024,256]{1,0:T(8,128)(2,1)S(1)}, u32[]{:S(2)}) copy-start(bf16[1024,256]{1,0:T(8,128)(2,1)S(1)} %get-tuple-element.46) | copy-start | bytes 1572868
  20.7 11.3 %collective-permute-start.2 = (bf16[1024,256]{1,0:T(8,128)(2,1)S(1)}, bf16[1024,256]{1,0:T(8,128)(2,1)S(1)}, u32[]{:S(2)}, u32[]{:S(2)}) collective-permute-start(bf16[1024,256]{1,0:T(8,128)(2,1)S(1)} %get-tuple-element.47), channel_id=1, source_target_pairs={{0,16},{9,25},{18,2},{27,11},{8,24},{1,17},{26,10},{19,3},{4,12},{... | collective-permute-start | bytes 1572872 | tf_op jit(solution)/shard_map/ppermute | solution.py:186
  22.1 15.8 %collective-permute-start.6 = (bf16[1024,256]{1,0:T(8,128)(2,1)S(1)}, bf16[1024,256]{1,0:T(8,128)(2,1)}, u32[]{:S(2)}, u32[]{:S(2)}) collective-permute-start(bf16[1024,256]{1,0:T(8,128)(2,1)S(1)} %get-tuple-element.46), channel_id=1, source_target_pairs={{0,16},{9,25},{18,2},{27,11},{8,24},{1,17},{26,10},{19,3},{4,12},{... | collective-permute-start | bytes 1572872 | tf_op jit(solution)/shard_map/ppermute | solution.py:186
  24.2 13.1 %all-to-all-start = ((bf16[8,32,512]{2,1,0:T(8,128)(2,1)}), bf16[8,32,512]{2,1,0:T(8,128)(2,1)S(1)}, u32[]{:S(2)}, u32[]{:S(2)}) async-start(bf16[8,32,512]{2,1,0:T(8,128)(2,1)} %bitcast.13), calls=%async_computation | async-start | bytes 524288 | tf_op jit(solution)/shard_map/all_to_all | solution.py:254
  27.8 11.1 %collective-permute-start.3 = (bf16[144,512]{1,0:T(8,128)(2,1)}, bf16[144,512]{1,0:T(8,128)(2,1)S(1)}, u32[]{:S(2)}, u32[]{:S(2)}) collective-permute-start(bf16[144,512]{1,0:T(8,128)(2,1)} %get-tuple-element.31), channel_id=1, source_target_pairs={{0,1},{1,0},{2,3},{3,2},{4,5},{5,4},{6,7},{7,6},{8,9},{9,8},{10,11... | collective-permute-start | bytes 442376 | tf_op jit(solution)/shard_map/ppermute | solution.py:37
  30.1 14.2 %collective-permute-start.4 = (bf16[144,512]{1,0:T(8,128)(2,1)}, bf16[144,512]{1,0:T(8,128)(2,1)S(1)}, u32[]{:S(2)}, u32[]{:S(2)}) collective-permute-start(bf16[144,512]{1,0:T(8,128)(2,1)} %get-tuple-element.32), channel_id=1, source_target_pairs={{0,2},{1,3},{2,0},{3,1},{4,6},{5,7},{6,4},{7,5},{8,10},{9,11},{10,... | collective-permute-start | bytes 442376 | tf_op jit(solution)/shard_map/ppermute | solution.py:37
  32.0 12.3 %collective-permute-start.5 = (bf16[144,512]{1,0:T(8,128)(2,1)S(1)}, bf16[144,512]{1,0:T(8,128)(2,1)S(1)}, u32[]{:S(2)}, u32[]{:S(2)}) collective-permute-start(bf16[144,512]{1,0:T(8,128)(2,1)S(1)} %copy-done.13), channel_id=1, source_target_pairs={{0,3},{1,2},{2,1},{3,0},{4,7},{5,6},{6,5},{7,4},{8,11},{9,10},{10,... | collective-permute-start | bytes 442376 | tf_op jit(solution)/shard_map/ppermute | solution.py:37
  37.7 7.7 %copy-start = (bf16[512,1024]{1,0:T(8,128)(2,1)S(1)}, bf16[512,1024]{1,0:T(8,128)(2,1)}, u32[]{:S(2)}) copy-start(bf16[512,1024]{1,0:T(8,128)(2,1)} %get-tuple-element.25.kept_ref) | copy-start | bytes 3145732
  37.7 7.7 %copy-start.9 = (bf16[1024,256]{1,0:T(8,128)(2,1)S(1)}, bf16[1024,256]{1,0:T(8,128)(2,1)}, u32[]{:S(2)}) copy-start(bf16[1024,256]{1,0:T(8,128)(2,1)} %copy-done.8) | copy-start | bytes 1572868
  37.8 7.7 %copy-start.12 = (bf16[1024,256]{1,0:T(8,128)(2,1)S(1)}, bf16[1024,256]{1,0:T(8,128)(2,1)}, u32[]{:S(2)}) copy-start(bf16[1024,256]{1,0:T(8,128)(2,1)} %copy-done.11) | copy-start | bytes 1572868
  37.8 7.6 %collective-permute-start.13 = (bf16[512,256]{1,0:T(8,128)(2,1)S(1)}, bf16[512,256]{1,0:T(8,128)(2,1)S(1)}, u32[]{:S(2)}, u32[]{:S(2)}) collective-permute-start(bf16[512,256]{1,0:T(8,128)(2,1)S(1)} %convolution_convert_fusion.1), channel_id=1, source_target_pairs={{0,4},{4,0},{8,12},{12,8},{16,20},{20,16},{24,28},{28,24},{1,5},{5... | collective-permute-start | bytes 786440 | tf_op jit(solution)/shard_map/ppermute | solution.py:29
  38.3 10.5 %collective-permute-start.7 = (bf16[512,256]{1,0:T(8,128)(2,1)S(1)}, bf16[512,256]{1,0:T(8,128)(2,1)S(1)}, u32[]{:S(2)}, u32[]{:S(2)}) collective-permute-start(bf16[512,256]{1,0:T(8,128)(2,1)S(1)} %convolution_convert_fusion.2), channel_id=1, source_target_pairs={{0,4},{4,0},{8,12},{12,8},{16,20},{20,16},{24,28},{28,24},{1,5},{5... | collective-permute-start | bytes 786440 | tf_op jit(solution)/shard_map/ppermute | solution.py:29
  38.9 9.9 %copy-start.7 = (bf16[1024,256]{1,0:T(8,128)(2,1)S(1)}, bf16[1024,256]{1,0:T(8,128)(2,1)}, u32[]{:S(2)}) copy-start(bf16[1024,256]{1,0:T(8,128)(2,1)} %copy-done.6) | copy-start | bytes 1572868
  45.9 6.8 %collective-permute-start.14 = (bf16[256,256]{1,0:T(8,128)(2,1)S(1)}, bf16[256,256]{1,0:T(8,128)(2,1)S(1)}, u32[]{:S(2)}, u32[]{:S(2)}) collective-permute-start(bf16[256,256]{1,0:T(8,128)(2,1)S(1)} %slice.134), channel_id=1, source_target_pairs={{0,1},{1,0},{2,3},{3,2},{4,5},{5,4},{6,7},{7,6},{8,9},{9,8},{10,11... | collective-permute-start | bytes 393224 | tf_op jit(solution)/shard_map/ppermute | solution.py:37
  49.3 7.3 %collective-permute-start.8 = (bf16[256,256]{1,0:T(8,128)(2,1)S(1)}, bf16[256,256]{1,0:T(8,128)(2,1)S(1)}, u32[]{:S(2)}, u32[]{:S(2)}) collective-permute-start(bf16[256,256]{1,0:T(8,128)(2,1)S(1)} %slice.135), channel_id=1, source_target_pairs={{0,1},{1,0},{2,3},{3,2},{4,5},{5,4},{6,7},{7,6},{8,9},{9,8},{10,11... | collective-permute-start | bytes 393224 | tf_op jit(solution)/shard_map/ppermute | solution.py:37
  52.7 7.7 %collective-permute-start.15 = (bf16[128,256]{1,0:T(8,128)(2,1)S(1)}, bf16[128,256]{1,0:T(8,128)(2,1)S(1)}, u32[]{:S(2)}, u32[]{:S(2)}) collective-permute-start(bf16[128,256]{1,0:T(8,128)(2,1)S(1)} %slice.136), channel_id=1, source_target_pairs={{0,2},{1,3},{2,0},{3,1},{4,6},{5,7},{6,4},{7,5},{8,10},{9,11},{10,... | collective-permute-start | bytes 196616 | tf_op jit(solution)/shard_map/ppermute | solution.py:37
  56.7 5.5 %collective-permute-start.9 = (bf16[128,256]{1,0:T(8,128)(2,1)S(1)}, bf16[128,256]{1,0:T(8,128)(2,1)S(1)}, u32[]{:S(2)}, u32[]{:S(2)}) collective-permute-start(bf16[128,256]{1,0:T(8,128)(2,1)S(1)} %slice.137), channel_id=1, source_target_pairs={{0,2},{1,3},{2,0},{3,1},{4,6},{5,7},{6,4},{7,5},{8,10},{9,11},{10,... | collective-permute-start | bytes 196616 | tf_op jit(solution)/shard_map/ppermute | solution.py:37
  62.3 5.3 %collective-permute-start.16 = (bf16[128,256]{1,0:T(8,128)(2,1)S(1)}, bf16[128,256]{1,0:T(8,128)(2,1)S(1)}, u32[]{:S(2)}, u32[]{:S(2)}) collective-permute-start(bf16[128,256]{1,0:T(8,128)(2,1)S(1)} %get-tuple-element.51), channel_id=1, source_target_pairs={{0,2},{1,3},{2,0},{3,1},{4,6},{5,7},{6,4},{7,5},{8,10},{9,11},{10,... | collective-permute-start | bytes 196616 | tf_op jit(solution)/shard_map/ppermute | solution.py:37
  64.2 5.9 %collective-permute-start.10 = (bf16[128,256]{1,0:T(8,128)(2,1)S(1)}, bf16[128,256]{1,0:T(8,128)(2,1)S(1)}, u32[]{:S(2)}, u32[]{:S(2)}) collective-permute-start(bf16[128,256]{1,0:T(8,128)(2,1)S(1)} %get-tuple-element.52), channel_id=1, source_target_pairs={{0,2},{1,3},{2,0},{3,1},{4,6},{5,7},{6,4},{7,5},{8,10},{9,11},{10,... | collective-permute-start | bytes 196616 | tf_op jit(solution)/shard_map/ppermute | solution.py:37
  67.5 5.1 %collective-permute-start.17 = (bf16[256,256]{1,0:T(8,128)(2,1)S(1)}, bf16[256,256]{1,0:T(8,128)(2,1)S(1)}, u32[]{:S(2)}, u32[]{:S(2)}) collective-permute-start(bf16[256,256]{1,0:T(8,128)(2,1)S(1)} %pad_maximum_fusion.4), channel_id=1, source_target_pairs={{0,1},{1,0},{2,3},{3,2},{4,5},{5,4},{6,7},{7,6},{8,9},{9,8},{10,11... | collective-permute-start | bytes 393224 | tf_op jit(solution)/shard_map/ppermute | solution.py:37
  70.1 5.0 %collective-permute-start.11 = (bf16[256,256]{1,0:T(8,128)(2,1)S(1)}, bf16[256,256]{1,0:T(8,128)(2,1)S(1)}, u32[]{:S(2)}, u32[]{:S(2)}) collective-permute-start(bf16[256,256]{1,0:T(8,128)(2,1)S(1)} %pad_maximum_fusion.3), channel_id=1, source_target_pairs={{0,1},{1,0},{2,3},{3,2},{4,5},{5,4},{6,7},{7,6},{8,9},{9,8},{10,11... | collective-permute-start | bytes 393224 | tf_op jit(solution)/shard_map/ppermute | solution.py:37
  72.6 2.6 %collective-permute-start.18 = (bf16[512,256]{1,0:T(8,128)(2,1)S(1)}, bf16[512,256]{1,0:T(8,128)(2,1)S(1)}, u32[]{:S(2)}, u32[]{:S(2)}) collective-permute-start(bf16[512,256]{1,0:T(8,128)(2,1)S(1)} %pad_maximum_fusion.1.slope_ref), channel_id=1, source_target_pairs={{0,4},{4,0},{8,12},{12,8},{16,20},{20,16},{24,28},{28,24},{1,5},{5... | collective-permute-start | bytes 786440 | tf_op jit(solution)/shard_map/ppermute | solution.py:29
  75.1 3.4 %collective-permute-start.12 = (bf16[512,256]{1,0:T(8,128)(2,1)S(1)}, bf16[512,256]{1,0:T(8,128)(2,1)S(1)}, u32[]{:S(2)}, u32[]{:S(2)}) collective-permute-start(bf16[512,256]{1,0:T(8,128)(2,1)S(1)} %pad_maximum_fusion.slope_ref), channel_id=1, source_target_pairs={{0,4},{4,0},{8,12},{12,8},{16,20},{20,16},{24,28},{28,24},{1,5},{5... | collective-permute-start | bytes 786440 | tf_op jit(solution)/shard_map/ppermute | solution.py:29
  76.7 6.4 %collective-permute-start.21 = (bf16[512,256]{1,0:T(8,128)(2,1)S(1)}, bf16[512,256]{1,0:T(8,128)(2,1)S(1)}, u32[]{:S(2)}, u32[]{:S(2)}) collective-permute-start(bf16[512,256]{1,0:T(8,128)(2,1)S(1)} %get-tuple-element.45), channel_id=1, source_target_pairs={{0,8},{4,20},{8,0},{12,28},{16,24},{20,4},{24,16},{28,12},{1,9},{5... | collective-permute-start | bytes 786440 | tf_op jit(solution)/shard_map/ppermute | solution.py:362
  79.9 7.2 %collective-permute-start.19 = (bf16[512,256]{1,0:T(8,128)(2,1)S(1)}, bf16[512,256]{1,0:T(8,128)(2,1)S(1)}, u32[]{:S(2)}, u32[]{:S(2)}) collective-permute-start(bf16[512,256]{1,0:T(8,128)(2,1)S(1)} %get-tuple-element.43), channel_id=1, source_target_pairs={{0,8},{4,20},{8,0},{12,28},{16,24},{20,4},{24,16},{28,12},{1,9},{5... | collective-permute-start | bytes 786440 | tf_op jit(solution)/shard_map/ppermute | solution.py:362
  83.2 5.0 %collective-permute-start.22 = (bf16[256,256]{1,0:T(8,128)(2,1)S(1)}, bf16[256,256]{1,0:T(8,128)(2,1)S(1)}, u32[]{:S(2)}, u32[]{:S(2)}) collective-permute-start(bf16[256,256]{1,0:T(8,128)(2,1)S(1)} %slice.132), channel_id=1, source_target_pairs={{0,16},{4,12},{8,24},{12,4},{16,0},{20,28},{24,8},{28,20},{1,17},{... | collective-permute-start | bytes 393224 | tf_op jit(solution)/shard_map/ppermute | solution.py:362
  87.2 5.0 %collective-permute-start.20 = (bf16[256,256]{1,0:T(8,128)(2,1)S(1)}, bf16[256,256]{1,0:T(8,128)(2,1)S(1)}, u32[]{:S(2)}, u32[]{:S(2)}) collective-permute-start(bf16[256,256]{1,0:T(8,128)(2,1)S(1)} %slice.133), channel_id=1, source_target_pairs={{0,16},{4,12},{8,24},{12,4},{16,0},{20,28},{24,8},{28,20},{1,17},{... | collective-permute-start | bytes 393224 | tf_op jit(solution)/shard_map/ppermute | solution.py:362
  92.3 13.9 %collective-permute-start.23 = (bf16[256,512]{1,0:T(8,128)(2,1)S(1)}, bf16[256,512]{1,0:T(8,128)(2,1)S(1)}, u32[]{:S(2)}, u32[]{:S(2)}) collective-permute-start(bf16[256,512]{1,0:T(8,128)(2,1)S(1)} %pad_maximum_fusion.2), channel_id=1, source_target_pairs={{0,0},{1,10},{2,17},{3,27},{4,4},{5,14},{6,21},{7,31},{8,1},{9,11}... | collective-permute-start | bytes 786440 | tf_op jit(solution)/shard_map/ppermute | solution.py:373
  (7 other events, 41.5 us)

commit v11 on v9

--- a/solution.py
+++ b/solution.py
@@ -371,7 +371,8 @@
         for c in range(cores)
         for z in range(tensor_count)
     ]
-    grad_weight = lax.ppermute(jnp.concatenate(grads, axis=1), AXES, pairs).astype(F32)
+    grad, policy_values = lax.optimization_barrier((jnp.concatenate(grads, axis=1), policy_values))
+    grad_weight = lax.ppermute(grad, AXES, pairs).astype(F32)
     return (policy_values.reshape(1, 1, slot_count, value_width), grad_weight)
 
 

time: 106 us -> 107 us (level)
  the two profiles are of different devices: /device:TPU:0 before, /device:TPU:4 now
where the time goes in v11:
time: 107 us; the launch traced here: 106 us
  starting transfers between devices  45.5 us (43%)
  waiting for transfers between devices  36.7 us (34%)
  Pallas kernels  11.5 us (11%)
  matrix products  4.96 us (5%)
  other arithmetic  4.48 us (4%)
  local copies, waits for them, and re-layouts  1.92 us (2%)
  between operations  1.07 us (1%)
    ppermute x11, waiting for transfers between devices, crossed(): return lax.ppermute(array, 'tensor', [(i, i ^ step) for i in range(count)])  17.8 us
    ppermute x11, starting transfers between devices, crossed(): return lax.ppermute(array, 'tensor', [(i, i ^ step) for i in range(count)])  17.5 us
    all_to_all x1, starting transfers between devices, on_device(): got_cot = lax.all_to_all(cot, 'dp', split_axis=0, concat_axis=0, tiled=True)  12.2 us
    ppermute x1, waiting for transfers between devices, on_device(): grad_weight = lax.ppermute(grad, AXES, pairs).astype(F32)  9.1 us
    pallas_call x1, Pallas kernels, on_device(): pl.pallas_call(functools.partial(prepare_kernel, tensor_count, steps), gr...  6.95 us
    ppermute x4, waiting for transfers between devices, on_device(): total = total + lax.ppermute(given, 'dp', pairs).astype(F32)  5.24 us
    all_to_all x1, waiting for transfers between devices, on_device(): got_cot = lax.all_to_all(cot, 'dp', split_axis=0, concat_axis=0, tiled=True)  4.46 us
    all_to_all x1, starting transfers between devices, on_device(): lax.all_to_all(sent, 'dp', split_axis=0, concat_axis=0, tiled=True)  4.23 us
  transfers between devices with their start and end apart: 26, of which 13 were waited for; matrix products, arithmetic and copies ran while one was open for 8% of the time, Pallas kernels for 11%

profile of v11, /device:TPU:4, one launch (start us, length us, event | category | flops | bytes accessed | tf_op | source)
XLA Modules:
  0.0 106.1 jit_solution(7594592770473858529)
XLA Ops:
  2.0 6.9 %prepare.1 = (bf16[512,1024]{1,0:T(8,128)(2,1)}, bf16[512,1024]{1,0:T(8,128)(2,1)}, bf16[144,512]{1,0:T(8,128)(2,1)}, bf16[144,512]{1,0:T(8,128)(2,1)}, bf16[144...) custom-call(s32[2]{0:T(128)} %pad_add_fusion.1.at, bf16[512,2048]{1,0:T(8,128)(2,1)} %x_ref.1, f32[1,2048]{1,0:T(1,128)} %bitcast.31, ...), custom_call_target="tpu_custom_call" | custom-call | flops 1073741824 | bytes 8388608 | tf_op jit(solution)/shard_map/prepare/pallas_call | solution.py:198
  10.4 1.6 %slice_select_fusion = (bf16[1024,256]{1,0:T(8,128)(2,1)S(1)}, bf16[1024,256]{1,0:T(8,128)(2,1)S(1)}) fusion(bf16[1024,512]{1,0:T(8,128)(2,1)} %param.14, bf16[1024,512]{1,0:T(8,128)(2,1)} %copy-done.8, pred[]{:T(512)S(6)} %or.15), kind=kLoop, calls=%fused_computation.7 | loop fusion | flops 524288 | bytes 3145729 | tf_op jit(solution)/shard_map/jit(_where)/select_n | solution.py:248
  12.0 1.3 %collective-permute-start.2 = (bf16[1024,256]{1,0:T(8,128)(2,1)S(1)}, bf16[1024,256]{1,0:T(8,128)(2,1)S(1)}, u32[]{:S(2)}, u32[]{:S(2)}) collective-permute-start(bf16[1024,256]{1,0:T(8,128)(2,1)S(1)} %get-tuple-element.49), channel_id=1, source_target_pairs={{0,16},{9,25},{18,2},{27,11},{8,24},{1,17},{26,10},{19,3},{4,12},{... | collective-permute-start | bytes 1572872 | tf_op jit(solution)/shard_map/ppermute | solution.py:186
  13.3 1.3 %collective-permute-start.6 = (bf16[1024,256]{1,0:T(8,128)(2,1)S(1)}, bf16[1024,256]{1,0:T(8,128)(2,1)}, u32[]{:S(2)}, u32[]{:S(2)}) collective-permute-start(bf16[1024,256]{1,0:T(8,128)(2,1)S(1)} %get-tuple-element.48), channel_id=1, source_target_pairs={{0,16},{9,25},{18,2},{27,11},{8,24},{1,17},{26,10},{19,3},{4,12},{... | collective-permute-start | bytes 1572872 | tf_op jit(solution)/shard_map/ppermute | solution.py:186
  14.6 12.2 %all-to-all-start = ((bf16[8,32,512]{2,1,0:T(8,128)(2,1)}), bf16[8,32,512]{2,1,0:T(8,128)(2,1)S(1)}, u32[]{:S(2)}, u32[]{:S(2)}) async-start(bf16[8,32,512]{2,1,0:T(8,128)(2,1)} %bitcast.13), calls=%async_computation | async-start | bytes 524288 | tf_op jit(solution)/shard_map/all_to_all | solution.py:254
  26.9 2.1 %collective-permute-start.3 = (bf16[144,512]{1,0:T(8,128)(2,1)}, bf16[144,512]{1,0:T(8,128)(2,1)S(1)}, u32[]{:S(2)}, u32[]{:S(2)}) collective-permute-start(bf16[144,512]{1,0:T(8,128)(2,1)} %get-tuple-element.32), channel_id=1, source_target_pairs={{0,1},{1,0},{2,3},{3,2},{4,5},{5,4},{6,7},{7,6},{8,9},{9,8},{10,11... | collective-permute-start | bytes 442376 | tf_op jit(solution)/shard_map/ppermute | solution.py:37
  29.0 2.2 %collective-permute-start.4 = (bf16[144,512]{1,0:T(8,128)(2,1)}, bf16[144,512]{1,0:T(8,128)(2,1)S(1)}, u32[]{:S(2)}, u32[]{:S(2)}) collective-permute-start(bf16[144,512]{1,0:T(8,128)(2,1)} %get-tuple-element.33), channel_id=1, source_target_pairs={{0,2},{1,3},{2,0},{3,1},{4,6},{5,7},{6,4},{7,5},{8,10},{9,11},{10,... | collective-permute-start | bytes 442376 | tf_op jit(solution)/shard_map/ppermute | solution.py:37
  32.2 4.5 %all-to-all-done = bf16[8,32,512]{2,1,0:T(8,128)(2,1)S(1)} async-done(((bf16[8,32,512]{2,1,0:T(8,128)(2,1)}), bf16[8,32,512]{2,1,0:T(8,128)(2,1)S(1)}, u32[]{:S(2)}, u32[]{:S(2)}) %all-to-all-start) | async-done | bytes 262176 | tf_op jit(solution)/shard_map/all_to_all | solution.py:254
  37.3 1.6 %convolution_convert_fusion.2 = bf16[512,256]{1,0:T(8,128)(2,1)S(1)} fusion(bf16[512,1024]{1,0:T(8,128)(2,1)S(1)} %collective-permute-done.1.got_ref, bf16[1024,256]{1,0:T(8,128)(2,1)} %collective-permute-done.6, bf16[1024,256]{1,0:T(8,128)(2,1)S(1)} %get-tuple-element.48, pred[]{:T(512)S(6)} %or.18), kind=kOutput, calls=%fused_computation.4 | convolution fusion | flops 268828672 | bytes 2359297 | tf_op jit(solution)/shard_map/dot_general | solution.py:21
  39.0 4.2 %collective-permute-done.4.refs_2_ = bf16[144,512]{1,0:T(8,128)(2,1)S(1)} collective-permute-done((bf16[144,512]{1,0:T(8,128)(2,1)}, bf16[144,512]{1,0:T(8,128)(2,1)S(1)}, u32[]{:S(2)}, u32[]{:S(2)}) %collective-permute-start.4) | collective-permute-done | bytes 147488 | tf_op jit(solution)/shard_map/ppermute | solution.py:37
  43.2 1.1 %rows.1 = (f32[128,512]{1,0:T(8,128)S(1)}, f32[128,128]{1,0:T(8,128)S(1)}, f32[128,128]{1,0:T(8,128)S(1)}, bf16[128,256]{1,0:T(8,128)(2,1)S(1)}) custom-call(s32[8]{0:T(128)S(1)} %bitcast.24, s32[8]{0:T(128)S(1)} %bitcast.25, f32[8]{0:T(128)S(1)} %bitcast.26, f32[1,128]{1,0:T(1,128)S(1)} %bitcast.27, bf16[256,512]{1,0:T(8,128)(2,1)S(1)} %bitcast.23, ...), custom_call_target="tpu_custom_call" | custom-call | flops 33554432 | bytes 2097152 | tf_op jit(solution)/shard_map/rows/pallas_call | solution.py:277
  44.8 2.7 %collective-permute-start.13 = (bf16[256,256]{1,0:T(8,128)(2,1)S(1)}, bf16[256,256]{1,0:T(8,128)(2,1)S(1)}, u32[]{:S(2)}, u32[]{:S(2)}) collective-permute-start(bf16[256,256]{1,0:T(8,128)(2,1)S(1)} %slice.134), channel_id=1, source_target_pairs={{0,1},{1,0},{2,3},{3,2},{4,5},{5,4},{6,7},{7,6},{8,9},{9,8},{10,11... | collective-permute-start | bytes 393224 | tf_op jit(solution)/shard_map/ppermute | solution.py:37
  47.5 1.5 %convolution_add_fusion.1 = f32[512,256]{1,0:T(8,128)S(1)} fusion(bf16[512,1024]{1,0:T(8,128)(2,1)S(1)} %copy-done, bf16[512,256]{1,0:T(8,128)(2,1)S(1)} %collective-permute-done.7, bf16[1024,256]{1,0:T(8,128)(2,1)} %collective-permute-done.6, bf16[1024,256]{1,0:T(8,128)(2,1)S(1)} %get-tuple-element.48, pred[]{:T(512)S(6)} %or.18), kind=kOutput, calls=%fused_computation.1 | convolution fusion | flops 268959744 | bytes 2883585 | tf_op jit(solution)/shard_map/dot_general | solution.py:21
  49.1 2.5 %collective-permute-done.13 = bf16[256,256]{1,0:T(8,128)(2,1)S(1)} collective-permute-done((bf16[256,256]{1,0:T(8,128)(2,1)S(1)}, bf16[256,256]{1,0:T(8,128)(2,1)S(1)}, u32[]{:S(2)}, u32[]{:S(2)}) %collective-permute-start.13) | collective-permute-done | bytes 131104 | tf_op jit(solution)/shard_map/ppermute | solution.py:37
  51.6 3.7 %collective-permute-start.14 = (bf16[128,256]{1,0:T(8,128)(2,1)S(1)}, bf16[128,256]{1,0:T(8,128)(2,1)S(1)}, u32[]{:S(2)}, u32[]{:S(2)}) collective-permute-start(bf16[128,256]{1,0:T(8,128)(2,1)S(1)} %slice.136), channel_id=1, source_target_pairs={{0,2},{1,3},{2,0},{3,1},{4,6},{5,7},{6,4},{7,5},{8,10},{9,11},{10,... | collective-permute-start | bytes 196616 | tf_op jit(solution)/shard_map/ppermute | solution.py:37
  55.4 2.0 %collective-permute-start.9 = (bf16[128,256]{1,0:T(8,128)(2,1)S(1)}, bf16[128,256]{1,0:T(8,128)(2,1)S(1)}, u32[]{:S(2)}, u32[]{:S(2)}) collective-permute-start(bf16[128,256]{1,0:T(8,128)(2,1)S(1)} %slice.137), channel_id=1, source_target_pairs={{0,2},{1,3},{2,0},{3,1},{4,6},{5,7},{6,4},{7,5},{8,10},{9,11},{10,... | collective-permute-start | bytes 196616 | tf_op jit(solution)/shard_map/ppermute | solution.py:37
  57.5 1.3 %collective-permute-done.14 = bf16[128,256]{1,0:T(8,128)(2,1)S(1)} collective-permute-done((bf16[128,256]{1,0:T(8,128)(2,1)S(1)}, bf16[128,256]{1,0:T(8,128)(2,1)S(1)}, u32[]{:S(2)}, u32[]{:S(2)}) %collective-permute-start.14) | collective-permute-done | bytes 65568 | tf_op jit(solution)/shard_map/ppermute | solution.py:37
  58.8 2.3 %collective-permute-done.9 = bf16[128,256]{1,0:T(8,128)(2,1)S(1)} collective-permute-done((bf16[128,256]{1,0:T(8,128)(2,1)S(1)}, bf16[128,256]{1,0:T(8,128)(2,1)S(1)}, u32[]{:S(2)}, u32[]{:S(2)}) %collective-permute-start.9) | collective-permute-done | bytes 65568 | tf_op jit(solution)/shard_map/ppermute | solution.py:37
  61.2 1.5 %collective-permute-start.18 = (bf16[128,256]{1,0:T(8,128)(2,1)S(1)}, bf16[128,256]{1,0:T(8,128)(2,1)S(1)}, u32[]{:S(2)}, u32[]{:S(2)}) collective-permute-start(bf16[128,256]{1,0:T(8,128)(2,1)S(1)} %get-tuple-element.53), channel_id=1, source_target_pairs={{0,2},{1,3},{2,0},{3,1},{4,6},{5,7},{6,4},{7,5},{8,10},{9,11},{10,... | collective-permute-start | bytes 196616 | tf_op jit(solution)/shard_map/ppermute | solution.py:37
  62.7 1.4 %collective-permute-start.10 = (bf16[128,256]{1,0:T(8,128)(2,1)S(1)}, bf16[128,256]{1,0:T(8,128)(2,1)S(1)}, u32[]{:S(2)}, u32[]{:S(2)}) collective-permute-start(bf16[128,256]{1,0:T(8,128)(2,1)S(1)} %get-tuple-element.54), channel_id=1, source_target_pairs={{0,2},{1,3},{2,0},{3,1},{4,6},{5,7},{6,4},{7,5},{8,10},{9,11},{10,... | collective-permute-start | bytes 196616 | tf_op jit(solution)/shard_map/ppermute | solution.py:37
  64.2 2.7 %collective-permute-done.18 = bf16[128,256]{1,0:T(8,128)(2,1)S(1)} collective-permute-done((bf16[128,256]{1,0:T(8,128)(2,1)S(1)}, bf16[128,256]{1,0:T(8,128)(2,1)S(1)}, u32[]{:S(2)}, u32[]{:S(2)}) %collective-permute-start.18) | collective-permute-done | bytes 65568 | tf_op jit(solution)/shard_map/ppermute | solution.py:37
  67.0 1.5 %collective-permute-done.10 = bf16[128,256]{1,0:T(8,128)(2,1)S(1)} collective-permute-done((bf16[128,256]{1,0:T(8,128)(2,1)S(1)}, bf16[128,256]{1,0:T(8,128)(2,1)S(1)}, u32[]{:S(2)}, u32[]{:S(2)}) %collective-permute-start.10) | collective-permute-done | bytes 65568 | tf_op jit(solution)/shard_map/ppermute | solution.py:37
  69.0 2.9 %collective-permute-done.19 = bf16[256,256]{1,0:T(8,128)(2,1)S(1)} collective-permute-done((bf16[256,256]{1,0:T(8,128)(2,1)S(1)}, bf16[256,256]{1,0:T(8,128)(2,1)S(1)}, u32[]{:S(2)}, u32[]{:S(2)}) %collective-permute-start.19) | collective-permute-done | bytes 131104 | tf_op jit(solution)/shard_map/ppermute | solution.py:37
  73.7 2.1 %gradient.3 = (f32[512,256]{1,0:T(8,128)S(1)}, bf16[512,256]{1,0:T(8,128)(2,1)}) custom-call(s32[4]{0:T(128)S(1)} %pad_add_fusion.at, bf16[512,1024]{1,0:T(8,128)(2,1)S(1)} %copy-done, bf16[512,1024]{1,0:T(8,128)(2,1)S(1)} %collective-permute-done.1.got_ref, bf16[512,256]{1,0:T(8,128)(2,1)S(1)} %pad_maximum_fusion.1.slope_ref, ...), custom_call_target="tpu_custom_call" | custom-call | flops 536870912 | bytes 4194304 | tf_op jit(solution)/shard_map/gradient/pallas_call | solution.py:326
  75.8 1.5 %collective-permute-start.21 = (bf16[512,256]{1,0:T(8,128)(2,1)}, bf16[512,256]{1,0:T(8,128)(2,1)}, u32[]{:S(2)}, u32[]{:S(2)}) collective-permute-start(bf16[512,256]{1,0:T(8,128)(2,1)} %get-tuple-element.44), channel_id=1, source_target_pairs={{0,8},{4,20},{8,0},{12,28},{16,24},{20,4},{24,16},{28,12},{1,9},{5... | collective-permute-start | bytes 786440 | tf_op jit(solution)/shard_map/ppermute | solution.py:363
  77.3 1.4 %gradient.2 = (f32[512,256]{1,0:T(8,128)S(1)}, bf16[512,256]{1,0:T(8,128)(2,1)S(1)}) custom-call(s32[4]{0:T(128)S(1)} %pad_add_fusion.at, bf16[512,1024]{1,0:T(8,128)(2,1)S(1)} %copy-done, bf16[512,1024]{1,0:T(8,128)(2,1)S(1)} %collective-permute-done.1.got_ref, bf16[512,256]{1,0:T(8,128)(2,1)S(1)} %pad_maximum_fusion.slope_ref, ...), custom_call_target="tpu_custom_call" | custom-call | flops 536870912 | bytes 4194304 | tf_op jit(solution)/shard_map/gradient/pallas_call | solution.py:326
  79.3 4.2 %all-to-all-start.1 = ((bf16[8,32,512]{2,1,0:T(8,128)(2,1)}), bf16[8,32,512]{2,1,0:T(8,128)(2,1)S(1)}, u32[]{:S(2)}, u32[]{:S(2)}) async-start(bf16[8,32,512]{2,1,0:T(8,128)(2,1)} %bitcast.28), calls=%async_computation.1 | async-start | bytes 524288 | tf_op jit(solution)/shard_map/all_to_all | solution.py:321
  85.3 1.5 %collective-permute-start.17 = (bf16[256,256]{1,0:T(8,128)(2,1)S(1)}, bf16[256,256]{1,0:T(8,128)(2,1)S(1)}, u32[]{:S(2)}, u32[]{:S(2)}) collective-permute-start(bf16[256,256]{1,0:T(8,128)(2,1)S(1)} %slice.133), channel_id=1, source_target_pairs={{0,16},{4,12},{8,24},{12,4},{16,0},{20,28},{24,8},{28,20},{1,17},{... | collective-permute-start | bytes 393224 | tf_op jit(solution)/shard_map/ppermute | solution.py:363
  86.8 3.3 %collective-permute-done.22 = bf16[256,256]{1,0:T(8,128)(2,1)S(1)} collective-permute-done((bf16[256,256]{1,0:T(8,128)(2,1)S(1)}, bf16[256,256]{1,0:T(8,128)(2,1)S(1)}, u32[]{:S(2)}, u32[]{:S(2)}) %collective-permute-start.22) | collective-permute-done | bytes 131104 | tf_op jit(solution)/shard_map/ppermute | solution.py:363
  90.2 1.4 %collective-permute-done.17 = bf16[256,256]{1,0:T(8,128)(2,1)S(1)} collective-permute-done((bf16[256,256]{1,0:T(8,128)(2,1)S(1)}, bf16[256,256]{1,0:T(8,128)(2,1)S(1)}, u32[]{:S(2)}, u32[]{:S(2)}) %collective-permute-start.17) | collective-permute-done | bytes 131104 | tf_op jit(solution)/shard_map/ppermute | solution.py:363
  91.6 3.8 %collective-permute-start.23 = (bf16[256,512]{1,0:T(8,128)(2,1)S(1)}, bf16[256,512]{1,0:T(8,128)(2,1)S(1)}, u32[]{:S(2)}, u32[]{:S(2)}) collective-permute-start(bf16[256,512]{1,0:T(8,128)(2,1)S(1)} %pad_maximum_fusion.2), channel_id=1, source_target_pairs={{0,0},{1,10},{2,17},{3,27},{4,4},{5,14},{6,21},{7,31},{8,1},{9,11}... | collective-permute-start | bytes 786440 | tf_op jit(solution)/shard_map/ppermute | solution.py:375
  95.4 9.1 %collective-permute-done.23 = bf16[256,512]{1,0:T(8,128)(2,1)S(1)} collective-permute-done((bf16[256,512]{1,0:T(8,128)(2,1)S(1)}, bf16[256,512]{1,0:T(8,128)(2,1)S(1)}, u32[]{:S(2)}, u32[]{:S(2)}) %collective-permute-start.23) | collective-permute-done | bytes 262176 | tf_op jit(solution)/shard_map/ppermute | solution.py:375
  (77 shorter events, 11.6 us)
Async XLA Ops:
  0.6 8.8 %collective-permute-start = (bf16[1024,512]{1,0:T(8,128)(2,1)}, bf16[1024,512]{1,0:T(8,128)(2,1)S(1)}, u32[]{:S(2)}, u32[]{:S(2)}) collective-permute-start(bf16[1024,512]{1,0:T(8,128)(2,1)} %param.14), channel_id=1, source_target_pairs={{0,8},{9,1},{18,26},{27,19},{4,20},{13,29},{22,6},{31,15}} | collective-permute-start | bytes 3145736 | tf_op jit(solution)/shard_map/ppermute | solution.py:186
  8.9 22.3 %copy-start.11 = (bf16[144,512]{1,0:T(8,128)(2,1)S(1)}, bf16[144,512]{1,0:T(8,128)(2,1)}, u32[]{:S(2)}) copy-start(bf16[144,512]{1,0:T(8,128)(2,1)} %get-tuple-element.34) | copy-start | bytes 442372
  8.9 27.7 %collective-permute-start.1 = (bf16[512,1024]{1,0:T(8,128)(2,1)}, bf16[512,1024]{1,0:T(8,128)(2,1)S(1)}, u32[]{:S(2)}, u32[]{:S(2)}) collective-permute-start(bf16[512,1024]{1,0:T(8,128)(2,1)} %get-tuple-element.27), channel_id=1, source_target_pairs={{0,4},{4,0},{8,12},{12,8},{16,20},{20,16},{24,28},{28,24},{1,5},{5... | collective-permute-start | bytes 3145736 | tf_op jit(solution)/shard_map/ppermute | solution.py:29
  12.0 24.7 %copy-start.6 = (bf16[1024,256]{1,0:T(8,128)(2,1)}, bf16[1024,256]{1,0:T(8,128)(2,1)S(1)}, u32[]{:S(2)}) copy-start(bf16[1024,256]{1,0:T(8,128)(2,1)S(1)} %get-tuple-element.49) | copy-start | bytes 1572868
  12.0 19.2 %collective-permute-start.2 = (bf16[1024,256]{1,0:T(8,128)(2,1)S(1)}, bf16[1024,256]{1,0:T(8,128)(2,1)S(1)}, u32[]{:S(2)}, u32[]{:S(2)}) collective-permute-start(bf16[1024,256]{1,0:T(8,128)(2,1)S(1)} %get-tuple-element.49), channel_id=1, source_target_pairs={{0,16},{9,25},{18,2},{27,11},{8,24},{1,17},{26,10},{19,3},{4,12},{... | collective-permute-start | bytes 1572872 | tf_op jit(solution)/shard_map/ppermute | solution.py:186
  13.3 23.9 %collective-permute-start.6 = (bf16[1024,256]{1,0:T(8,128)(2,1)S(1)}, bf16[1024,256]{1,0:T(8,128)(2,1)}, u32[]{:S(2)}, u32[]{:S(2)}) collective-permute-start(bf16[1024,256]{1,0:T(8,128)(2,1)S(1)} %get-tuple-element.48), channel_id=1, source_target_pairs={{0,16},{9,25},{18,2},{27,11},{8,24},{1,17},{26,10},{19,3},{4,12},{... | collective-permute-start | bytes 1572872 | tf_op jit(solution)/shard_map/ppermute | solution.py:186
  14.6 22.0 %all-to-all-start = ((bf16[8,32,512]{2,1,0:T(8,128)(2,1)}), bf16[8,32,512]{2,1,0:T(8,128)(2,1)S(1)}, u32[]{:S(2)}, u32[]{:S(2)}) async-start(bf16[8,32,512]{2,1,0:T(8,128)(2,1)} %bitcast.13), calls=%async_computation | async-start | bytes 524288 | tf_op jit(solution)/shard_map/all_to_all | solution.py:254
  26.9 12.1 %collective-permute-start.3 = (bf16[144,512]{1,0:T(8,128)(2,1)}, bf16[144,512]{1,0:T(8,128)(2,1)S(1)}, u32[]{:S(2)}, u32[]{:S(2)}) collective-permute-start(bf16[144,512]{1,0:T(8,128)(2,1)} %get-tuple-element.32), channel_id=1, source_target_pairs={{0,1},{1,0},{2,3},{3,2},{4,5},{5,4},{6,7},{7,6},{8,9},{9,8},{10,11... | collective-permute-start | bytes 442376 | tf_op jit(solution)/shard_map/ppermute | solution.py:37
  29.0 14.2 %collective-permute-start.4 = (bf16[144,512]{1,0:T(8,128)(2,1)}, bf16[144,512]{1,0:T(8,128)(2,1)S(1)}, u32[]{:S(2)}, u32[]{:S(2)}) collective-permute-start(bf16[144,512]{1,0:T(8,128)(2,1)} %get-tuple-element.33), channel_id=1, source_target_pairs={{0,2},{1,3},{2,0},{3,1},{4,6},{5,7},{6,4},{7,5},{8,10},{9,11},{10,... | collective-permute-start | bytes 442376 | tf_op jit(solution)/shard_map/ppermute | solution.py:37
  31.2 12.0 %collective-permute-start.5 = (bf16[144,512]{1,0:T(8,128)(2,1)S(1)}, bf16[144,512]{1,0:T(8,128)(2,1)S(1)}, u32[]{:S(2)}, u32[]{:S(2)}) collective-permute-start(bf16[144,512]{1,0:T(8,128)(2,1)S(1)} %copy-done.11), channel_id=1, source_target_pairs={{0,3},{1,2},{2,1},{3,0},{4,7},{5,6},{6,5},{7,4},{8,11},{9,10},{10,... | collective-permute-start | bytes 442376 | tf_op jit(solution)/shard_map/ppermute | solution.py:37
  36.6 6.5 %copy-start.5 = (f32[128]{0:T(128)S(1)}, f32[128]{0:T(128)}, u32[]{:S(2)}) copy-start(f32[128]{0:T(128)} %param.18) | copy-start | bytes 1540
  37.1 7.1 %copy-start = (bf16[512,1024]{1,0:T(8,128)(2,1)S(1)}, bf16[512,1024]{1,0:T(8,128)(2,1)}, u32[]{:S(2)}) copy-start(bf16[512,1024]{1,0:T(8,128)(2,1)} %get-tuple-element.26.kept_ref) | copy-start | bytes 3145732
  37.2 7.1 %copy-start.7 = (bf16[1024,256]{1,0:T(8,128)(2,1)S(1)}, bf16[1024,256]{1,0:T(8,128)(2,1)}, u32[]{:S(2)}) copy-start(bf16[1024,256]{1,0:T(8,128)(2,1)} %copy-done.6) | copy-start | bytes 1572868
  37.2 7.1 %copy-start.10 = (bf16[1024,256]{1,0:T(8,128)(2,1)S(1)}, bf16[1024,256]{1,0:T(8,128)(2,1)}, u32[]{:S(2)}) copy-start(bf16[1024,256]{1,0:T(8,128)(2,1)} %copy-done.9) | copy-start | bytes 1572868
  37.2 7.1 %collective-permute-start.12 = (bf16[512,256]{1,0:T(8,128)(2,1)S(1)}, bf16[512,256]{1,0:T(8,128)(2,1)S(1)}, u32[]{:S(2)}, u32[]{:S(2)}) collective-permute-start(bf16[512,256]{1,0:T(8,128)(2,1)S(1)} %convolution_convert_fusion.1), channel_id=1, source_target_pairs={{0,4},{4,0},{8,12},{12,8},{16,20},{20,16},{24,28},{28,24},{1,5},{5... | collective-permute-start | bytes 786440 | tf_op jit(solution)/shard_map/ppermute | solution.py:29
  38.9 8.6 %collective-permute-start.7 = (bf16[512,256]{1,0:T(8,128)(2,1)S(1)}, bf16[512,256]{1,0:T(8,128)(2,1)S(1)}, u32[]{:S(2)}, u32[]{:S(2)}) collective-permute-start(bf16[512,256]{1,0:T(8,128)(2,1)S(1)} %convolution_convert_fusion.2), channel_id=1, source_target_pairs={{0,4},{4,0},{8,12},{12,8},{16,20},{20,16},{24,28},{28,24},{1,5},{5... | collective-permute-start | bytes 786440 | tf_op jit(solution)/shard_map/ppermute | solution.py:29
  44.8 6.8 %collective-permute-start.13 = (bf16[256,256]{1,0:T(8,128)(2,1)S(1)}, bf16[256,256]{1,0:T(8,128)(2,1)S(1)}, u32[]{:S(2)}, u32[]{:S(2)}) collective-permute-start(bf16[256,256]{1,0:T(8,128)(2,1)S(1)} %slice.134), channel_id=1, source_target_pairs={{0,1},{1,0},{2,3},{3,2},{4,5},{5,4},{6,7},{7,6},{8,9},{9,8},{10,11... | collective-permute-start | bytes 393224 | tf_op jit(solution)/shard_map/ppermute | solution.py:37
  49.0 6.3 %collective-permute-start.8 = (bf16[256,256]{1,0:T(8,128)(2,1)S(1)}, bf16[256,256]{1,0:T(8,128)(2,1)S(1)}, u32[]{:S(2)}, u32[]{:S(2)}) collective-permute-start(bf16[256,256]{1,0:T(8,128)(2,1)S(1)} %slice.135), channel_id=1, source_target_pairs={{0,1},{1,0},{2,3},{3,2},{4,5},{5,4},{6,7},{7,6},{8,9},{9,8},{10,11... | collective-permute-start | bytes 393224 | tf_op jit(solution)/shard_map/ppermute | solution.py:37
  51.6 7.1 %collective-permute-start.14 = (bf16[128,256]{1,0:T(8,128)(2,1)S(1)}, bf16[128,256]{1,0:T(8,128)(2,1)S(1)}, u32[]{:S(2)}, u32[]{:S(2)}) collective-permute-start(bf16[128,256]{1,0:T(8,128)(2,1)S(1)} %slice.136), channel_id=1, source_target_pairs={{0,2},{1,3},{2,0},{3,1},{4,6},{5,7},{6,4},{7,5},{8,10},{9,11},{10,... | collective-permute-start | bytes 196616 | tf_op jit(solution)/shard_map/ppermute | solution.py:37
  55.4 5.7 %collective-permute-start.9 = (bf16[128,256]{1,0:T(8,128)(2,1)S(1)}, bf16[128,256]{1,0:T(8,128)(2,1)S(1)}, u32[]{:S(2)}, u32[]{:S(2)}) collective-permute-start(bf16[128,256]{1,0:T(8,128)(2,1)S(1)} %slice.137), channel_id=1, source_target_pairs={{0,2},{1,3},{2,0},{3,1},{4,6},{5,7},{6,4},{7,5},{8,10},{9,11},{10,... | collective-permute-start | bytes 196616 | tf_op jit(solution)/shard_map/ppermute | solution.py:37
  61.2 5.7 %collective-permute-start.18 = (bf16[128,256]{1,0:T(8,128)(2,1)S(1)}, bf16[128,256]{1,0:T(8,128)(2,1)S(1)}, u32[]{:S(2)}, u32[]{:S(2)}) collective-permute-start(bf16[128,256]{1,0:T(8,128)(2,1)S(1)} %get-tuple-element.53), channel_id=1, source_target_pairs={{0,2},{1,3},{2,0},{3,1},{4,6},{5,7},{6,4},{7,5},{8,10},{9,11},{10,... | collective-permute-start | bytes 196616 | tf_op jit(solution)/shard_map/ppermute | solution.py:37
  62.7 5.7 %collective-permute-start.10 = (bf16[128,256]{1,0:T(8,128)(2,1)S(1)}, bf16[128,256]{1,0:T(8,128)(2,1)S(1)}, u32[]{:S(2)}, u32[]{:S(2)}) collective-permute-start(bf16[128,256]{1,0:T(8,128)(2,1)S(1)} %get-tuple-element.54), channel_id=1, source_target_pairs={{0,2},{1,3},{2,0},{3,1},{4,6},{5,7},{6,4},{7,5},{8,10},{9,11},{10,... | collective-permute-start | bytes 196616 | tf_op jit(solution)/shard_map/ppermute | solution.py:37
  66.9 5.0 %collective-permute-start.19 = (bf16[256,256]{1,0:T(8,128)(2,1)S(1)}, bf16[256,256]{1,0:T(8,128)(2,1)S(1)}, u32[]{:S(2)}, u32[]{:S(2)}) collective-permute-start(bf16[256,256]{1,0:T(8,128)(2,1)S(1)} %pad_maximum_fusion.4), channel_id=1, source_target_pairs={{0,1},{1,0},{2,3},{3,2},{4,5},{5,4},{6,7},{7,6},{8,9},{9,8},{10,11... | collective-permute-start | bytes 393224 | tf_op jit(solution)/shard_map/ppermute | solution.py:37
  68.5 5.0 %collective-permute-start.11 = (bf16[256,256]{1,0:T(8,128)(2,1)S(1)}, bf16[256,256]{1,0:T(8,128)(2,1)S(1)}, u32[]{:S(2)}, u32[]{:S(2)}) collective-permute-start(bf16[256,256]{1,0:T(8,128)(2,1)S(1)} %pad_maximum_fusion.3), channel_id=1, source_target_pairs={{0,1},{1,0},{2,3},{3,2},{4,5},{5,4},{6,7},{7,6},{8,9},{9,8},{10,11... | collective-permute-start | bytes 393224 | tf_op jit(solution)/shard_map/ppermute | solution.py:37
  71.9 1.8 %collective-permute-start.20 = (bf16[512,256]{1,0:T(8,128)(2,1)S(1)}, bf16[512,256]{1,0:T(8,128)(2,1)S(1)}, u32[]{:S(2)}, u32[]{:S(2)}) collective-permute-start(bf16[512,256]{1,0:T(8,128)(2,1)S(1)} %pad_maximum_fusion.1.slope_ref), channel_id=1, source_target_pairs={{0,4},{4,0},{8,12},{12,8},{16,20},{20,16},{24,28},{28,24},{1,5},{5... | collective-permute-start | bytes 786440 | tf_op jit(solution)/shard_map/ppermute | solution.py:29
  73.6 3.8 %collective-permute-start.15 = (bf16[512,256]{1,0:T(8,128)(2,1)S(1)}, bf16[512,256]{1,0:T(8,128)(2,1)S(1)}, u32[]{:S(2)}, u32[]{:S(2)}) collective-permute-start(bf16[512,256]{1,0:T(8,128)(2,1)S(1)} %pad_maximum_fusion.slope_ref), channel_id=1, source_target_pairs={{0,4},{4,0},{8,12},{12,8},{16,20},{20,16},{24,28},{28,24},{1,5},{5... | collective-permute-start | bytes 786440 | tf_op jit(solution)/shard_map/ppermute | solution.py:29
  75.8 7.7 %collective-permute-start.21 = (bf16[512,256]{1,0:T(8,128)(2,1)}, bf16[512,256]{1,0:T(8,128)(2,1)}, u32[]{:S(2)}, u32[]{:S(2)}) collective-permute-start(bf16[512,256]{1,0:T(8,128)(2,1)} %get-tuple-element.44), channel_id=1, source_target_pairs={{0,8},{4,20},{8,0},{12,28},{16,24},{20,4},{24,16},{28,12},{1,9},{5... | collective-permute-start | bytes 786440 | tf_op jit(solution)/shard_map/ppermute | solution.py:363
  78.7 6.5 %collective-permute-start.16 = (bf16[512,256]{1,0:T(8,128)(2,1)S(1)}, bf16[512,256]{1,0:T(8,128)(2,1)S(1)}, u32[]{:S(2)}, u32[]{:S(2)}) collective-permute-start(bf16[512,256]{1,0:T(8,128)(2,1)S(1)} %get-tuple-element.42), channel_id=1, source_target_pairs={{0,8},{4,20},{8,0},{12,28},{16,24},{20,4},{24,16},{28,12},{1,9},{5... | collective-permute-start | bytes 786440 | tf_op jit(solution)/shard_map/ppermute | solution.py:363
  79.3 12.3 %all-to-all-start.1 = ((bf16[8,32,512]{2,1,0:T(8,128)(2,1)}), bf16[8,32,512]{2,1,0:T(8,128)(2,1)S(1)}, u32[]{:S(2)}, u32[]{:S(2)}) async-start(bf16[8,32,512]{2,1,0:T(8,128)(2,1)} %bitcast.28), calls=%async_computation.1 | async-start | bytes 524288 | tf_op jit(solution)/shard_map/all_to_all | solution.py:321
  84.6 5.6 %collective-permute-start.22 = (bf16[256,256]{1,0:T(8,128)(2,1)S(1)}, bf16[256,256]{1,0:T(8,128)(2,1)S(1)}, u32[]{:S(2)}, u32[]{:S(2)}) collective-permute-start(bf16[256,256]{1,0:T(8,128)(2,1)S(1)} %slice.132), channel_id=1, source_target_pairs={{0,16},{4,12},{8,24},{12,4},{16,0},{20,28},{24,8},{28,20},{1,17},{... | collective-permute-start | bytes 393224 | tf_op jit(solution)/shard_map/ppermute | solution.py:363
  85.3 6.2 %collective-permute-start.17 = (bf16[256,256]{1,0:T(8,128)(2,1)S(1)}, bf16[256,256]{1,0:T(8,128)(2,1)S(1)}, u32[]{:S(2)}, u32[]{:S(2)}) collective-permute-start(bf16[256,256]{1,0:T(8,128)(2,1)S(1)} %slice.133), channel_id=1, source_target_pairs={{0,16},{4,12},{8,24},{12,4},{16,0},{20,28},{24,8},{28,20},{1,17},{... | collective-permute-start | bytes 393224 | tf_op jit(solution)/shard_map/ppermute | solution.py:363
  91.6 12.9 %collective-permute-start.23 = (bf16[256,512]{1,0:T(8,128)(2,1)S(1)}, bf16[256,512]{1,0:T(8,128)(2,1)S(1)}, u32[]{:S(2)}, u32[]{:S(2)}) collective-permute-start(bf16[256,512]{1,0:T(8,128)(2,1)S(1)} %pad_maximum_fusion.2), channel_id=1, source_target_pairs={{0,0},{1,10},{2,17},{3,27},{4,4},{5,14},{6,21},{7,31},{8,1},{9,11}... | collective-permute-start | bytes 786440 | tf_op jit(solution)/shard_map/ppermute | solution.py:375
  (6 other events, 32.6 us)

commit v12 on v9

--- a/solution.py
+++ b/solution.py
@@ -262,15 +262,15 @@
         chunk_at.append(place ^ away ^ turned(t, levels))
     chunk_at = jnp.stack(chunk_at).astype(jnp.int32)
 
-    value_parts = []
+    value_got, value_kept = [], []
     for j in range(PARTS):
         held_part, got_part, is_getter_part = parts[j]
         if j == PARTS - 1:
-            got_part, got_cot = lax.optimization_barrier((got_part, got_cot))
+            tied = lax.optimization_barrier((got_part, got_cot, *value_kept))
+            got_part, got_cot, *value_kept = tied
         weight = jnp.where(is_getter_part, got_part, held_part)
-        value_given = dot(got_rows, weight).astype(BF16)
-        value_got = swapped(value_given, dp_count).astype(F32)
-        value_parts.append(dot(kept_rows, weight) + value_got)
+        value_got.append(swapped(dot(got_rows, weight).astype(BF16), dp_count))
+        value_kept.append(dot(kept_rows, weight))
 
     smem = pl.BlockSpec(memory_space=pltpu.SMEM)
     vmem = pl.BlockSpec(memory_space=pltpu.VMEM)
@@ -302,7 +302,7 @@
 
     values, slopes = [], []
     for j in range(PARTS):
-        total = value_parts[j]
+        total = value_kept[j] + value_got[j].astype(F32)
         for level in range(levels):
             rows = total.shape[0] // 2
             sent = total[rows:].astype(BF16)
@@ -364,14 +364,17 @@
             half_rows = total.shape[0] // 2
             if level < levels - 1:
                 total, given = total[:half_rows], total[half_rows:].astype(BF16)
-        grads.append(total.astype(BF16))
-    pairs = [
-        (flat(p, c, z), flat(z, c, p ^ turned(z, levels)))
-        for p in range(places)
-        for c in range(cores)
-        for z in range(tensor_count)
-    ]
-    grad_weight = lax.ppermute(jnp.concatenate(grads, axis=1), AXES, pairs).astype(F32)
+        total = total.astype(BF16)
+        if j == PARTS - 1:
+            total, policy_values = lax.optimization_barrier((total, policy_values))
+        pairs = [
+            (flat(p, c, z), flat(z, c, p ^ turned(z, levels)))
+            for p in range(places)
+            for c in range(cores)
+            for z in range(tensor_count)
+        ]
+        grads.append(lax.ppermute(total, AXES, pairs))
+    grad_weight = jnp.concatenate(grads, axis=1).astype(F32)
     return (policy_values.reshape(1, 1, slot_count, value_width), grad_weight)
 
 

time: 106 us -> 107 us (level)
  the two profiles are of different devices: /device:TPU:0 before, /device:TPU:4 now
where the time goes in v12:
time: 107 us
  starting transfers between devices  46.2 us (43%)
  waiting for transfers between devices  33 us (31%)
  Pallas kernels  11.7 us (11%)
  matrix products  7.62 us (7%)
  other arithmetic  5.95 us (6%)
  between operations  1.08 us (1%)
    ppermute x11, starting transfers between devices, crossed(): return lax.ppermute(array, 'tensor', [(i, i ^ step) for i in range(count)])  21.8 us
    ppermute x11, waiting for transfers between devices, crossed(): return lax.ppermute(array, 'tensor', [(i, i ^ step) for i in range(count)])  17.4 us
    ppermute x2, starting transfers between devices, on_device(): grads.append(lax.ppermute(total, AXES, pairs))  7.76 us
    pallas_call x1, Pallas kernels, on_device(): pl.pallas_call(functools.partial(prepare_kernel, tensor_count, steps), gr...  7.18 us
    dot_general x4, matrix products, dot(): return jnp.dot(a, b, preferred_element_type=F32)  6.67 us
    ppermute x2, waiting for transfers between devices, on_device(): grads.append(lax.ppermute(total, AXES, pairs))  6.32 us
    ppermute x4, waiting for transfers between devices, on_device(): total = total + lax.ppermute(given, 'dp', pairs).astype(F32)  4.68 us
    ppermute x3, waiting for transfers between devices, stage(): return (lax.ppermute(held, AXES, pairs), is_getter)  4.58 us
  transfers between devices with their start and end apart: 27, of which 13 were waited for; matrix products, arithmetic and copies ran while one was open for 12% of the time, Pallas kernels for 11%

profile of v12, /device:TPU:4, one launch (start us, length us, event | category | flops | bytes accessed | tf_op | source)
XLA Modules:
  0.0 106.5 jit_solution(1511577220275154620)
XLA Ops:
  0.6 1.7 %collective-permute-start = (bf16[1024,512]{1,0:T(8,128)(2,1)}, bf16[1024,512]{1,0:T(8,128)(2,1)}, u32[]{:S(2)}, u32[]{:S(2)}) collective-permute-start(bf16[1024,512]{1,0:T(8,128)(2,1)} %param.14), channel_id=1, source_target_pairs={{0,8},{9,1},{18,26},{27,19},{4,20},{13,29},{22,6},{31,15}} | collective-permute-start | bytes 3145736 | tf_op jit(solution)/shard_map/ppermute | solution.py:186
  2.9 7.2 %prepare.1 = (bf16[512,1024]{1,0:T(8,128)(2,1)}, bf16[512,1024]{1,0:T(8,128)(2,1)}, bf16[144,512]{1,0:T(8,128)(2,1)}, bf16[144,512]{1,0:T(8,128)(2,1)}, bf16[144...) custom-call(s32[2]{0:T(128)} %pad_add_fusion.1.at, bf16[512,2048]{1,0:T(8,128)(2,1)} %x_ref.1, f32[1,2048]{1,0:T(1,128)} %bitcast.32, ...), custom_call_target="tpu_custom_call" | custom-call | flops 1073741824 | bytes 8388608 | tf_op jit(solution)/shard_map/prepare/pallas_call | solution.py:198
  10.2 2.1 %slice_select_fusion = (bf16[1024,256]{1,0:T(8,128)(2,1)S(1)}, bf16[1024,256]{1,0:T(8,128)(2,1)}) fusion(bf16[1024,512]{1,0:T(8,128)(2,1)S(1)} %copy-done.7, bf16[1024,512]{1,0:T(8,128)(2,1)} %collective-permute-done, pred[]{:T(512)S(6)} %or.15), kind=kLoop, calls=%fused_computation.7 | loop fusion | flops 524288 | bytes 3145729 | tf_op jit(solution)/shard_map/jit(_where)/select_n | solution.py:248
  12.3 1.4 %collective-permute-start.3 = (bf16[1024,256]{1,0:T(8,128)(2,1)S(1)}, bf16[1024,256]{1,0:T(8,128)(2,1)}, u32[]{:S(2)}, u32[]{:S(2)}) collective-permute-start(bf16[1024,256]{1,0:T(8,128)(2,1)S(1)} %get-tuple-element.50), channel_id=1, source_target_pairs={{0,16},{9,25},{18,2},{27,11},{8,24},{1,17},{26,10},{19,3},{4,12},{... | collective-permute-start | bytes 1572872 | tf_op jit(solution)/shard_map/ppermute | solution.py:186
  13.7 1.7 %collective-permute-start.4 = (bf16[144,512]{1,0:T(8,128)(2,1)}, bf16[144,512]{1,0:T(8,128)(2,1)S(1)}, u32[]{:S(2)}, u32[]{:S(2)}) collective-permute-start(bf16[144,512]{1,0:T(8,128)(2,1)} %get-tuple-element.33), channel_id=1, source_target_pairs={{0,1},{1,0},{2,3},{3,2},{4,5},{5,4},{6,7},{7,6},{8,9},{9,8},{10,11... | collective-permute-start | bytes 442376 | tf_op jit(solution)/shard_map/ppermute | solution.py:37
  15.4 10.8 %collective-permute-start.5 = (bf16[144,512]{1,0:T(8,128)(2,1)}, bf16[144,512]{1,0:T(8,128)(2,1)S(1)}, u32[]{:S(2)}, u32[]{:S(2)}) collective-permute-start(bf16[144,512]{1,0:T(8,128)(2,1)} %get-tuple-element.34), channel_id=1, source_target_pairs={{0,2},{1,3},{2,0},{3,1},{4,6},{5,7},{6,4},{7,5},{8,10},{9,11},{10,... | collective-permute-start | bytes 442376 | tf_op jit(solution)/shard_map/ppermute | solution.py:37
  26.1 4.1 %all-to-all-start = ((bf16[8,32,512]{2,1,0:T(8,128)(2,1)}), bf16[8,32,512]{2,1,0:T(8,128)(2,1)S(1)}, u32[]{:S(2)}, u32[]{:S(2)}) async-start(bf16[8,32,512]{2,1,0:T(8,128)(2,1)} %bitcast.30), calls=%async_computation | async-start | bytes 524288 | tf_op jit(solution)/shard_map/all_to_all | solution.py:254
  31.6 2.2 %convolution_convert_fusion.1 = bf16[512,256]{1,0:T(8,128)(2,1)} fusion(bf16[512,1024]{1,0:T(8,128)(2,1)S(1)} %collective-permute-done.1.got_ref, bf16[1024,256]{1,0:T(8,128)(2,1)} %collective-permute-done.3, bf16[1024,256]{1,0:T(8,128)(2,1)S(1)} %get-tuple-element.50, pred[]{:T(512)S(6)} %or.18), kind=kOutput, calls=%fused_computation.2 | convolution fusion | flops 268828672 | bytes 2359297 | tf_op jit(solution)/shard_map/dot_general | solution.py:21
  33.8 1.8 %collective-permute-start.15 = (bf16[512,256]{1,0:T(8,128)(2,1)}, bf16[512,256]{1,0:T(8,128)(2,1)}, u32[]{:S(2)}, u32[]{:S(2)}) collective-permute-start(bf16[512,256]{1,0:T(8,128)(2,1)} %convolution_convert_fusion.1), channel_id=1, source_target_pairs={{0,4},{4,0},{8,12},{12,8},{16,20},{20,16},{24,28},{28,24},{1,5},{5... | collective-permute-start | bytes 786440 | tf_op jit(solution)/shard_map/ppermute | solution.py:29
  35.6 1.5 %fusion.2 = f32[512,256]{1,0:T(8,128)S(1)} fusion(bf16[512,1024]{1,0:T(8,128)(2,1)S(1)} %copy-done, bf16[1024,256]{1,0:T(8,128)(2,1)} %collective-permute-done.3, bf16[1024,256]{1,0:T(8,128)(2,1)} %copy-done.6, pred[]{:T(512)S(6)} %or.18), kind=kOutput, calls=%fused_computation.24 | convolution fusion | flops 268697600 | bytes 2621441 | tf_op jit(solution)/shard_map/dot_general | solution.py:21
  37.1 4.6 %collective-permute-done.2 = bf16[1024,256]{1,0:T(8,128)(2,1)} collective-permute-done((bf16[1024,256]{1,0:T(8,128)(2,1)}, bf16[1024,256]{1,0:T(8,128)(2,1)}, u32[]{:S(2)}, u32[]{:S(2)}) %collective-permute-start.2) | collective-permute-done | bytes 524320 | tf_op jit(solution)/shard_map/ppermute | solution.py:186
  41.6 1.5 %convolution_convert_fusion.2 = bf16[512,256]{1,0:T(8,128)(2,1)S(1)} fusion(bf16[512,1024]{1,0:T(8,128)(2,1)S(1)} %collective-permute-done.1.got_ref, bf16[1024,256]{1,0:T(8,128)(2,1)} %collective-permute-done.2, bf16[1024,256]{1,0:T(8,128)(2,1)} %get-tuple-element.51, pred[]{:T(512)S(6)} %or.18), kind=kOutput, calls=%fused_computation.3 | convolution fusion | flops 268828672 | bytes 2359297 | tf_op jit(solution)/shard_map/dot_general | solution.py:21
  46.2 1.5 %convolution_add_fusion = f32[512,256]{1,0:T(8,128)S(1)} fusion(bf16[512,1024]{1,0:T(8,128)(2,1)S(1)} %copy-done, bf16[512,256]{1,0:T(8,128)(2,1)S(1)} %collective-permute-done.7, bf16[1024,256]{1,0:T(8,128)(2,1)} %collective-permute-done.2, bf16[1024,256]{1,0:T(8,128)(2,1)} %get-tuple-element.51, pred[]{:T(512)S(6)} %or.18), kind=kOutput, calls=%fused_computation | convolution fusion | flops 268959744 | bytes 2883585 | tf_op jit(solution)/shard_map/dot_general | solution.py:21
  47.8 1.3 %collective-permute-start.8 = (bf16[256,256]{1,0:T(8,128)(2,1)S(1)}, bf16[256,256]{1,0:T(8,128)(2,1)S(1)}, u32[]{:S(2)}, u32[]{:S(2)}) collective-permute-start(bf16[256,256]{1,0:T(8,128)(2,1)S(1)} %slice.135), channel_id=1, source_target_pairs={{0,1},{1,0},{2,3},{3,2},{4,5},{5,4},{6,7},{7,6},{8,9},{9,8},{10,11... | collective-permute-start | bytes 393224 | tf_op jit(solution)/shard_map/ppermute | solution.py:37
  49.1 2.7 %collective-permute-done.16 = bf16[256,256]{1,0:T(8,128)(2,1)S(1)} collective-permute-done((bf16[256,256]{1,0:T(8,128)(2,1)S(1)}, bf16[256,256]{1,0:T(8,128)(2,1)S(1)}, u32[]{:S(2)}, u32[]{:S(2)}) %collective-permute-start.16) | collective-permute-done | bytes 131104 | tf_op jit(solution)/shard_map/ppermute | solution.py:37
  52.6 1.5 %collective-permute-done.8 = bf16[256,256]{1,0:T(8,128)(2,1)S(1)} collective-permute-done((bf16[256,256]{1,0:T(8,128)(2,1)S(1)}, bf16[256,256]{1,0:T(8,128)(2,1)S(1)}, u32[]{:S(2)}, u32[]{:S(2)}) %collective-permute-start.8) | collective-permute-done | bytes 131104 | tf_op jit(solution)/shard_map/ppermute | solution.py:37
  55.6 3.0 %collective-permute-done.17 = bf16[128,256]{1,0:T(8,128)(2,1)S(1)} collective-permute-done((bf16[128,256]{1,0:T(8,128)(2,1)S(1)}, bf16[128,256]{1,0:T(8,128)(2,1)S(1)}, u32[]{:S(2)}, u32[]{:S(2)}) %collective-permute-start.17) | collective-permute-done | bytes 65568 | tf_op jit(solution)/shard_map/ppermute | solution.py:37
  58.6 1.9 %collective-permute-done.9 = bf16[128,256]{1,0:T(8,128)(2,1)S(1)} collective-permute-done((bf16[128,256]{1,0:T(8,128)(2,1)S(1)}, bf16[128,256]{1,0:T(8,128)(2,1)S(1)}, u32[]{:S(2)}, u32[]{:S(2)}) %collective-permute-start.9) | collective-permute-done | bytes 65568 | tf_op jit(solution)/shard_map/ppermute | solution.py:37
  60.9 2.7 %collective-permute-start.10 = (bf16[128,256]{1,0:T(8,128)(2,1)S(1)}, bf16[128,256]{1,0:T(8,128)(2,1)S(1)}, u32[]{:S(2)}, u32[]{:S(2)}) collective-permute-start(bf16[128,256]{1,0:T(8,128)(2,1)S(1)} %get-tuple-element.55), channel_id=1, source_target_pairs={{0,2},{1,3},{2,0},{3,1},{4,6},{5,7},{6,4},{7,5},{8,10},{9,11},{10,... | collective-permute-start | bytes 196616 | tf_op jit(solution)/shard_map/ppermute | solution.py:37
  63.6 4.1 %collective-permute-done.18 = bf16[128,256]{1,0:T(8,128)(2,1)S(1)} collective-permute-done((bf16[128,256]{1,0:T(8,128)(2,1)S(1)}, bf16[128,256]{1,0:T(8,128)(2,1)S(1)}, u32[]{:S(2)}, u32[]{:S(2)}) %collective-permute-start.18) | collective-permute-done | bytes 65568 | tf_op jit(solution)/shard_map/ppermute | solution.py:37
  68.8 2.0 %collective-permute-start.11 = (bf16[256,256]{1,0:T(8,128)(2,1)S(1)}, bf16[256,256]{1,0:T(8,128)(2,1)S(1)}, u32[]{:S(2)}, u32[]{:S(2)}) collective-permute-start(bf16[256,256]{1,0:T(8,128)(2,1)S(1)} %pad_maximum_fusion.2), channel_id=1, source_target_pairs={{0,1},{1,0},{2,3},{3,2},{4,5},{5,4},{6,7},{7,6},{8,9},{9,8},{10,11... | collective-permute-start | bytes 393224 | tf_op jit(solution)/shard_map/ppermute | solution.py:37
  70.8 2.8 %collective-permute-done.19 = bf16[256,256]{1,0:T(8,128)(2,1)S(1)} collective-permute-done((bf16[256,256]{1,0:T(8,128)(2,1)S(1)}, bf16[256,256]{1,0:T(8,128)(2,1)S(1)}, u32[]{:S(2)}, u32[]{:S(2)}) %collective-permute-start.19) | collective-permute-done | bytes 131104 | tf_op jit(solution)/shard_map/ppermute | solution.py:37
  75.3 2.1 %gradient.3 = (f32[512,256]{1,0:T(8,128)S(1)}, bf16[512,256]{1,0:T(8,128)(2,1)}) custom-call(s32[4]{0:T(128)S(1)} %pad_add_fusion.at, bf16[512,1024]{1,0:T(8,128)(2,1)S(1)} %copy-done, bf16[512,1024]{1,0:T(8,128)(2,1)S(1)} %collective-permute-done.1.got_ref, bf16[512,256]{1,0:T(8,128)(2,1)S(1)} %pad_maximum_fusion.1.slope_ref, ...), custom_call_target="tpu_custom_call" | custom-call | flops 536870912 | bytes 4194304 | tf_op jit(solution)/shard_map/gradient/pallas_call | solution.py:326
  77.9 1.4 %gradient.2 = (f32[512,256]{1,0:T(8,128)S(1)}, bf16[512,256]{1,0:T(8,128)(2,1)S(1)}) custom-call(s32[4]{0:T(128)S(1)} %pad_add_fusion.at, bf16[512,1024]{1,0:T(8,128)(2,1)S(1)} %copy-done, bf16[512,1024]{1,0:T(8,128)(2,1)S(1)} %collective-permute-done.1.got_ref, bf16[512,256]{1,0:T(8,128)(2,1)S(1)} %pad_maximum_fusion.slope_ref, ...), custom_call_target="tpu_custom_call" | custom-call | flops 536870912 | bytes 4194304 | tf_op jit(solution)/shard_map/gradient/pallas_call | solution.py:326
  79.3 1.5 %collective-permute-start.13 = (bf16[512,256]{1,0:T(8,128)(2,1)S(1)}, bf16[512,256]{1,0:T(8,128)(2,1)S(1)}, u32[]{:S(2)}, u32[]{:S(2)}) collective-permute-start(bf16[512,256]{1,0:T(8,128)(2,1)S(1)} %get-tuple-element.40), channel_id=1, source_target_pairs={{0,8},{4,20},{8,0},{12,28},{16,24},{20,4},{24,16},{28,12},{1,9},{5... | collective-permute-start | bytes 786440 | tf_op jit(solution)/shard_map/ppermute | solution.py:363
  80.9 3.4 %all-to-all-start.1 = ((bf16[8,32,512]{2,1,0:T(8,128)(2,1)}), bf16[8,32,512]{2,1,0:T(8,128)(2,1)S(1)}, u32[]{:S(2)}, u32[]{:S(2)}) async-start(bf16[8,32,512]{2,1,0:T(8,128)(2,1)} %bitcast.28), calls=%async_computation.1 | async-start | bytes 524288 | tf_op jit(solution)/shard_map/all_to_all | solution.py:321
  85.3 1.4 %collective-permute-done.13 = bf16[512,256]{1,0:T(8,128)(2,1)S(1)} collective-permute-done((bf16[512,256]{1,0:T(8,128)(2,1)S(1)}, bf16[512,256]{1,0:T(8,128)(2,1)S(1)}, u32[]{:S(2)}, u32[]{:S(2)}) %collective-permute-start.13) | collective-permute-done | bytes 262176 | tf_op jit(solution)/shard_map/ppermute | solution.py:363
  87.5 3.3 %collective-permute-done.22 = bf16[256,256]{1,0:T(8,128)(2,1)S(1)} collective-permute-done((bf16[256,256]{1,0:T(8,128)(2,1)S(1)}, bf16[256,256]{1,0:T(8,128)(2,1)S(1)}, u32[]{:S(2)}, u32[]{:S(2)}) %collective-permute-start.22) | collective-permute-done | bytes 131104 | tf_op jit(solution)/shard_map/ppermute | solution.py:363
  90.8 4.3 %collective-permute-start.23 = (bf16[256,256]{1,0:T(8,128)(2,1)S(1)}, bf16[256,256]{1,0:T(8,128)(2,1)S(1)}, u32[]{:S(2)}, u32[]{:S(2)}) collective-permute-start(bf16[256,256]{1,0:T(8,128)(2,1)S(1)} %fusion), channel_id=1, source_target_pairs={{0,0},{1,10},{2,17},{3,27},{4,4},{5,14},{6,21},{7,31},{8,1},{9,11}... | collective-permute-start | bytes 393224 | tf_op jit(solution)/shard_map/ppermute | solution.py:376
  95.2 3.5 %collective-permute-start.24 = (bf16[256,256]{1,0:T(8,128)(2,1)S(1)}, bf16[256,256]{1,0:T(8,128)(2,1)S(1)}, u32[]{:S(2)}, u32[]{:S(2)}) collective-permute-start(bf16[256,256]{1,0:T(8,128)(2,1)S(1)} %fusion.1), channel_id=1, source_target_pairs={{0,0},{1,10},{2,17},{3,27},{4,4},{5,14},{6,21},{7,31},{8,1},{9,11}... | collective-permute-start | bytes 393224 | tf_op jit(solution)/shard_map/ppermute | solution.py:376
  98.6 2.5 %collective-permute-done.23 = bf16[256,256]{1,0:T(8,128)(2,1)S(1)} collective-permute-done((bf16[256,256]{1,0:T(8,128)(2,1)S(1)}, bf16[256,256]{1,0:T(8,128)(2,1)S(1)}, u32[]{:S(2)}, u32[]{:S(2)}) %collective-permute-start.23) | collective-permute-done | bytes 131104 | tf_op jit(solution)/shard_map/ppermute | solution.py:376
  101.2 3.8 %collective-permute-done.24 = bf16[256,256]{1,0:T(8,128)(2,1)S(1)} collective-permute-done((bf16[256,256]{1,0:T(8,128)(2,1)S(1)}, bf16[256,256]{1,0:T(8,128)(2,1)S(1)}, u32[]{:S(2)}, u32[]{:S(2)}) %collective-permute-start.24) | collective-permute-done | bytes 131104 | tf_op jit(solution)/shard_map/ppermute | solution.py:376
  (71 shorter events, 14.4 us)
Async XLA Ops:
  0.6 9.5 %collective-permute-start = (bf16[1024,512]{1,0:T(8,128)(2,1)}, bf16[1024,512]{1,0:T(8,128)(2,1)}, u32[]{:S(2)}, u32[]{:S(2)}) collective-permute-start(bf16[1024,512]{1,0:T(8,128)(2,1)} %param.14), channel_id=1, source_target_pairs={{0,8},{9,1},{18,26},{27,19},{4,20},{13,29},{22,6},{31,15}} | collective-permute-start | bytes 3145736 | tf_op jit(solution)/shard_map/ppermute | solution.py:186
  10.1 20.2 %collective-permute-start.1 = (bf16[512,1024]{1,0:T(8,128)(2,1)}, bf16[512,1024]{1,0:T(8,128)(2,1)S(1)}, u32[]{:S(2)}, u32[]{:S(2)}) collective-permute-start(bf16[512,1024]{1,0:T(8,128)(2,1)} %get-tuple-element.28), channel_id=1, source_target_pairs={{0,4},{4,0},{8,12},{12,8},{16,20},{20,16},{24,28},{28,24},{1,5},{5... | collective-permute-start | bytes 3145736 | tf_op jit(solution)/shard_map/ppermute | solution.py:29
  12.3 21.5 %copy-start.6 = (bf16[1024,256]{1,0:T(8,128)(2,1)}, bf16[1024,256]{1,0:T(8,128)(2,1)S(1)}, u32[]{:S(2)}) copy-start(bf16[1024,256]{1,0:T(8,128)(2,1)S(1)} %get-tuple-element.50) | copy-start | bytes 1572868
  12.3 23.3 %copy-start = (bf16[512,1024]{1,0:T(8,128)(2,1)S(1)}, bf16[512,1024]{1,0:T(8,128)(2,1)}, u32[]{:S(2)}) copy-start(bf16[512,1024]{1,0:T(8,128)(2,1)} %get-tuple-element.27.kept_ref) | copy-start | bytes 3145732
  12.3 19.3 %collective-permute-start.3 = (bf16[1024,256]{1,0:T(8,128)(2,1)S(1)}, bf16[1024,256]{1,0:T(8,128)(2,1)}, u32[]{:S(2)}, u32[]{:S(2)}) collective-permute-start(bf16[1024,256]{1,0:T(8,128)(2,1)S(1)} %get-tuple-element.50), channel_id=1, source_target_pairs={{0,16},{9,25},{18,2},{27,11},{8,24},{1,17},{26,10},{19,3},{4,12},{... | collective-permute-start | bytes 1572872 | tf_op jit(solution)/shard_map/ppermute | solution.py:186
  13.7 29.5 %collective-permute-start.4 = (bf16[144,512]{1,0:T(8,128)(2,1)}, bf16[144,512]{1,0:T(8,128)(2,1)S(1)}, u32[]{:S(2)}, u32[]{:S(2)}) collective-permute-start(bf16[144,512]{1,0:T(8,128)(2,1)} %get-tuple-element.33), channel_id=1, source_target_pairs={{0,1},{1,0},{2,3},{3,2},{4,5},{5,4},{6,7},{7,6},{8,9},{9,8},{10,11... | collective-permute-start | bytes 442376 | tf_op jit(solution)/shard_map/ppermute | solution.py:37
  15.4 27.9 %collective-permute-start.5 = (bf16[144,512]{1,0:T(8,128)(2,1)}, bf16[144,512]{1,0:T(8,128)(2,1)S(1)}, u32[]{:S(2)}, u32[]{:S(2)}) collective-permute-start(bf16[144,512]{1,0:T(8,128)(2,1)} %get-tuple-element.34), channel_id=1, source_target_pairs={{0,2},{1,3},{2,0},{3,1},{4,6},{5,7},{6,4},{7,5},{8,10},{9,11},{10,... | collective-permute-start | bytes 442376 | tf_op jit(solution)/shard_map/ppermute | solution.py:37
  26.1 17.1 %collective-permute-start.6 = (bf16[144,512]{1,0:T(8,128)(2,1)}, bf16[144,512]{1,0:T(8,128)(2,1)S(1)}, u32[]{:S(2)}, u32[]{:S(2)}) collective-permute-start(bf16[144,512]{1,0:T(8,128)(2,1)} %get-tuple-element.35), channel_id=1, source_target_pairs={{0,3},{1,2},{2,1},{3,0},{4,7},{5,6},{6,5},{7,4},{8,11},{9,10},{10,... | collective-permute-start | bytes 442376 | tf_op jit(solution)/shard_map/ppermute | solution.py:37
  26.1 10.9 %all-to-all-start = ((bf16[8,32,512]{2,1,0:T(8,128)(2,1)}), bf16[8,32,512]{2,1,0:T(8,128)(2,1)S(1)}, u32[]{:S(2)}, u32[]{:S(2)}) async-start(bf16[8,32,512]{2,1,0:T(8,128)(2,1)} %bitcast.30), calls=%async_computation | async-start | bytes 524288 | tf_op jit(solution)/shard_map/all_to_all | solution.py:254
  30.3 11.4 %collective-permute-start.2 = (bf16[1024,256]{1,0:T(8,128)(2,1)}, bf16[1024,256]{1,0:T(8,128)(2,1)}, u32[]{:S(2)}, u32[]{:S(2)}) collective-permute-start(bf16[1024,256]{1,0:T(8,128)(2,1)} %get-tuple-element.51), channel_id=1, source_target_pairs={{0,16},{9,25},{18,2},{27,11},{8,24},{1,17},{26,10},{19,3},{4,12},{... | collective-permute-start | bytes 1572872 | tf_op jit(solution)/shard_map/ppermute | solution.py:186
  33.8 9.5 %copy-start.3 = (s32[1,1,8]{2,1,0:T(1,128)S(1)}, s32[1,1,8]{2,1,0:T(1,128)}, u32[]{:S(2)}) copy-start(s32[1,1,8]{2,1,0:T(1,128)} %param.16) | copy-start | bytes 100
  33.8 9.5 %copy-start.4 = (f32[1,1,8]{2,1,0:T(1,128)S(1)}, f32[1,1,8]{2,1,0:T(1,128)}, u32[]{:S(2)}) copy-start(f32[1,1,8]{2,1,0:T(1,128)} %param.17) | copy-start | bytes 100
  33.8 9.5 %copy-start.5 = (f32[128]{0:T(128)S(1)}, f32[128]{0:T(128)}, u32[]{:S(2)}) copy-start(f32[128]{0:T(128)} %param.18) | copy-start | bytes 1540
  33.8 10.6 %collective-permute-start.15 = (bf16[512,256]{1,0:T(8,128)(2,1)}, bf16[512,256]{1,0:T(8,128)(2,1)}, u32[]{:S(2)}, u32[]{:S(2)}) collective-permute-start(bf16[512,256]{1,0:T(8,128)(2,1)} %convolution_convert_fusion.1), channel_id=1, source_target_pairs={{0,4},{4,0},{8,12},{12,8},{16,20},{20,16},{24,28},{28,24},{1,5},{5... | collective-permute-start | bytes 786440 | tf_op jit(solution)/shard_map/ppermute | solution.py:29
  43.1 3.1 %collective-permute-start.7 = (bf16[512,256]{1,0:T(8,128)(2,1)S(1)}, bf16[512,256]{1,0:T(8,128)(2,1)S(1)}, u32[]{:S(2)}, u32[]{:S(2)}) collective-permute-start(bf16[512,256]{1,0:T(8,128)(2,1)S(1)} %convolution_convert_fusion.2), channel_id=1, source_target_pairs={{0,4},{4,0},{8,12},{12,8},{16,20},{20,16},{24,28},{28,24},{1,5},{5... | collective-permute-start | bytes 786440 | tf_op jit(solution)/shard_map/ppermute | solution.py:29
  45.4 6.4 %collective-permute-start.16 = (bf16[256,256]{1,0:T(8,128)(2,1)S(1)}, bf16[256,256]{1,0:T(8,128)(2,1)S(1)}, u32[]{:S(2)}, u32[]{:S(2)}) collective-permute-start(bf16[256,256]{1,0:T(8,128)(2,1)S(1)} %slice.133), channel_id=1, source_target_pairs={{0,1},{1,0},{2,3},{3,2},{4,5},{5,4},{6,7},{7,6},{8,9},{9,8},{10,11... | collective-permute-start | bytes 393224 | tf_op jit(solution)/shard_map/ppermute | solution.py:37
  47.8 6.4 %collective-permute-start.8 = (bf16[256,256]{1,0:T(8,128)(2,1)S(1)}, bf16[256,256]{1,0:T(8,128)(2,1)S(1)}, u32[]{:S(2)}, u32[]{:S(2)}) collective-permute-start(bf16[256,256]{1,0:T(8,128)(2,1)S(1)} %slice.135), channel_id=1, source_target_pairs={{0,1},{1,0},{2,3},{3,2},{4,5},{5,4},{6,7},{7,6},{8,9},{9,8},{10,11... | collective-permute-start | bytes 393224 | tf_op jit(solution)/shard_map/ppermute | solution.py:37
  51.8 6.8 %collective-permute-start.17 = (bf16[128,256]{1,0:T(8,128)(2,1)S(1)}, bf16[128,256]{1,0:T(8,128)(2,1)S(1)}, u32[]{:S(2)}, u32[]{:S(2)}) collective-permute-start(bf16[128,256]{1,0:T(8,128)(2,1)S(1)} %slice.136), channel_id=1, source_target_pairs={{0,2},{1,3},{2,0},{3,1},{4,6},{5,7},{6,4},{7,5},{8,10},{9,11},{10,... | collective-permute-start | bytes 196616 | tf_op jit(solution)/shard_map/ppermute | solution.py:37
  54.2 6.3 %collective-permute-start.9 = (bf16[128,256]{1,0:T(8,128)(2,1)S(1)}, bf16[128,256]{1,0:T(8,128)(2,1)S(1)}, u32[]{:S(2)}, u32[]{:S(2)}) collective-permute-start(bf16[128,256]{1,0:T(8,128)(2,1)S(1)} %slice.137), channel_id=1, source_target_pairs={{0,2},{1,3},{2,0},{3,1},{4,6},{5,7},{6,4},{7,5},{8,10},{9,11},{10,... | collective-permute-start | bytes 196616 | tf_op jit(solution)/shard_map/ppermute | solution.py:37
  60.6 7.1 %collective-permute-start.18 = (bf16[128,256]{1,0:T(8,128)(2,1)S(1)}, bf16[128,256]{1,0:T(8,128)(2,1)S(1)}, u32[]{:S(2)}, u32[]{:S(2)}) collective-permute-start(bf16[128,256]{1,0:T(8,128)(2,1)S(1)} %get-tuple-element.56), channel_id=1, source_target_pairs={{0,2},{1,3},{2,0},{3,1},{4,6},{5,7},{6,4},{7,5},{8,10},{9,11},{10,... | collective-permute-start | bytes 196616 | tf_op jit(solution)/shard_map/ppermute | solution.py:37
  60.9 7.9 %collective-permute-start.10 = (bf16[128,256]{1,0:T(8,128)(2,1)S(1)}, bf16[128,256]{1,0:T(8,128)(2,1)S(1)}, u32[]{:S(2)}, u32[]{:S(2)}) collective-permute-start(bf16[128,256]{1,0:T(8,128)(2,1)S(1)} %get-tuple-element.55), channel_id=1, source_target_pairs={{0,2},{1,3},{2,0},{3,1},{4,6},{5,7},{6,4},{7,5},{8,10},{9,11},{10,... | collective-permute-start | bytes 196616 | tf_op jit(solution)/shard_map/ppermute | solution.py:37
  67.7 5.9 %collective-permute-start.19 = (bf16[256,256]{1,0:T(8,128)(2,1)S(1)}, bf16[256,256]{1,0:T(8,128)(2,1)S(1)}, u32[]{:S(2)}, u32[]{:S(2)}) collective-permute-start(bf16[256,256]{1,0:T(8,128)(2,1)S(1)} %pad_maximum_fusion.3), channel_id=1, source_target_pairs={{0,1},{1,0},{2,3},{3,2},{4,5},{5,4},{6,7},{7,6},{8,9},{9,8},{10,11... | collective-permute-start | bytes 393224 | tf_op jit(solution)/shard_map/ppermute | solution.py:37
  68.8 6.2 %collective-permute-start.11 = (bf16[256,256]{1,0:T(8,128)(2,1)S(1)}, bf16[256,256]{1,0:T(8,128)(2,1)S(1)}, u32[]{:S(2)}, u32[]{:S(2)}) collective-permute-start(bf16[256,256]{1,0:T(8,128)(2,1)S(1)} %pad_maximum_fusion.2), channel_id=1, source_target_pairs={{0,1},{1,0},{2,3},{3,2},{4,5},{5,4},{6,7},{7,6},{8,9},{9,8},{10,11... | collective-permute-start | bytes 393224 | tf_op jit(solution)/shard_map/ppermute | solution.py:37
  73.7 1.6 %collective-permute-start.20 = (bf16[512,256]{1,0:T(8,128)(2,1)S(1)}, bf16[512,256]{1,0:T(8,128)(2,1)S(1)}, u32[]{:S(2)}, u32[]{:S(2)}) collective-permute-start(bf16[512,256]{1,0:T(8,128)(2,1)S(1)} %pad_maximum_fusion.1.slope_ref), channel_id=1, source_target_pairs={{0,4},{4,0},{8,12},{12,8},{16,20},{20,16},{24,28},{28,24},{1,5},{5... | collective-permute-start | bytes 786440 | tf_op jit(solution)/shard_map/ppermute | solution.py:29
  75.1 2.9 %collective-permute-start.12 = (bf16[512,256]{1,0:T(8,128)(2,1)S(1)}, bf16[512,256]{1,0:T(8,128)(2,1)S(1)}, u32[]{:S(2)}, u32[]{:S(2)}) collective-permute-start(bf16[512,256]{1,0:T(8,128)(2,1)S(1)} %pad_maximum_fusion.slope_ref), channel_id=1, source_target_pairs={{0,4},{4,0},{8,12},{12,8},{16,20},{20,16},{24,28},{28,24},{1,5},{5... | collective-permute-start | bytes 786440 | tf_op jit(solution)/shard_map/ppermute | solution.py:29
  77.4 6.9 %collective-permute-start.21 = (bf16[512,256]{1,0:T(8,128)(2,1)}, bf16[512,256]{1,0:T(8,128)(2,1)}, u32[]{:S(2)}, u32[]{:S(2)}) collective-permute-start(bf16[512,256]{1,0:T(8,128)(2,1)} %get-tuple-element.48), channel_id=1, source_target_pairs={{0,8},{4,20},{8,0},{12,28},{16,24},{20,4},{24,16},{28,12},{1,9},{5... | collective-permute-start | bytes 786440 | tf_op jit(solution)/shard_map/ppermute | solution.py:363
  79.3 7.4 %collective-permute-start.13 = (bf16[512,256]{1,0:T(8,128)(2,1)S(1)}, bf16[512,256]{1,0:T(8,128)(2,1)S(1)}, u32[]{:S(2)}, u32[]{:S(2)}) collective-permute-start(bf16[512,256]{1,0:T(8,128)(2,1)S(1)} %get-tuple-element.40), channel_id=1, source_target_pairs={{0,8},{4,20},{8,0},{12,28},{16,24},{20,4},{24,16},{28,12},{1,9},{5... | collective-permute-start | bytes 786440 | tf_op jit(solution)/shard_map/ppermute | solution.py:363
  80.9 14.3 %all-to-all-start.1 = ((bf16[8,32,512]{2,1,0:T(8,128)(2,1)}), bf16[8,32,512]{2,1,0:T(8,128)(2,1)S(1)}, u32[]{:S(2)}, u32[]{:S(2)}) async-start(bf16[8,32,512]{2,1,0:T(8,128)(2,1)} %bitcast.28), calls=%async_computation.1 | async-start | bytes 524288 | tf_op jit(solution)/shard_map/all_to_all | solution.py:321
  85.3 5.5 %collective-permute-start.22 = (bf16[256,256]{1,0:T(8,128)(2,1)S(1)}, bf16[256,256]{1,0:T(8,128)(2,1)S(1)}, u32[]{:S(2)}, u32[]{:S(2)}) collective-permute-start(bf16[256,256]{1,0:T(8,128)(2,1)S(1)} %slice.132), channel_id=1, source_target_pairs={{0,16},{4,12},{8,24},{12,4},{16,0},{20,28},{24,8},{28,20},{1,17},{... | collective-permute-start | bytes 393224 | tf_op jit(solution)/shard_map/ppermute | solution.py:363
  86.8 8.3 %collective-permute-start.14 = (bf16[256,256]{1,0:T(8,128)(2,1)S(1)}, bf16[256,256]{1,0:T(8,128)(2,1)S(1)}, u32[]{:S(2)}, u32[]{:S(2)}) collective-permute-start(bf16[256,256]{1,0:T(8,128)(2,1)S(1)} %slice.134), channel_id=1, source_target_pairs={{0,16},{4,12},{8,24},{12,4},{16,0},{20,28},{24,8},{28,20},{1,17},{... | collective-permute-start | bytes 393224 | tf_op jit(solution)/shard_map/ppermute | solution.py:363
  90.8 10.4 %collective-permute-start.23 = (bf16[256,256]{1,0:T(8,128)(2,1)S(1)}, bf16[256,256]{1,0:T(8,128)(2,1)S(1)}, u32[]{:S(2)}, u32[]{:S(2)}) collective-permute-start(bf16[256,256]{1,0:T(8,128)(2,1)S(1)} %fusion), channel_id=1, source_target_pairs={{0,0},{1,10},{2,17},{3,27},{4,4},{5,14},{6,21},{7,31},{8,1},{9,11}... | collective-permute-start | bytes 393224 | tf_op jit(solution)/shard_map/ppermute | solution.py:376
  95.2 9.8 %collective-permute-start.24 = (bf16[256,256]{1,0:T(8,128)(2,1)S(1)}, bf16[256,256]{1,0:T(8,128)(2,1)S(1)}, u32[]{:S(2)}, u32[]{:S(2)}) collective-permute-start(bf16[256,256]{1,0:T(8,128)(2,1)S(1)} %fusion.1), channel_id=1, source_target_pairs={{0,0},{1,10},{2,17},{3,27},{4,4},{5,14},{6,21},{7,31},{8,1},{9,11}... | collective-permute-start | bytes 393224 | tf_op jit(solution)/shard_map/ppermute | solution.py:376
  (3 other events, 26.3 us)

commit v13 on v11

--- a/solution.py
+++ b/solution.py
@@ -265,7 +265,7 @@
     value_parts = []
     for j in range(PARTS):
         held_part, got_part, is_getter_part = parts[j]
-        if j == PARTS - 1:
+        if j == 0:
             got_part, got_cot = lax.optimization_barrier((got_part, got_cot))
         weight = jnp.where(is_getter_part, got_part, held_part)
         value_given = dot(got_rows, weight).astype(BF16)

time: 107 us -> 105 us (0.981)
  waiting for transfers between devices: 36.7 us -> 30.3 us
  starting transfers between devices: 45.5 us -> 47.8 us
  matrix products: 4.96 us -> 6.56 us
    all_to_all x1, starting transfers between devices: 12.2 us -> 3.36 us  [on_device(): got_cot = lax.all_to_all(cot, 'dp', split_axis=0, concat_axis=0, tiled=True)]
    ppermute x11, starting transfers between devices: 17.5 us -> 25.9 us  [crossed(): return lax.ppermute(array, 'tensor', [(i, i ^ step) for i in range(count)])]
    ppermute x11, waiting for transfers between devices: 17.8 us -> 13.1 us  [crossed(): return lax.ppermute(array, 'tensor', [(i, i ^ step) for i in range(count)])]
    all_to_all x1, starting transfers between devices: 4.23 us -> 6.98 us  [on_device(): lax.all_to_all(sent, 'dp', split_axis=0, concat_axis=0, tiled=True)]
    all_to_all x1, waiting for transfers between devices: 4.46 us -> 2.69 us  [on_device(): got_cot = lax.all_to_all(cot, 'dp', split_axis=0, concat_axis=0, tiled=True)]
    dot_general x4, matrix products: 4 us -> 5.61 us  [dot(): return jnp.dot(a, b, preferred_element_type=F32)]
    unnamed x25 -> x23, local copies, waits for them, and re-layouts: 1.74 us -> 2.52 us
  transfers between devices with their start and end apart: 26 -> 26, of which waited for: 13 -> 12; matrix products, arithmetic and copies ran while one was open for 8% -> 10% of each run, Pallas kernels for 11% -> 11%
where the time goes in v13:
time: 105 us; the launch traced here: 104 us
  starting transfers between devices  47.8 us (46%)
  waiting for transfers between devices  30.3 us (29%)
  Pallas kernels  11.6 us (11%)
  matrix products  6.56 us (6%)
  other arithmetic  4.47 us (4%)
  local copies, waits for them, and re-layouts  2.7 us (3%)
    ppermute x11, starting transfers between devices, crossed(): return lax.ppermute(array, 'tensor', [(i, i ^ step) for i in range(count)])  25.9 us
    ppermute x11, waiting for transfers between devices, crossed(): return lax.ppermute(array, 'tensor', [(i, i ^ step) for i in range(count)])  13.1 us
    ppermute x1, waiting for transfers between devices, on_device(): grad_weight = lax.ppermute(grad, AXES, pairs).astype(F32)  9.73 us
    pallas_call x1, Pallas kernels, on_device(): pl.pallas_call(functools.partial(prepare_kernel, tensor_count, steps), gr...  7.01 us
    all_to_all x1, starting transfers between devices, on_device(): lax.all_to_all(sent, 'dp', split_axis=0, concat_axis=0, tiled=True)  6.98 us
    dot_general x4, matrix products, dot(): return jnp.dot(a, b, preferred_element_type=F32)  5.61 us
    ppermute x4, waiting for transfers between devices, on_device(): total = total + lax.ppermute(given, 'dp', pairs).astype(F32)  4.69 us
    ppermute x4, starting transfers between devices, on_device(): total = total + lax.ppermute(given, 'dp', pairs).astype(F32)  4.25 us
  transfers between devices with their start and end apart: 26, of which 12 were waited for; matrix products, arithmetic and copies ran while one was open for 10% of the time, Pallas kernels for 11%

profile of v13, /device:TPU:4, one launch (start us, length us, event | category | flops | bytes accessed | tf_op | source)
XLA Modules:
  0.0 104.3 jit_solution(2891332981865531230)
XLA Ops:
  2.0 7.0 %prepare.1 = (bf16[512,1024]{1,0:T(8,128)(2,1)}, bf16[512,1024]{1,0:T(8,128)(2,1)}, bf16[144,512]{1,0:T(8,128)(2,1)}, bf16[144,512]{1,0:T(8,128)(2,1)}, bf16[144...) custom-call(s32[2]{0:T(128)} %pad_add_fusion.1.at, bf16[512,2048]{1,0:T(8,128)(2,1)} %x_ref.1, f32[1,2048]{1,0:T(1,128)} %bitcast.31, ...), custom_call_target="tpu_custom_call" | custom-call | flops 1073741824 | bytes 8388608 | tf_op jit(solution)/shard_map/prepare/pallas_call | solution.py:198
  10.4 1.6 %slice_select_fusion = (bf16[1024,256]{1,0:T(8,128)(2,1)S(1)}, bf16[1024,256]{1,0:T(8,128)(2,1)S(1)}) fusion(bf16[1024,512]{1,0:T(8,128)(2,1)} %param.14, bf16[1024,512]{1,0:T(8,128)(2,1)} %copy-done.8, pred[]{:T(512)S(6)} %or.15), kind=kLoop, calls=%fused_computation.7 | loop fusion | flops 524288 | bytes 3145729 | tf_op jit(solution)/shard_map/jit(_where)/select_n | solution.py:248
  12.1 1.3 %collective-permute-start.11 = (bf16[1024,256]{1,0:T(8,128)(2,1)S(1)}, bf16[1024,256]{1,0:T(8,128)(2,1)S(1)}, u32[]{:S(2)}, u32[]{:S(2)}) collective-permute-start(bf16[1024,256]{1,0:T(8,128)(2,1)S(1)} %get-tuple-element.48), channel_id=1, source_target_pairs={{0,16},{9,25},{18,2},{27,11},{8,24},{1,17},{26,10},{19,3},{4,12},{... | collective-permute-start | bytes 1572872 | tf_op jit(solution)/shard_map/ppermute | solution.py:186
  13.4 1.3 %collective-permute-start.2 = (bf16[1024,256]{1,0:T(8,128)(2,1)S(1)}, bf16[1024,256]{1,0:T(8,128)(2,1)}, u32[]{:S(2)}, u32[]{:S(2)}) collective-permute-start(bf16[1024,256]{1,0:T(8,128)(2,1)S(1)} %get-tuple-element.49), channel_id=1, source_target_pairs={{0,16},{9,25},{18,2},{27,11},{8,24},{1,17},{26,10},{19,3},{4,12},{... | collective-permute-start | bytes 1572872 | tf_op jit(solution)/shard_map/ppermute | solution.py:186
  14.7 1.3 %collective-permute-start.3 = (bf16[144,512]{1,0:T(8,128)(2,1)}, bf16[144,512]{1,0:T(8,128)(2,1)S(1)}, u32[]{:S(2)}, u32[]{:S(2)}) collective-permute-start(bf16[144,512]{1,0:T(8,128)(2,1)} %get-tuple-element.32), channel_id=1, source_target_pairs={{0,1},{1,0},{2,3},{3,2},{4,5},{5,4},{6,7},{7,6},{8,9},{9,8},{10,11... | collective-permute-start | bytes 442376 | tf_op jit(solution)/shard_map/ppermute | solution.py:37
  16.0 11.8 %collective-permute-start.4 = (bf16[144,512]{1,0:T(8,128)(2,1)}, bf16[144,512]{1,0:T(8,128)(2,1)S(1)}, u32[]{:S(2)}, u32[]{:S(2)}) collective-permute-start(bf16[144,512]{1,0:T(8,128)(2,1)} %get-tuple-element.33), channel_id=1, source_target_pairs={{0,2},{1,3},{2,0},{3,1},{4,6},{5,7},{6,4},{7,5},{8,10},{9,11},{10,... | collective-permute-start | bytes 442376 | tf_op jit(solution)/shard_map/ppermute | solution.py:37
  27.7 3.4 %all-to-all-start = ((bf16[8,32,512]{2,1,0:T(8,128)(2,1)}), bf16[8,32,512]{2,1,0:T(8,128)(2,1)S(1)}, u32[]{:S(2)}, u32[]{:S(2)}) async-start(bf16[8,32,512]{2,1,0:T(8,128)(2,1)} %bitcast.13), calls=%async_computation | async-start | bytes 524288 | tf_op jit(solution)/shard_map/all_to_all | solution.py:254
  32.8 1.1 %convolution_convert_fusion.1 = bf16[512,256]{1,0:T(8,128)(2,1)} fusion(bf16[512,1024]{1,0:T(8,128)(2,1)S(1)} %collective-permute-done.1.got_ref, bf16[1024,256]{1,0:T(8,128)(2,1)S(1)} %collective-permute-done.11, bf16[1024,256]{1,0:T(8,128)(2,1)S(1)} %get-tuple-element.48, pred[]{:T(512)S(6)} %or.18), kind=kOutput, calls=%fused_computation.3 | convolution fusion | flops 268828672 | bytes 2359297 | tf_op jit(solution)/shard_map/dot_general | solution.py:21
  33.9 2.7 %all-to-all-done = bf16[8,32,512]{2,1,0:T(8,128)(2,1)S(1)} async-done(((bf16[8,32,512]{2,1,0:T(8,128)(2,1)}), bf16[8,32,512]{2,1,0:T(8,128)(2,1)S(1)}, u32[]{:S(2)}, u32[]{:S(2)}) %all-to-all-start) | async-done | bytes 262176 | tf_op jit(solution)/shard_map/all_to_all | solution.py:254
  36.6 1.6 %convolution_convert_fusion.2 = bf16[512,256]{1,0:T(8,128)(2,1)S(1)} fusion(bf16[512,1024]{1,0:T(8,128)(2,1)S(1)} %collective-permute-done.1.got_ref, bf16[1024,256]{1,0:T(8,128)(2,1)} %collective-permute-done.2, bf16[1024,256]{1,0:T(8,128)(2,1)S(1)} %get-tuple-element.49, pred[]{:T(512)S(6)} %or.18), kind=kOutput, calls=%fused_computation.4 | convolution fusion | flops 268828672 | bytes 2359297 | tf_op jit(solution)/shard_map/dot_general | solution.py:21
  40.3 1.4 %convolution_add_fusion = f32[512,256]{1,0:T(8,128)S(1)} fusion(bf16[512,1024]{1,0:T(8,128)(2,1)S(1)} %copy-done, bf16[512,256]{1,0:T(8,128)(2,1)} %collective-permute-done.12, bf16[1024,256]{1,0:T(8,128)(2,1)S(1)} %copy-done.10, bf16[1024,256]{1,0:T(8,128)(2,1)S(1)} %copy-done.7, pred[]{:T(512)S(6)} %or.18), kind=kOutput, calls=%fused_computation | convolution fusion | flops 268959744 | bytes 2883585 | tf_op jit(solution)/shard_map/dot_general | solution.py:21
  41.7 2.7 %collective-permute-start.13 = (bf16[256,256]{1,0:T(8,128)(2,1)S(1)}, bf16[256,256]{1,0:T(8,128)(2,1)S(1)}, u32[]{:S(2)}, u32[]{:S(2)}) collective-permute-start(bf16[256,256]{1,0:T(8,128)(2,1)S(1)} %slice.134), channel_id=1, source_target_pairs={{0,1},{1,0},{2,3},{3,2},{4,5},{5,4},{6,7},{7,6},{8,9},{9,8},{10,11... | collective-permute-start | bytes 393224 | tf_op jit(solution)/shard_map/ppermute | solution.py:37
  44.4 1.5 %convolution_add_fusion.1 = f32[512,256]{1,0:T(8,128)S(1)} fusion(bf16[512,1024]{1,0:T(8,128)(2,1)S(1)} %copy-done, bf16[512,256]{1,0:T(8,128)(2,1)S(1)} %collective-permute-done.6, bf16[1024,256]{1,0:T(8,128)(2,1)} %collective-permute-done.2, bf16[1024,256]{1,0:T(8,128)(2,1)S(1)} %get-tuple-element.49, pred[]{:T(512)S(6)} %or.18), kind=kOutput, calls=%fused_computation.1 | convolution fusion | flops 268959744 | bytes 2883585 | tf_op jit(solution)/shard_map/dot_general | solution.py:21
  46.1 2.4 %collective-permute-done.13 = bf16[256,256]{1,0:T(8,128)(2,1)S(1)} collective-permute-done((bf16[256,256]{1,0:T(8,128)(2,1)S(1)}, bf16[256,256]{1,0:T(8,128)(2,1)S(1)}, u32[]{:S(2)}, u32[]{:S(2)}) %collective-permute-start.13) | collective-permute-done | bytes 131104 | tf_op jit(solution)/shard_map/ppermute | solution.py:37
  48.5 2.0 %collective-permute-start.14 = (bf16[128,256]{1,0:T(8,128)(2,1)S(1)}, bf16[128,256]{1,0:T(8,128)(2,1)S(1)}, u32[]{:S(2)}, u32[]{:S(2)}) collective-permute-start(bf16[128,256]{1,0:T(8,128)(2,1)S(1)} %slice.136), channel_id=1, source_target_pairs={{0,2},{1,3},{2,0},{3,1},{4,6},{5,7},{6,4},{7,5},{8,10},{9,11},{10,... | collective-permute-start | bytes 196616 | tf_op jit(solution)/shard_map/ppermute | solution.py:37
  50.5 1.2 %collective-permute-done.7 = bf16[256,256]{1,0:T(8,128)(2,1)S(1)} collective-permute-done((bf16[256,256]{1,0:T(8,128)(2,1)S(1)}, bf16[256,256]{1,0:T(8,128)(2,1)S(1)}, u32[]{:S(2)}, u32[]{:S(2)}) %collective-permute-start.7) | collective-permute-done | bytes 131104 | tf_op jit(solution)/shard_map/ppermute | solution.py:37
  52.7 1.1 %collective-permute-done.14 = bf16[128,256]{1,0:T(8,128)(2,1)S(1)} collective-permute-done((bf16[128,256]{1,0:T(8,128)(2,1)S(1)}, bf16[128,256]{1,0:T(8,128)(2,1)S(1)}, u32[]{:S(2)}, u32[]{:S(2)}) %collective-permute-start.14) | collective-permute-done | bytes 65568 | tf_op jit(solution)/shard_map/ppermute | solution.py:37
  53.8 3.2 %collective-permute-done.8 = bf16[128,256]{1,0:T(8,128)(2,1)S(1)} collective-permute-done((bf16[128,256]{1,0:T(8,128)(2,1)S(1)}, bf16[128,256]{1,0:T(8,128)(2,1)S(1)}, u32[]{:S(2)}, u32[]{:S(2)}) %collective-permute-start.8) | collective-permute-done | bytes 65568 | tf_op jit(solution)/shard_map/ppermute | solution.py:37
  58.0 2.0 %collective-permute-start.9 = (bf16[128,256]{1,0:T(8,128)(2,1)S(1)}, bf16[128,256]{1,0:T(8,128)(2,1)S(1)}, u32[]{:S(2)}, u32[]{:S(2)}) collective-permute-start(bf16[128,256]{1,0:T(8,128)(2,1)S(1)} %get-tuple-element.54), channel_id=1, source_target_pairs={{0,2},{1,3},{2,0},{3,1},{4,6},{5,7},{6,4},{7,5},{8,10},{9,11},{10,... | collective-permute-start | bytes 196616 | tf_op jit(solution)/shard_map/ppermute | solution.py:37
  60.1 2.3 %collective-permute-done.18 = bf16[128,256]{1,0:T(8,128)(2,1)S(1)} collective-permute-done((bf16[128,256]{1,0:T(8,128)(2,1)S(1)}, bf16[128,256]{1,0:T(8,128)(2,1)S(1)}, u32[]{:S(2)}, u32[]{:S(2)}) %collective-permute-start.18) | collective-permute-done | bytes 65568 | tf_op jit(solution)/shard_map/ppermute | solution.py:37
  62.4 1.4 %collective-permute-start.19 = (bf16[256,256]{1,0:T(8,128)(2,1)S(1)}, bf16[256,256]{1,0:T(8,128)(2,1)S(1)}, u32[]{:S(2)}, u32[]{:S(2)}) collective-permute-start(bf16[256,256]{1,0:T(8,128)(2,1)S(1)} %pad_maximum_fusion.4), channel_id=1, source_target_pairs={{0,1},{1,0},{2,3},{3,2},{4,5},{5,4},{6,7},{7,6},{8,9},{9,8},{10,11... | collective-permute-start | bytes 393224 | tf_op jit(solution)/shard_map/ppermute | solution.py:37
  63.9 1.9 %collective-permute-start.10 = (bf16[256,256]{1,0:T(8,128)(2,1)S(1)}, bf16[256,256]{1,0:T(8,128)(2,1)S(1)}, u32[]{:S(2)}, u32[]{:S(2)}) collective-permute-start(bf16[256,256]{1,0:T(8,128)(2,1)S(1)} %pad_maximum_fusion.3), channel_id=1, source_target_pairs={{0,1},{1,0},{2,3},{3,2},{4,5},{5,4},{6,7},{7,6},{8,9},{9,8},{10,11... | collective-permute-start | bytes 393224 | tf_op jit(solution)/shard_map/ppermute | solution.py:37
  65.8 1.7 %collective-permute-done.19 = bf16[256,256]{1,0:T(8,128)(2,1)S(1)} collective-permute-done((bf16[256,256]{1,0:T(8,128)(2,1)S(1)}, bf16[256,256]{1,0:T(8,128)(2,1)S(1)}, u32[]{:S(2)}, u32[]{:S(2)}) %collective-permute-start.19) | collective-permute-done | bytes 131104 | tf_op jit(solution)/shard_map/ppermute | solution.py:37
  69.2 2.1 %gradient.3 = (f32[512,256]{1,0:T(8,128)S(1)}, bf16[512,256]{1,0:T(8,128)(2,1)}) custom-call(s32[4]{0:T(128)S(1)} %pad_add_fusion.at, bf16[512,1024]{1,0:T(8,128)(2,1)S(1)} %copy-done, bf16[512,1024]{1,0:T(8,128)(2,1)S(1)} %collective-permute-done.1.got_ref, bf16[512,256]{1,0:T(8,128)(2,1)S(1)} %pad_maximum_fusion.1.slope_ref, ...), custom_call_target="tpu_custom_call" | custom-call | flops 536870912 | bytes 4194304 | tf_op jit(solution)/shard_map/gradient/pallas_call | solution.py:326
  71.3 1.5 %collective-permute-start.21 = (bf16[512,256]{1,0:T(8,128)(2,1)}, bf16[512,256]{1,0:T(8,128)(2,1)}, u32[]{:S(2)}, u32[]{:S(2)}) collective-permute-start(bf16[512,256]{1,0:T(8,128)(2,1)} %get-tuple-element.44), channel_id=1, source_target_pairs={{0,8},{4,20},{8,0},{12,28},{16,24},{20,4},{24,16},{28,12},{1,9},{5... | collective-permute-start | bytes 786440 | tf_op jit(solution)/shard_map/ppermute | solution.py:363
  72.8 1.4 %gradient.2 = (f32[512,256]{1,0:T(8,128)S(1)}, bf16[512,256]{1,0:T(8,128)(2,1)S(1)}) custom-call(s32[4]{0:T(128)S(1)} %pad_add_fusion.at, bf16[512,1024]{1,0:T(8,128)(2,1)S(1)} %copy-done, bf16[512,1024]{1,0:T(8,128)(2,1)S(1)} %collective-permute-done.1.got_ref, bf16[512,256]{1,0:T(8,128)(2,1)S(1)} %pad_maximum_fusion.slope_ref, ...), custom_call_target="tpu_custom_call" | custom-call | flops 536870912 | bytes 4194304 | tf_op jit(solution)/shard_map/gradient/pallas_call | solution.py:326
  74.8 7.0 %all-to-all-start.1 = ((bf16[8,32,512]{2,1,0:T(8,128)(2,1)}), bf16[8,32,512]{2,1,0:T(8,128)(2,1)S(1)}, u32[]{:S(2)}, u32[]{:S(2)}) async-start(bf16[8,32,512]{2,1,0:T(8,128)(2,1)} %bitcast.28), calls=%async_computation.1 | async-start | bytes 524288 | tf_op jit(solution)/shard_map/all_to_all | solution.py:321
  83.0 2.0 %collective-permute-start.17 = (bf16[256,256]{1,0:T(8,128)(2,1)S(1)}, bf16[256,256]{1,0:T(8,128)(2,1)S(1)}, u32[]{:S(2)}, u32[]{:S(2)}) collective-permute-start(bf16[256,256]{1,0:T(8,128)(2,1)S(1)} %slice.133), channel_id=1, source_target_pairs={{0,16},{4,12},{8,24},{12,4},{16,0},{20,28},{24,8},{28,20},{1,17},{... | collective-permute-start | bytes 393224 | tf_op jit(solution)/shard_map/ppermute | solution.py:363
  85.0 3.3 %collective-permute-done.22 = bf16[256,256]{1,0:T(8,128)(2,1)S(1)} collective-permute-done((bf16[256,256]{1,0:T(8,128)(2,1)S(1)}, bf16[256,256]{1,0:T(8,128)(2,1)S(1)}, u32[]{:S(2)}, u32[]{:S(2)}) %collective-permute-start.22) | collective-permute-done | bytes 131104 | tf_op jit(solution)/shard_map/ppermute | solution.py:363
  88.4 1.4 %collective-permute-done.17 = bf16[256,256]{1,0:T(8,128)(2,1)S(1)} collective-permute-done((bf16[256,256]{1,0:T(8,128)(2,1)S(1)}, bf16[256,256]{1,0:T(8,128)(2,1)S(1)}, u32[]{:S(2)}, u32[]{:S(2)}) %collective-permute-start.17) | collective-permute-done | bytes 131104 | tf_op jit(solution)/shard_map/ppermute | solution.py:363
  89.8 3.2 %collective-permute-start.23 = (bf16[256,512]{1,0:T(8,128)(2,1)S(1)}, bf16[256,512]{1,0:T(8,128)(2,1)S(1)}, u32[]{:S(2)}, u32[]{:S(2)}) collective-permute-start(bf16[256,512]{1,0:T(8,128)(2,1)S(1)} %pad_maximum_fusion.2), channel_id=1, source_target_pairs={{0,0},{1,10},{2,17},{3,27},{4,4},{5,14},{6,21},{7,31},{8,1},{9,11}... | collective-permute-start | bytes 786440 | tf_op jit(solution)/shard_map/ppermute | solution.py:375
  93.0 9.7 %collective-permute-done.23 = bf16[256,512]{1,0:T(8,128)(2,1)S(1)} collective-permute-done((bf16[256,512]{1,0:T(8,128)(2,1)S(1)}, bf16[256,512]{1,0:T(8,128)(2,1)S(1)}, u32[]{:S(2)}, u32[]{:S(2)}) %collective-permute-start.23) | collective-permute-done | bytes 262176 | tf_op jit(solution)/shard_map/ppermute | solution.py:375
  (75 shorter events, 13.8 us)
Async XLA Ops:
  0.6 8.8 %collective-permute-start = (bf16[1024,512]{1,0:T(8,128)(2,1)}, bf16[1024,512]{1,0:T(8,128)(2,1)S(1)}, u32[]{:S(2)}, u32[]{:S(2)}) collective-permute-start(bf16[1024,512]{1,0:T(8,128)(2,1)} %param.14), channel_id=1, source_target_pairs={{0,8},{9,1},{18,26},{27,19},{4,20},{13,29},{22,6},{31,15}} | collective-permute-start | bytes 3145736 | tf_op jit(solution)/shard_map/ppermute | solution.py:186
  9.0 22.1 %collective-permute-start.1 = (bf16[512,1024]{1,0:T(8,128)(2,1)}, bf16[512,1024]{1,0:T(8,128)(2,1)S(1)}, u32[]{:S(2)}, u32[]{:S(2)}) collective-permute-start(bf16[512,1024]{1,0:T(8,128)(2,1)} %get-tuple-element.27), channel_id=1, source_target_pairs={{0,4},{4,0},{8,12},{12,8},{16,20},{20,16},{24,28},{28,24},{1,5},{5... | collective-permute-start | bytes 3145736 | tf_op jit(solution)/shard_map/ppermute | solution.py:29
  12.0 19.9 %copy-start.6 = (bf16[1024,256]{1,0:T(8,128)(2,1)}, bf16[1024,256]{1,0:T(8,128)(2,1)S(1)}, u32[]{:S(2)}) copy-start(bf16[1024,256]{1,0:T(8,128)(2,1)S(1)} %get-tuple-element.48) | copy-start | bytes 1572868
  12.1 19.9 %collective-permute-start.11 = (bf16[1024,256]{1,0:T(8,128)(2,1)S(1)}, bf16[1024,256]{1,0:T(8,128)(2,1)S(1)}, u32[]{:S(2)}, u32[]{:S(2)}) collective-permute-start(bf16[1024,256]{1,0:T(8,128)(2,1)S(1)} %get-tuple-element.48), channel_id=1, source_target_pairs={{0,16},{9,25},{18,2},{27,11},{8,24},{1,17},{26,10},{19,3},{4,12},{... | collective-permute-start | bytes 1572872 | tf_op jit(solution)/shard_map/ppermute | solution.py:186
  13.4 23.3 %collective-permute-start.2 = (bf16[1024,256]{1,0:T(8,128)(2,1)S(1)}, bf16[1024,256]{1,0:T(8,128)(2,1)}, u32[]{:S(2)}, u32[]{:S(2)}) collective-permute-start(bf16[1024,256]{1,0:T(8,128)(2,1)S(1)} %get-tuple-element.49), channel_id=1, source_target_pairs={{0,16},{9,25},{18,2},{27,11},{8,24},{1,17},{26,10},{19,3},{4,12},{... | collective-permute-start | bytes 1572872 | tf_op jit(solution)/shard_map/ppermute | solution.py:186
  14.7 23.6 %collective-permute-start.3 = (bf16[144,512]{1,0:T(8,128)(2,1)}, bf16[144,512]{1,0:T(8,128)(2,1)S(1)}, u32[]{:S(2)}, u32[]{:S(2)}) collective-permute-start(bf16[144,512]{1,0:T(8,128)(2,1)} %get-tuple-element.32), channel_id=1, source_target_pairs={{0,1},{1,0},{2,3},{3,2},{4,5},{5,4},{6,7},{7,6},{8,9},{9,8},{10,11... | collective-permute-start | bytes 442376 | tf_op jit(solution)/shard_map/ppermute | solution.py:37
  16.0 22.4 %collective-permute-start.4 = (bf16[144,512]{1,0:T(8,128)(2,1)}, bf16[144,512]{1,0:T(8,128)(2,1)S(1)}, u32[]{:S(2)}, u32[]{:S(2)}) collective-permute-start(bf16[144,512]{1,0:T(8,128)(2,1)} %get-tuple-element.33), channel_id=1, source_target_pairs={{0,2},{1,3},{2,0},{3,1},{4,6},{5,7},{6,4},{7,5},{8,10},{9,11},{10,... | collective-permute-start | bytes 442376 | tf_op jit(solution)/shard_map/ppermute | solution.py:37
  27.7 8.9 %all-to-all-start = ((bf16[8,32,512]{2,1,0:T(8,128)(2,1)}), bf16[8,32,512]{2,1,0:T(8,128)(2,1)S(1)}, u32[]{:S(2)}, u32[]{:S(2)}) async-start(bf16[8,32,512]{2,1,0:T(8,128)(2,1)} %bitcast.13), calls=%async_computation | async-start | bytes 524288 | tf_op jit(solution)/shard_map/all_to_all | solution.py:254
  31.1 8.1 %copy-start.1 = (bf16[144,512]{1,0:T(8,128)(2,1)S(1)}, bf16[144,512]{1,0:T(8,128)(2,1)}, u32[]{:S(2)}) copy-start(bf16[144,512]{1,0:T(8,128)(2,1)} %get-tuple-element.31.refs_0_) | copy-start | bytes 442372
  31.1 8.1 %copy-start.2 = (s32[1,1,8]{2,1,0:T(1,128)S(1)}, s32[1,1,8]{2,1,0:T(1,128)}, u32[]{:S(2)}) copy-start(s32[1,1,8]{2,1,0:T(1,128)} %param.15) | copy-start | bytes 100
  31.1 8.0 %copy-start.3 = (s32[1,1,8]{2,1,0:T(1,128)S(1)}, s32[1,1,8]{2,1,0:T(1,128)}, u32[]{:S(2)}) copy-start(s32[1,1,8]{2,1,0:T(1,128)} %param.16) | copy-start | bytes 100
  31.2 8.0 %copy-start.4 = (f32[1,1,8]{2,1,0:T(1,128)S(1)}, f32[1,1,8]{2,1,0:T(1,128)}, u32[]{:S(2)}) copy-start(f32[1,1,8]{2,1,0:T(1,128)} %param.17) | copy-start | bytes 100
  31.2 8.0 %copy-start.5 = (f32[128]{0:T(128)S(1)}, f32[128]{0:T(128)}, u32[]{:S(2)}) copy-start(f32[128]{0:T(128)} %param.18) | copy-start | bytes 1540
  31.2 8.0 %collective-permute-start.5 = (bf16[144,512]{1,0:T(8,128)(2,1)}, bf16[144,512]{1,0:T(8,128)(2,1)S(1)}, u32[]{:S(2)}, u32[]{:S(2)}) collective-permute-start(bf16[144,512]{1,0:T(8,128)(2,1)} %get-tuple-element.34), channel_id=1, source_target_pairs={{0,3},{1,2},{2,1},{3,0},{4,7},{5,6},{6,5},{7,4},{8,11},{9,10},{10,... | collective-permute-start | bytes 442376 | tf_op jit(solution)/shard_map/ppermute | solution.py:37
  33.9 6.4 %collective-permute-start.12 = (bf16[512,256]{1,0:T(8,128)(2,1)}, bf16[512,256]{1,0:T(8,128)(2,1)}, u32[]{:S(2)}, u32[]{:S(2)}) collective-permute-start(bf16[512,256]{1,0:T(8,128)(2,1)} %convolution_convert_fusion.1), channel_id=1, source_target_pairs={{0,4},{4,0},{8,12},{12,8},{16,20},{20,16},{24,28},{28,24},{1,5},{5... | collective-permute-start | bytes 786440 | tf_op jit(solution)/shard_map/ppermute | solution.py:29
  38.2 6.2 %collective-permute-start.6 = (bf16[512,256]{1,0:T(8,128)(2,1)S(1)}, bf16[512,256]{1,0:T(8,128)(2,1)S(1)}, u32[]{:S(2)}, u32[]{:S(2)}) collective-permute-start(bf16[512,256]{1,0:T(8,128)(2,1)S(1)} %convolution_convert_fusion.2), channel_id=1, source_target_pairs={{0,4},{4,0},{8,12},{12,8},{16,20},{20,16},{24,28},{28,24},{1,5},{5... | collective-permute-start | bytes 786440 | tf_op jit(solution)/shard_map/ppermute | solution.py:29
  41.7 6.7 %collective-permute-start.13 = (bf16[256,256]{1,0:T(8,128)(2,1)S(1)}, bf16[256,256]{1,0:T(8,128)(2,1)S(1)}, u32[]{:S(2)}, u32[]{:S(2)}) collective-permute-start(bf16[256,256]{1,0:T(8,128)(2,1)S(1)} %slice.134), channel_id=1, source_target_pairs={{0,1},{1,0},{2,3},{3,2},{4,5},{5,4},{6,7},{7,6},{8,9},{9,8},{10,11... | collective-permute-start | bytes 393224 | tf_op jit(solution)/shard_map/ppermute | solution.py:37
  46.0 5.7 %collective-permute-start.7 = (bf16[256,256]{1,0:T(8,128)(2,1)S(1)}, bf16[256,256]{1,0:T(8,128)(2,1)S(1)}, u32[]{:S(2)}, u32[]{:S(2)}) collective-permute-start(bf16[256,256]{1,0:T(8,128)(2,1)S(1)} %slice.135), channel_id=1, source_target_pairs={{0,1},{1,0},{2,3},{3,2},{4,5},{5,4},{6,7},{7,6},{8,9},{9,8},{10,11... | collective-permute-start | bytes 393224 | tf_op jit(solution)/shard_map/ppermute | solution.py:37
  48.5 5.4 %collective-permute-start.14 = (bf16[128,256]{1,0:T(8,128)(2,1)S(1)}, bf16[128,256]{1,0:T(8,128)(2,1)S(1)}, u32[]{:S(2)}, u32[]{:S(2)}) collective-permute-start(bf16[128,256]{1,0:T(8,128)(2,1)S(1)} %slice.136), channel_id=1, source_target_pairs={{0,2},{1,3},{2,0},{3,1},{4,6},{5,7},{6,4},{7,5},{8,10},{9,11},{10,... | collective-permute-start | bytes 196616 | tf_op jit(solution)/shard_map/ppermute | solution.py:37
  51.7 5.2 %collective-permute-start.8 = (bf16[128,256]{1,0:T(8,128)(2,1)S(1)}, bf16[128,256]{1,0:T(8,128)(2,1)S(1)}, u32[]{:S(2)}, u32[]{:S(2)}) collective-permute-start(bf16[128,256]{1,0:T(8,128)(2,1)S(1)} %slice.137), channel_id=1, source_target_pairs={{0,2},{1,3},{2,0},{3,1},{4,6},{5,7},{6,4},{7,5},{8,10},{9,11},{10,... | collective-permute-start | bytes 196616 | tf_op jit(solution)/shard_map/ppermute | solution.py:37
  57.1 5.3 %collective-permute-start.18 = (bf16[128,256]{1,0:T(8,128)(2,1)S(1)}, bf16[128,256]{1,0:T(8,128)(2,1)S(1)}, u32[]{:S(2)}, u32[]{:S(2)}) collective-permute-start(bf16[128,256]{1,0:T(8,128)(2,1)S(1)} %get-tuple-element.53), channel_id=1, source_target_pairs={{0,2},{1,3},{2,0},{3,1},{4,6},{5,7},{6,4},{7,5},{8,10},{9,11},{10,... | collective-permute-start | bytes 196616 | tf_op jit(solution)/shard_map/ppermute | solution.py:37
  58.0 5.8 %collective-permute-start.9 = (bf16[128,256]{1,0:T(8,128)(2,1)S(1)}, bf16[128,256]{1,0:T(8,128)(2,1)S(1)}, u32[]{:S(2)}, u32[]{:S(2)}) collective-permute-start(bf16[128,256]{1,0:T(8,128)(2,1)S(1)} %get-tuple-element.54), channel_id=1, source_target_pairs={{0,2},{1,3},{2,0},{3,1},{4,6},{5,7},{6,4},{7,5},{8,10},{9,11},{10,... | collective-permute-start | bytes 196616 | tf_op jit(solution)/shard_map/ppermute | solution.py:37
  62.4 5.0 %collective-permute-start.19 = (bf16[256,256]{1,0:T(8,128)(2,1)S(1)}, bf16[256,256]{1,0:T(8,128)(2,1)S(1)}, u32[]{:S(2)}, u32[]{:S(2)}) collective-permute-start(bf16[256,256]{1,0:T(8,128)(2,1)S(1)} %pad_maximum_fusion.4), channel_id=1, source_target_pairs={{0,1},{1,0},{2,3},{3,2},{4,5},{5,4},{6,7},{7,6},{8,9},{9,8},{10,11... | collective-permute-start | bytes 393224 | tf_op jit(solution)/shard_map/ppermute | solution.py:37
  63.9 5.0 %collective-permute-start.10 = (bf16[256,256]{1,0:T(8,128)(2,1)S(1)}, bf16[256,256]{1,0:T(8,128)(2,1)S(1)}, u32[]{:S(2)}, u32[]{:S(2)}) collective-permute-start(bf16[256,256]{1,0:T(8,128)(2,1)S(1)} %pad_maximum_fusion.3), channel_id=1, source_target_pairs={{0,1},{1,0},{2,3},{3,2},{4,5},{5,4},{6,7},{7,6},{8,9},{9,8},{10,11... | collective-permute-start | bytes 393224 | tf_op jit(solution)/shard_map/ppermute | solution.py:37
  67.5 1.7 %collective-permute-start.20 = (bf16[512,256]{1,0:T(8,128)(2,1)S(1)}, bf16[512,256]{1,0:T(8,128)(2,1)S(1)}, u32[]{:S(2)}, u32[]{:S(2)}) collective-permute-start(bf16[512,256]{1,0:T(8,128)(2,1)S(1)} %pad_maximum_fusion.1.slope_ref), channel_id=1, source_target_pairs={{0,4},{4,0},{8,12},{12,8},{16,20},{20,16},{24,28},{28,24},{1,5},{5... | collective-permute-start | bytes 786440 | tf_op jit(solution)/shard_map/ppermute | solution.py:29
  68.9 3.8 %collective-permute-start.15 = (bf16[512,256]{1,0:T(8,128)(2,1)S(1)}, bf16[512,256]{1,0:T(8,128)(2,1)S(1)}, u32[]{:S(2)}, u32[]{:S(2)}) collective-permute-start(bf16[512,256]{1,0:T(8,128)(2,1)S(1)} %pad_maximum_fusion.slope_ref), channel_id=1, source_target_pairs={{0,4},{4,0},{8,12},{12,8},{16,20},{20,16},{24,28},{28,24},{1,5},{5... | collective-permute-start | bytes 786440 | tf_op jit(solution)/shard_map/ppermute | solution.py:29
  71.3 10.5 %collective-permute-start.21 = (bf16[512,256]{1,0:T(8,128)(2,1)}, bf16[512,256]{1,0:T(8,128)(2,1)}, u32[]{:S(2)}, u32[]{:S(2)}) collective-permute-start(bf16[512,256]{1,0:T(8,128)(2,1)} %get-tuple-element.44), channel_id=1, source_target_pairs={{0,8},{4,20},{8,0},{12,28},{16,24},{20,4},{24,16},{28,12},{1,9},{5... | collective-permute-start | bytes 786440 | tf_op jit(solution)/shard_map/ppermute | solution.py:363
  74.2 8.8 %collective-permute-start.16 = (bf16[512,256]{1,0:T(8,128)(2,1)S(1)}, bf16[512,256]{1,0:T(8,128)(2,1)S(1)}, u32[]{:S(2)}, u32[]{:S(2)}) collective-permute-start(bf16[512,256]{1,0:T(8,128)(2,1)S(1)} %get-tuple-element.42), channel_id=1, source_target_pairs={{0,8},{4,20},{8,0},{12,28},{16,24},{20,4},{24,16},{28,12},{1,9},{5... | collective-permute-start | bytes 786440 | tf_op jit(solution)/shard_map/ppermute | solution.py:363
  74.8 15.0 %all-to-all-start.1 = ((bf16[8,32,512]{2,1,0:T(8,128)(2,1)}), bf16[8,32,512]{2,1,0:T(8,128)(2,1)S(1)}, u32[]{:S(2)}, u32[]{:S(2)}) async-start(bf16[8,32,512]{2,1,0:T(8,128)(2,1)} %bitcast.28), calls=%async_computation.1 | async-start | bytes 524288 | tf_op jit(solution)/shard_map/all_to_all | solution.py:321
  82.8 5.5 %collective-permute-start.22 = (bf16[256,256]{1,0:T(8,128)(2,1)S(1)}, bf16[256,256]{1,0:T(8,128)(2,1)S(1)}, u32[]{:S(2)}, u32[]{:S(2)}) collective-permute-start(bf16[256,256]{1,0:T(8,128)(2,1)S(1)} %slice.132), channel_id=1, source_target_pairs={{0,16},{4,12},{8,24},{12,4},{16,0},{20,28},{24,8},{28,20},{1,17},{... | collective-permute-start | bytes 393224 | tf_op jit(solution)/shard_map/ppermute | solution.py:363
  83.0 6.7 %collective-permute-start.17 = (bf16[256,256]{1,0:T(8,128)(2,1)S(1)}, bf16[256,256]{1,0:T(8,128)(2,1)S(1)}, u32[]{:S(2)}, u32[]{:S(2)}) collective-permute-start(bf16[256,256]{1,0:T(8,128)(2,1)S(1)} %slice.133), channel_id=1, source_target_pairs={{0,16},{4,12},{8,24},{12,4},{16,0},{20,28},{24,8},{28,20},{1,17},{... | collective-permute-start | bytes 393224 | tf_op jit(solution)/shard_map/ppermute | solution.py:363
  89.8 12.9 %collective-permute-start.23 = (bf16[256,512]{1,0:T(8,128)(2,1)S(1)}, bf16[256,512]{1,0:T(8,128)(2,1)S(1)}, u32[]{:S(2)}, u32[]{:S(2)}) collective-permute-start(bf16[256,512]{1,0:T(8,128)(2,1)S(1)} %pad_maximum_fusion.2), channel_id=1, source_target_pairs={{0,0},{1,10},{2,17},{3,27},{4,4},{5,14},{6,21},{7,31},{8,1},{9,11}... | collective-permute-start | bytes 786440 | tf_op jit(solution)/shard_map/ppermute | solution.py:375
  (5 other events, 15.5 us)

commit v14 on v13

--- a/solution.py
+++ b/solution.py
@@ -131,6 +131,10 @@
         out_ref = out_refs[s // count]
         place = s % count
         out_ref[place * rows : (place + 1) * rows, :] = chunk.astype(out_ref.dtype)
+
+
+def write_kernel(in_ref, out_ref):
+    out_ref[...] = in_ref[...]
 
 
 def on_device(
@@ -267,7 +271,7 @@
         held_part, got_part, is_getter_part = parts[j]
         if j == 0:
             got_part, got_cot = lax.optimization_barrier((got_part, got_cot))
-        weight = jnp.where(is_getter_part, got_part, held_part)
+        weight = lax.optimization_barrier(jnp.where(is_getter_part, got_part, held_part))
         value_given = dot(got_rows, weight).astype(BF16)
         value_got = swapped(value_given, dp_count).astype(F32)
         value_parts.append(dot(kept_rows, weight) + value_got)
@@ -373,6 +377,12 @@
     ]
     grad, policy_values = lax.optimization_barrier((jnp.concatenate(grads, axis=1), policy_values))
     grad_weight = lax.ppermute(grad, AXES, pairs).astype(F32)
+    policy_values = pl.pallas_call(
+        write_kernel,
+        out_shape=jax.ShapeDtypeStruct(policy_values.shape, BF16),
+        cost_estimate=pl.CostEstimate(flops=0, bytes_accessed=2**19, transcendentals=0),
+        name="write",
+    )(policy_values)
     return (policy_values.reshape(1, 1, slot_count, value_width), grad_weight)
 
 

time: 105 us -> 108 us (1.029)
  waiting for transfers between devices: 30.3 us -> 39 us
  starting transfers between devices: 47.8 us -> 41.4 us
  other arithmetic: 4.47 us -> 6.8 us
  matrix products: 6.56 us -> 4.36 us
  Pallas kernels: 11.6 us -> 13.2 us
    ppermute x11, waiting for transfers between devices: 13.1 us -> 19.7 us  [crossed(): return lax.ppermute(array, 'tensor', [(i, i ^ step) for i in range(count)])]
    ppermute x3, waiting for transfers between devices: 0.01 us -> 5.81 us  [stage(): return (lax.ppermute(held, AXES, pairs), is_getter)]
    ppermute x11, starting transfers between devices: 25.9 us -> 20.4 us  [crossed(): return lax.ppermute(array, 'tensor', [(i, i ^ step) for i in range(count)])]
    all_to_all x1, waiting for transfers between devices: 2.69 us -> 0.01 us  [on_device(): got_cot = lax.all_to_all(cot, 'dp', split_axis=0, concat_axis=0, tiled=True)]
    all_to_all x1, starting transfers between devices: 6.98 us -> 4.32 us  [on_device(): lax.all_to_all(sent, 'dp', split_axis=0, concat_axis=0, tiled=True)]
    select_n x0 -> x2, other arithmetic: none -> 2.32 us  [on_device(): jnp.where(is_getter_part, got_part, held_part)]
    dot_general x4, matrix products: 5.61 us -> 3.41 us  [dot(): return jnp.dot(a, b, preferred_element_type=F32)]
    ppermute x5, starting transfers between devices: 0.8 us -> 2.59 us  [swapped(): return lax.ppermute(array, 'dp', [(i, i ^ 1) for i in range(dp_count)])]
  transfers between devices with their start and end apart: 26 -> 26, of which waited for: 12 -> 13; matrix products, arithmetic and copies ran while one was open for 10% -> 10% of each run, Pallas kernels for 11% -> 12%
where the time goes in v14:
time: 108 us
  starting transfers between devices  41.4 us (38%)
  waiting for transfers between devices  39 us (36%)
  Pallas kernels  13.2 us (12%)
  other arithmetic  6.8 us (6%)
  matrix products  4.36 us (4%)
  local copies, waits for them, and re-layouts  1.99 us (2%)
    ppermute x11, starting transfers between devices, crossed(): return lax.ppermute(array, 'tensor', [(i, i ^ step) for i in range(count)])  20.4 us
    ppermute x11, waiting for transfers between devices, crossed(): return lax.ppermute(array, 'tensor', [(i, i ^ step) for i in range(count)])  19.7 us
    ppermute x1, waiting for transfers between devices, on_device(): grad_weight = lax.ppermute(grad, AXES, pairs).astype(F32)  8.28 us
    pallas_call x1, Pallas kernels, on_device(): pl.pallas_call(functools.partial(prepare_kernel, tensor_count, steps), gr...  7.01 us
    ppermute x3, waiting for transfers between devices, stage(): return (lax.ppermute(held, AXES, pairs), is_getter)  5.81 us
    ppermute x4, waiting for transfers between devices, on_device(): total = total + lax.ppermute(given, 'dp', pairs).astype(F32)  5.19 us
    all_to_all x1, starting transfers between devices, on_device(): lax.all_to_all(sent, 'dp', split_axis=0, concat_axis=0, tiled=True)  4.32 us
    all_to_all x1, starting transfers between devices, on_device(): got_cot = lax.all_to_all(cot, 'dp', split_axis=0, concat_axis=0, tiled=True)  4.11 us
  transfers between devices with their start and end apart: 26, of which 13 were waited for; matrix products, arithmetic and copies ran while one was open for 10% of the time, Pallas kernels for 12%

profile of v14, /device:TPU:4, one launch (start us, length us, event | category | flops | bytes accessed | tf_op | source)
XLA Modules:
  0.0 107.9 jit_solution(13724668632634994606)
XLA Ops:
  2.0 7.0 %prepare.1 = (bf16[512,1024]{1,0:T(8,128)(2,1)}, bf16[512,1024]{1,0:T(8,128)(2,1)}, bf16[144,512]{1,0:T(8,128)(2,1)}, bf16[144,512]{1,0:T(8,128)(2,1)}, bf16[144...) custom-call(s32[2]{0:T(128)} %pad_add_fusion.1.at, bf16[512,2048]{1,0:T(8,128)(2,1)} %x_ref.1, f32[1,2048]{1,0:T(1,128)} %bitcast.37, ...), custom_call_target="tpu_custom_call" | custom-call | flops 1073741824 | bytes 8388608 | tf_op jit(solution)/shard_map/prepare/pallas_call | solution.py:202
  10.4 1.6 %slice_select_fusion = (bf16[1024,256]{1,0:T(8,128)(2,1)S(1)}, bf16[1024,256]{1,0:T(8,128)(2,1)S(1)}) fusion(bf16[1024,512]{1,0:T(8,128)(2,1)} %param.14, bf16[1024,512]{1,0:T(8,128)(2,1)} %copy-done.8, pred[]{:T(512)S(6)} %or.15), kind=kLoop, calls=%fused_computation.7 | loop fusion | flops 524288 | bytes 3145729 | tf_op jit(solution)/shard_map/jit(_where)/select_n | solution.py:252
  12.0 1.3 %collective-permute-start.11 = (bf16[1024,256]{1,0:T(8,128)(2,1)S(1)}, bf16[1024,256]{1,0:T(8,128)(2,1)S(1)}, u32[]{:S(2)}, u32[]{:S(2)}) collective-permute-start(bf16[1024,256]{1,0:T(8,128)(2,1)S(1)} %get-tuple-element.48), channel_id=1, source_target_pairs={{0,16},{9,25},{18,2},{27,11},{8,24},{1,17},{26,10},{19,3},{4,12},{... | collective-permute-start | bytes 1572872 | tf_op jit(solution)/shard_map/ppermute | solution.py:190
  13.3 1.3 %collective-permute-start.3 = (bf16[144,512]{1,0:T(8,128)(2,1)}, bf16[144,512]{1,0:T(8,128)(2,1)S(1)}, u32[]{:S(2)}, u32[]{:S(2)}) collective-permute-start(bf16[144,512]{1,0:T(8,128)(2,1)} %get-tuple-element.32), channel_id=1, source_target_pairs={{0,1},{1,0},{2,3},{3,2},{4,5},{5,4},{6,7},{7,6},{8,9},{9,8},{10,11... | collective-permute-start | bytes 442376 | tf_op jit(solution)/shard_map/ppermute | solution.py:37
  14.6 11.0 %collective-permute-start.4 = (bf16[144,512]{1,0:T(8,128)(2,1)}, bf16[144,512]{1,0:T(8,128)(2,1)S(1)}, u32[]{:S(2)}, u32[]{:S(2)}) collective-permute-start(bf16[144,512]{1,0:T(8,128)(2,1)} %get-tuple-element.33), channel_id=1, source_target_pairs={{0,2},{1,3},{2,0},{3,1},{4,6},{5,7},{6,4},{7,5},{8,10},{9,11},{10,... | collective-permute-start | bytes 442376 | tf_op jit(solution)/shard_map/ppermute | solution.py:37
  25.7 4.1 %all-to-all-start = ((bf16[8,32,512]{2,1,0:T(8,128)(2,1)}), bf16[8,32,512]{2,1,0:T(8,128)(2,1)S(1)}, u32[]{:S(2)}, u32[]{:S(2)}) async-start(bf16[8,32,512]{2,1,0:T(8,128)(2,1)} %bitcast.34), calls=%async_computation | async-start | bytes 524288 | tf_op jit(solution)/shard_map/all_to_all | solution.py:258
  30.6 1.3 %collective-permute-start.2 = (bf16[1024,256]{1,0:T(8,128)(2,1)S(1)}, bf16[1024,256]{1,0:T(8,128)(2,1)}, u32[]{:S(2)}, u32[]{:S(2)}) collective-permute-start(bf16[1024,256]{1,0:T(8,128)(2,1)S(1)} %get-tuple-element.49), channel_id=1, source_target_pairs={{0,16},{9,25},{18,2},{27,11},{8,24},{1,17},{26,10},{19,3},{4,12},{... | collective-permute-start | bytes 1572872 | tf_op jit(solution)/shard_map/ppermute | solution.py:190
  31.9 1.1 %broadcast_select_fusion = bf16[1024,256]{1,0:T(8,128)(2,1)S(1)} fusion(bf16[1024,256]{1,0:T(8,128)(2,1)} %copy-done.10, bf16[1024,256]{1,0:T(8,128)(2,1)S(1)} %get-tuple-element.48, pred[]{:T(512)S(6)} %or.18), kind=kLoop, calls=%fused_computation.9 | loop fusion | flops 262144 | bytes 1572865 | tf_op jit(solution)/shard_map/jit(_where)/select_n | solution.py:274
  33.0 1.1 %convolution_convert_fusion.1 = bf16[512,256]{1,0:T(8,128)(2,1)} fusion(bf16[512,1024]{1,0:T(8,128)(2,1)S(1)} %collective-permute-done.1.got_ref, bf16[1024,256]{1,0:T(8,128)(2,1)S(1)} %broadcast_select_fusion), kind=kOutput, calls=%fused_computation.3 | convolution fusion | flops 268566528 | bytes 1835008 | tf_op jit(solution)/shard_map/dot_general | solution.py:21
  34.2 1.8 %collective-permute-start.12 = (bf16[512,256]{1,0:T(8,128)(2,1)}, bf16[512,256]{1,0:T(8,128)(2,1)}, u32[]{:S(2)}, u32[]{:S(2)}) collective-permute-start(bf16[512,256]{1,0:T(8,128)(2,1)} %convolution_convert_fusion.1), channel_id=1, source_target_pairs={{0,4},{4,0},{8,12},{12,8},{16,20},{20,16},{24,28},{28,24},{1,5},{5... | collective-permute-start | bytes 786440 | tf_op jit(solution)/shard_map/ppermute | solution.py:29
  36.0 5.8 %collective-permute-done.2 = bf16[1024,256]{1,0:T(8,128)(2,1)} collective-permute-done((bf16[1024,256]{1,0:T(8,128)(2,1)S(1)}, bf16[1024,256]{1,0:T(8,128)(2,1)}, u32[]{:S(2)}, u32[]{:S(2)}) %collective-permute-start.2) | collective-permute-done | bytes 524320 | tf_op jit(solution)/shard_map/ppermute | solution.py:190
  41.8 1.2 %broadcast_select_fusion.1 = bf16[1024,256]{1,0:T(8,128)(2,1)S(1)} fusion(bf16[1024,256]{1,0:T(8,128)(2,1)} %collective-permute-done.2, bf16[1024,256]{1,0:T(8,128)(2,1)S(1)} %get-tuple-element.49, pred[]{:T(512)S(6)} %or.18), kind=kLoop, calls=%fused_computation.10 | loop fusion | flops 262144 | bytes 1572865 | tf_op jit(solution)/shard_map/jit(_where)/select_n | solution.py:274
  44.7 1.4 %convolution_add_fusion = f32[512,256]{1,0:T(8,128)S(1)} fusion(bf16[512,1024]{1,0:T(8,128)(2,1)S(1)} %copy-done, bf16[1024,256]{1,0:T(8,128)(2,1)S(1)} %copy-done.7, bf16[512,256]{1,0:T(8,128)(2,1)} %collective-permute-done.12), kind=kOutput, calls=%fused_computation | convolution fusion | flops 268697600 | bytes 2359296 | tf_op jit(solution)/shard_map/dot_general | solution.py:21
  47.5 1.3 %collective-permute-start.7 = (bf16[256,256]{1,0:T(8,128)(2,1)S(1)}, bf16[256,256]{1,0:T(8,128)(2,1)S(1)}, u32[]{:S(2)}, u32[]{:S(2)}) collective-permute-start(bf16[256,256]{1,0:T(8,128)(2,1)S(1)} %slice.135), channel_id=1, source_target_pairs={{0,1},{1,0},{2,3},{3,2},{4,5},{5,4},{6,7},{7,6},{8,9},{9,8},{10,11... | collective-permute-start | bytes 393224 | tf_op jit(solution)/shard_map/ppermute | solution.py:37
  48.8 3.7 %collective-permute-done.13 = bf16[256,256]{1,0:T(8,128)(2,1)S(1)} collective-permute-done((bf16[256,256]{1,0:T(8,128)(2,1)S(1)}, bf16[256,256]{1,0:T(8,128)(2,1)S(1)}, u32[]{:S(2)}, u32[]{:S(2)}) %collective-permute-start.13) | collective-permute-done | bytes 131104 | tf_op jit(solution)/shard_map/ppermute | solution.py:37
  53.2 1.7 %collective-permute-done.7 = bf16[256,256]{1,0:T(8,128)(2,1)S(1)} collective-permute-done((bf16[256,256]{1,0:T(8,128)(2,1)S(1)}, bf16[256,256]{1,0:T(8,128)(2,1)S(1)}, u32[]{:S(2)}, u32[]{:S(2)}) %collective-permute-start.7) | collective-permute-done | bytes 131104 | tf_op jit(solution)/shard_map/ppermute | solution.py:37
  55.7 3.7 %collective-permute-done.14 = bf16[128,256]{1,0:T(8,128)(2,1)S(1)} collective-permute-done((bf16[128,256]{1,0:T(8,128)(2,1)S(1)}, bf16[128,256]{1,0:T(8,128)(2,1)S(1)}, u32[]{:S(2)}, u32[]{:S(2)}) %collective-permute-start.14) | collective-permute-done | bytes 65568 | tf_op jit(solution)/shard_map/ppermute | solution.py:37
  59.5 1.8 %collective-permute-done.8 = bf16[128,256]{1,0:T(8,128)(2,1)S(1)} collective-permute-done((bf16[128,256]{1,0:T(8,128)(2,1)S(1)}, bf16[128,256]{1,0:T(8,128)(2,1)S(1)}, u32[]{:S(2)}, u32[]{:S(2)}) %collective-permute-start.8) | collective-permute-done | bytes 65568 | tf_op jit(solution)/shard_map/ppermute | solution.py:37
  61.5 2.9 %collective-permute-start.9 = (bf16[128,256]{1,0:T(8,128)(2,1)S(1)}, bf16[128,256]{1,0:T(8,128)(2,1)S(1)}, u32[]{:S(2)}, u32[]{:S(2)}) collective-permute-start(bf16[128,256]{1,0:T(8,128)(2,1)S(1)} %get-tuple-element.54), channel_id=1, source_target_pairs={{0,2},{1,3},{2,0},{3,1},{4,6},{5,7},{6,4},{7,5},{8,10},{9,11},{10,... | collective-permute-start | bytes 196616 | tf_op jit(solution)/shard_map/ppermute | solution.py:37
  64.4 4.7 %collective-permute-done.18 = bf16[128,256]{1,0:T(8,128)(2,1)S(1)} collective-permute-done((bf16[128,256]{1,0:T(8,128)(2,1)S(1)}, bf16[128,256]{1,0:T(8,128)(2,1)S(1)}, u32[]{:S(2)}, u32[]{:S(2)}) %collective-permute-start.18) | collective-permute-done | bytes 65568 | tf_op jit(solution)/shard_map/ppermute | solution.py:37
  69.8 1.5 %collective-permute-start.10 = (bf16[256,256]{1,0:T(8,128)(2,1)S(1)}, bf16[256,256]{1,0:T(8,128)(2,1)S(1)}, u32[]{:S(2)}, u32[]{:S(2)}) collective-permute-start(bf16[256,256]{1,0:T(8,128)(2,1)S(1)} %pad_maximum_fusion.3), channel_id=1, source_target_pairs={{0,1},{1,0},{2,3},{3,2},{4,5},{5,4},{6,7},{7,6},{8,9},{9,8},{10,11... | collective-permute-start | bytes 393224 | tf_op jit(solution)/shard_map/ppermute | solution.py:37
  71.3 3.1 %collective-permute-done.19 = bf16[256,256]{1,0:T(8,128)(2,1)S(1)} collective-permute-done((bf16[256,256]{1,0:T(8,128)(2,1)S(1)}, bf16[256,256]{1,0:T(8,128)(2,1)S(1)}, u32[]{:S(2)}, u32[]{:S(2)}) %collective-permute-start.19) | collective-permute-done | bytes 131104 | tf_op jit(solution)/shard_map/ppermute | solution.py:37
  76.1 2.1 %gradient.3 = (f32[512,256]{1,0:T(8,128)S(1)}, bf16[512,256]{1,0:T(8,128)(2,1)}) custom-call(s32[4]{0:T(128)S(1)} %pad_add_fusion.at, bf16[512,1024]{1,0:T(8,128)(2,1)S(1)} %copy-done, bf16[512,1024]{1,0:T(8,128)(2,1)S(1)} %collective-permute-done.1.got_ref, bf16[512,256]{1,0:T(8,128)(2,1)S(1)} %pad_maximum_fusion.1.slope_ref, ...), custom_call_target="tpu_custom_call" | custom-call | flops 536870912 | bytes 4194304 | tf_op jit(solution)/shard_map/gradient/pallas_call | solution.py:330
  78.2 1.6 %collective-permute-start.21 = (bf16[512,256]{1,0:T(8,128)(2,1)}, bf16[512,256]{1,0:T(8,128)(2,1)}, u32[]{:S(2)}, u32[]{:S(2)}) collective-permute-start(bf16[512,256]{1,0:T(8,128)(2,1)} %get-tuple-element.44), channel_id=1, source_target_pairs={{0,8},{4,20},{8,0},{12,28},{16,24},{20,4},{24,16},{28,12},{1,9},{5... | collective-permute-start | bytes 786440 | tf_op jit(solution)/shard_map/ppermute | solution.py:367
  79.8 1.4 %gradient.2 = (f32[512,256]{1,0:T(8,128)S(1)}, bf16[512,256]{1,0:T(8,128)(2,1)S(1)}) custom-call(s32[4]{0:T(128)S(1)} %pad_add_fusion.at, bf16[512,1024]{1,0:T(8,128)(2,1)S(1)} %copy-done, bf16[512,1024]{1,0:T(8,128)(2,1)S(1)} %collective-permute-done.1.got_ref, bf16[512,256]{1,0:T(8,128)(2,1)S(1)} %pad_maximum_fusion.slope_ref, ...), custom_call_target="tpu_custom_call" | custom-call | flops 536870912 | bytes 4194304 | tf_op jit(solution)/shard_map/gradient/pallas_call | solution.py:330
  81.7 4.3 %all-to-all-start.1 = ((bf16[8,32,512]{2,1,0:T(8,128)(2,1)}), bf16[8,32,512]{2,1,0:T(8,128)(2,1)S(1)}, u32[]{:S(2)}, u32[]{:S(2)}) async-start(bf16[8,32,512]{2,1,0:T(8,128)(2,1)} %bitcast.32), calls=%async_computation.1 | async-start | bytes 524288 | tf_op jit(solution)/shard_map/all_to_all | solution.py:325
  87.7 1.6 %collective-permute-start.17 = (bf16[256,256]{1,0:T(8,128)(2,1)S(1)}, bf16[256,256]{1,0:T(8,128)(2,1)S(1)}, u32[]{:S(2)}, u32[]{:S(2)}) collective-permute-start(bf16[256,256]{1,0:T(8,128)(2,1)S(1)} %slice.133), channel_id=1, source_target_pairs={{0,16},{4,12},{8,24},{12,4},{16,0},{20,28},{24,8},{28,20},{1,17},{... | collective-permute-start | bytes 393224 | tf_op jit(solution)/shard_map/ppermute | solution.py:367
  89.3 3.3 %collective-permute-done.22 = bf16[256,256]{1,0:T(8,128)(2,1)S(1)} collective-permute-done((bf16[256,256]{1,0:T(8,128)(2,1)S(1)}, bf16[256,256]{1,0:T(8,128)(2,1)S(1)}, u32[]{:S(2)}, u32[]{:S(2)}) %collective-permute-start.22) | collective-permute-done | bytes 131104 | tf_op jit(solution)/shard_map/ppermute | solution.py:367
  92.6 1.4 %collective-permute-done.17 = bf16[256,256]{1,0:T(8,128)(2,1)S(1)} collective-permute-done((bf16[256,256]{1,0:T(8,128)(2,1)S(1)}, bf16[256,256]{1,0:T(8,128)(2,1)S(1)}, u32[]{:S(2)}, u32[]{:S(2)}) %collective-permute-start.17) | collective-permute-done | bytes 131104 | tf_op jit(solution)/shard_map/ppermute | solution.py:367
  94.1 3.0 %collective-permute-start.23 = (bf16[256,512]{1,0:T(8,128)(2,1)S(1)}, bf16[256,512]{1,0:T(8,128)(2,1)S(1)}, u32[]{:S(2)}, u32[]{:S(2)}) collective-permute-start(bf16[256,512]{1,0:T(8,128)(2,1)S(1)} %pad_maximum_fusion.2), channel_id=1, source_target_pairs={{0,0},{1,10},{2,17},{3,27},{4,4},{5,14},{6,21},{7,31},{8,1},{9,11}... | collective-permute-start | bytes 786440 | tf_op jit(solution)/shard_map/ppermute | solution.py:379
  97.1 1.7 %write.1 = bf16[256,512]{1,0:T(8,128)(2,1)} custom-call(bf16[256,512]{1,0:T(8,128)(2,1)} %bitcast.33), custom_call_target="tpu_custom_call" | custom-call | bytes 524288 | tf_op jit(solution)/shard_map/write/pallas_call | solution.py:380
  98.7 8.3 %collective-permute-done.23 = bf16[256,512]{1,0:T(8,128)(2,1)S(1)} collective-permute-done((bf16[256,512]{1,0:T(8,128)(2,1)S(1)}, bf16[256,512]{1,0:T(8,128)(2,1)S(1)}, u32[]{:S(2)}, u32[]{:S(2)}) %collective-permute-start.23) | collective-permute-done | bytes 262176 | tf_op jit(solution)/shard_map/ppermute | solution.py:379
  (77 shorter events, 13.8 us)
Async XLA Ops:
  0.6 8.8 %collective-permute-start = (bf16[1024,512]{1,0:T(8,128)(2,1)}, bf16[1024,512]{1,0:T(8,128)(2,1)S(1)}, u32[]{:S(2)}, u32[]{:S(2)}) collective-permute-start(bf16[1024,512]{1,0:T(8,128)(2,1)} %param.14), channel_id=1, source_target_pairs={{0,8},{9,1},{18,26},{27,19},{4,20},{13,29},{22,6},{31,15}} | collective-permute-start | bytes 3145736 | tf_op jit(solution)/shard_map/ppermute | solution.py:190
  9.0 24.0 %collective-permute-start.1 = (bf16[512,1024]{1,0:T(8,128)(2,1)}, bf16[512,1024]{1,0:T(8,128)(2,1)S(1)}, u32[]{:S(2)}, u32[]{:S(2)}) collective-permute-start(bf16[512,1024]{1,0:T(8,128)(2,1)} %get-tuple-element.27), channel_id=1, source_target_pairs={{0,4},{4,0},{8,12},{12,8},{16,20},{20,16},{24,28},{28,24},{1,5},{5... | collective-permute-start | bytes 3145736 | tf_op jit(solution)/shard_map/ppermute | solution.py:29
  12.0 17.8 %collective-permute-start.11 = (bf16[1024,256]{1,0:T(8,128)(2,1)S(1)}, bf16[1024,256]{1,0:T(8,128)(2,1)S(1)}, u32[]{:S(2)}, u32[]{:S(2)}) collective-permute-start(bf16[1024,256]{1,0:T(8,128)(2,1)S(1)} %get-tuple-element.48), channel_id=1, source_target_pairs={{0,16},{9,25},{18,2},{27,11},{8,24},{1,17},{26,10},{19,3},{4,12},{... | collective-permute-start | bytes 1572872 | tf_op jit(solution)/shard_map/ppermute | solution.py:190
  13.3 30.2 %collective-permute-start.3 = (bf16[144,512]{1,0:T(8,128)(2,1)}, bf16[144,512]{1,0:T(8,128)(2,1)S(1)}, u32[]{:S(2)}, u32[]{:S(2)}) collective-permute-start(bf16[144,512]{1,0:T(8,128)(2,1)} %get-tuple-element.32), channel_id=1, source_target_pairs={{0,1},{1,0},{2,3},{3,2},{4,5},{5,4},{6,7},{7,6},{8,9},{9,8},{10,11... | collective-permute-start | bytes 442376 | tf_op jit(solution)/shard_map/ppermute | solution.py:37
  14.6 28.9 %collective-permute-start.4 = (bf16[144,512]{1,0:T(8,128)(2,1)}, bf16[144,512]{1,0:T(8,128)(2,1)S(1)}, u32[]{:S(2)}, u32[]{:S(2)}) collective-permute-start(bf16[144,512]{1,0:T(8,128)(2,1)} %get-tuple-element.33), channel_id=1, source_target_pairs={{0,2},{1,3},{2,0},{3,1},{4,6},{5,7},{6,4},{7,5},{8,10},{9,11},{10,... | collective-permute-start | bytes 442376 | tf_op jit(solution)/shard_map/ppermute | solution.py:37
  25.7 17.9 %collective-permute-start.5 = (bf16[144,512]{1,0:T(8,128)(2,1)}, bf16[144,512]{1,0:T(8,128)(2,1)S(1)}, u32[]{:S(2)}, u32[]{:S(2)}) collective-permute-start(bf16[144,512]{1,0:T(8,128)(2,1)} %get-tuple-element.34), channel_id=1, source_target_pairs={{0,3},{1,2},{2,1},{3,0},{4,7},{5,6},{6,5},{7,4},{8,11},{9,10},{10,... | collective-permute-start | bytes 442376 | tf_op jit(solution)/shard_map/ppermute | solution.py:37
  25.7 10.3 %all-to-all-start = ((bf16[8,32,512]{2,1,0:T(8,128)(2,1)}), bf16[8,32,512]{2,1,0:T(8,128)(2,1)S(1)}, u32[]{:S(2)}, u32[]{:S(2)}) async-start(bf16[8,32,512]{2,1,0:T(8,128)(2,1)} %bitcast.34), calls=%async_computation | async-start | bytes 524288 | tf_op jit(solution)/shard_map/all_to_all | solution.py:258
  30.6 11.2 %collective-permute-start.2 = (bf16[1024,256]{1,0:T(8,128)(2,1)S(1)}, bf16[1024,256]{1,0:T(8,128)(2,1)}, u32[]{:S(2)}, u32[]{:S(2)}) collective-permute-start(bf16[1024,256]{1,0:T(8,128)(2,1)S(1)} %get-tuple-element.49), channel_id=1, source_target_pairs={{0,16},{9,25},{18,2},{27,11},{8,24},{1,17},{26,10},{19,3},{4,12},{... | collective-permute-start | bytes 1572872 | tf_op jit(solution)/shard_map/ppermute | solution.py:190
  34.2 9.4 %copy-start.1 = (bf16[144,512]{1,0:T(8,128)(2,1)S(1)}, bf16[144,512]{1,0:T(8,128)(2,1)}, u32[]{:S(2)}) copy-start(bf16[144,512]{1,0:T(8,128)(2,1)} %get-tuple-element.31.refs_0_) | copy-start | bytes 442372
  34.2 9.4 %copy-start.2 = (s32[1,1,8]{2,1,0:T(1,128)S(1)}, s32[1,1,8]{2,1,0:T(1,128)}, u32[]{:S(2)}) copy-start(s32[1,1,8]{2,1,0:T(1,128)} %param.15) | copy-start | bytes 100
  34.2 9.4 %copy-start.3 = (s32[1,1,8]{2,1,0:T(1,128)S(1)}, s32[1,1,8]{2,1,0:T(1,128)}, u32[]{:S(2)}) copy-start(s32[1,1,8]{2,1,0:T(1,128)} %param.16) | copy-start | bytes 100
  34.2 9.4 %copy-start.4 = (f32[1,1,8]{2,1,0:T(1,128)S(1)}, f32[1,1,8]{2,1,0:T(1,128)}, u32[]{:S(2)}) copy-start(f32[1,1,8]{2,1,0:T(1,128)} %param.17) | copy-start | bytes 100
  34.2 9.4 %copy-start.5 = (f32[128]{0:T(128)S(1)}, f32[128]{0:T(128)}, u32[]{:S(2)}) copy-start(f32[128]{0:T(128)} %param.18) | copy-start | bytes 1540
  34.2 10.5 %collective-permute-start.12 = (bf16[512,256]{1,0:T(8,128)(2,1)}, bf16[512,256]{1,0:T(8,128)(2,1)}, u32[]{:S(2)}, u32[]{:S(2)}) collective-permute-start(bf16[512,256]{1,0:T(8,128)(2,1)} %convolution_convert_fusion.1), channel_id=1, source_target_pairs={{0,4},{4,0},{8,12},{12,8},{16,20},{20,16},{24,28},{28,24},{1,5},{5... | collective-permute-start | bytes 786440 | tf_op jit(solution)/shard_map/ppermute | solution.py:29
  43.4 3.6 %collective-permute-start.6 = (bf16[512,256]{1,0:T(8,128)(2,1)S(1)}, bf16[512,256]{1,0:T(8,128)(2,1)S(1)}, u32[]{:S(2)}, u32[]{:S(2)}) collective-permute-start(bf16[512,256]{1,0:T(8,128)(2,1)S(1)} %convolution_convert_fusion.2), channel_id=1, source_target_pairs={{0,4},{4,0},{8,12},{12,8},{16,20},{20,16},{24,28},{28,24},{1,5},{5... | collective-permute-start | bytes 786440 | tf_op jit(solution)/shard_map/ppermute | solution.py:29
  46.1 6.4 %collective-permute-start.13 = (bf16[256,256]{1,0:T(8,128)(2,1)S(1)}, bf16[256,256]{1,0:T(8,128)(2,1)S(1)}, u32[]{:S(2)}, u32[]{:S(2)}) collective-permute-start(bf16[256,256]{1,0:T(8,128)(2,1)S(1)} %slice.134), channel_id=1, source_target_pairs={{0,1},{1,0},{2,3},{3,2},{4,5},{5,4},{6,7},{7,6},{8,9},{9,8},{10,11... | collective-permute-start | bytes 393224 | tf_op jit(solution)/shard_map/ppermute | solution.py:37
  47.5 7.4 %collective-permute-start.7 = (bf16[256,256]{1,0:T(8,128)(2,1)S(1)}, bf16[256,256]{1,0:T(8,128)(2,1)S(1)}, u32[]{:S(2)}, u32[]{:S(2)}) collective-permute-start(bf16[256,256]{1,0:T(8,128)(2,1)S(1)} %slice.135), channel_id=1, source_target_pairs={{0,1},{1,0},{2,3},{3,2},{4,5},{5,4},{6,7},{7,6},{8,9},{9,8},{10,11... | collective-permute-start | bytes 393224 | tf_op jit(solution)/shard_map/ppermute | solution.py:37
  52.5 6.9 %collective-permute-start.14 = (bf16[128,256]{1,0:T(8,128)(2,1)S(1)}, bf16[128,256]{1,0:T(8,128)(2,1)S(1)}, u32[]{:S(2)}, u32[]{:S(2)}) collective-permute-start(bf16[128,256]{1,0:T(8,128)(2,1)S(1)} %slice.136), channel_id=1, source_target_pairs={{0,2},{1,3},{2,0},{3,1},{4,6},{5,7},{6,4},{7,5},{8,10},{9,11},{10,... | collective-permute-start | bytes 196616 | tf_op jit(solution)/shard_map/ppermute | solution.py:37
  54.9 6.4 %collective-permute-start.8 = (bf16[128,256]{1,0:T(8,128)(2,1)S(1)}, bf16[128,256]{1,0:T(8,128)(2,1)S(1)}, u32[]{:S(2)}, u32[]{:S(2)}) collective-permute-start(bf16[128,256]{1,0:T(8,128)(2,1)S(1)} %slice.137), channel_id=1, source_target_pairs={{0,2},{1,3},{2,0},{3,1},{4,6},{5,7},{6,4},{7,5},{8,10},{9,11},{10,... | collective-permute-start | bytes 196616 | tf_op jit(solution)/shard_map/ppermute | solution.py:37
  61.4 7.7 %collective-permute-start.18 = (bf16[128,256]{1,0:T(8,128)(2,1)S(1)}, bf16[128,256]{1,0:T(8,128)(2,1)S(1)}, u32[]{:S(2)}, u32[]{:S(2)}) collective-permute-start(bf16[128,256]{1,0:T(8,128)(2,1)S(1)} %get-tuple-element.53), channel_id=1, source_target_pairs={{0,2},{1,3},{2,0},{3,1},{4,6},{5,7},{6,4},{7,5},{8,10},{9,11},{10,... | collective-permute-start | bytes 196616 | tf_op jit(solution)/shard_map/ppermute | solution.py:37
  61.5 8.3 %collective-permute-start.9 = (bf16[128,256]{1,0:T(8,128)(2,1)S(1)}, bf16[128,256]{1,0:T(8,128)(2,1)S(1)}, u32[]{:S(2)}, u32[]{:S(2)}) collective-permute-start(bf16[128,256]{1,0:T(8,128)(2,1)S(1)} %get-tuple-element.54), channel_id=1, source_target_pairs={{0,2},{1,3},{2,0},{3,1},{4,6},{5,7},{6,4},{7,5},{8,10},{9,11},{10,... | collective-permute-start | bytes 196616 | tf_op jit(solution)/shard_map/ppermute | solution.py:37
  69.1 5.3 %collective-permute-start.19 = (bf16[256,256]{1,0:T(8,128)(2,1)S(1)}, bf16[256,256]{1,0:T(8,128)(2,1)S(1)}, u32[]{:S(2)}, u32[]{:S(2)}) collective-permute-start(bf16[256,256]{1,0:T(8,128)(2,1)S(1)} %pad_maximum_fusion.4), channel_id=1, source_target_pairs={{0,1},{1,0},{2,3},{3,2},{4,5},{5,4},{6,7},{7,6},{8,9},{9,8},{10,11... | collective-permute-start | bytes 393224 | tf_op jit(solution)/shard_map/ppermute | solution.py:37
  69.8 6.0 %collective-permute-start.10 = (bf16[256,256]{1,0:T(8,128)(2,1)S(1)}, bf16[256,256]{1,0:T(8,128)(2,1)S(1)}, u32[]{:S(2)}, u32[]{:S(2)}) collective-permute-start(bf16[256,256]{1,0:T(8,128)(2,1)S(1)} %pad_maximum_fusion.3), channel_id=1, source_target_pairs={{0,1},{1,0},{2,3},{3,2},{4,5},{5,4},{6,7},{7,6},{8,9},{9,8},{10,11... | collective-permute-start | bytes 393224 | tf_op jit(solution)/shard_map/ppermute | solution.py:37
  74.4 1.7 %collective-permute-start.20 = (bf16[512,256]{1,0:T(8,128)(2,1)S(1)}, bf16[512,256]{1,0:T(8,128)(2,1)S(1)}, u32[]{:S(2)}, u32[]{:S(2)}) collective-permute-start(bf16[512,256]{1,0:T(8,128)(2,1)S(1)} %pad_maximum_fusion.1.slope_ref), channel_id=1, source_target_pairs={{0,4},{4,0},{8,12},{12,8},{16,20},{20,16},{24,28},{28,24},{1,5},{5... | collective-permute-start | bytes 786440 | tf_op jit(solution)/shard_map/ppermute | solution.py:29
  75.8 4.0 %collective-permute-start.15 = (bf16[512,256]{1,0:T(8,128)(2,1)S(1)}, bf16[512,256]{1,0:T(8,128)(2,1)S(1)}, u32[]{:S(2)}, u32[]{:S(2)}) collective-permute-start(bf16[512,256]{1,0:T(8,128)(2,1)S(1)} %pad_maximum_fusion.slope_ref), channel_id=1, source_target_pairs={{0,4},{4,0},{8,12},{12,8},{16,20},{20,16},{24,28},{28,24},{1,5},{5... | collective-permute-start | bytes 786440 | tf_op jit(solution)/shard_map/ppermute | solution.py:29
  78.2 7.8 %collective-permute-start.21 = (bf16[512,256]{1,0:T(8,128)(2,1)}, bf16[512,256]{1,0:T(8,128)(2,1)}, u32[]{:S(2)}, u32[]{:S(2)}) collective-permute-start(bf16[512,256]{1,0:T(8,128)(2,1)} %get-tuple-element.44), channel_id=1, source_target_pairs={{0,8},{4,20},{8,0},{12,28},{16,24},{20,4},{24,16},{28,12},{1,9},{5... | collective-permute-start | bytes 786440 | tf_op jit(solution)/shard_map/ppermute | solution.py:367
  81.2 6.4 %collective-permute-start.16 = (bf16[512,256]{1,0:T(8,128)(2,1)S(1)}, bf16[512,256]{1,0:T(8,128)(2,1)S(1)}, u32[]{:S(2)}, u32[]{:S(2)}) collective-permute-start(bf16[512,256]{1,0:T(8,128)(2,1)S(1)} %get-tuple-element.42), channel_id=1, source_target_pairs={{0,8},{4,20},{8,0},{12,28},{16,24},{20,4},{24,16},{28,12},{1,9},{5... | collective-permute-start | bytes 786440 | tf_op jit(solution)/shard_map/ppermute | solution.py:367
  81.7 12.4 %all-to-all-start.1 = ((bf16[8,32,512]{2,1,0:T(8,128)(2,1)}), bf16[8,32,512]{2,1,0:T(8,128)(2,1)S(1)}, u32[]{:S(2)}, u32[]{:S(2)}) async-start(bf16[8,32,512]{2,1,0:T(8,128)(2,1)} %bitcast.32), calls=%async_computation.1 | async-start | bytes 524288 | tf_op jit(solution)/shard_map/all_to_all | solution.py:325
  87.1 5.6 %collective-permute-start.22 = (bf16[256,256]{1,0:T(8,128)(2,1)S(1)}, bf16[256,256]{1,0:T(8,128)(2,1)S(1)}, u32[]{:S(2)}, u32[]{:S(2)}) collective-permute-start(bf16[256,256]{1,0:T(8,128)(2,1)S(1)} %slice.132), channel_id=1, source_target_pairs={{0,16},{4,12},{8,24},{12,4},{16,0},{20,28},{24,8},{28,20},{1,17},{... | collective-permute-start | bytes 393224 | tf_op jit(solution)/shard_map/ppermute | solution.py:367
  87.7 6.3 %collective-permute-start.17 = (bf16[256,256]{1,0:T(8,128)(2,1)S(1)}, bf16[256,256]{1,0:T(8,128)(2,1)S(1)}, u32[]{:S(2)}, u32[]{:S(2)}) collective-permute-start(bf16[256,256]{1,0:T(8,128)(2,1)S(1)} %slice.133), channel_id=1, source_target_pairs={{0,16},{4,12},{8,24},{12,4},{16,0},{20,28},{24,8},{28,20},{1,17},{... | collective-permute-start | bytes 393224 | tf_op jit(solution)/shard_map/ppermute | solution.py:367
  94.1 3.0 %copy-start.9 = (bf16[8,32,512]{2,1,0:T(8,128)(2,1)}, bf16[8,32,512]{2,1,0:T(8,128)(2,1)S(1)}, u32[]{:S(2)}) copy-start(bf16[8,32,512]{2,1,0:T(8,128)(2,1)S(1)} %all-to-all-done.1) | copy-start | bytes 786436
  94.1 12.9 %collective-permute-start.23 = (bf16[256,512]{1,0:T(8,128)(2,1)S(1)}, bf16[256,512]{1,0:T(8,128)(2,1)S(1)}, u32[]{:S(2)}, u32[]{:S(2)}) collective-permute-start(bf16[256,512]{1,0:T(8,128)(2,1)S(1)} %pad_maximum_fusion.2), channel_id=1, source_target_pairs={{0,0},{1,10},{2,17},{3,27},{4,4},{5,14},{6,21},{7,31},{8,1},{9,11}... | collective-permute-start | bytes 786440 | tf_op jit(solution)/shard_map/ppermute | solution.py:379
  (5 other events, 8.8 us)

commit v15 on v14

--- a/solution.py
+++ b/solution.py
@@ -271,7 +271,7 @@
         held_part, got_part, is_getter_part = parts[j]
         if j == 0:
             got_part, got_cot = lax.optimization_barrier((got_part, got_cot))
-        weight = lax.optimization_barrier(jnp.where(is_getter_part, got_part, held_part))
+        weight = jnp.where(is_getter_part, got_part, held_part)
         value_given = dot(got_rows, weight).astype(BF16)
         value_got = swapped(value_given, dp_count).astype(F32)
         value_parts.append(dot(kept_rows, weight) + value_got)

time: 108 us -> 104 us (0.963)
  waiting for transfers between devices: 39 us -> 28.6 us
  starting transfers between devices: 41.4 us -> 47.7 us
  other arithmetic: 6.8 us -> 4.47 us
  matrix products: 4.36 us -> 6.57 us
    ppermute x11, waiting for transfers between devices: 19.7 us -> 13.1 us  [crossed(): return lax.ppermute(array, 'tensor', [(i, i ^ step) for i in range(count)])]
    ppermute x3, waiting for transfers between devices: 5.81 us -> 0.01 us  [stage(): return (lax.ppermute(held, AXES, pairs), is_getter)]
    ppermute x11, starting transfers between devices: 20.4 us -> 25.9 us  [crossed(): return lax.ppermute(array, 'tensor', [(i, i ^ step) for i in range(count)])]
    all_to_all x1, waiting for transfers between devices: 0.01 us -> 2.69 us  [on_device(): got_cot = lax.all_to_all(cot, 'dp', split_axis=0, concat_axis=0, tiled=True)]
    all_to_all x1, starting transfers between devices: 4.32 us -> 6.98 us  [on_device(): lax.all_to_all(sent, 'dp', split_axis=0, concat_axis=0, tiled=True)]
    select_n x2 -> x0, other arithmetic: 2.32 us -> none  [on_device(): jnp.where(is_getter_part, got_part, held_part)]
    dot_general x4, matrix products: 3.41 us -> 5.61 us  [dot(): return jnp.dot(a, b, preferred_element_type=F32)]
    ppermute x5, starting transfers between devices: 2.59 us -> 0.82 us  [swapped(): return lax.ppermute(array, 'dp', [(i, i ^ 1) for i in range(dp_count)])]
  transfers between devices with their start and end apart: 26 -> 26, of which waited for: 13 -> 12; matrix products, arithmetic and copies ran while one was open for 10% -> 10% of each run, Pallas kernels for 12% -> 13%
where the time goes in v15:
time: 104 us
  starting transfers between devices  47.7 us (46%)
  waiting for transfers between devices  28.6 us (28%)
  Pallas kernels  13.3 us (13%)
  matrix products  6.57 us (6%)
  other arithmetic  4.47 us (4%)
  local copies, waits for them, and re-layouts  2.02 us (2%)
    ppermute x11, starting transfers between devices, crossed(): return lax.ppermute(array, 'tensor', [(i, i ^ step) for i in range(count)])  25.9 us
    ppermute x11, waiting for transfers between devices, crossed(): return lax.ppermute(array, 'tensor', [(i, i ^ step) for i in range(count)])  13.1 us
    ppermute x1, waiting for transfers between devices, on_device(): grad_weight = lax.ppermute(grad, AXES, pairs).astype(F32)  8.08 us
    pallas_call x1, Pallas kernels, on_device(): pl.pallas_call(functools.partial(prepare_kernel, tensor_count, steps), gr...  7.02 us
    all_to_all x1, starting transfers between devices, on_device(): lax.all_to_all(sent, 'dp', split_axis=0, concat_axis=0, tiled=True)  6.98 us
    dot_general x4, matrix products, dot(): return jnp.dot(a, b, preferred_element_type=F32)  5.61 us
    ppermute x4, waiting for transfers between devices, on_device(): total = total + lax.ppermute(given, 'dp', pairs).astype(F32)  4.69 us
    ppermute x4, starting transfers between devices, on_device(): total = total + lax.ppermute(given, 'dp', pairs).astype(F32)  4.25 us
  transfers between devices with their start and end apart: 26, of which 12 were waited for; matrix products, arithmetic and copies ran while one was open for 10% of the time, Pallas kernels for 13%

profile of v15, /device:TPU:4, one launch (start us, length us, event | category | flops | bytes accessed | tf_op | source)
XLA Modules:
  0.0 103.6 jit_solution(2975679517438675943)
XLA Ops:
  2.0 7.0 %prepare.1 = (bf16[512,1024]{1,0:T(8,128)(2,1)}, bf16[512,1024]{1,0:T(8,128)(2,1)}, bf16[144,512]{1,0:T(8,128)(2,1)}, bf16[144,512]{1,0:T(8,128)(2,1)}, bf16[144...) custom-call(s32[2]{0:T(128)} %pad_add_fusion.1.at, bf16[512,2048]{1,0:T(8,128)(2,1)} %x_ref.1, f32[1,2048]{1,0:T(1,128)} %bitcast.32, ...), custom_call_target="tpu_custom_call" | custom-call | flops 1073741824 | bytes 8388608 | tf_op jit(solution)/shard_map/prepare/pallas_call | solution.py:202
  10.4 1.6 %slice_select_fusion = (bf16[1024,256]{1,0:T(8,128)(2,1)S(1)}, bf16[1024,256]{1,0:T(8,128)(2,1)S(1)}) fusion(bf16[1024,512]{1,0:T(8,128)(2,1)} %param.14, bf16[1024,512]{1,0:T(8,128)(2,1)} %copy-done.8, pred[]{:T(512)S(6)} %or.15), kind=kLoop, calls=%fused_computation.7 | loop fusion | flops 524288 | bytes 3145729 | tf_op jit(solution)/shard_map/jit(_where)/select_n | solution.py:252
  12.1 1.3 %collective-permute-start.11 = (bf16[1024,256]{1,0:T(8,128)(2,1)S(1)}, bf16[1024,256]{1,0:T(8,128)(2,1)S(1)}, u32[]{:S(2)}, u32[]{:S(2)}) collective-permute-start(bf16[1024,256]{1,0:T(8,128)(2,1)S(1)} %get-tuple-element.48), channel_id=1, source_target_pairs={{0,16},{9,25},{18,2},{27,11},{8,24},{1,17},{26,10},{19,3},{4,12},{... | collective-permute-start | bytes 1572872 | tf_op jit(solution)/shard_map/ppermute | solution.py:190
  13.4 1.3 %collective-permute-start.2 = (bf16[1024,256]{1,0:T(8,128)(2,1)S(1)}, bf16[1024,256]{1,0:T(8,128)(2,1)}, u32[]{:S(2)}, u32[]{:S(2)}) collective-permute-start(bf16[1024,256]{1,0:T(8,128)(2,1)S(1)} %get-tuple-element.49), channel_id=1, source_target_pairs={{0,16},{9,25},{18,2},{27,11},{8,24},{1,17},{26,10},{19,3},{4,12},{... | collective-permute-start | bytes 1572872 | tf_op jit(solution)/shard_map/ppermute | solution.py:190
  14.7 1.3 %collective-permute-start.3 = (bf16[144,512]{1,0:T(8,128)(2,1)}, bf16[144,512]{1,0:T(8,128)(2,1)S(1)}, u32[]{:S(2)}, u32[]{:S(2)}) collective-permute-start(bf16[144,512]{1,0:T(8,128)(2,1)} %get-tuple-element.32), channel_id=1, source_target_pairs={{0,1},{1,0},{2,3},{3,2},{4,5},{5,4},{6,7},{7,6},{8,9},{9,8},{10,11... | collective-permute-start | bytes 442376 | tf_op jit(solution)/shard_map/ppermute | solution.py:37
  16.0 11.8 %collective-permute-start.4 = (bf16[144,512]{1,0:T(8,128)(2,1)}, bf16[144,512]{1,0:T(8,128)(2,1)S(1)}, u32[]{:S(2)}, u32[]{:S(2)}) collective-permute-start(bf16[144,512]{1,0:T(8,128)(2,1)} %get-tuple-element.33), channel_id=1, source_target_pairs={{0,2},{1,3},{2,0},{3,1},{4,6},{5,7},{6,4},{7,5},{8,10},{9,11},{10,... | collective-permute-start | bytes 442376 | tf_op jit(solution)/shard_map/ppermute | solution.py:37
  27.8 3.4 %all-to-all-start = ((bf16[8,32,512]{2,1,0:T(8,128)(2,1)}), bf16[8,32,512]{2,1,0:T(8,128)(2,1)S(1)}, u32[]{:S(2)}, u32[]{:S(2)}) async-start(bf16[8,32,512]{2,1,0:T(8,128)(2,1)} %bitcast.13), calls=%async_computation | async-start | bytes 524288 | tf_op jit(solution)/shard_map/all_to_all | solution.py:258
  32.8 1.2 %convolution_convert_fusion.1 = bf16[512,256]{1,0:T(8,128)(2,1)} fusion(bf16[512,1024]{1,0:T(8,128)(2,1)S(1)} %collective-permute-done.1.got_ref, bf16[1024,256]{1,0:T(8,128)(2,1)S(1)} %collective-permute-done.11, bf16[1024,256]{1,0:T(8,128)(2,1)S(1)} %get-tuple-element.48, pred[]{:T(512)S(6)} %or.18), kind=kOutput, calls=%fused_computation.3 | convolution fusion | flops 268828672 | bytes 2359297 | tf_op jit(solution)/shard_map/dot_general | solution.py:21
  34.0 2.7 %all-to-all-done = bf16[8,32,512]{2,1,0:T(8,128)(2,1)S(1)} async-done(((bf16[8,32,512]{2,1,0:T(8,128)(2,1)}), bf16[8,32,512]{2,1,0:T(8,128)(2,1)S(1)}, u32[]{:S(2)}, u32[]{:S(2)}) %all-to-all-start) | async-done | bytes 262176 | tf_op jit(solution)/shard_map/all_to_all | solution.py:258
  36.6 1.6 %convolution_convert_fusion.2 = bf16[512,256]{1,0:T(8,128)(2,1)S(1)} fusion(bf16[512,1024]{1,0:T(8,128)(2,1)S(1)} %collective-permute-done.1.got_ref, bf16[1024,256]{1,0:T(8,128)(2,1)} %collective-permute-done.2, bf16[1024,256]{1,0:T(8,128)(2,1)S(1)} %get-tuple-element.49, pred[]{:T(512)S(6)} %or.18), kind=kOutput, calls=%fused_computation.4 | convolution fusion | flops 268828672 | bytes 2359297 | tf_op jit(solution)/shard_map/dot_general | solution.py:21
  40.3 1.4 %convolution_add_fusion = f32[512,256]{1,0:T(8,128)S(1)} fusion(bf16[512,1024]{1,0:T(8,128)(2,1)S(1)} %copy-done, bf16[512,256]{1,0:T(8,128)(2,1)} %collective-permute-done.12, bf16[1024,256]{1,0:T(8,128)(2,1)S(1)} %copy-done.11, bf16[1024,256]{1,0:T(8,128)(2,1)S(1)} %copy-done.7, pred[]{:T(512)S(6)} %or.18), kind=kOutput, calls=%fused_computation | convolution fusion | flops 268959744 | bytes 2883585 | tf_op jit(solution)/shard_map/dot_general | solution.py:21
  41.8 2.7 %collective-permute-start.13 = (bf16[256,256]{1,0:T(8,128)(2,1)S(1)}, bf16[256,256]{1,0:T(8,128)(2,1)S(1)}, u32[]{:S(2)}, u32[]{:S(2)}) collective-permute-start(bf16[256,256]{1,0:T(8,128)(2,1)S(1)} %slice.134), channel_id=1, source_target_pairs={{0,1},{1,0},{2,3},{3,2},{4,5},{5,4},{6,7},{7,6},{8,9},{9,8},{10,11... | collective-permute-start | bytes 393224 | tf_op jit(solution)/shard_map/ppermute | solution.py:37
  44.5 1.5 %convolution_add_fusion.1 = f32[512,256]{1,0:T(8,128)S(1)} fusion(bf16[512,1024]{1,0:T(8,128)(2,1)S(1)} %copy-done, bf16[512,256]{1,0:T(8,128)(2,1)S(1)} %collective-permute-done.6, bf16[1024,256]{1,0:T(8,128)(2,1)} %collective-permute-done.2, bf16[1024,256]{1,0:T(8,128)(2,1)S(1)} %get-tuple-element.49, pred[]{:T(512)S(6)} %or.18), kind=kOutput, calls=%fused_computation.1 | convolution fusion | flops 268959744 | bytes 2883585 | tf_op jit(solution)/shard_map/dot_general | solution.py:21
  46.1 2.3 %collective-permute-done.13 = bf16[256,256]{1,0:T(8,128)(2,1)S(1)} collective-permute-done((bf16[256,256]{1,0:T(8,128)(2,1)S(1)}, bf16[256,256]{1,0:T(8,128)(2,1)S(1)}, u32[]{:S(2)}, u32[]{:S(2)}) %collective-permute-start.13) | collective-permute-done | bytes 131104 | tf_op jit(solution)/shard_map/ppermute | solution.py:37
  48.5 2.0 %collective-permute-start.14 = (bf16[128,256]{1,0:T(8,128)(2,1)S(1)}, bf16[128,256]{1,0:T(8,128)(2,1)S(1)}, u32[]{:S(2)}, u32[]{:S(2)}) collective-permute-start(bf16[128,256]{1,0:T(8,128)(2,1)S(1)} %slice.136), channel_id=1, source_target_pairs={{0,2},{1,3},{2,0},{3,1},{4,6},{5,7},{6,4},{7,5},{8,10},{9,11},{10,... | collective-permute-start | bytes 196616 | tf_op jit(solution)/shard_map/ppermute | solution.py:37
  50.5 1.2 %collective-permute-done.7 = bf16[256,256]{1,0:T(8,128)(2,1)S(1)} collective-permute-done((bf16[256,256]{1,0:T(8,128)(2,1)S(1)}, bf16[256,256]{1,0:T(8,128)(2,1)S(1)}, u32[]{:S(2)}, u32[]{:S(2)}) %collective-permute-start.7) | collective-permute-done | bytes 131104 | tf_op jit(solution)/shard_map/ppermute | solution.py:37
  53.9 3.1 %collective-permute-done.8 = bf16[128,256]{1,0:T(8,128)(2,1)S(1)} collective-permute-done((bf16[128,256]{1,0:T(8,128)(2,1)S(1)}, bf16[128,256]{1,0:T(8,128)(2,1)S(1)}, u32[]{:S(2)}, u32[]{:S(2)}) %collective-permute-start.8) | collective-permute-done | bytes 65568 | tf_op jit(solution)/shard_map/ppermute | solution.py:37
  58.1 2.0 %collective-permute-start.9 = (bf16[128,256]{1,0:T(8,128)(2,1)S(1)}, bf16[128,256]{1,0:T(8,128)(2,1)S(1)}, u32[]{:S(2)}, u32[]{:S(2)}) collective-permute-start(bf16[128,256]{1,0:T(8,128)(2,1)S(1)} %get-tuple-element.54), channel_id=1, source_target_pairs={{0,2},{1,3},{2,0},{3,1},{4,6},{5,7},{6,4},{7,5},{8,10},{9,11},{10,... | collective-permute-start | bytes 196616 | tf_op jit(solution)/shard_map/ppermute | solution.py:37
  60.1 2.3 %collective-permute-done.18 = bf16[128,256]{1,0:T(8,128)(2,1)S(1)} collective-permute-done((bf16[128,256]{1,0:T(8,128)(2,1)S(1)}, bf16[128,256]{1,0:T(8,128)(2,1)S(1)}, u32[]{:S(2)}, u32[]{:S(2)}) %collective-permute-start.18) | collective-permute-done | bytes 65568 | tf_op jit(solution)/shard_map/ppermute | solution.py:37
  62.5 1.4 %collective-permute-start.19 = (bf16[256,256]{1,0:T(8,128)(2,1)S(1)}, bf16[256,256]{1,0:T(8,128)(2,1)S(1)}, u32[]{:S(2)}, u32[]{:S(2)}) collective-permute-start(bf16[256,256]{1,0:T(8,128)(2,1)S(1)} %pad_maximum_fusion.4), channel_id=1, source_target_pairs={{0,1},{1,0},{2,3},{3,2},{4,5},{5,4},{6,7},{7,6},{8,9},{9,8},{10,11... | collective-permute-start | bytes 393224 | tf_op jit(solution)/shard_map/ppermute | solution.py:37
  63.9 1.9 %collective-permute-start.10 = (bf16[256,256]{1,0:T(8,128)(2,1)S(1)}, bf16[256,256]{1,0:T(8,128)(2,1)S(1)}, u32[]{:S(2)}, u32[]{:S(2)}) collective-permute-start(bf16[256,256]{1,0:T(8,128)(2,1)S(1)} %pad_maximum_fusion.3), channel_id=1, source_target_pairs={{0,1},{1,0},{2,3},{3,2},{4,5},{5,4},{6,7},{7,6},{8,9},{9,8},{10,11... | collective-permute-start | bytes 393224 | tf_op jit(solution)/shard_map/ppermute | solution.py:37
  65.8 1.7 %collective-permute-done.19 = bf16[256,256]{1,0:T(8,128)(2,1)S(1)} collective-permute-done((bf16[256,256]{1,0:T(8,128)(2,1)S(1)}, bf16[256,256]{1,0:T(8,128)(2,1)S(1)}, u32[]{:S(2)}, u32[]{:S(2)}) %collective-permute-start.19) | collective-permute-done | bytes 131104 | tf_op jit(solution)/shard_map/ppermute | solution.py:37
  69.2 2.1 %gradient.3 = (f32[512,256]{1,0:T(8,128)S(1)}, bf16[512,256]{1,0:T(8,128)(2,1)}) custom-call(s32[4]{0:T(128)S(1)} %pad_add_fusion.at, bf16[512,1024]{1,0:T(8,128)(2,1)S(1)} %copy-done, bf16[512,1024]{1,0:T(8,128)(2,1)S(1)} %collective-permute-done.1.got_ref, bf16[512,256]{1,0:T(8,128)(2,1)S(1)} %pad_maximum_fusion.1.slope_ref, ...), custom_call_target="tpu_custom_call" | custom-call | flops 536870912 | bytes 4194304 | tf_op jit(solution)/shard_map/gradient/pallas_call | solution.py:330
  71.3 1.5 %collective-permute-start.21 = (bf16[512,256]{1,0:T(8,128)(2,1)}, bf16[512,256]{1,0:T(8,128)(2,1)}, u32[]{:S(2)}, u32[]{:S(2)}) collective-permute-start(bf16[512,256]{1,0:T(8,128)(2,1)} %get-tuple-element.44), channel_id=1, source_target_pairs={{0,8},{4,20},{8,0},{12,28},{16,24},{20,4},{24,16},{28,12},{1,9},{5... | collective-permute-start | bytes 786440 | tf_op jit(solution)/shard_map/ppermute | solution.py:367
  72.8 1.4 %gradient.2 = (f32[512,256]{1,0:T(8,128)S(1)}, bf16[512,256]{1,0:T(8,128)(2,1)S(1)}) custom-call(s32[4]{0:T(128)S(1)} %pad_add_fusion.at, bf16[512,1024]{1,0:T(8,128)(2,1)S(1)} %copy-done, bf16[512,1024]{1,0:T(8,128)(2,1)S(1)} %collective-permute-done.1.got_ref, bf16[512,256]{1,0:T(8,128)(2,1)S(1)} %pad_maximum_fusion.slope_ref, ...), custom_call_target="tpu_custom_call" | custom-call | flops 536870912 | bytes 4194304 | tf_op jit(solution)/shard_map/gradient/pallas_call | solution.py:330
  74.8 7.0 %all-to-all-start.1 = ((bf16[8,32,512]{2,1,0:T(8,128)(2,1)}), bf16[8,32,512]{2,1,0:T(8,128)(2,1)S(1)}, u32[]{:S(2)}, u32[]{:S(2)}) async-start(bf16[8,32,512]{2,1,0:T(8,128)(2,1)} %bitcast.28), calls=%async_computation.1 | async-start | bytes 524288 | tf_op jit(solution)/shard_map/all_to_all | solution.py:325
  83.1 2.0 %collective-permute-start.17 = (bf16[256,256]{1,0:T(8,128)(2,1)S(1)}, bf16[256,256]{1,0:T(8,128)(2,1)S(1)}, u32[]{:S(2)}, u32[]{:S(2)}) collective-permute-start(bf16[256,256]{1,0:T(8,128)(2,1)S(1)} %slice.133), channel_id=1, source_target_pairs={{0,16},{4,12},{8,24},{12,4},{16,0},{20,28},{24,8},{28,20},{1,17},{... | collective-permute-start | bytes 393224 | tf_op jit(solution)/shard_map/ppermute | solution.py:367
  85.1 3.3 %collective-permute-done.22 = bf16[256,256]{1,0:T(8,128)(2,1)S(1)} collective-permute-done((bf16[256,256]{1,0:T(8,128)(2,1)S(1)}, bf16[256,256]{1,0:T(8,128)(2,1)S(1)}, u32[]{:S(2)}, u32[]{:S(2)}) %collective-permute-start.22) | collective-permute-done | bytes 131104 | tf_op jit(solution)/shard_map/ppermute | solution.py:367
  88.4 1.4 %collective-permute-done.17 = bf16[256,256]{1,0:T(8,128)(2,1)S(1)} collective-permute-done((bf16[256,256]{1,0:T(8,128)(2,1)S(1)}, bf16[256,256]{1,0:T(8,128)(2,1)S(1)}, u32[]{:S(2)}, u32[]{:S(2)}) %collective-permute-start.17) | collective-permute-done | bytes 131104 | tf_op jit(solution)/shard_map/ppermute | solution.py:367
  89.9 3.2 %collective-permute-start.23 = (bf16[256,512]{1,0:T(8,128)(2,1)S(1)}, bf16[256,512]{1,0:T(8,128)(2,1)S(1)}, u32[]{:S(2)}, u32[]{:S(2)}) collective-permute-start(bf16[256,512]{1,0:T(8,128)(2,1)S(1)} %pad_maximum_fusion.2), channel_id=1, source_target_pairs={{0,0},{1,10},{2,17},{3,27},{4,4},{5,14},{6,21},{7,31},{8,1},{9,11}... | collective-permute-start | bytes 786440 | tf_op jit(solution)/shard_map/ppermute | solution.py:379
  93.0 1.7 %write.1 = bf16[256,512]{1,0:T(8,128)(2,1)} custom-call(bf16[256,512]{1,0:T(8,128)(2,1)} %bitcast.29), custom_call_target="tpu_custom_call" | custom-call | bytes 524288 | tf_op jit(solution)/shard_map/write/pallas_call | solution.py:380
  94.7 8.1 %collective-permute-done.23 = bf16[256,512]{1,0:T(8,128)(2,1)S(1)} collective-permute-done((bf16[256,512]{1,0:T(8,128)(2,1)S(1)}, bf16[256,512]{1,0:T(8,128)(2,1)S(1)}, u32[]{:S(2)}, u32[]{:S(2)}) %collective-permute-start.23) | collective-permute-done | bytes 262176 | tf_op jit(solution)/shard_map/ppermute | solution.py:379
  (77 shorter events, 14.3 us)
Async XLA Ops:
  0.6 8.8 %collective-permute-start = (bf16[1024,512]{1,0:T(8,128)(2,1)}, bf16[1024,512]{1,0:T(8,128)(2,1)S(1)}, u32[]{:S(2)}, u32[]{:S(2)}) collective-permute-start(bf16[1024,512]{1,0:T(8,128)(2,1)} %param.14), channel_id=1, source_target_pairs={{0,8},{9,1},{18,26},{27,19},{4,20},{13,29},{22,6},{31,15}} | collective-permute-start | bytes 3145736 | tf_op jit(solution)/shard_map/ppermute | solution.py:190
  9.0 22.1 %collective-permute-start.1 = (bf16[512,1024]{1,0:T(8,128)(2,1)}, bf16[512,1024]{1,0:T(8,128)(2,1)S(1)}, u32[]{:S(2)}, u32[]{:S(2)}) collective-permute-start(bf16[512,1024]{1,0:T(8,128)(2,1)} %get-tuple-element.27), channel_id=1, source_target_pairs={{0,4},{4,0},{8,12},{12,8},{16,20},{20,16},{24,28},{28,24},{1,5},{5... | collective-permute-start | bytes 3145736 | tf_op jit(solution)/shard_map/ppermute | solution.py:29
  12.1 19.9 %copy-start.6 = (bf16[1024,256]{1,0:T(8,128)(2,1)}, bf16[1024,256]{1,0:T(8,128)(2,1)S(1)}, u32[]{:S(2)}) copy-start(bf16[1024,256]{1,0:T(8,128)(2,1)S(1)} %get-tuple-element.48) | copy-start | bytes 1572868
  12.1 19.9 %collective-permute-start.11 = (bf16[1024,256]{1,0:T(8,128)(2,1)S(1)}, bf16[1024,256]{1,0:T(8,128)(2,1)S(1)}, u32[]{:S(2)}, u32[]{:S(2)}) collective-permute-start(bf16[1024,256]{1,0:T(8,128)(2,1)S(1)} %get-tuple-element.48), channel_id=1, source_target_pairs={{0,16},{9,25},{18,2},{27,11},{8,24},{1,17},{26,10},{19,3},{4,12},{... | collective-permute-start | bytes 1572872 | tf_op jit(solution)/shard_map/ppermute | solution.py:190
  13.4 23.3 %collective-permute-start.2 = (bf16[1024,256]{1,0:T(8,128)(2,1)S(1)}, bf16[1024,256]{1,0:T(8,128)(2,1)}, u32[]{:S(2)}, u32[]{:S(2)}) collective-permute-start(bf16[1024,256]{1,0:T(8,128)(2,1)S(1)} %get-tuple-element.49), channel_id=1, source_target_pairs={{0,16},{9,25},{18,2},{27,11},{8,24},{1,17},{26,10},{19,3},{4,12},{... | collective-permute-start | bytes 1572872 | tf_op jit(solution)/shard_map/ppermute | solution.py:190
  14.7 23.6 %collective-permute-start.3 = (bf16[144,512]{1,0:T(8,128)(2,1)}, bf16[144,512]{1,0:T(8,128)(2,1)S(1)}, u32[]{:S(2)}, u32[]{:S(2)}) collective-permute-start(bf16[144,512]{1,0:T(8,128)(2,1)} %get-tuple-element.32), channel_id=1, source_target_pairs={{0,1},{1,0},{2,3},{3,2},{4,5},{5,4},{6,7},{7,6},{8,9},{9,8},{10,11... | collective-permute-start | bytes 442376 | tf_op jit(solution)/shard_map/ppermute | solution.py:37
  16.0 22.3 %collective-permute-start.4 = (bf16[144,512]{1,0:T(8,128)(2,1)}, bf16[144,512]{1,0:T(8,128)(2,1)S(1)}, u32[]{:S(2)}, u32[]{:S(2)}) collective-permute-start(bf16[144,512]{1,0:T(8,128)(2,1)} %get-tuple-element.33), channel_id=1, source_target_pairs={{0,2},{1,3},{2,0},{3,1},{4,6},{5,7},{6,4},{7,5},{8,10},{9,11},{10,... | collective-permute-start | bytes 442376 | tf_op jit(solution)/shard_map/ppermute | solution.py:37
  27.8 8.9 %all-to-all-start = ((bf16[8,32,512]{2,1,0:T(8,128)(2,1)}), bf16[8,32,512]{2,1,0:T(8,128)(2,1)S(1)}, u32[]{:S(2)}, u32[]{:S(2)}) async-start(bf16[8,32,512]{2,1,0:T(8,128)(2,1)} %bitcast.13), calls=%async_computation | async-start | bytes 524288 | tf_op jit(solution)/shard_map/all_to_all | solution.py:258
  31.1 8.1 %copy-start.1 = (bf16[144,512]{1,0:T(8,128)(2,1)S(1)}, bf16[144,512]{1,0:T(8,128)(2,1)}, u32[]{:S(2)}) copy-start(bf16[144,512]{1,0:T(8,128)(2,1)} %get-tuple-element.31.refs_0_) | copy-start | bytes 442372
  31.1 8.1 %copy-start.2 = (s32[1,1,8]{2,1,0:T(1,128)S(1)}, s32[1,1,8]{2,1,0:T(1,128)}, u32[]{:S(2)}) copy-start(s32[1,1,8]{2,1,0:T(1,128)} %param.15) | copy-start | bytes 100
  31.2 8.0 %copy-start.3 = (s32[1,1,8]{2,1,0:T(1,128)S(1)}, s32[1,1,8]{2,1,0:T(1,128)}, u32[]{:S(2)}) copy-start(s32[1,1,8]{2,1,0:T(1,128)} %param.16) | copy-start | bytes 100
  31.2 8.0 %copy-start.4 = (f32[1,1,8]{2,1,0:T(1,128)S(1)}, f32[1,1,8]{2,1,0:T(1,128)}, u32[]{:S(2)}) copy-start(f32[1,1,8]{2,1,0:T(1,128)} %param.17) | copy-start | bytes 100
  31.2 8.0 %copy-start.5 = (f32[128]{0:T(128)S(1)}, f32[128]{0:T(128)}, u32[]{:S(2)}) copy-start(f32[128]{0:T(128)} %param.18) | copy-start | bytes 1540
  31.2 8.0 %collective-permute-start.5 = (bf16[144,512]{1,0:T(8,128)(2,1)}, bf16[144,512]{1,0:T(8,128)(2,1)S(1)}, u32[]{:S(2)}, u32[]{:S(2)}) collective-permute-start(bf16[144,512]{1,0:T(8,128)(2,1)} %get-tuple-element.34), channel_id=1, source_target_pairs={{0,3},{1,2},{2,1},{3,0},{4,7},{5,6},{6,5},{7,4},{8,11},{9,10},{10,... | collective-permute-start | bytes 442376 | tf_op jit(solution)/shard_map/ppermute | solution.py:37
  34.0 6.3 %collective-permute-start.12 = (bf16[512,256]{1,0:T(8,128)(2,1)}, bf16[512,256]{1,0:T(8,128)(2,1)}, u32[]{:S(2)}, u32[]{:S(2)}) collective-permute-start(bf16[512,256]{1,0:T(8,128)(2,1)} %convolution_convert_fusion.1), channel_id=1, source_target_pairs={{0,4},{4,0},{8,12},{12,8},{16,20},{20,16},{24,28},{28,24},{1,5},{5... | collective-permute-start | bytes 786440 | tf_op jit(solution)/shard_map/ppermute | solution.py:29
  38.2 6.2 %collective-permute-start.6 = (bf16[512,256]{1,0:T(8,128)(2,1)S(1)}, bf16[512,256]{1,0:T(8,128)(2,1)S(1)}, u32[]{:S(2)}, u32[]{:S(2)}) collective-permute-start(bf16[512,256]{1,0:T(8,128)(2,1)S(1)} %convolution_convert_fusion.2), channel_id=1, source_target_pairs={{0,4},{4,0},{8,12},{12,8},{16,20},{20,16},{24,28},{28,24},{1,5},{5... | collective-permute-start | bytes 786440 | tf_op jit(solution)/shard_map/ppermute | solution.py:29
  41.8 6.7 %collective-permute-start.13 = (bf16[256,256]{1,0:T(8,128)(2,1)S(1)}, bf16[256,256]{1,0:T(8,128)(2,1)S(1)}, u32[]{:S(2)}, u32[]{:S(2)}) collective-permute-start(bf16[256,256]{1,0:T(8,128)(2,1)S(1)} %slice.134), channel_id=1, source_target_pairs={{0,1},{1,0},{2,3},{3,2},{4,5},{5,4},{6,7},{7,6},{8,9},{9,8},{10,11... | collective-permute-start | bytes 393224 | tf_op jit(solution)/shard_map/ppermute | solution.py:37
  46.0 5.7 %collective-permute-start.7 = (bf16[256,256]{1,0:T(8,128)(2,1)S(1)}, bf16[256,256]{1,0:T(8,128)(2,1)S(1)}, u32[]{:S(2)}, u32[]{:S(2)}) collective-permute-start(bf16[256,256]{1,0:T(8,128)(2,1)S(1)} %slice.135), channel_id=1, source_target_pairs={{0,1},{1,0},{2,3},{3,2},{4,5},{5,4},{6,7},{7,6},{8,9},{9,8},{10,11... | collective-permute-start | bytes 393224 | tf_op jit(solution)/shard_map/ppermute | solution.py:37
  48.5 5.4 %collective-permute-start.14 = (bf16[128,256]{1,0:T(8,128)(2,1)S(1)}, bf16[128,256]{1,0:T(8,128)(2,1)S(1)}, u32[]{:S(2)}, u32[]{:S(2)}) collective-permute-start(bf16[128,256]{1,0:T(8,128)(2,1)S(1)} %slice.136), channel_id=1, source_target_pairs={{0,2},{1,3},{2,0},{3,1},{4,6},{5,7},{6,4},{7,5},{8,10},{9,11},{10,... | collective-permute-start | bytes 196616 | tf_op jit(solution)/shard_map/ppermute | solution.py:37
  51.8 5.2 %collective-permute-start.8 = (bf16[128,256]{1,0:T(8,128)(2,1)S(1)}, bf16[128,256]{1,0:T(8,128)(2,1)S(1)}, u32[]{:S(2)}, u32[]{:S(2)}) collective-permute-start(bf16[128,256]{1,0:T(8,128)(2,1)S(1)} %slice.137), channel_id=1, source_target_pairs={{0,2},{1,3},{2,0},{3,1},{4,6},{5,7},{6,4},{7,5},{8,10},{9,11},{10,... | collective-permute-start | bytes 196616 | tf_op jit(solution)/shard_map/ppermute | solution.py:37
  57.1 5.3 %collective-permute-start.18 = (bf16[128,256]{1,0:T(8,128)(2,1)S(1)}, bf16[128,256]{1,0:T(8,128)(2,1)S(1)}, u32[]{:S(2)}, u32[]{:S(2)}) collective-permute-start(bf16[128,256]{1,0:T(8,128)(2,1)S(1)} %get-tuple-element.53), channel_id=1, source_target_pairs={{0,2},{1,3},{2,0},{3,1},{4,6},{5,7},{6,4},{7,5},{8,10},{9,11},{10,... | collective-permute-start | bytes 196616 | tf_op jit(solution)/shard_map/ppermute | solution.py:37
  58.1 5.8 %collective-permute-start.9 = (bf16[128,256]{1,0:T(8,128)(2,1)S(1)}, bf16[128,256]{1,0:T(8,128)(2,1)S(1)}, u32[]{:S(2)}, u32[]{:S(2)}) collective-permute-start(bf16[128,256]{1,0:T(8,128)(2,1)S(1)} %get-tuple-element.54), channel_id=1, source_target_pairs={{0,2},{1,3},{2,0},{3,1},{4,6},{5,7},{6,4},{7,5},{8,10},{9,11},{10,... | collective-permute-start | bytes 196616 | tf_op jit(solution)/shard_map/ppermute | solution.py:37
  62.5 5.0 %collective-permute-start.19 = (bf16[256,256]{1,0:T(8,128)(2,1)S(1)}, bf16[256,256]{1,0:T(8,128)(2,1)S(1)}, u32[]{:S(2)}, u32[]{:S(2)}) collective-permute-start(bf16[256,256]{1,0:T(8,128)(2,1)S(1)} %pad_maximum_fusion.4), channel_id=1, source_target_pairs={{0,1},{1,0},{2,3},{3,2},{4,5},{5,4},{6,7},{7,6},{8,9},{9,8},{10,11... | collective-permute-start | bytes 393224 | tf_op jit(solution)/shard_map/ppermute | solution.py:37
  63.9 5.0 %collective-permute-start.10 = (bf16[256,256]{1,0:T(8,128)(2,1)S(1)}, bf16[256,256]{1,0:T(8,128)(2,1)S(1)}, u32[]{:S(2)}, u32[]{:S(2)}) collective-permute-start(bf16[256,256]{1,0:T(8,128)(2,1)S(1)} %pad_maximum_fusion.3), channel_id=1, source_target_pairs={{0,1},{1,0},{2,3},{3,2},{4,5},{5,4},{6,7},{7,6},{8,9},{9,8},{10,11... | collective-permute-start | bytes 393224 | tf_op jit(solution)/shard_map/ppermute | solution.py:37
  67.5 1.7 %collective-permute-start.20 = (bf16[512,256]{1,0:T(8,128)(2,1)S(1)}, bf16[512,256]{1,0:T(8,128)(2,1)S(1)}, u32[]{:S(2)}, u32[]{:S(2)}) collective-permute-start(bf16[512,256]{1,0:T(8,128)(2,1)S(1)} %pad_maximum_fusion.1.slope_ref), channel_id=1, source_target_pairs={{0,4},{4,0},{8,12},{12,8},{16,20},{20,16},{24,28},{28,24},{1,5},{5... | collective-permute-start | bytes 786440 | tf_op jit(solution)/shard_map/ppermute | solution.py:29
  68.9 3.9 %collective-permute-start.15 = (bf16[512,256]{1,0:T(8,128)(2,1)S(1)}, bf16[512,256]{1,0:T(8,128)(2,1)S(1)}, u32[]{:S(2)}, u32[]{:S(2)}) collective-permute-start(bf16[512,256]{1,0:T(8,128)(2,1)S(1)} %pad_maximum_fusion.slope_ref), channel_id=1, source_target_pairs={{0,4},{4,0},{8,12},{12,8},{16,20},{20,16},{24,28},{28,24},{1,5},{5... | collective-permute-start | bytes 786440 | tf_op jit(solution)/shard_map/ppermute | solution.py:29
  71.3 10.5 %collective-permute-start.21 = (bf16[512,256]{1,0:T(8,128)(2,1)}, bf16[512,256]{1,0:T(8,128)(2,1)}, u32[]{:S(2)}, u32[]{:S(2)}) collective-permute-start(bf16[512,256]{1,0:T(8,128)(2,1)} %get-tuple-element.44), channel_id=1, source_target_pairs={{0,8},{4,20},{8,0},{12,28},{16,24},{20,4},{24,16},{28,12},{1,9},{5... | collective-permute-start | bytes 786440 | tf_op jit(solution)/shard_map/ppermute | solution.py:367
  74.2 8.8 %collective-permute-start.16 = (bf16[512,256]{1,0:T(8,128)(2,1)S(1)}, bf16[512,256]{1,0:T(8,128)(2,1)S(1)}, u32[]{:S(2)}, u32[]{:S(2)}) collective-permute-start(bf16[512,256]{1,0:T(8,128)(2,1)S(1)} %get-tuple-element.42), channel_id=1, source_target_pairs={{0,8},{4,20},{8,0},{12,28},{16,24},{20,4},{24,16},{28,12},{1,9},{5... | collective-permute-start | bytes 786440 | tf_op jit(solution)/shard_map/ppermute | solution.py:367
  74.8 15.0 %all-to-all-start.1 = ((bf16[8,32,512]{2,1,0:T(8,128)(2,1)}), bf16[8,32,512]{2,1,0:T(8,128)(2,1)S(1)}, u32[]{:S(2)}, u32[]{:S(2)}) async-start(bf16[8,32,512]{2,1,0:T(8,128)(2,1)} %bitcast.28), calls=%async_computation.1 | async-start | bytes 524288 | tf_op jit(solution)/shard_map/all_to_all | solution.py:325
  82.8 5.5 %collective-permute-start.22 = (bf16[256,256]{1,0:T(8,128)(2,1)S(1)}, bf16[256,256]{1,0:T(8,128)(2,1)S(1)}, u32[]{:S(2)}, u32[]{:S(2)}) collective-permute-start(bf16[256,256]{1,0:T(8,128)(2,1)S(1)} %slice.132), channel_id=1, source_target_pairs={{0,16},{4,12},{8,24},{12,4},{16,0},{20,28},{24,8},{28,20},{1,17},{... | collective-permute-start | bytes 393224 | tf_op jit(solution)/shard_map/ppermute | solution.py:367
  83.1 6.7 %collective-permute-start.17 = (bf16[256,256]{1,0:T(8,128)(2,1)S(1)}, bf16[256,256]{1,0:T(8,128)(2,1)S(1)}, u32[]{:S(2)}, u32[]{:S(2)}) collective-permute-start(bf16[256,256]{1,0:T(8,128)(2,1)S(1)} %slice.133), channel_id=1, source_target_pairs={{0,16},{4,12},{8,24},{12,4},{16,0},{20,28},{24,8},{28,20},{1,17},{... | collective-permute-start | bytes 393224 | tf_op jit(solution)/shard_map/ppermute | solution.py:367
  89.9 12.9 %collective-permute-start.23 = (bf16[256,512]{1,0:T(8,128)(2,1)S(1)}, bf16[256,512]{1,0:T(8,128)(2,1)S(1)}, u32[]{:S(2)}, u32[]{:S(2)}) collective-permute-start(bf16[256,512]{1,0:T(8,128)(2,1)S(1)} %pad_maximum_fusion.2), channel_id=1, source_target_pairs={{0,0},{1,10},{2,17},{3,27},{4,4},{5,14},{6,21},{7,31},{8,1},{9,11}... | collective-permute-start | bytes 786440 | tf_op jit(solution)/shard_map/ppermute | solution.py:379
  (6 other events, 18.7 us)

commit v16 on v15

--- a/solution.py
+++ b/solution.py
@@ -276,6 +276,8 @@
         value_got = swapped(value_given, dp_count).astype(F32)
         value_parts.append(dot(kept_rows, weight) + value_got)
 
+    tied = (value_parts[-1], lengths, bins, advantage, logprob_gap)
+    value_parts[-1], lengths, bins, advantage, logprob_gap = lax.optimization_barrier(tied)
     smem = pl.BlockSpec(memory_space=pltpu.SMEM)
     vmem = pl.BlockSpec(memory_space=pltpu.VMEM)
     fixed, pull, row_scale, row_at = pl.pallas_call(

time: 104 us -> 104 us (level)
  starting transfers between devices: 47.7 us -> 45 us
  waiting for transfers between devices: 28.6 us -> 29.9 us
  matrix products: 6.57 us -> 7.69 us
    ppermute x11, starting transfers between devices: 25.9 us -> 23.8 us  [crossed(): return lax.ppermute(array, 'tensor', [(i, i ^ step) for i in range(count)])]
    all_to_all x1, starting transfers between devices: 6.98 us -> 5.13 us  [on_device(): lax.all_to_all(sent, 'dp', split_axis=0, concat_axis=0, tiled=True)]
    ppermute x11, waiting for transfers between devices: 13.1 us -> 14.8 us  [crossed(): return lax.ppermute(array, 'tensor', [(i, i ^ step) for i in range(count)])]
    ppermute x4, starting transfers between devices: 4.25 us -> 5.43 us  [on_device(): total = total + lax.ppermute(given, 'dp', pairs).astype(F32)]
    dot_general x4, matrix products: 5.61 us -> 6.73 us  [dot(): return jnp.dot(a, b, preferred_element_type=F32)]
  transfers between devices with their start and end apart: 26 -> 26, of which waited for: 12 -> 12; matrix products, arithmetic and copies ran while one was open for 10% -> 11% of each run, Pallas kernels for 13% -> 13%
where the time goes in v16:
time: 104 us; the launch traced here: 103 us
  starting transfers between devices  45 us (43%)
  waiting for transfers between devices  29.9 us (29%)
  Pallas kernels  13.3 us (13%)
  matrix products  7.69 us (7%)
  other arithmetic  4.96 us (5%)
  local copies, waits for them, and re-layouts  1.22 us (1%)
    ppermute x11, starting transfers between devices, crossed(): return lax.ppermute(array, 'tensor', [(i, i ^ step) for i in range(count)])  23.8 us
    ppermute x11, waiting for transfers between devices, crossed(): return lax.ppermute(array, 'tensor', [(i, i ^ step) for i in range(count)])  14.8 us
    ppermute x1, waiting for transfers between devices, on_device(): grad_weight = lax.ppermute(grad, AXES, pairs).astype(F32)  7.99 us
    pallas_call x1, Pallas kernels, on_device(): pl.pallas_call(functools.partial(prepare_kernel, tensor_count, steps), gr...  7.11 us
    dot_general x4, matrix products, dot(): return jnp.dot(a, b, preferred_element_type=F32)  6.73 us
    ppermute x4, starting transfers between devices, on_device(): total = total + lax.ppermute(given, 'dp', pairs).astype(F32)  5.43 us
    all_to_all x1, starting transfers between devices, on_device(): lax.all_to_all(sent, 'dp', split_axis=0, concat_axis=0, tiled=True)  5.13 us
    ppermute x4, waiting for transfers between devices, on_device(): total = total + lax.ppermute(given, 'dp', pairs).astype(F32)  4.72 us
  transfers between devices with their start and end apart: 26, of which 12 were waited for; matrix products, arithmetic and copies ran while one was open for 11% of the time, Pallas kernels for 13%

profile of v16, /device:TPU:4, one launch (start us, length us, event | category | flops | bytes accessed | tf_op | source)
XLA Modules:
  0.0 103.2 jit_solution(4329796580326840226)
XLA Ops:
  2.0 7.1 %prepare.1 = (bf16[512,1024]{1,0:T(8,128)(2,1)}, bf16[512,1024]{1,0:T(8,128)(2,1)}, bf16[144,512]{1,0:T(8,128)(2,1)}, bf16[144,512]{1,0:T(8,128)(2,1)}, bf16[144...) custom-call(s32[2]{0:T(128)} %pad_add_fusion.1.at, bf16[512,2048]{1,0:T(8,128)(2,1)} %x_ref.1, f32[1,2048]{1,0:T(1,128)} %bitcast.32, ...), custom_call_target="tpu_custom_call" | custom-call | flops 1073741824 | bytes 8388608 | tf_op jit(solution)/shard_map/prepare/pallas_call | solution.py:202
  10.6 2.1 %slice_select_fusion = (bf16[1024,256]{1,0:T(8,128)(2,1)S(1)}, bf16[1024,256]{1,0:T(8,128)(2,1)}) fusion(bf16[1024,512]{1,0:T(8,128)(2,1)S(1)} %copy-done.6, bf16[1024,512]{1,0:T(8,128)(2,1)} %copy-done.7, pred[]{:T(512)S(6)} %or.18), kind=kLoop, calls=%fused_computation.7 | loop fusion | flops 524288 | bytes 3145729 | tf_op jit(solution)/shard_map/jit(_where)/select_n | solution.py:252
  12.7 1.3 %collective-permute-start.2 = (bf16[1024,256]{1,0:T(8,128)(2,1)}, bf16[1024,256]{1,0:T(8,128)(2,1)}, u32[]{:S(2)}, u32[]{:S(2)}) collective-permute-start(bf16[1024,256]{1,0:T(8,128)(2,1)} %get-tuple-element.59), channel_id=1, source_target_pairs={{0,16},{9,25},{18,2},{27,11},{8,24},{1,17},{26,10},{19,3},{4,12},{... | collective-permute-start | bytes 1572872 | tf_op jit(solution)/shard_map/ppermute | solution.py:190
  13.9 1.3 %collective-permute-start.4 = (bf16[1024,256]{1,0:T(8,128)(2,1)S(1)}, bf16[1024,256]{1,0:T(8,128)(2,1)}, u32[]{:S(2)}, u32[]{:S(2)}) collective-permute-start(bf16[1024,256]{1,0:T(8,128)(2,1)S(1)} %get-tuple-element.58), channel_id=1, source_target_pairs={{0,16},{9,25},{18,2},{27,11},{8,24},{1,17},{26,10},{19,3},{4,12},{... | collective-permute-start | bytes 1572872 | tf_op jit(solution)/shard_map/ppermute | solution.py:190
  15.2 1.3 %collective-permute-start.5 = (bf16[144,512]{1,0:T(8,128)(2,1)}, bf16[144,512]{1,0:T(8,128)(2,1)S(1)}, u32[]{:S(2)}, u32[]{:S(2)}) collective-permute-start(bf16[144,512]{1,0:T(8,128)(2,1)} %get-tuple-element.41), channel_id=1, source_target_pairs={{0,1},{1,0},{2,3},{3,2},{4,5},{5,4},{6,7},{7,6},{8,9},{9,8},{10,11... | collective-permute-start | bytes 442376 | tf_op jit(solution)/shard_map/ppermute | solution.py:37
  16.5 12.4 %collective-permute-start.6 = (bf16[144,512]{1,0:T(8,128)(2,1)}, bf16[144,512]{1,0:T(8,128)(2,1)S(1)}, u32[]{:S(2)}, u32[]{:S(2)}) collective-permute-start(bf16[144,512]{1,0:T(8,128)(2,1)} %get-tuple-element.42), channel_id=1, source_target_pairs={{0,2},{1,3},{2,0},{3,1},{4,6},{5,7},{6,4},{7,5},{8,10},{9,11},{10,... | collective-permute-start | bytes 442376 | tf_op jit(solution)/shard_map/ppermute | solution.py:37
  29.0 3.4 %all-to-all-start = ((bf16[8,32,512]{2,1,0:T(8,128)(2,1)}), bf16[8,32,512]{2,1,0:T(8,128)(2,1)S(1)}, u32[]{:S(2)}, u32[]{:S(2)}) async-start(bf16[8,32,512]{2,1,0:T(8,128)(2,1)} %bitcast.13), calls=%async_computation | async-start | bytes 524288 | tf_op jit(solution)/shard_map/all_to_all | solution.py:258
  33.2 2.2 %convolution_convert_fusion.2 = bf16[512,256]{1,0:T(8,128)(2,1)} fusion(bf16[512,1024]{1,0:T(8,128)(2,1)S(1)} %collective-permute-done.1.got_ref, bf16[1024,256]{1,0:T(8,128)(2,1)} %collective-permute-done.2, bf16[1024,256]{1,0:T(8,128)(2,1)} %get-tuple-element.59, pred[]{:T(512)S(6)} %or.17), kind=kOutput, calls=%fused_computation.4 | convolution fusion | flops 268828672 | bytes 2359297 | tf_op jit(solution)/shard_map/dot_general | solution.py:21
  35.4 2.4 %all-to-all-done = bf16[8,32,512]{2,1,0:T(8,128)(2,1)S(1)} async-done(((bf16[8,32,512]{2,1,0:T(8,128)(2,1)}), bf16[8,32,512]{2,1,0:T(8,128)(2,1)S(1)}, u32[]{:S(2)}, u32[]{:S(2)}) %all-to-all-start) | async-done | bytes 262176 | tf_op jit(solution)/shard_map/all_to_all | solution.py:258
  37.7 1.5 %convolution_convert_fusion.1 = bf16[512,256]{1,0:T(8,128)(2,1)S(1)} fusion(bf16[512,1024]{1,0:T(8,128)(2,1)S(1)} %collective-permute-done.1.got_ref, bf16[1024,256]{1,0:T(8,128)(2,1)} %collective-permute-done.4, bf16[1024,256]{1,0:T(8,128)(2,1)S(1)} %get-tuple-element.58, pred[]{:T(512)S(6)} %or.17), kind=kOutput, calls=%fused_computation.3 | convolution fusion | flops 268828672 | bytes 2359297 | tf_op jit(solution)/shard_map/dot_general | solution.py:21
  39.3 1.6 %convolution_add_fusion.1 = f32[512,256]{1,0:T(8,128)S(1)} fusion(bf16[512,1024]{1,0:T(8,128)(2,1)S(1)} %copy-done, bf16[512,256]{1,0:T(8,128)(2,1)} %collective-permute-done.3, bf16[1024,256]{1,0:T(8,128)(2,1)} %collective-permute-done.2, bf16[1024,256]{1,0:T(8,128)(2,1)} %get-tuple-element.59, pred[]{:T(512)S(6)} %or.17), kind=kOutput, calls=%fused_computation.1 | convolution fusion | flops 268959744 | bytes 2883585 | tf_op jit(solution)/shard_map/dot_general | solution.py:21
  41.0 2.1 %collective-permute-start.13 = (bf16[256,256]{1,0:T(8,128)(2,1)S(1)}, bf16[256,256]{1,0:T(8,128)(2,1)S(1)}, u32[]{:S(2)}, u32[]{:S(2)}) collective-permute-start(bf16[256,256]{1,0:T(8,128)(2,1)S(1)} %slice.133), channel_id=1, source_target_pairs={{0,1},{1,0},{2,3},{3,2},{4,5},{5,4},{6,7},{7,6},{8,9},{9,8},{10,11... | collective-permute-start | bytes 393224 | tf_op jit(solution)/shard_map/ppermute | solution.py:37
  43.1 1.5 %convolution_add_fusion = f32[512,256]{1,0:T(8,128)S(1)} fusion(bf16[512,1024]{1,0:T(8,128)(2,1)S(1)} %copy-done, bf16[512,256]{1,0:T(8,128)(2,1)S(1)} %collective-permute-done.8, bf16[1024,256]{1,0:T(8,128)(2,1)} %collective-permute-done.4, bf16[1024,256]{1,0:T(8,128)(2,1)S(1)} %get-tuple-element.58, pred[]{:T(512)S(6)} %or.17), kind=kOutput, calls=%fused_computation | convolution fusion | flops 268959744 | bytes 2883585 | tf_op jit(solution)/shard_map/dot_general | solution.py:21
  44.8 1.1 %rows.1 = (f32[128,512]{1,0:T(8,128)S(1)}, f32[128,128]{1,0:T(8,128)S(1)}, f32[128,128]{1,0:T(8,128)S(1)}, bf16[128,256]{1,0:T(8,128)(2,1)S(1)}) custom-call(s32[8]{0:T(128)S(1)} %bitcast.24, s32[8]{0:T(128)S(1)} %bitcast.25, f32[8]{0:T(128)S(1)} %bitcast.26, f32[1,128]{1,0:T(1,128)S(1)} %bitcast.27, bf16[256,512]{1,0:T(8,128)(2,1)S(1)} %bitcast.23, ...), custom_call_target="tpu_custom_call" | custom-call | flops 33554432 | bytes 2097152 | tf_op jit(solution)/shard_map/rows/pallas_call | solution.py:283
  45.8 1.6 %collective-permute-done.13 = bf16[256,256]{1,0:T(8,128)(2,1)S(1)} collective-permute-done((bf16[256,256]{1,0:T(8,128)(2,1)S(1)}, bf16[256,256]{1,0:T(8,128)(2,1)S(1)}, u32[]{:S(2)}, u32[]{:S(2)}) %collective-permute-start.13) | collective-permute-done | bytes 131104 | tf_op jit(solution)/shard_map/ppermute | solution.py:37
  48.3 1.7 %collective-permute-done.9 = bf16[256,256]{1,0:T(8,128)(2,1)S(1)} collective-permute-done((bf16[256,256]{1,0:T(8,128)(2,1)S(1)}, bf16[256,256]{1,0:T(8,128)(2,1)S(1)}, u32[]{:S(2)}, u32[]{:S(2)}) %collective-permute-start.9) | collective-permute-done | bytes 131104 | tf_op jit(solution)/shard_map/ppermute | solution.py:37
  50.9 3.3 %collective-permute-done.14 = bf16[128,256]{1,0:T(8,128)(2,1)S(1)} collective-permute-done((bf16[128,256]{1,0:T(8,128)(2,1)S(1)}, bf16[128,256]{1,0:T(8,128)(2,1)S(1)}, u32[]{:S(2)}, u32[]{:S(2)}) %collective-permute-start.14) | collective-permute-done | bytes 65568 | tf_op jit(solution)/shard_map/ppermute | solution.py:37
  54.2 1.7 %collective-permute-done.10 = bf16[128,256]{1,0:T(8,128)(2,1)S(1)} collective-permute-done((bf16[128,256]{1,0:T(8,128)(2,1)S(1)}, bf16[128,256]{1,0:T(8,128)(2,1)S(1)}, u32[]{:S(2)}, u32[]{:S(2)}) %collective-permute-start.10) | collective-permute-done | bytes 65568 | tf_op jit(solution)/shard_map/ppermute | solution.py:37
  56.2 2.8 %collective-permute-start.11 = (bf16[128,256]{1,0:T(8,128)(2,1)S(1)}, bf16[128,256]{1,0:T(8,128)(2,1)S(1)}, u32[]{:S(2)}, u32[]{:S(2)}) collective-permute-start(bf16[128,256]{1,0:T(8,128)(2,1)S(1)} %get-tuple-element.64), channel_id=1, source_target_pairs={{0,2},{1,3},{2,0},{3,1},{4,6},{5,7},{6,4},{7,5},{8,10},{9,11},{10,... | collective-permute-start | bytes 196616 | tf_op jit(solution)/shard_map/ppermute | solution.py:37
  59.0 2.2 %collective-permute-done.18 = bf16[128,256]{1,0:T(8,128)(2,1)S(1)} collective-permute-done((bf16[128,256]{1,0:T(8,128)(2,1)S(1)}, bf16[128,256]{1,0:T(8,128)(2,1)S(1)}, u32[]{:S(2)}, u32[]{:S(2)}) %collective-permute-start.18) | collective-permute-done | bytes 65568 | tf_op jit(solution)/shard_map/ppermute | solution.py:37
  61.2 2.2 %collective-permute-start.19 = (bf16[256,256]{1,0:T(8,128)(2,1)S(1)}, bf16[256,256]{1,0:T(8,128)(2,1)S(1)}, u32[]{:S(2)}, u32[]{:S(2)}) collective-permute-start(bf16[256,256]{1,0:T(8,128)(2,1)S(1)} %pad_maximum_fusion.4), channel_id=1, source_target_pairs={{0,1},{1,0},{2,3},{3,2},{4,5},{5,4},{6,7},{7,6},{8,9},{9,8},{10,11... | collective-permute-start | bytes 393224 | tf_op jit(solution)/shard_map/ppermute | solution.py:37
  64.5 2.8 %collective-permute-done.19 = bf16[256,256]{1,0:T(8,128)(2,1)S(1)} collective-permute-done((bf16[256,256]{1,0:T(8,128)(2,1)S(1)}, bf16[256,256]{1,0:T(8,128)(2,1)S(1)}, u32[]{:S(2)}, u32[]{:S(2)}) %collective-permute-start.19) | collective-permute-done | bytes 131104 | tf_op jit(solution)/shard_map/ppermute | solution.py:37
  69.4 2.1 %gradient.3 = (f32[512,256]{1,0:T(8,128)S(1)}, bf16[512,256]{1,0:T(8,128)(2,1)}) custom-call(s32[4]{0:T(128)S(1)} %pad_add_fusion.at, bf16[512,1024]{1,0:T(8,128)(2,1)S(1)} %copy-done, bf16[512,1024]{1,0:T(8,128)(2,1)S(1)} %collective-permute-done.1.got_ref, bf16[512,256]{1,0:T(8,128)(2,1)S(1)} %pad_maximum_fusion.1.slope_ref, ...), custom_call_target="tpu_custom_call" | custom-call | flops 536870912 | bytes 4194304 | tf_op jit(solution)/shard_map/gradient/pallas_call | solution.py:332
  71.5 3.2 %collective-permute-start.21 = (bf16[512,256]{1,0:T(8,128)(2,1)}, bf16[512,256]{1,0:T(8,128)(2,1)}, u32[]{:S(2)}, u32[]{:S(2)}) collective-permute-start(bf16[512,256]{1,0:T(8,128)(2,1)} %get-tuple-element.54), channel_id=1, source_target_pairs={{0,8},{4,20},{8,0},{12,28},{16,24},{20,4},{24,16},{28,12},{1,9},{5... | collective-permute-start | bytes 786440 | tf_op jit(solution)/shard_map/ppermute | solution.py:369
  74.7 1.4 %gradient.2 = (f32[512,256]{1,0:T(8,128)S(1)}, bf16[512,256]{1,0:T(8,128)(2,1)S(1)}) custom-call(s32[4]{0:T(128)S(1)} %pad_add_fusion.at, bf16[512,1024]{1,0:T(8,128)(2,1)S(1)} %copy-done, bf16[512,1024]{1,0:T(8,128)(2,1)S(1)} %collective-permute-done.1.got_ref, bf16[512,256]{1,0:T(8,128)(2,1)S(1)} %pad_maximum_fusion.slope_ref, ...), custom_call_target="tpu_custom_call" | custom-call | flops 536870912 | bytes 4194304 | tf_op jit(solution)/shard_map/gradient/pallas_call | solution.py:332
  76.2 5.1 %all-to-all-start.1 = ((bf16[8,32,512]{2,1,0:T(8,128)(2,1)}), bf16[8,32,512]{2,1,0:T(8,128)(2,1)S(1)}, u32[]{:S(2)}, u32[]{:S(2)}) async-start(bf16[8,32,512]{2,1,0:T(8,128)(2,1)} %bitcast.28), calls=%async_computation.1 | async-start | bytes 524288 | tf_op jit(solution)/shard_map/all_to_all | solution.py:327
  82.6 2.0 %collective-permute-start.17 = (bf16[256,256]{1,0:T(8,128)(2,1)S(1)}, bf16[256,256]{1,0:T(8,128)(2,1)S(1)}, u32[]{:S(2)}, u32[]{:S(2)}) collective-permute-start(bf16[256,256]{1,0:T(8,128)(2,1)S(1)} %slice.132), channel_id=1, source_target_pairs={{0,16},{4,12},{8,24},{12,4},{16,0},{20,28},{24,8},{28,20},{1,17},{... | collective-permute-start | bytes 393224 | tf_op jit(solution)/shard_map/ppermute | solution.py:369
  84.6 3.3 %collective-permute-done.22 = bf16[256,256]{1,0:T(8,128)(2,1)S(1)} collective-permute-done((bf16[256,256]{1,0:T(8,128)(2,1)S(1)}, bf16[256,256]{1,0:T(8,128)(2,1)S(1)}, u32[]{:S(2)}, u32[]{:S(2)}) %collective-permute-start.22) | collective-permute-done | bytes 131104 | tf_op jit(solution)/shard_map/ppermute | solution.py:369
  88.0 1.4 %collective-permute-done.17 = bf16[256,256]{1,0:T(8,128)(2,1)S(1)} collective-permute-done((bf16[256,256]{1,0:T(8,128)(2,1)S(1)}, bf16[256,256]{1,0:T(8,128)(2,1)S(1)}, u32[]{:S(2)}, u32[]{:S(2)}) %collective-permute-start.17) | collective-permute-done | bytes 131104 | tf_op jit(solution)/shard_map/ppermute | solution.py:369
  89.4 3.3 %collective-permute-start.23 = (bf16[256,512]{1,0:T(8,128)(2,1)S(1)}, bf16[256,512]{1,0:T(8,128)(2,1)S(1)}, u32[]{:S(2)}, u32[]{:S(2)}) collective-permute-start(bf16[256,512]{1,0:T(8,128)(2,1)S(1)} %pad_maximum_fusion.2), channel_id=1, source_target_pairs={{0,0},{1,10},{2,17},{3,27},{4,4},{5,14},{6,21},{7,31},{8,1},{9,11}... | collective-permute-start | bytes 786440 | tf_op jit(solution)/shard_map/ppermute | solution.py:381
  92.7 1.7 %write.1 = bf16[256,512]{1,0:T(8,128)(2,1)} custom-call(bf16[256,512]{1,0:T(8,128)(2,1)} %bitcast.29), custom_call_target="tpu_custom_call" | custom-call | bytes 524288 | tf_op jit(solution)/shard_map/write/pallas_call | solution.py:382
  94.4 8.0 %collective-permute-done.23 = bf16[256,512]{1,0:T(8,128)(2,1)S(1)} collective-permute-done((bf16[256,512]{1,0:T(8,128)(2,1)S(1)}, bf16[256,512]{1,0:T(8,128)(2,1)S(1)}, u32[]{:S(2)}, u32[]{:S(2)}) %collective-permute-start.23) | collective-permute-done | bytes 262176 | tf_op jit(solution)/shard_map/ppermute | solution.py:381
  (73 shorter events, 11.2 us)
Async XLA Ops:
  0.6 8.9 %collective-permute-start = (bf16[1024,512]{1,0:T(8,128)(2,1)}, bf16[1024,512]{1,0:T(8,128)(2,1)S(1)}, u32[]{:S(2)}, u32[]{:S(2)}) collective-permute-start(bf16[1024,512]{1,0:T(8,128)(2,1)} %param.14), channel_id=1, source_target_pairs={{0,8},{9,1},{18,26},{27,19},{4,20},{13,29},{22,6},{31,15}} | collective-permute-start | bytes 3145736 | tf_op jit(solution)/shard_map/ppermute | solution.py:190
  2.0 8.6 %copy-start.6 = (bf16[1024,512]{1,0:T(8,128)(2,1)S(1)}, bf16[1024,512]{1,0:T(8,128)(2,1)}, u32[]{:S(2)}) copy-start(bf16[1024,512]{1,0:T(8,128)(2,1)} %param.14) | copy-start | bytes 3145732
  9.1 23.3 %copy-start.9 = (bf16[144,512]{1,0:T(8,128)(2,1)S(1)}, bf16[144,512]{1,0:T(8,128)(2,1)}, u32[]{:S(2)}) copy-start(bf16[144,512]{1,0:T(8,128)(2,1)} %get-tuple-element.43) | copy-start | bytes 442372
  9.1 23.2 %collective-permute-start.1 = (bf16[512,1024]{1,0:T(8,128)(2,1)}, bf16[512,1024]{1,0:T(8,128)(2,1)S(1)}, u32[]{:S(2)}, u32[]{:S(2)}) collective-permute-start(bf16[512,1024]{1,0:T(8,128)(2,1)} %get-tuple-element.32), channel_id=1, source_target_pairs={{0,4},{4,0},{8,12},{12,8},{16,20},{20,16},{24,28},{28,24},{1,5},{5... | collective-permute-start | bytes 3145736 | tf_op jit(solution)/shard_map/ppermute | solution.py:29
  12.7 20.5 %collective-permute-start.2 = (bf16[1024,256]{1,0:T(8,128)(2,1)}, bf16[1024,256]{1,0:T(8,128)(2,1)}, u32[]{:S(2)}, u32[]{:S(2)}) collective-permute-start(bf16[1024,256]{1,0:T(8,128)(2,1)} %get-tuple-element.59), channel_id=1, source_target_pairs={{0,16},{9,25},{18,2},{27,11},{8,24},{1,17},{26,10},{19,3},{4,12},{... | collective-permute-start | bytes 1572872 | tf_op jit(solution)/shard_map/ppermute | solution.py:190
  13.9 23.8 %collective-permute-start.4 = (bf16[1024,256]{1,0:T(8,128)(2,1)S(1)}, bf16[1024,256]{1,0:T(8,128)(2,1)}, u32[]{:S(2)}, u32[]{:S(2)}) collective-permute-start(bf16[1024,256]{1,0:T(8,128)(2,1)S(1)} %get-tuple-element.58), channel_id=1, source_target_pairs={{0,16},{9,25},{18,2},{27,11},{8,24},{1,17},{26,10},{19,3},{4,12},{... | collective-permute-start | bytes 1572872 | tf_op jit(solution)/shard_map/ppermute | solution.py:190
  15.2 29.4 %collective-permute-start.5 = (bf16[144,512]{1,0:T(8,128)(2,1)}, bf16[144,512]{1,0:T(8,128)(2,1)S(1)}, u32[]{:S(2)}, u32[]{:S(2)}) collective-permute-start(bf16[144,512]{1,0:T(8,128)(2,1)} %get-tuple-element.41), channel_id=1, source_target_pairs={{0,1},{1,0},{2,3},{3,2},{4,5},{5,4},{6,7},{7,6},{8,9},{9,8},{10,11... | collective-permute-start | bytes 442376 | tf_op jit(solution)/shard_map/ppermute | solution.py:37
  16.5 28.2 %collective-permute-start.6 = (bf16[144,512]{1,0:T(8,128)(2,1)}, bf16[144,512]{1,0:T(8,128)(2,1)S(1)}, u32[]{:S(2)}, u32[]{:S(2)}) collective-permute-start(bf16[144,512]{1,0:T(8,128)(2,1)} %get-tuple-element.42), channel_id=1, source_target_pairs={{0,2},{1,3},{2,0},{3,1},{4,6},{5,7},{6,4},{7,5},{8,10},{9,11},{10,... | collective-permute-start | bytes 442376 | tf_op jit(solution)/shard_map/ppermute | solution.py:37
  29.0 8.8 %all-to-all-start = ((bf16[8,32,512]{2,1,0:T(8,128)(2,1)}), bf16[8,32,512]{2,1,0:T(8,128)(2,1)S(1)}, u32[]{:S(2)}, u32[]{:S(2)}) async-start(bf16[8,32,512]{2,1,0:T(8,128)(2,1)} %bitcast.13), calls=%async_computation | async-start | bytes 524288 | tf_op jit(solution)/shard_map/all_to_all | solution.py:258
  32.3 7.0 %copy-start = (bf16[512,1024]{1,0:T(8,128)(2,1)S(1)}, bf16[512,1024]{1,0:T(8,128)(2,1)}, u32[]{:S(2)}) copy-start(bf16[512,1024]{1,0:T(8,128)(2,1)} %get-tuple-element.31.kept_ref) | copy-start | bytes 3145732
  32.4 12.3 %collective-permute-start.7 = (bf16[144,512]{1,0:T(8,128)(2,1)S(1)}, bf16[144,512]{1,0:T(8,128)(2,1)S(1)}, u32[]{:S(2)}, u32[]{:S(2)}) collective-permute-start(bf16[144,512]{1,0:T(8,128)(2,1)S(1)} %copy-done.9), channel_id=1, source_target_pairs={{0,3},{1,2},{2,1},{3,0},{4,7},{5,6},{6,5},{7,4},{8,11},{9,10},{10,... | collective-permute-start | bytes 442376 | tf_op jit(solution)/shard_map/ppermute | solution.py:37
  35.3 4.0 %collective-permute-start.3 = (bf16[512,256]{1,0:T(8,128)(2,1)}, bf16[512,256]{1,0:T(8,128)(2,1)}, u32[]{:S(2)}, u32[]{:S(2)}) collective-permute-start(bf16[512,256]{1,0:T(8,128)(2,1)} %convolution_convert_fusion.2), channel_id=1, source_target_pairs={{0,4},{4,0},{8,12},{12,8},{16,20},{20,16},{24,28},{28,24},{1,5},{5... | collective-permute-start | bytes 786440 | tf_op jit(solution)/shard_map/ppermute | solution.py:29
  39.2 3.8 %collective-permute-start.8 = (bf16[512,256]{1,0:T(8,128)(2,1)S(1)}, bf16[512,256]{1,0:T(8,128)(2,1)S(1)}, u32[]{:S(2)}, u32[]{:S(2)}) collective-permute-start(bf16[512,256]{1,0:T(8,128)(2,1)S(1)} %convolution_convert_fusion.1), channel_id=1, source_target_pairs={{0,4},{4,0},{8,12},{12,8},{16,20},{20,16},{24,28},{28,24},{1,5},{5... | collective-permute-start | bytes 786440 | tf_op jit(solution)/shard_map/ppermute | solution.py:29
  40.9 3.8 %copy-start.1 = (bf16[144,512]{1,0:T(8,128)(2,1)S(1)}, bf16[144,512]{1,0:T(8,128)(2,1)}, u32[]{:S(2)}) copy-start(bf16[144,512]{1,0:T(8,128)(2,1)} %get-tuple-element.40.refs_0_) | copy-start | bytes 442372
  40.9 3.8 %copy-start.2 = (s32[1,1,8]{2,1,0:T(1,128)S(1)}, s32[1,1,8]{2,1,0:T(1,128)}, u32[]{:S(2)}) copy-start(s32[1,1,8]{2,1,0:T(1,128)} %param.15) | copy-start | bytes 100
  40.9 3.8 %copy-start.3 = (s32[1,1,8]{2,1,0:T(1,128)S(1)}, s32[1,1,8]{2,1,0:T(1,128)}, u32[]{:S(2)}) copy-start(s32[1,1,8]{2,1,0:T(1,128)} %param.16) | copy-start | bytes 100
  41.0 6.4 %collective-permute-start.13 = (bf16[256,256]{1,0:T(8,128)(2,1)S(1)}, bf16[256,256]{1,0:T(8,128)(2,1)S(1)}, u32[]{:S(2)}, u32[]{:S(2)}) collective-permute-start(bf16[256,256]{1,0:T(8,128)(2,1)S(1)} %slice.133), channel_id=1, source_target_pairs={{0,1},{1,0},{2,3},{3,2},{4,5},{5,4},{6,7},{7,6},{8,9},{9,8},{10,11... | collective-permute-start | bytes 393224 | tf_op jit(solution)/shard_map/ppermute | solution.py:37
  44.6 5.4 %collective-permute-start.9 = (bf16[256,256]{1,0:T(8,128)(2,1)S(1)}, bf16[256,256]{1,0:T(8,128)(2,1)S(1)}, u32[]{:S(2)}, u32[]{:S(2)}) collective-permute-start(bf16[256,256]{1,0:T(8,128)(2,1)S(1)} %slice.134), channel_id=1, source_target_pairs={{0,1},{1,0},{2,3},{3,2},{4,5},{5,4},{6,7},{7,6},{8,9},{9,8},{10,11... | collective-permute-start | bytes 393224 | tf_op jit(solution)/shard_map/ppermute | solution.py:37
  47.5 6.7 %collective-permute-start.14 = (bf16[128,256]{1,0:T(8,128)(2,1)S(1)}, bf16[128,256]{1,0:T(8,128)(2,1)S(1)}, u32[]{:S(2)}, u32[]{:S(2)}) collective-permute-start(bf16[128,256]{1,0:T(8,128)(2,1)S(1)} %slice.135), channel_id=1, source_target_pairs={{0,2},{1,3},{2,0},{3,1},{4,6},{5,7},{6,4},{7,5},{8,10},{9,11},{10,... | collective-permute-start | bytes 196616 | tf_op jit(solution)/shard_map/ppermute | solution.py:37
  50.1 5.8 %collective-permute-start.10 = (bf16[128,256]{1,0:T(8,128)(2,1)S(1)}, bf16[128,256]{1,0:T(8,128)(2,1)S(1)}, u32[]{:S(2)}, u32[]{:S(2)}) collective-permute-start(bf16[128,256]{1,0:T(8,128)(2,1)S(1)} %slice.136), channel_id=1, source_target_pairs={{0,2},{1,3},{2,0},{3,1},{4,6},{5,7},{6,4},{7,5},{8,10},{9,11},{10,... | collective-permute-start | bytes 196616 | tf_op jit(solution)/shard_map/ppermute | solution.py:37
  56.0 5.2 %collective-permute-start.18 = (bf16[128,256]{1,0:T(8,128)(2,1)S(1)}, bf16[128,256]{1,0:T(8,128)(2,1)S(1)}, u32[]{:S(2)}, u32[]{:S(2)}) collective-permute-start(bf16[128,256]{1,0:T(8,128)(2,1)S(1)} %get-tuple-element.63), channel_id=1, source_target_pairs={{0,2},{1,3},{2,0},{3,1},{4,6},{5,7},{6,4},{7,5},{8,10},{9,11},{10,... | collective-permute-start | bytes 196616 | tf_op jit(solution)/shard_map/ppermute | solution.py:37
  56.2 8.0 %collective-permute-start.11 = (bf16[128,256]{1,0:T(8,128)(2,1)S(1)}, bf16[128,256]{1,0:T(8,128)(2,1)S(1)}, u32[]{:S(2)}, u32[]{:S(2)}) collective-permute-start(bf16[128,256]{1,0:T(8,128)(2,1)S(1)} %get-tuple-element.64), channel_id=1, source_target_pairs={{0,2},{1,3},{2,0},{3,1},{4,6},{5,7},{6,4},{7,5},{8,10},{9,11},{10,... | collective-permute-start | bytes 196616 | tf_op jit(solution)/shard_map/ppermute | solution.py:37
  61.2 6.0 %collective-permute-start.19 = (bf16[256,256]{1,0:T(8,128)(2,1)S(1)}, bf16[256,256]{1,0:T(8,128)(2,1)S(1)}, u32[]{:S(2)}, u32[]{:S(2)}) collective-permute-start(bf16[256,256]{1,0:T(8,128)(2,1)S(1)} %pad_maximum_fusion.4), channel_id=1, source_target_pairs={{0,1},{1,0},{2,3},{3,2},{4,5},{5,4},{6,7},{7,6},{8,9},{9,8},{10,11... | collective-permute-start | bytes 393224 | tf_op jit(solution)/shard_map/ppermute | solution.py:37
  64.2 5.0 %collective-permute-start.12 = (bf16[256,256]{1,0:T(8,128)(2,1)S(1)}, bf16[256,256]{1,0:T(8,128)(2,1)S(1)}, u32[]{:S(2)}, u32[]{:S(2)}) collective-permute-start(bf16[256,256]{1,0:T(8,128)(2,1)S(1)} %pad_maximum_fusion.3), channel_id=1, source_target_pairs={{0,1},{1,0},{2,3},{3,2},{4,5},{5,4},{6,7},{7,6},{8,9},{9,8},{10,11... | collective-permute-start | bytes 393224 | tf_op jit(solution)/shard_map/ppermute | solution.py:37
  67.3 2.1 %collective-permute-start.20 = (bf16[512,256]{1,0:T(8,128)(2,1)S(1)}, bf16[512,256]{1,0:T(8,128)(2,1)S(1)}, u32[]{:S(2)}, u32[]{:S(2)}) collective-permute-start(bf16[512,256]{1,0:T(8,128)(2,1)S(1)} %pad_maximum_fusion.1.slope_ref), channel_id=1, source_target_pairs={{0,4},{4,0},{8,12},{12,8},{16,20},{20,16},{24,28},{28,24},{1,5},{5... | collective-permute-start | bytes 786440 | tf_op jit(solution)/shard_map/ppermute | solution.py:29
  69.2 5.5 %collective-permute-start.15 = (bf16[512,256]{1,0:T(8,128)(2,1)S(1)}, bf16[512,256]{1,0:T(8,128)(2,1)S(1)}, u32[]{:S(2)}, u32[]{:S(2)}) collective-permute-start(bf16[512,256]{1,0:T(8,128)(2,1)S(1)} %pad_maximum_fusion.slope_ref), channel_id=1, source_target_pairs={{0,4},{4,0},{8,12},{12,8},{16,20},{20,16},{24,28},{28,24},{1,5},{5... | collective-permute-start | bytes 786440 | tf_op jit(solution)/shard_map/ppermute | solution.py:29
  71.5 9.9 %collective-permute-start.21 = (bf16[512,256]{1,0:T(8,128)(2,1)}, bf16[512,256]{1,0:T(8,128)(2,1)}, u32[]{:S(2)}, u32[]{:S(2)}) collective-permute-start(bf16[512,256]{1,0:T(8,128)(2,1)} %get-tuple-element.54), channel_id=1, source_target_pairs={{0,8},{4,20},{8,0},{12,28},{16,24},{20,4},{24,16},{28,12},{1,9},{5... | collective-permute-start | bytes 786440 | tf_op jit(solution)/shard_map/ppermute | solution.py:369
  76.1 6.4 %collective-permute-start.16 = (bf16[512,256]{1,0:T(8,128)(2,1)S(1)}, bf16[512,256]{1,0:T(8,128)(2,1)S(1)}, u32[]{:S(2)}, u32[]{:S(2)}) collective-permute-start(bf16[512,256]{1,0:T(8,128)(2,1)S(1)} %get-tuple-element.52), channel_id=1, source_target_pairs={{0,8},{4,20},{8,0},{12,28},{16,24},{20,4},{24,16},{28,12},{1,9},{5... | collective-permute-start | bytes 786440 | tf_op jit(solution)/shard_map/ppermute | solution.py:369
  76.2 13.2 %all-to-all-start.1 = ((bf16[8,32,512]{2,1,0:T(8,128)(2,1)}), bf16[8,32,512]{2,1,0:T(8,128)(2,1)S(1)}, u32[]{:S(2)}, u32[]{:S(2)}) async-start(bf16[8,32,512]{2,1,0:T(8,128)(2,1)} %bitcast.28), calls=%async_computation.1 | async-start | bytes 524288 | tf_op jit(solution)/shard_map/all_to_all | solution.py:327
  82.4 5.5 %collective-permute-start.22 = (bf16[256,256]{1,0:T(8,128)(2,1)S(1)}, bf16[256,256]{1,0:T(8,128)(2,1)S(1)}, u32[]{:S(2)}, u32[]{:S(2)}) collective-permute-start(bf16[256,256]{1,0:T(8,128)(2,1)S(1)} %slice.131), channel_id=1, source_target_pairs={{0,16},{4,12},{8,24},{12,4},{16,0},{20,28},{24,8},{28,20},{1,17},{... | collective-permute-start | bytes 393224 | tf_op jit(solution)/shard_map/ppermute | solution.py:369
  82.6 6.7 %collective-permute-start.17 = (bf16[256,256]{1,0:T(8,128)(2,1)S(1)}, bf16[256,256]{1,0:T(8,128)(2,1)S(1)}, u32[]{:S(2)}, u32[]{:S(2)}) collective-permute-start(bf16[256,256]{1,0:T(8,128)(2,1)S(1)} %slice.132), channel_id=1, source_target_pairs={{0,16},{4,12},{8,24},{12,4},{16,0},{20,28},{24,8},{28,20},{1,17},{... | collective-permute-start | bytes 393224 | tf_op jit(solution)/shard_map/ppermute | solution.py:369
  89.4 12.9 %collective-permute-start.23 = (bf16[256,512]{1,0:T(8,128)(2,1)S(1)}, bf16[256,512]{1,0:T(8,128)(2,1)S(1)}, u32[]{:S(2)}, u32[]{:S(2)}) collective-permute-start(bf16[256,512]{1,0:T(8,128)(2,1)S(1)} %pad_maximum_fusion.2), channel_id=1, source_target_pairs={{0,0},{1,10},{2,17},{3,27},{4,4},{5,14},{6,21},{7,31},{8,1},{9,11}... | collective-permute-start | bytes 786440 | tf_op jit(solution)/shard_map/ppermute | solution.py:381
  (4 other events, 11.9 us)

commit v17 on v16

--- a/solution.py
+++ b/solution.py
@@ -245,11 +245,12 @@
     got_rows = swapped(given_rows, dp_count)
 
     cot = cotangent.reshape(slot_count, value_width)
-    got, cot, kept_rows = lax.optimization_barrier((got, cot, kept_rows))
+    held = jnp.where(is_getter, got, pol_weight)
+    held, cot, kept_rows = lax.optimization_barrier((held, cot, kept_rows))
     parts = []
     for j in range(PARTS):
         cols = slice(j * width, (j + 1) * width)
-        held_part = jnp.where(is_getter, got[:, cols], pol_weight[:, cols])
+        held_part = held[:, cols]
         for number in range(1, levels):
             got_part, is_getter_part = stage(number, held_part)
             if number < levels - 1:

time: 104 us -> 103 us (level)
  starting transfers between devices: 45 us -> 48.6 us
  waiting for transfers between devices: 29.9 us -> 27.6 us
  other arithmetic: 4.96 us -> 2.97 us
    ppermute x11, starting transfers between devices: 23.8 us -> 26.3 us  [crossed(): return lax.ppermute(array, 'tensor', [(i, i ^ step) for i in range(count)])]
    ppermute x11, waiting for transfers between devices: 14.8 us -> 12.6 us  [crossed(): return lax.ppermute(array, 'tensor', [(i, i ^ step) for i in range(count)])]
    select_n x1, other arithmetic: 2.1 us -> 0.12 us  [on_device(): held = jnp.where(is_getter, got, pol_weight)]
where the time goes in v17:
time: 103 us
  starting transfers between devices  48.6 us (47%)
  waiting for transfers between devices  27.6 us (27%)
  Pallas kernels  13.4 us (13%)
  matrix products  7.93 us (8%)
  other arithmetic  2.97 us (3%)
  local copies, waits for them, and re-layouts  1.1 us (1%)
  between operations  1.08 us (1%)
    ppermute x11, starting transfers between devices, crossed(): return lax.ppermute(array, 'tensor', [(i, i ^ step) for i in range(count)])  26.3 us
    ppermute x11, waiting for transfers between devices, crossed(): return lax.ppermute(array, 'tensor', [(i, i ^ step) for i in range(count)])  12.6 us
    ppermute x1, waiting for transfers between devices, on_device(): grad_weight = lax.ppermute(grad, AXES, pairs).astype(F32)  8 us
    pallas_call x1, Pallas kernels, on_device(): pl.pallas_call(functools.partial(prepare_kernel, tensor_count, steps), gr...  7.14 us
    dot_general x4, matrix products, dot(): return jnp.dot(a, b, preferred_element_type=F32)  6.98 us
    ppermute x4, starting transfers between devices, on_device(): total = total + lax.ppermute(given, 'dp', pairs).astype(F32)  5.72 us
    all_to_all x1, starting transfers between devices, on_device(): lax.all_to_all(sent, 'dp', split_axis=0, concat_axis=0, tiled=True)  5.36 us
    ppermute x4, waiting for transfers between devices, on_device(): total = total + lax.ppermute(given, 'dp', pairs).astype(F32)  4.69 us
  transfers between devices with their start and end apart: 26, of which 12 were waited for; matrix products, arithmetic and copies ran while one was open for 11% of the time, Pallas kernels for 13%

profile of v17, /device:TPU:4, one launch (start us, length us, event | category | flops | bytes accessed | tf_op | source)
XLA Modules:
  0.0 102.7 jit_solution(16922351996162541628)
XLA Ops:
  0.6 1.6 %collective-permute-start = (bf16[1024,512]{1,0:T(8,128)(2,1)}, bf16[1024,512]{1,0:T(8,128)(2,1)}, u32[]{:S(2)}, u32[]{:S(2)}) collective-permute-start(bf16[1024,512]{1,0:T(8,128)(2,1)} %param.14), channel_id=1, source_target_pairs={{0,8},{9,1},{18,26},{27,19},{4,20},{13,29},{22,6},{31,15}} | collective-permute-start | bytes 3145736 | tf_op jit(solution)/shard_map/ppermute | solution.py:190
  2.9 7.1 %prepare.1 = (bf16[512,1024]{1,0:T(8,128)(2,1)}, bf16[512,1024]{1,0:T(8,128)(2,1)}, bf16[144,512]{1,0:T(8,128)(2,1)}, bf16[144,512]{1,0:T(8,128)(2,1)}, bf16[144...) custom-call(s32[2]{0:T(128)} %pad_add_fusion.1.at, bf16[512,2048]{1,0:T(8,128)(2,1)} %x_ref.1, f32[1,2048]{1,0:T(1,128)} %bitcast.32, ...), custom_call_target="tpu_custom_call" | custom-call | flops 1073741824 | bytes 8388608 | tf_op jit(solution)/shard_map/prepare/pallas_call | solution.py:202
  12.4 1.3 %collective-permute-start.4 = (bf16[1024,256]{1,0:T(8,128)(2,1)S(1)}, bf16[1024,256]{1,0:T(8,128)(2,1)}, u32[]{:S(2)}, u32[]{:S(2)}) collective-permute-start(bf16[1024,256]{1,0:T(8,128)(2,1)S(1)} %get-tuple-element.58), channel_id=1, source_target_pairs={{0,16},{9,25},{18,2},{27,11},{8,24},{1,17},{26,10},{19,3},{4,12},{... | collective-permute-start | bytes 1572872 | tf_op jit(solution)/shard_map/ppermute | solution.py:190
  13.7 1.7 %collective-permute-start.5 = (bf16[144,512]{1,0:T(8,128)(2,1)}, bf16[144,512]{1,0:T(8,128)(2,1)S(1)}, u32[]{:S(2)}, u32[]{:S(2)}) collective-permute-start(bf16[144,512]{1,0:T(8,128)(2,1)} %get-tuple-element.41), channel_id=1, source_target_pairs={{0,1},{1,0},{2,3},{3,2},{4,5},{5,4},{6,7},{7,6},{8,9},{9,8},{10,11... | collective-permute-start | bytes 442376 | tf_op jit(solution)/shard_map/ppermute | solution.py:37
  15.4 12.8 %collective-permute-start.6 = (bf16[144,512]{1,0:T(8,128)(2,1)}, bf16[144,512]{1,0:T(8,128)(2,1)S(1)}, u32[]{:S(2)}, u32[]{:S(2)}) collective-permute-start(bf16[144,512]{1,0:T(8,128)(2,1)} %get-tuple-element.42), channel_id=1, source_target_pairs={{0,2},{1,3},{2,0},{3,1},{4,6},{5,7},{6,4},{7,5},{8,10},{9,11},{10,... | collective-permute-start | bytes 442376 | tf_op jit(solution)/shard_map/ppermute | solution.py:37
  28.2 3.4 %all-to-all-start = ((bf16[8,32,512]{2,1,0:T(8,128)(2,1)}), bf16[8,32,512]{2,1,0:T(8,128)(2,1)S(1)}, u32[]{:S(2)}, u32[]{:S(2)}) async-start(bf16[8,32,512]{2,1,0:T(8,128)(2,1)} %bitcast.13), calls=%async_computation | async-start | bytes 524288 | tf_op jit(solution)/shard_map/all_to_all | solution.py:259
  32.4 2.2 %convolution_convert_fusion.2 = bf16[512,256]{1,0:T(8,128)(2,1)} fusion(bf16[512,1024]{1,0:T(8,128)(2,1)S(1)} %collective-permute-done.1.got_ref, bf16[1024,256]{1,0:T(8,128)(2,1)} %collective-permute-done.2, pred[]{:T(512)S(6)} %or.18, bf16[1024,512]{1,0:T(8,128)(2,1)S(1)} %broadcast_select_fusion), kind=kOutput, calls=%fused_computation.4 | convolution fusion | flops 268828672 | bytes 2359297 | tf_op jit(solution)/shard_map/dot_general | solution.py:21
  34.6 2.4 %all-to-all-done = bf16[8,32,512]{2,1,0:T(8,128)(2,1)S(1)} async-done(((bf16[8,32,512]{2,1,0:T(8,128)(2,1)}), bf16[8,32,512]{2,1,0:T(8,128)(2,1)S(1)}, u32[]{:S(2)}, u32[]{:S(2)}) %all-to-all-start) | async-done | bytes 262176 | tf_op jit(solution)/shard_map/all_to_all | solution.py:259
  37.0 1.7 %convolution_convert_fusion.1 = bf16[512,256]{1,0:T(8,128)(2,1)S(1)} fusion(bf16[512,1024]{1,0:T(8,128)(2,1)S(1)} %collective-permute-done.1.got_ref, bf16[1024,256]{1,0:T(8,128)(2,1)} %collective-permute-done.4, pred[]{:T(512)S(6)} %or.18, bf16[1024,512]{1,0:T(8,128)(2,1)} %copy-done.6), kind=kOutput, calls=%fused_computation.3 | convolution fusion | flops 268828672 | bytes 2359297 | tf_op jit(solution)/shard_map/dot_general | solution.py:21
  38.8 1.6 %convolution_add_fusion.1 = f32[512,256]{1,0:T(8,128)S(1)} fusion(bf16[512,1024]{1,0:T(8,128)(2,1)S(1)} %copy-done, bf16[512,256]{1,0:T(8,128)(2,1)} %collective-permute-done.3, bf16[1024,256]{1,0:T(8,128)(2,1)} %collective-permute-done.2, pred[]{:T(512)S(6)} %or.18, bf16[1024,512]{1,0:T(8,128)(2,1)S(1)} %copy-done.7), kind=kOutput, calls=%fused_computation.1 | convolution fusion | flops 268959744 | bytes 2883585 | tf_op jit(solution)/shard_map/dot_general | solution.py:21
  40.5 2.1 %collective-permute-start.13 = (bf16[256,256]{1,0:T(8,128)(2,1)S(1)}, bf16[256,256]{1,0:T(8,128)(2,1)S(1)}, u32[]{:S(2)}, u32[]{:S(2)}) collective-permute-start(bf16[256,256]{1,0:T(8,128)(2,1)S(1)} %slice.137), channel_id=1, source_target_pairs={{0,1},{1,0},{2,3},{3,2},{4,5},{5,4},{6,7},{7,6},{8,9},{9,8},{10,11... | collective-permute-start | bytes 393224 | tf_op jit(solution)/shard_map/ppermute | solution.py:37
  42.6 1.5 %convolution_add_fusion = f32[512,256]{1,0:T(8,128)S(1)} fusion(bf16[512,1024]{1,0:T(8,128)(2,1)S(1)} %copy-done, bf16[512,256]{1,0:T(8,128)(2,1)S(1)} %collective-permute-done.8, bf16[1024,256]{1,0:T(8,128)(2,1)} %collective-permute-done.4, pred[]{:T(512)S(6)} %or.18, bf16[1024,512]{1,0:T(8,128)(2,1)S(1)} %copy-done.7), kind=kOutput, calls=%fused_computation | convolution fusion | flops 268959744 | bytes 2883585 | tf_op jit(solution)/shard_map/dot_general | solution.py:21
  45.3 1.6 %collective-permute-done.13 = bf16[256,256]{1,0:T(8,128)(2,1)S(1)} collective-permute-done((bf16[256,256]{1,0:T(8,128)(2,1)S(1)}, bf16[256,256]{1,0:T(8,128)(2,1)S(1)}, u32[]{:S(2)}, u32[]{:S(2)}) %collective-permute-start.13) | collective-permute-done | bytes 131104 | tf_op jit(solution)/shard_map/ppermute | solution.py:37
  47.0 1.5 %collective-permute-start.14 = (bf16[128,256]{1,0:T(8,128)(2,1)S(1)}, bf16[128,256]{1,0:T(8,128)(2,1)S(1)}, u32[]{:S(2)}, u32[]{:S(2)}) collective-permute-start(bf16[128,256]{1,0:T(8,128)(2,1)S(1)} %slice.139), channel_id=1, source_target_pairs={{0,2},{1,3},{2,0},{3,1},{4,6},{5,7},{6,4},{7,5},{8,10},{9,11},{10,... | collective-permute-start | bytes 196616 | tf_op jit(solution)/shard_map/ppermute | solution.py:37
  49.6 1.6 %collective-permute-start.10 = (bf16[128,256]{1,0:T(8,128)(2,1)S(1)}, bf16[128,256]{1,0:T(8,128)(2,1)S(1)}, u32[]{:S(2)}, u32[]{:S(2)}) collective-permute-start(bf16[128,256]{1,0:T(8,128)(2,1)S(1)} %slice.140), channel_id=1, source_target_pairs={{0,2},{1,3},{2,0},{3,1},{4,6},{5,7},{6,4},{7,5},{8,10},{9,11},{10,... | collective-permute-start | bytes 196616 | tf_op jit(solution)/shard_map/ppermute | solution.py:37
  51.3 2.4 %collective-permute-done.14 = bf16[128,256]{1,0:T(8,128)(2,1)S(1)} collective-permute-done((bf16[128,256]{1,0:T(8,128)(2,1)S(1)}, bf16[128,256]{1,0:T(8,128)(2,1)S(1)}, u32[]{:S(2)}, u32[]{:S(2)}) %collective-permute-start.14) | collective-permute-done | bytes 65568 | tf_op jit(solution)/shard_map/ppermute | solution.py:37
  53.7 1.7 %collective-permute-done.10 = bf16[128,256]{1,0:T(8,128)(2,1)S(1)} collective-permute-done((bf16[128,256]{1,0:T(8,128)(2,1)S(1)}, bf16[128,256]{1,0:T(8,128)(2,1)S(1)}, u32[]{:S(2)}, u32[]{:S(2)}) %collective-permute-start.10) | collective-permute-done | bytes 65568 | tf_op jit(solution)/shard_map/ppermute | solution.py:37
  56.6 2.0 %collective-permute-start.11 = (bf16[128,256]{1,0:T(8,128)(2,1)S(1)}, bf16[128,256]{1,0:T(8,128)(2,1)S(1)}, u32[]{:S(2)}, u32[]{:S(2)}) collective-permute-start(bf16[128,256]{1,0:T(8,128)(2,1)S(1)} %get-tuple-element.64), channel_id=1, source_target_pairs={{0,2},{1,3},{2,0},{3,1},{4,6},{5,7},{6,4},{7,5},{8,10},{9,11},{10,... | collective-permute-start | bytes 196616 | tf_op jit(solution)/shard_map/ppermute | solution.py:37
  58.5 2.4 %collective-permute-done.18 = bf16[128,256]{1,0:T(8,128)(2,1)S(1)} collective-permute-done((bf16[128,256]{1,0:T(8,128)(2,1)S(1)}, bf16[128,256]{1,0:T(8,128)(2,1)S(1)}, u32[]{:S(2)}, u32[]{:S(2)}) %collective-permute-start.18) | collective-permute-done | bytes 65568 | tf_op jit(solution)/shard_map/ppermute | solution.py:37
  60.9 1.4 %collective-permute-start.19 = (bf16[256,256]{1,0:T(8,128)(2,1)S(1)}, bf16[256,256]{1,0:T(8,128)(2,1)S(1)}, u32[]{:S(2)}, u32[]{:S(2)}) collective-permute-start(bf16[256,256]{1,0:T(8,128)(2,1)S(1)} %pad_maximum_fusion.4), channel_id=1, source_target_pairs={{0,1},{1,0},{2,3},{3,2},{4,5},{5,4},{6,7},{7,6},{8,9},{9,8},{10,11... | collective-permute-start | bytes 393224 | tf_op jit(solution)/shard_map/ppermute | solution.py:37
  63.1 1.3 %collective-permute-start.12 = (bf16[256,256]{1,0:T(8,128)(2,1)S(1)}, bf16[256,256]{1,0:T(8,128)(2,1)S(1)}, u32[]{:S(2)}, u32[]{:S(2)}) collective-permute-start(bf16[256,256]{1,0:T(8,128)(2,1)S(1)} %pad_maximum_fusion.3), channel_id=1, source_target_pairs={{0,1},{1,0},{2,3},{3,2},{4,5},{5,4},{6,7},{7,6},{8,9},{9,8},{10,11... | collective-permute-start | bytes 393224 | tf_op jit(solution)/shard_map/ppermute | solution.py:37
  64.5 2.2 %collective-permute-done.19 = bf16[256,256]{1,0:T(8,128)(2,1)S(1)} collective-permute-done((bf16[256,256]{1,0:T(8,128)(2,1)S(1)}, bf16[256,256]{1,0:T(8,128)(2,1)S(1)}, u32[]{:S(2)}, u32[]{:S(2)}) %collective-permute-start.19) | collective-permute-done | bytes 131104 | tf_op jit(solution)/shard_map/ppermute | solution.py:37
  68.4 2.1 %gradient.3 = (f32[512,256]{1,0:T(8,128)S(1)}, bf16[512,256]{1,0:T(8,128)(2,1)}) custom-call(s32[4]{0:T(128)S(1)} %pad_add_fusion.at, bf16[512,1024]{1,0:T(8,128)(2,1)S(1)} %copy-done, bf16[512,1024]{1,0:T(8,128)(2,1)S(1)} %collective-permute-done.1.got_ref, bf16[512,256]{1,0:T(8,128)(2,1)S(1)} %pad_maximum_fusion.1.slope_ref, ...), custom_call_target="tpu_custom_call" | custom-call | flops 536870912 | bytes 4194304 | tf_op jit(solution)/shard_map/gradient/pallas_call | solution.py:333
  70.5 3.5 %collective-permute-start.21 = (bf16[512,256]{1,0:T(8,128)(2,1)}, bf16[512,256]{1,0:T(8,128)(2,1)}, u32[]{:S(2)}, u32[]{:S(2)}) collective-permute-start(bf16[512,256]{1,0:T(8,128)(2,1)} %get-tuple-element.54), channel_id=1, source_target_pairs={{0,8},{4,20},{8,0},{12,28},{16,24},{20,4},{24,16},{28,12},{1,9},{5... | collective-permute-start | bytes 786440 | tf_op jit(solution)/shard_map/ppermute | solution.py:370
  74.0 1.4 %gradient.2 = (f32[512,256]{1,0:T(8,128)S(1)}, bf16[512,256]{1,0:T(8,128)(2,1)S(1)}) custom-call(s32[4]{0:T(128)S(1)} %pad_add_fusion.at, bf16[512,1024]{1,0:T(8,128)(2,1)S(1)} %copy-done, bf16[512,1024]{1,0:T(8,128)(2,1)S(1)} %collective-permute-done.1.got_ref, bf16[512,256]{1,0:T(8,128)(2,1)S(1)} %pad_maximum_fusion.slope_ref, ...), custom_call_target="tpu_custom_call" | custom-call | flops 536870912 | bytes 4194304 | tf_op jit(solution)/shard_map/gradient/pallas_call | solution.py:333
  75.5 5.4 %all-to-all-start.1 = ((bf16[8,32,512]{2,1,0:T(8,128)(2,1)}), bf16[8,32,512]{2,1,0:T(8,128)(2,1)S(1)}, u32[]{:S(2)}, u32[]{:S(2)}) async-start(bf16[8,32,512]{2,1,0:T(8,128)(2,1)} %bitcast.28), calls=%async_computation.1 | async-start | bytes 524288 | tf_op jit(solution)/shard_map/all_to_all | solution.py:328
  82.1 2.0 %collective-permute-start.17 = (bf16[256,256]{1,0:T(8,128)(2,1)S(1)}, bf16[256,256]{1,0:T(8,128)(2,1)S(1)}, u32[]{:S(2)}, u32[]{:S(2)}) collective-permute-start(bf16[256,256]{1,0:T(8,128)(2,1)S(1)} %slice.136), channel_id=1, source_target_pairs={{0,16},{4,12},{8,24},{12,4},{16,0},{20,28},{24,8},{28,20},{1,17},{... | collective-permute-start | bytes 393224 | tf_op jit(solution)/shard_map/ppermute | solution.py:370
  84.1 3.3 %collective-permute-done.22 = bf16[256,256]{1,0:T(8,128)(2,1)S(1)} collective-permute-done((bf16[256,256]{1,0:T(8,128)(2,1)S(1)}, bf16[256,256]{1,0:T(8,128)(2,1)S(1)}, u32[]{:S(2)}, u32[]{:S(2)}) %collective-permute-start.22) | collective-permute-done | bytes 131104 | tf_op jit(solution)/shard_map/ppermute | solution.py:370
  87.5 1.4 %collective-permute-done.17 = bf16[256,256]{1,0:T(8,128)(2,1)S(1)} collective-permute-done((bf16[256,256]{1,0:T(8,128)(2,1)S(1)}, bf16[256,256]{1,0:T(8,128)(2,1)S(1)}, u32[]{:S(2)}, u32[]{:S(2)}) %collective-permute-start.17) | collective-permute-done | bytes 131104 | tf_op jit(solution)/shard_map/ppermute | solution.py:370
  88.9 3.3 %collective-permute-start.23 = (bf16[256,512]{1,0:T(8,128)(2,1)S(1)}, bf16[256,512]{1,0:T(8,128)(2,1)S(1)}, u32[]{:S(2)}, u32[]{:S(2)}) collective-permute-start(bf16[256,512]{1,0:T(8,128)(2,1)S(1)} %pad_maximum_fusion.2), channel_id=1, source_target_pairs={{0,0},{1,10},{2,17},{3,27},{4,4},{5,14},{6,21},{7,31},{8,1},{9,11}... | collective-permute-start | bytes 786440 | tf_op jit(solution)/shard_map/ppermute | solution.py:382
  92.2 1.7 %write.1 = bf16[256,512]{1,0:T(8,128)(2,1)} custom-call(bf16[256,512]{1,0:T(8,128)(2,1)} %bitcast.29), custom_call_target="tpu_custom_call" | custom-call | bytes 524288 | tf_op jit(solution)/shard_map/write/pallas_call | solution.py:383
  93.9 8.0 %collective-permute-done.23 = bf16[256,512]{1,0:T(8,128)(2,1)S(1)} collective-permute-done((bf16[256,512]{1,0:T(8,128)(2,1)S(1)}, bf16[256,512]{1,0:T(8,128)(2,1)S(1)}, u32[]{:S(2)}, u32[]{:S(2)}) %collective-permute-start.23) | collective-permute-done | bytes 262176 | tf_op jit(solution)/shard_map/ppermute | solution.py:382
  (76 shorter events, 12.2 us)
Async XLA Ops:
  0.6 9.5 %collective-permute-start = (bf16[1024,512]{1,0:T(8,128)(2,1)}, bf16[1024,512]{1,0:T(8,128)(2,1)}, u32[]{:S(2)}, u32[]{:S(2)}) collective-permute-start(bf16[1024,512]{1,0:T(8,128)(2,1)} %param.14), channel_id=1, source_target_pairs={{0,8},{9,1},{18,26},{27,19},{4,20},{13,29},{22,6},{31,15}} | collective-permute-start | bytes 3145736 | tf_op jit(solution)/shard_map/ppermute | solution.py:190
  2.9 7.3 %copy-start.8 = (bf16[1024,512]{1,0:T(8,128)(2,1)S(1)}, bf16[1024,512]{1,0:T(8,128)(2,1)}, u32[]{:S(2)}) copy-start(bf16[1024,512]{1,0:T(8,128)(2,1)} %param.14) | copy-start | bytes 3145732
  10.0 21.6 %collective-permute-start.1 = (bf16[512,1024]{1,0:T(8,128)(2,1)}, bf16[512,1024]{1,0:T(8,128)(2,1)S(1)}, u32[]{:S(2)}, u32[]{:S(2)}) collective-permute-start(bf16[512,1024]{1,0:T(8,128)(2,1)} %get-tuple-element.32), channel_id=1, source_target_pairs={{0,4},{4,0},{8,12},{12,8},{16,20},{20,16},{24,28},{28,24},{1,5},{5... | collective-permute-start | bytes 3145736 | tf_op jit(solution)/shard_map/ppermute | solution.py:29
  10.3 22.1 %copy-start.6 = (bf16[1024,512]{1,0:T(8,128)(2,1)}, bf16[1024,512]{1,0:T(8,128)(2,1)S(1)}, u32[]{:S(2)}) copy-start(bf16[1024,512]{1,0:T(8,128)(2,1)S(1)} %broadcast_select_fusion) | copy-start | bytes 3145732
  10.3 21.3 %copy-start.10 = (bf16[144,512]{1,0:T(8,128)(2,1)S(1)}, bf16[144,512]{1,0:T(8,128)(2,1)}, u32[]{:S(2)}) copy-start(bf16[144,512]{1,0:T(8,128)(2,1)} %get-tuple-element.43) | copy-start | bytes 442372
  11.2 21.2 %collective-permute-start.2 = (bf16[1024,256]{1,0:T(8,128)(2,1)}, bf16[1024,256]{1,0:T(8,128)(2,1)}, u32[]{:S(2)}, u32[]{:S(2)}) collective-permute-start(bf16[1024,256]{1,0:T(8,128)(2,1)} %get-tuple-element.59), channel_id=1, source_target_pairs={{0,16},{9,25},{18,2},{27,11},{8,24},{1,17},{26,10},{19,3},{4,12},{... | collective-permute-start | bytes 1572872 | tf_op jit(solution)/shard_map/ppermute | solution.py:190
  12.4 24.5 %collective-permute-start.4 = (bf16[1024,256]{1,0:T(8,128)(2,1)S(1)}, bf16[1024,256]{1,0:T(8,128)(2,1)}, u32[]{:S(2)}, u32[]{:S(2)}) collective-permute-start(bf16[1024,256]{1,0:T(8,128)(2,1)S(1)} %get-tuple-element.58), channel_id=1, source_target_pairs={{0,16},{9,25},{18,2},{27,11},{8,24},{1,17},{26,10},{19,3},{4,12},{... | collective-permute-start | bytes 1572872 | tf_op jit(solution)/shard_map/ppermute | solution.py:190
  13.7 30.5 %collective-permute-start.5 = (bf16[144,512]{1,0:T(8,128)(2,1)}, bf16[144,512]{1,0:T(8,128)(2,1)S(1)}, u32[]{:S(2)}, u32[]{:S(2)}) collective-permute-start(bf16[144,512]{1,0:T(8,128)(2,1)} %get-tuple-element.41), channel_id=1, source_target_pairs={{0,1},{1,0},{2,3},{3,2},{4,5},{5,4},{6,7},{7,6},{8,9},{9,8},{10,11... | collective-permute-start | bytes 442376 | tf_op jit(solution)/shard_map/ppermute | solution.py:37
  15.4 28.8 %collective-permute-start.6 = (bf16[144,512]{1,0:T(8,128)(2,1)}, bf16[144,512]{1,0:T(8,128)(2,1)S(1)}, u32[]{:S(2)}, u32[]{:S(2)}) collective-permute-start(bf16[144,512]{1,0:T(8,128)(2,1)} %get-tuple-element.42), channel_id=1, source_target_pairs={{0,2},{1,3},{2,0},{3,1},{4,6},{5,7},{6,4},{7,5},{8,10},{9,11},{10,... | collective-permute-start | bytes 442376 | tf_op jit(solution)/shard_map/ppermute | solution.py:37
  28.2 8.8 %all-to-all-start = ((bf16[8,32,512]{2,1,0:T(8,128)(2,1)}), bf16[8,32,512]{2,1,0:T(8,128)(2,1)S(1)}, u32[]{:S(2)}, u32[]{:S(2)}) async-start(bf16[8,32,512]{2,1,0:T(8,128)(2,1)} %bitcast.13), calls=%async_computation | async-start | bytes 524288 | tf_op jit(solution)/shard_map/all_to_all | solution.py:259
  31.6 12.6 %collective-permute-start.7 = (bf16[144,512]{1,0:T(8,128)(2,1)S(1)}, bf16[144,512]{1,0:T(8,128)(2,1)S(1)}, u32[]{:S(2)}, u32[]{:S(2)}) collective-permute-start(bf16[144,512]{1,0:T(8,128)(2,1)S(1)} %copy-done.10), channel_id=1, source_target_pairs={{0,3},{1,2},{2,1},{3,0},{4,7},{5,6},{6,5},{7,4},{8,11},{9,10},{10,... | collective-permute-start | bytes 442376 | tf_op jit(solution)/shard_map/ppermute | solution.py:37
  34.6 4.2 %copy-start = (bf16[512,1024]{1,0:T(8,128)(2,1)S(1)}, bf16[512,1024]{1,0:T(8,128)(2,1)}, u32[]{:S(2)}) copy-start(bf16[512,1024]{1,0:T(8,128)(2,1)} %get-tuple-element.31.kept_ref) | copy-start | bytes 3145732
  34.6 4.2 %collective-permute-start.3 = (bf16[512,256]{1,0:T(8,128)(2,1)}, bf16[512,256]{1,0:T(8,128)(2,1)}, u32[]{:S(2)}, u32[]{:S(2)}) collective-permute-start(bf16[512,256]{1,0:T(8,128)(2,1)} %convolution_convert_fusion.2), channel_id=1, source_target_pairs={{0,4},{4,0},{8,12},{12,8},{16,20},{20,16},{24,28},{28,24},{1,5},{5... | collective-permute-start | bytes 786440 | tf_op jit(solution)/shard_map/ppermute | solution.py:29
  38.7 3.9 %collective-permute-start.8 = (bf16[512,256]{1,0:T(8,128)(2,1)S(1)}, bf16[512,256]{1,0:T(8,128)(2,1)S(1)}, u32[]{:S(2)}, u32[]{:S(2)}) collective-permute-start(bf16[512,256]{1,0:T(8,128)(2,1)S(1)} %convolution_convert_fusion.1), channel_id=1, source_target_pairs={{0,4},{4,0},{8,12},{12,8},{16,20},{20,16},{24,28},{28,24},{1,5},{5... | collective-permute-start | bytes 786440 | tf_op jit(solution)/shard_map/ppermute | solution.py:29
  40.4 3.8 %copy-start.1 = (bf16[144,512]{1,0:T(8,128)(2,1)S(1)}, bf16[144,512]{1,0:T(8,128)(2,1)}, u32[]{:S(2)}) copy-start(bf16[144,512]{1,0:T(8,128)(2,1)} %get-tuple-element.40.refs_0_) | copy-start | bytes 442372
  40.4 3.8 %copy-start.2 = (s32[1,1,8]{2,1,0:T(1,128)S(1)}, s32[1,1,8]{2,1,0:T(1,128)}, u32[]{:S(2)}) copy-start(s32[1,1,8]{2,1,0:T(1,128)} %param.15) | copy-start | bytes 100
  40.5 6.4 %collective-permute-start.13 = (bf16[256,256]{1,0:T(8,128)(2,1)S(1)}, bf16[256,256]{1,0:T(8,128)(2,1)S(1)}, u32[]{:S(2)}, u32[]{:S(2)}) collective-permute-start(bf16[256,256]{1,0:T(8,128)(2,1)S(1)} %slice.137), channel_id=1, source_target_pairs={{0,1},{1,0},{2,3},{3,2},{4,5},{5,4},{6,7},{7,6},{8,9},{9,8},{10,11... | collective-permute-start | bytes 393224 | tf_op jit(solution)/shard_map/ppermute | solution.py:37
  44.1 5.4 %collective-permute-start.9 = (bf16[256,256]{1,0:T(8,128)(2,1)S(1)}, bf16[256,256]{1,0:T(8,128)(2,1)S(1)}, u32[]{:S(2)}, u32[]{:S(2)}) collective-permute-start(bf16[256,256]{1,0:T(8,128)(2,1)S(1)} %slice.138), channel_id=1, source_target_pairs={{0,1},{1,0},{2,3},{3,2},{4,5},{5,4},{6,7},{7,6},{8,9},{9,8},{10,11... | collective-permute-start | bytes 393224 | tf_op jit(solution)/shard_map/ppermute | solution.py:37
  47.0 6.7 %collective-permute-start.14 = (bf16[128,256]{1,0:T(8,128)(2,1)S(1)}, bf16[128,256]{1,0:T(8,128)(2,1)S(1)}, u32[]{:S(2)}, u32[]{:S(2)}) collective-permute-start(bf16[128,256]{1,0:T(8,128)(2,1)S(1)} %slice.139), channel_id=1, source_target_pairs={{0,2},{1,3},{2,0},{3,1},{4,6},{5,7},{6,4},{7,5},{8,10},{9,11},{10,... | collective-permute-start | bytes 196616 | tf_op jit(solution)/shard_map/ppermute | solution.py:37
  49.6 5.8 %collective-permute-start.10 = (bf16[128,256]{1,0:T(8,128)(2,1)S(1)}, bf16[128,256]{1,0:T(8,128)(2,1)S(1)}, u32[]{:S(2)}, u32[]{:S(2)}) collective-permute-start(bf16[128,256]{1,0:T(8,128)(2,1)S(1)} %slice.140), channel_id=1, source_target_pairs={{0,2},{1,3},{2,0},{3,1},{4,6},{5,7},{6,4},{7,5},{8,10},{9,11},{10,... | collective-permute-start | bytes 196616 | tf_op jit(solution)/shard_map/ppermute | solution.py:37
  55.5 5.4 %collective-permute-start.18 = (bf16[128,256]{1,0:T(8,128)(2,1)S(1)}, bf16[128,256]{1,0:T(8,128)(2,1)S(1)}, u32[]{:S(2)}, u32[]{:S(2)}) collective-permute-start(bf16[128,256]{1,0:T(8,128)(2,1)S(1)} %get-tuple-element.63), channel_id=1, source_target_pairs={{0,2},{1,3},{2,0},{3,1},{4,6},{5,7},{6,4},{7,5},{8,10},{9,11},{10,... | collective-permute-start | bytes 196616 | tf_op jit(solution)/shard_map/ppermute | solution.py:37
  56.6 6.5 %collective-permute-start.11 = (bf16[128,256]{1,0:T(8,128)(2,1)S(1)}, bf16[128,256]{1,0:T(8,128)(2,1)S(1)}, u32[]{:S(2)}, u32[]{:S(2)}) collective-permute-start(bf16[128,256]{1,0:T(8,128)(2,1)S(1)} %get-tuple-element.64), channel_id=1, source_target_pairs={{0,2},{1,3},{2,0},{3,1},{4,6},{5,7},{6,4},{7,5},{8,10},{9,11},{10,... | collective-permute-start | bytes 196616 | tf_op jit(solution)/shard_map/ppermute | solution.py:37
  60.9 5.8 %collective-permute-start.19 = (bf16[256,256]{1,0:T(8,128)(2,1)S(1)}, bf16[256,256]{1,0:T(8,128)(2,1)S(1)}, u32[]{:S(2)}, u32[]{:S(2)}) collective-permute-start(bf16[256,256]{1,0:T(8,128)(2,1)S(1)} %pad_maximum_fusion.4), channel_id=1, source_target_pairs={{0,1},{1,0},{2,3},{3,2},{4,5},{5,4},{6,7},{7,6},{8,9},{9,8},{10,11... | collective-permute-start | bytes 393224 | tf_op jit(solution)/shard_map/ppermute | solution.py:37
  63.1 5.0 %collective-permute-start.12 = (bf16[256,256]{1,0:T(8,128)(2,1)S(1)}, bf16[256,256]{1,0:T(8,128)(2,1)S(1)}, u32[]{:S(2)}, u32[]{:S(2)}) collective-permute-start(bf16[256,256]{1,0:T(8,128)(2,1)S(1)} %pad_maximum_fusion.3), channel_id=1, source_target_pairs={{0,1},{1,0},{2,3},{3,2},{4,5},{5,4},{6,7},{7,6},{8,9},{9,8},{10,11... | collective-permute-start | bytes 393224 | tf_op jit(solution)/shard_map/ppermute | solution.py:37
  66.7 1.7 %collective-permute-start.20 = (bf16[512,256]{1,0:T(8,128)(2,1)S(1)}, bf16[512,256]{1,0:T(8,128)(2,1)S(1)}, u32[]{:S(2)}, u32[]{:S(2)}) collective-permute-start(bf16[512,256]{1,0:T(8,128)(2,1)S(1)} %pad_maximum_fusion.1.slope_ref), channel_id=1, source_target_pairs={{0,4},{4,0},{8,12},{12,8},{16,20},{20,16},{24,28},{28,24},{1,5},{5... | collective-permute-start | bytes 786440 | tf_op jit(solution)/shard_map/ppermute | solution.py:29
  68.2 5.8 %collective-permute-start.15 = (bf16[512,256]{1,0:T(8,128)(2,1)S(1)}, bf16[512,256]{1,0:T(8,128)(2,1)S(1)}, u32[]{:S(2)}, u32[]{:S(2)}) collective-permute-start(bf16[512,256]{1,0:T(8,128)(2,1)S(1)} %pad_maximum_fusion.slope_ref), channel_id=1, source_target_pairs={{0,4},{4,0},{8,12},{12,8},{16,20},{20,16},{24,28},{28,24},{1,5},{5... | collective-permute-start | bytes 786440 | tf_op jit(solution)/shard_map/ppermute | solution.py:29
  70.5 10.3 %collective-permute-start.21 = (bf16[512,256]{1,0:T(8,128)(2,1)}, bf16[512,256]{1,0:T(8,128)(2,1)}, u32[]{:S(2)}, u32[]{:S(2)}) collective-permute-start(bf16[512,256]{1,0:T(8,128)(2,1)} %get-tuple-element.54), channel_id=1, source_target_pairs={{0,8},{4,20},{8,0},{12,28},{16,24},{20,4},{24,16},{28,12},{1,9},{5... | collective-permute-start | bytes 786440 | tf_op jit(solution)/shard_map/ppermute | solution.py:370
  75.4 6.6 %collective-permute-start.16 = (bf16[512,256]{1,0:T(8,128)(2,1)S(1)}, bf16[512,256]{1,0:T(8,128)(2,1)S(1)}, u32[]{:S(2)}, u32[]{:S(2)}) collective-permute-start(bf16[512,256]{1,0:T(8,128)(2,1)S(1)} %get-tuple-element.52), channel_id=1, source_target_pairs={{0,8},{4,20},{8,0},{12,28},{16,24},{20,4},{24,16},{28,12},{1,9},{5... | collective-permute-start | bytes 786440 | tf_op jit(solution)/shard_map/ppermute | solution.py:370
  75.5 13.4 %all-to-all-start.1 = ((bf16[8,32,512]{2,1,0:T(8,128)(2,1)}), bf16[8,32,512]{2,1,0:T(8,128)(2,1)S(1)}, u32[]{:S(2)}, u32[]{:S(2)}) async-start(bf16[8,32,512]{2,1,0:T(8,128)(2,1)} %bitcast.28), calls=%async_computation.1 | async-start | bytes 524288 | tf_op jit(solution)/shard_map/all_to_all | solution.py:328
  81.9 5.5 %collective-permute-start.22 = (bf16[256,256]{1,0:T(8,128)(2,1)S(1)}, bf16[256,256]{1,0:T(8,128)(2,1)S(1)}, u32[]{:S(2)}, u32[]{:S(2)}) collective-permute-start(bf16[256,256]{1,0:T(8,128)(2,1)S(1)} %slice.135), channel_id=1, source_target_pairs={{0,16},{4,12},{8,24},{12,4},{16,0},{20,28},{24,8},{28,20},{1,17},{... | collective-permute-start | bytes 393224 | tf_op jit(solution)/shard_map/ppermute | solution.py:370
  82.1 6.7 %collective-permute-start.17 = (bf16[256,256]{1,0:T(8,128)(2,1)S(1)}, bf16[256,256]{1,0:T(8,128)(2,1)S(1)}, u32[]{:S(2)}, u32[]{:S(2)}) collective-permute-start(bf16[256,256]{1,0:T(8,128)(2,1)S(1)} %slice.136), channel_id=1, source_target_pairs={{0,16},{4,12},{8,24},{12,4},{16,0},{20,28},{24,8},{28,20},{1,17},{... | collective-permute-start | bytes 393224 | tf_op jit(solution)/shard_map/ppermute | solution.py:370
  88.9 12.9 %collective-permute-start.23 = (bf16[256,512]{1,0:T(8,128)(2,1)S(1)}, bf16[256,512]{1,0:T(8,128)(2,1)S(1)}, u32[]{:S(2)}, u32[]{:S(2)}) collective-permute-start(bf16[256,512]{1,0:T(8,128)(2,1)S(1)} %pad_maximum_fusion.2), channel_id=1, source_target_pairs={{0,0},{1,10},{2,17},{3,27},{4,4},{5,14},{6,21},{7,31},{8,1},{9,11}... | collective-permute-start | bytes 786440 | tf_op jit(solution)/shard_map/ppermute | solution.py:382
  (5 other events, 16.5 us)

commit v18 on v17

--- a/solution.py
+++ b/solution.py
@@ -270,12 +270,12 @@
     value_parts = []
     for j in range(PARTS):
         held_part, got_part, is_getter_part = parts[j]
-        if j == 0:
-            got_part, got_cot = lax.optimization_barrier((got_part, got_cot))
         weight = jnp.where(is_getter_part, got_part, held_part)
         value_given = dot(got_rows, weight).astype(BF16)
-        value_got = swapped(value_given, dp_count).astype(F32)
-        value_parts.append(dot(kept_rows, weight) + value_got)
+        value_got = swapped(value_given, dp_count)
+        if j == 0:
+            value_got, got_cot = lax.optimization_barrier((value_got, got_cot))
+        value_parts.append(dot(kept_rows, weight) + value_got.astype(F32))
 
     tied = (value_parts[-1], lengths, bins, advantage, logprob_gap)
     value_parts[-1], lengths, bins, advantage, logprob_gap = lax.optimization_barrier(tied)

time: 103 us -> 106 us (1.029)
  the two profiles are of different devices: /device:TPU:4 before, /device:TPU:24 now
where the time goes in v18:
time: 106 us
  starting transfers between devices  41.3 us (39%)
  waiting for transfers between devices  36.2 us (34%)
  Pallas kernels  13.4 us (13%)
  matrix products  8.01 us (8%)
  other arithmetic  3.88 us (4%)
  local copies, waits for them, and re-layouts  1.82 us (2%)
  between operations  1.09 us (1%)
    ppermute x11, starting transfers between devices, crossed(): return lax.ppermute(array, 'tensor', [(i, i ^ step) for i in range(count)])  21.6 us
    ppermute x11, waiting for transfers between devices, crossed(): return lax.ppermute(array, 'tensor', [(i, i ^ step) for i in range(count)])  17.2 us
    ppermute x1, waiting for transfers between devices, on_device(): grad_weight = lax.ppermute(grad, AXES, pairs).astype(F32)  8.64 us
    pallas_call x1, Pallas kernels, on_device(): pl.pallas_call(functools.partial(prepare_kernel, tensor_count, steps), gr...  7.18 us
    dot_general x4, matrix products, dot(): return jnp.dot(a, b, preferred_element_type=F32)  7.06 us
    ppermute x4, waiting for transfers between devices, on_device(): total = total + lax.ppermute(given, 'dp', pairs).astype(F32)  5.46 us
    ppermute x3, waiting for transfers between devices, stage(): return (lax.ppermute(held, AXES, pairs), is_getter)  4.83 us
    ppermute x4, starting transfers between devices, on_device(): total = total + lax.ppermute(given, 'dp', pairs).astype(F32)  4.25 us
  transfers between devices with their start and end apart: 26, of which 12 were waited for; matrix products, arithmetic and copies ran while one was open for 12% of the time, Pallas kernels for 13%

profile of v18, /device:TPU:24, one launch (start us, length us, event | category | flops | bytes accessed | tf_op | source)
XLA Modules:
  0.0 105.7 jit_solution(9557989616447424267)
XLA Ops:
  0.6 1.7 %collective-permute-start = (bf16[1024,512]{1,0:T(8,128)(2,1)}, bf16[1024,512]{1,0:T(8,128)(2,1)}, u32[]{:S(2)}, u32[]{:S(2)}) collective-permute-start(bf16[1024,512]{1,0:T(8,128)(2,1)} %param.14), channel_id=1, source_target_pairs={{0,8},{9,1},{18,26},{27,19},{4,20},{13,29},{22,6},{31,15}} | collective-permute-start | bytes 3145736 | tf_op jit(solution)/shard_map/ppermute | solution.py:190
  2.9 7.2 %prepare.1 = (bf16[512,1024]{1,0:T(8,128)(2,1)}, bf16[512,1024]{1,0:T(8,128)(2,1)}, bf16[144,512]{1,0:T(8,128)(2,1)}, bf16[144,512]{1,0:T(8,128)(2,1)}, bf16[144...) custom-call(s32[2]{0:T(128)} %pad_add_fusion.1.at, bf16[512,2048]{1,0:T(8,128)(2,1)} %x_ref.1, f32[1,2048]{1,0:T(1,128)} %bitcast.32, ...), custom_call_target="tpu_custom_call" | custom-call | flops 1073741824 | bytes 8388608 | tf_op jit(solution)/shard_map/prepare/pallas_call | solution.py:202
  11.3 1.3 %collective-permute-start.2 = (bf16[1024,256]{1,0:T(8,128)(2,1)}, bf16[1024,256]{1,0:T(8,128)(2,1)}, u32[]{:S(2)}, u32[]{:S(2)}) collective-permute-start(bf16[1024,256]{1,0:T(8,128)(2,1)} %get-tuple-element.59), channel_id=1, source_target_pairs={{0,16},{9,25},{18,2},{27,11},{8,24},{1,17},{26,10},{19,3},{4,12},{... | collective-permute-start | bytes 1572872 | tf_op jit(solution)/shard_map/ppermute | solution.py:190
  12.5 1.3 %collective-permute-start.4 = (bf16[1024,256]{1,0:T(8,128)(2,1)S(1)}, bf16[1024,256]{1,0:T(8,128)(2,1)}, u32[]{:S(2)}, u32[]{:S(2)}) collective-permute-start(bf16[1024,256]{1,0:T(8,128)(2,1)S(1)} %get-tuple-element.58), channel_id=1, source_target_pairs={{0,16},{9,25},{18,2},{27,11},{8,24},{1,17},{26,10},{19,3},{4,12},{... | collective-permute-start | bytes 1572872 | tf_op jit(solution)/shard_map/ppermute | solution.py:190
  14.4 10.1 %collective-permute-start.7 = (bf16[144,512]{1,0:T(8,128)(2,1)}, bf16[144,512]{1,0:T(8,128)(2,1)S(1)}, u32[]{:S(2)}, u32[]{:S(2)}) collective-permute-start(bf16[144,512]{1,0:T(8,128)(2,1)} %get-tuple-element.42), channel_id=1, source_target_pairs={{0,2},{1,3},{2,0},{3,1},{4,6},{5,7},{6,4},{7,5},{8,10},{9,11},{10,... | collective-permute-start | bytes 442376 | tf_op jit(solution)/shard_map/ppermute | solution.py:37
  24.4 3.8 %all-to-all-start = ((bf16[8,32,512]{2,1,0:T(8,128)(2,1)}), bf16[8,32,512]{2,1,0:T(8,128)(2,1)S(1)}, u32[]{:S(2)}, u32[]{:S(2)}) async-start(bf16[8,32,512]{2,1,0:T(8,128)(2,1)} %bitcast.13), calls=%async_computation | async-start | bytes 524288 | tf_op jit(solution)/shard_map/all_to_all | solution.py:259
  28.3 3.1 %collective-permute-start.8 = (bf16[144,512]{1,0:T(8,128)(2,1)}, bf16[144,512]{1,0:T(8,128)(2,1)S(1)}, u32[]{:S(2)}, u32[]{:S(2)}) collective-permute-start(bf16[144,512]{1,0:T(8,128)(2,1)} %get-tuple-element.43), channel_id=1, source_target_pairs={{0,3},{1,2},{2,1},{3,0},{4,7},{5,6},{6,5},{7,4},{8,11},{9,10},{10,... | collective-permute-start | bytes 442376 | tf_op jit(solution)/shard_map/ppermute | solution.py:37
  31.3 1.5 %convolution_convert_fusion.2 = bf16[512,256]{1,0:T(8,128)(2,1)S(1)} fusion(bf16[512,1024]{1,0:T(8,128)(2,1)S(1)} %collective-permute-done.1.got_ref, bf16[1024,256]{1,0:T(8,128)(2,1)} %collective-permute-done.2, pred[]{:T(512)S(6)} %or.18, bf16[1024,512]{1,0:T(8,128)(2,1)S(1)} %broadcast_select_fusion), kind=kOutput, calls=%fused_computation.4 | convolution fusion | flops 268828672 | bytes 2359297 | tf_op jit(solution)/shard_map/dot_general | solution.py:21
  33.1 4.8 %collective-permute-done.4 = bf16[1024,256]{1,0:T(8,128)(2,1)} collective-permute-done((bf16[1024,256]{1,0:T(8,128)(2,1)S(1)}, bf16[1024,256]{1,0:T(8,128)(2,1)}, u32[]{:S(2)}, u32[]{:S(2)}) %collective-permute-start.4) | collective-permute-done | bytes 524320 | tf_op jit(solution)/shard_map/ppermute | solution.py:190
  37.9 2.4 %convolution_convert_fusion.1 = bf16[512,256]{1,0:T(8,128)(2,1)} fusion(bf16[512,1024]{1,0:T(8,128)(2,1)S(1)} %collective-permute-done.1.got_ref, bf16[1024,256]{1,0:T(8,128)(2,1)} %collective-permute-done.4, pred[]{:T(512)S(6)} %or.18, bf16[1024,512]{1,0:T(8,128)(2,1)} %copy-done.6), kind=kOutput, calls=%fused_computation.3 | convolution fusion | flops 268828672 | bytes 2359297 | tf_op jit(solution)/shard_map/dot_general | solution.py:21
  40.3 1.5 %convolution_add_fusion.1 = f32[512,256]{1,0:T(8,128)S(1)} fusion(bf16[512,1024]{1,0:T(8,128)(2,1)S(1)} %copy-done, bf16[512,256]{1,0:T(8,128)(2,1)S(1)} %collective-permute-done.3, bf16[1024,256]{1,0:T(8,128)(2,1)} %collective-permute-done.2, pred[]{:T(512)S(6)} %or.18, bf16[1024,512]{1,0:T(8,128)(2,1)S(1)} %copy-done.7), kind=kOutput, calls=%fused_computation.1 | convolution fusion | flops 268959744 | bytes 2883585 | tf_op jit(solution)/shard_map/dot_general | solution.py:21
  42.5 1.7 %convolution_add_fusion = f32[512,256]{1,0:T(8,128)S(1)} fusion(bf16[512,1024]{1,0:T(8,128)(2,1)S(1)} %copy-done, bf16[512,256]{1,0:T(8,128)(2,1)} %collective-permute-done.5, bf16[1024,256]{1,0:T(8,128)(2,1)} %collective-permute-done.4, pred[]{:T(512)S(6)} %or.18, bf16[1024,512]{1,0:T(8,128)(2,1)} %copy-done.6), kind=kOutput, calls=%fused_computation | convolution fusion | flops 268959744 | bytes 2883585 | tf_op jit(solution)/shard_map/dot_general | solution.py:21
  44.3 2.1 %collective-permute-start.9 = (bf16[256,256]{1,0:T(8,128)(2,1)S(1)}, bf16[256,256]{1,0:T(8,128)(2,1)S(1)}, u32[]{:S(2)}, u32[]{:S(2)}) collective-permute-start(bf16[256,256]{1,0:T(8,128)(2,1)S(1)} %slice.138), channel_id=1, source_target_pairs={{0,1},{1,0},{2,3},{3,2},{4,5},{5,4},{6,7},{7,6},{8,9},{9,8},{10,11... | collective-permute-start | bytes 393224 | tf_op jit(solution)/shard_map/ppermute | solution.py:37
  46.4 1.1 %rows.1 = (f32[128,512]{1,0:T(8,128)S(1)}, f32[128,128]{1,0:T(8,128)S(1)}, f32[128,128]{1,0:T(8,128)S(1)}, bf16[128,256]{1,0:T(8,128)(2,1)S(1)}) custom-call(s32[8]{0:T(128)S(1)} %bitcast.24, s32[8]{0:T(128)S(1)} %bitcast.25, f32[8]{0:T(128)S(1)} %bitcast.26, f32[1,128]{1,0:T(1,128)S(1)} %bitcast.27, bf16[256,512]{1,0:T(8,128)(2,1)S(1)} %bitcast.23, ...), custom_call_target="tpu_custom_call" | custom-call | flops 33554432 | bytes 2097152 | tf_op jit(solution)/shard_map/rows/pallas_call | solution.py:284
  47.5 1.6 %collective-permute-done.13 = bf16[256,256]{1,0:T(8,128)(2,1)} collective-permute-done((bf16[256,256]{1,0:T(8,128)(2,1)}, bf16[256,256]{1,0:T(8,128)(2,1)}, u32[]{:S(2)}, u32[]{:S(2)}) %collective-permute-start.13) | collective-permute-done | bytes 131104 | tf_op jit(solution)/shard_map/ppermute | solution.py:37
  50.1 1.3 %collective-permute-done.9 = bf16[256,256]{1,0:T(8,128)(2,1)S(1)} collective-permute-done((bf16[256,256]{1,0:T(8,128)(2,1)S(1)}, bf16[256,256]{1,0:T(8,128)(2,1)S(1)}, u32[]{:S(2)}, u32[]{:S(2)}) %collective-permute-start.9) | collective-permute-done | bytes 131104 | tf_op jit(solution)/shard_map/ppermute | solution.py:37
  51.5 1.7 %collective-permute-start.10 = (bf16[128,256]{1,0:T(8,128)(2,1)S(1)}, bf16[128,256]{1,0:T(8,128)(2,1)S(1)}, u32[]{:S(2)}, u32[]{:S(2)}) collective-permute-start(bf16[128,256]{1,0:T(8,128)(2,1)S(1)} %slice.140), channel_id=1, source_target_pairs={{0,2},{1,3},{2,0},{3,1},{4,6},{5,7},{6,4},{7,5},{8,10},{9,11},{10,... | collective-permute-start | bytes 196616 | tf_op jit(solution)/shard_map/ppermute | solution.py:37
  53.3 4.2 %collective-permute-done.14 = bf16[128,256]{1,0:T(8,128)(2,1)S(1)} collective-permute-done((bf16[128,256]{1,0:T(8,128)(2,1)S(1)}, bf16[128,256]{1,0:T(8,128)(2,1)S(1)}, u32[]{:S(2)}, u32[]{:S(2)}) %collective-permute-start.14) | collective-permute-done | bytes 65568 | tf_op jit(solution)/shard_map/ppermute | solution.py:37
  57.4 1.1 %collective-permute-done.10 = bf16[128,256]{1,0:T(8,128)(2,1)S(1)} collective-permute-done((bf16[128,256]{1,0:T(8,128)(2,1)S(1)}, bf16[128,256]{1,0:T(8,128)(2,1)S(1)}, u32[]{:S(2)}, u32[]{:S(2)}) %collective-permute-start.10) | collective-permute-done | bytes 65568 | tf_op jit(solution)/shard_map/ppermute | solution.py:37
  58.7 2.9 %collective-permute-start.11 = (bf16[128,256]{1,0:T(8,128)(2,1)S(1)}, bf16[128,256]{1,0:T(8,128)(2,1)S(1)}, u32[]{:S(2)}, u32[]{:S(2)}) collective-permute-start(bf16[128,256]{1,0:T(8,128)(2,1)S(1)} %get-tuple-element.64), channel_id=1, source_target_pairs={{0,2},{1,3},{2,0},{3,1},{4,6},{5,7},{6,4},{7,5},{8,10},{9,11},{10,... | collective-permute-start | bytes 196616 | tf_op jit(solution)/shard_map/ppermute | solution.py:37
  61.6 3.5 %collective-permute-done.18 = bf16[128,256]{1,0:T(8,128)(2,1)S(1)} collective-permute-done((bf16[128,256]{1,0:T(8,128)(2,1)S(1)}, bf16[128,256]{1,0:T(8,128)(2,1)S(1)}, u32[]{:S(2)}, u32[]{:S(2)}) %collective-permute-start.18) | collective-permute-done | bytes 65568 | tf_op jit(solution)/shard_map/ppermute | solution.py:37
  67.2 4.3 %collective-permute-done.19 = bf16[256,256]{1,0:T(8,128)(2,1)S(1)} collective-permute-done((bf16[256,256]{1,0:T(8,128)(2,1)S(1)}, bf16[256,256]{1,0:T(8,128)(2,1)S(1)}, u32[]{:S(2)}, u32[]{:S(2)}) %collective-permute-start.19) | collective-permute-done | bytes 131104 | tf_op jit(solution)/shard_map/ppermute | solution.py:37
  73.2 2.1 %gradient.3 = (f32[512,256]{1,0:T(8,128)S(1)}, bf16[512,256]{1,0:T(8,128)(2,1)}) custom-call(s32[4]{0:T(128)S(1)} %pad_add_fusion.at, bf16[512,1024]{1,0:T(8,128)(2,1)S(1)} %copy-done, bf16[512,1024]{1,0:T(8,128)(2,1)S(1)} %collective-permute-done.1.got_ref, bf16[512,256]{1,0:T(8,128)(2,1)S(1)} %pad_maximum_fusion.1.slope_ref, ...), custom_call_target="tpu_custom_call" | custom-call | flops 536870912 | bytes 4194304 | tf_op jit(solution)/shard_map/gradient/pallas_call | solution.py:333
  75.7 1.4 %gradient.2 = (f32[512,256]{1,0:T(8,128)S(1)}, bf16[512,256]{1,0:T(8,128)(2,1)S(1)}) custom-call(s32[4]{0:T(128)S(1)} %pad_add_fusion.at, bf16[512,1024]{1,0:T(8,128)(2,1)S(1)} %copy-done, bf16[512,1024]{1,0:T(8,128)(2,1)S(1)} %collective-permute-done.1.got_ref, bf16[512,256]{1,0:T(8,128)(2,1)S(1)} %pad_maximum_fusion.slope_ref, ...), custom_call_target="tpu_custom_call" | custom-call | flops 536870912 | bytes 4194304 | tf_op jit(solution)/shard_map/gradient/pallas_call | solution.py:333
  77.1 1.7 %collective-permute-start.16 = (bf16[512,256]{1,0:T(8,128)(2,1)S(1)}, bf16[512,256]{1,0:T(8,128)(2,1)S(1)}, u32[]{:S(2)}, u32[]{:S(2)}) collective-permute-start(bf16[512,256]{1,0:T(8,128)(2,1)S(1)} %get-tuple-element.52), channel_id=1, source_target_pairs={{0,8},{4,20},{8,0},{12,28},{16,24},{20,4},{24,16},{28,12},{1,9},{5... | collective-permute-start | bytes 786440 | tf_op jit(solution)/shard_map/ppermute | solution.py:370
  78.8 3.4 %all-to-all-start.1 = ((bf16[8,32,512]{2,1,0:T(8,128)(2,1)}), bf16[8,32,512]{2,1,0:T(8,128)(2,1)S(1)}, u32[]{:S(2)}, u32[]{:S(2)}) async-start(bf16[8,32,512]{2,1,0:T(8,128)(2,1)} %bitcast.28), calls=%async_computation.1 | async-start | bytes 524288 | tf_op jit(solution)/shard_map/all_to_all | solution.py:328
  83.3 2.0 %collective-permute-start.22 = (bf16[256,256]{1,0:T(8,128)(2,1)S(1)}, bf16[256,256]{1,0:T(8,128)(2,1)S(1)}, u32[]{:S(2)}, u32[]{:S(2)}) collective-permute-start(bf16[256,256]{1,0:T(8,128)(2,1)S(1)} %slice.135), channel_id=1, source_target_pairs={{0,16},{4,12},{8,24},{12,4},{16,0},{20,28},{24,8},{28,20},{1,17},{... | collective-permute-start | bytes 393224 | tf_op jit(solution)/shard_map/ppermute | solution.py:370
  85.5 4.1 %collective-permute-done.22 = bf16[256,256]{1,0:T(8,128)(2,1)S(1)} collective-permute-done((bf16[256,256]{1,0:T(8,128)(2,1)S(1)}, bf16[256,256]{1,0:T(8,128)(2,1)S(1)}, u32[]{:S(2)}, u32[]{:S(2)}) %collective-permute-start.22) | collective-permute-done | bytes 131104 | tf_op jit(solution)/shard_map/ppermute | solution.py:370
  89.6 1.4 %collective-permute-done.17 = bf16[256,256]{1,0:T(8,128)(2,1)S(1)} collective-permute-done((bf16[256,256]{1,0:T(8,128)(2,1)S(1)}, bf16[256,256]{1,0:T(8,128)(2,1)S(1)}, u32[]{:S(2)}, u32[]{:S(2)}) %collective-permute-start.17) | collective-permute-done | bytes 131104 | tf_op jit(solution)/shard_map/ppermute | solution.py:370
  91.1 3.5 %collective-permute-start.23 = (bf16[256,512]{1,0:T(8,128)(2,1)S(1)}, bf16[256,512]{1,0:T(8,128)(2,1)S(1)}, u32[]{:S(2)}, u32[]{:S(2)}) collective-permute-start(bf16[256,512]{1,0:T(8,128)(2,1)S(1)} %pad_maximum_fusion.2), channel_id=1, source_target_pairs={{0,0},{1,10},{2,17},{3,27},{4,4},{5,14},{6,21},{7,31},{8,1},{9,11}... | collective-permute-start | bytes 786440 | tf_op jit(solution)/shard_map/ppermute | solution.py:382
  94.6 1.7 %write.1 = bf16[256,512]{1,0:T(8,128)(2,1)} custom-call(bf16[256,512]{1,0:T(8,128)(2,1)} %bitcast.29), custom_call_target="tpu_custom_call" | custom-call | bytes 524288 | tf_op jit(solution)/shard_map/write/pallas_call | solution.py:383
  96.2 8.6 %collective-permute-done.23 = bf16[256,512]{1,0:T(8,128)(2,1)S(1)} collective-permute-done((bf16[256,512]{1,0:T(8,128)(2,1)S(1)}, bf16[256,512]{1,0:T(8,128)(2,1)S(1)}, u32[]{:S(2)}, u32[]{:S(2)}) %collective-permute-start.23) | collective-permute-done | bytes 262176 | tf_op jit(solution)/shard_map/ppermute | solution.py:382
  (74 shorter events, 11.0 us)
Async XLA Ops:
  0.6 9.5 %collective-permute-start = (bf16[1024,512]{1,0:T(8,128)(2,1)}, bf16[1024,512]{1,0:T(8,128)(2,1)}, u32[]{:S(2)}, u32[]{:S(2)}) collective-permute-start(bf16[1024,512]{1,0:T(8,128)(2,1)} %param.14), channel_id=1, source_target_pairs={{0,8},{9,1},{18,26},{27,19},{4,20},{13,29},{22,6},{31,15}} | collective-permute-start | bytes 3145736 | tf_op jit(solution)/shard_map/ppermute | solution.py:190
  2.9 7.3 %copy-start.8 = (bf16[1024,512]{1,0:T(8,128)(2,1)S(1)}, bf16[1024,512]{1,0:T(8,128)(2,1)}, u32[]{:S(2)}) copy-start(bf16[1024,512]{1,0:T(8,128)(2,1)} %param.14) | copy-start | bytes 3145732
  10.1 18.2 %collective-permute-start.1 = (bf16[512,1024]{1,0:T(8,128)(2,1)}, bf16[512,1024]{1,0:T(8,128)(2,1)S(1)}, u32[]{:S(2)}, u32[]{:S(2)}) collective-permute-start(bf16[512,1024]{1,0:T(8,128)(2,1)} %get-tuple-element.32), channel_id=1, source_target_pairs={{0,4},{4,0},{8,12},{12,8},{16,20},{20,16},{24,28},{28,24},{1,5},{5... | collective-permute-start | bytes 3145736 | tf_op jit(solution)/shard_map/ppermute | solution.py:29
  10.3 21.0 %copy-start.6 = (bf16[1024,512]{1,0:T(8,128)(2,1)}, bf16[1024,512]{1,0:T(8,128)(2,1)S(1)}, u32[]{:S(2)}) copy-start(bf16[1024,512]{1,0:T(8,128)(2,1)S(1)} %broadcast_select_fusion) | copy-start | bytes 3145732
  11.3 20.1 %collective-permute-start.2 = (bf16[1024,256]{1,0:T(8,128)(2,1)}, bf16[1024,256]{1,0:T(8,128)(2,1)}, u32[]{:S(2)}, u32[]{:S(2)}) collective-permute-start(bf16[1024,256]{1,0:T(8,128)(2,1)} %get-tuple-element.59), channel_id=1, source_target_pairs={{0,16},{9,25},{18,2},{27,11},{8,24},{1,17},{26,10},{19,3},{4,12},{... | collective-permute-start | bytes 1572872 | tf_op jit(solution)/shard_map/ppermute | solution.py:190
  12.5 25.4 %collective-permute-start.4 = (bf16[1024,256]{1,0:T(8,128)(2,1)S(1)}, bf16[1024,256]{1,0:T(8,128)(2,1)}, u32[]{:S(2)}, u32[]{:S(2)}) collective-permute-start(bf16[1024,256]{1,0:T(8,128)(2,1)S(1)} %get-tuple-element.58), channel_id=1, source_target_pairs={{0,16},{9,25},{18,2},{27,11},{8,24},{1,17},{26,10},{19,3},{4,12},{... | collective-permute-start | bytes 1572872 | tf_op jit(solution)/shard_map/ppermute | solution.py:190
  13.8 32.5 %collective-permute-start.6 = (bf16[144,512]{1,0:T(8,128)(2,1)}, bf16[144,512]{1,0:T(8,128)(2,1)S(1)}, u32[]{:S(2)}, u32[]{:S(2)}) collective-permute-start(bf16[144,512]{1,0:T(8,128)(2,1)} %get-tuple-element.41), channel_id=1, source_target_pairs={{0,1},{1,0},{2,3},{3,2},{4,5},{5,4},{6,7},{7,6},{8,9},{9,8},{10,11... | collective-permute-start | bytes 442376 | tf_op jit(solution)/shard_map/ppermute | solution.py:37
  14.4 32.0 %collective-permute-start.7 = (bf16[144,512]{1,0:T(8,128)(2,1)}, bf16[144,512]{1,0:T(8,128)(2,1)S(1)}, u32[]{:S(2)}, u32[]{:S(2)}) collective-permute-start(bf16[144,512]{1,0:T(8,128)(2,1)} %get-tuple-element.42), channel_id=1, source_target_pairs={{0,2},{1,3},{2,0},{3,1},{4,6},{5,7},{6,4},{7,5},{8,10},{9,11},{10,... | collective-permute-start | bytes 442376 | tf_op jit(solution)/shard_map/ppermute | solution.py:37
  24.4 18.1 %all-to-all-start = ((bf16[8,32,512]{2,1,0:T(8,128)(2,1)}), bf16[8,32,512]{2,1,0:T(8,128)(2,1)S(1)}, u32[]{:S(2)}, u32[]{:S(2)}) async-start(bf16[8,32,512]{2,1,0:T(8,128)(2,1)} %bitcast.13), calls=%async_computation | async-start | bytes 524288 | tf_op jit(solution)/shard_map/all_to_all | solution.py:259
  28.3 18.1 %collective-permute-start.8 = (bf16[144,512]{1,0:T(8,128)(2,1)}, bf16[144,512]{1,0:T(8,128)(2,1)S(1)}, u32[]{:S(2)}, u32[]{:S(2)}) collective-permute-start(bf16[144,512]{1,0:T(8,128)(2,1)} %get-tuple-element.43), channel_id=1, source_target_pairs={{0,3},{1,2},{2,1},{3,0},{4,7},{5,6},{6,5},{7,4},{8,11},{9,10},{10,... | collective-permute-start | bytes 442376 | tf_op jit(solution)/shard_map/ppermute | solution.py:37
  32.8 7.4 %copy-start = (bf16[512,1024]{1,0:T(8,128)(2,1)S(1)}, bf16[512,1024]{1,0:T(8,128)(2,1)}, u32[]{:S(2)}) copy-start(bf16[512,1024]{1,0:T(8,128)(2,1)} %get-tuple-element.31.kept_ref) | copy-start | bytes 3145732
  32.8 7.4 %copy-start.7 = (bf16[1024,512]{1,0:T(8,128)(2,1)S(1)}, bf16[1024,512]{1,0:T(8,128)(2,1)}, u32[]{:S(2)}) copy-start(bf16[1024,512]{1,0:T(8,128)(2,1)} %copy-done.6) | copy-start | bytes 3145732
  32.9 7.4 %collective-permute-start.3 = (bf16[512,256]{1,0:T(8,128)(2,1)S(1)}, bf16[512,256]{1,0:T(8,128)(2,1)S(1)}, u32[]{:S(2)}, u32[]{:S(2)}) collective-permute-start(bf16[512,256]{1,0:T(8,128)(2,1)S(1)} %convolution_convert_fusion.2), channel_id=1, source_target_pairs={{0,4},{4,0},{8,12},{12,8},{16,20},{20,16},{24,28},{28,24},{1,5},{5... | collective-permute-start | bytes 786440 | tf_op jit(solution)/shard_map/ppermute | solution.py:29
  40.3 2.3 %collective-permute-start.5 = (bf16[512,256]{1,0:T(8,128)(2,1)}, bf16[512,256]{1,0:T(8,128)(2,1)}, u32[]{:S(2)}, u32[]{:S(2)}) collective-permute-start(bf16[512,256]{1,0:T(8,128)(2,1)} %convolution_convert_fusion.1), channel_id=1, source_target_pairs={{0,4},{4,0},{8,12},{12,8},{16,20},{20,16},{24,28},{28,24},{1,5},{5... | collective-permute-start | bytes 786440 | tf_op jit(solution)/shard_map/ppermute | solution.py:29
  41.8 4.6 %copy-start.1 = (bf16[144,512]{1,0:T(8,128)(2,1)S(1)}, bf16[144,512]{1,0:T(8,128)(2,1)}, u32[]{:S(2)}) copy-start(bf16[144,512]{1,0:T(8,128)(2,1)} %get-tuple-element.40.refs_0_) | copy-start | bytes 442372
  41.8 4.6 %copy-start.2 = (s32[1,1,8]{2,1,0:T(1,128)S(1)}, s32[1,1,8]{2,1,0:T(1,128)}, u32[]{:S(2)}) copy-start(s32[1,1,8]{2,1,0:T(1,128)} %param.15) | copy-start | bytes 100
  42.5 6.6 %collective-permute-start.13 = (bf16[256,256]{1,0:T(8,128)(2,1)}, bf16[256,256]{1,0:T(8,128)(2,1)}, u32[]{:S(2)}, u32[]{:S(2)}) collective-permute-start(bf16[256,256]{1,0:T(8,128)(2,1)} %slice.137), channel_id=1, source_target_pairs={{0,1},{1,0},{2,3},{3,2},{4,5},{5,4},{6,7},{7,6},{8,9},{9,8},{10,11... | collective-permute-start | bytes 393224 | tf_op jit(solution)/shard_map/ppermute | solution.py:37
  44.3 7.2 %collective-permute-start.9 = (bf16[256,256]{1,0:T(8,128)(2,1)S(1)}, bf16[256,256]{1,0:T(8,128)(2,1)S(1)}, u32[]{:S(2)}, u32[]{:S(2)}) collective-permute-start(bf16[256,256]{1,0:T(8,128)(2,1)S(1)} %slice.138), channel_id=1, source_target_pairs={{0,1},{1,0},{2,3},{3,2},{4,5},{5,4},{6,7},{7,6},{8,9},{9,8},{10,11... | collective-permute-start | bytes 393224 | tf_op jit(solution)/shard_map/ppermute | solution.py:37
  50.1 7.4 %collective-permute-start.14 = (bf16[128,256]{1,0:T(8,128)(2,1)S(1)}, bf16[128,256]{1,0:T(8,128)(2,1)S(1)}, u32[]{:S(2)}, u32[]{:S(2)}) collective-permute-start(bf16[128,256]{1,0:T(8,128)(2,1)S(1)} %slice.139), channel_id=1, source_target_pairs={{0,2},{1,3},{2,0},{3,1},{4,6},{5,7},{6,4},{7,5},{8,10},{9,11},{10,... | collective-permute-start | bytes 196616 | tf_op jit(solution)/shard_map/ppermute | solution.py:37
  51.5 7.0 %collective-permute-start.10 = (bf16[128,256]{1,0:T(8,128)(2,1)S(1)}, bf16[128,256]{1,0:T(8,128)(2,1)S(1)}, u32[]{:S(2)}, u32[]{:S(2)}) collective-permute-start(bf16[128,256]{1,0:T(8,128)(2,1)S(1)} %slice.140), channel_id=1, source_target_pairs={{0,2},{1,3},{2,0},{3,1},{4,6},{5,7},{6,4},{7,5},{8,10},{9,11},{10,... | collective-permute-start | bytes 196616 | tf_op jit(solution)/shard_map/ppermute | solution.py:37
  58.6 6.4 %collective-permute-start.18 = (bf16[128,256]{1,0:T(8,128)(2,1)S(1)}, bf16[128,256]{1,0:T(8,128)(2,1)S(1)}, u32[]{:S(2)}, u32[]{:S(2)}) collective-permute-start(bf16[128,256]{1,0:T(8,128)(2,1)S(1)} %get-tuple-element.63), channel_id=1, source_target_pairs={{0,2},{1,3},{2,0},{3,1},{4,6},{5,7},{6,4},{7,5},{8,10},{9,11},{10,... | collective-permute-start | bytes 196616 | tf_op jit(solution)/shard_map/ppermute | solution.py:37
  58.7 7.5 %collective-permute-start.11 = (bf16[128,256]{1,0:T(8,128)(2,1)S(1)}, bf16[128,256]{1,0:T(8,128)(2,1)S(1)}, u32[]{:S(2)}, u32[]{:S(2)}) collective-permute-start(bf16[128,256]{1,0:T(8,128)(2,1)S(1)} %get-tuple-element.64), channel_id=1, source_target_pairs={{0,2},{1,3},{2,0},{3,1},{4,6},{5,7},{6,4},{7,5},{8,10},{9,11},{10,... | collective-permute-start | bytes 196616 | tf_op jit(solution)/shard_map/ppermute | solution.py:37
  65.1 6.4 %collective-permute-start.19 = (bf16[256,256]{1,0:T(8,128)(2,1)S(1)}, bf16[256,256]{1,0:T(8,128)(2,1)S(1)}, u32[]{:S(2)}, u32[]{:S(2)}) collective-permute-start(bf16[256,256]{1,0:T(8,128)(2,1)S(1)} %pad_maximum_fusion.4), channel_id=1, source_target_pairs={{0,1},{1,0},{2,3},{3,2},{4,5},{5,4},{6,7},{7,6},{8,9},{9,8},{10,11... | collective-permute-start | bytes 393224 | tf_op jit(solution)/shard_map/ppermute | solution.py:37
  66.2 6.7 %collective-permute-start.12 = (bf16[256,256]{1,0:T(8,128)(2,1)S(1)}, bf16[256,256]{1,0:T(8,128)(2,1)S(1)}, u32[]{:S(2)}, u32[]{:S(2)}) collective-permute-start(bf16[256,256]{1,0:T(8,128)(2,1)S(1)} %pad_maximum_fusion.3), channel_id=1, source_target_pairs={{0,1},{1,0},{2,3},{3,2},{4,5},{5,4},{6,7},{7,6},{8,9},{9,8},{10,11... | collective-permute-start | bytes 393224 | tf_op jit(solution)/shard_map/ppermute | solution.py:37
  71.5 1.7 %collective-permute-start.20 = (bf16[512,256]{1,0:T(8,128)(2,1)S(1)}, bf16[512,256]{1,0:T(8,128)(2,1)S(1)}, u32[]{:S(2)}, u32[]{:S(2)}) collective-permute-start(bf16[512,256]{1,0:T(8,128)(2,1)S(1)} %pad_maximum_fusion.1.slope_ref), channel_id=1, source_target_pairs={{0,4},{4,0},{8,12},{12,8},{16,20},{20,16},{24,28},{28,24},{1,5},{5... | collective-permute-start | bytes 786440 | tf_op jit(solution)/shard_map/ppermute | solution.py:29
  72.9 2.8 %collective-permute-start.15 = (bf16[512,256]{1,0:T(8,128)(2,1)S(1)}, bf16[512,256]{1,0:T(8,128)(2,1)S(1)}, u32[]{:S(2)}, u32[]{:S(2)}) collective-permute-start(bf16[512,256]{1,0:T(8,128)(2,1)S(1)} %pad_maximum_fusion.slope_ref), channel_id=1, source_target_pairs={{0,4},{4,0},{8,12},{12,8},{16,20},{20,16},{24,28},{28,24},{1,5},{5... | collective-permute-start | bytes 786440 | tf_op jit(solution)/shard_map/ppermute | solution.py:29
  75.3 6.9 %collective-permute-start.21 = (bf16[512,256]{1,0:T(8,128)(2,1)}, bf16[512,256]{1,0:T(8,128)(2,1)}, u32[]{:S(2)}, u32[]{:S(2)}) collective-permute-start(bf16[512,256]{1,0:T(8,128)(2,1)} %get-tuple-element.54), channel_id=1, source_target_pairs={{0,8},{4,20},{8,0},{12,28},{16,24},{20,4},{24,16},{28,12},{1,9},{5... | collective-permute-start | bytes 786440 | tf_op jit(solution)/shard_map/ppermute | solution.py:370
  77.1 8.1 %collective-permute-start.16 = (bf16[512,256]{1,0:T(8,128)(2,1)S(1)}, bf16[512,256]{1,0:T(8,128)(2,1)S(1)}, u32[]{:S(2)}, u32[]{:S(2)}) collective-permute-start(bf16[512,256]{1,0:T(8,128)(2,1)S(1)} %get-tuple-element.52), channel_id=1, source_target_pairs={{0,8},{4,20},{8,0},{12,28},{16,24},{20,4},{24,16},{28,12},{1,9},{5... | collective-permute-start | bytes 786440 | tf_op jit(solution)/shard_map/ppermute | solution.py:370
  78.8 12.2 %all-to-all-start.1 = ((bf16[8,32,512]{2,1,0:T(8,128)(2,1)}), bf16[8,32,512]{2,1,0:T(8,128)(2,1)S(1)}, u32[]{:S(2)}, u32[]{:S(2)}) async-start(bf16[8,32,512]{2,1,0:T(8,128)(2,1)} %bitcast.28), calls=%async_computation.1 | async-start | bytes 524288 | tf_op jit(solution)/shard_map/all_to_all | solution.py:328
  83.3 6.3 %collective-permute-start.22 = (bf16[256,256]{1,0:T(8,128)(2,1)S(1)}, bf16[256,256]{1,0:T(8,128)(2,1)S(1)}, u32[]{:S(2)}, u32[]{:S(2)}) collective-permute-start(bf16[256,256]{1,0:T(8,128)(2,1)S(1)} %slice.135), channel_id=1, source_target_pairs={{0,16},{4,12},{8,24},{12,4},{16,0},{20,28},{24,8},{28,20},{1,17},{... | collective-permute-start | bytes 393224 | tf_op jit(solution)/shard_map/ppermute | solution.py:370
  85.4 5.6 %collective-permute-start.17 = (bf16[256,256]{1,0:T(8,128)(2,1)S(1)}, bf16[256,256]{1,0:T(8,128)(2,1)S(1)}, u32[]{:S(2)}, u32[]{:S(2)}) collective-permute-start(bf16[256,256]{1,0:T(8,128)(2,1)S(1)} %slice.136), channel_id=1, source_target_pairs={{0,16},{4,12},{8,24},{12,4},{16,0},{20,28},{24,8},{28,20},{1,17},{... | collective-permute-start | bytes 393224 | tf_op jit(solution)/shard_map/ppermute | solution.py:370
  91.1 13.8 %collective-permute-start.23 = (bf16[256,512]{1,0:T(8,128)(2,1)S(1)}, bf16[256,512]{1,0:T(8,128)(2,1)S(1)}, u32[]{:S(2)}, u32[]{:S(2)}) collective-permute-start(bf16[256,512]{1,0:T(8,128)(2,1)S(1)} %pad_maximum_fusion.2), channel_id=1, source_target_pairs={{0,0},{1,10},{2,17},{3,27},{4,4},{5,14},{6,21},{7,31},{8,1},{9,11}... | collective-permute-start | bytes 786440 | tf_op jit(solution)/shard_map/ppermute | solution.py:382
  (4 other events, 17.2 us)

commit v19 on v17

--- a/solution.py
+++ b/solution.py
@@ -247,15 +247,14 @@
     cot = cotangent.reshape(slot_count, value_width)
     held = jnp.where(is_getter, got, pol_weight)
     held, cot, kept_rows = lax.optimization_barrier((held, cot, kept_rows))
+    for number in range(1, levels):
+        got, is_getter = stage(number, held)
+        if number < levels - 1:
+            held = jnp.where(is_getter, got, held)
     parts = []
     for j in range(PARTS):
         cols = slice(j * width, (j + 1) * width)
-        held_part = held[:, cols]
-        for number in range(1, levels):
-            got_part, is_getter_part = stage(number, held_part)
-            if number < levels - 1:
-                held_part = jnp.where(is_getter_part, got_part, held_part)
-        parts.append((held_part, got_part, is_getter_part))
+        parts.append((held[:, cols], got[:, cols], is_getter))
     got_cot = lax.all_to_all(cot, "dp", split_axis=0, concat_axis=0, tiled=True)
 
     def plane_bit(level):

time: 103 us -> 105 us (1.019)
  starting transfers between devices: 48.6 us -> 44.6 us
  waiting for transfers between devices: 27.6 us -> 31.1 us
  local copies, waits for them, and re-layouts: 1.1 us -> 2.39 us
    ppermute x3 -> x2, waiting for transfers between devices: 0.01 us -> 6.28 us  [stage(): return (lax.ppermute(held, AXES, pairs), is_getter)]
    all_to_all x1, waiting for transfers between devices: 2.38 us -> 0.01 us  [on_device(): got_cot = lax.all_to_all(cot, 'dp', split_axis=0, concat_axis=0, tiled=True)]
    ppermute x3 -> x2, starting transfers between devices: 4.22 us -> 2.01 us  [stage(): return (lax.ppermute(held, AXES, pairs), is_getter)]
    ppermute x11, starting transfers between devices: 26.3 us -> 24.3 us  [crossed(): return lax.ppermute(array, 'tensor', [(i, i ^ step) for i in range(count)])]
    ppermute x4, starting transfers between devices: 5.72 us -> 4.25 us  [on_device(): total = total + lax.ppermute(given, 'dp', pairs).astype(F32)]
  transfers between devices with their start and end apart: 26 -> 25, of which waited for: 12 -> 12; matrix products, arithmetic and copies ran while one was open for 11% -> 12% of each run, Pallas kernels for 13% -> 13%
where the time goes in v19:
time: 105 us; the launch traced here: 104 us
  starting transfers between devices  44.6 us (42%)
  waiting for transfers between devices  31.1 us (30%)
  Pallas kernels  13.3 us (13%)
  matrix products  7.77 us (7%)
  other arithmetic  3.95 us (4%)
  local copies, waits for them, and re-layouts  2.39 us (2%)
    ppermute x11, starting transfers between devices, crossed(): return lax.ppermute(array, 'tensor', [(i, i ^ step) for i in range(count)])  24.3 us
    ppermute x11, waiting for transfers between devices, crossed(): return lax.ppermute(array, 'tensor', [(i, i ^ step) for i in range(count)])  12.1 us
    ppermute x1, waiting for transfers between devices, on_device(): grad_weight = lax.ppermute(grad, AXES, pairs).astype(F32)  8 us
    pallas_call x1, Pallas kernels, on_device(): pl.pallas_call(functools.partial(prepare_kernel, tensor_count, steps), gr...  7.09 us
    dot_general x4, matrix products, dot(): return jnp.dot(a, b, preferred_element_type=F32)  6.81 us
    ppermute x2, waiting for transfers between devices, stage(): return (lax.ppermute(held, AXES, pairs), is_getter)  6.28 us
    all_to_all x1, starting transfers between devices, on_device(): lax.all_to_all(sent, 'dp', split_axis=0, concat_axis=0, tiled=True)  5.42 us
    ppermute x4, waiting for transfers between devices, on_device(): total = total + lax.ppermute(given, 'dp', pairs).astype(F32)  4.69 us
  transfers between devices with their start and end apart: 25, of which 12 were waited for; matrix products, arithmetic and copies ran while one was open for 12% of the time, Pallas kernels for 13%

profile of v19, /device:TPU:4, one launch (start us, length us, event | category | flops | bytes accessed | tf_op | source)
XLA Modules:
  0.0 104.1 jit_solution(17676877729148346269)
XLA Ops:
  2.0 7.1 %prepare.1 = (bf16[512,1024]{1,0:T(8,128)(2,1)}, bf16[512,1024]{1,0:T(8,128)(2,1)}, bf16[144,512]{1,0:T(8,128)(2,1)}, bf16[144,512]{1,0:T(8,128)(2,1)}, bf16[144...) custom-call(s32[2]{0:T(128)} %pad_add_fusion.1.at, bf16[512,2048]{1,0:T(8,128)(2,1)} %x_ref.1, f32[1,2048]{1,0:T(1,128)} %bitcast.32, ...), custom_call_target="tpu_custom_call" | custom-call | flops 1073741824 | bytes 8388608 | tf_op jit(solution)/shard_map/prepare/pallas_call | solution.py:202
  9.6 1.1 %broadcast_select_fusion = bf16[1024,512]{1,0:T(8,128)(2,1)} fusion(bf16[1024,512]{1,0:T(8,128)(2,1)S(1)} %collective-permute-done, bf16[1024,512]{1,0:T(8,128)(2,1)S(1)} %copy-done.6, pred[]{:T(512)S(6)} %or.12), kind=kLoop, calls=%fused_computation.5 | loop fusion | flops 524288 | bytes 3145729 | tf_op jit(solution)/shard_map/jit(_where)/select_n | solution.py:248
  10.6 1.3 %collective-permute-start.2 = (bf16[1024,512]{1,0:T(8,128)(2,1)}, bf16[1024,512]{1,0:T(8,128)(2,1)S(1)}, u32[]{:S(2)}, u32[]{:S(2)}) collective-permute-start(bf16[1024,512]{1,0:T(8,128)(2,1)} %broadcast_select_fusion), channel_id=1, source_target_pairs={{0,16},{9,25},{18,2},{27,11},{8,24},{1,17},{26,10},{19,3},{4,12},{... | collective-permute-start | bytes 3145736 | tf_op jit(solution)/shard_map/ppermute | solution.py:190
  11.9 1.3 %collective-permute-start.4 = (bf16[144,512]{1,0:T(8,128)(2,1)}, bf16[144,512]{1,0:T(8,128)(2,1)S(1)}, u32[]{:S(2)}, u32[]{:S(2)}) collective-permute-start(bf16[144,512]{1,0:T(8,128)(2,1)} %get-tuple-element.41), channel_id=1, source_target_pairs={{0,1},{1,0},{2,3},{3,2},{4,5},{5,4},{6,7},{7,6},{8,9},{9,8},{10,11... | collective-permute-start | bytes 442376 | tf_op jit(solution)/shard_map/ppermute | solution.py:37
  13.2 11.0 %collective-permute-start.5 = (bf16[144,512]{1,0:T(8,128)(2,1)}, bf16[144,512]{1,0:T(8,128)(2,1)S(1)}, u32[]{:S(2)}, u32[]{:S(2)}) collective-permute-start(bf16[144,512]{1,0:T(8,128)(2,1)} %get-tuple-element.42), channel_id=1, source_target_pairs={{0,2},{1,3},{2,0},{3,1},{4,6},{5,7},{6,4},{7,5},{8,10},{9,11},{10,... | collective-permute-start | bytes 442376 | tf_op jit(solution)/shard_map/ppermute | solution.py:37
  24.2 4.1 %all-to-all-start = ((bf16[8,32,512]{2,1,0:T(8,128)(2,1)}), bf16[8,32,512]{2,1,0:T(8,128)(2,1)S(1)}, u32[]{:S(2)}, u32[]{:S(2)}) async-start(bf16[8,32,512]{2,1,0:T(8,128)(2,1)} %bitcast.13), calls=%async_computation | async-start | bytes 524288 | tf_op jit(solution)/shard_map/all_to_all | solution.py:258
  28.3 6.3 %collective-permute-done.2 = bf16[1024,512]{1,0:T(8,128)(2,1)S(1)} collective-permute-done((bf16[1024,512]{1,0:T(8,128)(2,1)}, bf16[1024,512]{1,0:T(8,128)(2,1)S(1)}, u32[]{:S(2)}, u32[]{:S(2)}) %collective-permute-start.2) | collective-permute-done | bytes 1048608 | tf_op jit(solution)/shard_map/ppermute | solution.py:190
  35.6 2.2 %convolution_convert_fusion.2 = bf16[512,256]{1,0:T(8,128)(2,1)} fusion(bf16[512,1024]{1,0:T(8,128)(2,1)S(1)} %collective-permute-done.1.got_ref, bf16[1024,512]{1,0:T(8,128)(2,1)S(1)} %collective-permute-done.2, bf16[1024,512]{1,0:T(8,128)(2,1)} %broadcast_select_fusion, pred[]{:T(512)S(6)} %or.15), kind=kOutput, calls=%fused_computation.4 | convolution fusion | flops 268828672 | bytes 2359297 | tf_op jit(solution)/shard_map/dot_general | solution.py:21
  37.8 1.2 %slice.89 = bf16[1024,256]{1,0:T(8,128)(2,1)S(1)} slice(bf16[1024,512]{1,0:T(8,128)(2,1)} %copy-done.8), slice={[0:1024], [0:256]} | slice | bytes 1048576 | tf_op jit(solution)/shard_map/slice | solution.py:257
  39.0 1.6 %convolution_convert_fusion.1 = bf16[512,256]{1,0:T(8,128)(2,1)S(1)} fusion(bf16[512,1024]{1,0:T(8,128)(2,1)S(1)} %collective-permute-done.1.got_ref, bf16[1024,256]{1,0:T(8,128)(2,1)S(1)} %slice.89, bf16[1024,512]{1,0:T(8,128)(2,1)} %broadcast_select_fusion, pred[]{:T(512)S(6)} %or.15), kind=kOutput, calls=%fused_computation.3 | convolution fusion | flops 268828672 | bytes 2359297 | tf_op jit(solution)/shard_map/dot_general | solution.py:21
  41.1 1.6 %convolution_add_fusion.1 = f32[512,256]{1,0:T(8,128)S(1)} fusion(bf16[512,1024]{1,0:T(8,128)(2,1)S(1)} %copy-done, bf16[512,256]{1,0:T(8,128)(2,1)} %collective-permute-done.3, bf16[1024,512]{1,0:T(8,128)(2,1)S(1)} %copy-done.9, bf16[1024,512]{1,0:T(8,128)(2,1)} %broadcast_select_fusion, pred[]{:T(512)S(6)} %or.15), kind=kOutput, calls=%fused_computation.1 | convolution fusion | flops 268959744 | bytes 2883585 | tf_op jit(solution)/shard_map/dot_general | solution.py:21
  42.7 2.5 %collective-permute-start.12 = (bf16[256,256]{1,0:T(8,128)(2,1)S(1)}, bf16[256,256]{1,0:T(8,128)(2,1)S(1)}, u32[]{:S(2)}, u32[]{:S(2)}) collective-permute-start(bf16[256,256]{1,0:T(8,128)(2,1)S(1)} %slice.140), channel_id=1, source_target_pairs={{0,1},{1,0},{2,3},{3,2},{4,5},{5,4},{6,7},{7,6},{8,9},{9,8},{10,11... | collective-permute-start | bytes 393224 | tf_op jit(solution)/shard_map/ppermute | solution.py:37
  45.2 1.5 %convolution_add_fusion = f32[512,256]{1,0:T(8,128)S(1)} fusion(bf16[512,1024]{1,0:T(8,128)(2,1)S(1)} %copy-done, bf16[512,256]{1,0:T(8,128)(2,1)S(1)} %collective-permute-done.7, bf16[1024,256]{1,0:T(8,128)(2,1)S(1)} %slice.89, bf16[1024,512]{1,0:T(8,128)(2,1)} %broadcast_select_fusion, pred[]{:T(512)S(6)} %or.15), kind=kOutput, calls=%fused_computation | convolution fusion | flops 268959744 | bytes 2883585 | tf_op jit(solution)/shard_map/dot_general | solution.py:21
  48.0 1.1 %collective-permute-done.12 = bf16[256,256]{1,0:T(8,128)(2,1)S(1)} collective-permute-done((bf16[256,256]{1,0:T(8,128)(2,1)S(1)}, bf16[256,256]{1,0:T(8,128)(2,1)S(1)}, u32[]{:S(2)}, u32[]{:S(2)}) %collective-permute-start.12) | collective-permute-done | bytes 131104 | tf_op jit(solution)/shard_map/ppermute | solution.py:37
  49.1 1.8 %collective-permute-start.13 = (bf16[128,256]{1,0:T(8,128)(2,1)S(1)}, bf16[128,256]{1,0:T(8,128)(2,1)S(1)}, u32[]{:S(2)}, u32[]{:S(2)}) collective-permute-start(bf16[128,256]{1,0:T(8,128)(2,1)S(1)} %slice.142), channel_id=1, source_target_pairs={{0,2},{1,3},{2,0},{3,1},{4,6},{5,7},{6,4},{7,5},{8,10},{9,11},{10,... | collective-permute-start | bytes 196616 | tf_op jit(solution)/shard_map/ppermute | solution.py:37
  52.1 1.9 %collective-permute-start.9 = (bf16[128,256]{1,0:T(8,128)(2,1)S(1)}, bf16[128,256]{1,0:T(8,128)(2,1)S(1)}, u32[]{:S(2)}, u32[]{:S(2)}) collective-permute-start(bf16[128,256]{1,0:T(8,128)(2,1)S(1)} %slice.143), channel_id=1, source_target_pairs={{0,2},{1,3},{2,0},{3,1},{4,6},{5,7},{6,4},{7,5},{8,10},{9,11},{10,... | collective-permute-start | bytes 196616 | tf_op jit(solution)/shard_map/ppermute | solution.py:37
  54.7 3.0 %collective-permute-done.9 = bf16[128,256]{1,0:T(8,128)(2,1)S(1)} collective-permute-done((bf16[128,256]{1,0:T(8,128)(2,1)S(1)}, bf16[128,256]{1,0:T(8,128)(2,1)S(1)}, u32[]{:S(2)}, u32[]{:S(2)}) %collective-permute-start.9) | collective-permute-done | bytes 65568 | tf_op jit(solution)/shard_map/ppermute | solution.py:37
  57.8 1.6 %collective-permute-start.17 = (bf16[128,256]{1,0:T(8,128)(2,1)S(1)}, bf16[128,256]{1,0:T(8,128)(2,1)S(1)}, u32[]{:S(2)}, u32[]{:S(2)}) collective-permute-start(bf16[128,256]{1,0:T(8,128)(2,1)S(1)} %get-tuple-element.61), channel_id=1, source_target_pairs={{0,2},{1,3},{2,0},{3,1},{4,6},{5,7},{6,4},{7,5},{8,10},{9,11},{10,... | collective-permute-start | bytes 196616 | tf_op jit(solution)/shard_map/ppermute | solution.py:37
  59.4 1.4 %collective-permute-start.10 = (bf16[128,256]{1,0:T(8,128)(2,1)S(1)}, bf16[128,256]{1,0:T(8,128)(2,1)S(1)}, u32[]{:S(2)}, u32[]{:S(2)}) collective-permute-start(bf16[128,256]{1,0:T(8,128)(2,1)S(1)} %get-tuple-element.62), channel_id=1, source_target_pairs={{0,2},{1,3},{2,0},{3,1},{4,6},{5,7},{6,4},{7,5},{8,10},{9,11},{10,... | collective-permute-start | bytes 196616 | tf_op jit(solution)/shard_map/ppermute | solution.py:37
  60.8 3.6 %collective-permute-done.17 = bf16[128,256]{1,0:T(8,128)(2,1)S(1)} collective-permute-done((bf16[128,256]{1,0:T(8,128)(2,1)S(1)}, bf16[128,256]{1,0:T(8,128)(2,1)S(1)}, u32[]{:S(2)}, u32[]{:S(2)}) %collective-permute-start.17) | collective-permute-done | bytes 65568 | tf_op jit(solution)/shard_map/ppermute | solution.py:37
  65.2 2.2 %collective-permute-start.11 = (bf16[256,256]{1,0:T(8,128)(2,1)S(1)}, bf16[256,256]{1,0:T(8,128)(2,1)S(1)}, u32[]{:S(2)}, u32[]{:S(2)}) collective-permute-start(bf16[256,256]{1,0:T(8,128)(2,1)S(1)} %pad_maximum_fusion.3), channel_id=1, source_target_pairs={{0,1},{1,0},{2,3},{3,2},{4,5},{5,4},{6,7},{7,6},{8,9},{9,8},{10,11... | collective-permute-start | bytes 393224 | tf_op jit(solution)/shard_map/ppermute | solution.py:37
  67.4 2.1 %collective-permute-done.18 = bf16[256,256]{1,0:T(8,128)(2,1)S(1)} collective-permute-done((bf16[256,256]{1,0:T(8,128)(2,1)S(1)}, bf16[256,256]{1,0:T(8,128)(2,1)S(1)}, u32[]{:S(2)}, u32[]{:S(2)}) %collective-permute-start.18) | collective-permute-done | bytes 131104 | tf_op jit(solution)/shard_map/ppermute | solution.py:37
  71.2 2.1 %gradient.3 = (f32[512,256]{1,0:T(8,128)S(1)}, bf16[512,256]{1,0:T(8,128)(2,1)}) custom-call(s32[4]{0:T(128)S(1)} %pad_add_fusion.at, bf16[512,1024]{1,0:T(8,128)(2,1)S(1)} %copy-done, bf16[512,1024]{1,0:T(8,128)(2,1)S(1)} %collective-permute-done.1.got_ref, bf16[512,256]{1,0:T(8,128)(2,1)S(1)} %pad_maximum_fusion.1.slope_ref, ...), custom_call_target="tpu_custom_call" | custom-call | flops 536870912 | bytes 4194304 | tf_op jit(solution)/shard_map/gradient/pallas_call | solution.py:332
  73.3 1.3 %collective-permute-start.20 = (bf16[512,256]{1,0:T(8,128)(2,1)}, bf16[512,256]{1,0:T(8,128)(2,1)}, u32[]{:S(2)}, u32[]{:S(2)}) collective-permute-start(bf16[512,256]{1,0:T(8,128)(2,1)} %get-tuple-element.54), channel_id=1, source_target_pairs={{0,8},{4,20},{8,0},{12,28},{16,24},{20,4},{24,16},{28,12},{1,9},{5... | collective-permute-start | bytes 786440 | tf_op jit(solution)/shard_map/ppermute | solution.py:369
  74.6 1.4 %gradient.2 = (f32[512,256]{1,0:T(8,128)S(1)}, bf16[512,256]{1,0:T(8,128)(2,1)S(1)}) custom-call(s32[4]{0:T(128)S(1)} %pad_add_fusion.at, bf16[512,1024]{1,0:T(8,128)(2,1)S(1)} %copy-done, bf16[512,1024]{1,0:T(8,128)(2,1)S(1)} %collective-permute-done.1.got_ref, bf16[512,256]{1,0:T(8,128)(2,1)S(1)} %pad_maximum_fusion.slope_ref, ...), custom_call_target="tpu_custom_call" | custom-call | flops 536870912 | bytes 4194304 | tf_op jit(solution)/shard_map/gradient/pallas_call | solution.py:332
  76.8 5.4 %all-to-all-start.1 = ((bf16[8,32,512]{2,1,0:T(8,128)(2,1)}), bf16[8,32,512]{2,1,0:T(8,128)(2,1)S(1)}, u32[]{:S(2)}, u32[]{:S(2)}) async-start(bf16[8,32,512]{2,1,0:T(8,128)(2,1)} %bitcast.28), calls=%async_computation.1 | async-start | bytes 524288 | tf_op jit(solution)/shard_map/all_to_all | solution.py:327
  83.5 2.0 %collective-permute-start.16 = (bf16[256,256]{1,0:T(8,128)(2,1)S(1)}, bf16[256,256]{1,0:T(8,128)(2,1)S(1)}, u32[]{:S(2)}, u32[]{:S(2)}) collective-permute-start(bf16[256,256]{1,0:T(8,128)(2,1)S(1)} %slice.139), channel_id=1, source_target_pairs={{0,16},{4,12},{8,24},{12,4},{16,0},{20,28},{24,8},{28,20},{1,17},{... | collective-permute-start | bytes 393224 | tf_op jit(solution)/shard_map/ppermute | solution.py:369
  85.5 3.3 %collective-permute-done.21 = bf16[256,256]{1,0:T(8,128)(2,1)S(1)} collective-permute-done((bf16[256,256]{1,0:T(8,128)(2,1)S(1)}, bf16[256,256]{1,0:T(8,128)(2,1)S(1)}, u32[]{:S(2)}, u32[]{:S(2)}) %collective-permute-start.21) | collective-permute-done | bytes 131104 | tf_op jit(solution)/shard_map/ppermute | solution.py:369
  88.8 1.4 %collective-permute-done.16 = bf16[256,256]{1,0:T(8,128)(2,1)S(1)} collective-permute-done((bf16[256,256]{1,0:T(8,128)(2,1)S(1)}, bf16[256,256]{1,0:T(8,128)(2,1)S(1)}, u32[]{:S(2)}, u32[]{:S(2)}) %collective-permute-start.16) | collective-permute-done | bytes 131104 | tf_op jit(solution)/shard_map/ppermute | solution.py:369
  90.3 3.2 %collective-permute-start.22 = (bf16[256,512]{1,0:T(8,128)(2,1)S(1)}, bf16[256,512]{1,0:T(8,128)(2,1)S(1)}, u32[]{:S(2)}, u32[]{:S(2)}) collective-permute-start(bf16[256,512]{1,0:T(8,128)(2,1)S(1)} %pad_maximum_fusion.2), channel_id=1, source_target_pairs={{0,0},{1,10},{2,17},{3,27},{4,4},{5,14},{6,21},{7,31},{8,1},{9,11}... | collective-permute-start | bytes 786440 | tf_op jit(solution)/shard_map/ppermute | solution.py:381
  93.6 1.7 %write.1 = bf16[256,512]{1,0:T(8,128)(2,1)} custom-call(bf16[256,512]{1,0:T(8,128)(2,1)} %bitcast.29), custom_call_target="tpu_custom_call" | custom-call | bytes 524288 | tf_op jit(solution)/shard_map/write/pallas_call | solution.py:382
  95.2 8.0 %collective-permute-done.22 = bf16[256,512]{1,0:T(8,128)(2,1)S(1)} collective-permute-done((bf16[256,512]{1,0:T(8,128)(2,1)S(1)}, bf16[256,512]{1,0:T(8,128)(2,1)S(1)}, u32[]{:S(2)}, u32[]{:S(2)}) %collective-permute-start.22) | collective-permute-done | bytes 262176 | tf_op jit(solution)/shard_map/ppermute | solution.py:381
  (74 shorter events, 11.8 us)
Async XLA Ops:
  0.6 8.9 %collective-permute-start = (bf16[1024,512]{1,0:T(8,128)(2,1)}, bf16[1024,512]{1,0:T(8,128)(2,1)S(1)}, u32[]{:S(2)}, u32[]{:S(2)}) collective-permute-start(bf16[1024,512]{1,0:T(8,128)(2,1)} %param.14), channel_id=1, source_target_pairs={{0,8},{9,1},{18,26},{27,19},{4,20},{13,29},{22,6},{31,15}} | collective-permute-start | bytes 3145736 | tf_op jit(solution)/shard_map/ppermute | solution.py:190
  2.0 7.6 %copy-start.6 = (bf16[1024,512]{1,0:T(8,128)(2,1)S(1)}, bf16[1024,512]{1,0:T(8,128)(2,1)}, u32[]{:S(2)}) copy-start(bf16[1024,512]{1,0:T(8,128)(2,1)} %param.14) | copy-start | bytes 3145732
  9.1 15.1 %copy-start.10 = (bf16[144,512]{1,0:T(8,128)(2,1)S(1)}, bf16[144,512]{1,0:T(8,128)(2,1)}, u32[]{:S(2)}) copy-start(bf16[144,512]{1,0:T(8,128)(2,1)} %get-tuple-element.43) | copy-start | bytes 442372
  9.1 19.3 %collective-permute-start.1 = (bf16[512,1024]{1,0:T(8,128)(2,1)}, bf16[512,1024]{1,0:T(8,128)(2,1)S(1)}, u32[]{:S(2)}, u32[]{:S(2)}) collective-permute-start(bf16[512,1024]{1,0:T(8,128)(2,1)} %get-tuple-element.32), channel_id=1, source_target_pairs={{0,4},{4,0},{8,12},{12,8},{16,20},{20,16},{24,28},{28,24},{1,5},{5... | collective-permute-start | bytes 3145736 | tf_op jit(solution)/shard_map/ppermute | solution.py:29
  10.6 24.0 %collective-permute-start.2 = (bf16[1024,512]{1,0:T(8,128)(2,1)}, bf16[1024,512]{1,0:T(8,128)(2,1)S(1)}, u32[]{:S(2)}, u32[]{:S(2)}) collective-permute-start(bf16[1024,512]{1,0:T(8,128)(2,1)} %broadcast_select_fusion), channel_id=1, source_target_pairs={{0,16},{9,25},{18,2},{27,11},{8,24},{1,17},{26,10},{19,3},{4,12},{... | collective-permute-start | bytes 3145736 | tf_op jit(solution)/shard_map/ppermute | solution.py:190
  11.9 34.9 %collective-permute-start.4 = (bf16[144,512]{1,0:T(8,128)(2,1)}, bf16[144,512]{1,0:T(8,128)(2,1)S(1)}, u32[]{:S(2)}, u32[]{:S(2)}) collective-permute-start(bf16[144,512]{1,0:T(8,128)(2,1)} %get-tuple-element.41), channel_id=1, source_target_pairs={{0,1},{1,0},{2,3},{3,2},{4,5},{5,4},{6,7},{7,6},{8,9},{9,8},{10,11... | collective-permute-start | bytes 442376 | tf_op jit(solution)/shard_map/ppermute | solution.py:37
  13.2 33.6 %collective-permute-start.5 = (bf16[144,512]{1,0:T(8,128)(2,1)}, bf16[144,512]{1,0:T(8,128)(2,1)S(1)}, u32[]{:S(2)}, u32[]{:S(2)}) collective-permute-start(bf16[144,512]{1,0:T(8,128)(2,1)} %get-tuple-element.42), channel_id=1, source_target_pairs={{0,2},{1,3},{2,0},{3,1},{4,6},{5,7},{6,4},{7,5},{8,10},{9,11},{10,... | collective-permute-start | bytes 442376 | tf_op jit(solution)/shard_map/ppermute | solution.py:37
  24.2 22.6 %collective-permute-start.6 = (bf16[144,512]{1,0:T(8,128)(2,1)S(1)}, bf16[144,512]{1,0:T(8,128)(2,1)S(1)}, u32[]{:S(2)}, u32[]{:S(2)}) collective-permute-start(bf16[144,512]{1,0:T(8,128)(2,1)S(1)} %copy-done.10), channel_id=1, source_target_pairs={{0,3},{1,2},{2,1},{3,0},{4,7},{5,6},{6,5},{7,4},{8,11},{9,10},{10,... | collective-permute-start | bytes 442376 | tf_op jit(solution)/shard_map/ppermute | solution.py:37
  24.2 14.7 %all-to-all-start = ((bf16[8,32,512]{2,1,0:T(8,128)(2,1)}), bf16[8,32,512]{2,1,0:T(8,128)(2,1)S(1)}, u32[]{:S(2)}, u32[]{:S(2)}) async-start(bf16[8,32,512]{2,1,0:T(8,128)(2,1)} %bitcast.13), calls=%async_computation | async-start | bytes 524288 | tf_op jit(solution)/shard_map/all_to_all | solution.py:258
  37.8 3.3 %collective-permute-start.3 = (bf16[512,256]{1,0:T(8,128)(2,1)}, bf16[512,256]{1,0:T(8,128)(2,1)}, u32[]{:S(2)}, u32[]{:S(2)}) collective-permute-start(bf16[512,256]{1,0:T(8,128)(2,1)} %convolution_convert_fusion.2), channel_id=1, source_target_pairs={{0,4},{4,0},{8,12},{12,8},{16,20},{20,16},{24,28},{28,24},{1,5},{5... | collective-permute-start | bytes 786440 | tf_op jit(solution)/shard_map/ppermute | solution.py:29
  40.6 4.7 %collective-permute-start.7 = (bf16[512,256]{1,0:T(8,128)(2,1)S(1)}, bf16[512,256]{1,0:T(8,128)(2,1)S(1)}, u32[]{:S(2)}, u32[]{:S(2)}) collective-permute-start(bf16[512,256]{1,0:T(8,128)(2,1)S(1)} %convolution_convert_fusion.1), channel_id=1, source_target_pairs={{0,4},{4,0},{8,12},{12,8},{16,20},{20,16},{24,28},{28,24},{1,5},{5... | collective-permute-start | bytes 786440 | tf_op jit(solution)/shard_map/ppermute | solution.py:29
  42.6 4.2 %copy-start.1 = (bf16[144,512]{1,0:T(8,128)(2,1)S(1)}, bf16[144,512]{1,0:T(8,128)(2,1)}, u32[]{:S(2)}) copy-start(bf16[144,512]{1,0:T(8,128)(2,1)} %get-tuple-element.40.refs_0_) | copy-start | bytes 442372
  42.6 4.2 %copy-start.2 = (s32[1,1,8]{2,1,0:T(1,128)S(1)}, s32[1,1,8]{2,1,0:T(1,128)}, u32[]{:S(2)}) copy-start(s32[1,1,8]{2,1,0:T(1,128)} %param.15) | copy-start | bytes 100
  42.6 4.2 %copy-start.3 = (s32[1,1,8]{2,1,0:T(1,128)S(1)}, s32[1,1,8]{2,1,0:T(1,128)}, u32[]{:S(2)}) copy-start(s32[1,1,8]{2,1,0:T(1,128)} %param.16) | copy-start | bytes 100
  42.7 4.2 %copy-start.4 = (f32[1,1,8]{2,1,0:T(1,128)S(1)}, f32[1,1,8]{2,1,0:T(1,128)}, u32[]{:S(2)}) copy-start(f32[1,1,8]{2,1,0:T(1,128)} %param.17) | copy-start | bytes 100
  42.7 4.2 %copy-start.5 = (f32[128]{0:T(128)S(1)}, f32[128]{0:T(128)}, u32[]{:S(2)}) copy-start(f32[128]{0:T(128)} %param.18) | copy-start | bytes 1540
  42.7 6.4 %collective-permute-start.12 = (bf16[256,256]{1,0:T(8,128)(2,1)S(1)}, bf16[256,256]{1,0:T(8,128)(2,1)S(1)}, u32[]{:S(2)}, u32[]{:S(2)}) collective-permute-start(bf16[256,256]{1,0:T(8,128)(2,1)S(1)} %slice.140), channel_id=1, source_target_pairs={{0,1},{1,0},{2,3},{3,2},{4,5},{5,4},{6,7},{7,6},{8,9},{9,8},{10,11... | collective-permute-start | bytes 393224 | tf_op jit(solution)/shard_map/ppermute | solution.py:37
  46.8 5.3 %collective-permute-start.8 = (bf16[256,256]{1,0:T(8,128)(2,1)S(1)}, bf16[256,256]{1,0:T(8,128)(2,1)S(1)}, u32[]{:S(2)}, u32[]{:S(2)}) collective-permute-start(bf16[256,256]{1,0:T(8,128)(2,1)S(1)} %slice.141), channel_id=1, source_target_pairs={{0,1},{1,0},{2,3},{3,2},{4,5},{5,4},{6,7},{7,6},{8,9},{9,8},{10,11... | collective-permute-start | bytes 393224 | tf_op jit(solution)/shard_map/ppermute | solution.py:37
  49.1 5.5 %collective-permute-start.13 = (bf16[128,256]{1,0:T(8,128)(2,1)S(1)}, bf16[128,256]{1,0:T(8,128)(2,1)S(1)}, u32[]{:S(2)}, u32[]{:S(2)}) collective-permute-start(bf16[128,256]{1,0:T(8,128)(2,1)S(1)} %slice.142), channel_id=1, source_target_pairs={{0,2},{1,3},{2,0},{3,1},{4,6},{5,7},{6,4},{7,5},{8,10},{9,11},{10,... | collective-permute-start | bytes 196616 | tf_op jit(solution)/shard_map/ppermute | solution.py:37
  52.1 5.6 %collective-permute-start.9 = (bf16[128,256]{1,0:T(8,128)(2,1)S(1)}, bf16[128,256]{1,0:T(8,128)(2,1)S(1)}, u32[]{:S(2)}, u32[]{:S(2)}) collective-permute-start(bf16[128,256]{1,0:T(8,128)(2,1)S(1)} %slice.143), channel_id=1, source_target_pairs={{0,2},{1,3},{2,0},{3,1},{4,6},{5,7},{6,4},{7,5},{8,10},{9,11},{10,... | collective-permute-start | bytes 196616 | tf_op jit(solution)/shard_map/ppermute | solution.py:37
  57.8 6.6 %collective-permute-start.17 = (bf16[128,256]{1,0:T(8,128)(2,1)S(1)}, bf16[128,256]{1,0:T(8,128)(2,1)S(1)}, u32[]{:S(2)}, u32[]{:S(2)}) collective-permute-start(bf16[128,256]{1,0:T(8,128)(2,1)S(1)} %get-tuple-element.61), channel_id=1, source_target_pairs={{0,2},{1,3},{2,0},{3,1},{4,6},{5,7},{6,4},{7,5},{8,10},{9,11},{10,... | collective-permute-start | bytes 196616 | tf_op jit(solution)/shard_map/ppermute | solution.py:37
  59.4 5.7 %collective-permute-start.10 = (bf16[128,256]{1,0:T(8,128)(2,1)S(1)}, bf16[128,256]{1,0:T(8,128)(2,1)S(1)}, u32[]{:S(2)}, u32[]{:S(2)}) collective-permute-start(bf16[128,256]{1,0:T(8,128)(2,1)S(1)} %get-tuple-element.62), channel_id=1, source_target_pairs={{0,2},{1,3},{2,0},{3,1},{4,6},{5,7},{6,4},{7,5},{8,10},{9,11},{10,... | collective-permute-start | bytes 196616 | tf_op jit(solution)/shard_map/ppermute | solution.py:37
  64.5 5.0 %collective-permute-start.18 = (bf16[256,256]{1,0:T(8,128)(2,1)S(1)}, bf16[256,256]{1,0:T(8,128)(2,1)S(1)}, u32[]{:S(2)}, u32[]{:S(2)}) collective-permute-start(bf16[256,256]{1,0:T(8,128)(2,1)S(1)} %pad_maximum_fusion.4), channel_id=1, source_target_pairs={{0,1},{1,0},{2,3},{3,2},{4,5},{5,4},{6,7},{7,6},{8,9},{9,8},{10,11... | collective-permute-start | bytes 393224 | tf_op jit(solution)/shard_map/ppermute | solution.py:37
  65.2 5.7 %collective-permute-start.11 = (bf16[256,256]{1,0:T(8,128)(2,1)S(1)}, bf16[256,256]{1,0:T(8,128)(2,1)S(1)}, u32[]{:S(2)}, u32[]{:S(2)}) collective-permute-start(bf16[256,256]{1,0:T(8,128)(2,1)S(1)} %pad_maximum_fusion.3), channel_id=1, source_target_pairs={{0,1},{1,0},{2,3},{3,2},{4,5},{5,4},{6,7},{7,6},{8,9},{9,8},{10,11... | collective-permute-start | bytes 393224 | tf_op jit(solution)/shard_map/ppermute | solution.py:37
  69.5 1.7 %collective-permute-start.19 = (bf16[512,256]{1,0:T(8,128)(2,1)S(1)}, bf16[512,256]{1,0:T(8,128)(2,1)S(1)}, u32[]{:S(2)}, u32[]{:S(2)}) collective-permute-start(bf16[512,256]{1,0:T(8,128)(2,1)S(1)} %pad_maximum_fusion.1.slope_ref), channel_id=1, source_target_pairs={{0,4},{4,0},{8,12},{12,8},{16,20},{20,16},{24,28},{28,24},{1,5},{5... | collective-permute-start | bytes 786440 | tf_op jit(solution)/shard_map/ppermute | solution.py:29
  70.9 3.7 %collective-permute-start.14 = (bf16[512,256]{1,0:T(8,128)(2,1)S(1)}, bf16[512,256]{1,0:T(8,128)(2,1)S(1)}, u32[]{:S(2)}, u32[]{:S(2)}) collective-permute-start(bf16[512,256]{1,0:T(8,128)(2,1)S(1)} %pad_maximum_fusion.slope_ref), channel_id=1, source_target_pairs={{0,4},{4,0},{8,12},{12,8},{16,20},{20,16},{24,28},{28,24},{1,5},{5... | collective-permute-start | bytes 786440 | tf_op jit(solution)/shard_map/ppermute | solution.py:29
  73.3 8.9 %collective-permute-start.20 = (bf16[512,256]{1,0:T(8,128)(2,1)}, bf16[512,256]{1,0:T(8,128)(2,1)}, u32[]{:S(2)}, u32[]{:S(2)}) collective-permute-start(bf16[512,256]{1,0:T(8,128)(2,1)} %get-tuple-element.54), channel_id=1, source_target_pairs={{0,8},{4,20},{8,0},{12,28},{16,24},{20,4},{24,16},{28,12},{1,9},{5... | collective-permute-start | bytes 786440 | tf_op jit(solution)/shard_map/ppermute | solution.py:369
  76.0 7.4 %collective-permute-start.15 = (bf16[512,256]{1,0:T(8,128)(2,1)S(1)}, bf16[512,256]{1,0:T(8,128)(2,1)S(1)}, u32[]{:S(2)}, u32[]{:S(2)}) collective-permute-start(bf16[512,256]{1,0:T(8,128)(2,1)S(1)} %get-tuple-element.52), channel_id=1, source_target_pairs={{0,8},{4,20},{8,0},{12,28},{16,24},{20,4},{24,16},{28,12},{1,9},{5... | collective-permute-start | bytes 786440 | tf_op jit(solution)/shard_map/ppermute | solution.py:369
  76.8 13.5 %all-to-all-start.1 = ((bf16[8,32,512]{2,1,0:T(8,128)(2,1)}), bf16[8,32,512]{2,1,0:T(8,128)(2,1)S(1)}, u32[]{:S(2)}, u32[]{:S(2)}) async-start(bf16[8,32,512]{2,1,0:T(8,128)(2,1)} %bitcast.28), calls=%async_computation.1 | async-start | bytes 524288 | tf_op jit(solution)/shard_map/all_to_all | solution.py:327
  83.3 5.5 %collective-permute-start.21 = (bf16[256,256]{1,0:T(8,128)(2,1)S(1)}, bf16[256,256]{1,0:T(8,128)(2,1)S(1)}, u32[]{:S(2)}, u32[]{:S(2)}) collective-permute-start(bf16[256,256]{1,0:T(8,128)(2,1)S(1)} %slice.138), channel_id=1, source_target_pairs={{0,16},{4,12},{8,24},{12,4},{16,0},{20,28},{24,8},{28,20},{1,17},{... | collective-permute-start | bytes 393224 | tf_op jit(solution)/shard_map/ppermute | solution.py:369
  83.5 6.7 %collective-permute-start.16 = (bf16[256,256]{1,0:T(8,128)(2,1)S(1)}, bf16[256,256]{1,0:T(8,128)(2,1)S(1)}, u32[]{:S(2)}, u32[]{:S(2)}) collective-permute-start(bf16[256,256]{1,0:T(8,128)(2,1)S(1)} %slice.139), channel_id=1, source_target_pairs={{0,16},{4,12},{8,24},{12,4},{16,0},{20,28},{24,8},{28,20},{1,17},{... | collective-permute-start | bytes 393224 | tf_op jit(solution)/shard_map/ppermute | solution.py:369
  90.3 12.9 %collective-permute-start.22 = (bf16[256,512]{1,0:T(8,128)(2,1)S(1)}, bf16[256,512]{1,0:T(8,128)(2,1)S(1)}, u32[]{:S(2)}, u32[]{:S(2)}) collective-permute-start(bf16[256,512]{1,0:T(8,128)(2,1)S(1)} %pad_maximum_fusion.2), channel_id=1, source_target_pairs={{0,0},{1,10},{2,17},{3,27},{4,4},{5,14},{6,21},{7,31},{8,1},{9,11}... | collective-permute-start | bytes 786440 | tf_op jit(solution)/shard_map/ppermute | solution.py:381
  (4 other events, 9.6 us)

commit v20 on v19

--- a/solution.py
+++ b/solution.py
@@ -251,10 +251,7 @@
         got, is_getter = stage(number, held)
         if number < levels - 1:
             held = jnp.where(is_getter, got, held)
-    parts = []
-    for j in range(PARTS):
-        cols = slice(j * width, (j + 1) * width)
-        parts.append((held[:, cols], got[:, cols], is_getter))
+    weight_all = lax.optimization_barrier(jnp.where(is_getter, got, held))
     got_cot = lax.all_to_all(cot, "dp", split_axis=0, concat_axis=0, tiled=True)
 
     def plane_bit(level):
@@ -268,10 +265,9 @@
 
     value_parts = []
     for j in range(PARTS):
-        held_part, got_part, is_getter_part = parts[j]
+        weight = weight_all[:, j * width : (j + 1) * width]
         if j == 0:
-            got_part, got_cot = lax.optimization_barrier((got_part, got_cot))
-        weight = jnp.where(is_getter_part, got_part, held_part)
+            weight, got_cot = lax.optimization_barrier((weight, got_cot))
         value_given = dot(got_rows, weight).astype(BF16)
         value_got = swapped(value_given, dp_count).astype(F32)
         value_parts.append(dot(kept_rows, weight) + value_got)

time: 105 us -> 104 us (level)
  waiting for transfers between devices: 31.1 us -> 35.6 us
  matrix products: 7.77 us -> 4.54 us
  local copies, waits for them, and re-layouts: 2.39 us -> 0.28 us
  starting transfers between devices: 44.6 us -> 43.4 us
    ppermute x11, starting transfers between devices: 24.3 us -> 14.3 us  [crossed(): return lax.ppermute(array, 'tensor', [(i, i ^ step) for i in range(count)])]
    ppermute x5, starting transfers between devices: 1.24 us -> 8.86 us  [swapped(): return lax.ppermute(array, 'dp', [(i, i ^ 1) for i in range(dp_count)])]
    ppermute x11, waiting for transfers between devices: 12.1 us -> 18.3 us  [crossed(): return lax.ppermute(array, 'tensor', [(i, i ^ step) for i in range(count)])]
    dot_general x4, matrix products: 6.81 us -> 3.59 us  [dot(): return jnp.dot(a, b, preferred_element_type=F32)]
    ppermute x2, waiting for transfers between devices: 6.28 us -> 4.72 us  [stage(): return (lax.ppermute(held, AXES, pairs), is_getter)]
    select_n x0 -> x1, other arithmetic: none -> 1.34 us  [on_device(): weight_all = lax.optimization_barrier(jnp.where(is_getter, got, held))]
    slice x1, local copies, waits for them, and re-layouts: 1.16 us -> 0.04 us  [on_device(): weight = weight_all[:, j * width:(j + 1) * width]]
  transfers between devices with their start and end apart: 25 -> 25, of which waited for: 12 -> 13; matrix products, arithmetic and copies ran while one was open for 12% -> 8% of each run, Pallas kernels for 13% -> 13%
where the time goes in v20:
time: 104 us; the launch traced here: 103 us
  starting transfers between devices  43.4 us (42%)
  waiting for transfers between devices  35.6 us (34%)
  Pallas kernels  13.3 us (13%)
  matrix products  4.54 us (4%)
  other arithmetic  4.36 us (4%)
  between operations  1.08 us (1%)
    ppermute x11, waiting for transfers between devices, crossed(): return lax.ppermute(array, 'tensor', [(i, i ^ step) for i in range(count)])  18.3 us
    ppermute x11, starting transfers between devices, crossed(): return lax.ppermute(array, 'tensor', [(i, i ^ step) for i in range(count)])  14.3 us
    ppermute x5, starting transfers between devices, swapped(): return lax.ppermute(array, 'dp', [(i, i ^ 1) for i in range(dp_count)])  8.86 us
    pallas_call x1, Pallas kernels, on_device(): pl.pallas_call(functools.partial(prepare_kernel, tensor_count, steps), gr...  7.11 us
    ppermute x1, waiting for transfers between devices, on_device(): grad_weight = lax.ppermute(grad, AXES, pairs).astype(F32)  7.07 us
    all_to_all x1, starting transfers between devices, on_device(): lax.all_to_all(sent, 'dp', split_axis=0, concat_axis=0, tiled=True)  5.61 us
    ppermute x2, waiting for transfers between devices, stage(): return (lax.ppermute(held, AXES, pairs), is_getter)  4.72 us
    ppermute x4, waiting for transfers between devices, on_device(): total = total + lax.ppermute(given, 'dp', pairs).astype(F32)  4.69 us
  transfers between devices with their start and end apart: 25, of which 13 were waited for; matrix products, arithmetic and copies ran while one was open for 8% of the time, Pallas kernels for 13%

profile of v20, /device:TPU:4, one launch (start us, length us, event | category | flops | bytes accessed | tf_op | source)
XLA Modules:
  0.0 102.6 jit_solution(10191823034714642175)
XLA Ops:
  2.1 7.1 %prepare.1 = (bf16[512,1024]{1,0:T(8,128)(2,1)}, bf16[512,1024]{1,0:T(8,128)(2,1)}, bf16[144,512]{1,0:T(8,128)(2,1)}, bf16[144,512]{1,0:T(8,128)(2,1)}, bf16[144...) custom-call(s32[2]{0:T(128)} %pad_add_fusion.1.at, bf16[512,2048]{1,0:T(8,128)(2,1)} %x_ref.1, f32[1,2048]{1,0:T(1,128)} %bitcast.34, ...), custom_call_target="tpu_custom_call" | custom-call | flops 1073741824 | bytes 8388608 | tf_op jit(solution)/shard_map/prepare/pallas_call | solution.py:202
  9.3 1.3 %collective-permute-start.2 = (bf16[1024,512]{1,0:T(8,128)(2,1)S(1)}, bf16[1024,512]{1,0:T(8,128)(2,1)}, u32[]{:S(2)}, u32[]{:S(2)}) collective-permute-start(bf16[1024,512]{1,0:T(8,128)(2,1)S(1)} %broadcast_select_fusion.1), channel_id=1, source_target_pairs={{0,16},{9,25},{18,2},{27,11},{8,24},{1,17},{26,10},{19,3},{4,12},{... | collective-permute-start | bytes 3145736 | tf_op jit(solution)/shard_map/ppermute | solution.py:190
  10.6 8.0 %collective-permute-start.1 = (bf16[512,1024]{1,0:T(8,128)(2,1)}, bf16[512,1024]{1,0:T(8,128)(2,1)S(1)}, u32[]{:S(2)}, u32[]{:S(2)}) collective-permute-start(bf16[512,1024]{1,0:T(8,128)(2,1)} %get-tuple-element.32), channel_id=1, source_target_pairs={{0,4},{4,0},{8,12},{12,8},{16,20},{20,16},{24,28},{28,24},{1,5},{5... | collective-permute-start | bytes 3145736 | tf_op jit(solution)/shard_map/ppermute | solution.py:29
  18.6 5.5 %collective-permute-start.5 = (bf16[144,512]{1,0:T(8,128)(2,1)}, bf16[144,512]{1,0:T(8,128)(2,1)S(1)}, u32[]{:S(2)}, u32[]{:S(2)}) collective-permute-start(bf16[144,512]{1,0:T(8,128)(2,1)} %get-tuple-element.42), channel_id=1, source_target_pairs={{0,2},{1,3},{2,0},{3,1},{4,6},{5,7},{6,4},{7,5},{8,10},{9,11},{10,... | collective-permute-start | bytes 442376 | tf_op jit(solution)/shard_map/ppermute | solution.py:37
  24.1 4.2 %all-to-all-start = ((bf16[8,32,512]{2,1,0:T(8,128)(2,1)}), bf16[8,32,512]{2,1,0:T(8,128)(2,1)S(1)}, u32[]{:S(2)}, u32[]{:S(2)}) async-start(bf16[8,32,512]{2,1,0:T(8,128)(2,1)} %bitcast.13), calls=%async_computation | async-start | bytes 524288 | tf_op jit(solution)/shard_map/all_to_all | solution.py:255
  28.3 4.7 %collective-permute-done.2 = bf16[1024,512]{1,0:T(8,128)(2,1)} collective-permute-done((bf16[1024,512]{1,0:T(8,128)(2,1)S(1)}, bf16[1024,512]{1,0:T(8,128)(2,1)}, u32[]{:S(2)}, u32[]{:S(2)}) %collective-permute-start.2) | collective-permute-done | bytes 1048608 | tf_op jit(solution)/shard_map/ppermute | solution.py:190
  33.0 1.3 %broadcast_select_fusion = bf16[1024,512]{1,0:T(8,128)(2,1)S(1)} fusion(bf16[1024,512]{1,0:T(8,128)(2,1)} %collective-permute-done.2, bf16[1024,512]{1,0:T(8,128)(2,1)S(1)} %broadcast_select_fusion.1, pred[]{:T(512)S(6)} %or.15), kind=kLoop, calls=%fused_computation.5 | loop fusion | flops 524288 | bytes 3145729 | tf_op jit(solution)/shard_map/jit(_where)/select_n | solution.py:254
  34.4 1.2 %convolution_convert_fusion.2 = bf16[512,256]{1,0:T(8,128)(2,1)} fusion(bf16[512,1024]{1,0:T(8,128)(2,1)S(1)} %collective-permute-done.1.got_ref, bf16[1024,512]{1,0:T(8,128)(2,1)S(1)} %broadcast_select_fusion), kind=kOutput, calls=%fused_computation.4 | convolution fusion | flops 268566528 | bytes 1835008 | tf_op jit(solution)/shard_map/dot_general | solution.py:21
  37.4 1.5 %convolution_add_fusion.1 = f32[512,256]{1,0:T(8,128)S(1)} fusion(bf16[512,1024]{1,0:T(8,128)(2,1)S(1)} %copy-done, bf16[512,256]{1,0:T(8,128)(2,1)} %collective-permute-done.3, bf16[1024,512]{1,0:T(8,128)(2,1)} %copy-done.6), kind=kOutput, calls=%fused_computation.1 | convolution fusion | flops 268697600 | bytes 2359296 | tf_op jit(solution)/shard_map/dot_general | solution.py:21
  39.0 3.1 %collective-permute-start.12 = (bf16[256,256]{1,0:T(8,128)(2,1)S(1)}, bf16[256,256]{1,0:T(8,128)(2,1)S(1)}, u32[]{:S(2)}, u32[]{:S(2)}) collective-permute-start(bf16[256,256]{1,0:T(8,128)(2,1)S(1)} %slice.127), channel_id=1, source_target_pairs={{0,1},{1,0},{2,3},{3,2},{4,5},{5,4},{6,7},{7,6},{8,9},{9,8},{10,11... | collective-permute-start | bytes 393224 | tf_op jit(solution)/shard_map/ppermute | solution.py:37
  42.7 1.1 %rows.1 = (f32[128,512]{1,0:T(8,128)S(1)}, f32[128,128]{1,0:T(8,128)S(1)}, f32[128,128]{1,0:T(8,128)S(1)}, bf16[128,256]{1,0:T(8,128)(2,1)S(1)}) custom-call(s32[8]{0:T(128)S(1)} %bitcast.26, s32[8]{0:T(128)S(1)} %bitcast.27, f32[8]{0:T(128)S(1)} %bitcast.28, f32[1,128]{1,0:T(1,128)S(1)} %bitcast.29, bf16[256,512]{1,0:T(8,128)(2,1)S(1)} %bitcast.25, ...), custom_call_target="tpu_custom_call" | custom-call | flops 33554432 | bytes 2097152 | tf_op jit(solution)/shard_map/rows/pallas_call | solution.py:279
  43.8 2.6 %collective-permute-done.12 = bf16[256,256]{1,0:T(8,128)(2,1)S(1)} collective-permute-done((bf16[256,256]{1,0:T(8,128)(2,1)S(1)}, bf16[256,256]{1,0:T(8,128)(2,1)S(1)}, u32[]{:S(2)}, u32[]{:S(2)}) %collective-permute-start.12) | collective-permute-done | bytes 131104 | tf_op jit(solution)/shard_map/ppermute | solution.py:37
  46.8 1.9 %collective-permute-done.8 = bf16[256,256]{1,0:T(8,128)(2,1)S(1)} collective-permute-done((bf16[256,256]{1,0:T(8,128)(2,1)S(1)}, bf16[256,256]{1,0:T(8,128)(2,1)S(1)}, u32[]{:S(2)}, u32[]{:S(2)}) %collective-permute-start.8) | collective-permute-done | bytes 131104 | tf_op jit(solution)/shard_map/ppermute | solution.py:37
  49.7 2.0 %collective-permute-done.13 = bf16[128,256]{1,0:T(8,128)(2,1)S(1)} collective-permute-done((bf16[128,256]{1,0:T(8,128)(2,1)S(1)}, bf16[128,256]{1,0:T(8,128)(2,1)S(1)}, u32[]{:S(2)}, u32[]{:S(2)}) %collective-permute-start.13) | collective-permute-done | bytes 65568 | tf_op jit(solution)/shard_map/ppermute | solution.py:37
  51.7 3.1 %collective-permute-done.9 = bf16[128,256]{1,0:T(8,128)(2,1)S(1)} collective-permute-done((bf16[128,256]{1,0:T(8,128)(2,1)S(1)}, bf16[128,256]{1,0:T(8,128)(2,1)S(1)}, u32[]{:S(2)}, u32[]{:S(2)}) %collective-permute-start.9) | collective-permute-done | bytes 65568 | tf_op jit(solution)/shard_map/ppermute | solution.py:37
  55.0 2.9 %collective-permute-start.10 = (bf16[128,256]{1,0:T(8,128)(2,1)S(1)}, bf16[128,256]{1,0:T(8,128)(2,1)S(1)}, u32[]{:S(2)}, u32[]{:S(2)}) collective-permute-start(bf16[128,256]{1,0:T(8,128)(2,1)S(1)} %get-tuple-element.62), channel_id=1, source_target_pairs={{0,2},{1,3},{2,0},{3,1},{4,6},{5,7},{6,4},{7,5},{8,10},{9,11},{10,... | collective-permute-start | bytes 196616 | tf_op jit(solution)/shard_map/ppermute | solution.py:37
  57.9 4.9 %collective-permute-done.17 = bf16[128,256]{1,0:T(8,128)(2,1)S(1)} collective-permute-done((bf16[128,256]{1,0:T(8,128)(2,1)S(1)}, bf16[128,256]{1,0:T(8,128)(2,1)S(1)}, u32[]{:S(2)}, u32[]{:S(2)}) %collective-permute-start.17) | collective-permute-done | bytes 65568 | tf_op jit(solution)/shard_map/ppermute | solution.py:37
  63.4 1.5 %collective-permute-start.11 = (bf16[256,256]{1,0:T(8,128)(2,1)S(1)}, bf16[256,256]{1,0:T(8,128)(2,1)S(1)}, u32[]{:S(2)}, u32[]{:S(2)}) collective-permute-start(bf16[256,256]{1,0:T(8,128)(2,1)S(1)} %pad_maximum_fusion.3), channel_id=1, source_target_pairs={{0,1},{1,0},{2,3},{3,2},{4,5},{5,4},{6,7},{7,6},{8,9},{9,8},{10,11... | collective-permute-start | bytes 393224 | tf_op jit(solution)/shard_map/ppermute | solution.py:37
  64.9 2.9 %collective-permute-done.18 = bf16[256,256]{1,0:T(8,128)(2,1)S(1)} collective-permute-done((bf16[256,256]{1,0:T(8,128)(2,1)S(1)}, bf16[256,256]{1,0:T(8,128)(2,1)S(1)}, u32[]{:S(2)}, u32[]{:S(2)}) %collective-permute-start.18) | collective-permute-done | bytes 131104 | tf_op jit(solution)/shard_map/ppermute | solution.py:37
  67.9 1.0 convolution_convert_fusion
  69.5 2.1 %gradient.3 = (f32[512,256]{1,0:T(8,128)S(1)}, bf16[512,256]{1,0:T(8,128)(2,1)}) custom-call(s32[4]{0:T(128)S(1)} %pad_add_fusion.at, bf16[512,1024]{1,0:T(8,128)(2,1)S(1)} %copy-done, bf16[512,1024]{1,0:T(8,128)(2,1)S(1)} %collective-permute-done.1.got_ref, bf16[512,256]{1,0:T(8,128)(2,1)S(1)} %pad_maximum_fusion.1.slope_ref, ...), custom_call_target="tpu_custom_call" | custom-call | flops 536870912 | bytes 4194304 | tf_op jit(solution)/shard_map/gradient/pallas_call | solution.py:328
  71.6 1.5 %collective-permute-start.20 = (bf16[512,256]{1,0:T(8,128)(2,1)}, bf16[512,256]{1,0:T(8,128)(2,1)}, u32[]{:S(2)}, u32[]{:S(2)}) collective-permute-start(bf16[512,256]{1,0:T(8,128)(2,1)} %get-tuple-element.54), channel_id=1, source_target_pairs={{0,8},{4,20},{8,0},{12,28},{16,24},{20,4},{24,16},{28,12},{1,9},{5... | collective-permute-start | bytes 786440 | tf_op jit(solution)/shard_map/ppermute | solution.py:365
  73.1 1.4 %gradient.2 = (f32[512,256]{1,0:T(8,128)S(1)}, bf16[512,256]{1,0:T(8,128)(2,1)S(1)}) custom-call(s32[4]{0:T(128)S(1)} %pad_add_fusion.at, bf16[512,1024]{1,0:T(8,128)(2,1)S(1)} %copy-done, bf16[512,1024]{1,0:T(8,128)(2,1)S(1)} %collective-permute-done.1.got_ref, bf16[512,256]{1,0:T(8,128)(2,1)S(1)} %pad_maximum_fusion.slope_ref, ...), custom_call_target="tpu_custom_call" | custom-call | flops 536870912 | bytes 4194304 | tf_op jit(solution)/shard_map/gradient/pallas_call | solution.py:328
  75.1 5.6 %all-to-all-start.1 = ((bf16[8,32,512]{2,1,0:T(8,128)(2,1)}), bf16[8,32,512]{2,1,0:T(8,128)(2,1)S(1)}, u32[]{:S(2)}, u32[]{:S(2)}) async-start(bf16[8,32,512]{2,1,0:T(8,128)(2,1)} %bitcast.30), calls=%async_computation.1 | async-start | bytes 524288 | tf_op jit(solution)/shard_map/all_to_all | solution.py:323
  80.7 1.0 convert_add_fusion
  82.0 2.0 %collective-permute-start.16 = (bf16[256,256]{1,0:T(8,128)(2,1)S(1)}, bf16[256,256]{1,0:T(8,128)(2,1)S(1)}, u32[]{:S(2)}, u32[]{:S(2)}) collective-permute-start(bf16[256,256]{1,0:T(8,128)(2,1)S(1)} %slice.126), channel_id=1, source_target_pairs={{0,16},{4,12},{8,24},{12,4},{16,0},{20,28},{24,8},{28,20},{1,17},{... | collective-permute-start | bytes 393224 | tf_op jit(solution)/shard_map/ppermute | solution.py:365
  84.0 3.3 %collective-permute-done.21 = bf16[256,256]{1,0:T(8,128)(2,1)S(1)} collective-permute-done((bf16[256,256]{1,0:T(8,128)(2,1)S(1)}, bf16[256,256]{1,0:T(8,128)(2,1)S(1)}, u32[]{:S(2)}, u32[]{:S(2)}) %collective-permute-start.21) | collective-permute-done | bytes 131104 | tf_op jit(solution)/shard_map/ppermute | solution.py:365
  87.3 1.4 %collective-permute-done.16 = bf16[256,256]{1,0:T(8,128)(2,1)S(1)} collective-permute-done((bf16[256,256]{1,0:T(8,128)(2,1)S(1)}, bf16[256,256]{1,0:T(8,128)(2,1)S(1)}, u32[]{:S(2)}, u32[]{:S(2)}) %collective-permute-start.16) | collective-permute-done | bytes 131104 | tf_op jit(solution)/shard_map/ppermute | solution.py:365
  88.8 4.2 %collective-permute-start.22 = (bf16[256,512]{1,0:T(8,128)(2,1)S(1)}, bf16[256,512]{1,0:T(8,128)(2,1)S(1)}, u32[]{:S(2)}, u32[]{:S(2)}) collective-permute-start(bf16[256,512]{1,0:T(8,128)(2,1)S(1)} %pad_maximum_fusion.2), channel_id=1, source_target_pairs={{0,0},{1,10},{2,17},{3,27},{4,4},{5,14},{6,21},{7,31},{8,1},{9,11}... | collective-permute-start | bytes 786440 | tf_op jit(solution)/shard_map/ppermute | solution.py:377
  93.0 1.7 %write.1 = bf16[256,512]{1,0:T(8,128)(2,1)} custom-call(bf16[256,512]{1,0:T(8,128)(2,1)} %bitcast.31), custom_call_target="tpu_custom_call" | custom-call | bytes 524288 | tf_op jit(solution)/shard_map/write/pallas_call | solution.py:378
  94.6 7.1 %collective-permute-done.22 = bf16[256,512]{1,0:T(8,128)(2,1)S(1)} collective-permute-done((bf16[256,512]{1,0:T(8,128)(2,1)S(1)}, bf16[256,512]{1,0:T(8,128)(2,1)S(1)}, u32[]{:S(2)}, u32[]{:S(2)}) %collective-permute-start.22) | collective-permute-done | bytes 262176 | tf_op jit(solution)/shard_map/ppermute | solution.py:377
  101.7 0.9 convert_element_type.78
  (73 shorter events, 7.8 us)
Async XLA Ops:
  0.6 8.6 %collective-permute-start = (bf16[1024,512]{1,0:T(8,128)(2,1)}, bf16[1024,512]{1,0:T(8,128)(2,1)S(1)}, u32[]{:S(2)}, u32[]{:S(2)}) collective-permute-start(bf16[1024,512]{1,0:T(8,128)(2,1)} %param.14), channel_id=1, source_target_pairs={{0,8},{9,1},{18,26},{27,19},{4,20},{13,29},{22,6},{31,15}} | collective-permute-start | bytes 3145736 | tf_op jit(solution)/shard_map/ppermute | solution.py:190
  2.1 7.1 %copy-start.7 = (bf16[1024,512]{1,0:T(8,128)(2,1)S(1)}, bf16[1024,512]{1,0:T(8,128)(2,1)}, u32[]{:S(2)}) copy-start(bf16[1024,512]{1,0:T(8,128)(2,1)} %param.14) | copy-start | bytes 3145732
  9.2 14.9 %copy-start.9 = (bf16[144,512]{1,0:T(8,128)(2,1)S(1)}, bf16[144,512]{1,0:T(8,128)(2,1)}, u32[]{:S(2)}) copy-start(bf16[144,512]{1,0:T(8,128)(2,1)} %get-tuple-element.43) | copy-start | bytes 442372
  9.3 23.7 %collective-permute-start.2 = (bf16[1024,512]{1,0:T(8,128)(2,1)S(1)}, bf16[1024,512]{1,0:T(8,128)(2,1)}, u32[]{:S(2)}, u32[]{:S(2)}) collective-permute-start(bf16[1024,512]{1,0:T(8,128)(2,1)S(1)} %broadcast_select_fusion.1), channel_id=1, source_target_pairs={{0,16},{9,25},{18,2},{27,11},{8,24},{1,17},{26,10},{19,3},{4,12},{... | collective-permute-start | bytes 3145736 | tf_op jit(solution)/shard_map/ppermute | solution.py:190
  10.6 23.8 %collective-permute-start.1 = (bf16[512,1024]{1,0:T(8,128)(2,1)}, bf16[512,1024]{1,0:T(8,128)(2,1)S(1)}, u32[]{:S(2)}, u32[]{:S(2)}) collective-permute-start(bf16[512,1024]{1,0:T(8,128)(2,1)} %get-tuple-element.32), channel_id=1, source_target_pairs={{0,4},{4,0},{8,12},{12,8},{16,20},{20,16},{24,28},{28,24},{1,5},{5... | collective-permute-start | bytes 3145736 | tf_op jit(solution)/shard_map/ppermute | solution.py:29
  18.6 24.0 %collective-permute-start.4 = (bf16[144,512]{1,0:T(8,128)(2,1)}, bf16[144,512]{1,0:T(8,128)(2,1)S(1)}, u32[]{:S(2)}, u32[]{:S(2)}) collective-permute-start(bf16[144,512]{1,0:T(8,128)(2,1)} %get-tuple-element.41), channel_id=1, source_target_pairs={{0,1},{1,0},{2,3},{3,2},{4,5},{5,4},{6,7},{7,6},{8,9},{9,8},{10,11... | collective-permute-start | bytes 442376 | tf_op jit(solution)/shard_map/ppermute | solution.py:37
  18.6 24.0 %collective-permute-start.5 = (bf16[144,512]{1,0:T(8,128)(2,1)}, bf16[144,512]{1,0:T(8,128)(2,1)S(1)}, u32[]{:S(2)}, u32[]{:S(2)}) collective-permute-start(bf16[144,512]{1,0:T(8,128)(2,1)} %get-tuple-element.42), channel_id=1, source_target_pairs={{0,2},{1,3},{2,0},{3,1},{4,6},{5,7},{6,4},{7,5},{8,10},{9,11},{10,... | collective-permute-start | bytes 442376 | tf_op jit(solution)/shard_map/ppermute | solution.py:37
  24.1 18.6 %collective-permute-start.6 = (bf16[144,512]{1,0:T(8,128)(2,1)S(1)}, bf16[144,512]{1,0:T(8,128)(2,1)S(1)}, u32[]{:S(2)}, u32[]{:S(2)}) collective-permute-start(bf16[144,512]{1,0:T(8,128)(2,1)S(1)} %copy-done.9), channel_id=1, source_target_pairs={{0,3},{1,2},{2,1},{3,0},{4,7},{5,6},{6,5},{7,4},{8,11},{9,10},{10,... | collective-permute-start | bytes 442376 | tf_op jit(solution)/shard_map/ppermute | solution.py:37
  24.1 11.5 %all-to-all-start = ((bf16[8,32,512]{2,1,0:T(8,128)(2,1)}), bf16[8,32,512]{2,1,0:T(8,128)(2,1)S(1)}, u32[]{:S(2)}, u32[]{:S(2)}) async-start(bf16[8,32,512]{2,1,0:T(8,128)(2,1)} %bitcast.13), calls=%async_computation | async-start | bytes 524288 | tf_op jit(solution)/shard_map/all_to_all | solution.py:255
  35.6 1.9 %collective-permute-start.3 = (bf16[512,256]{1,0:T(8,128)(2,1)}, bf16[512,256]{1,0:T(8,128)(2,1)}, u32[]{:S(2)}, u32[]{:S(2)}) collective-permute-start(bf16[512,256]{1,0:T(8,128)(2,1)} %convolution_convert_fusion.2), channel_id=1, source_target_pairs={{0,4},{4,0},{8,12},{12,8},{16,20},{20,16},{24,28},{28,24},{1,5},{5... | collective-permute-start | bytes 786440 | tf_op jit(solution)/shard_map/ppermute | solution.py:29
  36.0 6.7 %copy-start.1 = (bf16[144,512]{1,0:T(8,128)(2,1)S(1)}, bf16[144,512]{1,0:T(8,128)(2,1)}, u32[]{:S(2)}) copy-start(bf16[144,512]{1,0:T(8,128)(2,1)} %get-tuple-element.40.refs_0_) | copy-start | bytes 442372
  36.0 6.7 %copy-start.2 = (s32[1,1,8]{2,1,0:T(1,128)S(1)}, s32[1,1,8]{2,1,0:T(1,128)}, u32[]{:S(2)}) copy-start(s32[1,1,8]{2,1,0:T(1,128)} %param.15) | copy-start | bytes 100
  36.0 6.7 %copy-start.3 = (s32[1,1,8]{2,1,0:T(1,128)S(1)}, s32[1,1,8]{2,1,0:T(1,128)}, u32[]{:S(2)}) copy-start(s32[1,1,8]{2,1,0:T(1,128)} %param.16) | copy-start | bytes 100
  36.1 6.7 %copy-start.4 = (f32[1,1,8]{2,1,0:T(1,128)S(1)}, f32[1,1,8]{2,1,0:T(1,128)}, u32[]{:S(2)}) copy-start(f32[1,1,8]{2,1,0:T(1,128)} %param.17) | copy-start | bytes 100
  36.1 6.7 %copy-start.5 = (f32[128]{0:T(128)S(1)}, f32[128]{0:T(128)}, u32[]{:S(2)}) copy-start(f32[128]{0:T(128)} %param.18) | copy-start | bytes 1540
  36.1 6.0 %collective-permute-start.7 = (bf16[512,256]{1,0:T(8,128)(2,1)S(1)}, bf16[512,256]{1,0:T(8,128)(2,1)S(1)}, u32[]{:S(2)}, u32[]{:S(2)}) collective-permute-start(bf16[512,256]{1,0:T(8,128)(2,1)S(1)} %convolution_convert_fusion.1), channel_id=1, source_target_pairs={{0,4},{4,0},{8,12},{12,8},{16,20},{20,16},{24,28},{28,24},{1,5},{5... | collective-permute-start | bytes 786440 | tf_op jit(solution)/shard_map/ppermute | solution.py:29
  39.0 7.4 %collective-permute-start.12 = (bf16[256,256]{1,0:T(8,128)(2,1)S(1)}, bf16[256,256]{1,0:T(8,128)(2,1)S(1)}, u32[]{:S(2)}, u32[]{:S(2)}) collective-permute-start(bf16[256,256]{1,0:T(8,128)(2,1)S(1)} %slice.127), channel_id=1, source_target_pairs={{0,1},{1,0},{2,3},{3,2},{4,5},{5,4},{6,7},{7,6},{8,9},{9,8},{10,11... | collective-permute-start | bytes 393224 | tf_op jit(solution)/shard_map/ppermute | solution.py:37
  42.6 6.1 %collective-permute-start.8 = (bf16[256,256]{1,0:T(8,128)(2,1)S(1)}, bf16[256,256]{1,0:T(8,128)(2,1)S(1)}, u32[]{:S(2)}, u32[]{:S(2)}) collective-permute-start(bf16[256,256]{1,0:T(8,128)(2,1)S(1)} %slice.128), channel_id=1, source_target_pairs={{0,1},{1,0},{2,3},{3,2},{4,5},{5,4},{6,7},{7,6},{8,9},{9,8},{10,11... | collective-permute-start | bytes 393224 | tf_op jit(solution)/shard_map/ppermute | solution.py:37
  46.4 5.2 %collective-permute-start.13 = (bf16[128,256]{1,0:T(8,128)(2,1)S(1)}, bf16[128,256]{1,0:T(8,128)(2,1)S(1)}, u32[]{:S(2)}, u32[]{:S(2)}) collective-permute-start(bf16[128,256]{1,0:T(8,128)(2,1)S(1)} %slice.129), channel_id=1, source_target_pairs={{0,2},{1,3},{2,0},{3,1},{4,6},{5,7},{6,4},{7,5},{8,10},{9,11},{10,... | collective-permute-start | bytes 196616 | tf_op jit(solution)/shard_map/ppermute | solution.py:37
  48.8 6.0 %collective-permute-start.9 = (bf16[128,256]{1,0:T(8,128)(2,1)S(1)}, bf16[128,256]{1,0:T(8,128)(2,1)S(1)}, u32[]{:S(2)}, u32[]{:S(2)}) collective-permute-start(bf16[128,256]{1,0:T(8,128)(2,1)S(1)} %slice.130), channel_id=1, source_target_pairs={{0,2},{1,3},{2,0},{3,1},{4,6},{5,7},{6,4},{7,5},{8,10},{9,11},{10,... | collective-permute-start | bytes 196616 | tf_op jit(solution)/shard_map/ppermute | solution.py:37
  54.9 7.9 %collective-permute-start.17 = (bf16[128,256]{1,0:T(8,128)(2,1)S(1)}, bf16[128,256]{1,0:T(8,128)(2,1)S(1)}, u32[]{:S(2)}, u32[]{:S(2)}) collective-permute-start(bf16[128,256]{1,0:T(8,128)(2,1)S(1)} %get-tuple-element.61), channel_id=1, source_target_pairs={{0,2},{1,3},{2,0},{3,1},{4,6},{5,7},{6,4},{7,5},{8,10},{9,11},{10,... | collective-permute-start | bytes 196616 | tf_op jit(solution)/shard_map/ppermute | solution.py:37
  55.0 8.4 %collective-permute-start.10 = (bf16[128,256]{1,0:T(8,128)(2,1)S(1)}, bf16[128,256]{1,0:T(8,128)(2,1)S(1)}, u32[]{:S(2)}, u32[]{:S(2)}) collective-permute-start(bf16[128,256]{1,0:T(8,128)(2,1)S(1)} %get-tuple-element.62), channel_id=1, source_target_pairs={{0,2},{1,3},{2,0},{3,1},{4,6},{5,7},{6,4},{7,5},{8,10},{9,11},{10,... | collective-permute-start | bytes 196616 | tf_op jit(solution)/shard_map/ppermute | solution.py:37
  62.7 5.0 %collective-permute-start.18 = (bf16[256,256]{1,0:T(8,128)(2,1)S(1)}, bf16[256,256]{1,0:T(8,128)(2,1)S(1)}, u32[]{:S(2)}, u32[]{:S(2)}) collective-permute-start(bf16[256,256]{1,0:T(8,128)(2,1)S(1)} %pad_maximum_fusion.4), channel_id=1, source_target_pairs={{0,1},{1,0},{2,3},{3,2},{4,5},{5,4},{6,7},{7,6},{8,9},{9,8},{10,11... | collective-permute-start | bytes 393224 | tf_op jit(solution)/shard_map/ppermute | solution.py:37
  63.4 5.7 %collective-permute-start.11 = (bf16[256,256]{1,0:T(8,128)(2,1)S(1)}, bf16[256,256]{1,0:T(8,128)(2,1)S(1)}, u32[]{:S(2)}, u32[]{:S(2)}) collective-permute-start(bf16[256,256]{1,0:T(8,128)(2,1)S(1)} %pad_maximum_fusion.3), channel_id=1, source_target_pairs={{0,1},{1,0},{2,3},{3,2},{4,5},{5,4},{6,7},{7,6},{8,9},{9,8},{10,11... | collective-permute-start | bytes 393224 | tf_op jit(solution)/shard_map/ppermute | solution.py:37
  67.8 1.7 %collective-permute-start.19 = (bf16[512,256]{1,0:T(8,128)(2,1)S(1)}, bf16[512,256]{1,0:T(8,128)(2,1)S(1)}, u32[]{:S(2)}, u32[]{:S(2)}) collective-permute-start(bf16[512,256]{1,0:T(8,128)(2,1)S(1)} %pad_maximum_fusion.1.slope_ref), channel_id=1, source_target_pairs={{0,4},{4,0},{8,12},{12,8},{16,20},{20,16},{24,28},{28,24},{1,5},{5... | collective-permute-start | bytes 786440 | tf_op jit(solution)/shard_map/ppermute | solution.py:29
  69.2 3.9 %collective-permute-start.14 = (bf16[512,256]{1,0:T(8,128)(2,1)S(1)}, bf16[512,256]{1,0:T(8,128)(2,1)S(1)}, u32[]{:S(2)}, u32[]{:S(2)}) collective-permute-start(bf16[512,256]{1,0:T(8,128)(2,1)S(1)} %pad_maximum_fusion.slope_ref), channel_id=1, source_target_pairs={{0,4},{4,0},{8,12},{12,8},{16,20},{20,16},{24,28},{28,24},{1,5},{5... | collective-permute-start | bytes 786440 | tf_op jit(solution)/shard_map/ppermute | solution.py:29
  71.6 9.1 %collective-permute-start.20 = (bf16[512,256]{1,0:T(8,128)(2,1)}, bf16[512,256]{1,0:T(8,128)(2,1)}, u32[]{:S(2)}, u32[]{:S(2)}) collective-permute-start(bf16[512,256]{1,0:T(8,128)(2,1)} %get-tuple-element.54), channel_id=1, source_target_pairs={{0,8},{4,20},{8,0},{12,28},{16,24},{20,4},{24,16},{28,12},{1,9},{5... | collective-permute-start | bytes 786440 | tf_op jit(solution)/shard_map/ppermute | solution.py:365
  74.5 7.4 %collective-permute-start.15 = (bf16[512,256]{1,0:T(8,128)(2,1)S(1)}, bf16[512,256]{1,0:T(8,128)(2,1)S(1)}, u32[]{:S(2)}, u32[]{:S(2)}) collective-permute-start(bf16[512,256]{1,0:T(8,128)(2,1)S(1)} %get-tuple-element.52), channel_id=1, source_target_pairs={{0,8},{4,20},{8,0},{12,28},{16,24},{20,4},{24,16},{28,12},{1,9},{5... | collective-permute-start | bytes 786440 | tf_op jit(solution)/shard_map/ppermute | solution.py:365
  75.1 13.7 %all-to-all-start.1 = ((bf16[8,32,512]{2,1,0:T(8,128)(2,1)}), bf16[8,32,512]{2,1,0:T(8,128)(2,1)S(1)}, u32[]{:S(2)}, u32[]{:S(2)}) async-start(bf16[8,32,512]{2,1,0:T(8,128)(2,1)} %bitcast.30), calls=%async_computation.1 | async-start | bytes 524288 | tf_op jit(solution)/shard_map/all_to_all | solution.py:323
  81.7 5.5 %collective-permute-start.21 = (bf16[256,256]{1,0:T(8,128)(2,1)S(1)}, bf16[256,256]{1,0:T(8,128)(2,1)S(1)}, u32[]{:S(2)}, u32[]{:S(2)}) collective-permute-start(bf16[256,256]{1,0:T(8,128)(2,1)S(1)} %slice.125), channel_id=1, source_target_pairs={{0,16},{4,12},{8,24},{12,4},{16,0},{20,28},{24,8},{28,20},{1,17},{... | collective-permute-start | bytes 393224 | tf_op jit(solution)/shard_map/ppermute | solution.py:365
  82.0 6.7 %collective-permute-start.16 = (bf16[256,256]{1,0:T(8,128)(2,1)S(1)}, bf16[256,256]{1,0:T(8,128)(2,1)S(1)}, u32[]{:S(2)}, u32[]{:S(2)}) collective-permute-start(bf16[256,256]{1,0:T(8,128)(2,1)S(1)} %slice.126), channel_id=1, source_target_pairs={{0,16},{4,12},{8,24},{12,4},{16,0},{20,28},{24,8},{28,20},{1,17},{... | collective-permute-start | bytes 393224 | tf_op jit(solution)/shard_map/ppermute | solution.py:365
  88.8 12.9 %collective-permute-start.22 = (bf16[256,512]{1,0:T(8,128)(2,1)S(1)}, bf16[256,512]{1,0:T(8,128)(2,1)S(1)}, u32[]{:S(2)}, u32[]{:S(2)}) collective-permute-start(bf16[256,512]{1,0:T(8,128)(2,1)S(1)} %pad_maximum_fusion.2), channel_id=1, source_target_pairs={{0,0},{1,10},{2,17},{3,27},{4,4},{5,14},{6,21},{7,31},{8,1},{9,11}... | collective-permute-start | bytes 786440 | tf_op jit(solution)/shard_map/ppermute | solution.py:377
  (3 other events, 8.5 us)
